TPU v7x, 32 devices: a whole 2x2x4 slice. The times are simulated.
32 devices in a mesh: req: 32 (over z, y, x, core), seq: 1.
Axes of the slice: x: 2, y: 2, z: 4, core: 2. Of those that a mesh axis runs over, the one named last changes fastest.
Arguments:
- hidden_in: bfloat16 [32, 256, 1792], P('req', 'seq'), may hold values from -6 to 6
- lengths: int32 [32], P('req'), may hold values from 1 to 256, 4096 in all
- log_decay: float32 [32, 256, 8], P('req', 'seq'), may hold values from -1 to 0
- mix_gain: float32 [1792], replicated, may hold values from 0.1 to 1.9
- conv_weight: float32 [3, 1792], replicated, may hold values from -3 to 3
- query_weight: bfloat16 [1792, 128], replicated, may hold values from -0.375 to 0.375
- key_weight: bfloat16 [1792, 128], replicated, may hold values from -0.375 to 0.375
- value_weight: bfloat16 [1792, 896], replicated, may hold values from -0.125 to 0.125
- out_weight: bfloat16 [896, 1792], replicated, may hold values from -0.1875 to 0.1875
- mlp_gain: float32 [1792], replicated, may hold values from 0.1 to 1.9
- gate_weight: bfloat16 [1792, 1792], P(None, 'req'), may hold values from -0.125 to 0.125
- up_weight: bfloat16 [1792, 1792], P(None, 'req'), may hold values from -0.125 to 0.125
- down_weight: bfloat16 [1792, 1792], P(None, 'req'), may hold values from -0.125 to 0.125
Outputs:
- layer_out: bfloat16 [32, 256, 1792], P('req', 'seq')
- end_states: float32 [32, 1, 273, 896], P('req', 'seq')
- end_norms: float32 [32, 1, 273, 8], P('req', 'seq')
Inputs may be any that keep to these rules, and one draw needn't show every extreme that they name: Each prompt has at least one token; the lengths sum to 4096 and the longest fills all 256 slots.
All inputs are finite; a program needn't handle non-finite values. No bound on the sum of `lengths` on one device may be relied on, other than what follows from the above.
Results may differ from a plain program's by a relative error of at most 0.0085.
Values may be sent and summed in bfloat16 or wider, within the bound.
No kernel may reach another device: no remote copies, remote signals or barrier semaphores. Data moves between devices by JAX's collectives and lax.ppermute only.
A program may use at most 128 MiB of HBM per device.

v0:
```python
import jax
import jax.numpy as jnp
from jax import lax
from jax.sharding import PartitionSpec as P


def from_behind(array, axis, by):
    count = lax.axis_size(axis)
    pairs = [(i, i + by) for i in range(count) if 0 <= i + by < count]
    return lax.ppermute(array, axis, pairs)


def entering(array, axis, combine, identity):
    count, here = (lax.axis_size(axis), lax.axis_index(axis))
    everything = jax.tree.map(
        lambda part, kind: lax.all_gather(part.astype(kind), axis),
        array,
        (jnp.bfloat16, jnp.bfloat16, jnp.bfloat16),
    )
    start = jax.tree.map(
        lambda part, zero: jnp.broadcast_to(jnp.asarray(zero, part.dtype), part.shape),
        array,
        identity,
    )

    def hop(k, before):
        reached = k < here
        new = combine(
            before, jax.tree.map(lambda part, own: part[k].astype(own.dtype), everything, array)
        )
        return jax.tree.map(lambda a, b: jnp.where(reached, a, b), new, before)

    return lax.fori_loop(0, count, hop, start)


def features(vectors):
    constant = jnp.ones(vectors.shape[:-1] + (1,), jnp.float32)
    width = vectors.shape[-1]
    squares = (vectors[..., :, None] * vectors[..., None, :]).reshape(
        vectors.shape[:-1] + (width * width,)
    )
    return jnp.concatenate([constant, vectors, squares * 0.5**0.5], axis=-1)


def block_step(carry, inputs):
    memory, key_sum = carry
    query_blk, key_blk, value_blk, value_half, decay_rate, valid_mask = inputs
    highest = lax.Precision.HIGHEST
    cumulative = jnp.cumsum(decay_rate, axis=0)
    scores = jnp.einsum("thi,uhi->htu", query_blk, key_blk, precision=highest)
    kernel = 1.0 + scores + 0.5 * scores * scores
    gap_log = cumulative.T[:, :, None] - cumulative.T[:, None, :]
    block_len = decay_rate.shape[0]
    causal = jnp.arange(block_len)[:, None] >= jnp.arange(block_len)[None, :]
    weights = (
        jnp.where(causal[None], jnp.exp(jnp.minimum(gap_log, 0.0)), 0.0)
        * kernel
        * valid_mask[None, None, :]
    )
    numerator = jnp.einsum(
        "htu,uhv->thv", weights.astype(jnp.bfloat16), value_half, preferred_element_type=jnp.float32
    )
    denominator = jnp.sum(weights, axis=2).T
    query_feat = features(query_blk)
    key_feat = features(key_blk) * valid_mask[:, None, None]
    growth = jnp.exp(cumulative)
    numerator = (
        numerator
        + jnp.einsum("thf,fhv->thv", query_feat, memory, precision=highest) * growth[:, :, None]
    )
    denominator = (
        denominator + jnp.einsum("thf,fh->th", query_feat, key_sum, precision=highest) * growth
    )
    closing = cumulative[-1]
    fading = jnp.exp(closing[None, :] - cumulative)
    faded_keys = key_feat * fading[:, :, None]
    memory = memory * jnp.exp(closing)[None, :, None] + jnp.einsum(
        "uhf,uhv->fhv", faded_keys, value_blk, precision=highest
    )
    key_sum = key_sum * jnp.exp(closing)[None, :] + jnp.sum(faded_keys, axis=0).T
    return ((memory, key_sum), (numerator, denominator))


def span_attention(
    query_f32, key_f32, value_f32, value_half, decay_rate, valid_mask, memory, key_sum, block_len
):
    span = query_f32.shape[0]
    blocks = span // block_len

    def split(array):
        return array.reshape((blocks, block_len) + array.shape[1:])

    carry, outputs = lax.scan(
        block_step,
        (memory, key_sum),
        (
            split(query_f32),
            split(key_f32),
            split(value_f32),
            split(value_half),
            split(decay_rate),
            split(valid_mask),
        ),
    )
    numerator = outputs[0].reshape((span,) + outputs[0].shape[2:])
    denominator = outputs[1].reshape((span,) + outputs[1].shape[2:])
    return (carry[0], carry[1], numerator, denominator)


def rms_scale(rows, gain):
    rows_f32 = rows.astype(jnp.float32)
    factor = lax.rsqrt(jnp.mean(rows_f32 * rows_f32, axis=-1, keepdims=True) + 1e-05)
    return (rows_f32 * factor * gain).astype(jnp.bfloat16)


def feed_forward(row_data, valid_count, gate_weight, up_weight, down_weight):
    row_total = row_data.shape[0]
    block_len = min(256, row_total)
    live_blocks = (valid_count + block_len - 1) // block_len
    initial = jnp.zeros((row_total, row_data.shape[1]), jnp.float32)
    gate_piece = lax.all_gather(gate_weight, "req", axis=1, tiled=True)
    up_piece = lax.all_gather(up_weight, "req", axis=1, tiled=True)
    down_piece = lax.all_gather(down_weight, "req", axis=1, tiled=True)

    def add_block(index, accumulated):
        gate_act = jnp.dot(row_data, gate_piece, preferred_element_type=jnp.float32)
        up_act = jnp.dot(row_data, up_piece, preferred_element_type=jnp.float32)
        hidden_units = (jax.nn.silu(gate_act) * up_act).astype(jnp.bfloat16)
        increment = lax.dot_general(
            hidden_units, down_piece, (((1,), (1,)), ((), ())), preferred_element_type=jnp.float32
        )
        return accumulated + increment

    return lax.fori_loop(0, live_blocks, add_block, initial)


def finish_rows(mixed_rows, valid_mask, mlp_gain, gate_weight, up_weight, down_weight):
    mlp_in = rms_scale(mixed_rows, mlp_gain)
    valid_count = jnp.sum(valid_mask).astype(jnp.int32)
    ffn_out = feed_forward(mlp_in, valid_count, gate_weight, up_weight, down_weight)
    return ((mixed_rows.astype(jnp.float32) + ffn_out) * valid_mask[:, None]).astype(jnp.bfloat16)


def local(
    hidden_in,
    lengths,
    log_decay,
    mix_gain,
    conv_weight,
    query_weight,
    key_weight,
    value_weight,
    out_weight,
    mlp_gain,
    gate_weight,
    up_weight,
    down_weight,
):
    local_len = hidden_in.shape[1]
    rows_in = hidden_in[0]
    decays = log_decay[0]
    head_count = log_decay.shape[2]
    value_len = value_weight.shape[1] // head_count
    feat_in = query_weight.shape[1] // head_count
    feat_len = 1 + feat_in + feat_in * feat_in
    tap_count = conv_weight.shape[0]
    block_len = min(256, local_len)
    feature_scale = feat_in ** (-0.25)
    token_positions = lax.axis_index("seq") * local_len + jnp.arange(local_len, dtype=jnp.int32)
    valid_mask = (token_positions < lengths[0]).astype(jnp.float32)
    normed = rms_scale(rows_in, mix_gain)
    edge_rows = from_behind(normed[local_len - (tap_count - 1) :], "seq", 1)
    extended = jnp.concatenate([edge_rows, normed], axis=0)
    convolved = jnp.zeros(normed.shape, jnp.float32)
    for tap in range(tap_count):
        convolved = convolved + conv_weight[tap][None, :] * extended[
            tap_count - 1 - tap : tap_count - 1 - tap + local_len
        ].astype(jnp.float32)
    gated_rows = (convolved * jax.nn.sigmoid(normed.astype(jnp.float32))).astype(jnp.bfloat16)
    queries = (
        jnp.dot(gated_rows, query_weight, preferred_element_type=jnp.float32) * feature_scale
    ).astype(jnp.bfloat16)
    key_rows = (
        jnp.dot(gated_rows, key_weight, preferred_element_type=jnp.float32) * feature_scale
    ).astype(jnp.bfloat16)
    values = jnp.dot(gated_rows, value_weight, preferred_element_type=jnp.float32).astype(
        jnp.bfloat16
    )
    query_f32 = queries.astype(jnp.float32).reshape(local_len, head_count, feat_in)
    key_f32 = key_rows.astype(jnp.float32).reshape(local_len, head_count, feat_in)
    value_half = values.reshape(local_len, head_count, value_len)
    value_f32 = value_half.astype(jnp.float32)
    decay_rate = jnp.where(valid_mask[:, None] > 0, decays, 0.0)
    empty_memory = jnp.zeros((feat_len, head_count, value_len), jnp.float32)
    empty_keys = jnp.zeros((feat_len, head_count), jnp.float32)
    memory, key_sum, numerator, denominator = span_attention(
        query_f32,
        key_f32,
        value_f32,
        value_half,
        decay_rate,
        valid_mask,
        empty_memory,
        empty_keys,
        block_len,
    )
    span_decay = jnp.sum(decay_rate, axis=0)
    flat_memory = memory.reshape(feat_len, head_count * value_len)

    def merge_states(earlier, later):
        factor = jnp.exp(later[0])
        return (
            earlier[0] + later[0],
            earlier[1] * jnp.repeat(factor, value_len)[None, :] + later[1],
            earlier[2] * factor[None, :] + later[2],
        )

    neutral = (jnp.zeros_like(span_decay), jnp.zeros_like(flat_memory), jnp.zeros_like(key_sum))
    carried = entering((span_decay, flat_memory, key_sum), "seq", merge_states, neutral)
    prior_memory = carried[1]
    prior_keys = carried[2]
    highest = lax.Precision.HIGHEST
    growth = jnp.exp(jnp.cumsum(decay_rate, axis=0))
    query_feat = features(query_f32)
    numerator = (
        numerator
        + jnp.einsum(
            "thf,fhv->thv",
            query_feat,
            prior_memory.reshape(feat_len, head_count, value_len),
            precision=highest,
        )
        * growth[:, :, None]
    )
    denominator = (
        denominator + jnp.einsum("thf,fh->th", query_feat, prior_keys, precision=highest) * growth
    )
    attended = (
        (numerator / denominator[:, :, None])
        .reshape(local_len, head_count * value_len)
        .astype(jnp.bfloat16)
    )
    mixed_rows = (
        rows_in.astype(jnp.float32)
        + jnp.dot(attended, out_weight, preferred_element_type=jnp.float32)
    ).astype(jnp.bfloat16)
    span_factor = jnp.exp(span_decay)
    end_state = prior_memory * jnp.repeat(span_factor, value_len)[None, :] + flat_memory
    end_norm = prior_keys * span_factor[None, :] + key_sum
    result = finish_rows(mixed_rows, valid_mask, mlp_gain, gate_weight, up_weight, down_weight)
    return (result[None], end_state[None, None], end_norm[None, None])


def solution(mesh):
    return jax.shard_map(
        local,
        mesh=mesh,
        in_specs=(
            P("req", "seq", None),
            P("req"),
            P("req", "seq", None),
            P(),
            P(),
            P(),
            P(),
            P(),
            P(),
            P(),
            P(None, "req"),
            P(None, "req"),
            P(None, "req"),
        ),
        out_specs=(P("req", "seq", None), P("req", "seq", None, None), P("req", "seq", None, None)),
        check_vma=False,
    )
```

profile of v0, /device:TPU:0, one launch (start us, length us, event | category | flops | bytes accessed | tf_op | source)
XLA Modules:
  0.0 251.1 jit_solution(1959030512881141647)
XLA Ops:
  7.2 0.7 all-gather.4.cloned.1.call-update
  8.0 0.7 all-gather.6.cloned.1.call-update
  8.7 0.7 all-gather.8.cloned.1.call-update
  9.4 1.4 fusion.18
  10.9 1.5 fusion.20
  12.3 0.9 copy-done.5
  13.3 0.7 collective-permute-start
  14.6 0.1 fusion.52
  14.7 0.6 reduce-window.12
  15.3 0.2 slice_reduce_fusion
  15.5 0.7 fusion.63
  16.2 0.7 multiply_reduce_fusion
  17.0 0.5 exponential_multiply_fusion
  17.5 0.7 add_bitcast_fusion.2
  18.2 0.6 fusion.55
  19.4 0.1 mul.345
  19.6 3.0 %fusion.9 = bf16[256,1792]{1,0:T(8,128)(2,1)S(1)} fusion(bf16[256,1792]{1,0:T(8,128)(2,1)} %copy-done.5, bf16[2,1792]{1,0:T(2,128)(2,1)S(1)} %collective-permute-done, f32[1792]{0:T(1024)S(1)} %get-tuple-element.198, f32[1792]{0:T(1024)S(1)} %get-tuple-element.199, f32[1792]{0:T(1024)S(1)} %get-tuple-element.197), kind=kLoop, calls=%fused_computation.23 | loop fusion | flops 8716288 | bytes 1863680 | tf_op jit(solution)/shard_map/convert_element_type | solution.py:179
  22.5 0.9 copy-done.3
  23.4 3.8 %convolution_convert_fusion = bf16[256,896]{1,0:T(8,128)(2,1)} fusion(bf16[256,1792]{1,0:T(8,128)(2,1)S(1)} %fusion.9, bf16[1792,896]{1,0:T(8,128)(2,1)} %param.22), kind=kOutput, calls=%fused_computation.45 | convolution fusion | flops 822312960 | bytes 4587520 | tf_op jit(solution)/shard_map/dot_general | solution.py:186
  27.3 2.0 copy.28
  29.3 1.8 fusion.41
  31.1 0.3 multiply_multiply_fusion.2
  31.4 1.5 fusion.21
  33.0 0.5 bitcast_convert_fusion
  33.4 2.2 fusion.64
  35.7 0.1 subtract_exponential_fusion
  35.8 0.3 multiply_multiply_fusion.1
  36.1 0.6 copy-done.9
  36.7 1.6 fusion.29
  38.3 1.2 copy.30
  39.5 2.7 %reshape.215 = f32[1,1,273,896]{3,2,1,0:T(8,128)} reshape(f32[273,8,112]{2,1,0:T(8,128)} %copy.30) | data formatting | bytes 1956864 | tf_op jit(solution)/shard_map/reshape | solution.py:208
  42.1 1.4 broadcast_add_fusion
  43.6 1.9 copy.31
  45.6 0.7 fusion.23
  46.2 0.3 convolution_bitcast_fusion
  46.5 0.6 copy-done.8
  47.1 2.6 %fusion.35 = bf16[256,8,112]{0,2,1:T(8,128)(2,1)S(1)} fusion(f32[256,8,112]{0,2,1:T(8,128)S(1)} %convolution_bitcast_fusion, f32[256,8,256]{0,2,1:T(8,128)S(1)} %bitcast.80, f32[256,8,16]{0,2,1:T(8,128)S(1)} %bitcast_convert_fusion.1, f32[273]{0:T(512)S(1)} %copy-done.15, f32[256,8]{0,1:T(8,128)S(1)} %get-tuple-element.215, f32[256,8]{0,1:T(8,128)S(1)} %copy-done.16), kind=kOutput, calls=%fused_computation.47 | convolution fusion | flops 753700864 | bytes 3621956 | tf_op jit(solution)/shard_map/while/body/eval_jaxpr/thf,fhv->thv/dot_general | solution.py:69
  49.8 2.1 fusion.13
  51.9 0.7 add_bitcast_fusion
  52.6 31.0 %all-gather.4.cloned.1.call-done = bf16[1792,1792]{0,1:T(8,128)(2,1)} async-done(((bf16[1792,56]{0,1:T(8,128)(2,1)}), bf16[1792,1792]{0,1:T(8,128)(2,1)}) %all-gather.4.cloned.1.call-update) | async-done | bytes 6422544 | tf_op jit(solution)/shard_map/all_gather | solution.py:121
  83.6 6.2 %fusion.50 = f32[256,1792]{1,0:T(8,128)} fusion(bf16[1792,1792]{0,1:T(8,128)(2,1)} %all-gather.4.cloned.1.call-done, bf16[256,1792]{1,0:T(8,128)(2,1)} %get-tuple-element.219, f32[1792]{0:T(1024)S(1)} %copy-done.24, f32[256]{0:T(256)S(1)} %add_rsqrt_fusion), kind=kOutput, calls=%fused_computation.67 | convolution fusion | flops 1646002176 | bytes 9183232 | tf_op jit(solution)/shard_map/while/body/dot_general | solution.py:126
  89.9 65.1 %all-gather.6.cloned.1.call-done = bf16[1792,1792]{0,1:T(8,128)(2,1)} async-done(((bf16[1792,56]{0,1:T(8,128)(2,1)}), bf16[1792,1792]{0,1:T(8,128)(2,1)}) %all-gather.6.cloned.1.call-update) | async-done | bytes 6422544 | tf_op jit(solution)/shard_map/all_gather | solution.py:122
  155.0 71.4 %all-gather.8.cloned.1.call-done = bf16[1792,1792]{0,1:T(8,128)(2,1)} async-done(((bf16[1792,56]{0,1:T(8,128)(2,1)}), bf16[1792,1792]{0,1:T(8,128)(2,1)}) %all-gather.8.cloned.1.call-update) | async-done | bytes 6422544 | tf_op jit(solution)/shard_map/all_gather | solution.py:123
  226.3 10.4 %fusion.46 = f32[256,1792]{1,0:T(8,128)} fusion(bf16[1792,1792]{0,1:T(8,128)(2,1)} %all-gather.8.cloned.1.call-done, bf16[1792,1792]{0,1:T(8,128)(2,1)} %all-gather.6.cloned.1.call-done, f32[256,1792]{1,0:T(8,128)} %fusion.50, bf16[256,1792]{1,0:T(8,128)(2,1)} %get-tuple-element.219, f32[1792]{0:T(1024)S(1)} %copy-done.24, f32[256]{0:T(256)S(1)} %add_rsqrt_fusion), kind=kOutput, calls=%fused_computation.63 | convolution fusion | flops 3292921856 | bytes 17440768 | tf_op jit(solution)/shard_map/while/body/dot_general | solution.py:129
  236.8 1.4 broadcast_in_dim.101
  238.2 3.5 %while.10 = (s32[]{:T(128)}, f32[256,1792]{1,0:T(8,128)}, s32[]{:T(128)}, f32[256,1792]{1,0:T(8,128)}, s32[]{:T(128)}) while((s32[]{:T(128)}, f32[256,1792]{1,0:T(8,128)}, s32[]{:T(128)}, f32[256,1792]{1,0:T(8,128)}, s32[]{:T(128)}) %tuple.53), condition=%wide.region_7.8_spmd, body=%wide.region_6.7_spmd.sunk | while | flops 458754 | bytes 5505085 | solution.py:134
  238.2 3.5 %add.214 = f32[256,1792]{1,0:T(8,128)} add(f32[256,1792]{1,0:T(8,128)} %get-tuple-element.258, f32[256,1792]{1,0:T(8,128)} %get-tuple-element.265) | non-fusion elementwise | flops 458752 | bytes 5505024 | tf_op jit(solution)/shard_map/while/body/add | solution.py:132
  241.6 2.9 %fusion.45 = bf16[1,256,1792]{2,1,0:T(8,128)(2,1)} fusion(f32[256,1792]{1,0:T(8,128)} %get-tuple-element.190, bf16[256,1792]{1,0:T(8,128)(2,1)} %get-tuple-element.219, f32[256]{0:T(256)S(1)} %get-tuple-element.222), kind=kLoop, calls=%fused_computation.61 | loop fusion | flops 1835008 | bytes 3671040 | tf_op jit(solution)/shard_map/broadcast_in_dim | solution.py:251
  (64 shorter events, 0.5 us)
Async XLA Ops:
  7.2 42.6 %copy-start = (bf16[896,1792]{1,0:T(8,128)(2,1)S(1)}, bf16[896,1792]{1,0:T(8,128)(2,1)}, u32[]{:S(2)}) copy-start(bf16[896,1792]{1,0:T(8,128)(2,1)} %param.23) | copy-start | bytes 9633796
  7.2 7.4 %copy-start.17 = (f32[1,256,8]{1,2,0:T(8,128)S(1)}, f32[1,256,8]{1,2,0:T(8,128)}, u32[]{:S(2)}) copy-start(f32[1,256,8]{1,2,0:T(8,128)} %param.17) | copy-start | bytes 24580
  7.2 9.7 %copy-start.13 = (f32[3,1792]{1,0:T(4,128)S(1)}, f32[3,1792]{1,0:T(4,128)}, u32[]{:S(2)}) copy-start(f32[3,1792]{1,0:T(4,128)} %param.19) | copy-start | bytes 64516
  7.2 76.4 %all-gather.4.cloned.1.call-start = ((), (), s32[]{:S(2)}) async-start(), calls=%async_computation | async-start | bytes 6623232 | tf_op jit(solution)/shard_map/all_gather | solution.py:121
  7.9 147.0 %all-gather.6.cloned.1.call-start = ((), (), s32[]{:S(2)}) async-start(), calls=%async_computation.1 | async-start | bytes 6623232 | tf_op jit(solution)/shard_map/all_gather | solution.py:122
  8.7 217.7 %all-gather.8.cloned.1.call-start = ((), (), s32[]{:S(2)}) async-start(), calls=%async_computation.2 | async-start | bytes 6623232 | tf_op jit(solution)/shard_map/all_gather | solution.py:123
  12.3 0.9 copy-start.5
  13.3 6.3 %collective-permute-start = (bf16[2,1792]{1,0:T(2,128)(2,1)S(1)}, bf16[2,1792]{1,0:T(2,128)(2,1)S(1)}, u32[]{:S(2)}, u32[]{:S(2)}) collective-permute-start(bf16[2,1792]{1,0:T(2,128)(2,1)S(1)} %slice.39), channel_id=1, source_target_pairs={} | collective-permute-start | bytes 21512 | tf_op jit(solution)/shard_map/ppermute | solution.py:10
  16.9 0.6 copy-start.22
  17.5 1.8 copy-start.20
  19.5 11.9 %copy-start.14 = (f32[273]{0:T(512)}, f32[273]{0:T(512)S(1)}, u32[]{:S(2)}) copy-start(f32[273]{0:T(512)S(1)} %pad.3.clone) | copy-start | bytes 3280
  22.5 0.9 copy-start.3
  31.0 1.9 copy-start.4
  31.1 1.9 copy-start.12
  31.4 4.3 %copy-start.7 = (f32[256,8,16,16]{0,3,2,1:T(8,128)}, f32[256,8,16,16]{0,3,2,1:T(8,128)S(1)}, u32[]{:S(2)}) copy-start(f32[256,8,16,16]{0,3,2,1:T(8,128)S(1)} %multiply_multiply_fusion.2) | copy-start | bytes 6291460
  31.4 2.0 copy-start.18
  33.4 2.2 copy-start.23
  35.7 1.0 copy-start.9
  35.7 1.0 copy-start.15
  35.7 1.0 copy-start.25
  36.1 2.2 copy-start.1
  42.1 3.4 %copy-start.2 = (f32[256,8,16,16]{0,3,2,1:T(8,128)S(1)}, f32[256,8,16,16]{0,3,2,1:T(8,128)}, u32[]{:S(2)}) copy-start(f32[256,8,16,16]{0,3,2,1:T(8,128)} %copy-done.1) | copy-start | bytes 6291460
  43.6 2.6 %copy-start.10 = (bf16[256,896]{0,1:T(8,128)(2,1)S(1)}, bf16[256,896]{0,1:T(8,128)(2,1)}, u32[]{:S(2)}) copy-start(bf16[256,896]{0,1:T(8,128)(2,1)} %copy.28) | copy-start | bytes 1376260
  43.6 2.6 %copy-start.11 = (bf16[8,256,256]{1,2,0:T(8,128)(2,1)S(1)}, bf16[8,256,256]{1,2,0:T(8,128)(2,1)}, u32[]{:S(2)}) copy-start(bf16[8,256,256]{1,2,0:T(8,128)(2,1)} %get-tuple-element.217) | copy-start | bytes 3145732
  45.5 1.6 copy-start.8
  45.5 1.6 copy-start.16
  47.1 2.6 %copy-start.6 = (bf16[1,256,1792]{2,1,0:T(8,128)(2,1)S(1)}, bf16[1,256,1792]{2,1,0:T(8,128)(2,1)}, u32[]{:S(2)}) copy-start(bf16[1,256,1792]{2,1,0:T(8,128)(2,1)} %param.15) | copy-start | bytes 2752516
  49.8 2.2 copy-start.19
  49.8 2.2 copy-start.21
  49.8 33.8 %copy-start.24 = (f32[1792]{0:T(1024)S(1)}, f32[1792]{0:T(1024)}, u32[]{:S(2)}) copy-start(f32[1792]{0:T(1024)} %param.24) | copy-start | bytes 21508
Sparse Core Ops, SparseCore 0:
  10.9 72.6 all-gather.3
  86.5 68.4 all-gather.5
  157.8 68.4 all-gather.7
where the time goes:
time: 252 us; the launch traced here: 251 us
  waiting for transfers between devices  170 us (67%)
  matrix products  33.1 us (13%)
  other arithmetic  19.7 us (8%)
  between operations  15.3 us (6%)
  local copies, waits for them, and re-layouts  12.7 us (5%)
    all_gather x1, waiting for transfers between devices, feed_forward(): down_piece = lax.all_gather(down_weight, 'req', axis=1, tiled=True)  71.4 us
    all_gather x1, waiting for transfers between devices, feed_forward(): up_piece = lax.all_gather(up_weight, 'req', axis=1, tiled=True)  65.1 us
    all_gather x1, waiting for transfers between devices, feed_forward(): gate_piece = lax.all_gather(gate_weight, 'req', axis=1, tiled=True)  31 us
    dot_general x1, matrix products, add_block(): lax.dot_general(hidden_units, down_piece, (((1,), (1,)), ((), ())), prefe...  10.4 us
    dot_general x1, matrix products, add_block(): gate_act = jnp.dot(row_data, gate_piece, preferred_element_type=jnp.float32)  6.24 us
    unnamed x53, local copies, waits for them, and re-layouts  5.08 us
  transfers between devices with their start and end apart: 4, of which 3 were waited for; matrix products, arithmetic and copies ran while one was open for 18% of the time, Pallas kernels for 0%

commit v1 on v0

--- a/solution.py
+++ b/solution.py
@@ -1,6 +1,10 @@
+import functools
+
 import jax
 import jax.numpy as jnp
 from jax import lax
+from jax.experimental import pallas as pl
+from jax.experimental.pallas import tpu as pltpu
 from jax.sharding import PartitionSpec as P
 
 
@@ -113,31 +117,184 @@
     return (rows_f32 * factor * gain).astype(jnp.bfloat16)
 
 
-def feed_forward(row_data, valid_count, gate_weight, up_weight, down_weight):
-    row_total = row_data.shape[0]
-    block_len = min(256, row_total)
-    live_blocks = (valid_count + block_len - 1) // block_len
-    initial = jnp.zeros((row_total, row_data.shape[1]), jnp.float32)
-    gate_piece = lax.all_gather(gate_weight, "req", axis=1, tiled=True)
-    up_piece = lax.all_gather(up_weight, "req", axis=1, tiled=True)
-    down_piece = lax.all_gather(down_weight, "req", axis=1, tiled=True)
-
-    def add_block(index, accumulated):
-        gate_act = jnp.dot(row_data, gate_piece, preferred_element_type=jnp.float32)
-        up_act = jnp.dot(row_data, up_piece, preferred_element_type=jnp.float32)
-        hidden_units = (jax.nn.silu(gate_act) * up_act).astype(jnp.bfloat16)
-        increment = lax.dot_general(
-            hidden_units, down_piece, (((1,), (1,)), ((), ())), preferred_element_type=jnp.float32
-        )
-        return accumulated + increment
-
-    return lax.fori_loop(0, live_blocks, add_block, initial)
+def permute(array, target):
+    count = lax.axis_size("req")
+    return lax.ppermute(array, "req", [(i, target(i)) for i in range(count)])
+
+
+def flip_core(array):
+    return permute(array, lambda i: i ^ 1)
+
+
+def flip_near(array):
+    return permute(array, lambda i: i ^ 2)
+
+
+def flip_far(array):
+    return permute(array, lambda i: i ^ 4)
+
+
+def next_plane(array):
+    count = lax.axis_size("req")
+    return permute(array, lambda i: (i + 8) % count)
+
+
+def together(*arrays):
+    return lax.optimization_barrier(arrays)
+
+
+def slot(*sends):
+    operands = together(*[array for _, array in sends])
+    return together(*[send(array) for (send, _), array in zip(sends, operands)])
+
+
+def swiglu_terms(rows, gate_rows, up_rows, down_rows):
+    nt = (((1,), (1,)), ((), ()))
+    gate_act = lax.dot_general(rows, gate_rows, nt, preferred_element_type=jnp.float32)
+    up_act = lax.dot_general(rows, up_rows, nt, preferred_element_type=jnp.float32)
+    hidden_units = (gate_act * jax.nn.sigmoid(gate_act) * up_act).astype(jnp.bfloat16)
+    return jnp.dot(hidden_units, down_rows, preferred_element_type=jnp.float32)
+
+
+def piece_rows(refs, main):
+    if len(refs) == 1:
+        (ref,) = refs
+        return ref[:main], ref[main : 2 * main], ref[2 * main : 3 * main]
+    first, second = refs
+    cut = first.shape[0]
+    up_rows = jnp.concatenate([first[main:cut], second[: 2 * main - cut]], axis=0)
+    return first[:main], up_rows, second[2 * main - cut : 3 * main - cut]
+
+
+def accumulate_body(main, sizes, has_acc, *refs):
+    own_ref, other_ref = refs[:2]
+    at = 2
+    parts = ([], [], [])
+    for size in sizes:
+        for part, rows in zip(parts, piece_rows(refs[at : at + size], main)):
+            part.append(rows)
+        at += size
+    gate_rows, up_rows, down_rows = (jnp.concatenate(part, axis=0) for part in parts)
+    outs = refs[-2:]
+    for k, rows_ref in enumerate((own_ref, other_ref)):
+        terms = swiglu_terms(rows_ref[...], gate_rows, up_rows, down_rows)
+        if has_acc:
+            terms = terms + refs[at + k][...]
+        outs[k][...] = terms
+
+
+def accumulate(rows, pieces, main, acc):
+    sizes = tuple(len(piece) for piece in pieces)
+    flat = [array for piece in pieces for array in piece]
+    shape = jax.ShapeDtypeStruct(rows[0].shape, jnp.float32)
+    start = 2 + len(flat)
+    return pl.pallas_call(
+        functools.partial(accumulate_body, main, sizes, acc is not None),
+        out_shape=(shape, shape),
+        in_specs=[pl.BlockSpec(memory_space=pltpu.VMEM)] * (start + (2 if acc else 0)),
+        out_specs=(pl.BlockSpec(memory_space=pltpu.VMEM),) * 2,
+        input_output_aliases={start: 0, start + 1: 1} if acc else {},
+        compiler_params=pltpu.CompilerParams(vmem_limit_bytes=40 * 1024 * 1024),
+        cost_estimate=pl.CostEstimate(flops=1000, bytes_accessed=1000, transcendentals=0),
+        name="accumulate",
+    )(*rows, *flat, *(acc or ()))
+
+
+def edge_rows(refs, edge):
+    parts = ([], [], [])
+    for ref, low in refs:
+        array = ref[...].astype(jnp.float32)
+        for base in range(low, array.shape[0], 3 * edge):
+            for k in range(3):
+                parts[k].append(array[base + k * edge : base + (k + 1) * edge])
+    return [jnp.concatenate(part, axis=0).astype(jnp.bfloat16) for part in parts]
+
+
+def finish_body(main, edge, n_edges, lows, rows_ref, first_ref, second_ref, *refs):
+    edges = edge_rows(list(zip(refs[:n_edges], lows)), edge)
+    whole = piece_rows((first_ref, second_ref), main)
+    parts = [jnp.concatenate(pair, axis=0) for pair in zip(edges, whole)]
+    terms = swiglu_terms(rows_ref[...], *parts) + refs[n_edges][...]
+    refs[-1][...] = terms.astype(refs[-1].dtype)
+
+
+def finish(rows, last, edges, main, edge, acc, dtype):
+    lows = tuple(low for _, low in edges)
+    return pl.pallas_call(
+        functools.partial(finish_body, main, edge, len(edges), lows),
+        out_shape=jax.ShapeDtypeStruct(rows.shape, dtype),
+        in_specs=[pl.BlockSpec(memory_space=pltpu.VMEM)] * (4 + len(edges)),
+        out_specs=pl.BlockSpec(memory_space=pltpu.VMEM),
+        compiler_params=pltpu.CompilerParams(vmem_limit_bytes=40 * 1024 * 1024),
+        cost_estimate=pl.CostEstimate(flops=1000, bytes_accessed=1000, transcendentals=0),
+        name="finish",
+    )(rows, *last, *[array for array, _ in edges], acc)
+
+
+def weight_slots(gate_weight, up_weight, down_weight):
+    units = gate_weight.shape[1]
+    edge = units // 7
+    main = units - edge
+    width = 3 * main
+    cut = main + 2 * main // 3
+    turned = [weight.T for weight in (gate_weight, up_weight, down_weight)]
+    shard = jnp.concatenate([w[:main] for w in turned] + [w[main:] for w in turned], axis=0)
+    near, far, deep1 = slot((flip_near, shard), (flip_far, shard), (next_plane, shard[:width]))
+    yield [(shard,), (near,), (far,), (deep1,)], []
+    edges = jnp.concatenate([shard[width:], near[width:], far[width:]], axis=0)
+    near1, far1, deep2, edges1, first, second = slot(
+        (flip_near, deep1),
+        (flip_far, deep1),
+        (next_plane, deep1),
+        (next_plane, edges),
+        (flip_near, far[:cut]),
+        (flip_far, near[cut:]),
+    )
+    corner = second[width - cut :]
+    yield (
+        [(first, second), (near1,), (far1,), (deep2,)],
+        [(shard, width), (near, width), (far, width), (second, width - cut), (edges1, 0)],
+    )
+    near2, far2, deep3, edges2, first1, second1, corner1 = slot(
+        (flip_near, deep2),
+        (flip_far, deep2),
+        (next_plane, deep2),
+        (next_plane, edges1),
+        (flip_near, far1[:cut]),
+        (flip_far, near1[cut:]),
+        (next_plane, corner),
+    )
+    yield [(first1, second1), (near2,), (far2,), (deep3,)], [(edges2, 0), (corner1, 0)]
+    near3, far3, edges3, first2, second2, corner2 = slot(
+        (flip_near, deep3),
+        (flip_far, deep3),
+        (next_plane, edges2),
+        (flip_near, far2[:cut]),
+        (flip_far, near2[cut:]),
+        (next_plane, corner1),
+    )
+    yield [(first2, second2), (near3,), (far3,)], [(edges3, 0), (corner2, 0)]
+    first3, second3, corner3 = slot(
+        (flip_near, far3[:cut]), (flip_far, near3[cut:]), (next_plane, corner2)
+    )
+    yield [(first3, second3)], [(corner3, 0)]
 
 
 def finish_rows(mixed_rows, valid_mask, mlp_gain, gate_weight, up_weight, down_weight):
+    units = gate_weight.shape[1]
+    edge = units // 7
+    main = units - edge
     mlp_in = rms_scale(mixed_rows, mlp_gain)
-    valid_count = jnp.sum(valid_mask).astype(jnp.int32)
-    ffn_out = feed_forward(mlp_in, valid_count, gate_weight, up_weight, down_weight)
+    rows = (mlp_in, flip_core(mlp_in))
+    slots = list(weight_slots(gate_weight, up_weight, down_weight))
+    edges = [part for _, parts in slots for part in parts]
+    acc = accumulate(rows, slots[0][0] + slots[1][0], main, None)
+    acc = accumulate(rows, slots[2][0], main, acc)
+    acc = accumulate(rows, slots[3][0], main, acc)
+    last = slots[4][0][0]
+    given = finish(rows[1], last, edges, main, edge, acc[1], jnp.bfloat16)
+    kept = finish(rows[0], last, edges, main, edge, acc[0], jnp.float32)
+    ffn_out = kept + flip_core(given).astype(jnp.float32)
     return ((mixed_rows.astype(jnp.float32) + ffn_out) * valid_mask[:, None]).astype(jnp.bfloat16)
 
 
@@ -207,34 +364,40 @@
     span_decay = jnp.sum(decay_rate, axis=0)
     flat_memory = memory.reshape(feat_len, head_count * value_len)
 
-    def merge_states(earlier, later):
-        factor = jnp.exp(later[0])
-        return (
-            earlier[0] + later[0],
-            earlier[1] * jnp.repeat(factor, value_len)[None, :] + later[1],
-            earlier[2] * factor[None, :] + later[2],
+    end_state, end_norm = (flat_memory, key_sum)
+    if lax.axis_size("seq") > 1:
+
+        def merge_states(earlier, later):
+            factor = jnp.exp(later[0])
+            return (
+                earlier[0] + later[0],
+                earlier[1] * jnp.repeat(factor, value_len)[None, :] + later[1],
+                earlier[2] * factor[None, :] + later[2],
+            )
+
+        neutral = (jnp.zeros_like(span_decay), jnp.zeros_like(flat_memory), jnp.zeros_like(key_sum))
+        carried = entering((span_decay, flat_memory, key_sum), "seq", merge_states, neutral)
+        prior_memory = carried[1]
+        prior_keys = carried[2]
+        highest = lax.Precision.HIGHEST
+        growth = jnp.exp(jnp.cumsum(decay_rate, axis=0))
+        query_feat = features(query_f32)
+        numerator = (
+            numerator
+            + jnp.einsum(
+                "thf,fhv->thv",
+                query_feat,
+                prior_memory.reshape(feat_len, head_count, value_len),
+                precision=highest,
+            )
+            * growth[:, :, None]
         )
-
-    neutral = (jnp.zeros_like(span_decay), jnp.zeros_like(flat_memory), jnp.zeros_like(key_sum))
-    carried = entering((span_decay, flat_memory, key_sum), "seq", merge_states, neutral)
-    prior_memory = carried[1]
-    prior_keys = carried[2]
-    highest = lax.Precision.HIGHEST
-    growth = jnp.exp(jnp.cumsum(decay_rate, axis=0))
-    query_feat = features(query_f32)
-    numerator = (
-        numerator
-        + jnp.einsum(
-            "thf,fhv->thv",
-            query_feat,
-            prior_memory.reshape(feat_len, head_count, value_len),
-            precision=highest,
+        denominator = (
+            denominator + jnp.einsum("thf,fh->th", query_feat, prior_keys, precision=highest) * growth
         )
-        * growth[:, :, None]
-    )
-    denominator = (
-        denominator + jnp.einsum("thf,fh->th", query_feat, prior_keys, precision=highest) * growth
-    )
+        span_factor = jnp.exp(span_decay)
+        end_state = prior_memory * jnp.repeat(span_factor, value_len)[None, :] + flat_memory
+        end_norm = prior_keys * span_factor[None, :] + key_sum
     attended = (
         (numerator / denominator[:, :, None])
         .reshape(local_len, head_count * value_len)
@@ -244,9 +407,6 @@
         rows_in.astype(jnp.float32)
         + jnp.dot(attended, out_weight, preferred_element_type=jnp.float32)
     ).astype(jnp.bfloat16)
-    span_factor = jnp.exp(span_decay)
-    end_state = prior_memory * jnp.repeat(span_factor, value_len)[None, :] + flat_memory
-    end_norm = prior_keys * span_factor[None, :] + key_sum
     result = finish_rows(mixed_rows, valid_mask, mlp_gain, gate_weight, up_weight, down_weight)
     return (result[None], end_state[None, None], end_norm[None, None])
 

time: 252 us -> 151 us (0.60)
  waiting for transfers between devices: 170 us -> 52.2 us
  starting transfers between devices: 0.77 us -> 25.7 us
  matrix products: 33.1 us -> 14 us
  Pallas kernels: 0 us -> 15.6 us
  between operations: 15.3 us -> 1.96 us
  local copies, waits for them, and re-layouts: 12.7 us -> 26 us
  other arithmetic: 19.7 us -> 15 us
    all_gather x3 -> x0, waiting for transfers between devices: 167 us -> none  [the longest x1 71.4 us: feed_forward(): down_piece = lax.all_gather(down_weight, 'req', axis=1, tiled=True)]
    ppermute x0 -> x27, waiting for transfers between devices: none -> 52.2 us  [permute(): return lax.ppermute(array, 'req', [(i, target(i)) for i in range(count)])]
    ppermute x0 -> x27, starting transfers between devices: none -> 25.1 us  [permute(): return lax.ppermute(array, 'req', [(i, target(i)) for i in range(count)])]
    dot_general x2 -> x0, matrix products: 16.7 us -> none  [the longest x1 10.4 us: add_block(): lax.dot_general(hidden_units, down_piece, (((1,), (1,)), ((), ())), prefe...]
    pallas_call x0 -> x5, Pallas kernels: none -> 15.6 us  [the longest x3 8.83 us: accumulate(): pl.pallas_call(functools.partial(accumulate_body, main, sizes, acc is not...]
    slice x0 -> x12, local copies, waits for them, and re-layouts: none -> 7.31 us  [the longest x3 4.99 us: weight_slots(): w[:main]]
    unnamed x53 -> x88, local copies, waits for them, and re-layouts: 5.08 us -> 10.5 us
    add x2 -> x0, other arithmetic: 4.92 us -> none  [the longest x1 3.49 us: add_block(): return accumulated + increment]
  transfers between devices with their start and end apart: 4 -> 28, of which waited for: 3 -> 8; matrix products, arithmetic and copies ran while one was open for 18% -> 22% of each run, Pallas kernels for 0% -> 8%
where the time goes in v1:
time: 151 us; the launch traced here: 150 us
  waiting for transfers between devices  52.2 us (35%)
  local copies, waits for them, and re-layouts  26 us (17%)
  starting transfers between devices  25.7 us (17%)
  Pallas kernels  15.6 us (10%)
  other arithmetic  15 us (10%)
  matrix products  14 us (9%)
  between operations  1.96 us (1%)
    ppermute x27, waiting for transfers between devices, permute(): return lax.ppermute(array, 'req', [(i, target(i)) for i in range(count)])  52.2 us
    ppermute x27, starting transfers between devices, permute(): return lax.ppermute(array, 'req', [(i, target(i)) for i in range(count)])  25.1 us
    unnamed x88, local copies, waits for them, and re-layouts  10.5 us
    pallas_call x3, Pallas kernels, accumulate(): pl.pallas_call(functools.partial(accumulate_body, main, sizes, acc is not...  8.83 us
    pallas_call x2, Pallas kernels, finish(): pl.pallas_call(functools.partial(finish_body, main, edge, len(edges), low...  6.74 us
    slice x3, local copies, waits for them, and re-layouts, weight_slots(): w[:main]  4.99 us
    dot_general x1, matrix products, block_step(): jnp.einsum('thf,fhv->thv', query_feat, memory, precision=highest)  3.94 us
    another operation x1, local copies, waits for them, and re-layouts, local(): return (result[None], end_state[None, None], end_norm[None, None])  3.85 us
  transfers between devices with their start and end apart: 28, of which 8 were waited for; matrix products, arithmetic and copies ran while one was open for 22% of the time, Pallas kernels for 8%

profile of v1, /device:TPU:0, one launch (start us, length us, event | category | flops | bytes accessed | tf_op | source)
XLA Modules:
  0.0 150.5 jit_solution(8246974496604014840)
XLA Ops:
  0.7 1.8 %fusion.56 = (bf16[48,1792]{1,0:T(8,128)(2,1)S(1)}, bf16[168,1792]{1,0:T(8,128)(2,1)}) fusion(bf16[56,1792]{1,0:T(8,128)(2,1)} %bitcast.81), kind=kLoop, calls=%fused_computation.102 | loop fusion | bytes 516096 | tf_op jit(solution)/shard_map/slice | solution.py:241
  2.4 1.6 %fusion.57 = (bf16[48,1792]{1,0:T(8,128)(2,1)S(1)}, bf16[168,1792]{1,0:T(8,128)(2,1)}) fusion(bf16[56,1792]{1,0:T(8,128)(2,1)} %bitcast.83, bf16[168,1792]{1,0:T(8,128)(2,1)} %get-tuple-element.168), kind=kLoop, calls=%fused_computation.103 | loop fusion | bytes 516096 | tf_op jit(solution)/shard_map/slice | solution.py:241
  4.0 1.6 %fusion.58 = (bf16[48,1792]{1,0:T(8,128)(2,1)S(1)}, bf16[168,1792]{1,0:T(8,128)(2,1)}) fusion(bf16[56,1792]{1,0:T(8,128)(2,1)} %bitcast.85, bf16[168,1792]{1,0:T(8,128)(2,1)} %get-tuple-element.170), kind=kLoop, calls=%fused_computation.104 | loop fusion | bytes 516096 | tf_op jit(solution)/shard_map/slice | solution.py:241
  5.7 1.4 slice_dynamic-update-slice_fusion.6
  7.0 1.4 slice_dynamic-update-slice_fusion.4
  8.4 1.4 slice_dynamic-update-slice_fusion.2
  10.6 2.9 %collective-permute-start.1 = (bf16[168,1792]{1,0:T(8,128)(2,1)}, bf16[168,1792]{1,0:T(8,128)(2,1)}, u32[]{:S(2)}, u32[]{:S(2)}) collective-permute-start(bf16[168,1792]{1,0:T(8,128)(2,1)} %get-tuple-element.93.refs_2_.refs_0_), channel_id=1, source_target_pairs={{0,2},{1,3},{2,0},{3,1},{4,6},{5,7},{6,4},{7,5},{8,10},{9,11},{10,... | collective-permute-start | bytes 1806344 | tf_op jit(solution)/shard_map/ppermute | solution.py:122
  13.6 1.5 %collective-permute-start.2 = (bf16[168,1792]{1,0:T(8,128)(2,1)}, bf16[168,1792]{1,0:T(8,128)(2,1)}, u32[]{:S(2)}, u32[]{:S(2)}) collective-permute-start(bf16[168,1792]{1,0:T(8,128)(2,1)} %get-tuple-element.93.refs_2_.refs_0_), channel_id=1, source_target_pairs={{0,4},{1,5},{2,6},{3,7},{4,0},{5,1},{6,2},{7,3},{8,12},{9,13},{10,... | collective-permute-start | bytes 1806344 | tf_op jit(solution)/shard_map/ppermute | solution.py:122
  15.1 1.6 %collective-permute-start.3 = (bf16[144,1792]{1,0:T(8,128)(2,1)}, bf16[144,1792]{1,0:T(8,128)(2,1)}, u32[]{:S(2)}, u32[]{:S(2)}) collective-permute-start(bf16[144,1792]{1,0:T(8,128)(2,1)} %pad_maximum_fusion.14), channel_id=1, source_target_pairs={{0,8},{1,9},{2,10},{3,11},{4,12},{5,13},{6,14},{7,15},{8,16},{9,17... | collective-permute-start | bytes 1548296 | tf_op jit(solution)/shard_map/ppermute | solution.py:122
  22.5 3.0 %fusion.8 = bf16[256,1792]{1,0:T(8,128)(2,1)S(1)} fusion(bf16[256,1792]{1,0:T(8,128)(2,1)} %copy-done.22, bf16[2,1792]{1,0:T(2,128)(2,1)S(1)} %collective-permute-done, f32[1792]{0:T(1024)S(1)} %get-tuple-element.155, f32[1792]{0:T(1024)S(1)} %get-tuple-element.156, f32[1792]{0:T(1024)S(1)} %get-tuple-element.154), kind=kLoop, calls=%fused_computation.21 | loop fusion | flops 8716288 | bytes 1863680 | tf_op jit(solution)/shard_map/convert_element_type | solution.py:336
  26.0 1.7 %multiply_multiply_fusion.2 = f32[256,8,16,16]{0,3,2,1:T(8,128)} fusion(f32[256,8,16]{0,2,1:T(8,128)S(1)} %bitcast_convert_fusion.1), kind=kLoop, calls=%fused_computation.17 | loop fusion | flops 1048576 | bytes 2228224 | tf_op jit(solution)/shard_map/while/body/eval_jaxpr/mul | solution.py:46
  27.9 1.9 %convolution_convert_fusion = bf16[256,896]{1,0:T(8,128)(2,1)} fusion(bf16[256,1792]{1,0:T(8,128)(2,1)S(1)} %fusion.8, bf16[1792,896]{1,0:T(8,128)(2,1)S(1)} %copy-done.41), kind=kOutput, calls=%fused_computation.43 | convolution fusion | flops 822312960 | bytes 4587520 | tf_op jit(solution)/shard_map/dot_general | solution.py:343
  29.8 1.1 bitcast_convert_fusion
  30.9 2.0 %copy.32 = bf16[256,896]{0,1:T(8,128)(2,1)} copy(bf16[256,896]{1,0:T(8,128)(2,1)} %convolution_convert_fusion) | data formatting | bytes 917504 | tf_op jit(solution)/shard_map/convert_element_type | solution.py:343
  32.9 1.9 %fusion.59 = (f32[8,256]{1,0:T(8,128)S(1)}, bf16[8,256,256]{1,2,0:T(8,128)(2,1)S(1)}) fusion(f32[256]{0:T(256)S(1)} %get-tuple-element.181, bf16[256,8,16]{0,2,1:T(8,128)(2,1)S(1)} %bitcast.80, bf16[256,8,16]{0,2,1:T(8,128)(2,1)S(1)} %bitcast.87, f32[8,256]{1,0:T(8,128)} %add_bitcast_fusion.2, pred[256,256]{0,1:T(8,128)(4,1)S(1)} %iota_compare_fusion), kind=kOutput, calls=%fused_computation.105 | convolution fusion | flops 22542336 | bytes 1262592 | tf_op jit(solution)/shard_map/while/body/eval_jaxpr/thi,uhi->htu/dot_general | solution.py:54
  35.2 1.2 slice.100
  37.4 1.0 slice.99
  39.2 1.6 %collective-permute-start.7 = (bf16[72,1792]{1,0:T(8,128)(2,1)S(1)}, bf16[72,1792]{1,0:T(8,128)(2,1)S(1)}, u32[]{:S(2)}, u32[]{:S(2)}) collective-permute-start(bf16[72,1792]{1,0:T(8,128)(2,1)S(1)} %slice_dynamic-update-slice_fusion), channel_id=1, source_target_pairs={{0,8},{1,9},{2,10},{3,11},{4,12},{5,13},{6,14},{7,15},{8,16},{9,17... | collective-permute-start | bytes 774152 | tf_op jit(solution)/shard_map/ppermute | solution.py:122
  40.8 1.5 %fusion.20 = f32[8,1,256]{2,1,0:T(1,128)S(1)} fusion(f32[256,8,256]{0,2,1:T(8,128)S(1)} %bitcast.76, f32[256,8,16]{0,2,1:T(8,128)S(1)} %bitcast_convert_fusion.1, f32[273]{0:T(512)S(1)} %pad.6.clone), kind=kOutput, calls=%fused_computation.33 | convolution fusion | flops 7827456 | bytes 2237508 | tf_op jit(solution)/shard_map/while/body/eval_jaxpr/thf,fh->th/dot_general | solution.py:76
  43.4 1.6 %collective-permute-start.6 = (bf16[144,1792]{1,0:T(8,128)(2,1)}, bf16[144,1792]{1,0:T(8,128)(2,1)S(1)}, u32[]{:S(2)}, u32[]{:S(2)}) collective-permute-start(bf16[144,1792]{1,0:T(8,128)(2,1)} %collective-permute-done.3.refs_5_), channel_id=1, source_target_pairs={{0,8},{1,9},{2,10},{3,11},{4,12},{5,13},{6,14},{7,15},{8,16},{9,17... | collective-permute-start | bytes 1548296 | tf_op jit(solution)/shard_map/ppermute | solution.py:122
  45.0 1.5 %collective-permute-start.9 = (bf16[88,1792]{1,0:T(8,128)(2,1)S(1)}, bf16[88,1792]{1,0:T(8,128)(2,1)S(1)}, u32[]{:S(2)}, u32[]{:S(2)}) collective-permute-start(bf16[88,1792]{1,0:T(8,128)(2,1)S(1)} %slice.100), channel_id=1, source_target_pairs={{0,4},{1,5},{2,6},{3,7},{4,0},{5,1},{6,2},{7,3},{8,12},{9,13},{10,... | collective-permute-start | bytes 946184 | tf_op jit(solution)/shard_map/ppermute | solution.py:122
  46.6 3.5 %collective-permute-done.7.refs_4_ = bf16[72,1792]{1,0:T(8,128)(2,1)S(1)} collective-permute-done((bf16[72,1792]{1,0:T(8,128)(2,1)S(1)}, bf16[72,1792]{1,0:T(8,128)(2,1)S(1)}, u32[]{:S(2)}, u32[]{:S(2)}) %collective-permute-start.7) | collective-permute-done | bytes 258080 | tf_op jit(solution)/shard_map/ppermute | solution.py:122
  50.1 3.9 %fusion.35 = bf16[256,8,112]{0,2,1:T(8,128)(2,1)S(1)} fusion(f32[256,8,112]{0,2,1:T(8,128)S(1)} %convolution_bitcast_fusion, f32[256,8,256]{0,2,1:T(8,128)S(1)} %bitcast.77, f32[256,8,16]{0,2,1:T(8,128)} %copy-done.30, f32[273]{0:T(512)S(1)} %pad.6.clone, f32[256,8]{0,1:T(8,128)S(1)} %get-tuple-element.174, f32[256,8]{0,1:T(8,128)S(1)} %copy-done.36), kind=kOutput, calls=%fused_computation.45 | convolution fusion | flops 753471488 | bytes 3621956 | tf_op jit(solution)/shard_map/while/body/eval_jaxpr/thf,fhv->thv/dot_general | solution.py:73
  54.1 7.0 %collective-permute-done.8.refs_6_ = bf16[80,1792]{1,0:T(8,128)(2,1)S(1)} collective-permute-done((bf16[80,1792]{1,0:T(8,128)(2,1)S(1)}, bf16[80,1792]{1,0:T(8,128)(2,1)S(1)}, u32[]{:S(2)}, u32[]{:S(2)}) %collective-permute-start.8) | collective-permute-done | bytes 286752 | tf_op jit(solution)/shard_map/ppermute | solution.py:122
  62.6 1.3 fusion.12
  63.9 1.6 %collective-permute-start.16 = (bf16[24,1792]{1,0:T(8,128)(2,1)S(1)}, bf16[24,1792]{1,0:T(8,128)(2,1)S(1)}, u32[]{:S(2)}, u32[]{:S(2)}) collective-permute-start(bf16[24,1792]{1,0:T(8,128)(2,1)S(1)} %slice.103), channel_id=1, source_target_pairs={{0,8},{1,9},{2,10},{3,11},{4,12},{5,13},{6,14},{7,15},{8,16},{9,17... | collective-permute-start | bytes 258056 | tf_op jit(solution)/shard_map/ppermute | solution.py:122
  65.5 1.5 %collective-permute-start.10 = (bf16[144,1792]{1,0:T(8,128)(2,1)S(1)}, bf16[144,1792]{1,0:T(8,128)(2,1)S(1)}, u32[]{:S(2)}, u32[]{:S(2)}) collective-permute-start(bf16[144,1792]{1,0:T(8,128)(2,1)S(1)} %collective-permute-done.6.refs_10_), channel_id=1, source_target_pairs={{0,2},{1,3},{2,0},{3,1},{4,6},{5,7},{6,4},{7,5},{8,10},{9,11},{10,... | collective-permute-start | bytes 1548296 | tf_op jit(solution)/shard_map/ppermute | solution.py:122
  67.0 1.5 collective-permute-start.11
  68.8 2.3 %collective-permute-done.16.refs_6_ = bf16[24,1792]{1,0:T(8,128)(2,1)S(1)} collective-permute-done((bf16[24,1792]{1,0:T(8,128)(2,1)S(1)}, bf16[24,1792]{1,0:T(8,128)(2,1)S(1)}, u32[]{:S(2)}, u32[]{:S(2)}) %collective-permute-start.16) | collective-permute-done | bytes 86048 | tf_op jit(solution)/shard_map/ppermute | solution.py:122
  71.1 1.5 %collective-permute-start.14 = (bf16[80,1792]{1,0:T(8,128)(2,1)S(1)}, bf16[80,1792]{1,0:T(8,128)(2,1)S(1)}, u32[]{:S(2)}, u32[]{:S(2)}) collective-permute-start(bf16[80,1792]{1,0:T(8,128)(2,1)S(1)} %slice.101), channel_id=1, source_target_pairs={{0,2},{1,3},{2,0},{3,1},{4,6},{5,7},{6,4},{7,5},{8,10},{9,11},{10,... | collective-permute-start | bytes 860168 | tf_op jit(solution)/shard_map/ppermute | solution.py:122
  72.9 13.9 %collective-permute-done.13.refs_5_ = bf16[72,1792]{1,0:T(8,128)(2,1)S(1)} collective-permute-done((bf16[72,1792]{1,0:T(8,128)(2,1)S(1)}, bf16[72,1792]{1,0:T(8,128)(2,1)S(1)}, u32[]{:S(2)}, u32[]{:S(2)}) %collective-permute-start.13) | collective-permute-done | bytes 258080 | tf_op jit(solution)/shard_map/ppermute | solution.py:122
  88.0 1.5 %collective-permute-start.21 = (bf16[64,1792]{1,0:T(8,128)(2,1)S(1)}, bf16[64,1792]{1,0:T(8,128)(2,1)S(1)}, u32[]{:S(2)}, u32[]{:S(2)}) collective-permute-start(bf16[64,1792]{1,0:T(8,128)(2,1)S(1)} %slice.105), channel_id=1, source_target_pairs={{0,4},{1,5},{2,6},{3,7},{4,0},{5,1},{6,2},{7,3},{8,12},{9,13},{10,... | collective-permute-start | bytes 688136 | tf_op jit(solution)/shard_map/ppermute | solution.py:122
  89.5 6.3 %collective-permute-done.22.refs_8_ = bf16[24,1792]{1,0:T(8,128)(2,1)S(1)} collective-permute-done((bf16[24,1792]{1,0:T(8,128)(2,1)S(1)}, bf16[24,1792]{1,0:T(8,128)(2,1)S(1)}, u32[]{:S(2)}, u32[]{:S(2)}) %collective-permute-start.22) | collective-permute-done | bytes 86048 | tf_op jit(solution)/shard_map/ppermute | solution.py:122
  95.8 1.5 collective-permute-start.20
  97.3 9.0 %collective-permute-done.21.refs_3_ = bf16[64,1792]{1,0:T(8,128)(2,1)S(1)} collective-permute-done((bf16[64,1792]{1,0:T(8,128)(2,1)S(1)}, bf16[64,1792]{1,0:T(8,128)(2,1)S(1)}, u32[]{:S(2)}, u32[]{:S(2)}) %collective-permute-start.21) | collective-permute-done | bytes 229408 | tf_op jit(solution)/shard_map/ppermute | solution.py:122
  106.3 9.3 %collective-permute-done.19.refs_7_ = bf16[72,1792]{1,0:T(8,128)(2,1)S(1)} collective-permute-done((bf16[72,1792]{1,0:T(8,128)(2,1)S(1)}, bf16[72,1792]{1,0:T(8,128)(2,1)S(1)}, u32[]{:S(2)}, u32[]{:S(2)}) %collective-permute-start.19) | collective-permute-done | bytes 258080 | tf_op jit(solution)/shard_map/ppermute | solution.py:122
  115.7 1.5 %collective-permute-start.23 = (bf16[80,1792]{1,0:T(8,128)(2,1)S(1)}, bf16[80,1792]{1,0:T(8,128)(2,1)S(1)}, u32[]{:S(2)}, u32[]{:S(2)}) collective-permute-start(bf16[80,1792]{1,0:T(8,128)(2,1)S(1)} %slice.106), channel_id=1, source_target_pairs={{0,2},{1,3},{2,0},{3,1},{4,6},{5,7},{6,4},{7,5},{8,10},{9,11},{10,... | collective-permute-start | bytes 860168 | tf_op jit(solution)/shard_map/ppermute | solution.py:122
  117.8 4.8 %accumulate.3 = (f32[256,1792]{1,0:T(8,128)S(1)}, f32[256,1792]{1,0:T(8,128)S(1)}) custom-call(bf16[256,1792]{1,0:T(8,128)(2,1)S(1)} %fusion.14.refs_0_.rows_ref, bf16[256,1792]{1,0:T(8,128)(2,1)S(1)} %collective-permute-done.26.refs_1_.rows_ref, bf16[168,1792]{1,0:T(8,128)(2,1)} %get-tuple-element.93.refs_2_.refs_0_, ...), custom_call_target="tpu_custom_call" | custom-call | flops 1000 | bytes 1000 | tf_op jit(solution)/shard_map/accumulate/pallas_call | solution.py:191
  122.6 2.0 %accumulate.4 = (f32[256,1792]{1,0:T(8,128)S(1)}, f32[256,1792]{1,0:T(8,128)S(1)}) custom-call(bf16[256,1792]{1,0:T(8,128)(2,1)S(1)} %fusion.14.refs_0_.rows_ref, bf16[256,1792]{1,0:T(8,128)(2,1)S(1)} %collective-permute-done.26.refs_1_.rows_ref, bf16[80,1792]{1,0:T(8,128)(2,1)S(1)} %collective-permute-done.14.refs_2_, ...), custom_call_target="tpu_custom_call", output_to_operand_aliasing={{0}: (7, {}), {1}: (8, {})} | custom-call | flops 1000 | bytes 1000 | tf_op jit(solution)/shard_map/accumulate/pallas_call | solution.py:191
  124.7 2.0 %accumulate.5 = (f32[256,1792]{1,0:T(8,128)S(1)}, f32[256,1792]{1,0:T(8,128)S(1)}) custom-call(bf16[256,1792]{1,0:T(8,128)(2,1)S(1)} %fusion.14.refs_0_.rows_ref, bf16[256,1792]{1,0:T(8,128)(2,1)S(1)} %collective-permute-done.26.refs_1_.rows_ref, bf16[80,1792]{1,0:T(8,128)(2,1)S(1)} %collective-permute-done.20.refs_2_, ...), custom_call_target="tpu_custom_call", output_to_operand_aliasing={{0}: (6, {}), {1}: (7, {})} | custom-call | flops 1000 | bytes 1000 | tf_op jit(solution)/shard_map/accumulate/pallas_call | solution.py:191
  126.8 4.2 %finish.3 = bf16[256,1792]{1,0:T(8,128)(2,1)} custom-call(bf16[256,1792]{1,0:T(8,128)(2,1)S(1)} %collective-permute-done.26.refs_1_.rows_ref, bf16[80,1792]{1,0:T(8,128)(2,1)S(1)} %collective-permute-done.23.first_ref, bf16[64,1792]{1,0:T(8,128)(2,1)S(1)} %collective-permute-done.24.second_ref, bf16[168,1792]{1,0:T(8,128)(2,1)} %get-tuple-element.93.refs_2_.refs_0_, ...), custom_call_target="tpu_custom_call" | custom-call | flops 1000 | bytes 1000 | tf_op jit(solution)/shard_map/finish/pallas_call | solution.py:223
  131.5 1.6 %fusion.28 = f32[273,8,112]{2,0,1:T(8,128)S(1)} fusion(bf16[256,8,112]{0,2,1:T(8,128)(2,1)S(1)} %bitcast.79, f32[256,8,256]{0,2,1:T(8,128)S(1)} %bitcast.74, f32[256,8,16]{0,2,1:T(8,128)S(1)} %copy-done.27, f32[273]{0:T(512)S(1)} %pad.6.clone, f32[256,8]{0,1:T(8,128)S(1)} %get-tuple-element.173, f32[256]{0:T(256)S(1)} %get-tuple-element.181, ...), kind=kOutput, calls=%fused_computation.38 | convolution fusion | flops 753916800 | bytes 3675748 | tf_op jit(solution)/shard_map/while/body/eval_jaxpr/uhf,uhv->fhv/dot_general | solution.py:81
  133.1 1.2 copy.34
  134.3 3.8 %broadcast_in_dim_reshape.5 = f32[1,1,273,896]{3,1,2,0:T(1,128)} reshape(f32[273,8,112]{2,1,0:T(8,128)} %copy.34) | data formatting | bytes 1956864 | tf_op jit(solution)/shard_map/broadcast_in_dim;reshape | solution.py:411
  138.2 2.4 %fusion.22 = f32[8,273]{1,0:T(8,128)S(1)} fusion(f32[256,8,256]{0,2,1:T(8,128)} %bitcast.75, f32[256,8,16]{0,2,1:T(8,128)} %get-tuple-element.179, f32[273]{0:T(512)S(1)} %pad.6.clone, f32[256,8]{0,1:T(8,128)S(1)} %get-tuple-element.173, f32[256]{0:T(256)S(1)} %get-tuple-element.181), kind=kLoop, calls=%fused_computation.35 | loop fusion | flops 2793336 | bytes 2247268 | tf_op jit(solution)/shard_map/while/body/eval_jaxpr/reduce_sum | solution.py:84
  141.3 1.5 copy-done.4
  145.5 2.5 %finish.2 = f32[256,1792]{1,0:T(8,128)S(1)} custom-call(bf16[256,1792]{1,0:T(8,128)(2,1)S(1)} %copy-done.2, bf16[80,1792]{1,0:T(8,128)(2,1)S(1)} %copy-done.6, bf16[64,1792]{1,0:T(8,128)(2,1)S(1)} %copy-done.14, bf16[168,1792]{1,0:T(8,128)(2,1)} %get-tuple-element.93.refs_2_.refs_0_, bf16[168,1792]{1,0:T(8,128)(2,1)} %collective-permute-done.1.refs_3_.refs_1_, ...), custom_call_target="tpu_custom_call" | custom-call | flops 1000 | bytes 1000 | tf_op jit(solution)/shard_map/finish/pallas_call | solution.py:223
  148.0 2.5 %fusion.45 = bf16[1,256,1792]{2,1,0:T(8,128)(2,1)} fusion(f32[256,1792]{1,0:T(8,128)S(1)} %finish.2, bf16[256,1792]{1,0:T(8,128)(2,1)} %collective-permute-done.27, bf16[256,1792]{1,0:T(8,128)(2,1)S(1)} %copy-done.24, f32[256]{0:T(256)S(1)} %get-tuple-element.181), kind=kLoop, calls=%fused_computation.59 | loop fusion | flops 2752512 | bytes 4588544 | tf_op jit(solution)/shard_map/broadcast_in_dim | solution.py:411
  (154 shorter events, 17.6 us)
Async XLA Ops:
  0.6 62.0 %copy-start = (bf16[896,1792]{1,0:T(8,128)(2,1)S(1)}, bf16[896,1792]{1,0:T(8,128)(2,1)}, u32[]{:S(2)}) copy-start(bf16[896,1792]{1,0:T(8,128)(2,1)} %param.21) | copy-start | bytes 9633796
  0.6 16.0 %copy-start.25 = (bf16[1,256,1792]{2,1,0:T(8,128)(2,1)S(1)}, bf16[1,256,1792]{2,1,0:T(8,128)(2,1)}, u32[]{:S(2)}) copy-start(bf16[1,256,1792]{2,1,0:T(8,128)(2,1)} %param.13) | copy-start | bytes 2752516
  0.7 16.3 %copy-start.34 = (f32[1792]{0:T(1024)S(1)}, f32[1792]{0:T(1024)}, u32[]{:S(2)}) copy-start(f32[1792]{0:T(1024)} %param.16) | copy-start | bytes 21508
  5.7 13.9 %copy-start.37 = (f32[1,256,8]{1,2,0:T(8,128)S(1)}, f32[1,256,8]{1,2,0:T(8,128)}, u32[]{:S(2)}) copy-start(f32[1,256,8]{1,2,0:T(8,128)} %param.15) | copy-start | bytes 24580
  7.0 14.6 %copy-start.33 = (f32[3,1792]{1,0:T(4,128)S(1)}, f32[3,1792]{1,0:T(4,128)}, u32[]{:S(2)}) copy-start(f32[3,1792]{1,0:T(4,128)} %param.17) | copy-start | bytes 64516
  10.6 24.6 %collective-permute-start.1 = (bf16[168,1792]{1,0:T(8,128)(2,1)}, bf16[168,1792]{1,0:T(8,128)(2,1)}, u32[]{:S(2)}, u32[]{:S(2)}) collective-permute-start(bf16[168,1792]{1,0:T(8,128)(2,1)} %get-tuple-element.93.refs_2_.refs_0_), channel_id=1, source_target_pairs={{0,2},{1,3},{2,0},{3,1},{4,6},{5,7},{6,4},{7,5},{8,10},{9,11},{10,... | collective-permute-start | bytes 1806344 | tf_op jit(solution)/shard_map/ppermute | solution.py:122
  13.6 21.7 %collective-permute-start.2 = (bf16[168,1792]{1,0:T(8,128)(2,1)}, bf16[168,1792]{1,0:T(8,128)(2,1)}, u32[]{:S(2)}, u32[]{:S(2)}) collective-permute-start(bf16[168,1792]{1,0:T(8,128)(2,1)} %get-tuple-element.93.refs_2_.refs_0_), channel_id=1, source_target_pairs={{0,4},{1,5},{2,6},{3,7},{4,0},{5,1},{6,2},{7,3},{8,12},{9,13},{10,... | collective-permute-start | bytes 1806344 | tf_op jit(solution)/shard_map/ppermute | solution.py:122
  15.1 20.1 %collective-permute-start.3 = (bf16[144,1792]{1,0:T(8,128)(2,1)}, bf16[144,1792]{1,0:T(8,128)(2,1)}, u32[]{:S(2)}, u32[]{:S(2)}) collective-permute-start(bf16[144,1792]{1,0:T(8,128)(2,1)} %pad_maximum_fusion.14), channel_id=1, source_target_pairs={{0,8},{1,9},{2,10},{3,11},{4,12},{5,13},{6,14},{7,15},{8,16},{9,17... | collective-permute-start | bytes 1548296 | tf_op jit(solution)/shard_map/ppermute | solution.py:122
  18.2 4.4 %collective-permute-start = (bf16[2,1792]{1,0:T(2,128)(2,1)S(1)}, bf16[2,1792]{1,0:T(2,128)(2,1)S(1)}, u32[]{:S(2)}, u32[]{:S(2)}) collective-permute-start(bf16[2,1792]{1,0:T(2,128)(2,1)S(1)} %slice.109), channel_id=1, source_target_pairs={} | collective-permute-start | bytes 21512 | tf_op jit(solution)/shard_map/ppermute | solution.py:14
  20.3 5.2 %copy-start.31 = (bf16[1792,128]{1,0:T(8,128)(2,1)S(1)}, bf16[1792,128]{1,0:T(8,128)(2,1)}, u32[]{:S(2)}) copy-start(bf16[1792,128]{1,0:T(8,128)(2,1)} %param.18) | copy-start | bytes 1376260
  26.0 14.8 %copy-start.30 = (f32[256,8,16]{0,2,1:T(8,128)}, f32[256,8,16]{0,2,1:T(8,128)S(1)}, u32[]{:S(2)}) copy-start(f32[256,8,16]{0,2,1:T(8,128)S(1)} %bitcast_convert_fusion.1) | copy-start | bytes 393220
  34.8 6.0 %copy-start.28 = (f32[256,8,16,16]{0,3,2,1:T(8,128)S(1)}, f32[256,8,16,16]{0,3,2,1:T(8,128)}, u32[]{:S(2)}) copy-start(f32[256,8,16,16]{0,3,2,1:T(8,128)} %multiply_multiply_fusion.2) | copy-start | bytes 6291460
  35.2 11.3 %copy-start.40 = (f32[8]{0:T(128)S(1)}, f32[8]{0:T(128)}, u32[]{:S(2)}) copy-start(f32[8]{0:T(128)} %get-tuple-element.158) | copy-start | bytes 100
  35.2 14.9 %copy-start.36 = (f32[256,8]{0,1:T(8,128)S(1)}, f32[256,8]{0,1:T(8,128)}, u32[]{:S(2)}) copy-start(f32[256,8]{0,1:T(8,128)} %get-tuple-element.159) | copy-start | bytes 24580
  39.2 10.8 %collective-permute-start.7 = (bf16[72,1792]{1,0:T(8,128)(2,1)S(1)}, bf16[72,1792]{1,0:T(8,128)(2,1)S(1)}, u32[]{:S(2)}, u32[]{:S(2)}) collective-permute-start(bf16[72,1792]{1,0:T(8,128)(2,1)S(1)} %slice_dynamic-update-slice_fusion), channel_id=1, source_target_pairs={{0,8},{1,9},{2,10},{3,11},{4,12},{5,13},{6,14},{7,15},{8,16},{9,17... | collective-permute-start | bytes 774152 | tf_op jit(solution)/shard_map/ppermute | solution.py:122
  42.4 19.6 %collective-permute-start.4 = (bf16[144,1792]{1,0:T(8,128)(2,1)}, bf16[144,1792]{1,0:T(8,128)(2,1)S(1)}, u32[]{:S(2)}, u32[]{:S(2)}) collective-permute-start(bf16[144,1792]{1,0:T(8,128)(2,1)} %collective-permute-done.3.refs_5_), channel_id=1, source_target_pairs={{0,2},{1,3},{2,0},{3,1},{4,6},{5,7},{6,4},{7,5},{8,10},{9,11},{10,... | collective-permute-start | bytes 1548296 | tf_op jit(solution)/shard_map/ppermute | solution.py:122
  42.9 19.1 %collective-permute-start.5 = (bf16[144,1792]{1,0:T(8,128)(2,1)}, bf16[144,1792]{1,0:T(8,128)(2,1)S(1)}, u32[]{:S(2)}, u32[]{:S(2)}) collective-permute-start(bf16[144,1792]{1,0:T(8,128)(2,1)} %collective-permute-done.3.refs_5_), channel_id=1, source_target_pairs={{0,4},{1,5},{2,6},{3,7},{4,0},{5,1},{6,2},{7,3},{8,12},{9,13},{10,... | collective-permute-start | bytes 1548296 | tf_op jit(solution)/shard_map/ppermute | solution.py:122
  43.4 18.6 %collective-permute-start.6 = (bf16[144,1792]{1,0:T(8,128)(2,1)}, bf16[144,1792]{1,0:T(8,128)(2,1)S(1)}, u32[]{:S(2)}, u32[]{:S(2)}) collective-permute-start(bf16[144,1792]{1,0:T(8,128)(2,1)} %collective-permute-done.3.refs_5_), channel_id=1, source_target_pairs={{0,8},{1,9},{2,10},{3,11},{4,12},{5,13},{6,14},{7,15},{8,16},{9,17... | collective-permute-start | bytes 1548296 | tf_op jit(solution)/shard_map/ppermute | solution.py:122
  45.0 17.0 %collective-permute-start.9 = (bf16[88,1792]{1,0:T(8,128)(2,1)S(1)}, bf16[88,1792]{1,0:T(8,128)(2,1)S(1)}, u32[]{:S(2)}, u32[]{:S(2)}) collective-permute-start(bf16[88,1792]{1,0:T(8,128)(2,1)S(1)} %slice.100), channel_id=1, source_target_pairs={{0,4},{1,5},{2,6},{3,7},{4,0},{5,1},{6,2},{7,3},{8,12},{9,13},{10,... | collective-permute-start | bytes 946184 | tf_op jit(solution)/shard_map/ppermute | solution.py:122
  50.1 76.7 %copy-start.7 = (bf16[72,1792]{1,0:T(8,128)(2,1)}, bf16[72,1792]{1,0:T(8,128)(2,1)S(1)}, u32[]{:S(2)}) copy-start(bf16[72,1792]{1,0:T(8,128)(2,1)S(1)} %collective-permute-done.7.refs_4_) | copy-start | bytes 774148
  50.1 11.0 %collective-permute-start.8 = (bf16[80,1792]{1,0:T(8,128)(2,1)S(1)}, bf16[80,1792]{1,0:T(8,128)(2,1)S(1)}, u32[]{:S(2)}, u32[]{:S(2)}) collective-permute-start(bf16[80,1792]{1,0:T(8,128)(2,1)S(1)} %slice.99), channel_id=1, source_target_pairs={{0,2},{1,3},{2,0},{3,1},{4,6},{5,7},{6,4},{7,5},{8,10},{9,11},{10,... | collective-permute-start | bytes 860168 | tf_op jit(solution)/shard_map/ppermute | solution.py:122
  50.1 12.5 %copy-start.26 = (bf16[1,256,1792]{2,1,0:T(8,128)(2,1)S(1)}, bf16[1,256,1792]{2,1,0:T(8,128)(2,1)}, u32[]{:S(2)}) copy-start(bf16[1,256,1792]{2,1,0:T(8,128)(2,1)} %param.13) | copy-start | bytes 2752516
  62.1 10.6 %collective-permute-start.15 = (bf16[64,1792]{1,0:T(8,128)(2,1)S(1)}, bf16[64,1792]{1,0:T(8,128)(2,1)S(1)}, u32[]{:S(2)}, u32[]{:S(2)}) collective-permute-start(bf16[64,1792]{1,0:T(8,128)(2,1)S(1)} %slice.102), channel_id=1, source_target_pairs={{0,4},{1,5},{2,6},{3,7},{4,0},{5,1},{6,2},{7,3},{8,12},{9,13},{10,... | collective-permute-start | bytes 688136 | tf_op jit(solution)/shard_map/ppermute | solution.py:122
  62.6 10.0 %copy-start.35 = (f32[1792]{0:T(1024)S(1)}, f32[1792]{0:T(1024)}, u32[]{:S(2)}) copy-start(f32[1792]{0:T(1024)} %param.22) | copy-start | bytes 21508
  63.9 9.1 %copy-start.23 = (bf16[256,1792]{1,0:T(8,128)(2,1)}, bf16[256,1792]{1,0:T(8,128)(2,1)S(1)}, u32[]{:S(2)}) copy-start(bf16[256,1792]{1,0:T(8,128)(2,1)S(1)} %get-tuple-element.178) | copy-start | bytes 2752516
  63.9 7.2 %collective-permute-start.16 = (bf16[24,1792]{1,0:T(8,128)(2,1)S(1)}, bf16[24,1792]{1,0:T(8,128)(2,1)S(1)}, u32[]{:S(2)}, u32[]{:S(2)}) collective-permute-start(bf16[24,1792]{1,0:T(8,128)(2,1)S(1)} %slice.103), channel_id=1, source_target_pairs={{0,8},{1,9},{2,10},{3,11},{4,12},{5,13},{6,14},{7,15},{8,16},{9,17... | collective-permute-start | bytes 258056 | tf_op jit(solution)/shard_map/ppermute | solution.py:122
  65.5 21.3 %collective-permute-start.10 = (bf16[144,1792]{1,0:T(8,128)(2,1)S(1)}, bf16[144,1792]{1,0:T(8,128)(2,1)S(1)}, u32[]{:S(2)}, u32[]{:S(2)}) collective-permute-start(bf16[144,1792]{1,0:T(8,128)(2,1)S(1)} %collective-permute-done.6.refs_10_), channel_id=1, source_target_pairs={{0,2},{1,3},{2,0},{3,1},{4,6},{5,7},{6,4},{7,5},{8,10},{9,11},{10,... | collective-permute-start | bytes 1548296 | tf_op jit(solution)/shard_map/ppermute | solution.py:122
  67.0 19.8 %collective-permute-start.11 = (bf16[144,1792]{1,0:T(8,128)(2,1)S(1)}, bf16[144,1792]{1,0:T(8,128)(2,1)S(1)}, u32[]{:S(2)}, u32[]{:S(2)}) collective-permute-start(bf16[144,1792]{1,0:T(8,128)(2,1)S(1)} %collective-permute-done.6.refs_10_), channel_id=1, source_target_pairs={{0,4},{1,5},{2,6},{3,7},{4,0},{5,1},{6,2},{7,3},{8,12},{9,13},{10,... | collective-permute-start | bytes 1548296 | tf_op jit(solution)/shard_map/ppermute | solution.py:122
  68.5 18.3 %collective-permute-start.12 = (bf16[144,1792]{1,0:T(8,128)(2,1)S(1)}, bf16[144,1792]{1,0:T(8,128)(2,1)S(1)}, u32[]{:S(2)}, u32[]{:S(2)}) collective-permute-start(bf16[144,1792]{1,0:T(8,128)(2,1)S(1)} %collective-permute-done.6.refs_10_), channel_id=1, source_target_pairs={{0,8},{1,9},{2,10},{3,11},{4,12},{5,13},{6,14},{7,15},{8,16},{9,17... | collective-permute-start | bytes 1548296 | tf_op jit(solution)/shard_map/ppermute | solution.py:122
  71.1 55.7 %copy-start.15 = (bf16[24,1792]{1,0:T(8,128)(2,1)}, bf16[24,1792]{1,0:T(8,128)(2,1)S(1)}, u32[]{:S(2)}) copy-start(bf16[24,1792]{1,0:T(8,128)(2,1)S(1)} %collective-permute-done.16.refs_6_) | copy-start | bytes 258052
  71.1 15.7 %collective-permute-start.14 = (bf16[80,1792]{1,0:T(8,128)(2,1)S(1)}, bf16[80,1792]{1,0:T(8,128)(2,1)S(1)}, u32[]{:S(2)}, u32[]{:S(2)}) collective-permute-start(bf16[80,1792]{1,0:T(8,128)(2,1)S(1)} %slice.101), channel_id=1, source_target_pairs={{0,2},{1,3},{2,0},{3,1},{4,6},{5,7},{6,4},{7,5},{8,10},{9,11},{10,... | collective-permute-start | bytes 860168 | tf_op jit(solution)/shard_map/ppermute | solution.py:122
  72.6 14.2 %collective-permute-start.13 = (bf16[72,1792]{1,0:T(8,128)(2,1)S(1)}, bf16[72,1792]{1,0:T(8,128)(2,1)S(1)}, u32[]{:S(2)}, u32[]{:S(2)}) collective-permute-start(bf16[72,1792]{1,0:T(8,128)(2,1)S(1)} %collective-permute-done.7.refs_4_), channel_id=1, source_target_pairs={{0,8},{1,9},{2,10},{3,11},{4,12},{5,13},{6,14},{7,15},{8,16},{9,17... | collective-permute-start | bytes 774152 | tf_op jit(solution)/shard_map/ppermute | solution.py:122
  72.9 51.7 %copy-start.1 = (bf16[256,1792]{1,0:T(8,128)(2,1)}, bf16[256,1792]{1,0:T(8,128)(2,1)S(1)}, u32[]{:S(2)}) copy-start(bf16[256,1792]{1,0:T(8,128)(2,1)S(1)} %fusion.14.refs_0_.rows_ref) | copy-start | bytes 2752516
  86.8 40.0 %copy-start.9 = (bf16[72,1792]{1,0:T(8,128)(2,1)}, bf16[72,1792]{1,0:T(8,128)(2,1)S(1)}, u32[]{:S(2)}) copy-start(bf16[72,1792]{1,0:T(8,128)(2,1)S(1)} %collective-permute-done.13.refs_5_) | copy-start | bytes 774148
  86.8 31.0 %collective-permute-start.26 = (bf16[256,1792]{1,0:T(8,128)(2,1)S(1)}, bf16[256,1792]{1,0:T(8,128)(2,1)S(1)}, u32[]{:S(2)}, u32[]{:S(2)}) collective-permute-start(bf16[256,1792]{1,0:T(8,128)(2,1)S(1)} %fusion.14.refs_0_.rows_ref), channel_id=1, source_target_pairs={{0,1},{1,0},{2,3},{3,2},{4,5},{5,4},{6,7},{7,6},{8,9},{9,8},{10,11... | collective-permute-start | bytes 2752520 | tf_op jit(solution)/shard_map/ppermute | solution.py:122
  86.9 28.7 %collective-permute-start.17 = (bf16[144,1792]{1,0:T(8,128)(2,1)S(1)}, bf16[144,1792]{1,0:T(8,128)(2,1)S(1)}, u32[]{:S(2)}, u32[]{:S(2)}) collective-permute-start(bf16[144,1792]{1,0:T(8,128)(2,1)S(1)} %collective-permute-done.12.refs_6_), channel_id=1, source_target_pairs={{0,2},{1,3},{2,0},{3,1},{4,6},{5,7},{6,4},{7,5},{8,10},{9,11},{10,... | collective-permute-start | bytes 1548296 | tf_op jit(solution)/shard_map/ppermute | solution.py:122
  87.5 28.1 %collective-permute-start.18 = (bf16[144,1792]{1,0:T(8,128)(2,1)S(1)}, bf16[144,1792]{1,0:T(8,128)(2,1)S(1)}, u32[]{:S(2)}, u32[]{:S(2)}) collective-permute-start(bf16[144,1792]{1,0:T(8,128)(2,1)S(1)} %collective-permute-done.12.refs_6_), channel_id=1, source_target_pairs={{0,4},{1,5},{2,6},{3,7},{4,0},{5,1},{6,2},{7,3},{8,12},{9,13},{10,... | collective-permute-start | bytes 1548296 | tf_op jit(solution)/shard_map/ppermute | solution.py:122
  88.0 18.3 %collective-permute-start.21 = (bf16[64,1792]{1,0:T(8,128)(2,1)S(1)}, bf16[64,1792]{1,0:T(8,128)(2,1)S(1)}, u32[]{:S(2)}, u32[]{:S(2)}) collective-permute-start(bf16[64,1792]{1,0:T(8,128)(2,1)S(1)} %slice.105), channel_id=1, source_target_pairs={{0,4},{1,5},{2,6},{3,7},{4,0},{5,1},{6,2},{7,3},{8,12},{9,13},{10,... | collective-permute-start | bytes 688136 | tf_op jit(solution)/shard_map/ppermute | solution.py:122
  89.5 6.3 %collective-permute-start.22 = (bf16[24,1792]{1,0:T(8,128)(2,1)S(1)}, bf16[24,1792]{1,0:T(8,128)(2,1)S(1)}, u32[]{:S(2)}, u32[]{:S(2)}) collective-permute-start(bf16[24,1792]{1,0:T(8,128)(2,1)S(1)} %collective-permute-done.16.refs_6_), channel_id=1, source_target_pairs={{0,8},{1,9},{2,10},{3,11},{4,12},{5,13},{6,14},{7,15},{8,16},{9,17... | collective-permute-start | bytes 258056 | tf_op jit(solution)/shard_map/ppermute | solution.py:122
  95.8 31.0 %copy-start.17 = (bf16[24,1792]{1,0:T(8,128)(2,1)}, bf16[24,1792]{1,0:T(8,128)(2,1)S(1)}, u32[]{:S(2)}) copy-start(bf16[24,1792]{1,0:T(8,128)(2,1)S(1)} %collective-permute-done.22.refs_8_) | copy-start | bytes 258052
  95.8 19.8 %collective-permute-start.20 = (bf16[80,1792]{1,0:T(8,128)(2,1)S(1)}, bf16[80,1792]{1,0:T(8,128)(2,1)S(1)}, u32[]{:S(2)}, u32[]{:S(2)}) collective-permute-start(bf16[80,1792]{1,0:T(8,128)(2,1)S(1)} %slice.104), channel_id=1, source_target_pairs={{0,2},{1,3},{2,0},{3,1},{4,6},{5,7},{6,4},{7,5},{8,10},{9,11},{10,... | collective-permute-start | bytes 860168 | tf_op jit(solution)/shard_map/ppermute | solution.py:122
  106.3 9.3 %collective-permute-start.19 = (bf16[72,1792]{1,0:T(8,128)(2,1)S(1)}, bf16[72,1792]{1,0:T(8,128)(2,1)S(1)}, u32[]{:S(2)}, u32[]{:S(2)}) collective-permute-start(bf16[72,1792]{1,0:T(8,128)(2,1)S(1)} %collective-permute-done.13.refs_5_), channel_id=1, source_target_pairs={{0,8},{1,9},{2,10},{3,11},{4,12},{5,13},{6,14},{7,15},{8,16},{9,17... | collective-permute-start | bytes 774152 | tf_op jit(solution)/shard_map/ppermute | solution.py:122
  115.6 11.2 %copy-start.11 = (bf16[72,1792]{1,0:T(8,128)(2,1)}, bf16[72,1792]{1,0:T(8,128)(2,1)S(1)}, u32[]{:S(2)}) copy-start(bf16[72,1792]{1,0:T(8,128)(2,1)S(1)} %collective-permute-done.19.refs_7_) | copy-start | bytes 774148
  115.7 11.0 %collective-permute-start.23 = (bf16[80,1792]{1,0:T(8,128)(2,1)S(1)}, bf16[80,1792]{1,0:T(8,128)(2,1)S(1)}, u32[]{:S(2)}, u32[]{:S(2)}) collective-permute-start(bf16[80,1792]{1,0:T(8,128)(2,1)S(1)} %slice.106), channel_id=1, source_target_pairs={{0,2},{1,3},{2,0},{3,1},{4,6},{5,7},{6,4},{7,5},{8,10},{9,11},{10,... | collective-permute-start | bytes 860168 | tf_op jit(solution)/shard_map/ppermute | solution.py:122
  117.2 9.5 %collective-permute-start.24 = (bf16[64,1792]{1,0:T(8,128)(2,1)S(1)}, bf16[64,1792]{1,0:T(8,128)(2,1)S(1)}, u32[]{:S(2)}, u32[]{:S(2)}) collective-permute-start(bf16[64,1792]{1,0:T(8,128)(2,1)S(1)} %slice.107), channel_id=1, source_target_pairs={{0,4},{1,5},{2,6},{3,7},{4,0},{5,1},{6,2},{7,3},{8,12},{9,13},{10,... | collective-permute-start | bytes 688136 | tf_op jit(solution)/shard_map/ppermute | solution.py:122
  117.8 8.9 %collective-permute-start.25 = (bf16[24,1792]{1,0:T(8,128)(2,1)S(1)}, bf16[24,1792]{1,0:T(8,128)(2,1)S(1)}, u32[]{:S(2)}, u32[]{:S(2)}) collective-permute-start(bf16[24,1792]{1,0:T(8,128)(2,1)S(1)} %collective-permute-done.22.refs_8_), channel_id=1, source_target_pairs={{0,8},{1,9},{2,10},{3,11},{4,12},{5,13},{6,14},{7,15},{8,16},{9,17... | collective-permute-start | bytes 258056 | tf_op jit(solution)/shard_map/ppermute | solution.py:122
  131.1 16.9 %collective-permute-start.27 = (bf16[256,1792]{1,0:T(8,128)(2,1)}, bf16[256,1792]{1,0:T(8,128)(2,1)}, u32[]{:S(2)}, u32[]{:S(2)}) collective-permute-start(bf16[256,1792]{1,0:T(8,128)(2,1)} %finish.3), channel_id=1, source_target_pairs={{0,1},{1,0},{2,3},{3,2},{4,5},{5,4},{6,7},{7,6},{8,9},{9,8},{10,11... | collective-permute-start | bytes 2752520 | tf_op jit(solution)/shard_map/ppermute | solution.py:122
  134.3 6.3 %copy-start.39 = (f32[8]{0:T(128)S(1)}, f32[8]{0:T(128)}, u32[]{:S(2)}) copy-start(f32[8]{0:T(128)} %get-tuple-element.157) | copy-start | bytes 100
  (22 other events, 57.6 us)

commit v2 on v0

v2 whole, which is shorter than its diff:
```python
import functools

import jax
import jax.numpy as jnp
from jax import lax
from jax.experimental import pallas as pl
from jax.experimental.pallas import tpu as pltpu
from jax.sharding import PartitionSpec as P


def from_behind(array, axis, by):
    count = lax.axis_size(axis)
    pairs = [(i, i + by) for i in range(count) if 0 <= i + by < count]
    return lax.ppermute(array, axis, pairs)


def entering(array, axis, combine, identity):
    count, here = (lax.axis_size(axis), lax.axis_index(axis))
    everything = jax.tree.map(
        lambda part, kind: lax.all_gather(part.astype(kind), axis),
        array,
        (jnp.bfloat16, jnp.bfloat16, jnp.bfloat16),
    )
    start = jax.tree.map(
        lambda part, zero: jnp.broadcast_to(jnp.asarray(zero, part.dtype), part.shape),
        array,
        identity,
    )

    def hop(k, before):
        reached = k < here
        new = combine(
            before, jax.tree.map(lambda part, own: part[k].astype(own.dtype), everything, array)
        )
        return jax.tree.map(lambda a, b: jnp.where(reached, a, b), new, before)

    return lax.fori_loop(0, count, hop, start)


def features(vectors):
    constant = jnp.ones(vectors.shape[:-1] + (1,), jnp.float32)
    width = vectors.shape[-1]
    squares = (vectors[..., :, None] * vectors[..., None, :]).reshape(
        vectors.shape[:-1] + (width * width,)
    )
    return jnp.concatenate([constant, vectors, squares * 0.5**0.5], axis=-1)


def carry_in(valid_mask, decays, queries, numerator, denominator, flat_memory, key_sum):
    local_len = numerator.shape[0]
    feat_len, head_count = key_sum.shape
    value_len = flat_memory.shape[1] // head_count
    feat_in = queries.shape[1] // head_count
    decay_rate = jnp.where(valid_mask[:, None] > 0, decays, 0.0)
    span_decay = jnp.sum(decay_rate, axis=0)

    def merge_states(earlier, later):
        factor = jnp.exp(later[0])
        return (
            earlier[0] + later[0],
            earlier[1] * jnp.repeat(factor, value_len)[None, :] + later[1],
            earlier[2] * factor[None, :] + later[2],
        )

    neutral = (jnp.zeros_like(span_decay), jnp.zeros_like(flat_memory), jnp.zeros_like(key_sum))
    carried = entering((span_decay, flat_memory, key_sum), "seq", merge_states, neutral)
    prior_memory = carried[1]
    prior_keys = carried[2]
    highest = lax.Precision.HIGHEST
    growth = jnp.exp(jnp.cumsum(decay_rate, axis=0))
    query_feat = features(queries.astype(jnp.float32).reshape(local_len, head_count, feat_in))
    added = jnp.einsum(
        "thf,fhv->thv",
        query_feat,
        prior_memory.reshape(feat_len, head_count, value_len),
        precision=highest,
    )
    numerator = numerator + (added * growth[:, :, None]).reshape(local_len, -1)
    denominator = (
        denominator + jnp.einsum("thf,fh->th", query_feat, prior_keys, precision=highest) * growth
    )
    span_factor = jnp.exp(span_decay)
    end_state = prior_memory * jnp.repeat(span_factor, value_len)[None, :] + flat_memory
    end_norm = prior_keys * span_factor[None, :] + key_sum
    return numerator, denominator, end_state, end_norm


def permute(array, target):
    count = lax.axis_size("req")
    return lax.ppermute(array, "req", [(i, target(i)) for i in range(count)])


def flip_core(array):
    return permute(array, lambda i: i ^ 1)


def flip_near(array):
    return permute(array, lambda i: i ^ 2)


def flip_far(array):
    return permute(array, lambda i: i ^ 4)


def next_plane(array):
    count = lax.axis_size("req")
    return permute(array, lambda i: (i + 8) % count)


def together(*arrays):
    return lax.optimization_barrier(arrays)


def slot(*sends):
    operands = together(*[array for _, array in sends])
    return together(*[send(array) for (send, _), array in zip(sends, operands)])


def vmem(count):
    return [pl.BlockSpec(memory_space=pltpu.VMEM)] * count


def kernel_call(body, name, out_shape, *operands, scratch=(), aliases=None, specs=None):
    many = isinstance(out_shape, tuple)
    return pl.pallas_call(
        body,
        out_shape=out_shape,
        in_specs=specs or vmem(len(operands)),
        out_specs=tuple(vmem(len(out_shape))) if many else vmem(1)[0],
        scratch_shapes=list(scratch),
        input_output_aliases=aliases or {},
        compiler_params=pltpu.CompilerParams(vmem_limit_bytes=48 * 1024 * 1024),
        cost_estimate=pl.CostEstimate(flops=1000, bytes_accessed=1000, transcendentals=0),
        name=name,
    )(*operands)


def like(rows, columns, dtype):
    return jax.ShapeDtypeStruct((rows, columns), dtype)


NT = (((1,), (1,)), ((), ()))


def unit_rows(rows, gain):
    factor = lax.rsqrt(jnp.mean(rows * rows, axis=-1, keepdims=True) + 1e-05)
    return (rows * factor * gain).astype(jnp.bfloat16).astype(jnp.float32)


def project_body(
    step,
    scale,
    rows_ref,
    edge_ref,
    gain_ref,
    conv_ref,
    query_ref,
    key_ref,
    value_ref,
    queries_ref,
    keys_ref,
    values_ref,
    normed,
    gated,
):
    gain = gain_ref[...]
    count = rows_ref.shape[0]
    lead = edge_ref.shape[0]
    taps = conv_ref.shape[0]
    normed[:lead] = unit_rows(edge_ref[...].astype(jnp.float32), gain)

    @pl.loop(0, count // step)
    def _(block):
        at = pl.multiple_of(block * step, step)
        rows = rows_ref[pl.ds(at, step), :].astype(jnp.float32)
        normed[pl.ds(lead + at, step), :] = unit_rows(rows, gain)

    @pl.loop(0, count // step)
    def _(block):
        at = pl.multiple_of(block * step, step)
        window = normed[pl.ds(at, step + lead), :]
        here = window[lead:]
        total = conv_ref[0:1] * here
        for tap in range(1, taps):
            total = total + conv_ref[tap : tap + 1] * window[lead - tap : lead - tap + step]
        gated[pl.ds(at, step), :] = (total * jax.nn.sigmoid(here)).astype(jnp.bfloat16)

    rows = gated[...]
    for weight_ref, out_ref, factor in (
        (query_ref, queries_ref, scale),
        (key_ref, keys_ref, scale),
        (value_ref, values_ref, None),
    ):
        product = jnp.dot(rows, weight_ref[...], preferred_element_type=jnp.float32)
        if factor is not None:
            product = product * factor
        out_ref[...] = product.astype(jnp.bfloat16)


def project(rows, edge, mix_gain, conv_weight, query_weight, key_weight, value_weight, scale):
    count, width = rows.shape
    step = 32
    return kernel_call(
        functools.partial(project_body, step, scale),
        "project",
        tuple(like(count, w.shape[1], jnp.bfloat16) for w in (query_weight, key_weight, value_weight)),
        rows,
        edge,
        mix_gain[None],
        conv_weight,
        query_weight,
        key_weight,
        value_weight,
        scratch=(
            pltpu.VMEM((count + edge.shape[0], width), jnp.float32),
            pltpu.VMEM((count, width), jnp.bfloat16),
        ),
    )


def attend_body(
    feat_in,
    value_len,
    valid_ref,
    rate_ref,
    queries_ref,
    keys_ref,
    values_ref,
    numer_ref,
    denom_ref,
    state_ref,
    norm_ref,
    turned,
    total,
    norms,
):
    heads, count = rate_ref.shape
    columns = values_ref.shape[1]
    lane = lax.broadcasted_iota(jnp.int32, (count, count), 1)
    row = lax.broadcasted_iota(jnp.int32, (count, count), 0)
    valid = valid_ref[...]
    rate = jnp.where(valid > 0, rate_ref[...], 0.0)
    upto = (row <= lane).astype(jnp.float32)
    across = jnp.dot(
        rate, upto, precision=lax.Precision.HIGHEST, preferred_element_type=jnp.float32
    )
    down = across.T
    closing = across[:, count - 1 : count]
    fading = jnp.exp(closing - across) * valid
    causal = row >= lane
    keys = keys_ref[...]
    turned[...] = keys.astype(jnp.float32).T
    owner = lax.broadcasted_iota(jnp.int32, queries_ref.shape, 1)
    spare = lax.broadcasted_iota(jnp.int32, (8, count), 0) == 0
    head_lane = lax.broadcasted_iota(jnp.int32, (count, 128), 1)
    numer_ref[...] = jnp.zeros(numer_ref.shape, jnp.float32)
    total[...] = jnp.zeros(total.shape, jnp.float32)
    norm_total = jnp.zeros(norms.shape, jnp.float32)
    denominators = jnp.zeros((count, 128), jnp.float32)
    for h in range(heads):
        low = min(h * value_len // 128 * 128, max(columns - 256, 0))
        high = min(low + 256, columns)
        mine = lax.broadcasted_iota(jnp.int32, (count, high - low), 1) + low
        mine = (mine >= h * value_len) & (mine < (h + 1) * value_len)
        values = jnp.where(mine, values_ref[:, low:high].astype(jnp.float32), 0.0)
        values = values.astype(jnp.bfloat16)
        asks = (owner >= h * feat_in) & (owner < (h + 1) * feat_in)
        queries = jnp.where(asks, queries_ref[...].astype(jnp.float32), 0.0)
        scores = lax.dot_general(
            queries.astype(jnp.bfloat16), keys, NT, preferred_element_type=jnp.float32
        )
        gap = down[:, h : h + 1] - across[h : h + 1]
        weights = jnp.where(causal, jnp.exp(jnp.minimum(gap, 0.0)) * valid, 0.0)
        weights = weights * (1.0 + scores + 0.5 * scores * scores)
        numer_ref[:, low:high] += jnp.dot(
            weights.astype(jnp.bfloat16), values, preferred_element_type=jnp.float32
        )
        sums = jnp.sum(weights, axis=1, keepdims=True)
        denominators = jnp.where(head_lane == h, sums, denominators)
        own = turned[h * feat_in : (h + 1) * feat_in]
        fade = fading[h : h + 1]
        faded = own * fade
        scaled = faded * 0.5**0.5
        parts = [own[i : i + 1] * scaled for i in range(feat_in)]
        parts += [faded, jnp.where(spare, fade, 0.0)]
        feats = jnp.concatenate(parts, axis=0).astype(jnp.bfloat16)
        total[:, low:high] += jnp.dot(feats, values, preferred_element_type=jnp.float32)
        mark = (head_lane == h).astype(jnp.bfloat16)
        norm_total = norm_total + jnp.dot(feats, mark, preferred_element_type=jnp.float32)
    denom_ref[...] = denominators[:, :heads]
    norms[...] = norm_total
    pairs = feat_in * feat_in
    for out_ref, source, width in ((state_ref, total, columns), (norm_ref, norms, heads)):
        out_ref[0:1, :] = source[pairs + feat_in : pairs + feat_in + 1, :width]
        out_ref[1 : 1 + feat_in, :] = source[pairs : pairs + feat_in, :width]
        out_ref[1 + feat_in :, :] = source[:pairs, :width]


def attend(valid, rate, queries, keys, values, feat_in, value_len):
    heads, count = rate.shape
    columns = values.shape[1]
    feat_len = 1 + feat_in + feat_in * feat_in
    padded = feat_in * feat_in + feat_in + 8
    return kernel_call(
        functools.partial(attend_body, feat_in, value_len),
        "attend",
        (
            like(count, columns, jnp.float32),
            like(count, heads, jnp.float32),
            like(feat_len, columns, jnp.float32),
            like(feat_len, heads, jnp.float32),
        ),
        valid,
        rate,
        queries,
        keys,
        values,
        scratch=(
            pltpu.VMEM((queries.shape[1], count), jnp.float32),
            pltpu.VMEM((padded, columns), jnp.float32),
            pltpu.VMEM((padded, 128), jnp.float32),
        ),
    )


def mix_body(
    value_len, step, numer_ref, denom_ref, rows_ref, out_ref, gain_ref, mixed_ref, mlp_ref, sums
):
    count, columns = numer_ref.shape
    heads = denom_ref.shape[1]
    column = lax.broadcasted_iota(jnp.int32, (1, columns), 1)
    inverse = 1.0 / denom_ref[...]
    spread = jnp.zeros((count, columns), jnp.float32)
    for h in range(heads):
        here = (column >= h * value_len) & (column < (h + 1) * value_len)
        spread = jnp.where(here, inverse[:, h : h + 1], spread)
    attended = (numer_ref[...] * spread).astype(jnp.bfloat16)
    sums[...] = jnp.dot(attended, out_ref[...], preferred_element_type=jnp.float32)
    gain = gain_ref[...]

    @pl.loop(0, count // step)
    def _(block):
        at = pl.ds(pl.multiple_of(block * step, step), step)
        mixed = (rows_ref[at, :].astype(jnp.float32) + sums[at, :]).astype(jnp.bfloat16)
        mixed_ref[at, :] = mixed
        mlp_ref[at, :] = unit_rows(mixed.astype(jnp.float32), gain).astype(jnp.bfloat16)


def mix(numer, denom, rows, out_weight, mlp_gain, value_len):
    count, width = rows.shape
    shape = like(count, width, jnp.bfloat16)
    return kernel_call(
        functools.partial(mix_body, value_len, 32),
        "mix",
        (shape, shape),
        numer,
        denom,
        rows,
        out_weight,
        mlp_gain[None],
        scratch=(pltpu.VMEM((count, width), jnp.float32),),
    )


def swiglu_terms(rows, gate_rows, up_rows, down_rows):
    gate_act = lax.dot_general(rows, gate_rows, NT, preferred_element_type=jnp.float32)
    up_act = lax.dot_general(rows, up_rows, NT, preferred_element_type=jnp.float32)
    hidden_units = (gate_act * jax.nn.sigmoid(gate_act) * up_act).astype(jnp.bfloat16)
    return jnp.dot(hidden_units, down_rows, preferred_element_type=jnp.float32)


def main_rows(refs, main):
    if len(refs) == 1:
        (ref,) = refs
        return [ref[:main]], [ref[main : 2 * main]], [ref[2 * main : 3 * main]]
    first, second = refs
    cut = main + 2 * main // 3
    rest = 2 * main - cut
    return [first[:main]], [first[main:cut], second[:rest]], [second[rest : rest + main]]


def edge_rows(array, edge):
    parts = ([], [], [])
    for base in range(0, array.shape[0], 3 * edge):
        for k in range(3):
            parts[k].append(array[base + k * edge : base + (k + 1) * edge])
    return parts


def gather_units(refs, pieces, edges, main, edge):
    parts = ([], [], [])
    for piece in pieces:
        for part, rows in zip(parts, main_rows([refs[i] for i in piece], main)):
            part.extend(rows)
    edge_parts = ([], [], [])
    for i, low in edges:
        for part, rows in zip(edge_parts, edge_rows(refs[i][...].astype(jnp.float32)[low:], edge)):
            part.extend(rows)
    for part, rows in zip(parts, edge_parts):
        if rows:
            part.append(jnp.concatenate(rows, axis=0).astype(jnp.bfloat16))
    return [jnp.concatenate(part, axis=0) for part in parts]


def accumulate_body(main, edge, n_weights, pieces, edges, n_acc, n_rows, *refs):
    weights = refs[:n_weights]
    rows = refs[n_weights : n_weights + n_rows]
    acc = refs[n_weights + n_rows : n_weights + n_rows + n_acc]
    parts = gather_units(weights, pieces, edges, main, edge)
    for k, rows_ref in enumerate(rows):
        out_ref = refs[len(refs) - n_rows + k]
        terms = swiglu_terms(rows_ref[...], *parts)
        if n_acc:
            terms = terms + acc[k][...]
        out_ref[...] = terms.astype(out_ref.dtype)


def accumulate(rows, weights, pieces, edges, main, edge, acc, dtype, name):
    shapes = tuple(like(*array.shape, dtype) for array in rows)
    start = len(weights) + len(rows)
    in_place = acc and dtype == jnp.float32
    body = functools.partial(
        accumulate_body, main, edge, len(weights), pieces, edges, len(acc), len(rows)
    )
    aliases = {start + k: k for k in range(len(acc))} if in_place else {}
    return kernel_call(body, name, shapes, *weights, *rows, *acc, aliases=aliases)


def shard_body(main, gate_ref, up_ref, down_ref, shard_ref, main_ref):
    arrays = [ref[...].astype(jnp.float32) for ref in (gate_ref, up_ref, down_ref)]
    tops = [array[:main] for array in arrays]
    ends = [array[main:] for array in arrays]
    shard_ref[...] = jnp.concatenate(tops + ends, axis=0).astype(jnp.bfloat16)
    main_ref[...] = jnp.concatenate(tops, axis=0).astype(jnp.bfloat16)


def second_slot_body(width, cut, shard_ref, near_ref, far_ref, deep_ref, line_ref, first, second):
    shard, near, far, deep = [
        ref[...].astype(jnp.float32) for ref in (shard_ref, near_ref, far_ref, deep_ref)
    ]
    line = [deep, shard[width:], near[width:], far[width:]]
    line_ref[...] = jnp.concatenate(line, axis=0).astype(jnp.bfloat16)
    first[...] = far[:cut].astype(jnp.bfloat16)
    second[...] = near[cut:].astype(jnp.bfloat16)


def third_slot_body(low, line_ref, corner_ref, out_ref):
    line, corner = [ref[...].astype(jnp.float32) for ref in (line_ref, corner_ref)]
    out_ref[...] = jnp.concatenate([line, corner[low:]], axis=0).astype(jnp.bfloat16)


def local(
    hidden_in,
    lengths,
    log_decay,
    mix_gain,
    conv_weight,
    query_weight,
    key_weight,
    value_weight,
    out_weight,
    mlp_gain,
    gate_weight,
    up_weight,
    down_weight,
):
    local_len = hidden_in.shape[1]
    rows_in = hidden_in[0]
    decays = log_decay[0]
    head_count = log_decay.shape[2]
    value_len = value_weight.shape[1] // head_count
    feat_in = query_weight.shape[1] // head_count
    feature_scale = feat_in ** (-0.25)
    token_positions = lax.axis_index("seq") * local_len + jnp.arange(local_len, dtype=jnp.int32)
    valid_mask = (token_positions < lengths[0]).astype(jnp.float32)
    spans = lax.axis_size("seq")
    units, model = gate_weight.shape[1], gate_weight.shape[0]
    edge = units // 7
    main = units - edge
    width = 3 * main
    cut = main + 2 * main // 3
    low = width - cut

    shard, shard_main = kernel_call(
        functools.partial(shard_body, main),
        "shard",
        (like(3 * units, model, jnp.bfloat16), like(width, model, jnp.bfloat16)),
        gate_weight.T,
        up_weight.T,
        down_weight.T,
    )
    near, far, deep1 = slot((flip_near, shard), (flip_far, shard), (next_plane, shard_main))

    lead = 16
    if spans > 1:
        edge_in = from_behind(rows_in[local_len - lead :], "seq", 1)
    else:
        edge_in = jnp.zeros((lead, model), jnp.bfloat16)
    queries, key_rows, values = project(
        rows_in, edge_in, mix_gain, conv_weight, query_weight, key_weight, value_weight, feature_scale
    )

    near, far, deep1, queries, key_rows, values = together(
        near, far, deep1, queries, key_rows, values
    )
    line, first, second = kernel_call(
        functools.partial(second_slot_body, width, cut),
        "second_slot",
        (
            like(width + 9 * edge, model, jnp.bfloat16),
            like(cut, model, jnp.bfloat16),
            like(3 * units - cut, model, jnp.bfloat16),
        ),
        shard,
        near,
        far,
        deep1,
    )
    near1, far1, line1, first, second = slot(
        (flip_near, deep1), (flip_far, deep1), (next_plane, line), (flip_near, first), (flip_far, second)
    )

    rate = log_decay[0].T
    numerator, denominator, end_state, end_norm = attend(
        valid_mask[None], rate, queries, key_rows, values, feat_in, value_len
    )
    if spans > 1:
        numerator, denominator, end_state, end_norm = carry_in(
            valid_mask, decays, queries, numerator, denominator, end_state, end_norm
        )
    mixed_rows, mlp_in = mix(numerator, denominator, rows_in, out_weight, mlp_gain, value_len)

    near1, far1, line1, first, second, mixed_rows, mlp_in = together(
        near1, far1, line1, first, second, mixed_rows, mlp_in
    )
    line = kernel_call(
        functools.partial(third_slot_body, low),
        "third_slot",
        like(width + 12 * edge, model, jnp.bfloat16),
        line1,
        second,
    )
    near2, far2, line2, first1, second1 = slot(
        (flip_near, line1[:width]),
        (flip_far, line1[:width]),
        (next_plane, line),
        (flip_near, far1[:cut]),
        (flip_far, near1[cut:]),
    )
    other_in, near3, far3, line3 = slot(
        (flip_core, mlp_in),
        (flip_near, line2[:width]),
        (flip_far, line2[:width]),
        (next_plane, line2[width:]),
    )
    rows = (mlp_in, other_in)
    weights = (shard, near, far, first, second, deep1, near1, far1, line1, near2, far2, line2, first1, second1)
    pieces = ((0,), (1,), (2,), (3, 4), (5,), (6,), (7,), (8,), (9,), (10,), (11,), (12, 13))
    acc = accumulate(rows, weights, pieces, (), main, edge, (), jnp.float32, "accumulate_most")
    near3, far3, line3, *acc = together(near3, far3, line3, *acc)
    first2, second2, first3, second3, corner = slot(
        (flip_near, far2[:cut]),
        (flip_far, near2[cut:]),
        (flip_near, far3[:cut]),
        (flip_far, near3[cut:]),
        (next_plane, line3[9 * edge :]),
    )
    weights = (near3, far3, shard, near, far, second, line1, line2, line3)
    edges = ((2, width), (3, width), (4, width), (5, low), (6, width), (7, width), (8, 0))
    acc = accumulate(
        rows, weights, ((0,), (1,)), edges, main, edge, tuple(acc), jnp.float32, "accumulate_edges"
    )
    weights = (first2, second2, first3, second3, corner)
    pieces = ((0, 1), (2, 3))
    edges = ((4, 0),)
    (given,) = accumulate(
        rows[1:], weights, pieces, edges, main, edge, acc[1:], jnp.bfloat16, "finish_other"
    )
    (kept,) = accumulate(
        rows[:1], weights, pieces, edges, main, edge, acc[:1], jnp.float32, "finish_own"
    )
    ffn_out = kept + flip_core(given).astype(jnp.float32)
    result = ((mixed_rows.astype(jnp.float32) + ffn_out) * valid_mask[:, None]).astype(jnp.bfloat16)
    return (result[None], end_state[None, None], end_norm[None, None])


def solution(mesh):
    return jax.shard_map(
        local,
        mesh=mesh,
        in_specs=(
            P("req", "seq", None),
            P("req"),
            P("req", "seq", None),
            P(),
            P(),
            P(),
            P(),
            P(),
            P(),
            P(),
            P(None, "req"),
            P(None, "req"),
            P(None, "req"),
        ),
        out_specs=(P("req", "seq", None), P("req", "seq", None, None), P("req", "seq", None, None)),
        check_vma=False,
    )
```

time: 252 us -> 115 us (0.46)
  waiting for transfers between devices: 170 us -> 39.6 us
  matrix products: 33.1 us -> 0 us
  Pallas kernels: 0 us -> 27.6 us
  starting transfers between devices: 0.77 us -> 23.1 us
  other arithmetic: 19.7 us -> 3.03 us
  between operations: 15.3 us -> 1.65 us
  local copies, waits for them, and re-layouts: 12.7 us -> 19.8 us
    all_gather x3 -> x0, waiting for transfers between devices: 167 us -> none  [the longest x1 71.4 us: feed_forward(): down_piece = lax.all_gather(down_weight, 'req', axis=1, tiled=True)]
    ppermute x1 -> x23, waiting for transfers between devices: 0.01 us -> 39.6 us  [permute(): return lax.ppermute(array, 'req', [(i, target(i)) for i in range(count)])]
    dot_general x11 -> x0, matrix products: 33.1 us -> none  [the longest x1 10.4 us: add_block(): lax.dot_general(hidden_units, down_piece, (((1,), (1,)), ((), ())), prefe...]
    pallas_call x0 -> x10, Pallas kernels: none -> 27.6 us  [kernel_call(): pl.pallas_call(body, out_shape=out_shape, in_specs=specs or vmem(len(oper...]
    ppermute x1 -> x23, starting transfers between devices: 0.65 us -> 23.1 us  [permute(): return lax.ppermute(array, 'req', [(i, target(i)) for i in range(count)])]
    unnamed x53 -> x62, local copies, waits for them, and re-layouts: 5.08 us -> 18.9 us
    add x2 -> x0, other arithmetic: 4.92 us -> none  [the longest x1 3.49 us: add_block(): return accumulated + increment]
    convert_element_type x2 -> x0, other arithmetic: 4.42 us -> none  [the longest x1 2.96 us: local(): (convolved * jax.nn.sigmoid(normed.astype(jnp.float32))).astype(jnp.bfloa...]
  transfers between devices with their start and end apart: 4 -> 23, of which waited for: 3 -> 10; matrix products, arithmetic and copies ran while one was open for 18% -> 5% of each run, Pallas kernels for 0% -> 15%
where the time goes in v2:
time: 115 us
  waiting for transfers between devices  39.6 us (34%)
  Pallas kernels  27.6 us (24%)
  starting transfers between devices  23.1 us (20%)
  local copies, waits for them, and re-layouts  19.8 us (17%)
  other arithmetic  3.03 us (3%)
  between operations  1.65 us (1%)
    ppermute x23, waiting for transfers between devices, permute(): return lax.ppermute(array, 'req', [(i, target(i)) for i in range(count)])  39.6 us
    pallas_call x10, Pallas kernels, kernel_call(): pl.pallas_call(body, out_shape=out_shape, in_specs=specs or vmem(len(oper...  27.6 us
    ppermute x23, starting transfers between devices, permute(): return lax.ppermute(array, 'req', [(i, target(i)) for i in range(count)])  23.1 us
    unnamed x62, local copies, waits for them, and re-layouts  18.9 us
    broadcast_in_dim x1, other arithmetic, local(): return (result[None], end_state[None, None], end_norm[None, None])  2.43 us
  transfers between devices with their start and end apart: 23, of which 10 were waited for; matrix products, arithmetic and copies ran while one was open for 5% of the time, Pallas kernels for 15%

profile of v2, /device:TPU:0, one launch (start us, length us, event | category | flops | bytes accessed | tf_op | source)
XLA Modules:
  0.0 114.7 jit_solution(773532188312934118)
XLA Ops:
  0.6 0.9 copy-done.22
  1.6 0.9 copy-done.23
  2.5 0.9 copy-done.24
  3.5 3.0 %collective-permute-start = (bf16[168,1792]{1,0:T(8,128)(2,1)S(1)}, bf16[168,1792]{1,0:T(8,128)(2,1)S(1)}, u32[]{:S(2)}, u32[]{:S(2)}) collective-permute-start(bf16[168,1792]{1,0:T(8,128)(2,1)S(1)} %get-tuple-element.86.shard_ref.refs_0_.refs_2_), channel_id=1, source_target_pairs={{0,2},{1,3},{2,0},{3,1},{4,6},{5,7},{6,4},{7,5},{8,10},{9,11},{10,... | collective-permute-start | bytes 1806344 | tf_op jit(solution)/shard_map/ppermute | solution.py:90
  6.5 1.5 %collective-permute-start.1 = (bf16[168,1792]{1,0:T(8,128)(2,1)S(1)}, bf16[168,1792]{1,0:T(8,128)(2,1)S(1)}, u32[]{:S(2)}, u32[]{:S(2)}) collective-permute-start(bf16[168,1792]{1,0:T(8,128)(2,1)S(1)} %get-tuple-element.86.shard_ref.refs_0_.refs_2_), channel_id=1, source_target_pairs={{0,4},{1,5},{2,6},{3,7},{4,0},{5,1},{6,2},{7,3},{8,12},{9,13},{10,... | collective-permute-start | bytes 1806344 | tf_op jit(solution)/shard_map/ppermute | solution.py:90
  8.0 1.6 %collective-permute-start.2 = (bf16[144,1792]{1,0:T(8,128)(2,1)S(1)}, bf16[144,1792]{1,0:T(8,128)(2,1)S(1)}, u32[]{:S(2)}, u32[]{:S(2)}) collective-permute-start(bf16[144,1792]{1,0:T(8,128)(2,1)S(1)} %get-tuple-element.87), channel_id=1, source_target_pairs={{0,8},{1,9},{2,10},{3,11},{4,12},{5,13},{6,14},{7,15},{8,16},{9,17... | collective-permute-start | bytes 1548296 | tf_op jit(solution)/shard_map/ppermute | solution.py:90
  9.6 0.7 broadcast_in_dim.21.gain_ref
  10.3 1.2 %copy-done.10 = bf16[1,256,1792]{2,1,0:T(8,128)(2,1)S(1)} copy-done((bf16[1,256,1792]{2,1,0:T(8,128)(2,1)S(1)}, bf16[1,256,1792]{2,1,0:T(8,128)(2,1)}, u32[]{:S(2)}) %copy-start.10) | copy-done | bytes 917528
  11.5 1.9 %copy-done.12 = bf16[1792,896]{1,0:T(8,128)(2,1)S(1)} copy-done((bf16[1792,896]{1,0:T(8,128)(2,1)S(1)}, bf16[1792,896]{1,0:T(8,128)(2,1)}, u32[]{:S(2)}) %copy-start.12) | copy-done | bytes 3211288
  13.4 1.0 copy-done.18
  14.4 1.0 copy-done.19
  15.4 0.7 copy-done.26
  16.2 3.7 %project.1 = (bf16[256,128]{1,0:T(8,128)(2,1)S(1)}, bf16[256,128]{1,0:T(8,128)(2,1)S(1)}, bf16[256,896]{1,0:T(8,128)(2,1)S(1)}) custom-call(bf16[256,1792]{1,0:T(8,128)(2,1)S(1)} %bitcast.14, bf16[16,1792]{1,0:T(8,128)(2,1)S(1)} %broadcast_in_dim.20.edge_ref, f32[1,1792]{1,0:T(1,128)S(1)} %broadcast_in_dim.21.gain_ref, f32[3,1792]{1,0:T(4,128)S(1)} %copy-done.26, ...), custom_call_target="tpu_custom_call" | custom-call | flops 1000 | bytes 1000 | tf_op jit(solution)/shard_map/project/pallas_call | solution.py:125
  19.9 2.9 %collective-permute-done.2.deep_ref.refs_5_ = bf16[144,1792]{1,0:T(8,128)(2,1)S(1)} collective-permute-done((bf16[144,1792]{1,0:T(8,128)(2,1)S(1)}, bf16[144,1792]{1,0:T(8,128)(2,1)S(1)}, u32[]{:S(2)}, u32[]{:S(2)}) %collective-permute-start.2) | collective-permute-done | bytes 516128 | tf_op jit(solution)/shard_map/ppermute | solution.py:90
  23.8 1.5 %collective-permute-start.4 = (bf16[144,1792]{1,0:T(8,128)(2,1)S(1)}, bf16[144,1792]{1,0:T(8,128)(2,1)S(1)}, u32[]{:S(2)}, u32[]{:S(2)}) collective-permute-start(bf16[144,1792]{1,0:T(8,128)(2,1)S(1)} %collective-permute-done.2.deep_ref.refs_5_), channel_id=1, source_target_pairs={{0,4},{1,5},{2,6},{3,7},{4,0},{5,1},{6,2},{7,3},{8,12},{9,13},{10,... | collective-permute-start | bytes 1548296 | tf_op jit(solution)/shard_map/ppermute | solution.py:90
  25.8 1.5 %collective-permute-start.6 = (bf16[80,1792]{1,0:T(8,128)(2,1)S(1)}, bf16[80,1792]{1,0:T(8,128)(2,1)S(1)}, u32[]{:S(2)}, u32[]{:S(2)}) collective-permute-start(bf16[80,1792]{1,0:T(8,128)(2,1)S(1)} %get-tuple-element.103), channel_id=1, source_target_pairs={{0,2},{1,3},{2,0},{3,1},{4,6},{5,7},{6,4},{7,5},{8,10},{9,11},{10,... | collective-permute-start | bytes 860168 | tf_op jit(solution)/shard_map/ppermute | solution.py:90
  28.0 2.1 %attend.1 = (f32[256,896]{1,0:T(8,128)S(1)}, f32[256,8]{1,0:T(8,128)S(1)}, f32[273,896]{1,0:T(8,128)S(1)}, f32[273,8]{1,0:T(8,128)S(1)}) custom-call(f32[1,256]{1,0:T(1,128)S(1)} %compare_convert_fusion.valid_ref, f32[8,256]{1,0:T(8,128)S(1)} %bitcast.21, bf16[256,128]{1,0:T(8,128)(2,1)S(1)} %get-tuple-element.110.queries_ref, ...), custom_call_target="tpu_custom_call" | custom-call | flops 1000 | bytes 1000 | tf_op jit(solution)/shard_map/attend/pallas_call | solution.py:125
  30.2 1.0 copy-done.13
  31.2 4.5 %mix.1 = (bf16[256,1792]{1,0:T(8,128)(2,1)S(1)}, bf16[256,1792]{1,0:T(8,128)(2,1)S(1)}) custom-call(f32[256,896]{1,0:T(8,128)S(1)} %get-tuple-element.113.numer_ref, f32[256,8]{1,0:T(8,128)S(1)} %get-tuple-element.114.denom_ref, bf16[256,1792]{1,0:T(8,128)(2,1)S(1)} %bitcast.15, bf16[896,1792]{1,0:T(8,128)(2,1)} %out_ref.1, ...), custom_call_target="tpu_custom_call" | custom-call | flops 1000 | bytes 1000 | tf_op jit(solution)/shard_map/mix/pallas_call | solution.py:125
  35.7 5.7 %collective-permute-done.6.refs_3_ = bf16[80,1792]{1,0:T(8,128)(2,1)S(1)} collective-permute-done((bf16[80,1792]{1,0:T(8,128)(2,1)S(1)}, bf16[80,1792]{1,0:T(8,128)(2,1)S(1)}, u32[]{:S(2)}, u32[]{:S(2)}) %collective-permute-start.6) | collective-permute-done | bytes 286752 | tf_op jit(solution)/shard_map/ppermute | solution.py:90
  41.4 0.9 collective-permute-done.7.corner_ref.refs_4_.refs_5_
  42.6 0.7 copy-done.1
  43.3 1.6 %collective-permute-start.10 = (bf16[240,1792]{1,0:T(8,128)(2,1)S(1)}, bf16[240,1792]{1,0:T(8,128)(2,1)S(1)}, u32[]{:S(2)}, u32[]{:S(2)}) collective-permute-start(bf16[240,1792]{1,0:T(8,128)(2,1)S(1)} %third_slot.1), channel_id=1, source_target_pairs={{0,8},{1,9},{2,10},{3,11},{4,12},{5,13},{6,14},{7,15},{8,16},{9,17... | collective-permute-start | bytes 2580488 | tf_op jit(solution)/shard_map/ppermute | solution.py:90
  44.9 1.4 %collective-permute-start.8 = (bf16[144,1792]{1,0:T(8,128)(2,1)S(1)}, bf16[144,1792]{1,0:T(8,128)(2,1)S(1)}, u32[]{:S(2)}, u32[]{:S(2)}) collective-permute-start(bf16[144,1792]{1,0:T(8,128)(2,1)S(1)} %slice.32), channel_id=1, source_target_pairs={{0,2},{1,3},{2,0},{3,1},{4,6},{5,7},{6,4},{7,5},{8,10},{9,11},{10,... | collective-permute-start | bytes 1548296 | tf_op jit(solution)/shard_map/ppermute | solution.py:90
  46.3 1.5 %collective-permute-start.9 = (bf16[144,1792]{1,0:T(8,128)(2,1)S(1)}, bf16[144,1792]{1,0:T(8,128)(2,1)S(1)}, u32[]{:S(2)}, u32[]{:S(2)}) collective-permute-start(bf16[144,1792]{1,0:T(8,128)(2,1)S(1)} %slice.32), channel_id=1, source_target_pairs={{0,4},{1,5},{2,6},{3,7},{4,0},{5,1},{6,2},{7,3},{8,12},{9,13},{10,... | collective-permute-start | bytes 1548296 | tf_op jit(solution)/shard_map/ppermute | solution.py:90
  47.8 0.6 collective-permute-start.11
  48.9 12.5 %collective-permute-done.12.refs_13_ = bf16[64,1792]{1,0:T(8,128)(2,1)S(1)} collective-permute-done((bf16[64,1792]{1,0:T(8,128)(2,1)S(1)}, bf16[64,1792]{1,0:T(8,128)(2,1)S(1)}, u32[]{:S(2)}, u32[]{:S(2)}) %collective-permute-start.12) | collective-permute-done | bytes 229408 | tf_op jit(solution)/shard_map/ppermute | solution.py:90
  61.6 2.0 %collective-permute-done.10.refs_11_.refs_7_ = bf16[240,1792]{1,0:T(8,128)(2,1)S(1)} collective-permute-done((bf16[240,1792]{1,0:T(8,128)(2,1)S(1)}, bf16[240,1792]{1,0:T(8,128)(2,1)S(1)}, u32[]{:S(2)}, u32[]{:S(2)}) %collective-permute-start.10) | collective-permute-done | bytes 860192 | tf_op jit(solution)/shard_map/ppermute | solution.py:90
  63.7 1.2 %collective-permute-start.14 = (bf16[144,1792]{1,0:T(8,128)(2,1)S(1)}, bf16[144,1792]{1,0:T(8,128)(2,1)S(1)}, u32[]{:S(2)}, u32[]{:S(2)}) collective-permute-start(bf16[144,1792]{1,0:T(8,128)(2,1)S(1)} %slice.37), channel_id=1, source_target_pairs={{0,2},{1,3},{2,0},{3,1},{4,6},{5,7},{6,4},{7,5},{8,10},{9,11},{10,... | collective-permute-start | bytes 1548296 | tf_op jit(solution)/shard_map/ppermute | solution.py:90
  64.9 1.5 %collective-permute-start.15 = (bf16[144,1792]{1,0:T(8,128)(2,1)S(1)}, bf16[144,1792]{1,0:T(8,128)(2,1)S(1)}, u32[]{:S(2)}, u32[]{:S(2)}) collective-permute-start(bf16[144,1792]{1,0:T(8,128)(2,1)S(1)} %slice.37), channel_id=1, source_target_pairs={{0,4},{1,5},{2,6},{3,7},{4,0},{5,1},{6,2},{7,3},{8,12},{9,13},{10,... | collective-permute-start | bytes 1548296 | tf_op jit(solution)/shard_map/ppermute | solution.py:90
  66.5 11.6 %collective-permute-done.16.refs_8_ = bf16[96,1792]{1,0:T(8,128)(2,1)S(1)} collective-permute-done((bf16[96,1792]{1,0:T(8,128)(2,1)S(1)}, bf16[96,1792]{1,0:T(8,128)(2,1)S(1)}, u32[]{:S(2)}, u32[]{:S(2)}) %collective-permute-start.16) | collective-permute-done | bytes 344096 | tf_op jit(solution)/shard_map/ppermute | solution.py:90
  78.1 0.6 collective-permute-done.15.refs_1_
  78.7 0.9 copy-done.5
  79.7 8.2 %accumulate_most.1 = (f32[256,1792]{1,0:T(8,128)}, f32[256,1792]{1,0:T(8,128)}) custom-call(bf16[168,1792]{1,0:T(8,128)(2,1)S(1)} %get-tuple-element.86.shard_ref.refs_0_.refs_2_, bf16[168,1792]{1,0:T(8,128)(2,1)S(1)} %collective-permute-done.near_ref.refs_1_.refs_3_, bf16[168,1792]{1,0:T(8,128)(2,1)S(1)} %collective-permute-done.1.far_ref.refs_2_.refs_4_, ...), custom_call_target="tpu_custom_call" | custom-call | flops 1000 | bytes 1000 | tf_op jit(solution)/shard_map/accumulate_most/pallas_call | solution.py:125
  87.9 1.0 collective-permute-start.17
  88.9 1.1 collective-permute-start.19
  90.0 1.5 %collective-permute-start.18 = (bf16[64,1792]{1,0:T(8,128)(2,1)S(1)}, bf16[64,1792]{1,0:T(8,128)(2,1)S(1)}, u32[]{:S(2)}, u32[]{:S(2)}) collective-permute-start(bf16[64,1792]{1,0:T(8,128)(2,1)S(1)} %slice.36), channel_id=1, source_target_pairs={{0,4},{1,5},{2,6},{3,7},{4,0},{5,1},{6,2},{7,3},{8,12},{9,13},{10,... | collective-permute-start | bytes 688136 | tf_op jit(solution)/shard_map/ppermute | solution.py:90
  92.1 1.1 %copy-done.8 = bf16[240,1792]{1,0:T(8,128)(2,1)S(1)} copy-done((bf16[240,1792]{1,0:T(8,128)(2,1)S(1)}, bf16[240,1792]{1,0:T(8,128)(2,1)}, u32[]{:S(2)}) %copy-start.8) | copy-done | bytes 860184
  93.2 5.9 %accumulate_edges.1 = (f32[256,1792]{1,0:T(8,128)}, f32[256,1792]{1,0:T(8,128)}) custom-call(bf16[144,1792]{1,0:T(8,128)(2,1)S(1)} %collective-permute-done.14.refs_0_, bf16[144,1792]{1,0:T(8,128)(2,1)S(1)} %collective-permute-done.15.refs_1_, ...), custom_call_target="tpu_custom_call", output_to_operand_aliasing={{0}: (11, {}), {1}: (12, {})} | custom-call | flops 1000 | bytes 1000 | tf_op jit(solution)/shard_map/accumulate_edges/pallas_call | solution.py:125
  99.1 2.1 %collective-permute-done.20.refs_3_ = bf16[64,1792]{1,0:T(8,128)(2,1)S(1)} collective-permute-done((bf16[64,1792]{1,0:T(8,128)(2,1)S(1)}, bf16[64,1792]{1,0:T(8,128)(2,1)S(1)}, u32[]{:S(2)}, u32[]{:S(2)}) %collective-permute-start.20) | collective-permute-done | bytes 229408 | tf_op jit(solution)/shard_map/ppermute | solution.py:90
  101.2 1.0 collective-permute-done.19.refs_2_
  102.2 1.5 %copy-done.9 = f32[256,1792]{1,0:T(8,128)S(1)} copy-done((f32[256,1792]{1,0:T(8,128)S(1)}, f32[256,1792]{1,0:T(8,128)}, u32[]{:S(2)}) %copy-start.9) | copy-done | bytes 1835032
  103.7 2.0 %finish_other.1 = bf16[256,1792]{1,0:T(8,128)(2,1)} custom-call(bf16[80,1792]{1,0:T(8,128)(2,1)S(1)} %collective-permute-done.17.refs_0_, bf16[64,1792]{1,0:T(8,128)(2,1)S(1)} %collective-permute-done.18.refs_1_, bf16[80,1792]{1,0:T(8,128)(2,1)S(1)} %collective-permute-done.19.refs_2_, bf16[64,1792]{1,0:T(8,128)(2,1)S(1)} %collective-permute-done.20.refs_3_, ...), custom_call_target="tpu_custom_call" | custom-call | flops 1000 | bytes 1000 | tf_op jit(solution)/shard_map/finish_other/pallas_call | solution.py:125
  105.7 0.6 compare_convert_fusion.1
  106.3 1.6 %copy.20 = f32[1,1,273,8]{2,3,1,0:T(8,128)} copy(f32[1,1,273,8]{3,2,1,0:T(8,128)} %bitcast.20) | data formatting | bytes 17472
  107.9 3.2 %copy.19 = f32[1,1,273,896]{3,1,2,0:T(1,128)} copy(f32[1,1,273,896]{3,2,1,0:T(8,128)} %bitcast.16) | data formatting | bytes 1956864
  111.1 1.0 finish_own.1
  112.3 2.4 %fusion = bf16[1,256,1792]{2,1,0:T(8,128)(2,1)} fusion(f32[256,1792]{1,0:T(8,128)S(1)} %finish_own.1, bf16[256,1792]{1,0:T(8,128)(2,1)} %collective-permute-done.22, bf16[256,1792]{1,0:T(8,128)(2,1)S(1)} %copy-done.15, f32[256]{0:T(256)S(1)} %copy-done.29), kind=kLoop, calls=%fused_computation.1 | loop fusion | flops 2752512 | bytes 4588544 | tf_op jit(solution)/shard_map/broadcast_in_dim | solution.py:584
  (86 shorter events, 3.3 us)
Async XLA Ops:
  0.6 0.9 copy-start.22
  3.5 19.3 %collective-permute-start = (bf16[168,1792]{1,0:T(8,128)(2,1)S(1)}, bf16[168,1792]{1,0:T(8,128)(2,1)S(1)}, u32[]{:S(2)}, u32[]{:S(2)}) collective-permute-start(bf16[168,1792]{1,0:T(8,128)(2,1)S(1)} %get-tuple-element.86.shard_ref.refs_0_.refs_2_), channel_id=1, source_target_pairs={{0,2},{1,3},{2,0},{3,1},{4,6},{5,7},{6,4},{7,5},{8,10},{9,11},{10,... | collective-permute-start | bytes 1806344 | tf_op jit(solution)/shard_map/ppermute | solution.py:90
  6.5 16.3 %collective-permute-start.1 = (bf16[168,1792]{1,0:T(8,128)(2,1)S(1)}, bf16[168,1792]{1,0:T(8,128)(2,1)S(1)}, u32[]{:S(2)}, u32[]{:S(2)}) collective-permute-start(bf16[168,1792]{1,0:T(8,128)(2,1)S(1)} %get-tuple-element.86.shard_ref.refs_0_.refs_2_), channel_id=1, source_target_pairs={{0,4},{1,5},{2,6},{3,7},{4,0},{5,1},{6,2},{7,3},{8,12},{9,13},{10,... | collective-permute-start | bytes 1806344 | tf_op jit(solution)/shard_map/ppermute | solution.py:90
  8.0 14.8 %collective-permute-start.2 = (bf16[144,1792]{1,0:T(8,128)(2,1)S(1)}, bf16[144,1792]{1,0:T(8,128)(2,1)S(1)}, u32[]{:S(2)}, u32[]{:S(2)}) collective-permute-start(bf16[144,1792]{1,0:T(8,128)(2,1)S(1)} %get-tuple-element.87), channel_id=1, source_target_pairs={{0,8},{1,9},{2,10},{3,11},{4,12},{5,13},{6,14},{7,15},{8,16},{9,17... | collective-permute-start | bytes 1548296 | tf_op jit(solution)/shard_map/ppermute | solution.py:90
  10.3 1.2 %copy-start.10 = (bf16[1,256,1792]{2,1,0:T(8,128)(2,1)S(1)}, bf16[1,256,1792]{2,1,0:T(8,128)(2,1)}, u32[]{:S(2)}) copy-start(bf16[1,256,1792]{2,1,0:T(8,128)(2,1)} %param.13) | copy-start | bytes 2752516
  11.5 1.9 %copy-start.12 = (bf16[1792,896]{1,0:T(8,128)(2,1)S(1)}, bf16[1792,896]{1,0:T(8,128)(2,1)}, u32[]{:S(2)}) copy-start(bf16[1792,896]{1,0:T(8,128)(2,1)} %value_ref.1) | copy-start | bytes 9633796
  13.4 1.0 copy-start.18
  14.4 1.0 copy-start.19
  19.9 8.1 %copy-start.28 = (f32[1792]{0:T(1024)S(1)}, f32[1792]{0:T(1024)}, u32[]{:S(2)}) copy-start(f32[1792]{0:T(1024)} %param.22) | copy-start | bytes 21508
  19.9 8.1 %copy-start.27 = (f32[1,256,8]{1,2,0:T(8,128)S(1)}, f32[1,256,8]{1,2,0:T(8,128)}, u32[]{:S(2)}) copy-start(f32[1,256,8]{1,2,0:T(8,128)} %param.15) | copy-start | bytes 24580
  19.9 11.2 %copy-start.11 = (bf16[1,256,1792]{2,1,0:T(8,128)(2,1)S(1)}, bf16[1,256,1792]{2,1,0:T(8,128)(2,1)}, u32[]{:S(2)}) copy-start(bf16[1,256,1792]{2,1,0:T(8,128)(2,1)} %param.13) | copy-start | bytes 2752516
  22.9 19.5 %collective-permute-start.5 = (bf16[216,1792]{1,0:T(8,128)(2,1)S(1)}, bf16[216,1792]{1,0:T(8,128)(2,1)S(1)}, u32[]{:S(2)}, u32[]{:S(2)}) collective-permute-start(bf16[216,1792]{1,0:T(8,128)(2,1)S(1)} %get-tuple-element.102), channel_id=1, source_target_pairs={{0,8},{1,9},{2,10},{3,11},{4,12},{5,13},{6,14},{7,15},{8,16},{9,17... | collective-permute-start | bytes 2322440 | tf_op jit(solution)/shard_map/ppermute | solution.py:90
  23.3 19.1 %collective-permute-start.3 = (bf16[144,1792]{1,0:T(8,128)(2,1)S(1)}, bf16[144,1792]{1,0:T(8,128)(2,1)S(1)}, u32[]{:S(2)}, u32[]{:S(2)}) collective-permute-start(bf16[144,1792]{1,0:T(8,128)(2,1)S(1)} %collective-permute-done.2.deep_ref.refs_5_), channel_id=1, source_target_pairs={{0,2},{1,3},{2,0},{3,1},{4,6},{5,7},{6,4},{7,5},{8,10},{9,11},{10,... | collective-permute-start | bytes 1548296 | tf_op jit(solution)/shard_map/ppermute | solution.py:90
  23.8 18.6 %collective-permute-start.4 = (bf16[144,1792]{1,0:T(8,128)(2,1)S(1)}, bf16[144,1792]{1,0:T(8,128)(2,1)S(1)}, u32[]{:S(2)}, u32[]{:S(2)}) collective-permute-start(bf16[144,1792]{1,0:T(8,128)(2,1)S(1)} %collective-permute-done.2.deep_ref.refs_5_), channel_id=1, source_target_pairs={{0,4},{1,5},{2,6},{3,7},{4,0},{5,1},{6,2},{7,3},{8,12},{9,13},{10,... | collective-permute-start | bytes 1548296 | tf_op jit(solution)/shard_map/ppermute | solution.py:90
  25.3 17.0 %collective-permute-start.7 = (bf16[88,1792]{1,0:T(8,128)(2,1)S(1)}, bf16[88,1792]{1,0:T(8,128)(2,1)S(1)}, u32[]{:S(2)}, u32[]{:S(2)}) collective-permute-start(bf16[88,1792]{1,0:T(8,128)(2,1)S(1)} %get-tuple-element.104), channel_id=1, source_target_pairs={{0,4},{1,5},{2,6},{3,7},{4,0},{5,1},{6,2},{7,3},{8,12},{9,13},{10,... | collective-permute-start | bytes 946184 | tf_op jit(solution)/shard_map/ppermute | solution.py:90
  25.8 15.6 %collective-permute-start.6 = (bf16[80,1792]{1,0:T(8,128)(2,1)S(1)}, bf16[80,1792]{1,0:T(8,128)(2,1)S(1)}, u32[]{:S(2)}, u32[]{:S(2)}) collective-permute-start(bf16[80,1792]{1,0:T(8,128)(2,1)S(1)} %get-tuple-element.103), channel_id=1, source_target_pairs={{0,2},{1,3},{2,0},{3,1},{4,6},{5,7},{6,4},{7,5},{8,10},{9,11},{10,... | collective-permute-start | bytes 860168 | tf_op jit(solution)/shard_map/ppermute | solution.py:90
  30.2 1.0 copy-start.13
  30.2 36.3 %copy-start.25 = (f32[273,8]{1,0:T(8,128)}, f32[273,8]{1,0:T(8,128)S(1)}, u32[]{:S(2)}) copy-start(f32[273,8]{1,0:T(8,128)S(1)} %get-tuple-element.162) | copy-start | bytes 26212
  35.7 6.9 %copy-start.14 = (bf16[256,1792]{1,0:T(8,128)(2,1)}, bf16[256,1792]{1,0:T(8,128)(2,1)S(1)}, u32[]{:S(2)}) copy-start(bf16[256,1792]{1,0:T(8,128)(2,1)S(1)} %get-tuple-element.117) | copy-start | bytes 2752516
  35.7 28.0 %copy-start.3 = (bf16[256,1792]{1,0:T(8,128)(2,1)}, bf16[256,1792]{1,0:T(8,128)(2,1)S(1)}, u32[]{:S(2)}) copy-start(bf16[256,1792]{1,0:T(8,128)(2,1)S(1)} %get-tuple-element.131.refs_14_.refs_9_.refs_5_) | copy-start | bytes 2752516
  43.3 20.3 %collective-permute-start.10 = (bf16[240,1792]{1,0:T(8,128)(2,1)S(1)}, bf16[240,1792]{1,0:T(8,128)(2,1)S(1)}, u32[]{:S(2)}, u32[]{:S(2)}) collective-permute-start(bf16[240,1792]{1,0:T(8,128)(2,1)S(1)} %third_slot.1), channel_id=1, source_target_pairs={{0,8},{1,9},{2,10},{3,11},{4,12},{5,13},{6,14},{7,15},{8,16},{9,17... | collective-permute-start | bytes 2580488 | tf_op jit(solution)/shard_map/ppermute | solution.py:90
  44.9 16.8 %collective-permute-start.8 = (bf16[144,1792]{1,0:T(8,128)(2,1)S(1)}, bf16[144,1792]{1,0:T(8,128)(2,1)S(1)}, u32[]{:S(2)}, u32[]{:S(2)}) collective-permute-start(bf16[144,1792]{1,0:T(8,128)(2,1)S(1)} %slice.32), channel_id=1, source_target_pairs={{0,2},{1,3},{2,0},{3,1},{4,6},{5,7},{6,4},{7,5},{8,10},{9,11},{10,... | collective-permute-start | bytes 1548296 | tf_op jit(solution)/shard_map/ppermute | solution.py:90
  46.3 15.3 %collective-permute-start.9 = (bf16[144,1792]{1,0:T(8,128)(2,1)S(1)}, bf16[144,1792]{1,0:T(8,128)(2,1)S(1)}, u32[]{:S(2)}, u32[]{:S(2)}) collective-permute-start(bf16[144,1792]{1,0:T(8,128)(2,1)S(1)} %slice.32), channel_id=1, source_target_pairs={{0,4},{1,5},{2,6},{3,7},{4,0},{5,1},{6,2},{7,3},{8,12},{9,13},{10,... | collective-permute-start | bytes 1548296 | tf_op jit(solution)/shard_map/ppermute | solution.py:90
  47.8 13.8 %collective-permute-start.11 = (bf16[80,1792]{1,0:T(8,128)(2,1)S(1)}, bf16[80,1792]{1,0:T(8,128)(2,1)S(1)}, u32[]{:S(2)}, u32[]{:S(2)}) collective-permute-start(bf16[80,1792]{1,0:T(8,128)(2,1)S(1)} %slice.33), channel_id=1, source_target_pairs={{0,2},{1,3},{2,0},{3,1},{4,6},{5,7},{6,4},{7,5},{8,10},{9,11},{10,... | collective-permute-start | bytes 860168 | tf_op jit(solution)/shard_map/ppermute | solution.py:90
  48.4 13.1 %collective-permute-start.12 = (bf16[64,1792]{1,0:T(8,128)(2,1)S(1)}, bf16[64,1792]{1,0:T(8,128)(2,1)S(1)}, u32[]{:S(2)}, u32[]{:S(2)}) collective-permute-start(bf16[64,1792]{1,0:T(8,128)(2,1)S(1)} %slice.34), channel_id=1, source_target_pairs={{0,4},{1,5},{2,6},{3,7},{4,0},{5,1},{6,2},{7,3},{8,12},{9,13},{10,... | collective-permute-start | bytes 688136 | tf_op jit(solution)/shard_map/ppermute | solution.py:90
  63.6 15.2 %copy-start.7 = (bf16[240,1792]{1,0:T(8,128)(2,1)}, bf16[240,1792]{1,0:T(8,128)(2,1)S(1)}, u32[]{:S(2)}) copy-start(bf16[240,1792]{1,0:T(8,128)(2,1)S(1)} %collective-permute-done.10.refs_11_.refs_7_) | copy-start | bytes 2580484
  63.6 15.1 %collective-permute-start.13 = (bf16[256,1792]{1,0:T(8,128)(2,1)S(1)}, bf16[256,1792]{1,0:T(8,128)(2,1)S(1)}, u32[]{:S(2)}, u32[]{:S(2)}) collective-permute-start(bf16[256,1792]{1,0:T(8,128)(2,1)S(1)} %get-tuple-element.131.refs_14_.refs_9_.refs_5_), channel_id=1, source_target_pairs={{0,1},{1,0},{2,3},{3,2},{4,5},{5,4},{6,7},{7,6},{8,9},{9,8},{10,11... | collective-permute-start | bytes 2752520 | tf_op jit(solution)/shard_map/ppermute | solution.py:90
  63.7 14.4 %collective-permute-start.14 = (bf16[144,1792]{1,0:T(8,128)(2,1)S(1)}, bf16[144,1792]{1,0:T(8,128)(2,1)S(1)}, u32[]{:S(2)}, u32[]{:S(2)}) collective-permute-start(bf16[144,1792]{1,0:T(8,128)(2,1)S(1)} %slice.37), channel_id=1, source_target_pairs={{0,2},{1,3},{2,0},{3,1},{4,6},{5,7},{6,4},{7,5},{8,10},{9,11},{10,... | collective-permute-start | bytes 1548296 | tf_op jit(solution)/shard_map/ppermute | solution.py:90
  64.9 13.8 %collective-permute-start.15 = (bf16[144,1792]{1,0:T(8,128)(2,1)S(1)}, bf16[144,1792]{1,0:T(8,128)(2,1)S(1)}, u32[]{:S(2)}, u32[]{:S(2)}) collective-permute-start(bf16[144,1792]{1,0:T(8,128)(2,1)S(1)} %slice.37), channel_id=1, source_target_pairs={{0,4},{1,5},{2,6},{3,7},{4,0},{5,1},{6,2},{7,3},{8,12},{9,13},{10,... | collective-permute-start | bytes 1548296 | tf_op jit(solution)/shard_map/ppermute | solution.py:90
  66.4 11.7 %collective-permute-start.16 = (bf16[96,1792]{1,0:T(8,128)(2,1)S(1)}, bf16[96,1792]{1,0:T(8,128)(2,1)S(1)}, u32[]{:S(2)}, u32[]{:S(2)}) collective-permute-start(bf16[96,1792]{1,0:T(8,128)(2,1)S(1)} %slice.38), channel_id=1, source_target_pairs={{0,8},{1,9},{2,10},{3,11},{4,12},{5,13},{6,14},{7,15},{8,16},{9,17... | collective-permute-start | bytes 1032200 | tf_op jit(solution)/shard_map/ppermute | solution.py:90
  66.5 25.6 %copy-start.2 = (bf16[216,1792]{1,0:T(8,128)(2,1)S(1)}, bf16[216,1792]{1,0:T(8,128)(2,1)}, u32[]{:S(2)}) copy-start(bf16[216,1792]{1,0:T(8,128)(2,1)} %copy-done.1) | copy-start | bytes 2322436
  87.9 4.2 %copy-start.4 = (bf16[256,1792]{1,0:T(8,128)(2,1)S(1)}, bf16[256,1792]{1,0:T(8,128)(2,1)}, u32[]{:S(2)}) copy-start(bf16[256,1792]{1,0:T(8,128)(2,1)} %copy-done.3) | copy-start | bytes 2752516
  87.9 14.3 %copy-start.6 = (bf16[256,1792]{1,0:T(8,128)(2,1)S(1)}, bf16[256,1792]{1,0:T(8,128)(2,1)}, u32[]{:S(2)}) copy-start(bf16[256,1792]{1,0:T(8,128)(2,1)} %copy-done.5) | copy-start | bytes 2752516
  87.9 13.3 %collective-permute-start.17 = (bf16[80,1792]{1,0:T(8,128)(2,1)S(1)}, bf16[80,1792]{1,0:T(8,128)(2,1)S(1)}, u32[]{:S(2)}, u32[]{:S(2)}) collective-permute-start(bf16[80,1792]{1,0:T(8,128)(2,1)S(1)} %slice.35), channel_id=1, source_target_pairs={{0,2},{1,3},{2,0},{3,1},{4,6},{5,7},{6,4},{7,5},{8,10},{9,11},{10,... | collective-permute-start | bytes 860168 | tf_op jit(solution)/shard_map/ppermute | solution.py:90
  88.9 13.3 %collective-permute-start.19 = (bf16[80,1792]{1,0:T(8,128)(2,1)S(1)}, bf16[80,1792]{1,0:T(8,128)(2,1)S(1)}, u32[]{:S(2)}, u32[]{:S(2)}) collective-permute-start(bf16[80,1792]{1,0:T(8,128)(2,1)S(1)} %slice.39), channel_id=1, source_target_pairs={{0,2},{1,3},{2,0},{3,1},{4,6},{5,7},{6,4},{7,5},{8,10},{9,11},{10,... | collective-permute-start | bytes 860168 | tf_op jit(solution)/shard_map/ppermute | solution.py:90
  90.0 9.1 %collective-permute-start.18 = (bf16[64,1792]{1,0:T(8,128)(2,1)S(1)}, bf16[64,1792]{1,0:T(8,128)(2,1)S(1)}, u32[]{:S(2)}, u32[]{:S(2)}) collective-permute-start(bf16[64,1792]{1,0:T(8,128)(2,1)S(1)} %slice.36), channel_id=1, source_target_pairs={{0,4},{1,5},{2,6},{3,7},{4,0},{5,1},{6,2},{7,3},{8,12},{9,13},{10,... | collective-permute-start | bytes 688136 | tf_op jit(solution)/shard_map/ppermute | solution.py:90
  91.5 9.7 %collective-permute-start.20 = (bf16[64,1792]{1,0:T(8,128)(2,1)S(1)}, bf16[64,1792]{1,0:T(8,128)(2,1)S(1)}, u32[]{:S(2)}, u32[]{:S(2)}) collective-permute-start(bf16[64,1792]{1,0:T(8,128)(2,1)S(1)} %slice.40), channel_id=1, source_target_pairs={{0,4},{1,5},{2,6},{3,7},{4,0},{5,1},{6,2},{7,3},{8,12},{9,13},{10,... | collective-permute-start | bytes 688136 | tf_op jit(solution)/shard_map/ppermute | solution.py:90
  92.1 7.0 %collective-permute-start.21 = (bf16[24,1792]{1,0:T(8,128)(2,1)S(1)}, bf16[24,1792]{1,0:T(8,128)(2,1)S(1)}, u32[]{:S(2)}, u32[]{:S(2)}) collective-permute-start(bf16[24,1792]{1,0:T(8,128)(2,1)S(1)} %slice.41), channel_id=1, source_target_pairs={{0,8},{1,9},{2,10},{3,11},{4,12},{5,13},{6,14},{7,15},{8,16},{9,17... | collective-permute-start | bytes 258056 | tf_op jit(solution)/shard_map/ppermute | solution.py:90
  92.1 1.2 %copy-start.8 = (bf16[240,1792]{1,0:T(8,128)(2,1)S(1)}, bf16[240,1792]{1,0:T(8,128)(2,1)}, u32[]{:S(2)}) copy-start(bf16[240,1792]{1,0:T(8,128)(2,1)} %copy-done.7) | copy-start | bytes 2580484
  99.1 6.6 %copy-start.20 = (bf16[24,1792]{1,0:T(8,128)(2,1)}, bf16[24,1792]{1,0:T(8,128)(2,1)S(1)}, u32[]{:S(2)}) copy-start(bf16[24,1792]{1,0:T(8,128)(2,1)S(1)} %collective-permute-done.21.refs_4_) | copy-start | bytes 258052
  101.2 4.5 %copy-start.16 = (bf16[64,1792]{1,0:T(8,128)(2,1)}, bf16[64,1792]{1,0:T(8,128)(2,1)S(1)}, u32[]{:S(2)}) copy-start(bf16[64,1792]{1,0:T(8,128)(2,1)S(1)} %collective-permute-done.20.refs_3_) | copy-start | bytes 688132
  102.2 1.5 %copy-start.9 = (f32[256,1792]{1,0:T(8,128)S(1)}, f32[256,1792]{1,0:T(8,128)}, u32[]{:S(2)}) copy-start(f32[256,1792]{1,0:T(8,128)} %get-tuple-element.160.refs_6_) | copy-start | bytes 5505028
  105.7 5.4 %copy-start = (f32[256,1792]{1,0:T(8,128)S(1)}, f32[256,1792]{1,0:T(8,128)}, u32[]{:S(2)}) copy-start(f32[256,1792]{1,0:T(8,128)} %get-tuple-element.159.refs_6_) | copy-start | bytes 5505028
  105.7 6.5 %collective-permute-start.22 = (bf16[256,1792]{1,0:T(8,128)(2,1)}, bf16[256,1792]{1,0:T(8,128)(2,1)}, u32[]{:S(2)}, u32[]{:S(2)}) collective-permute-start(bf16[256,1792]{1,0:T(8,128)(2,1)} %finish_other.1), channel_id=1, source_target_pairs={{0,1},{1,0},{2,3},{3,2},{4,5},{5,4},{6,7},{7,6},{8,9},{9,8},{10,11... | collective-permute-start | bytes 2752520 | tf_op jit(solution)/shard_map/ppermute | solution.py:90
  107.9 3.2 %copy-start.17 = (bf16[64,1792]{1,0:T(8,128)(2,1)S(1)}, bf16[64,1792]{1,0:T(8,128)(2,1)}, u32[]{:S(2)}) copy-start(bf16[64,1792]{1,0:T(8,128)(2,1)} %copy-done.16) | copy-start | bytes 688132
  107.9 3.2 %copy-start.21 = (bf16[24,1792]{1,0:T(8,128)(2,1)S(1)}, bf16[24,1792]{1,0:T(8,128)(2,1)}, u32[]{:S(2)}) copy-start(bf16[24,1792]{1,0:T(8,128)(2,1)} %copy-done.20) | copy-start | bytes 258052
  111.1 1.2 %copy-start.15 = (bf16[256,1792]{1,0:T(8,128)(2,1)S(1)}, bf16[256,1792]{1,0:T(8,128)(2,1)}, u32[]{:S(2)}) copy-start(bf16[256,1792]{1,0:T(8,128)(2,1)} %copy-done.14) | copy-start | bytes 2752516
  111.1 1.2 %copy-start.29 = (f32[256]{0:T(256)S(1)}, f32[256]{0:T(256)}, u32[]{:S(2)}) copy-start(f32[256]{0:T(256)} %compare_convert_fusion.1) | copy-start | bytes 3076
  (5 other events, 4.4 us)

commit v3 on v2

--- a/solution.py
+++ b/solution.py
@@ -120,7 +120,7 @@
     return [pl.BlockSpec(memory_space=pltpu.VMEM)] * count
 
 
-def kernel_call(body, name, out_shape, *operands, scratch=(), aliases=None, specs=None):
+def kernel_call(body, name, out_shape, *operands, scratch=(), aliases=None, specs=None, mib=24):
     many = isinstance(out_shape, tuple)
     return pl.pallas_call(
         body,
@@ -129,7 +129,7 @@
         out_specs=tuple(vmem(len(out_shape))) if many else vmem(1)[0],
         scratch_shapes=list(scratch),
         input_output_aliases=aliases or {},
-        compiler_params=pltpu.CompilerParams(vmem_limit_bytes=48 * 1024 * 1024),
+        compiler_params=pltpu.CompilerParams(vmem_limit_bytes=mib * 1024 * 1024),
         cost_estimate=pl.CostEstimate(flops=1000, bytes_accessed=1000, transcendentals=0),
         name=name,
     )(*operands)
@@ -221,7 +221,7 @@
 def attend_body(
     feat_in,
     value_len,
-    valid_ref,
+    count_ref,
     rate_ref,
     queries_ref,
     keys_ref,
@@ -238,7 +238,7 @@
     columns = values_ref.shape[1]
     lane = lax.broadcasted_iota(jnp.int32, (count, count), 1)
     row = lax.broadcasted_iota(jnp.int32, (count, count), 0)
-    valid = valid_ref[...]
+    valid = (lane[:1] < count_ref[0]).astype(jnp.float32)
     rate = jnp.where(valid > 0, rate_ref[...], 0.0)
     upto = (row <= lane).astype(jnp.float32)
     across = jnp.dot(
@@ -296,7 +296,7 @@
         out_ref[1 + feat_in :, :] = source[:pairs, :width]
 
 
-def attend(valid, rate, queries, keys, values, feat_in, value_len):
+def attend(valid_count, rate, queries, keys, values, feat_in, value_len):
     heads, count = rate.shape
     columns = values.shape[1]
     feat_len = 1 + feat_in + feat_in * feat_in
@@ -310,11 +310,12 @@
             like(feat_len, columns, jnp.float32),
             like(feat_len, heads, jnp.float32),
         ),
-        valid,
+        valid_count,
         rate,
         queries,
         keys,
         values,
+        specs=[pl.BlockSpec(memory_space=pltpu.SMEM)] + vmem(4),
         scratch=(
             pltpu.VMEM((queries.shape[1], count), jnp.float32),
             pltpu.VMEM((padded, columns), jnp.float32),
@@ -369,84 +370,105 @@
     return jnp.dot(hidden_units, down_rows, preferred_element_type=jnp.float32)
 
 
-def main_rows(refs, main):
-    if len(refs) == 1:
-        (ref,) = refs
-        return [ref[:main]], [ref[main : 2 * main]], [ref[2 * main : 3 * main]]
-    first, second = refs
-    cut = main + 2 * main // 3
-    rest = 2 * main - cut
-    return [first[:main]], [first[main:cut], second[:rest]], [second[rest : rest + main]]
-
-
-def edge_rows(array, edge):
-    parts = ([], [], [])
-    for base in range(0, array.shape[0], 3 * edge):
-        for k in range(3):
-            parts[k].append(array[base + k * edge : base + (k + 1) * edge])
+def on_grid(run):
+    return all(low % 16 == 0 and high % 16 == 0 for _, low, high in run)
+
+
+def read_units(refs, units):
+    parts = []
+    for k in range(3):
+        rows = [refs[run[k][0]][run[k][1] : run[k][2]] for run in units if on_grid(run)]
+        rest = [
+            refs[run[k][0]][...].astype(jnp.float32)[run[k][1] : run[k][2]]
+            for run in units
+            if not on_grid(run)
+        ]
+        if rest:
+            rows.append(jnp.concatenate(rest, axis=0).astype(jnp.bfloat16))
+        parts.append(jnp.concatenate(rows, axis=0))
     return parts
 
 
-def gather_units(refs, pieces, edges, main, edge):
-    parts = ([], [], [])
-    for piece in pieces:
-        for part, rows in zip(parts, main_rows([refs[i] for i in piece], main)):
-            part.extend(rows)
-    edge_parts = ([], [], [])
-    for i, low in edges:
-        for part, rows in zip(edge_parts, edge_rows(refs[i][...].astype(jnp.float32)[low:], edge)):
-            part.extend(rows)
-    for part, rows in zip(parts, edge_parts):
-        if rows:
-            part.append(jnp.concatenate(rows, axis=0).astype(jnp.bfloat16))
-    return [jnp.concatenate(part, axis=0) for part in parts]
-
-
-def accumulate_body(main, edge, n_weights, pieces, edges, n_acc, n_rows, *refs):
+def accumulate_body(units, n_weights, n_rows, n_acc, residual, *refs):
     weights = refs[:n_weights]
     rows = refs[n_weights : n_weights + n_rows]
     acc = refs[n_weights + n_rows : n_weights + n_rows + n_acc]
-    parts = gather_units(weights, pieces, edges, main, edge)
+    parts = read_units(weights, units)
     for k, rows_ref in enumerate(rows):
         out_ref = refs[len(refs) - n_rows + k]
         terms = swiglu_terms(rows_ref[...], *parts)
         if n_acc:
             terms = terms + acc[k][...]
+        if residual:
+            terms = terms + refs[n_weights + n_rows + n_acc][...].astype(jnp.float32)
         out_ref[...] = terms.astype(out_ref.dtype)
 
 
-def accumulate(rows, weights, pieces, edges, main, edge, acc, dtype, name):
+def accumulate(rows, weights, units, acc, dtype, name, residual=None):
     shapes = tuple(like(*array.shape, dtype) for array in rows)
     start = len(weights) + len(rows)
-    in_place = acc and dtype == jnp.float32
+    aliases = {start + k: k for k in range(len(acc))} if dtype == jnp.float32 else {}
+    extra = () if residual is None else (residual,)
     body = functools.partial(
-        accumulate_body, main, edge, len(weights), pieces, edges, len(acc), len(rows)
-    )
-    aliases = {start + k: k for k in range(len(acc))} if in_place else {}
-    return kernel_call(body, name, shapes, *weights, *rows, *acc, aliases=aliases)
-
-
-def shard_body(main, gate_ref, up_ref, down_ref, shard_ref, main_ref):
-    arrays = [ref[...].astype(jnp.float32) for ref in (gate_ref, up_ref, down_ref)]
+        accumulate_body, tuple(units), len(weights), len(rows), len(acc), bool(extra)
+    )
+    return kernel_call(body, name, shapes, *weights, *rows, *acc, *extra, aliases=aliases)
+
+
+def runs(which, low, size):
+    return tuple((which, low + k * size, low + (k + 1) * size) for k in range(3))
+
+
+def split_runs(first, second, main):
+    (i, at), (j, then) = first, second
+    held = 2 * main // 3
+    rest = main - held
+    return (
+        ((i, at, at + held), (i, at + main, at + main + held), (j, then + rest, then + main)),
+        ((i, at + held, at + main), (j, then, then + rest), (j, then + main, then + rest + main)),
+    )
+
+
+def collect_body(plans, *refs):
+    outs = refs[len(refs) - len(plans) :]
+    for out_ref, plan in zip(outs, plans):
+        rows = [refs[i][...].astype(jnp.float32)[low:high] for i, low, high in plan]
+        out_ref[...] = jnp.concatenate(rows, axis=0).astype(jnp.bfloat16)
+
+
+def collect(arrays, plans, name):
+    columns = arrays[0].shape[1]
+    shapes = tuple(like(sum(h - l for _, l, h in plan), columns, jnp.bfloat16) for plan in plans)
+    return kernel_call(functools.partial(collect_body, plans), name, shapes, *arrays)
+
+
+def shard_body(main, gate_ref, up_ref, down_ref, shard_ref, main_ref, *rest):
+    buffers, sems = rest[:3], rest[3]
+    copies = [
+        pltpu.make_async_copy(source, buffer, sems.at[k])
+        for k, (source, buffer) in enumerate(zip((gate_ref, up_ref, down_ref), buffers))
+    ]
+    for copy in copies:
+        copy.start()
+    for copy in copies:
+        copy.wait()
+    arrays = [buffer[...].astype(jnp.float32) for buffer in buffers]
     tops = [array[:main] for array in arrays]
     ends = [array[main:] for array in arrays]
     shard_ref[...] = jnp.concatenate(tops + ends, axis=0).astype(jnp.bfloat16)
     main_ref[...] = jnp.concatenate(tops, axis=0).astype(jnp.bfloat16)
 
 
-def second_slot_body(width, cut, shard_ref, near_ref, far_ref, deep_ref, line_ref, first, second):
-    shard, near, far, deep = [
-        ref[...].astype(jnp.float32) for ref in (shard_ref, near_ref, far_ref, deep_ref)
-    ]
-    line = [deep, shard[width:], near[width:], far[width:]]
-    line_ref[...] = jnp.concatenate(line, axis=0).astype(jnp.bfloat16)
-    first[...] = far[:cut].astype(jnp.bfloat16)
-    second[...] = near[cut:].astype(jnp.bfloat16)
-
-
-def third_slot_body(low, line_ref, corner_ref, out_ref):
-    line, corner = [ref[...].astype(jnp.float32) for ref in (line_ref, corner_ref)]
-    out_ref[...] = jnp.concatenate([line, corner[low:]], axis=0).astype(jnp.bfloat16)
+def final_body(step, count_ref, kept_ref, given_ref, out_ref):
+    count = kept_ref.shape[0]
+
+    @pl.loop(0, count // step)
+    def _(block):
+        first = pl.multiple_of(block * step, step)
+        at = pl.ds(first, step)
+        total = kept_ref[at, :] + given_ref[at, :].astype(jnp.float32)
+        row = lax.broadcasted_iota(jnp.int32, total.shape, 0) + first
+        out_ref[at, :] = jnp.where(row < count_ref[0], total, 0.0).astype(out_ref.dtype)
 
 
 def local(
@@ -471,25 +493,28 @@
     value_len = value_weight.shape[1] // head_count
     feat_in = query_weight.shape[1] // head_count
     feature_scale = feat_in ** (-0.25)
-    token_positions = lax.axis_index("seq") * local_len + jnp.arange(local_len, dtype=jnp.int32)
-    valid_mask = (token_positions < lengths[0]).astype(jnp.float32)
+    valid_count = lengths - lax.axis_index("seq") * local_len
     spans = lax.axis_size("seq")
     units, model = gate_weight.shape[1], gate_weight.shape[0]
     edge = units // 7
     main = units - edge
-    width = 3 * main
+    wide = 3 * main
+    full = 3 * units
+    narrow = full - wide
     cut = main + 2 * main // 3
-    low = width - cut
 
     shard, shard_main = kernel_call(
         functools.partial(shard_body, main),
         "shard",
-        (like(3 * units, model, jnp.bfloat16), like(width, model, jnp.bfloat16)),
+        (like(full, model, jnp.bfloat16), like(wide, model, jnp.bfloat16)),
         gate_weight.T,
         up_weight.T,
         down_weight.T,
-    )
-    near, far, deep1 = slot((flip_near, shard), (flip_far, shard), (next_plane, shard_main))
+        specs=[pl.BlockSpec(memory_space=pl.ANY)] * 3,
+        scratch=[pltpu.VMEM((units, model), jnp.bfloat16)] * 3 + [pltpu.SemaphoreType.DMA((3,))],
+        mib=56,
+    )
+    near, far, deep = slot((flip_near, shard), (flip_far, shard), (next_plane, shard_main))
 
     lead = 16
     if spans > 1:
@@ -499,89 +524,123 @@
     queries, key_rows, values = project(
         rows_in, edge_in, mix_gain, conv_weight, query_weight, key_weight, value_weight, feature_scale
     )
-
-    near, far, deep1, queries, key_rows, values = together(
-        near, far, deep1, queries, key_rows, values
-    )
-    line, first, second = kernel_call(
-        functools.partial(second_slot_body, width, cut),
-        "second_slot",
+    near, far, deep, queries, key_rows, values = together(
+        near, far, deep, queries, key_rows, values
+    )
+
+    sends = collect(
+        (shard, near, far, deep),
         (
-            like(width + 9 * edge, model, jnp.bfloat16),
-            like(cut, model, jnp.bfloat16),
-            like(3 * units - cut, model, jnp.bfloat16),
-        ),
-        shard,
-        near,
-        far,
-        deep1,
-    )
-    near1, far1, line1, first, second = slot(
-        (flip_near, deep1), (flip_far, deep1), (next_plane, line), (flip_near, first), (flip_far, second)
-    )
-
-    rate = log_decay[0].T
+            ((3, 0, wide), (2, 0, cut)),
+            ((3, 0, wide), (1, cut, full)),
+            ((3, 0, wide), (0, wide, full), (1, wide, full), (2, wide, full)),
+        ),
+        "collect_second",
+    )
+    near1, far1, deep1 = slot(*zip((flip_near, flip_far, next_plane), sends))
+
     numerator, denominator, end_state, end_norm = attend(
-        valid_mask[None], rate, queries, key_rows, values, feat_in, value_len
+        valid_count, log_decay[0].T, queries, key_rows, values, feat_in, value_len
     )
     if spans > 1:
+        positions = jnp.arange(local_len, dtype=jnp.int32)
         numerator, denominator, end_state, end_norm = carry_in(
-            valid_mask, decays, queries, numerator, denominator, end_state, end_norm
+            (positions < valid_count).astype(jnp.float32),
+            decays,
+            queries,
+            numerator,
+            denominator,
+            end_state,
+            end_norm,
         )
     mixed_rows, mlp_in = mix(numerator, denominator, rows_in, out_weight, mlp_gain, value_len)
-
-    near1, far1, line1, first, second, mixed_rows, mlp_in = together(
-        near1, far1, line1, first, second, mixed_rows, mlp_in
-    )
-    line = kernel_call(
-        functools.partial(third_slot_body, low),
-        "third_slot",
-        like(width + 12 * edge, model, jnp.bfloat16),
-        line1,
-        second,
-    )
-    near2, far2, line2, first1, second1 = slot(
-        (flip_near, line1[:width]),
-        (flip_far, line1[:width]),
-        (next_plane, line),
-        (flip_near, far1[:cut]),
-        (flip_far, near1[cut:]),
-    )
-    other_in, near3, far3, line3 = slot(
-        (flip_core, mlp_in),
-        (flip_near, line2[:width]),
-        (flip_far, line2[:width]),
-        (next_plane, line2[width:]),
-    )
-    rows = (mlp_in, other_in)
-    weights = (shard, near, far, first, second, deep1, near1, far1, line1, near2, far2, line2, first1, second1)
-    pieces = ((0,), (1,), (2,), (3, 4), (5,), (6,), (7,), (8,), (9,), (10,), (11,), (12, 13))
-    acc = accumulate(rows, weights, pieces, (), main, edge, (), jnp.float32, "accumulate_most")
-    near3, far3, line3, *acc = together(near3, far3, line3, *acc)
-    first2, second2, first3, second3, corner = slot(
-        (flip_near, far2[:cut]),
-        (flip_far, near2[cut:]),
-        (flip_near, far3[:cut]),
-        (flip_far, near3[cut:]),
-        (next_plane, line3[9 * edge :]),
-    )
-    weights = (near3, far3, shard, near, far, second, line1, line2, line3)
-    edges = ((2, width), (3, width), (4, width), (5, low), (6, width), (7, width), (8, 0))
+    near1, far1, deep1, mixed_rows, mlp_in, end_state, end_norm = together(
+        near1, far1, deep1, mixed_rows, mlp_in, end_state[None, None], end_norm[None, None]
+    )
+
+    sends = collect(
+        (near1, far1, deep1),
+        (
+            ((2, 0, wide), (1, 0, cut)),
+            ((2, 0, wide), (0, cut, wide)),
+            ((2, 0, wide + 3 * narrow), (1, wide + wide - cut, wide + full - cut)),
+        ),
+        "collect_third",
+    )
+    near2, far2, deep2 = slot(*zip((flip_near, flip_far, next_plane), sends))
+    rows = (mlp_in, flip_core(mlp_in))
     acc = accumulate(
-        rows, weights, ((0,), (1,)), edges, main, edge, tuple(acc), jnp.float32, "accumulate_edges"
-    )
-    weights = (first2, second2, first3, second3, corner)
-    pieces = ((0, 1), (2, 3))
-    edges = ((4, 0),)
-    (given,) = accumulate(
-        rows[1:], weights, pieces, edges, main, edge, acc[1:], jnp.bfloat16, "finish_other"
-    )
+        rows,
+        (shard, near, far, deep, near1, far1, deep1),
+        [runs(i, 0, main) for i in range(7)] + list(split_runs((4, wide), (5, wide), main)),
+        (),
+        jnp.float32,
+        "accumulate_second",
+    )
+    near2, far2, deep2, *acc = together(near2, far2, deep2, *acc)
+
+    deep3_main, line = collect(
+        (far2, deep2),
+        (
+            ((1, 0, wide),),
+            ((1, wide, wide + 4 * narrow), (0, wide + wide - cut - main, wide + wide - cut)),
+        ),
+        "collect_fourth",
+    )
+    near3, far3, deep3 = slot((flip_near, deep3_main), (flip_far, deep3_main), (next_plane, line))
+    acc = accumulate(
+        rows,
+        (shard, near, far, far1, deep1, near2, far2, deep2),
+        [runs(i, 0, main) for i in (5, 6, 7)]
+        + list(split_runs((5, wide), (6, wide), main))
+        + [runs(i, wide, edge) for i in (0, 1, 2)]
+        + [runs(3, wide + wide - cut, edge)]
+        + [runs(4, wide + k * narrow, edge) for k in range(3)]
+        + [runs(7, wide + k * narrow, edge) for k in range(4)],
+        tuple(acc),
+        jnp.float32,
+        "accumulate_third",
+    )
+    near3, far3, deep3, *acc = together(near3, far3, deep3, *acc)
+
+    sends = collect(
+        (near2, far2, near3, far3, deep3),
+        (
+            ((1, 0, main), (3, 0, main)),
+            ((0, main, 2 * main), (2, main, 2 * main)),
+            ((4, 3 * narrow, 4 * narrow + main),),
+        ),
+        "collect_fifth",
+    )
+    near4, far4, deep4 = slot(*zip((flip_near, flip_far, next_plane), sends))
+    acc = accumulate(
+        rows,
+        (near3, far3, deep3),
+        [runs(0, 0, main), runs(1, 0, main)] + [runs(2, k * narrow, edge) for k in range(4)],
+        tuple(acc),
+        jnp.float32,
+        "accumulate_fourth",
+    )
+    weights = (near4, far4, deep3, deep4)
+    last = [
+        ((0, 0, main), (1, 0, main), (2, 4 * narrow, 4 * narrow + main)),
+        ((0, main, 2 * main), (1, main, 2 * main), (3, narrow, narrow + main)),
+        runs(3, 0, edge),
+    ]
+    (given,) = accumulate(rows[1:], weights, last, acc[1:], jnp.bfloat16, "finish_other")
     (kept,) = accumulate(
-        rows[:1], weights, pieces, edges, main, edge, acc[:1], jnp.float32, "finish_own"
-    )
-    ffn_out = kept + flip_core(given).astype(jnp.float32)
-    result = ((mixed_rows.astype(jnp.float32) + ffn_out) * valid_mask[:, None]).astype(jnp.bfloat16)
-    return (result[None], end_state[None, None], end_norm[None, None])
+        rows[:1], weights, last, acc[:1], jnp.float32, "finish_own", residual=mixed_rows
+    )
+    result = kernel_call(
+        functools.partial(final_body, 64),
+        "final",
+        like(local_len, model, jnp.bfloat16),
+        valid_count,
+        kept,
+        flip_core(given),
+        specs=[pl.BlockSpec(memory_space=pltpu.SMEM)] + vmem(2),
+    )
+    return (result[None], end_state, end_norm)
 
 
 def solution(mesh):

time: 115 us -> 108 us (0.939)
  waiting for transfers between devices: 39.6 us -> 51 us
  starting transfers between devices: 23.1 us -> 15.6 us
  local copies, waits for them, and re-layouts: 19.8 us -> 13.2 us
  other arithmetic: 3.03 us -> 0 us
  Pallas kernels: 27.6 us -> 25.9 us
    ppermute x23 -> x17, waiting for transfers between devices: 39.6 us -> 51 us  [permute(): return lax.ppermute(array, 'req', [(i, target(i)) for i in range(count)])]
    ppermute x23 -> x17, starting transfers between devices: 23.1 us -> 15.6 us  [permute(): return lax.ppermute(array, 'req', [(i, target(i)) for i in range(count)])]
    unnamed x62 -> x38, local copies, waits for them, and re-layouts: 18.9 us -> 12.4 us
    broadcast_in_dim x1 -> x0, other arithmetic: 2.43 us -> none  [local(): return (result[None], end_state[None, None], end_norm[None, None])]
    pallas_call x10 -> x14, Pallas kernels: 27.6 us -> 25.9 us  [kernel_call(): pl.pallas_call(body, out_shape=out_shape, in_specs=specs or vmem(len(oper...]
  transfers between devices with their start and end apart: 23 -> 17, of which waited for: 10 -> 9; matrix products, arithmetic and copies ran while one was open for 5% -> 5% of each run, Pallas kernels for 15% -> 15%
where the time goes in v3:
time: 108 us; the launch traced here: 107 us
  waiting for transfers between devices  51 us (47%)
  Pallas kernels  25.9 us (24%)
  starting transfers between devices  15.6 us (14%)
  local copies, waits for them, and re-layouts  13.2 us (12%)
  between operations  1.52 us (1%)
    ppermute x17, waiting for transfers between devices, permute(): return lax.ppermute(array, 'req', [(i, target(i)) for i in range(count)])  51 us
    pallas_call x14, Pallas kernels, kernel_call(): pl.pallas_call(body, out_shape=out_shape, in_specs=specs or vmem(len(oper...  25.9 us
    ppermute x17, starting transfers between devices, permute(): return lax.ppermute(array, 'req', [(i, target(i)) for i in range(count)])  15.6 us
    unnamed x38, local copies, waits for them, and re-layouts  12.4 us
  transfers between devices with their start and end apart: 17, of which 9 were waited for; matrix products, arithmetic and copies ran while one was open for 5% of the time, Pallas kernels for 15%

profile of v3, /device:TPU:0, one launch (start us, length us, event | category | flops | bytes accessed | tf_op | source)
XLA Modules:
  0.0 107.2 jit_solution(5104822931367327975)
XLA Ops:
  0.6 2.2 %shard.1 = (bf16[168,1792]{1,0:T(8,128)(2,1)}, bf16[144,1792]{1,0:T(8,128)(2,1)}) custom-call(bf16[56,1792]{1,0:T(8,128)(2,1)} %bitcast.16, bf16[56,1792]{1,0:T(8,128)(2,1)} %bitcast.17, bf16[56,1792]{1,0:T(8,128)(2,1)} %bitcast.18), custom_call_target="tpu_custom_call" | custom-call | flops 1000 | bytes 1000 | tf_op jit(solution)/shard_map/shard/pallas_call | solution.py:125
  2.8 3.0 %collective-permute-start = (bf16[168,1792]{1,0:T(8,128)(2,1)}, bf16[168,1792]{1,0:T(8,128)(2,1)S(1)}, u32[]{:S(2)}, u32[]{:S(2)}) collective-permute-start(bf16[168,1792]{1,0:T(8,128)(2,1)} %get-tuple-element.78.refs_0_), channel_id=1, source_target_pairs={{0,2},{1,3},{2,0},{3,1},{4,6},{5,7},{6,4},{7,5},{8,10},{9,11},{10,... | collective-permute-start | bytes 1806344 | tf_op jit(solution)/shard_map/ppermute | solution.py:90
  5.8 1.5 %collective-permute-start.1 = (bf16[168,1792]{1,0:T(8,128)(2,1)}, bf16[168,1792]{1,0:T(8,128)(2,1)S(1)}, u32[]{:S(2)}, u32[]{:S(2)}) collective-permute-start(bf16[168,1792]{1,0:T(8,128)(2,1)} %get-tuple-element.78.refs_0_), channel_id=1, source_target_pairs={{0,4},{1,5},{2,6},{3,7},{4,0},{5,1},{6,2},{7,3},{8,12},{9,13},{10,... | collective-permute-start | bytes 1806344 | tf_op jit(solution)/shard_map/ppermute | solution.py:90
  7.4 1.6 %collective-permute-start.2 = (bf16[144,1792]{1,0:T(8,128)(2,1)}, bf16[144,1792]{1,0:T(8,128)(2,1)S(1)}, u32[]{:S(2)}, u32[]{:S(2)}) collective-permute-start(bf16[144,1792]{1,0:T(8,128)(2,1)} %get-tuple-element.79), channel_id=1, source_target_pairs={{0,8},{1,9},{2,10},{3,11},{4,12},{5,13},{6,14},{7,15},{8,16},{9,17... | collective-permute-start | bytes 1548296 | tf_op jit(solution)/shard_map/ppermute | solution.py:90
  8.9 0.7 broadcast_in_dim.19.gain_ref
  9.7 1.2 %copy-done.1 = bf16[1,256,1792]{2,1,0:T(8,128)(2,1)S(1)} copy-done((bf16[1,256,1792]{2,1,0:T(8,128)(2,1)S(1)}, bf16[1,256,1792]{2,1,0:T(8,128)(2,1)}, u32[]{:S(2)}) %copy-start.1) | copy-done | bytes 917528
  10.8 1.9 %copy-done.3 = bf16[1792,896]{1,0:T(8,128)(2,1)S(1)} copy-done((bf16[1792,896]{1,0:T(8,128)(2,1)S(1)}, bf16[1792,896]{1,0:T(8,128)(2,1)}, u32[]{:S(2)}) %copy-start.3) | copy-done | bytes 3211288
  12.7 1.0 copy-done.12
  13.8 1.0 copy-done.13
  14.8 0.7 copy-done.15
  15.5 3.7 %project.1 = (bf16[256,128]{1,0:T(8,128)(2,1)S(1)}, bf16[256,128]{1,0:T(8,128)(2,1)S(1)}, bf16[256,896]{1,0:T(8,128)(2,1)S(1)}) custom-call(bf16[256,1792]{1,0:T(8,128)(2,1)S(1)} %bitcast.10, bf16[16,1792]{1,0:T(8,128)(2,1)S(1)} %broadcast_in_dim.18.edge_ref, f32[1,1792]{1,0:T(1,128)S(1)} %broadcast_in_dim.19.gain_ref, f32[3,1792]{1,0:T(4,128)S(1)} %copy-done.15, ...), custom_call_target="tpu_custom_call" | custom-call | flops 1000 | bytes 1000 | tf_op jit(solution)/shard_map/project/pallas_call | solution.py:125
  19.3 0.0 copy-start.17
  19.3 0.0 copy-start.16
  19.3 3.0 %collective-permute-done.2.refs_3_ = bf16[144,1792]{1,0:T(8,128)(2,1)S(1)} collective-permute-done((bf16[144,1792]{1,0:T(8,128)(2,1)}, bf16[144,1792]{1,0:T(8,128)(2,1)S(1)}, u32[]{:S(2)}, u32[]{:S(2)}) %collective-permute-start.2) | collective-permute-done | bytes 516128 | tf_op jit(solution)/shard_map/ppermute | solution.py:90
  22.4 0.2 collect_second.1
  22.5 0.6 collective-permute-start.4
  23.1 0.5 collective-permute-start.3
  23.6 1.3 %collective-permute-start.5 = (bf16[216,1792]{1,0:T(8,128)(2,1)S(1)}, bf16[216,1792]{1,0:T(8,128)(2,1)S(1)}, u32[]{:S(2)}, u32[]{:S(2)}) collective-permute-start(bf16[216,1792]{1,0:T(8,128)(2,1)S(1)} %get-tuple-element.91), channel_id=1, source_target_pairs={{0,8},{1,9},{2,10},{3,11},{4,12},{5,13},{6,14},{7,15},{8,16},{9,17... | collective-permute-start | bytes 2322440 | tf_op jit(solution)/shard_map/ppermute | solution.py:90
  25.7 2.1 %attend.1 = (f32[256,896]{1,0:T(8,128)S(1)}, f32[256,8]{1,0:T(8,128)S(1)}, f32[273,896]{1,0:T(8,128)S(1)}, f32[273,8]{1,0:T(8,128)S(1)}) custom-call(s32[1]{0:T(128)S(6)} %copy.28.count_ref, f32[8,256]{1,0:T(8,128)S(1)} %bitcast.14, bf16[256,128]{1,0:T(8,128)(2,1)S(1)} %get-tuple-element.95.queries_ref, bf16[256,128]{1,0:T(8,128)(2,1)S(1)} %get-tuple-element.96.keys_ref, ...), custom_call_target="tpu_custom_call" | custom-call | flops 1000 | bytes 1000 | tf_op jit(solution)/shard_map/attend/pallas_call | solution.py:125
  27.8 1.0 copy-done.9
  28.8 0.7 copy-done.14
  29.4 2.6 %mix.1 = (bf16[256,1792]{1,0:T(8,128)(2,1)S(1)}, bf16[256,1792]{1,0:T(8,128)(2,1)S(1)}) custom-call(f32[256,896]{1,0:T(8,128)S(1)} %get-tuple-element.98.numer_ref, f32[256,8]{1,0:T(8,128)S(1)} %get-tuple-element.99.denom_ref, bf16[256,1792]{1,0:T(8,128)(2,1)S(1)} %bitcast.11, bf16[896,1792]{1,0:T(8,128)(2,1)S(1)} %copy-done.4, ...), custom_call_target="tpu_custom_call" | custom-call | flops 1000 | bytes 1000 | tf_op jit(solution)/shard_map/mix/pallas_call | solution.py:125
  32.1 10.7 %collective-permute-done.5.refs_2_.refs_6_.refs_4_ = bf16[216,1792]{1,0:T(8,128)(2,1)S(1)} collective-permute-done((bf16[216,1792]{1,0:T(8,128)(2,1)S(1)}, bf16[216,1792]{1,0:T(8,128)(2,1)S(1)}, u32[]{:S(2)}, u32[]{:S(2)}) %collective-permute-start.5) | collective-permute-done | bytes 774176 | tf_op jit(solution)/shard_map/ppermute | solution.py:90
  42.7 0.2 collect_third.1
  42.9 0.1 collective-permute-start.8
  43.0 1.4 %collective-permute-start.6 = (bf16[224,1792]{1,0:T(8,128)(2,1)S(1)}, bf16[224,1792]{1,0:T(8,128)(2,1)S(1)}, u32[]{:S(2)}, u32[]{:S(2)}) collective-permute-start(bf16[224,1792]{1,0:T(8,128)(2,1)S(1)} %get-tuple-element.107), channel_id=1, source_target_pairs={{0,2},{1,3},{2,0},{3,1},{4,6},{5,7},{6,4},{7,5},{8,10},{9,11},{10,... | collective-permute-start | bytes 2408456 | tf_op jit(solution)/shard_map/ppermute | solution.py:90
  44.3 1.5 %collective-permute-start.7 = (bf16[208,1792]{1,0:T(8,128)(2,1)S(1)}, bf16[208,1792]{1,0:T(8,128)(2,1)S(1)}, u32[]{:S(2)}, u32[]{:S(2)}) collective-permute-start(bf16[208,1792]{1,0:T(8,128)(2,1)S(1)} %get-tuple-element.108), channel_id=1, source_target_pairs={{0,4},{1,5},{2,6},{3,7},{4,0},{5,1},{6,2},{7,3},{8,12},{9,13},{10,... | collective-permute-start | bytes 2236424 | tf_op jit(solution)/shard_map/ppermute | solution.py:90
  45.8 17.3 %collective-permute-done.7.refs_0_.refs_6_.refs_1_ = bf16[208,1792]{1,0:T(8,128)(2,1)S(1)} collective-permute-done((bf16[208,1792]{1,0:T(8,128)(2,1)S(1)}, bf16[208,1792]{1,0:T(8,128)(2,1)S(1)}, u32[]{:S(2)}, u32[]{:S(2)}) %collective-permute-start.7) | collective-permute-done | bytes 745504 | tf_op jit(solution)/shard_map/ppermute | solution.py:90
  63.1 0.2 collective-permute-done.6.refs_5_.refs_0_
  63.3 2.9 %collective-permute-done.8.refs_1_.refs_7_ = bf16[240,1792]{1,0:T(8,128)(2,1)S(1)} collective-permute-done((bf16[240,1792]{1,0:T(8,128)(2,1)S(1)}, bf16[240,1792]{1,0:T(8,128)(2,1)S(1)}, u32[]{:S(2)}, u32[]{:S(2)}) %collective-permute-start.8) | collective-permute-done | bytes 860192 | tf_op jit(solution)/shard_map/ppermute | solution.py:90
  66.3 3.2 %accumulate_second.1 = (f32[256,1792]{1,0:T(8,128)S(1)}, f32[256,1792]{1,0:T(8,128)S(1)}) custom-call(bf16[168,1792]{1,0:T(8,128)(2,1)S(1)} %copy-done, bf16[168,1792]{1,0:T(8,128)(2,1)S(1)} %collective-permute-done.refs_1_, bf16[168,1792]{1,0:T(8,128)(2,1)S(1)} %collective-permute-done.1.refs_2_, bf16[144,1792]{1,0:T(8,128)(2,1)S(1)} %collective-permute-done.2.refs_3_, ...), custom_call_target="tpu_custom_call" | custom-call | flops 1000 | bytes 1000 | tf_op jit(solution)/shard_map/accumulate_second/pallas_call | solution.py:125
  69.5 0.1 collect_fourth.1
  69.6 1.4 %collective-permute-start.10 = (bf16[144,1792]{1,0:T(8,128)(2,1)S(1)}, bf16[144,1792]{1,0:T(8,128)(2,1)S(1)}, u32[]{:S(2)}, u32[]{:S(2)}) collective-permute-start(bf16[144,1792]{1,0:T(8,128)(2,1)S(1)} %get-tuple-element.122), channel_id=1, source_target_pairs={{0,2},{1,3},{2,0},{3,1},{4,6},{5,7},{6,4},{7,5},{8,10},{9,11},{10,... | collective-permute-start | bytes 1548296 | tf_op jit(solution)/shard_map/ppermute | solution.py:90
  70.9 1.5 %collective-permute-start.11 = (bf16[144,1792]{1,0:T(8,128)(2,1)S(1)}, bf16[144,1792]{1,0:T(8,128)(2,1)S(1)}, u32[]{:S(2)}, u32[]{:S(2)}) collective-permute-start(bf16[144,1792]{1,0:T(8,128)(2,1)S(1)} %get-tuple-element.122), channel_id=1, source_target_pairs={{0,4},{1,5},{2,6},{3,7},{4,0},{5,1},{6,2},{7,3},{8,12},{9,13},{10,... | collective-permute-start | bytes 1548296 | tf_op jit(solution)/shard_map/ppermute | solution.py:90
  72.4 3.9 %accumulate_third.1 = (f32[256,1792]{1,0:T(8,128)S(1)}, f32[256,1792]{1,0:T(8,128)S(1)}) custom-call(bf16[168,1792]{1,0:T(8,128)(2,1)S(1)} %copy-done, bf16[168,1792]{1,0:T(8,128)(2,1)S(1)} %collective-permute-done.refs_1_, bf16[168,1792]{1,0:T(8,128)(2,1)S(1)} %collective-permute-done.1.refs_2_, ...), custom_call_target="tpu_custom_call", output_to_operand_aliasing={{0}: (10, {}), {1}: (11, {})} | custom-call | flops 1000 | bytes 1000 | tf_op jit(solution)/shard_map/accumulate_third/pallas_call | solution.py:125
  76.3 6.7 %collective-permute-done.10.refs_2_.refs_0_ = bf16[144,1792]{1,0:T(8,128)(2,1)S(1)} collective-permute-done((bf16[144,1792]{1,0:T(8,128)(2,1)S(1)}, bf16[144,1792]{1,0:T(8,128)(2,1)S(1)}, u32[]{:S(2)}, u32[]{:S(2)}) %collective-permute-start.10) | collective-permute-done | bytes 516128 | tf_op jit(solution)/shard_map/ppermute | solution.py:90
  83.0 1.0 collective-permute-done.11.refs_3_.refs_1_
  84.0 3.0 %collective-permute-done.12.refs_4_.refs_2_ = bf16[144,1792]{1,0:T(8,128)(2,1)S(1)} collective-permute-done((bf16[144,1792]{1,0:T(8,128)(2,1)S(1)}, bf16[144,1792]{1,0:T(8,128)(2,1)S(1)}, u32[]{:S(2)}, u32[]{:S(2)}) %collective-permute-start.12) | collective-permute-done | bytes 516128 | tf_op jit(solution)/shard_map/ppermute | solution.py:90
  87.0 0.1 collect_fifth.1
  87.1 0.6 collective-permute-start.13
  87.7 0.7 collective-permute-start.14
  88.4 2.0 %accumulate_fourth.1 = (f32[256,1792]{1,0:T(8,128)S(1)}, f32[256,1792]{1,0:T(8,128)S(1)}) custom-call(bf16[144,1792]{1,0:T(8,128)(2,1)S(1)} %collective-permute-done.10.refs_2_.refs_0_, bf16[144,1792]{1,0:T(8,128)(2,1)S(1)} %collective-permute-done.11.refs_3_.refs_1_, ...), custom_call_target="tpu_custom_call", output_to_operand_aliasing={{0}: (5, {}), {1}: (6, {})} | custom-call | flops 1000 | bytes 1000 | tf_op jit(solution)/shard_map/accumulate_fourth/pallas_call | solution.py:125
  90.4 6.1 %collective-permute-done.15.refs_3_ = bf16[72,1792]{1,0:T(8,128)(2,1)S(1)} collective-permute-done((bf16[72,1792]{1,0:T(8,128)(2,1)S(1)}, bf16[72,1792]{1,0:T(8,128)(2,1)S(1)}, u32[]{:S(2)}, u32[]{:S(2)}) %collective-permute-start.15) | collective-permute-done | bytes 258080 | tf_op jit(solution)/shard_map/ppermute | solution.py:90
  96.6 2.0 %finish_other.1 = bf16[256,1792]{1,0:T(8,128)(2,1)} custom-call(bf16[96,1792]{1,0:T(8,128)(2,1)S(1)} %collective-permute-done.13.refs_0_, bf16[96,1792]{1,0:T(8,128)(2,1)S(1)} %collective-permute-done.14.refs_1_, bf16[144,1792]{1,0:T(8,128)(2,1)S(1)} %collective-permute-done.12.refs_4_.refs_2_, bf16[72,1792]{1,0:T(8,128)(2,1)S(1)} %collective-permute-done.15.refs_3_, ...), custom_call_target="tpu_custom_call" | custom-call | flops 1000 | bytes 1000 | tf_op jit(solution)/shard_map/finish_other/pallas_call | solution.py:125
  98.6 1.6 %copy.22 = f32[1,1,273,8]{2,3,1,0:T(8,128)} copy(f32[1,1,273,8]{3,2,1,0:T(8,128)} %bitcast.13) | data formatting | bytes 17472
  100.2 3.3 %copy.21 = f32[1,1,273,896]{3,1,2,0:T(1,128)} copy(f32[1,1,273,896]{3,2,1,0:T(8,128)} %bitcast.12) | data formatting | bytes 1956864
  103.5 1.4 %finish_own.1.kept_ref = f32[256,1792]{1,0:T(8,128)S(1)} custom-call(bf16[96,1792]{1,0:T(8,128)(2,1)S(1)} %copy-done.6, bf16[96,1792]{1,0:T(8,128)(2,1)S(1)} %copy-done.8, bf16[144,1792]{1,0:T(8,128)(2,1)S(1)} %collective-permute-done.12.refs_4_.refs_2_, bf16[72,1792]{1,0:T(8,128)(2,1)S(1)} %collective-permute-done.15.refs_3_, ...), custom_call_target="tpu_custom_call", output_to_operand_aliasing={{}: (5, {})} | custom-call | flops 1000 | bytes 1000 | tf_op jit(solution)/shard_map/finish_own/pallas_call | solution.py:125
  104.8 2.3 %final.1 = bf16[256,1792]{1,0:T(8,128)(2,1)} custom-call(s32[1]{0:T(128)S(6)} %copy.28.count_ref, f32[256,1792]{1,0:T(8,128)S(1)} %finish_own.1.kept_ref, bf16[256,1792]{1,0:T(8,128)(2,1)} %collective-permute-done.16.given_ref), custom_call_target="tpu_custom_call" | custom-call | flops 1000 | bytes 1000 | tf_op jit(solution)/shard_map/final/pallas_call | solution.py:125
  (41 shorter events, 0.1 us)
Async XLA Ops:
  2.8 19.5 %collective-permute-start = (bf16[168,1792]{1,0:T(8,128)(2,1)}, bf16[168,1792]{1,0:T(8,128)(2,1)S(1)}, u32[]{:S(2)}, u32[]{:S(2)}) collective-permute-start(bf16[168,1792]{1,0:T(8,128)(2,1)} %get-tuple-element.78.refs_0_), channel_id=1, source_target_pairs={{0,2},{1,3},{2,0},{3,1},{4,6},{5,7},{6,4},{7,5},{8,10},{9,11},{10,... | collective-permute-start | bytes 1806344 | tf_op jit(solution)/shard_map/ppermute | solution.py:90
  5.8 16.5 %collective-permute-start.1 = (bf16[168,1792]{1,0:T(8,128)(2,1)}, bf16[168,1792]{1,0:T(8,128)(2,1)S(1)}, u32[]{:S(2)}, u32[]{:S(2)}) collective-permute-start(bf16[168,1792]{1,0:T(8,128)(2,1)} %get-tuple-element.78.refs_0_), channel_id=1, source_target_pairs={{0,4},{1,5},{2,6},{3,7},{4,0},{5,1},{6,2},{7,3},{8,12},{9,13},{10,... | collective-permute-start | bytes 1806344 | tf_op jit(solution)/shard_map/ppermute | solution.py:90
  7.4 15.0 %collective-permute-start.2 = (bf16[144,1792]{1,0:T(8,128)(2,1)}, bf16[144,1792]{1,0:T(8,128)(2,1)S(1)}, u32[]{:S(2)}, u32[]{:S(2)}) collective-permute-start(bf16[144,1792]{1,0:T(8,128)(2,1)} %get-tuple-element.79), channel_id=1, source_target_pairs={{0,8},{1,9},{2,10},{3,11},{4,12},{5,13},{6,14},{7,15},{8,16},{9,17... | collective-permute-start | bytes 1548296 | tf_op jit(solution)/shard_map/ppermute | solution.py:90
  9.7 1.2 %copy-start.1 = (bf16[1,256,1792]{2,1,0:T(8,128)(2,1)S(1)}, bf16[1,256,1792]{2,1,0:T(8,128)(2,1)}, u32[]{:S(2)}) copy-start(bf16[1,256,1792]{2,1,0:T(8,128)(2,1)} %param.13) | copy-start | bytes 2752516
  10.8 1.9 %copy-start.3 = (bf16[1792,896]{1,0:T(8,128)(2,1)S(1)}, bf16[1792,896]{1,0:T(8,128)(2,1)}, u32[]{:S(2)}) copy-start(bf16[1792,896]{1,0:T(8,128)(2,1)} %value_ref.1) | copy-start | bytes 9633796
  12.7 1.0 copy-start.12
  13.8 1.0 copy-start.13
  14.8 0.7 copy-start.15
  15.5 6.8 %copy-start = (bf16[168,1792]{1,0:T(8,128)(2,1)S(1)}, bf16[168,1792]{1,0:T(8,128)(2,1)}, u32[]{:S(2)}) copy-start(bf16[168,1792]{1,0:T(8,128)(2,1)} %get-tuple-element.78.refs_0_) | copy-start | bytes 1806340
  15.5 13.9 %copy-start.4 = (bf16[896,1792]{1,0:T(8,128)(2,1)S(1)}, bf16[896,1792]{1,0:T(8,128)(2,1)}, u32[]{:S(2)}) copy-start(bf16[896,1792]{1,0:T(8,128)(2,1)} %out_ref.1) | copy-start | bytes 9633796
  19.3 6.3 %copy-start.17 = (f32[1792]{0:T(1024)S(1)}, f32[1792]{0:T(1024)}, u32[]{:S(2)}) copy-start(f32[1792]{0:T(1024)} %param.22) | copy-start | bytes 21508
  19.3 6.3 %copy-start.16 = (f32[1,256,8]{1,2,0:T(8,128)S(1)}, f32[1,256,8]{1,2,0:T(8,128)}, u32[]{:S(2)}) copy-start(f32[1,256,8]{1,2,0:T(8,128)} %param.15) | copy-start | bytes 24580
  19.3 10.1 %copy-start.2 = (bf16[1,256,1792]{2,1,0:T(8,128)(2,1)S(1)}, bf16[1,256,1792]{2,1,0:T(8,128)(2,1)}, u32[]{:S(2)}) copy-start(bf16[1,256,1792]{2,1,0:T(8,128)(2,1)} %param.13) | copy-start | bytes 2752516
  22.5 20.2 %collective-permute-start.4 = (bf16[232,1792]{1,0:T(8,128)(2,1)S(1)}, bf16[232,1792]{1,0:T(8,128)(2,1)S(1)}, u32[]{:S(2)}, u32[]{:S(2)}) collective-permute-start(bf16[232,1792]{1,0:T(8,128)(2,1)S(1)} %get-tuple-element.90), channel_id=1, source_target_pairs={{0,4},{1,5},{2,6},{3,7},{4,0},{5,1},{6,2},{7,3},{8,12},{9,13},{10,... | collective-permute-start | bytes 2494472 | tf_op jit(solution)/shard_map/ppermute | solution.py:90
  23.1 19.6 %collective-permute-start.3 = (bf16[224,1792]{1,0:T(8,128)(2,1)S(1)}, bf16[224,1792]{1,0:T(8,128)(2,1)S(1)}, u32[]{:S(2)}, u32[]{:S(2)}) collective-permute-start(bf16[224,1792]{1,0:T(8,128)(2,1)S(1)} %get-tuple-element.89), channel_id=1, source_target_pairs={{0,2},{1,3},{2,0},{3,1},{4,6},{5,7},{6,4},{7,5},{8,10},{9,11},{10,... | collective-permute-start | bytes 2408456 | tf_op jit(solution)/shard_map/ppermute | solution.py:90
  23.6 19.1 %collective-permute-start.5 = (bf16[216,1792]{1,0:T(8,128)(2,1)S(1)}, bf16[216,1792]{1,0:T(8,128)(2,1)S(1)}, u32[]{:S(2)}, u32[]{:S(2)}) collective-permute-start(bf16[216,1792]{1,0:T(8,128)(2,1)S(1)} %get-tuple-element.91), channel_id=1, source_target_pairs={{0,8},{1,9},{2,10},{3,11},{4,12},{5,13},{6,14},{7,15},{8,16},{9,17... | collective-permute-start | bytes 2322440 | tf_op jit(solution)/shard_map/ppermute | solution.py:90
  27.8 1.0 copy-start.9
  28.8 0.7 copy-start.14
  32.0 10.9 %copy-start.10 = (bf16[256,1792]{1,0:T(8,128)(2,1)}, bf16[256,1792]{1,0:T(8,128)(2,1)S(1)}, u32[]{:S(2)}) copy-start(bf16[256,1792]{1,0:T(8,128)(2,1)S(1)} %get-tuple-element.143.refs_6_) | copy-start | bytes 2752516
  42.7 23.6 %collective-permute-start.9 = (bf16[256,1792]{1,0:T(8,128)(2,1)S(1)}, bf16[256,1792]{1,0:T(8,128)(2,1)S(1)}, u32[]{:S(2)}, u32[]{:S(2)}) collective-permute-start(bf16[256,1792]{1,0:T(8,128)(2,1)S(1)} %get-tuple-element.113.refs_7_.refs_8_.refs_3_.refs_4_), channel_id=1, source_target_pairs={{0,1},{1,0},{2,3},{3,2},{4,5},{5,4},{6,7},{7,6},{8,9},{9,8},{10,11... | collective-permute-start | bytes 2752520 | tf_op jit(solution)/shard_map/ppermute | solution.py:90
  42.9 23.4 %collective-permute-start.8 = (bf16[240,1792]{1,0:T(8,128)(2,1)S(1)}, bf16[240,1792]{1,0:T(8,128)(2,1)S(1)}, u32[]{:S(2)}, u32[]{:S(2)}) collective-permute-start(bf16[240,1792]{1,0:T(8,128)(2,1)S(1)} %get-tuple-element.109), channel_id=1, source_target_pairs={{0,8},{1,9},{2,10},{3,11},{4,12},{5,13},{6,14},{7,15},{8,16},{9,17... | collective-permute-start | bytes 2580488 | tf_op jit(solution)/shard_map/ppermute | solution.py:90
  43.0 20.4 %collective-permute-start.6 = (bf16[224,1792]{1,0:T(8,128)(2,1)S(1)}, bf16[224,1792]{1,0:T(8,128)(2,1)S(1)}, u32[]{:S(2)}, u32[]{:S(2)}) collective-permute-start(bf16[224,1792]{1,0:T(8,128)(2,1)S(1)} %get-tuple-element.107), channel_id=1, source_target_pairs={{0,2},{1,3},{2,0},{3,1},{4,6},{5,7},{6,4},{7,5},{8,10},{9,11},{10,... | collective-permute-start | bytes 2408456 | tf_op jit(solution)/shard_map/ppermute | solution.py:90
  44.3 18.8 %collective-permute-start.7 = (bf16[208,1792]{1,0:T(8,128)(2,1)S(1)}, bf16[208,1792]{1,0:T(8,128)(2,1)S(1)}, u32[]{:S(2)}, u32[]{:S(2)}) collective-permute-start(bf16[208,1792]{1,0:T(8,128)(2,1)S(1)} %get-tuple-element.108), channel_id=1, source_target_pairs={{0,4},{1,5},{2,6},{3,7},{4,0},{5,1},{6,2},{7,3},{8,12},{9,13},{10,... | collective-permute-start | bytes 2236424 | tf_op jit(solution)/shard_map/ppermute | solution.py:90
  69.6 13.4 %collective-permute-start.10 = (bf16[144,1792]{1,0:T(8,128)(2,1)S(1)}, bf16[144,1792]{1,0:T(8,128)(2,1)S(1)}, u32[]{:S(2)}, u32[]{:S(2)}) collective-permute-start(bf16[144,1792]{1,0:T(8,128)(2,1)S(1)} %get-tuple-element.122), channel_id=1, source_target_pairs={{0,2},{1,3},{2,0},{3,1},{4,6},{5,7},{6,4},{7,5},{8,10},{9,11},{10,... | collective-permute-start | bytes 1548296 | tf_op jit(solution)/shard_map/ppermute | solution.py:90
  70.9 13.1 %collective-permute-start.11 = (bf16[144,1792]{1,0:T(8,128)(2,1)S(1)}, bf16[144,1792]{1,0:T(8,128)(2,1)S(1)}, u32[]{:S(2)}, u32[]{:S(2)}) collective-permute-start(bf16[144,1792]{1,0:T(8,128)(2,1)S(1)} %get-tuple-element.122), channel_id=1, source_target_pairs={{0,4},{1,5},{2,6},{3,7},{4,0},{5,1},{6,2},{7,3},{8,12},{9,13},{10,... | collective-permute-start | bytes 1548296 | tf_op jit(solution)/shard_map/ppermute | solution.py:90
  72.4 14.6 %collective-permute-start.12 = (bf16[144,1792]{1,0:T(8,128)(2,1)S(1)}, bf16[144,1792]{1,0:T(8,128)(2,1)S(1)}, u32[]{:S(2)}, u32[]{:S(2)}) collective-permute-start(bf16[144,1792]{1,0:T(8,128)(2,1)S(1)} %get-tuple-element.123), channel_id=1, source_target_pairs={{0,8},{1,9},{2,10},{3,11},{4,12},{5,13},{6,14},{7,15},{8,16},{9,17... | collective-permute-start | bytes 1548296 | tf_op jit(solution)/shard_map/ppermute | solution.py:90
  87.1 9.5 %collective-permute-start.13 = (bf16[96,1792]{1,0:T(8,128)(2,1)S(1)}, bf16[96,1792]{1,0:T(8,128)(2,1)S(1)}, u32[]{:S(2)}, u32[]{:S(2)}) collective-permute-start(bf16[96,1792]{1,0:T(8,128)(2,1)S(1)} %get-tuple-element.134), channel_id=1, source_target_pairs={{0,2},{1,3},{2,0},{3,1},{4,6},{5,7},{6,4},{7,5},{8,10},{9,11},{10,... | collective-permute-start | bytes 1032200 | tf_op jit(solution)/shard_map/ppermute | solution.py:90
  87.7 8.9 %collective-permute-start.14 = (bf16[96,1792]{1,0:T(8,128)(2,1)S(1)}, bf16[96,1792]{1,0:T(8,128)(2,1)S(1)}, u32[]{:S(2)}, u32[]{:S(2)}) collective-permute-start(bf16[96,1792]{1,0:T(8,128)(2,1)S(1)} %get-tuple-element.135), channel_id=1, source_target_pairs={{0,4},{1,5},{2,6},{3,7},{4,0},{5,1},{6,2},{7,3},{8,12},{9,13},{10,... | collective-permute-start | bytes 1032200 | tf_op jit(solution)/shard_map/ppermute | solution.py:90
  88.4 8.1 %collective-permute-start.15 = (bf16[72,1792]{1,0:T(8,128)(2,1)S(1)}, bf16[72,1792]{1,0:T(8,128)(2,1)S(1)}, u32[]{:S(2)}, u32[]{:S(2)}) collective-permute-start(bf16[72,1792]{1,0:T(8,128)(2,1)S(1)} %get-tuple-element.136), channel_id=1, source_target_pairs={{0,8},{1,9},{2,10},{3,11},{4,12},{5,13},{6,14},{7,15},{8,16},{9,17... | collective-permute-start | bytes 774152 | tf_op jit(solution)/shard_map/ppermute | solution.py:90
  96.6 2.0 %copy-start.5 = (bf16[96,1792]{1,0:T(8,128)(2,1)}, bf16[96,1792]{1,0:T(8,128)(2,1)S(1)}, u32[]{:S(2)}) copy-start(bf16[96,1792]{1,0:T(8,128)(2,1)S(1)} %collective-permute-done.13.refs_0_) | copy-start | bytes 1032196
  96.6 2.0 %copy-start.7 = (bf16[96,1792]{1,0:T(8,128)(2,1)}, bf16[96,1792]{1,0:T(8,128)(2,1)S(1)}, u32[]{:S(2)}) copy-start(bf16[96,1792]{1,0:T(8,128)(2,1)S(1)} %collective-permute-done.14.refs_1_) | copy-start | bytes 1032196
  98.6 6.3 %collective-permute-start.16 = (bf16[256,1792]{1,0:T(8,128)(2,1)}, bf16[256,1792]{1,0:T(8,128)(2,1)}, u32[]{:S(2)}, u32[]{:S(2)}) collective-permute-start(bf16[256,1792]{1,0:T(8,128)(2,1)} %finish_other.1), channel_id=1, source_target_pairs={{0,1},{1,0},{2,3},{3,2},{4,5},{5,4},{6,7},{7,6},{8,9},{9,8},{10,11... | collective-permute-start | bytes 2752520 | tf_op jit(solution)/shard_map/ppermute | solution.py:90
  100.2 3.3 %copy-start.6 = (bf16[96,1792]{1,0:T(8,128)(2,1)S(1)}, bf16[96,1792]{1,0:T(8,128)(2,1)}, u32[]{:S(2)}) copy-start(bf16[96,1792]{1,0:T(8,128)(2,1)} %copy-done.5) | copy-start | bytes 1032196
  100.2 3.3 %copy-start.8 = (bf16[96,1792]{1,0:T(8,128)(2,1)S(1)}, bf16[96,1792]{1,0:T(8,128)(2,1)}, u32[]{:S(2)}) copy-start(bf16[96,1792]{1,0:T(8,128)(2,1)} %copy-done.7) | copy-start | bytes 1032196
  100.2 3.3 %copy-start.11 = (bf16[256,1792]{1,0:T(8,128)(2,1)S(1)}, bf16[256,1792]{1,0:T(8,128)(2,1)}, u32[]{:S(2)}) copy-start(bf16[256,1792]{1,0:T(8,128)(2,1)} %copy-done.10) | copy-start | bytes 2752516

commit v4 on v3

--- a/solution.py
+++ b/solution.py
@@ -255,7 +255,8 @@
     head_lane = lax.broadcasted_iota(jnp.int32, (count, 128), 1)
     numer_ref[...] = jnp.zeros(numer_ref.shape, jnp.float32)
     total[...] = jnp.zeros(total.shape, jnp.float32)
-    norm_total = jnp.zeros(norms.shape, jnp.float32)
+    norms[...] = jnp.zeros(norms.shape, jnp.float32)
+    norm_total = jnp.zeros((total.shape[0], 128), jnp.float32)
     denominators = jnp.zeros((count, 128), jnp.float32)
     for h in range(heads):
         low = min(h * value_len // 128 * 128, max(columns - 256, 0))
@@ -288,12 +289,21 @@
         mark = (head_lane == h).astype(jnp.bfloat16)
         norm_total = norm_total + jnp.dot(feats, mark, preferred_element_type=jnp.float32)
     denom_ref[...] = denominators[:, :heads]
-    norms[...] = norm_total
     pairs = feat_in * feat_in
-    for out_ref, source, width in ((state_ref, total, columns), (norm_ref, norms, heads)):
-        out_ref[0:1, :] = source[pairs + feat_in : pairs + feat_in + 1, :width]
-        out_ref[1 : 1 + feat_in, :] = source[pairs : pairs + feat_in, :width]
-        out_ref[1 + feat_in :, :] = source[:pairs, :width]
+    state_ref[0] = total[pairs + feat_in : pairs + feat_in + 1, :]
+    for f in range(feat_in):
+        state_ref[1 + f] = total[pairs + f : pairs + f + 1, :]
+
+    @pl.loop(0, pairs // 8)
+    def _(block):
+        for k in range(8):
+            f = block * 8 + k
+            state_ref[1 + feat_in + f] = total[pl.ds(f, 1), :]
+
+    norms[0:1, :] = norm_total[pairs + feat_in : pairs + feat_in + 1]
+    norms[1 : 1 + feat_in, :] = norm_total[pairs : pairs + feat_in]
+    norms[1 + feat_in : 1 + feat_in + pairs, :] = norm_total[:pairs]
+    norm_ref[...] = norms[...].T[:heads, : 1 + feat_in + pairs]
 
 
 def attend(valid_count, rate, queries, keys, values, feat_in, value_len):
@@ -307,8 +317,8 @@
         (
             like(count, columns, jnp.float32),
             like(count, heads, jnp.float32),
-            like(feat_len, columns, jnp.float32),
-            like(feat_len, heads, jnp.float32),
+            jax.ShapeDtypeStruct((feat_len, 1, columns), jnp.float32),
+            like(heads, feat_len, jnp.float32),
         ),
         valid_count,
         rate,
@@ -319,7 +329,7 @@
         scratch=(
             pltpu.VMEM((queries.shape[1], count), jnp.float32),
             pltpu.VMEM((padded, columns), jnp.float32),
-            pltpu.VMEM((padded, 128), jnp.float32),
+            pltpu.VMEM(((feat_len + 127) // 128 * 128, 128), jnp.float32),
         ),
     )
 
@@ -550,12 +560,14 @@
             queries,
             numerator,
             denominator,
-            end_state,
-            end_norm,
+            end_state[:, 0],
+            end_norm.T,
         )
+    else:
+        end_norm = end_norm.T
     mixed_rows, mlp_in = mix(numerator, denominator, rows_in, out_weight, mlp_gain, value_len)
     near1, far1, deep1, mixed_rows, mlp_in, end_state, end_norm = together(
-        near1, far1, deep1, mixed_rows, mlp_in, end_state[None, None], end_norm[None, None]
+        near1, far1, deep1, mixed_rows, mlp_in, end_state, end_norm
     )
 
     sends = collect(
@@ -577,7 +589,7 @@
         jnp.float32,
         "accumulate_second",
     )
-    near2, far2, deep2, *acc = together(near2, far2, deep2, *acc)
+    near2, far2, deep2 = together(near2, far2, deep2)
 
     deep3_main, line = collect(
         (far2, deep2),
@@ -640,7 +652,11 @@
         flip_core(given),
         specs=[pl.BlockSpec(memory_space=pltpu.SMEM)] + vmem(2),
     )
-    return (result[None], end_state, end_norm)
+    return (
+        result[None],
+        end_state.reshape((1, 1) + end_state.shape[:1] + end_state.shape[-1:]),
+        end_norm[None, None],
+    )
 
 
 def solution(mesh):

time: 108 us -> 91.4 us (0.85)
  waiting for transfers between devices: 51 us -> 41.3 us
  local copies, waits for them, and re-layouts: 13.2 us -> 6.61 us
    ppermute x17, waiting for transfers between devices: 51 us -> 41.3 us  [permute(): return lax.ppermute(array, 'req', [(i, target(i)) for i in range(count)])]
    unnamed x38 -> x20, local copies, waits for them, and re-layouts: 12.4 us -> 5.89 us
  transfers between devices with their start and end apart: 17 -> 17, of which waited for: 9 -> 9; matrix products, arithmetic and copies ran while one was open for 5% -> 1% of each run, Pallas kernels for 15% -> 23%
where the time goes in v4:
time: 91.4 us; the launch traced here: 90.9 us
  waiting for transfers between devices  41.3 us (45%)
  Pallas kernels  25.3 us (28%)
  starting transfers between devices  16.3 us (18%)
  local copies, waits for them, and re-layouts  6.61 us (7%)
  between operations  1.46 us (2%)
    ppermute x17, waiting for transfers between devices, permute(): return lax.ppermute(array, 'req', [(i, target(i)) for i in range(count)])  41.3 us
    pallas_call x14, Pallas kernels, kernel_call(): pl.pallas_call(body, out_shape=out_shape, in_specs=specs or vmem(len(oper...  25.3 us
    ppermute x17, starting transfers between devices, permute(): return lax.ppermute(array, 'req', [(i, target(i)) for i in range(count)])  16.3 us
    unnamed x20, local copies, waits for them, and re-layouts  5.89 us
  transfers between devices with their start and end apart: 17, of which 9 were waited for; matrix products, arithmetic and copies ran while one was open for 1% of the time, Pallas kernels for 23%

profile of v4, /device:TPU:0, one launch (start us, length us, event | category | flops | bytes accessed | tf_op | source)
XLA Modules:
  0.0 90.9 jit_solution(8735580178986845523)
XLA Ops:
  0.6 2.2 %shard.1 = (bf16[168,1792]{1,0:T(8,128)(2,1)}, bf16[144,1792]{1,0:T(8,128)(2,1)}) custom-call(bf16[56,1792]{1,0:T(8,128)(2,1)} %bitcast.17, bf16[56,1792]{1,0:T(8,128)(2,1)} %bitcast.18, bf16[56,1792]{1,0:T(8,128)(2,1)} %bitcast.19), custom_call_target="tpu_custom_call" | custom-call | flops 1000 | bytes 1000 | tf_op jit(solution)/shard_map/shard/pallas_call | solution.py:125
  2.8 3.0 %collective-permute-start = (bf16[168,1792]{1,0:T(8,128)(2,1)}, bf16[168,1792]{1,0:T(8,128)(2,1)S(1)}, u32[]{:S(2)}, u32[]{:S(2)}) collective-permute-start(bf16[168,1792]{1,0:T(8,128)(2,1)} %get-tuple-element.73.refs_0_), channel_id=1, source_target_pairs={{0,2},{1,3},{2,0},{3,1},{4,6},{5,7},{6,4},{7,5},{8,10},{9,11},{10,... | collective-permute-start | bytes 1806344 | tf_op jit(solution)/shard_map/ppermute | solution.py:90
  5.8 1.5 %collective-permute-start.1 = (bf16[168,1792]{1,0:T(8,128)(2,1)}, bf16[168,1792]{1,0:T(8,128)(2,1)S(1)}, u32[]{:S(2)}, u32[]{:S(2)}) collective-permute-start(bf16[168,1792]{1,0:T(8,128)(2,1)} %get-tuple-element.73.refs_0_), channel_id=1, source_target_pairs={{0,4},{1,5},{2,6},{3,7},{4,0},{5,1},{6,2},{7,3},{8,12},{9,13},{10,... | collective-permute-start | bytes 1806344 | tf_op jit(solution)/shard_map/ppermute | solution.py:90
  7.4 1.6 %collective-permute-start.2 = (bf16[144,1792]{1,0:T(8,128)(2,1)}, bf16[144,1792]{1,0:T(8,128)(2,1)S(1)}, u32[]{:S(2)}, u32[]{:S(2)}) collective-permute-start(bf16[144,1792]{1,0:T(8,128)(2,1)} %get-tuple-element.74), channel_id=1, source_target_pairs={{0,8},{1,9},{2,10},{3,11},{4,12},{5,13},{6,14},{7,15},{8,16},{9,17... | collective-permute-start | bytes 1548296 | tf_op jit(solution)/shard_map/ppermute | solution.py:90
  8.9 0.7 broadcast_in_dim.16.gain_ref
  9.7 0.0 copy-start.1
  9.7 1.2 %copy-done.1 = bf16[1,256,1792]{2,1,0:T(8,128)(2,1)S(1)} copy-done((bf16[1,256,1792]{2,1,0:T(8,128)(2,1)S(1)}, bf16[1,256,1792]{2,1,0:T(8,128)(2,1)}, u32[]{:S(2)}) %copy-start.1) | copy-done | bytes 917528
  10.8 1.9 %copy-done.3 = bf16[1792,896]{1,0:T(8,128)(2,1)S(1)} copy-done((bf16[1792,896]{1,0:T(8,128)(2,1)S(1)}, bf16[1792,896]{1,0:T(8,128)(2,1)}, u32[]{:S(2)}) %copy-start.3) | copy-done | bytes 3211288
  12.7 1.0 %copy-done.5 = bf16[1792,128]{1,0:T(8,128)(2,1)S(1)} copy-done((bf16[1792,128]{1,0:T(8,128)(2,1)S(1)}, bf16[1792,128]{1,0:T(8,128)(2,1)}, u32[]{:S(2)}) %copy-start.5) | copy-done | bytes 458776
  13.8 1.0 %copy-done.6 = bf16[1792,128]{1,0:T(8,128)(2,1)S(1)} copy-done((bf16[1792,128]{1,0:T(8,128)(2,1)S(1)}, bf16[1792,128]{1,0:T(8,128)(2,1)}, u32[]{:S(2)}) %copy-start.6) | copy-done | bytes 458776
  14.8 0.7 copy-done.7
  15.5 3.7 %project.1 = (bf16[256,128]{1,0:T(8,128)(2,1)S(1)}, bf16[256,128]{1,0:T(8,128)(2,1)S(1)}, bf16[256,896]{1,0:T(8,128)(2,1)S(1)}) custom-call(bf16[256,1792]{1,0:T(8,128)(2,1)S(1)} %bitcast.13, bf16[16,1792]{1,0:T(8,128)(2,1)S(1)} %broadcast_in_dim.15.edge_ref, f32[1,1792]{1,0:T(1,128)S(1)} %broadcast_in_dim.16.gain_ref, f32[3,1792]{1,0:T(4,128)S(1)} %copy-done.7, ...), custom_call_target="tpu_custom_call" | custom-call | flops 1000 | bytes 1000 | tf_op jit(solution)/shard_map/project/pallas_call | solution.py:125
  19.3 0.0 copy-start.9
  19.3 0.0 copy-start.8
  19.3 0.0 copy-start.2
  19.3 3.1 %collective-permute-done.2.refs_3_ = bf16[144,1792]{1,0:T(8,128)(2,1)S(1)} collective-permute-done((bf16[144,1792]{1,0:T(8,128)(2,1)}, bf16[144,1792]{1,0:T(8,128)(2,1)S(1)}, u32[]{:S(2)}, u32[]{:S(2)}) %collective-permute-start.2) | collective-permute-done | bytes 516128 | tf_op jit(solution)/shard_map/ppermute | solution.py:90
  22.4 0.2 collect_second.1
  22.5 0.6 collective-permute-start.4
  23.1 0.5 collective-permute-start.3
  23.6 1.3 %collective-permute-start.5 = (bf16[216,1792]{1,0:T(8,128)(2,1)S(1)}, bf16[216,1792]{1,0:T(8,128)(2,1)S(1)}, u32[]{:S(2)}, u32[]{:S(2)}) collective-permute-start(bf16[216,1792]{1,0:T(8,128)(2,1)S(1)} %get-tuple-element.86), channel_id=1, source_target_pairs={{0,8},{1,9},{2,10},{3,11},{4,12},{5,13},{6,14},{7,15},{8,16},{9,17... | collective-permute-start | bytes 2322440 | tf_op jit(solution)/shard_map/ppermute | solution.py:90
  25.7 3.7 %attend.1 = (f32[256,896]{1,0:T(8,128)S(1)}, f32[256,8]{1,0:T(8,128)S(1)}, f32[273,1,896]{2,1,0:T(1,128)}, f32[8,273]{1,0:T(8,128)}) custom-call(s32[1]{0:T(128)S(6)} %copy.27.count_ref, f32[8,256]{1,0:T(8,128)S(1)} %bitcast.15, bf16[256,128]{1,0:T(8,128)(2,1)S(1)} %get-tuple-element.90.queries_ref, bf16[256,128]{1,0:T(8,128)(2,1)S(1)} %get-tuple-element.91.keys_ref, ...), custom_call_target="tpu_custom_call" | custom-call | flops 1000 | bytes 1000 | tf_op jit(solution)/shard_map/attend/pallas_call | solution.py:125
  29.4 2.6 %mix.1 = (bf16[256,1792]{1,0:T(8,128)(2,1)S(1)}, bf16[256,1792]{1,0:T(8,128)(2,1)S(1)}) custom-call(f32[256,896]{1,0:T(8,128)S(1)} %get-tuple-element.93.numer_ref, f32[256,8]{1,0:T(8,128)S(1)} %get-tuple-element.94.denom_ref, bf16[256,1792]{1,0:T(8,128)(2,1)S(1)} %bitcast.14, bf16[896,1792]{1,0:T(8,128)(2,1)S(1)} %copy-done.4, ...), custom_call_target="tpu_custom_call" | custom-call | flops 1000 | bytes 1000 | tf_op jit(solution)/shard_map/mix/pallas_call | solution.py:125
  32.0 10.7 %collective-permute-done.5.refs_2_.refs_6_.refs_4_ = bf16[216,1792]{1,0:T(8,128)(2,1)S(1)} collective-permute-done((bf16[216,1792]{1,0:T(8,128)(2,1)S(1)}, bf16[216,1792]{1,0:T(8,128)(2,1)S(1)}, u32[]{:S(2)}, u32[]{:S(2)}) %collective-permute-start.5) | collective-permute-done | bytes 774176 | tf_op jit(solution)/shard_map/ppermute | solution.py:90
  42.7 0.2 collect_third.1
  42.9 0.1 collective-permute-start.8
  43.0 1.4 %collective-permute-start.6 = (bf16[224,1792]{1,0:T(8,128)(2,1)S(1)}, bf16[224,1792]{1,0:T(8,128)(2,1)S(1)}, u32[]{:S(2)}, u32[]{:S(2)}) collective-permute-start(bf16[224,1792]{1,0:T(8,128)(2,1)S(1)} %get-tuple-element.102), channel_id=1, source_target_pairs={{0,2},{1,3},{2,0},{3,1},{4,6},{5,7},{6,4},{7,5},{8,10},{9,11},{10,... | collective-permute-start | bytes 2408456 | tf_op jit(solution)/shard_map/ppermute | solution.py:90
  44.3 1.5 %collective-permute-start.7 = (bf16[208,1792]{1,0:T(8,128)(2,1)S(1)}, bf16[208,1792]{1,0:T(8,128)(2,1)S(1)}, u32[]{:S(2)}, u32[]{:S(2)}) collective-permute-start(bf16[208,1792]{1,0:T(8,128)(2,1)S(1)} %get-tuple-element.103), channel_id=1, source_target_pairs={{0,4},{1,5},{2,6},{3,7},{4,0},{5,1},{6,2},{7,3},{8,12},{9,13},{10,... | collective-permute-start | bytes 2236424 | tf_op jit(solution)/shard_map/ppermute | solution.py:90
  45.8 13.8 %collective-permute-done.7.refs_0_.refs_6_.refs_1_ = bf16[208,1792]{1,0:T(8,128)(2,1)S(1)} collective-permute-done((bf16[208,1792]{1,0:T(8,128)(2,1)S(1)}, bf16[208,1792]{1,0:T(8,128)(2,1)S(1)}, u32[]{:S(2)}, u32[]{:S(2)}) %collective-permute-start.7) | collective-permute-done | bytes 745504 | tf_op jit(solution)/shard_map/ppermute | solution.py:90
  59.6 0.4 collective-permute-done.6.refs_5_.refs_0_
  60.0 2.9 %collective-permute-done.8.refs_1_.refs_7_ = bf16[240,1792]{1,0:T(8,128)(2,1)S(1)} collective-permute-done((bf16[240,1792]{1,0:T(8,128)(2,1)S(1)}, bf16[240,1792]{1,0:T(8,128)(2,1)S(1)}, u32[]{:S(2)}, u32[]{:S(2)}) %collective-permute-start.8) | collective-permute-done | bytes 860192 | tf_op jit(solution)/shard_map/ppermute | solution.py:90
  62.9 0.1 collect_fourth.1
  63.0 1.1 %collective-permute-start.10 = (bf16[144,1792]{1,0:T(8,128)(2,1)S(1)}, bf16[144,1792]{1,0:T(8,128)(2,1)S(1)}, u32[]{:S(2)}, u32[]{:S(2)}) collective-permute-start(bf16[144,1792]{1,0:T(8,128)(2,1)S(1)} %get-tuple-element.111), channel_id=1, source_target_pairs={{0,4},{1,5},{2,6},{3,7},{4,0},{5,1},{6,2},{7,3},{8,12},{9,13},{10,... | collective-permute-start | bytes 1548296 | tf_op jit(solution)/shard_map/ppermute | solution.py:90
  64.1 0.0 collective-permute-start.11
  64.1 1.5 %collective-permute-start.9 = (bf16[144,1792]{1,0:T(8,128)(2,1)S(1)}, bf16[144,1792]{1,0:T(8,128)(2,1)S(1)}, u32[]{:S(2)}, u32[]{:S(2)}) collective-permute-start(bf16[144,1792]{1,0:T(8,128)(2,1)S(1)} %get-tuple-element.111), channel_id=1, source_target_pairs={{0,2},{1,3},{2,0},{3,1},{4,6},{5,7},{6,4},{7,5},{8,10},{9,11},{10,... | collective-permute-start | bytes 1548296 | tf_op jit(solution)/shard_map/ppermute | solution.py:90
  65.6 3.2 %accumulate_second.1 = (f32[256,1792]{1,0:T(8,128)S(1)}, f32[256,1792]{1,0:T(8,128)S(1)}) custom-call(bf16[168,1792]{1,0:T(8,128)(2,1)S(1)} %copy-done, bf16[168,1792]{1,0:T(8,128)(2,1)S(1)} %collective-permute-done.refs_1_, bf16[168,1792]{1,0:T(8,128)(2,1)S(1)} %collective-permute-done.1.refs_2_, bf16[144,1792]{1,0:T(8,128)(2,1)S(1)} %collective-permute-done.2.refs_3_, ...), custom_call_target="tpu_custom_call" | custom-call | flops 1000 | bytes 1000 | tf_op jit(solution)/shard_map/accumulate_second/pallas_call | solution.py:125
  68.8 3.9 %accumulate_third.1 = (f32[256,1792]{1,0:T(8,128)S(1)}, f32[256,1792]{1,0:T(8,128)S(1)}) custom-call(bf16[168,1792]{1,0:T(8,128)(2,1)S(1)} %copy-done, bf16[168,1792]{1,0:T(8,128)(2,1)S(1)} %collective-permute-done.refs_1_, bf16[168,1792]{1,0:T(8,128)(2,1)S(1)} %collective-permute-done.1.refs_2_, ...), custom_call_target="tpu_custom_call", output_to_operand_aliasing={{0}: (10, {}), {1}: (11, {})} | custom-call | flops 1000 | bytes 1000 | tf_op jit(solution)/shard_map/accumulate_third/pallas_call | solution.py:125
  72.7 0.2 collective-permute-done.10.refs_3_.refs_1_
  73.0 2.3 %collective-permute-done.11.refs_4_.refs_2_ = bf16[144,1792]{1,0:T(8,128)(2,1)S(1)} collective-permute-done((bf16[144,1792]{1,0:T(8,128)(2,1)S(1)}, bf16[144,1792]{1,0:T(8,128)(2,1)S(1)}, u32[]{:S(2)}, u32[]{:S(2)}) %collective-permute-start.11) | collective-permute-done | bytes 516128 | tf_op jit(solution)/shard_map/ppermute | solution.py:90
  75.3 0.1 collect_fifth.1
  75.4 1.6 %collective-permute-start.13 = (bf16[96,1792]{1,0:T(8,128)(2,1)S(1)}, bf16[96,1792]{1,0:T(8,128)(2,1)S(1)}, u32[]{:S(2)}, u32[]{:S(2)}) collective-permute-start(bf16[96,1792]{1,0:T(8,128)(2,1)S(1)} %get-tuple-element.124), channel_id=1, source_target_pairs={{0,2},{1,3},{2,0},{3,1},{4,6},{5,7},{6,4},{7,5},{8,10},{9,11},{10,... | collective-permute-start | bytes 1032200 | tf_op jit(solution)/shard_map/ppermute | solution.py:90
  76.9 0.6 collective-permute-start.14
  77.5 2.0 %accumulate_fourth.1 = (f32[256,1792]{1,0:T(8,128)S(1)}, f32[256,1792]{1,0:T(8,128)S(1)}) custom-call(bf16[144,1792]{1,0:T(8,128)(2,1)S(1)} %collective-permute-done.9.refs_2_.refs_0_, bf16[144,1792]{1,0:T(8,128)(2,1)S(1)} %collective-permute-done.10.refs_3_.refs_1_, ...), custom_call_target="tpu_custom_call", output_to_operand_aliasing={{0}: (5, {}), {1}: (6, {})} | custom-call | flops 1000 | bytes 1000 | tf_op jit(solution)/shard_map/accumulate_fourth/pallas_call | solution.py:125
  79.5 6.7 %collective-permute-done.15.refs_3_ = bf16[72,1792]{1,0:T(8,128)(2,1)S(1)} collective-permute-done((bf16[72,1792]{1,0:T(8,128)(2,1)S(1)}, bf16[72,1792]{1,0:T(8,128)(2,1)S(1)}, u32[]{:S(2)}, u32[]{:S(2)}) %collective-permute-start.15) | collective-permute-done | bytes 258080 | tf_op jit(solution)/shard_map/ppermute | solution.py:90
  86.2 1.0 %finish_other.1 = bf16[256,1792]{1,0:T(8,128)(2,1)S(1)} custom-call(bf16[96,1792]{1,0:T(8,128)(2,1)S(1)} %collective-permute-done.13.refs_0_, bf16[96,1792]{1,0:T(8,128)(2,1)S(1)} %collective-permute-done.14.refs_1_, bf16[144,1792]{1,0:T(8,128)(2,1)S(1)} %collective-permute-done.11.refs_4_.refs_2_, bf16[72,1792]{1,0:T(8,128)(2,1)S(1)} %collective-permute-done.15.refs_3_, ...), custom_call_target="tpu_custom_call" | custom-call | flops 1000 | bytes 1000 | tf_op jit(solution)/shard_map/finish_other/pallas_call | solution.py:125
  87.2 0.1 collective-permute-start.16
  87.3 1.4 %finish_own.1.kept_ref = f32[256,1792]{1,0:T(8,128)S(1)} custom-call(bf16[96,1792]{1,0:T(8,128)(2,1)S(1)} %collective-permute-done.13.refs_0_, bf16[96,1792]{1,0:T(8,128)(2,1)S(1)} %collective-permute-done.14.refs_1_, bf16[144,1792]{1,0:T(8,128)(2,1)S(1)} %collective-permute-done.11.refs_4_.refs_2_, ...), custom_call_target="tpu_custom_call", output_to_operand_aliasing={{}: (5, {})} | custom-call | flops 1000 | bytes 1000 | tf_op jit(solution)/shard_map/finish_own/pallas_call | solution.py:125
  88.7 1.1 %collective-permute-done.16.given_ref = bf16[256,1792]{1,0:T(8,128)(2,1)S(1)} collective-permute-done((bf16[256,1792]{1,0:T(8,128)(2,1)S(1)}, bf16[256,1792]{1,0:T(8,128)(2,1)S(1)}, u32[]{:S(2)}, u32[]{:S(2)}) %collective-permute-start.16) | collective-permute-done | bytes 917536 | tf_op jit(solution)/shard_map/ppermute | solution.py:90
  89.8 1.2 %final.1 = bf16[256,1792]{1,0:T(8,128)(2,1)} custom-call(s32[1]{0:T(128)S(6)} %copy.27.count_ref, f32[256,1792]{1,0:T(8,128)S(1)} %finish_own.1.kept_ref, bf16[256,1792]{1,0:T(8,128)(2,1)S(1)} %collective-permute-done.16.given_ref), custom_call_target="tpu_custom_call" | custom-call | flops 1000 | bytes 1000 | tf_op jit(solution)/shard_map/final/pallas_call | solution.py:125
  (23 shorter events, 0.1 us)
Async XLA Ops:
  2.8 19.5 %collective-permute-start = (bf16[168,1792]{1,0:T(8,128)(2,1)}, bf16[168,1792]{1,0:T(8,128)(2,1)S(1)}, u32[]{:S(2)}, u32[]{:S(2)}) collective-permute-start(bf16[168,1792]{1,0:T(8,128)(2,1)} %get-tuple-element.73.refs_0_), channel_id=1, source_target_pairs={{0,2},{1,3},{2,0},{3,1},{4,6},{5,7},{6,4},{7,5},{8,10},{9,11},{10,... | collective-permute-start | bytes 1806344 | tf_op jit(solution)/shard_map/ppermute | solution.py:90
  5.8 16.5 %collective-permute-start.1 = (bf16[168,1792]{1,0:T(8,128)(2,1)}, bf16[168,1792]{1,0:T(8,128)(2,1)S(1)}, u32[]{:S(2)}, u32[]{:S(2)}) collective-permute-start(bf16[168,1792]{1,0:T(8,128)(2,1)} %get-tuple-element.73.refs_0_), channel_id=1, source_target_pairs={{0,4},{1,5},{2,6},{3,7},{4,0},{5,1},{6,2},{7,3},{8,12},{9,13},{10,... | collective-permute-start | bytes 1806344 | tf_op jit(solution)/shard_map/ppermute | solution.py:90
  7.4 15.0 %collective-permute-start.2 = (bf16[144,1792]{1,0:T(8,128)(2,1)}, bf16[144,1792]{1,0:T(8,128)(2,1)S(1)}, u32[]{:S(2)}, u32[]{:S(2)}) collective-permute-start(bf16[144,1792]{1,0:T(8,128)(2,1)} %get-tuple-element.74), channel_id=1, source_target_pairs={{0,8},{1,9},{2,10},{3,11},{4,12},{5,13},{6,14},{7,15},{8,16},{9,17... | collective-permute-start | bytes 1548296 | tf_op jit(solution)/shard_map/ppermute | solution.py:90
  9.7 1.2 %copy-start.1 = (bf16[1,256,1792]{2,1,0:T(8,128)(2,1)S(1)}, bf16[1,256,1792]{2,1,0:T(8,128)(2,1)}, u32[]{:S(2)}) copy-start(bf16[1,256,1792]{2,1,0:T(8,128)(2,1)} %param.13) | copy-start | bytes 2752516
  10.8 1.9 %copy-start.3 = (bf16[1792,896]{1,0:T(8,128)(2,1)S(1)}, bf16[1792,896]{1,0:T(8,128)(2,1)}, u32[]{:S(2)}) copy-start(bf16[1792,896]{1,0:T(8,128)(2,1)} %value_ref.1) | copy-start | bytes 9633796
  12.7 1.0 %copy-start.5 = (bf16[1792,128]{1,0:T(8,128)(2,1)S(1)}, bf16[1792,128]{1,0:T(8,128)(2,1)}, u32[]{:S(2)}) copy-start(bf16[1792,128]{1,0:T(8,128)(2,1)} %query_ref.1) | copy-start | bytes 1376260
  13.8 1.0 %copy-start.6 = (bf16[1792,128]{1,0:T(8,128)(2,1)S(1)}, bf16[1792,128]{1,0:T(8,128)(2,1)}, u32[]{:S(2)}) copy-start(bf16[1792,128]{1,0:T(8,128)(2,1)} %key_ref.1) | copy-start | bytes 1376260
  14.8 0.7 copy-start.7
  15.5 6.8 %copy-start = (bf16[168,1792]{1,0:T(8,128)(2,1)S(1)}, bf16[168,1792]{1,0:T(8,128)(2,1)}, u32[]{:S(2)}) copy-start(bf16[168,1792]{1,0:T(8,128)(2,1)} %get-tuple-element.73.refs_0_) | copy-start | bytes 1806340
  15.5 13.8 %copy-start.4 = (bf16[896,1792]{1,0:T(8,128)(2,1)S(1)}, bf16[896,1792]{1,0:T(8,128)(2,1)}, u32[]{:S(2)}) copy-start(bf16[896,1792]{1,0:T(8,128)(2,1)} %out_ref.1) | copy-start | bytes 9633796
  19.3 6.4 %copy-start.9 = (f32[1792]{0:T(1024)S(1)}, f32[1792]{0:T(1024)}, u32[]{:S(2)}) copy-start(f32[1792]{0:T(1024)} %param.22) | copy-start | bytes 21508
  19.3 6.4 %copy-start.8 = (f32[1,256,8]{1,2,0:T(8,128)S(1)}, f32[1,256,8]{1,2,0:T(8,128)}, u32[]{:S(2)}) copy-start(f32[1,256,8]{1,2,0:T(8,128)} %param.15) | copy-start | bytes 24580
  19.3 10.1 %copy-start.2 = (bf16[1,256,1792]{2,1,0:T(8,128)(2,1)S(1)}, bf16[1,256,1792]{2,1,0:T(8,128)(2,1)}, u32[]{:S(2)}) copy-start(bf16[1,256,1792]{2,1,0:T(8,128)(2,1)} %param.13) | copy-start | bytes 2752516
  22.5 20.2 %collective-permute-start.4 = (bf16[232,1792]{1,0:T(8,128)(2,1)S(1)}, bf16[232,1792]{1,0:T(8,128)(2,1)S(1)}, u32[]{:S(2)}, u32[]{:S(2)}) collective-permute-start(bf16[232,1792]{1,0:T(8,128)(2,1)S(1)} %get-tuple-element.85), channel_id=1, source_target_pairs={{0,4},{1,5},{2,6},{3,7},{4,0},{5,1},{6,2},{7,3},{8,12},{9,13},{10,... | collective-permute-start | bytes 2494472 | tf_op jit(solution)/shard_map/ppermute | solution.py:90
  23.1 19.6 %collective-permute-start.3 = (bf16[224,1792]{1,0:T(8,128)(2,1)S(1)}, bf16[224,1792]{1,0:T(8,128)(2,1)S(1)}, u32[]{:S(2)}, u32[]{:S(2)}) collective-permute-start(bf16[224,1792]{1,0:T(8,128)(2,1)S(1)} %get-tuple-element.84), channel_id=1, source_target_pairs={{0,2},{1,3},{2,0},{3,1},{4,6},{5,7},{6,4},{7,5},{8,10},{9,11},{10,... | collective-permute-start | bytes 2408456 | tf_op jit(solution)/shard_map/ppermute | solution.py:90
  23.6 19.1 %collective-permute-start.5 = (bf16[216,1792]{1,0:T(8,128)(2,1)S(1)}, bf16[216,1792]{1,0:T(8,128)(2,1)S(1)}, u32[]{:S(2)}, u32[]{:S(2)}) collective-permute-start(bf16[216,1792]{1,0:T(8,128)(2,1)S(1)} %get-tuple-element.86), channel_id=1, source_target_pairs={{0,8},{1,9},{2,10},{3,11},{4,12},{5,13},{6,14},{7,15},{8,16},{9,17... | collective-permute-start | bytes 2322440 | tf_op jit(solution)/shard_map/ppermute | solution.py:90
  42.9 20.0 %collective-permute-start.8 = (bf16[240,1792]{1,0:T(8,128)(2,1)S(1)}, bf16[240,1792]{1,0:T(8,128)(2,1)S(1)}, u32[]{:S(2)}, u32[]{:S(2)}) collective-permute-start(bf16[240,1792]{1,0:T(8,128)(2,1)S(1)} %get-tuple-element.104), channel_id=1, source_target_pairs={{0,8},{1,9},{2,10},{3,11},{4,12},{5,13},{6,14},{7,15},{8,16},{9,17... | collective-permute-start | bytes 2580488 | tf_op jit(solution)/shard_map/ppermute | solution.py:90
  43.0 17.0 %collective-permute-start.6 = (bf16[224,1792]{1,0:T(8,128)(2,1)S(1)}, bf16[224,1792]{1,0:T(8,128)(2,1)S(1)}, u32[]{:S(2)}, u32[]{:S(2)}) collective-permute-start(bf16[224,1792]{1,0:T(8,128)(2,1)S(1)} %get-tuple-element.102), channel_id=1, source_target_pairs={{0,2},{1,3},{2,0},{3,1},{4,6},{5,7},{6,4},{7,5},{8,10},{9,11},{10,... | collective-permute-start | bytes 2408456 | tf_op jit(solution)/shard_map/ppermute | solution.py:90
  44.3 15.3 %collective-permute-start.7 = (bf16[208,1792]{1,0:T(8,128)(2,1)S(1)}, bf16[208,1792]{1,0:T(8,128)(2,1)S(1)}, u32[]{:S(2)}, u32[]{:S(2)}) collective-permute-start(bf16[208,1792]{1,0:T(8,128)(2,1)S(1)} %get-tuple-element.103), channel_id=1, source_target_pairs={{0,4},{1,5},{2,6},{3,7},{4,0},{5,1},{6,2},{7,3},{8,12},{9,13},{10,... | collective-permute-start | bytes 2236424 | tf_op jit(solution)/shard_map/ppermute | solution.py:90
  45.8 19.8 %collective-permute-start.12 = (bf16[256,1792]{1,0:T(8,128)(2,1)S(1)}, bf16[256,1792]{1,0:T(8,128)(2,1)S(1)}, u32[]{:S(2)}, u32[]{:S(2)}) collective-permute-start(bf16[256,1792]{1,0:T(8,128)(2,1)S(1)} %get-tuple-element.116.refs_7_.refs_8_.refs_3_.refs_4_), channel_id=1, source_target_pairs={{0,1},{1,0},{2,3},{3,2},{4,5},{5,4},{6,7},{7,6},{8,9},{9,8},{10,11... | collective-permute-start | bytes 2752520 | tf_op jit(solution)/shard_map/ppermute | solution.py:90
  63.0 10.0 %collective-permute-start.10 = (bf16[144,1792]{1,0:T(8,128)(2,1)S(1)}, bf16[144,1792]{1,0:T(8,128)(2,1)S(1)}, u32[]{:S(2)}, u32[]{:S(2)}) collective-permute-start(bf16[144,1792]{1,0:T(8,128)(2,1)S(1)} %get-tuple-element.111), channel_id=1, source_target_pairs={{0,4},{1,5},{2,6},{3,7},{4,0},{5,1},{6,2},{7,3},{8,12},{9,13},{10,... | collective-permute-start | bytes 1548296 | tf_op jit(solution)/shard_map/ppermute | solution.py:90
  64.1 11.2 %collective-permute-start.11 = (bf16[144,1792]{1,0:T(8,128)(2,1)S(1)}, bf16[144,1792]{1,0:T(8,128)(2,1)S(1)}, u32[]{:S(2)}, u32[]{:S(2)}) collective-permute-start(bf16[144,1792]{1,0:T(8,128)(2,1)S(1)} %get-tuple-element.112), channel_id=1, source_target_pairs={{0,8},{1,9},{2,10},{3,11},{4,12},{5,13},{6,14},{7,15},{8,16},{9,17... | collective-permute-start | bytes 1548296 | tf_op jit(solution)/shard_map/ppermute | solution.py:90
  64.1 11.2 %collective-permute-start.9 = (bf16[144,1792]{1,0:T(8,128)(2,1)S(1)}, bf16[144,1792]{1,0:T(8,128)(2,1)S(1)}, u32[]{:S(2)}, u32[]{:S(2)}) collective-permute-start(bf16[144,1792]{1,0:T(8,128)(2,1)S(1)} %get-tuple-element.111), channel_id=1, source_target_pairs={{0,2},{1,3},{2,0},{3,1},{4,6},{5,7},{6,4},{7,5},{8,10},{9,11},{10,... | collective-permute-start | bytes 1548296 | tf_op jit(solution)/shard_map/ppermute | solution.py:90
  75.4 10.8 %collective-permute-start.13 = (bf16[96,1792]{1,0:T(8,128)(2,1)S(1)}, bf16[96,1792]{1,0:T(8,128)(2,1)S(1)}, u32[]{:S(2)}, u32[]{:S(2)}) collective-permute-start(bf16[96,1792]{1,0:T(8,128)(2,1)S(1)} %get-tuple-element.124), channel_id=1, source_target_pairs={{0,2},{1,3},{2,0},{3,1},{4,6},{5,7},{6,4},{7,5},{8,10},{9,11},{10,... | collective-permute-start | bytes 1032200 | tf_op jit(solution)/shard_map/ppermute | solution.py:90
  76.9 9.3 %collective-permute-start.14 = (bf16[96,1792]{1,0:T(8,128)(2,1)S(1)}, bf16[96,1792]{1,0:T(8,128)(2,1)S(1)}, u32[]{:S(2)}, u32[]{:S(2)}) collective-permute-start(bf16[96,1792]{1,0:T(8,128)(2,1)S(1)} %get-tuple-element.125), channel_id=1, source_target_pairs={{0,4},{1,5},{2,6},{3,7},{4,0},{5,1},{6,2},{7,3},{8,12},{9,13},{10,... | collective-permute-start | bytes 1032200 | tf_op jit(solution)/shard_map/ppermute | solution.py:90
  77.5 8.7 %collective-permute-start.15 = (bf16[72,1792]{1,0:T(8,128)(2,1)S(1)}, bf16[72,1792]{1,0:T(8,128)(2,1)S(1)}, u32[]{:S(2)}, u32[]{:S(2)}) collective-permute-start(bf16[72,1792]{1,0:T(8,128)(2,1)S(1)} %get-tuple-element.126), channel_id=1, source_target_pairs={{0,8},{1,9},{2,10},{3,11},{4,12},{5,13},{6,14},{7,15},{8,16},{9,17... | collective-permute-start | bytes 774152 | tf_op jit(solution)/shard_map/ppermute | solution.py:90
  87.2 2.5 %collective-permute-start.16 = (bf16[256,1792]{1,0:T(8,128)(2,1)S(1)}, bf16[256,1792]{1,0:T(8,128)(2,1)S(1)}, u32[]{:S(2)}, u32[]{:S(2)}) collective-permute-start(bf16[256,1792]{1,0:T(8,128)(2,1)S(1)} %finish_other.1), channel_id=1, source_target_pairs={{0,1},{1,0},{2,3},{3,2},{4,5},{5,4},{6,7},{7,6},{8,9},{9,8},{10,11... | collective-permute-start | bytes 2752520 | tf_op jit(solution)/shard_map/ppermute | solution.py:90

commit v5 on v4

--- a/solution.py
+++ b/solution.py
@@ -452,21 +452,21 @@
     return kernel_call(functools.partial(collect_body, plans), name, shapes, *arrays)
 
 
-def shard_body(main, gate_ref, up_ref, down_ref, shard_ref, main_ref, *rest):
+def shard_body(main, gate_ref, up_ref, down_ref, shard_ref, *rest):
     buffers, sems = rest[:3], rest[3]
-    copies = [
-        pltpu.make_async_copy(source, buffer, sems.at[k])
-        for k, (source, buffer) in enumerate(zip((gate_ref, up_ref, down_ref), buffers))
-    ]
-    for copy in copies:
-        copy.start()
+    sources = (gate_ref, up_ref, down_ref)
+    copies = []
+    for k, source in enumerate(sources):
+        copies.append(pltpu.make_async_copy(source, buffers[k], sems.at[k]))
+        copies[-1].start()
+    for k, source in enumerate(sources):
+        place = shard_ref.at[pl.ds(k * main, main), :]
+        copies.append(pltpu.make_async_copy(source.at[pl.ds(0, main), :], place, sems.at[3 + k]))
+        copies[-1].start()
     for copy in copies:
         copy.wait()
-    arrays = [buffer[...].astype(jnp.float32) for buffer in buffers]
-    tops = [array[:main] for array in arrays]
-    ends = [array[main:] for array in arrays]
-    shard_ref[...] = jnp.concatenate(tops + ends, axis=0).astype(jnp.bfloat16)
-    main_ref[...] = jnp.concatenate(tops, axis=0).astype(jnp.bfloat16)
+    ends = [buffer[...].astype(jnp.float32)[main:] for buffer in buffers]
+    shard_ref[3 * main :, :] = jnp.concatenate(ends, axis=0).astype(jnp.bfloat16)
 
 
 def final_body(step, count_ref, kept_ref, given_ref, out_ref):
@@ -513,18 +513,18 @@
     narrow = full - wide
     cut = main + 2 * main // 3
 
-    shard, shard_main = kernel_call(
+    shard = kernel_call(
         functools.partial(shard_body, main),
         "shard",
-        (like(full, model, jnp.bfloat16), like(wide, model, jnp.bfloat16)),
+        like(full, model, jnp.bfloat16),
         gate_weight.T,
         up_weight.T,
         down_weight.T,
         specs=[pl.BlockSpec(memory_space=pl.ANY)] * 3,
-        scratch=[pltpu.VMEM((units, model), jnp.bfloat16)] * 3 + [pltpu.SemaphoreType.DMA((3,))],
+        scratch=[pltpu.VMEM((units, model), jnp.bfloat16)] * 3 + [pltpu.SemaphoreType.DMA((6,))],
         mib=56,
     )
-    near, far, deep = slot((flip_near, shard), (flip_far, shard), (next_plane, shard_main))
+    near, far, deep = slot((flip_near, shard), (flip_far, shard), (next_plane, shard))
 
     lead = 16
     if spans > 1:
@@ -543,7 +543,7 @@
         (
             ((3, 0, wide), (2, 0, cut)),
             ((3, 0, wide), (1, cut, full)),
-            ((3, 0, wide), (0, wide, full), (1, wide, full), (2, wide, full)),
+            ((3, 0, full), (1, wide, full), (2, wide, full)),
         ),
         "collect_second",
     )
@@ -595,20 +595,20 @@
         (far2, deep2),
         (
             ((1, 0, wide),),
-            ((1, wide, wide + 4 * narrow), (0, wide + wide - cut - main, wide + wide - cut)),
+            ((1, full, full + 3 * narrow), (0, wide + wide - cut - main, wide + wide - cut)),
         ),
         "collect_fourth",
     )
     near3, far3, deep3 = slot((flip_near, deep3_main), (flip_far, deep3_main), (next_plane, line))
     acc = accumulate(
         rows,
-        (shard, near, far, far1, deep1, near2, far2, deep2),
-        [runs(i, 0, main) for i in (5, 6, 7)]
-        + list(split_runs((5, wide), (6, wide), main))
-        + [runs(i, wide, edge) for i in (0, 1, 2)]
-        + [runs(3, wide + wide - cut, edge)]
-        + [runs(4, wide + k * narrow, edge) for k in range(3)]
-        + [runs(7, wide + k * narrow, edge) for k in range(4)],
+        (shard, near, far, deep, far1, deep1, near2, far2, deep2),
+        [runs(i, 0, main) for i in (6, 7, 8)]
+        + list(split_runs((6, wide), (7, wide), main))
+        + [runs(i, wide, edge) for i in (0, 1, 2, 3)]
+        + [runs(4, wide + wide - cut, edge)]
+        + [runs(5, wide + k * narrow, edge) for k in range(3)]
+        + [runs(8, wide + k * narrow, edge) for k in range(4)],
         tuple(acc),
         jnp.float32,
         "accumulate_third",
@@ -620,7 +620,7 @@
         (
             ((1, 0, main), (3, 0, main)),
             ((0, main, 2 * main), (2, main, 2 * main)),
-            ((4, 3 * narrow, 4 * narrow + main),),
+            ((4, 2 * narrow, 3 * narrow + main),),
         ),
         "collect_fifth",
     )
@@ -628,14 +628,14 @@
     acc = accumulate(
         rows,
         (near3, far3, deep3),
-        [runs(0, 0, main), runs(1, 0, main)] + [runs(2, k * narrow, edge) for k in range(4)],
+        [runs(0, 0, main), runs(1, 0, main)] + [runs(2, k * narrow, edge) for k in range(3)],
         tuple(acc),
         jnp.float32,
         "accumulate_fourth",
     )
     weights = (near4, far4, deep3, deep4)
     last = [
-        ((0, 0, main), (1, 0, main), (2, 4 * narrow, 4 * narrow + main)),
+        ((0, 0, main), (1, 0, main), (2, 3 * narrow, 3 * narrow + main)),
         ((0, main, 2 * main), (1, main, 2 * main), (3, narrow, narrow + main)),
         runs(3, 0, edge),
     ]

time: 91.4 us -> 92.4 us (1.011)
  waiting for transfers between devices: 41.3 us -> 45.4 us
  starting transfers between devices: 16.3 us -> 14.4 us
  local copies, waits for them, and re-layouts: 6.61 us -> 5.43 us
    ppermute x17, waiting for transfers between devices: 41.3 us -> 45.4 us  [permute(): return lax.ppermute(array, 'req', [(i, target(i)) for i in range(count)])]
    ppermute x17, starting transfers between devices: 16.3 us -> 14.4 us  [permute(): return lax.ppermute(array, 'req', [(i, target(i)) for i in range(count)])]
    unnamed x20 -> x18, local copies, waits for them, and re-layouts: 5.89 us -> 4.71 us
  transfers between devices with their start and end apart: 17 -> 17, of which waited for: 9 -> 10; matrix products, arithmetic and copies ran while one was open for 1% -> 1% of each run, Pallas kernels for 23% -> 22%
where the time goes in v5:
time: 92.4 us; the launch traced here: 92 us
  waiting for transfers between devices  45.4 us (49%)
  Pallas kernels  25.3 us (27%)
  starting transfers between devices  14.4 us (16%)
  local copies, waits for them, and re-layouts  5.43 us (6%)
  between operations  1.46 us (2%)
    ppermute x17, waiting for transfers between devices, permute(): return lax.ppermute(array, 'req', [(i, target(i)) for i in range(count)])  45.4 us
    pallas_call x14, Pallas kernels, kernel_call(): pl.pallas_call(body, out_shape=out_shape, in_specs=specs or vmem(len(oper...  25.3 us
    ppermute x17, starting transfers between devices, permute(): return lax.ppermute(array, 'req', [(i, target(i)) for i in range(count)])  14.4 us
    unnamed x18, local copies, waits for them, and re-layouts  4.71 us
  transfers between devices with their start and end apart: 17, of which 10 were waited for; matrix products, arithmetic and copies ran while one was open for 1% of the time, Pallas kernels for 22%

profile of v5, /device:TPU:0, one launch (start us, length us, event | category | flops | bytes accessed | tf_op | source)
XLA Modules:
  0.0 92.0 jit_solution(15438365429270860092)
XLA Ops:
  0.6 2.3 %shard.1.refs_0_ = bf16[168,1792]{1,0:T(8,128)(2,1)} custom-call(bf16[56,1792]{1,0:T(8,128)(2,1)} %bitcast.17, bf16[56,1792]{1,0:T(8,128)(2,1)} %bitcast.18, bf16[56,1792]{1,0:T(8,128)(2,1)} %bitcast.19), custom_call_target="tpu_custom_call" | custom-call | flops 1000 | bytes 1000 | tf_op jit(solution)/shard_map/shard/pallas_call | solution.py:125
  2.9 3.0 %collective-permute-start = (bf16[168,1792]{1,0:T(8,128)(2,1)}, bf16[168,1792]{1,0:T(8,128)(2,1)S(1)}, u32[]{:S(2)}, u32[]{:S(2)}) collective-permute-start(bf16[168,1792]{1,0:T(8,128)(2,1)} %shard.1.refs_0_), channel_id=1, source_target_pairs={{0,2},{1,3},{2,0},{3,1},{4,6},{5,7},{6,4},{7,5},{8,10},{9,11},{10,... | collective-permute-start | bytes 1806344 | tf_op jit(solution)/shard_map/ppermute | solution.py:90
  5.9 1.5 %collective-permute-start.1 = (bf16[168,1792]{1,0:T(8,128)(2,1)}, bf16[168,1792]{1,0:T(8,128)(2,1)S(1)}, u32[]{:S(2)}, u32[]{:S(2)}) collective-permute-start(bf16[168,1792]{1,0:T(8,128)(2,1)} %shard.1.refs_0_), channel_id=1, source_target_pairs={{0,4},{1,5},{2,6},{3,7},{4,0},{5,1},{6,2},{7,3},{8,12},{9,13},{10,... | collective-permute-start | bytes 1806344 | tf_op jit(solution)/shard_map/ppermute | solution.py:90
  7.4 1.6 %collective-permute-start.2 = (bf16[168,1792]{1,0:T(8,128)(2,1)}, bf16[168,1792]{1,0:T(8,128)(2,1)S(1)}, u32[]{:S(2)}, u32[]{:S(2)}) collective-permute-start(bf16[168,1792]{1,0:T(8,128)(2,1)} %shard.1.refs_0_), channel_id=1, source_target_pairs={{0,8},{1,9},{2,10},{3,11},{4,12},{5,13},{6,14},{7,15},{8,16},{9,17... | collective-permute-start | bytes 1806344 | tf_op jit(solution)/shard_map/ppermute | solution.py:90
  9.0 0.7 broadcast_in_dim.16.gain_ref
  9.7 0.0 copy-start.2
  9.7 1.9 %copy-done.2 = bf16[1792,896]{1,0:T(8,128)(2,1)S(1)} copy-done((bf16[1792,896]{1,0:T(8,128)(2,1)S(1)}, bf16[1792,896]{1,0:T(8,128)(2,1)}, u32[]{:S(2)}) %copy-start.2) | copy-done | bytes 3211288
  11.7 1.0 %copy-done.4 = bf16[1792,128]{1,0:T(8,128)(2,1)S(1)} copy-done((bf16[1792,128]{1,0:T(8,128)(2,1)S(1)}, bf16[1792,128]{1,0:T(8,128)(2,1)}, u32[]{:S(2)}) %copy-start.4) | copy-done | bytes 458776
  12.7 1.0 %copy-done.5 = bf16[1792,128]{1,0:T(8,128)(2,1)S(1)} copy-done((bf16[1792,128]{1,0:T(8,128)(2,1)S(1)}, bf16[1792,128]{1,0:T(8,128)(2,1)}, u32[]{:S(2)}) %copy-start.5) | copy-done | bytes 458776
  13.7 0.7 copy-done.6
  14.4 3.7 %project.1 = (bf16[256,128]{1,0:T(8,128)(2,1)S(1)}, bf16[256,128]{1,0:T(8,128)(2,1)S(1)}, bf16[256,896]{1,0:T(8,128)(2,1)S(1)}) custom-call(bf16[256,1792]{1,0:T(8,128)(2,1)S(1)} %bitcast.13, bf16[16,1792]{1,0:T(8,128)(2,1)S(1)} %broadcast_in_dim.15.edge_ref, f32[1,1792]{1,0:T(1,128)S(1)} %broadcast_in_dim.16.gain_ref, f32[3,1792]{1,0:T(4,128)S(1)} %copy-done.6, ...), custom_call_target="tpu_custom_call" | custom-call | flops 1000 | bytes 1000 | tf_op jit(solution)/shard_map/project/pallas_call | solution.py:125
  18.2 0.0 copy-start.8
  18.2 0.0 copy-start.7
  18.2 1.5 %collective-permute-done.refs_1_ = bf16[168,1792]{1,0:T(8,128)(2,1)S(1)} collective-permute-done((bf16[168,1792]{1,0:T(8,128)(2,1)}, bf16[168,1792]{1,0:T(8,128)(2,1)S(1)}, u32[]{:S(2)}, u32[]{:S(2)}) %collective-permute-start) | collective-permute-done | bytes 602144 | tf_op jit(solution)/shard_map/ppermute | solution.py:90
  19.7 1.5 %collective-permute-done.1.refs_2_ = bf16[168,1792]{1,0:T(8,128)(2,1)S(1)} collective-permute-done((bf16[168,1792]{1,0:T(8,128)(2,1)}, bf16[168,1792]{1,0:T(8,128)(2,1)S(1)}, u32[]{:S(2)}, u32[]{:S(2)}) %collective-permute-start.1) | collective-permute-done | bytes 602144 | tf_op jit(solution)/shard_map/ppermute | solution.py:90
  21.2 3.1 %collective-permute-done.2.refs_3_ = bf16[168,1792]{1,0:T(8,128)(2,1)S(1)} collective-permute-done((bf16[168,1792]{1,0:T(8,128)(2,1)}, bf16[168,1792]{1,0:T(8,128)(2,1)S(1)}, u32[]{:S(2)}, u32[]{:S(2)}) %collective-permute-start.2) | collective-permute-done | bytes 602144 | tf_op jit(solution)/shard_map/ppermute | solution.py:90
  24.3 0.2 collect_second.1
  24.5 0.6 collective-permute-start.4
  25.0 0.5 collective-permute-start.3
  26.3 3.6 %attend.1 = (f32[256,896]{1,0:T(8,128)S(1)}, f32[256,8]{1,0:T(8,128)S(1)}, f32[273,1,896]{2,1,0:T(1,128)}, f32[8,273]{1,0:T(8,128)}) custom-call(s32[1]{0:T(128)S(6)} %copy.27.count_ref, f32[8,256]{1,0:T(8,128)S(1)} %bitcast.15, bf16[256,128]{1,0:T(8,128)(2,1)S(1)} %get-tuple-element.86.queries_ref, bf16[256,128]{1,0:T(8,128)(2,1)S(1)} %get-tuple-element.87.keys_ref, ...), custom_call_target="tpu_custom_call" | custom-call | flops 1000 | bytes 1000 | tf_op jit(solution)/shard_map/attend/pallas_call | solution.py:125
  29.9 2.6 %mix.1 = (bf16[256,1792]{1,0:T(8,128)(2,1)S(1)}, bf16[256,1792]{1,0:T(8,128)(2,1)S(1)}) custom-call(f32[256,896]{1,0:T(8,128)S(1)} %get-tuple-element.89.numer_ref, f32[256,8]{1,0:T(8,128)S(1)} %get-tuple-element.90.denom_ref, bf16[256,1792]{1,0:T(8,128)(2,1)S(1)} %bitcast.14, bf16[896,1792]{1,0:T(8,128)(2,1)S(1)} %copy-done.3, ...), custom_call_target="tpu_custom_call" | custom-call | flops 1000 | bytes 1000 | tf_op jit(solution)/shard_map/mix/pallas_call | solution.py:125
  32.5 12.2 %collective-permute-done.5.refs_2_.refs_6_.refs_5_ = bf16[216,1792]{1,0:T(8,128)(2,1)S(1)} collective-permute-done((bf16[216,1792]{1,0:T(8,128)(2,1)S(1)}, bf16[216,1792]{1,0:T(8,128)(2,1)S(1)}, u32[]{:S(2)}, u32[]{:S(2)}) %collective-permute-start.5) | collective-permute-done | bytes 774176 | tf_op jit(solution)/shard_map/ppermute | solution.py:90
  44.7 0.2 collect_third.1
  44.8 0.1 collective-permute-start.8
  44.9 1.4 %collective-permute-start.6 = (bf16[224,1792]{1,0:T(8,128)(2,1)S(1)}, bf16[224,1792]{1,0:T(8,128)(2,1)S(1)}, u32[]{:S(2)}, u32[]{:S(2)}) collective-permute-start(bf16[224,1792]{1,0:T(8,128)(2,1)S(1)} %get-tuple-element.98), channel_id=1, source_target_pairs={{0,2},{1,3},{2,0},{3,1},{4,6},{5,7},{6,4},{7,5},{8,10},{9,11},{10,... | collective-permute-start | bytes 2408456 | tf_op jit(solution)/shard_map/ppermute | solution.py:90
  46.2 1.5 %collective-permute-start.7 = (bf16[208,1792]{1,0:T(8,128)(2,1)S(1)}, bf16[208,1792]{1,0:T(8,128)(2,1)S(1)}, u32[]{:S(2)}, u32[]{:S(2)}) collective-permute-start(bf16[208,1792]{1,0:T(8,128)(2,1)S(1)} %get-tuple-element.99), channel_id=1, source_target_pairs={{0,4},{1,5},{2,6},{3,7},{4,0},{5,1},{6,2},{7,3},{8,12},{9,13},{10,... | collective-permute-start | bytes 2236424 | tf_op jit(solution)/shard_map/ppermute | solution.py:90
  47.8 0.0 collective-permute-start.12
  47.8 13.7 %collective-permute-done.7.refs_0_.refs_7_.refs_1_ = bf16[208,1792]{1,0:T(8,128)(2,1)S(1)} collective-permute-done((bf16[208,1792]{1,0:T(8,128)(2,1)S(1)}, bf16[208,1792]{1,0:T(8,128)(2,1)S(1)}, u32[]{:S(2)}, u32[]{:S(2)}) %collective-permute-start.7) | collective-permute-done | bytes 745504 | tf_op jit(solution)/shard_map/ppermute | solution.py:90
  61.5 0.4 collective-permute-done.6.refs_6_.refs_0_
  61.9 2.9 %collective-permute-done.8.refs_1_.refs_8_ = bf16[240,1792]{1,0:T(8,128)(2,1)S(1)} collective-permute-done((bf16[240,1792]{1,0:T(8,128)(2,1)S(1)}, bf16[240,1792]{1,0:T(8,128)(2,1)S(1)}, u32[]{:S(2)}, u32[]{:S(2)}) %collective-permute-start.8) | collective-permute-done | bytes 860192 | tf_op jit(solution)/shard_map/ppermute | solution.py:90
  64.9 0.1 collect_fourth.1
  64.9 1.2 %collective-permute-start.10 = (bf16[144,1792]{1,0:T(8,128)(2,1)S(1)}, bf16[144,1792]{1,0:T(8,128)(2,1)S(1)}, u32[]{:S(2)}, u32[]{:S(2)}) collective-permute-start(bf16[144,1792]{1,0:T(8,128)(2,1)S(1)} %get-tuple-element.107), channel_id=1, source_target_pairs={{0,4},{1,5},{2,6},{3,7},{4,0},{5,1},{6,2},{7,3},{8,12},{9,13},{10,... | collective-permute-start | bytes 1548296 | tf_op jit(solution)/shard_map/ppermute | solution.py:90
  66.1 1.5 %collective-permute-start.9 = (bf16[144,1792]{1,0:T(8,128)(2,1)S(1)}, bf16[144,1792]{1,0:T(8,128)(2,1)S(1)}, u32[]{:S(2)}, u32[]{:S(2)}) collective-permute-start(bf16[144,1792]{1,0:T(8,128)(2,1)S(1)} %get-tuple-element.107), channel_id=1, source_target_pairs={{0,2},{1,3},{2,0},{3,1},{4,6},{5,7},{6,4},{7,5},{8,10},{9,11},{10,... | collective-permute-start | bytes 1548296 | tf_op jit(solution)/shard_map/ppermute | solution.py:90
  67.6 3.2 %accumulate_second.1 = (f32[256,1792]{1,0:T(8,128)S(1)}, f32[256,1792]{1,0:T(8,128)S(1)}) custom-call(bf16[168,1792]{1,0:T(8,128)(2,1)S(1)} %copy-done, bf16[168,1792]{1,0:T(8,128)(2,1)S(1)} %collective-permute-done.refs_1_, bf16[168,1792]{1,0:T(8,128)(2,1)S(1)} %collective-permute-done.1.refs_2_, bf16[168,1792]{1,0:T(8,128)(2,1)S(1)} %collective-permute-done.2.refs_3_, ...), custom_call_target="tpu_custom_call" | custom-call | flops 1000 | bytes 1000 | tf_op jit(solution)/shard_map/accumulate_second/pallas_call | solution.py:125
  70.8 3.9 %accumulate_third.1 = (f32[256,1792]{1,0:T(8,128)S(1)}, f32[256,1792]{1,0:T(8,128)S(1)}) custom-call(bf16[168,1792]{1,0:T(8,128)(2,1)S(1)} %copy-done, bf16[168,1792]{1,0:T(8,128)(2,1)S(1)} %collective-permute-done.refs_1_, bf16[168,1792]{1,0:T(8,128)(2,1)S(1)} %collective-permute-done.1.refs_2_, ...), custom_call_target="tpu_custom_call", output_to_operand_aliasing={{0}: (11, {}), {1}: (12, {})} | custom-call | flops 1000 | bytes 1000 | tf_op jit(solution)/shard_map/accumulate_third/pallas_call | solution.py:125
  74.7 2.9 %collective-permute-done.11.refs_4_.refs_2_ = bf16[120,1792]{1,0:T(8,128)(2,1)S(1)} collective-permute-done((bf16[120,1792]{1,0:T(8,128)(2,1)S(1)}, bf16[120,1792]{1,0:T(8,128)(2,1)S(1)}, u32[]{:S(2)}, u32[]{:S(2)}) %collective-permute-start.11) | collective-permute-done | bytes 430112 | tf_op jit(solution)/shard_map/ppermute | solution.py:90
  77.6 0.1 collect_fifth.1
  77.6 1.3 %collective-permute-start.13 = (bf16[96,1792]{1,0:T(8,128)(2,1)S(1)}, bf16[96,1792]{1,0:T(8,128)(2,1)S(1)}, u32[]{:S(2)}, u32[]{:S(2)}) collective-permute-start(bf16[96,1792]{1,0:T(8,128)(2,1)S(1)} %get-tuple-element.120), channel_id=1, source_target_pairs={{0,2},{1,3},{2,0},{3,1},{4,6},{5,7},{6,4},{7,5},{8,10},{9,11},{10,... | collective-permute-start | bytes 1032200 | tf_op jit(solution)/shard_map/ppermute | solution.py:90
  78.9 0.2 collective-permute-start.14
  79.2 0.0 collective-permute-start.15
  79.2 2.0 %accumulate_fourth.1 = (f32[256,1792]{1,0:T(8,128)S(1)}, f32[256,1792]{1,0:T(8,128)S(1)}) custom-call(bf16[144,1792]{1,0:T(8,128)(2,1)S(1)} %collective-permute-done.9.refs_2_.refs_0_, bf16[144,1792]{1,0:T(8,128)(2,1)S(1)} %collective-permute-done.10.refs_3_.refs_1_, ...), custom_call_target="tpu_custom_call", output_to_operand_aliasing={{0}: (5, {}), {1}: (6, {})} | custom-call | flops 1000 | bytes 1000 | tf_op jit(solution)/shard_map/accumulate_fourth/pallas_call | solution.py:125
  81.1 6.1 %collective-permute-done.15.refs_3_ = bf16[72,1792]{1,0:T(8,128)(2,1)S(1)} collective-permute-done((bf16[72,1792]{1,0:T(8,128)(2,1)S(1)}, bf16[72,1792]{1,0:T(8,128)(2,1)S(1)}, u32[]{:S(2)}, u32[]{:S(2)}) %collective-permute-start.15) | collective-permute-done | bytes 258080 | tf_op jit(solution)/shard_map/ppermute | solution.py:90
  87.3 0.0 collective-permute-done.13.refs_0_
  87.3 1.0 %finish_other.1 = bf16[256,1792]{1,0:T(8,128)(2,1)S(1)} custom-call(bf16[96,1792]{1,0:T(8,128)(2,1)S(1)} %collective-permute-done.13.refs_0_, bf16[96,1792]{1,0:T(8,128)(2,1)S(1)} %collective-permute-done.14.refs_1_, bf16[120,1792]{1,0:T(8,128)(2,1)S(1)} %collective-permute-done.11.refs_4_.refs_2_, bf16[72,1792]{1,0:T(8,128)(2,1)S(1)} %collective-permute-done.15.refs_3_, ...), custom_call_target="tpu_custom_call" | custom-call | flops 1000 | bytes 1000 | tf_op jit(solution)/shard_map/finish_other/pallas_call | solution.py:125
  88.3 0.1 collective-permute-start.16
  88.4 1.4 %finish_own.1.kept_ref = f32[256,1792]{1,0:T(8,128)S(1)} custom-call(bf16[96,1792]{1,0:T(8,128)(2,1)S(1)} %collective-permute-done.13.refs_0_, bf16[96,1792]{1,0:T(8,128)(2,1)S(1)} %collective-permute-done.14.refs_1_, bf16[120,1792]{1,0:T(8,128)(2,1)S(1)} %collective-permute-done.11.refs_4_.refs_2_, ...), custom_call_target="tpu_custom_call", output_to_operand_aliasing={{}: (5, {})} | custom-call | flops 1000 | bytes 1000 | tf_op jit(solution)/shard_map/finish_own/pallas_call | solution.py:125
  89.8 1.1 %collective-permute-done.16.given_ref = bf16[256,1792]{1,0:T(8,128)(2,1)S(1)} collective-permute-done((bf16[256,1792]{1,0:T(8,128)(2,1)S(1)}, bf16[256,1792]{1,0:T(8,128)(2,1)S(1)}, u32[]{:S(2)}, u32[]{:S(2)}) %collective-permute-start.16) | collective-permute-done | bytes 917536 | tf_op jit(solution)/shard_map/ppermute | solution.py:90
  90.8 1.2 %final.1 = bf16[256,1792]{1,0:T(8,128)(2,1)} custom-call(s32[1]{0:T(128)S(6)} %copy.27.count_ref, f32[256,1792]{1,0:T(8,128)S(1)} %finish_own.1.kept_ref, bf16[256,1792]{1,0:T(8,128)(2,1)S(1)} %collective-permute-done.16.given_ref), custom_call_target="tpu_custom_call" | custom-call | flops 1000 | bytes 1000 | tf_op jit(solution)/shard_map/final/pallas_call | solution.py:125
  (21 shorter events, 0.1 us)
Async XLA Ops:
  0.6 9.1 %copy-start.1 = (bf16[1,256,1792]{2,1,0:T(8,128)(2,1)S(1)}, bf16[1,256,1792]{2,1,0:T(8,128)(2,1)}, u32[]{:S(2)}) copy-start(bf16[1,256,1792]{2,1,0:T(8,128)(2,1)} %param.13) | copy-start | bytes 2752516
  2.9 16.8 %collective-permute-start = (bf16[168,1792]{1,0:T(8,128)(2,1)}, bf16[168,1792]{1,0:T(8,128)(2,1)S(1)}, u32[]{:S(2)}, u32[]{:S(2)}) collective-permute-start(bf16[168,1792]{1,0:T(8,128)(2,1)} %shard.1.refs_0_), channel_id=1, source_target_pairs={{0,2},{1,3},{2,0},{3,1},{4,6},{5,7},{6,4},{7,5},{8,10},{9,11},{10,... | collective-permute-start | bytes 1806344 | tf_op jit(solution)/shard_map/ppermute | solution.py:90
  5.9 15.3 %collective-permute-start.1 = (bf16[168,1792]{1,0:T(8,128)(2,1)}, bf16[168,1792]{1,0:T(8,128)(2,1)S(1)}, u32[]{:S(2)}, u32[]{:S(2)}) collective-permute-start(bf16[168,1792]{1,0:T(8,128)(2,1)} %shard.1.refs_0_), channel_id=1, source_target_pairs={{0,4},{1,5},{2,6},{3,7},{4,0},{5,1},{6,2},{7,3},{8,12},{9,13},{10,... | collective-permute-start | bytes 1806344 | tf_op jit(solution)/shard_map/ppermute | solution.py:90
  7.4 16.9 %collective-permute-start.2 = (bf16[168,1792]{1,0:T(8,128)(2,1)}, bf16[168,1792]{1,0:T(8,128)(2,1)S(1)}, u32[]{:S(2)}, u32[]{:S(2)}) collective-permute-start(bf16[168,1792]{1,0:T(8,128)(2,1)} %shard.1.refs_0_), channel_id=1, source_target_pairs={{0,8},{1,9},{2,10},{3,11},{4,12},{5,13},{6,14},{7,15},{8,16},{9,17... | collective-permute-start | bytes 1806344 | tf_op jit(solution)/shard_map/ppermute | solution.py:90
  9.7 1.9 %copy-start.2 = (bf16[1792,896]{1,0:T(8,128)(2,1)S(1)}, bf16[1792,896]{1,0:T(8,128)(2,1)}, u32[]{:S(2)}) copy-start(bf16[1792,896]{1,0:T(8,128)(2,1)} %value_ref.1) | copy-start | bytes 9633796
  11.6 1.0 %copy-start.4 = (bf16[1792,128]{1,0:T(8,128)(2,1)S(1)}, bf16[1792,128]{1,0:T(8,128)(2,1)}, u32[]{:S(2)}) copy-start(bf16[1792,128]{1,0:T(8,128)(2,1)} %query_ref.1) | copy-start | bytes 1376260
  12.7 1.0 %copy-start.5 = (bf16[1792,128]{1,0:T(8,128)(2,1)S(1)}, bf16[1792,128]{1,0:T(8,128)(2,1)}, u32[]{:S(2)}) copy-start(bf16[1792,128]{1,0:T(8,128)(2,1)} %key_ref.1) | copy-start | bytes 1376260
  13.7 0.7 copy-start.6
  14.4 9.9 %copy-start = (bf16[168,1792]{1,0:T(8,128)(2,1)S(1)}, bf16[168,1792]{1,0:T(8,128)(2,1)}, u32[]{:S(2)}) copy-start(bf16[168,1792]{1,0:T(8,128)(2,1)} %shard.1.refs_0_) | copy-start | bytes 1806340
  14.4 15.5 %copy-start.3 = (bf16[896,1792]{1,0:T(8,128)(2,1)S(1)}, bf16[896,1792]{1,0:T(8,128)(2,1)}, u32[]{:S(2)}) copy-start(bf16[896,1792]{1,0:T(8,128)(2,1)} %out_ref.1) | copy-start | bytes 9633796
  18.2 8.0 %copy-start.8 = (f32[1792]{0:T(1024)S(1)}, f32[1792]{0:T(1024)}, u32[]{:S(2)}) copy-start(f32[1792]{0:T(1024)} %param.22) | copy-start | bytes 21508
  18.2 8.1 %copy-start.7 = (f32[1,256,8]{1,2,0:T(8,128)S(1)}, f32[1,256,8]{1,2,0:T(8,128)}, u32[]{:S(2)}) copy-start(f32[1,256,8]{1,2,0:T(8,128)} %param.15) | copy-start | bytes 24580
  24.5 20.2 %collective-permute-start.4 = (bf16[232,1792]{1,0:T(8,128)(2,1)S(1)}, bf16[232,1792]{1,0:T(8,128)(2,1)S(1)}, u32[]{:S(2)}, u32[]{:S(2)}) collective-permute-start(bf16[232,1792]{1,0:T(8,128)(2,1)S(1)} %get-tuple-element.81), channel_id=1, source_target_pairs={{0,4},{1,5},{2,6},{3,7},{4,0},{5,1},{6,2},{7,3},{8,12},{9,13},{10,... | collective-permute-start | bytes 2494472 | tf_op jit(solution)/shard_map/ppermute | solution.py:90
  25.0 19.6 %collective-permute-start.3 = (bf16[224,1792]{1,0:T(8,128)(2,1)S(1)}, bf16[224,1792]{1,0:T(8,128)(2,1)S(1)}, u32[]{:S(2)}, u32[]{:S(2)}) collective-permute-start(bf16[224,1792]{1,0:T(8,128)(2,1)S(1)} %get-tuple-element.80), channel_id=1, source_target_pairs={{0,2},{1,3},{2,0},{3,1},{4,6},{5,7},{6,4},{7,5},{8,10},{9,11},{10,... | collective-permute-start | bytes 2408456 | tf_op jit(solution)/shard_map/ppermute | solution.py:90
  25.6 19.1 %collective-permute-start.5 = (bf16[216,1792]{1,0:T(8,128)(2,1)S(1)}, bf16[216,1792]{1,0:T(8,128)(2,1)S(1)}, u32[]{:S(2)}, u32[]{:S(2)}) collective-permute-start(bf16[216,1792]{1,0:T(8,128)(2,1)S(1)} %get-tuple-element.82), channel_id=1, source_target_pairs={{0,8},{1,9},{2,10},{3,11},{4,12},{5,13},{6,14},{7,15},{8,16},{9,17... | collective-permute-start | bytes 2322440 | tf_op jit(solution)/shard_map/ppermute | solution.py:90
  44.8 20.0 %collective-permute-start.8 = (bf16[240,1792]{1,0:T(8,128)(2,1)S(1)}, bf16[240,1792]{1,0:T(8,128)(2,1)S(1)}, u32[]{:S(2)}, u32[]{:S(2)}) collective-permute-start(bf16[240,1792]{1,0:T(8,128)(2,1)S(1)} %get-tuple-element.100), channel_id=1, source_target_pairs={{0,8},{1,9},{2,10},{3,11},{4,12},{5,13},{6,14},{7,15},{8,16},{9,17... | collective-permute-start | bytes 2580488 | tf_op jit(solution)/shard_map/ppermute | solution.py:90
  44.9 17.0 %collective-permute-start.6 = (bf16[224,1792]{1,0:T(8,128)(2,1)S(1)}, bf16[224,1792]{1,0:T(8,128)(2,1)S(1)}, u32[]{:S(2)}, u32[]{:S(2)}) collective-permute-start(bf16[224,1792]{1,0:T(8,128)(2,1)S(1)} %get-tuple-element.98), channel_id=1, source_target_pairs={{0,2},{1,3},{2,0},{3,1},{4,6},{5,7},{6,4},{7,5},{8,10},{9,11},{10,... | collective-permute-start | bytes 2408456 | tf_op jit(solution)/shard_map/ppermute | solution.py:90
  46.2 15.2 %collective-permute-start.7 = (bf16[208,1792]{1,0:T(8,128)(2,1)S(1)}, bf16[208,1792]{1,0:T(8,128)(2,1)S(1)}, u32[]{:S(2)}, u32[]{:S(2)}) collective-permute-start(bf16[208,1792]{1,0:T(8,128)(2,1)S(1)} %get-tuple-element.99), channel_id=1, source_target_pairs={{0,4},{1,5},{2,6},{3,7},{4,0},{5,1},{6,2},{7,3},{8,12},{9,13},{10,... | collective-permute-start | bytes 2236424 | tf_op jit(solution)/shard_map/ppermute | solution.py:90
  47.8 19.8 %collective-permute-start.12 = (bf16[256,1792]{1,0:T(8,128)(2,1)S(1)}, bf16[256,1792]{1,0:T(8,128)(2,1)S(1)}, u32[]{:S(2)}, u32[]{:S(2)}) collective-permute-start(bf16[256,1792]{1,0:T(8,128)(2,1)S(1)} %get-tuple-element.112.refs_7_.refs_9_.refs_3_.refs_4_), channel_id=1, source_target_pairs={{0,1},{1,0},{2,3},{3,2},{4,5},{5,4},{6,7},{7,6},{8,9},{9,8},{10,11... | collective-permute-start | bytes 2752520 | tf_op jit(solution)/shard_map/ppermute | solution.py:90
  64.9 12.6 %collective-permute-start.10 = (bf16[144,1792]{1,0:T(8,128)(2,1)S(1)}, bf16[144,1792]{1,0:T(8,128)(2,1)S(1)}, u32[]{:S(2)}, u32[]{:S(2)}) collective-permute-start(bf16[144,1792]{1,0:T(8,128)(2,1)S(1)} %get-tuple-element.107), channel_id=1, source_target_pairs={{0,4},{1,5},{2,6},{3,7},{4,0},{5,1},{6,2},{7,3},{8,12},{9,13},{10,... | collective-permute-start | bytes 1548296 | tf_op jit(solution)/shard_map/ppermute | solution.py:90
  66.1 11.5 %collective-permute-start.9 = (bf16[144,1792]{1,0:T(8,128)(2,1)S(1)}, bf16[144,1792]{1,0:T(8,128)(2,1)S(1)}, u32[]{:S(2)}, u32[]{:S(2)}) collective-permute-start(bf16[144,1792]{1,0:T(8,128)(2,1)S(1)} %get-tuple-element.107), channel_id=1, source_target_pairs={{0,2},{1,3},{2,0},{3,1},{4,6},{5,7},{6,4},{7,5},{8,10},{9,11},{10,... | collective-permute-start | bytes 1548296 | tf_op jit(solution)/shard_map/ppermute | solution.py:90
  67.6 10.0 %collective-permute-start.11 = (bf16[120,1792]{1,0:T(8,128)(2,1)S(1)}, bf16[120,1792]{1,0:T(8,128)(2,1)S(1)}, u32[]{:S(2)}, u32[]{:S(2)}) collective-permute-start(bf16[120,1792]{1,0:T(8,128)(2,1)S(1)} %get-tuple-element.108), channel_id=1, source_target_pairs={{0,8},{1,9},{2,10},{3,11},{4,12},{5,13},{6,14},{7,15},{8,16},{9,17... | collective-permute-start | bytes 1290248 | tf_op jit(solution)/shard_map/ppermute | solution.py:90
  77.6 9.6 %collective-permute-start.13 = (bf16[96,1792]{1,0:T(8,128)(2,1)S(1)}, bf16[96,1792]{1,0:T(8,128)(2,1)S(1)}, u32[]{:S(2)}, u32[]{:S(2)}) collective-permute-start(bf16[96,1792]{1,0:T(8,128)(2,1)S(1)} %get-tuple-element.120), channel_id=1, source_target_pairs={{0,2},{1,3},{2,0},{3,1},{4,6},{5,7},{6,4},{7,5},{8,10},{9,11},{10,... | collective-permute-start | bytes 1032200 | tf_op jit(solution)/shard_map/ppermute | solution.py:90
  78.9 8.4 %collective-permute-start.14 = (bf16[96,1792]{1,0:T(8,128)(2,1)S(1)}, bf16[96,1792]{1,0:T(8,128)(2,1)S(1)}, u32[]{:S(2)}, u32[]{:S(2)}) collective-permute-start(bf16[96,1792]{1,0:T(8,128)(2,1)S(1)} %get-tuple-element.121), channel_id=1, source_target_pairs={{0,4},{1,5},{2,6},{3,7},{4,0},{5,1},{6,2},{7,3},{8,12},{9,13},{10,... | collective-permute-start | bytes 1032200 | tf_op jit(solution)/shard_map/ppermute | solution.py:90
  79.2 8.1 %collective-permute-start.15 = (bf16[72,1792]{1,0:T(8,128)(2,1)S(1)}, bf16[72,1792]{1,0:T(8,128)(2,1)S(1)}, u32[]{:S(2)}, u32[]{:S(2)}) collective-permute-start(bf16[72,1792]{1,0:T(8,128)(2,1)S(1)} %get-tuple-element.122), channel_id=1, source_target_pairs={{0,8},{1,9},{2,10},{3,11},{4,12},{5,13},{6,14},{7,15},{8,16},{9,17... | collective-permute-start | bytes 774152 | tf_op jit(solution)/shard_map/ppermute | solution.py:90
  88.3 2.5 %collective-permute-start.16 = (bf16[256,1792]{1,0:T(8,128)(2,1)S(1)}, bf16[256,1792]{1,0:T(8,128)(2,1)S(1)}, u32[]{:S(2)}, u32[]{:S(2)}) collective-permute-start(bf16[256,1792]{1,0:T(8,128)(2,1)S(1)} %finish_other.1), channel_id=1, source_target_pairs={{0,1},{1,0},{2,3},{3,2},{4,5},{5,4},{6,7},{7,6},{8,9},{9,8},{10,11... | collective-permute-start | bytes 2752520 | tf_op jit(solution)/shard_map/ppermute | solution.py:90

commit v6 on v4

--- a/solution.py
+++ b/solution.py
@@ -95,11 +95,11 @@
 
 
 def flip_near(array):
-    return permute(array, lambda i: i ^ 2)
+    return permute(array, lambda i: i ^ (4 if i % 2 else 2))
 
 
 def flip_far(array):
-    return permute(array, lambda i: i ^ 4)
+    return permute(array, lambda i: i ^ (2 if i % 2 else 4))
 
 
 def next_plane(array):

time: 91.4 us -> 95 us (1.039)
  waiting for transfers between devices: 41.3 us -> 46.7 us
  starting transfers between devices: 16.3 us -> 14.4 us
    ppermute x17, waiting for transfers between devices: 41.3 us -> 46.7 us  [permute(): return lax.ppermute(array, 'req', [(i, target(i)) for i in range(count)])]
    ppermute x17, starting transfers between devices: 16.3 us -> 14.4 us  [permute(): return lax.ppermute(array, 'req', [(i, target(i)) for i in range(count)])]
  transfers between devices with their start and end apart: 17 -> 17, of which waited for: 9 -> 8; matrix products, arithmetic and copies ran while one was open for 1% -> 1% of each run, Pallas kernels for 23% -> 22%
where the time goes in v6:
time: 95 us; the launch traced here: 94.5 us
  waiting for transfers between devices  46.7 us (49%)
  Pallas kernels  25.3 us (27%)
  starting transfers between devices  14.4 us (15%)
  local copies, waits for them, and re-layouts  6.61 us (7%)
  between operations  1.45 us (2%)
    ppermute x17, waiting for transfers between devices, permute(): return lax.ppermute(array, 'req', [(i, target(i)) for i in range(count)])  46.7 us
    pallas_call x14, Pallas kernels, kernel_call(): pl.pallas_call(body, out_shape=out_shape, in_specs=specs or vmem(len(oper...  25.3 us
    ppermute x17, starting transfers between devices, permute(): return lax.ppermute(array, 'req', [(i, target(i)) for i in range(count)])  14.4 us
    unnamed x20, local copies, waits for them, and re-layouts  5.89 us
  transfers between devices with their start and end apart: 17, of which 8 were waited for; matrix products, arithmetic and copies ran while one was open for 1% of the time, Pallas kernels for 22%

profile of v6, /device:TPU:0, one launch (start us, length us, event | category | flops | bytes accessed | tf_op | source)
XLA Modules:
  0.0 94.5 jit_solution(8636908822584072098)
XLA Ops:
  0.6 2.2 %shard.1 = (bf16[168,1792]{1,0:T(8,128)(2,1)}, bf16[144,1792]{1,0:T(8,128)(2,1)}) custom-call(bf16[56,1792]{1,0:T(8,128)(2,1)} %bitcast.17, bf16[56,1792]{1,0:T(8,128)(2,1)} %bitcast.18, bf16[56,1792]{1,0:T(8,128)(2,1)} %bitcast.19), custom_call_target="tpu_custom_call" | custom-call | flops 1000 | bytes 1000 | tf_op jit(solution)/shard_map/shard/pallas_call | solution.py:125
  2.8 3.0 %collective-permute-start = (bf16[168,1792]{1,0:T(8,128)(2,1)}, bf16[168,1792]{1,0:T(8,128)(2,1)S(1)}, u32[]{:S(2)}, u32[]{:S(2)}) collective-permute-start(bf16[168,1792]{1,0:T(8,128)(2,1)} %get-tuple-element.73.refs_0_), channel_id=1, source_target_pairs={{0,2},{1,5},{2,0},{3,7},{4,6},{5,1},{6,4},{7,3},{8,10},{9,13},{10,... | collective-permute-start | bytes 1806344 | tf_op jit(solution)/shard_map/ppermute | solution.py:90
  5.8 1.5 %collective-permute-start.1 = (bf16[168,1792]{1,0:T(8,128)(2,1)}, bf16[168,1792]{1,0:T(8,128)(2,1)S(1)}, u32[]{:S(2)}, u32[]{:S(2)}) collective-permute-start(bf16[168,1792]{1,0:T(8,128)(2,1)} %get-tuple-element.73.refs_0_), channel_id=1, source_target_pairs={{0,4},{1,3},{2,6},{3,1},{4,0},{5,7},{6,2},{7,5},{8,12},{9,11},{10,... | collective-permute-start | bytes 1806344 | tf_op jit(solution)/shard_map/ppermute | solution.py:90
  7.4 1.6 %collective-permute-start.2 = (bf16[144,1792]{1,0:T(8,128)(2,1)}, bf16[144,1792]{1,0:T(8,128)(2,1)S(1)}, u32[]{:S(2)}, u32[]{:S(2)}) collective-permute-start(bf16[144,1792]{1,0:T(8,128)(2,1)} %get-tuple-element.74), channel_id=1, source_target_pairs={{0,8},{1,9},{2,10},{3,11},{4,12},{5,13},{6,14},{7,15},{8,16},{9,17... | collective-permute-start | bytes 1548296 | tf_op jit(solution)/shard_map/ppermute | solution.py:90
  8.9 0.7 broadcast_in_dim.16.gain_ref
  9.7 0.0 copy-start.1
  9.7 1.2 %copy-done.1 = bf16[1,256,1792]{2,1,0:T(8,128)(2,1)S(1)} copy-done((bf16[1,256,1792]{2,1,0:T(8,128)(2,1)S(1)}, bf16[1,256,1792]{2,1,0:T(8,128)(2,1)}, u32[]{:S(2)}) %copy-start.1) | copy-done | bytes 917528
  10.8 1.9 %copy-done.3 = bf16[1792,896]{1,0:T(8,128)(2,1)S(1)} copy-done((bf16[1792,896]{1,0:T(8,128)(2,1)S(1)}, bf16[1792,896]{1,0:T(8,128)(2,1)}, u32[]{:S(2)}) %copy-start.3) | copy-done | bytes 3211288
  12.7 1.0 %copy-done.5 = bf16[1792,128]{1,0:T(8,128)(2,1)S(1)} copy-done((bf16[1792,128]{1,0:T(8,128)(2,1)S(1)}, bf16[1792,128]{1,0:T(8,128)(2,1)}, u32[]{:S(2)}) %copy-start.5) | copy-done | bytes 458776
  13.8 1.0 %copy-done.6 = bf16[1792,128]{1,0:T(8,128)(2,1)S(1)} copy-done((bf16[1792,128]{1,0:T(8,128)(2,1)S(1)}, bf16[1792,128]{1,0:T(8,128)(2,1)}, u32[]{:S(2)}) %copy-start.6) | copy-done | bytes 458776
  14.8 0.7 copy-done.7
  15.5 3.7 %project.1 = (bf16[256,128]{1,0:T(8,128)(2,1)S(1)}, bf16[256,128]{1,0:T(8,128)(2,1)S(1)}, bf16[256,896]{1,0:T(8,128)(2,1)S(1)}) custom-call(bf16[256,1792]{1,0:T(8,128)(2,1)S(1)} %bitcast.13, bf16[16,1792]{1,0:T(8,128)(2,1)S(1)} %broadcast_in_dim.15.edge_ref, f32[1,1792]{1,0:T(1,128)S(1)} %broadcast_in_dim.16.gain_ref, f32[3,1792]{1,0:T(4,128)S(1)} %copy-done.7, ...), custom_call_target="tpu_custom_call" | custom-call | flops 1000 | bytes 1000 | tf_op jit(solution)/shard_map/project/pallas_call | solution.py:125
  19.3 0.0 copy-start.9
  19.3 0.0 copy-start.8
  19.3 0.0 copy-start.2
  19.3 3.1 %collective-permute-done.2.refs_3_ = bf16[144,1792]{1,0:T(8,128)(2,1)S(1)} collective-permute-done((bf16[144,1792]{1,0:T(8,128)(2,1)}, bf16[144,1792]{1,0:T(8,128)(2,1)S(1)}, u32[]{:S(2)}, u32[]{:S(2)}) %collective-permute-start.2) | collective-permute-done | bytes 516128 | tf_op jit(solution)/shard_map/ppermute | solution.py:90
  22.4 0.2 collect_second.1
  22.5 0.6 collective-permute-start.4
  23.1 0.5 collective-permute-start.3
  23.6 1.3 %collective-permute-start.5 = (bf16[216,1792]{1,0:T(8,128)(2,1)S(1)}, bf16[216,1792]{1,0:T(8,128)(2,1)S(1)}, u32[]{:S(2)}, u32[]{:S(2)}) collective-permute-start(bf16[216,1792]{1,0:T(8,128)(2,1)S(1)} %get-tuple-element.86), channel_id=1, source_target_pairs={{0,8},{1,9},{2,10},{3,11},{4,12},{5,13},{6,14},{7,15},{8,16},{9,17... | collective-permute-start | bytes 2322440 | tf_op jit(solution)/shard_map/ppermute | solution.py:90
  25.6 3.7 %attend.1 = (f32[256,896]{1,0:T(8,128)S(1)}, f32[256,8]{1,0:T(8,128)S(1)}, f32[273,1,896]{2,1,0:T(1,128)}, f32[8,273]{1,0:T(8,128)}) custom-call(s32[1]{0:T(128)S(6)} %copy.27.count_ref, f32[8,256]{1,0:T(8,128)S(1)} %bitcast.15, bf16[256,128]{1,0:T(8,128)(2,1)S(1)} %get-tuple-element.90.queries_ref, bf16[256,128]{1,0:T(8,128)(2,1)S(1)} %get-tuple-element.91.keys_ref, ...), custom_call_target="tpu_custom_call" | custom-call | flops 1000 | bytes 1000 | tf_op jit(solution)/shard_map/attend/pallas_call | solution.py:125
  29.3 2.6 %mix.1 = (bf16[256,1792]{1,0:T(8,128)(2,1)S(1)}, bf16[256,1792]{1,0:T(8,128)(2,1)S(1)}) custom-call(f32[256,896]{1,0:T(8,128)S(1)} %get-tuple-element.93.numer_ref, f32[256,8]{1,0:T(8,128)S(1)} %get-tuple-element.94.denom_ref, bf16[256,1792]{1,0:T(8,128)(2,1)S(1)} %bitcast.14, bf16[896,1792]{1,0:T(8,128)(2,1)S(1)} %copy-done.4, ...), custom_call_target="tpu_custom_call" | custom-call | flops 1000 | bytes 1000 | tf_op jit(solution)/shard_map/mix/pallas_call | solution.py:125
  32.0 11.6 %collective-permute-done.5.refs_2_.refs_6_.refs_4_ = bf16[216,1792]{1,0:T(8,128)(2,1)S(1)} collective-permute-done((bf16[216,1792]{1,0:T(8,128)(2,1)S(1)}, bf16[216,1792]{1,0:T(8,128)(2,1)S(1)}, u32[]{:S(2)}, u32[]{:S(2)}) %collective-permute-start.5) | collective-permute-done | bytes 774176 | tf_op jit(solution)/shard_map/ppermute | solution.py:90
  43.6 0.0 collective-permute-done.3.refs_0_.refs_4_
  43.6 0.2 collect_third.1
  43.7 0.3 collective-permute-start.8
  44.0 0.9 collective-permute-start.6
  44.9 1.2 %collective-permute-start.7 = (bf16[208,1792]{1,0:T(8,128)(2,1)S(1)}, bf16[208,1792]{1,0:T(8,128)(2,1)S(1)}, u32[]{:S(2)}, u32[]{:S(2)}) collective-permute-start(bf16[208,1792]{1,0:T(8,128)(2,1)S(1)} %get-tuple-element.103), channel_id=1, source_target_pairs={{0,4},{1,3},{2,6},{3,1},{4,0},{5,7},{6,2},{7,5},{8,12},{9,11},{10,... | collective-permute-start | bytes 2236424 | tf_op jit(solution)/shard_map/ppermute | solution.py:90
  46.1 16.9 %collective-permute-done.7.refs_0_.refs_6_.refs_1_ = bf16[208,1792]{1,0:T(8,128)(2,1)S(1)} collective-permute-done((bf16[208,1792]{1,0:T(8,128)(2,1)S(1)}, bf16[208,1792]{1,0:T(8,128)(2,1)S(1)}, u32[]{:S(2)}, u32[]{:S(2)}) %collective-permute-start.7) | collective-permute-done | bytes 745504 | tf_op jit(solution)/shard_map/ppermute | solution.py:90
  63.0 0.0 collective-permute-done.6.refs_5_.refs_0_
  63.0 2.4 %collective-permute-done.8.refs_1_.refs_7_ = bf16[240,1792]{1,0:T(8,128)(2,1)S(1)} collective-permute-done((bf16[240,1792]{1,0:T(8,128)(2,1)S(1)}, bf16[240,1792]{1,0:T(8,128)(2,1)S(1)}, u32[]{:S(2)}, u32[]{:S(2)}) %collective-permute-start.8) | collective-permute-done | bytes 860192 | tf_op jit(solution)/shard_map/ppermute | solution.py:90
  65.4 0.1 collect_fourth.1
  65.5 1.3 %collective-permute-start.10 = (bf16[144,1792]{1,0:T(8,128)(2,1)S(1)}, bf16[144,1792]{1,0:T(8,128)(2,1)S(1)}, u32[]{:S(2)}, u32[]{:S(2)}) collective-permute-start(bf16[144,1792]{1,0:T(8,128)(2,1)S(1)} %get-tuple-element.111), channel_id=1, source_target_pairs={{0,4},{1,3},{2,6},{3,1},{4,0},{5,7},{6,2},{7,5},{8,12},{9,11},{10,... | collective-permute-start | bytes 1548296 | tf_op jit(solution)/shard_map/ppermute | solution.py:90
  66.7 0.0 collective-permute-start.11
  66.8 3.2 %accumulate_second.1 = (f32[256,1792]{1,0:T(8,128)S(1)}, f32[256,1792]{1,0:T(8,128)S(1)}) custom-call(bf16[168,1792]{1,0:T(8,128)(2,1)S(1)} %copy-done, bf16[168,1792]{1,0:T(8,128)(2,1)S(1)} %collective-permute-done.refs_1_, bf16[168,1792]{1,0:T(8,128)(2,1)S(1)} %collective-permute-done.1.refs_2_, bf16[144,1792]{1,0:T(8,128)(2,1)S(1)} %collective-permute-done.2.refs_3_, ...), custom_call_target="tpu_custom_call" | custom-call | flops 1000 | bytes 1000 | tf_op jit(solution)/shard_map/accumulate_second/pallas_call | solution.py:125
  70.0 3.9 %accumulate_third.1 = (f32[256,1792]{1,0:T(8,128)S(1)}, f32[256,1792]{1,0:T(8,128)S(1)}) custom-call(bf16[168,1792]{1,0:T(8,128)(2,1)S(1)} %copy-done, bf16[168,1792]{1,0:T(8,128)(2,1)S(1)} %collective-permute-done.refs_1_, bf16[168,1792]{1,0:T(8,128)(2,1)S(1)} %collective-permute-done.1.refs_2_, ...), custom_call_target="tpu_custom_call", output_to_operand_aliasing={{0}: (10, {}), {1}: (11, {})} | custom-call | flops 1000 | bytes 1000 | tf_op jit(solution)/shard_map/accumulate_third/pallas_call | solution.py:125
  73.9 4.2 %collective-permute-done.10.refs_3_.refs_1_ = bf16[144,1792]{1,0:T(8,128)(2,1)S(1)} collective-permute-done((bf16[144,1792]{1,0:T(8,128)(2,1)S(1)}, bf16[144,1792]{1,0:T(8,128)(2,1)S(1)}, u32[]{:S(2)}, u32[]{:S(2)}) %collective-permute-start.10) | collective-permute-done | bytes 516128 | tf_op jit(solution)/shard_map/ppermute | solution.py:90
  78.1 1.0 %collective-permute-done.11.refs_4_.refs_2_ = bf16[144,1792]{1,0:T(8,128)(2,1)S(1)} collective-permute-done((bf16[144,1792]{1,0:T(8,128)(2,1)S(1)}, bf16[144,1792]{1,0:T(8,128)(2,1)S(1)}, u32[]{:S(2)}, u32[]{:S(2)}) %collective-permute-start.11) | collective-permute-done | bytes 516128 | tf_op jit(solution)/shard_map/ppermute | solution.py:90
  79.1 0.1 collect_fifth.1
  79.2 1.6 %collective-permute-start.13 = (bf16[96,1792]{1,0:T(8,128)(2,1)S(1)}, bf16[96,1792]{1,0:T(8,128)(2,1)S(1)}, u32[]{:S(2)}, u32[]{:S(2)}) collective-permute-start(bf16[96,1792]{1,0:T(8,128)(2,1)S(1)} %get-tuple-element.124), channel_id=1, source_target_pairs={{0,2},{1,5},{2,0},{3,7},{4,6},{5,1},{6,4},{7,3},{8,10},{9,13},{10,... | collective-permute-start | bytes 1032200 | tf_op jit(solution)/shard_map/ppermute | solution.py:90
  80.7 0.7 collective-permute-start.14
  81.4 2.0 %accumulate_fourth.1 = (f32[256,1792]{1,0:T(8,128)S(1)}, f32[256,1792]{1,0:T(8,128)S(1)}) custom-call(bf16[144,1792]{1,0:T(8,128)(2,1)S(1)} %collective-permute-done.9.refs_2_.refs_0_, bf16[144,1792]{1,0:T(8,128)(2,1)S(1)} %collective-permute-done.10.refs_3_.refs_1_, ...), custom_call_target="tpu_custom_call", output_to_operand_aliasing={{0}: (5, {}), {1}: (6, {})} | custom-call | flops 1000 | bytes 1000 | tf_op jit(solution)/shard_map/accumulate_fourth/pallas_call | solution.py:125
  83.4 6.4 %collective-permute-done.15.refs_3_ = bf16[72,1792]{1,0:T(8,128)(2,1)S(1)} collective-permute-done((bf16[72,1792]{1,0:T(8,128)(2,1)S(1)}, bf16[72,1792]{1,0:T(8,128)(2,1)S(1)}, u32[]{:S(2)}, u32[]{:S(2)}) %collective-permute-start.15) | collective-permute-done | bytes 258080 | tf_op jit(solution)/shard_map/ppermute | solution.py:90
  89.8 1.0 %finish_other.1 = bf16[256,1792]{1,0:T(8,128)(2,1)S(1)} custom-call(bf16[96,1792]{1,0:T(8,128)(2,1)S(1)} %collective-permute-done.13.refs_0_, bf16[96,1792]{1,0:T(8,128)(2,1)S(1)} %collective-permute-done.14.refs_1_, bf16[144,1792]{1,0:T(8,128)(2,1)S(1)} %collective-permute-done.11.refs_4_.refs_2_, bf16[72,1792]{1,0:T(8,128)(2,1)S(1)} %collective-permute-done.15.refs_3_, ...), custom_call_target="tpu_custom_call" | custom-call | flops 1000 | bytes 1000 | tf_op jit(solution)/shard_map/finish_other/pallas_call | solution.py:125
  90.8 0.1 collective-permute-start.16
  90.9 1.4 %finish_own.1.kept_ref = f32[256,1792]{1,0:T(8,128)S(1)} custom-call(bf16[96,1792]{1,0:T(8,128)(2,1)S(1)} %collective-permute-done.13.refs_0_, bf16[96,1792]{1,0:T(8,128)(2,1)S(1)} %collective-permute-done.14.refs_1_, bf16[144,1792]{1,0:T(8,128)(2,1)S(1)} %collective-permute-done.11.refs_4_.refs_2_, ...), custom_call_target="tpu_custom_call", output_to_operand_aliasing={{}: (5, {})} | custom-call | flops 1000 | bytes 1000 | tf_op jit(solution)/shard_map/finish_own/pallas_call | solution.py:125
  92.3 1.1 %collective-permute-done.16.given_ref = bf16[256,1792]{1,0:T(8,128)(2,1)S(1)} collective-permute-done((bf16[256,1792]{1,0:T(8,128)(2,1)S(1)}, bf16[256,1792]{1,0:T(8,128)(2,1)S(1)}, u32[]{:S(2)}, u32[]{:S(2)}) %collective-permute-start.16) | collective-permute-done | bytes 917536 | tf_op jit(solution)/shard_map/ppermute | solution.py:90
  93.4 1.2 %final.1 = bf16[256,1792]{1,0:T(8,128)(2,1)} custom-call(s32[1]{0:T(128)S(6)} %copy.27.count_ref, f32[256,1792]{1,0:T(8,128)S(1)} %finish_own.1.kept_ref, bf16[256,1792]{1,0:T(8,128)(2,1)S(1)} %collective-permute-done.16.given_ref), custom_call_target="tpu_custom_call" | custom-call | flops 1000 | bytes 1000 | tf_op jit(solution)/shard_map/final/pallas_call | solution.py:125
  (23 shorter events, 0.1 us)
Async XLA Ops:
  2.8 19.5 %collective-permute-start = (bf16[168,1792]{1,0:T(8,128)(2,1)}, bf16[168,1792]{1,0:T(8,128)(2,1)S(1)}, u32[]{:S(2)}, u32[]{:S(2)}) collective-permute-start(bf16[168,1792]{1,0:T(8,128)(2,1)} %get-tuple-element.73.refs_0_), channel_id=1, source_target_pairs={{0,2},{1,5},{2,0},{3,7},{4,6},{5,1},{6,4},{7,3},{8,10},{9,13},{10,... | collective-permute-start | bytes 1806344 | tf_op jit(solution)/shard_map/ppermute | solution.py:90
  5.8 16.5 %collective-permute-start.1 = (bf16[168,1792]{1,0:T(8,128)(2,1)}, bf16[168,1792]{1,0:T(8,128)(2,1)S(1)}, u32[]{:S(2)}, u32[]{:S(2)}) collective-permute-start(bf16[168,1792]{1,0:T(8,128)(2,1)} %get-tuple-element.73.refs_0_), channel_id=1, source_target_pairs={{0,4},{1,3},{2,6},{3,1},{4,0},{5,7},{6,2},{7,5},{8,12},{9,11},{10,... | collective-permute-start | bytes 1806344 | tf_op jit(solution)/shard_map/ppermute | solution.py:90
  7.4 15.0 %collective-permute-start.2 = (bf16[144,1792]{1,0:T(8,128)(2,1)}, bf16[144,1792]{1,0:T(8,128)(2,1)S(1)}, u32[]{:S(2)}, u32[]{:S(2)}) collective-permute-start(bf16[144,1792]{1,0:T(8,128)(2,1)} %get-tuple-element.74), channel_id=1, source_target_pairs={{0,8},{1,9},{2,10},{3,11},{4,12},{5,13},{6,14},{7,15},{8,16},{9,17... | collective-permute-start | bytes 1548296 | tf_op jit(solution)/shard_map/ppermute | solution.py:90
  9.7 1.2 %copy-start.1 = (bf16[1,256,1792]{2,1,0:T(8,128)(2,1)S(1)}, bf16[1,256,1792]{2,1,0:T(8,128)(2,1)}, u32[]{:S(2)}) copy-start(bf16[1,256,1792]{2,1,0:T(8,128)(2,1)} %param.13) | copy-start | bytes 2752516
  10.8 1.9 %copy-start.3 = (bf16[1792,896]{1,0:T(8,128)(2,1)S(1)}, bf16[1792,896]{1,0:T(8,128)(2,1)}, u32[]{:S(2)}) copy-start(bf16[1792,896]{1,0:T(8,128)(2,1)} %value_ref.1) | copy-start | bytes 9633796
  12.7 1.0 %copy-start.5 = (bf16[1792,128]{1,0:T(8,128)(2,1)S(1)}, bf16[1792,128]{1,0:T(8,128)(2,1)}, u32[]{:S(2)}) copy-start(bf16[1792,128]{1,0:T(8,128)(2,1)} %query_ref.1) | copy-start | bytes 1376260
  13.8 1.0 %copy-start.6 = (bf16[1792,128]{1,0:T(8,128)(2,1)S(1)}, bf16[1792,128]{1,0:T(8,128)(2,1)}, u32[]{:S(2)}) copy-start(bf16[1792,128]{1,0:T(8,128)(2,1)} %key_ref.1) | copy-start | bytes 1376260
  14.8 0.7 copy-start.7
  15.5 6.8 %copy-start = (bf16[168,1792]{1,0:T(8,128)(2,1)S(1)}, bf16[168,1792]{1,0:T(8,128)(2,1)}, u32[]{:S(2)}) copy-start(bf16[168,1792]{1,0:T(8,128)(2,1)} %get-tuple-element.73.refs_0_) | copy-start | bytes 1806340
  15.5 13.8 %copy-start.4 = (bf16[896,1792]{1,0:T(8,128)(2,1)S(1)}, bf16[896,1792]{1,0:T(8,128)(2,1)}, u32[]{:S(2)}) copy-start(bf16[896,1792]{1,0:T(8,128)(2,1)} %out_ref.1) | copy-start | bytes 9633796
  19.3 6.3 %copy-start.9 = (f32[1792]{0:T(1024)S(1)}, f32[1792]{0:T(1024)}, u32[]{:S(2)}) copy-start(f32[1792]{0:T(1024)} %param.22) | copy-start | bytes 21508
  19.3 6.4 %copy-start.8 = (f32[1,256,8]{1,2,0:T(8,128)S(1)}, f32[1,256,8]{1,2,0:T(8,128)}, u32[]{:S(2)}) copy-start(f32[1,256,8]{1,2,0:T(8,128)} %param.15) | copy-start | bytes 24580
  19.3 10.1 %copy-start.2 = (bf16[1,256,1792]{2,1,0:T(8,128)(2,1)S(1)}, bf16[1,256,1792]{2,1,0:T(8,128)(2,1)}, u32[]{:S(2)}) copy-start(bf16[1,256,1792]{2,1,0:T(8,128)(2,1)} %param.13) | copy-start | bytes 2752516
  22.5 21.0 %collective-permute-start.4 = (bf16[232,1792]{1,0:T(8,128)(2,1)S(1)}, bf16[232,1792]{1,0:T(8,128)(2,1)S(1)}, u32[]{:S(2)}, u32[]{:S(2)}) collective-permute-start(bf16[232,1792]{1,0:T(8,128)(2,1)S(1)} %get-tuple-element.85), channel_id=1, source_target_pairs={{0,4},{1,3},{2,6},{3,1},{4,0},{5,7},{6,2},{7,5},{8,12},{9,11},{10,... | collective-permute-start | bytes 2494472 | tf_op jit(solution)/shard_map/ppermute | solution.py:90
  23.1 20.5 %collective-permute-start.3 = (bf16[224,1792]{1,0:T(8,128)(2,1)S(1)}, bf16[224,1792]{1,0:T(8,128)(2,1)S(1)}, u32[]{:S(2)}, u32[]{:S(2)}) collective-permute-start(bf16[224,1792]{1,0:T(8,128)(2,1)S(1)} %get-tuple-element.84), channel_id=1, source_target_pairs={{0,2},{1,5},{2,0},{3,7},{4,6},{5,1},{6,4},{7,3},{8,10},{9,13},{10,... | collective-permute-start | bytes 2408456 | tf_op jit(solution)/shard_map/ppermute | solution.py:90
  23.6 19.9 %collective-permute-start.5 = (bf16[216,1792]{1,0:T(8,128)(2,1)S(1)}, bf16[216,1792]{1,0:T(8,128)(2,1)S(1)}, u32[]{:S(2)}, u32[]{:S(2)}) collective-permute-start(bf16[216,1792]{1,0:T(8,128)(2,1)S(1)} %get-tuple-element.86), channel_id=1, source_target_pairs={{0,8},{1,9},{2,10},{3,11},{4,12},{5,13},{6,14},{7,15},{8,16},{9,17... | collective-permute-start | bytes 2322440 | tf_op jit(solution)/shard_map/ppermute | solution.py:90
  43.7 21.7 %collective-permute-start.8 = (bf16[240,1792]{1,0:T(8,128)(2,1)S(1)}, bf16[240,1792]{1,0:T(8,128)(2,1)S(1)}, u32[]{:S(2)}, u32[]{:S(2)}) collective-permute-start(bf16[240,1792]{1,0:T(8,128)(2,1)S(1)} %get-tuple-element.104), channel_id=1, source_target_pairs={{0,8},{1,9},{2,10},{3,11},{4,12},{5,13},{6,14},{7,15},{8,16},{9,17... | collective-permute-start | bytes 2580488 | tf_op jit(solution)/shard_map/ppermute | solution.py:90
  44.0 19.0 %collective-permute-start.6 = (bf16[224,1792]{1,0:T(8,128)(2,1)S(1)}, bf16[224,1792]{1,0:T(8,128)(2,1)S(1)}, u32[]{:S(2)}, u32[]{:S(2)}) collective-permute-start(bf16[224,1792]{1,0:T(8,128)(2,1)S(1)} %get-tuple-element.102), channel_id=1, source_target_pairs={{0,2},{1,5},{2,0},{3,7},{4,6},{5,1},{6,4},{7,3},{8,10},{9,13},{10,... | collective-permute-start | bytes 2408456 | tf_op jit(solution)/shard_map/ppermute | solution.py:90
  44.9 18.1 %collective-permute-start.7 = (bf16[208,1792]{1,0:T(8,128)(2,1)S(1)}, bf16[208,1792]{1,0:T(8,128)(2,1)S(1)}, u32[]{:S(2)}, u32[]{:S(2)}) collective-permute-start(bf16[208,1792]{1,0:T(8,128)(2,1)S(1)} %get-tuple-element.103), channel_id=1, source_target_pairs={{0,4},{1,3},{2,6},{3,1},{4,0},{5,7},{6,2},{7,5},{8,12},{9,11},{10,... | collective-permute-start | bytes 2236424 | tf_op jit(solution)/shard_map/ppermute | solution.py:90
  46.1 20.6 %collective-permute-start.12 = (bf16[256,1792]{1,0:T(8,128)(2,1)S(1)}, bf16[256,1792]{1,0:T(8,128)(2,1)S(1)}, u32[]{:S(2)}, u32[]{:S(2)}) collective-permute-start(bf16[256,1792]{1,0:T(8,128)(2,1)S(1)} %get-tuple-element.116.refs_7_.refs_8_.refs_3_.refs_4_), channel_id=1, source_target_pairs={{0,1},{1,0},{2,3},{3,2},{4,5},{5,4},{6,7},{7,6},{8,9},{9,8},{10,11... | collective-permute-start | bytes 2752520 | tf_op jit(solution)/shard_map/ppermute | solution.py:90
  65.5 12.6 %collective-permute-start.10 = (bf16[144,1792]{1,0:T(8,128)(2,1)S(1)}, bf16[144,1792]{1,0:T(8,128)(2,1)S(1)}, u32[]{:S(2)}, u32[]{:S(2)}) collective-permute-start(bf16[144,1792]{1,0:T(8,128)(2,1)S(1)} %get-tuple-element.111), channel_id=1, source_target_pairs={{0,4},{1,3},{2,6},{3,1},{4,0},{5,7},{6,2},{7,5},{8,12},{9,11},{10,... | collective-permute-start | bytes 1548296 | tf_op jit(solution)/shard_map/ppermute | solution.py:90
  66.7 12.4 %collective-permute-start.11 = (bf16[144,1792]{1,0:T(8,128)(2,1)S(1)}, bf16[144,1792]{1,0:T(8,128)(2,1)S(1)}, u32[]{:S(2)}, u32[]{:S(2)}) collective-permute-start(bf16[144,1792]{1,0:T(8,128)(2,1)S(1)} %get-tuple-element.112), channel_id=1, source_target_pairs={{0,8},{1,9},{2,10},{3,11},{4,12},{5,13},{6,14},{7,15},{8,16},{9,17... | collective-permute-start | bytes 1548296 | tf_op jit(solution)/shard_map/ppermute | solution.py:90
  66.7 12.4 %collective-permute-start.9 = (bf16[144,1792]{1,0:T(8,128)(2,1)S(1)}, bf16[144,1792]{1,0:T(8,128)(2,1)S(1)}, u32[]{:S(2)}, u32[]{:S(2)}) collective-permute-start(bf16[144,1792]{1,0:T(8,128)(2,1)S(1)} %get-tuple-element.111), channel_id=1, source_target_pairs={{0,2},{1,5},{2,0},{3,7},{4,6},{5,1},{6,4},{7,3},{8,10},{9,13},{10,... | collective-permute-start | bytes 1548296 | tf_op jit(solution)/shard_map/ppermute | solution.py:90
  79.2 10.6 %collective-permute-start.13 = (bf16[96,1792]{1,0:T(8,128)(2,1)S(1)}, bf16[96,1792]{1,0:T(8,128)(2,1)S(1)}, u32[]{:S(2)}, u32[]{:S(2)}) collective-permute-start(bf16[96,1792]{1,0:T(8,128)(2,1)S(1)} %get-tuple-element.124), channel_id=1, source_target_pairs={{0,2},{1,5},{2,0},{3,7},{4,6},{5,1},{6,4},{7,3},{8,10},{9,13},{10,... | collective-permute-start | bytes 1032200 | tf_op jit(solution)/shard_map/ppermute | solution.py:90
  80.7 9.1 %collective-permute-start.14 = (bf16[96,1792]{1,0:T(8,128)(2,1)S(1)}, bf16[96,1792]{1,0:T(8,128)(2,1)S(1)}, u32[]{:S(2)}, u32[]{:S(2)}) collective-permute-start(bf16[96,1792]{1,0:T(8,128)(2,1)S(1)} %get-tuple-element.125), channel_id=1, source_target_pairs={{0,4},{1,3},{2,6},{3,1},{4,0},{5,7},{6,2},{7,5},{8,12},{9,11},{10,... | collective-permute-start | bytes 1032200 | tf_op jit(solution)/shard_map/ppermute | solution.py:90
  81.4 8.4 %collective-permute-start.15 = (bf16[72,1792]{1,0:T(8,128)(2,1)S(1)}, bf16[72,1792]{1,0:T(8,128)(2,1)S(1)}, u32[]{:S(2)}, u32[]{:S(2)}) collective-permute-start(bf16[72,1792]{1,0:T(8,128)(2,1)S(1)} %get-tuple-element.126), channel_id=1, source_target_pairs={{0,8},{1,9},{2,10},{3,11},{4,12},{5,13},{6,14},{7,15},{8,16},{9,17... | collective-permute-start | bytes 774152 | tf_op jit(solution)/shard_map/ppermute | solution.py:90
  90.8 2.5 %collective-permute-start.16 = (bf16[256,1792]{1,0:T(8,128)(2,1)S(1)}, bf16[256,1792]{1,0:T(8,128)(2,1)S(1)}, u32[]{:S(2)}, u32[]{:S(2)}) collective-permute-start(bf16[256,1792]{1,0:T(8,128)(2,1)S(1)} %finish_other.1), channel_id=1, source_target_pairs={{0,1},{1,0},{2,3},{3,2},{4,5},{5,4},{6,7},{7,6},{8,9},{9,8},{10,11... | collective-permute-start | bytes 2752520 | tf_op jit(solution)/shard_map/ppermute | solution.py:90

commit v7 on v4

--- a/solution.py
+++ b/solution.py
@@ -615,16 +615,17 @@
     )
     near3, far3, deep3, *acc = together(near3, far3, deep3, *acc)
 
+    held = 2 * main // 3
     sends = collect(
         (near2, far2, near3, far3, deep3),
         (
-            ((1, 0, main), (3, 0, main)),
-            ((0, main, 2 * main), (2, main, 2 * main)),
-            ((4, 3 * narrow, 4 * narrow + main),),
+            ((1, 0, main), (3, 0, main), (3, 2 * main, 2 * main + held)),
+            ((0, main, 2 * main), (2, main, 2 * main), (2, 2 * main + held, wide))
+            + ((4, narrow, 2 * narrow),),
         ),
         "collect_fifth",
     )
-    near4, far4, deep4 = slot(*zip((flip_near, flip_far, next_plane), sends))
+    near4, far4 = slot(*zip((flip_near, flip_far), sends))
     acc = accumulate(
         rows,
         (near3, far3, deep3),
@@ -633,11 +634,13 @@
         jnp.float32,
         "accumulate_fourth",
     )
-    weights = (near4, far4, deep3, deep4)
+    weights = (near4, far4, deep3)
+    two, tail = 2 * main, 2 * main + main - held
     last = [
         ((0, 0, main), (1, 0, main), (2, 4 * narrow, 4 * narrow + main)),
-        ((0, main, 2 * main), (1, main, 2 * main), (3, narrow, narrow + main)),
-        runs(3, 0, edge),
+        ((0, main, main + held), (1, main, main + held), (0, two, two + held)),
+        ((0, main + held, two), (1, main + held, two), (1, two, tail)),
+        runs(1, tail, edge),
     ]
     (given,) = accumulate(rows[1:], weights, last, acc[1:], jnp.bfloat16, "finish_other")
     (kept,) = accumulate(

time: 91.4 us -> 90.3 us (0.988)
  waiting for transfers between devices: 41.3 us -> 40.2 us
    ppermute x17 -> x16, waiting for transfers between devices: 41.3 us -> 40.2 us  [permute(): return lax.ppermute(array, 'req', [(i, target(i)) for i in range(count)])]
    ppermute x17 -> x16, starting transfers between devices: 16.3 us -> 16.3 us  [permute(): return lax.ppermute(array, 'req', [(i, target(i)) for i in range(count)])]
  transfers between devices with their start and end apart: 17 -> 16, of which waited for: 9 -> 9; matrix products, arithmetic and copies ran while one was open for 1% -> 1% of each run, Pallas kernels for 23% -> 23%
where the time goes in v7:
time: 90.3 us; the launch traced here: 89.9 us
  waiting for transfers between devices  40.2 us (45%)
  Pallas kernels  25.3 us (28%)
  starting transfers between devices  16.3 us (18%)
  local copies, waits for them, and re-layouts  6.61 us (7%)
  between operations  1.46 us (2%)
    ppermute x16, waiting for transfers between devices, permute(): return lax.ppermute(array, 'req', [(i, target(i)) for i in range(count)])  40.2 us
    pallas_call x14, Pallas kernels, kernel_call(): pl.pallas_call(body, out_shape=out_shape, in_specs=specs or vmem(len(oper...  25.3 us
    ppermute x16, starting transfers between devices, permute(): return lax.ppermute(array, 'req', [(i, target(i)) for i in range(count)])  16.3 us
    unnamed x20, local copies, waits for them, and re-layouts  5.89 us
  transfers between devices with their start and end apart: 16, of which 9 were waited for; matrix products, arithmetic and copies ran while one was open for 1% of the time, Pallas kernels for 23%

profile of v7, /device:TPU:0, one launch (start us, length us, event | category | flops | bytes accessed | tf_op | source)
XLA Modules:
  0.0 89.9 jit_solution(14424340810177636273)
XLA Ops:
  0.6 2.2 %shard.1 = (bf16[168,1792]{1,0:T(8,128)(2,1)}, bf16[144,1792]{1,0:T(8,128)(2,1)}) custom-call(bf16[56,1792]{1,0:T(8,128)(2,1)} %bitcast.17, bf16[56,1792]{1,0:T(8,128)(2,1)} %bitcast.18, bf16[56,1792]{1,0:T(8,128)(2,1)} %bitcast.19), custom_call_target="tpu_custom_call" | custom-call | flops 1000 | bytes 1000 | tf_op jit(solution)/shard_map/shard/pallas_call | solution.py:125
  2.8 3.0 %collective-permute-start = (bf16[168,1792]{1,0:T(8,128)(2,1)}, bf16[168,1792]{1,0:T(8,128)(2,1)S(1)}, u32[]{:S(2)}, u32[]{:S(2)}) collective-permute-start(bf16[168,1792]{1,0:T(8,128)(2,1)} %get-tuple-element.71.refs_0_), channel_id=1, source_target_pairs={{0,2},{1,3},{2,0},{3,1},{4,6},{5,7},{6,4},{7,5},{8,10},{9,11},{10,... | collective-permute-start | bytes 1806344 | tf_op jit(solution)/shard_map/ppermute | solution.py:90
  5.8 1.5 %collective-permute-start.1 = (bf16[168,1792]{1,0:T(8,128)(2,1)}, bf16[168,1792]{1,0:T(8,128)(2,1)S(1)}, u32[]{:S(2)}, u32[]{:S(2)}) collective-permute-start(bf16[168,1792]{1,0:T(8,128)(2,1)} %get-tuple-element.71.refs_0_), channel_id=1, source_target_pairs={{0,4},{1,5},{2,6},{3,7},{4,0},{5,1},{6,2},{7,3},{8,12},{9,13},{10,... | collective-permute-start | bytes 1806344 | tf_op jit(solution)/shard_map/ppermute | solution.py:90
  7.4 1.6 %collective-permute-start.2 = (bf16[144,1792]{1,0:T(8,128)(2,1)}, bf16[144,1792]{1,0:T(8,128)(2,1)S(1)}, u32[]{:S(2)}, u32[]{:S(2)}) collective-permute-start(bf16[144,1792]{1,0:T(8,128)(2,1)} %get-tuple-element.72), channel_id=1, source_target_pairs={{0,8},{1,9},{2,10},{3,11},{4,12},{5,13},{6,14},{7,15},{8,16},{9,17... | collective-permute-start | bytes 1548296 | tf_op jit(solution)/shard_map/ppermute | solution.py:90
  8.9 0.7 broadcast_in_dim.16.gain_ref
  9.7 0.0 copy-start.1
  9.7 1.2 %copy-done.1 = bf16[1,256,1792]{2,1,0:T(8,128)(2,1)S(1)} copy-done((bf16[1,256,1792]{2,1,0:T(8,128)(2,1)S(1)}, bf16[1,256,1792]{2,1,0:T(8,128)(2,1)}, u32[]{:S(2)}) %copy-start.1) | copy-done | bytes 917528
  10.8 1.9 %copy-done.3 = bf16[1792,896]{1,0:T(8,128)(2,1)S(1)} copy-done((bf16[1792,896]{1,0:T(8,128)(2,1)S(1)}, bf16[1792,896]{1,0:T(8,128)(2,1)}, u32[]{:S(2)}) %copy-start.3) | copy-done | bytes 3211288
  12.7 1.0 %copy-done.5 = bf16[1792,128]{1,0:T(8,128)(2,1)S(1)} copy-done((bf16[1792,128]{1,0:T(8,128)(2,1)S(1)}, bf16[1792,128]{1,0:T(8,128)(2,1)}, u32[]{:S(2)}) %copy-start.5) | copy-done | bytes 458776
  13.8 1.0 %copy-done.6 = bf16[1792,128]{1,0:T(8,128)(2,1)S(1)} copy-done((bf16[1792,128]{1,0:T(8,128)(2,1)S(1)}, bf16[1792,128]{1,0:T(8,128)(2,1)}, u32[]{:S(2)}) %copy-start.6) | copy-done | bytes 458776
  14.8 0.7 copy-done.7
  15.5 3.7 %project.1 = (bf16[256,128]{1,0:T(8,128)(2,1)S(1)}, bf16[256,128]{1,0:T(8,128)(2,1)S(1)}, bf16[256,896]{1,0:T(8,128)(2,1)S(1)}) custom-call(bf16[256,1792]{1,0:T(8,128)(2,1)S(1)} %bitcast.13, bf16[16,1792]{1,0:T(8,128)(2,1)S(1)} %broadcast_in_dim.15.edge_ref, f32[1,1792]{1,0:T(1,128)S(1)} %broadcast_in_dim.16.gain_ref, f32[3,1792]{1,0:T(4,128)S(1)} %copy-done.7, ...), custom_call_target="tpu_custom_call" | custom-call | flops 1000 | bytes 1000 | tf_op jit(solution)/shard_map/project/pallas_call | solution.py:125
  19.3 0.0 copy-start.9
  19.3 0.0 copy-start.8
  19.3 0.0 copy-start.2
  19.3 3.1 %collective-permute-done.2.refs_3_ = bf16[144,1792]{1,0:T(8,128)(2,1)S(1)} collective-permute-done((bf16[144,1792]{1,0:T(8,128)(2,1)}, bf16[144,1792]{1,0:T(8,128)(2,1)S(1)}, u32[]{:S(2)}, u32[]{:S(2)}) %collective-permute-start.2) | collective-permute-done | bytes 516128 | tf_op jit(solution)/shard_map/ppermute | solution.py:90
  22.4 0.2 collect_second.1
  22.5 0.6 collective-permute-start.4
  23.1 0.5 collective-permute-start.3
  23.6 1.3 %collective-permute-start.5 = (bf16[216,1792]{1,0:T(8,128)(2,1)S(1)}, bf16[216,1792]{1,0:T(8,128)(2,1)S(1)}, u32[]{:S(2)}, u32[]{:S(2)}) collective-permute-start(bf16[216,1792]{1,0:T(8,128)(2,1)S(1)} %get-tuple-element.84), channel_id=1, source_target_pairs={{0,8},{1,9},{2,10},{3,11},{4,12},{5,13},{6,14},{7,15},{8,16},{9,17... | collective-permute-start | bytes 2322440 | tf_op jit(solution)/shard_map/ppermute | solution.py:90
  25.7 3.7 %attend.1 = (f32[256,896]{1,0:T(8,128)S(1)}, f32[256,8]{1,0:T(8,128)S(1)}, f32[273,1,896]{2,1,0:T(1,128)}, f32[8,273]{1,0:T(8,128)}) custom-call(s32[1]{0:T(128)S(6)} %copy.27.count_ref, f32[8,256]{1,0:T(8,128)S(1)} %bitcast.15, bf16[256,128]{1,0:T(8,128)(2,1)S(1)} %get-tuple-element.88.queries_ref, bf16[256,128]{1,0:T(8,128)(2,1)S(1)} %get-tuple-element.89.keys_ref, ...), custom_call_target="tpu_custom_call" | custom-call | flops 1000 | bytes 1000 | tf_op jit(solution)/shard_map/attend/pallas_call | solution.py:125
  29.4 2.6 %mix.1 = (bf16[256,1792]{1,0:T(8,128)(2,1)S(1)}, bf16[256,1792]{1,0:T(8,128)(2,1)S(1)}) custom-call(f32[256,896]{1,0:T(8,128)S(1)} %get-tuple-element.91.numer_ref, f32[256,8]{1,0:T(8,128)S(1)} %get-tuple-element.92.denom_ref, bf16[256,1792]{1,0:T(8,128)(2,1)S(1)} %bitcast.14, bf16[896,1792]{1,0:T(8,128)(2,1)S(1)} %copy-done.4, ...), custom_call_target="tpu_custom_call" | custom-call | flops 1000 | bytes 1000 | tf_op jit(solution)/shard_map/mix/pallas_call | solution.py:125
  32.0 10.7 %collective-permute-done.5.refs_2_.refs_6_.refs_4_ = bf16[216,1792]{1,0:T(8,128)(2,1)S(1)} collective-permute-done((bf16[216,1792]{1,0:T(8,128)(2,1)S(1)}, bf16[216,1792]{1,0:T(8,128)(2,1)S(1)}, u32[]{:S(2)}, u32[]{:S(2)}) %collective-permute-start.5) | collective-permute-done | bytes 774176 | tf_op jit(solution)/shard_map/ppermute | solution.py:90
  42.7 0.2 collect_third.1
  42.9 0.1 collective-permute-start.8
  43.0 1.4 %collective-permute-start.6 = (bf16[224,1792]{1,0:T(8,128)(2,1)S(1)}, bf16[224,1792]{1,0:T(8,128)(2,1)S(1)}, u32[]{:S(2)}, u32[]{:S(2)}) collective-permute-start(bf16[224,1792]{1,0:T(8,128)(2,1)S(1)} %get-tuple-element.100), channel_id=1, source_target_pairs={{0,2},{1,3},{2,0},{3,1},{4,6},{5,7},{6,4},{7,5},{8,10},{9,11},{10,... | collective-permute-start | bytes 2408456 | tf_op jit(solution)/shard_map/ppermute | solution.py:90
  44.3 1.5 %collective-permute-start.7 = (bf16[208,1792]{1,0:T(8,128)(2,1)S(1)}, bf16[208,1792]{1,0:T(8,128)(2,1)S(1)}, u32[]{:S(2)}, u32[]{:S(2)}) collective-permute-start(bf16[208,1792]{1,0:T(8,128)(2,1)S(1)} %get-tuple-element.101), channel_id=1, source_target_pairs={{0,4},{1,5},{2,6},{3,7},{4,0},{5,1},{6,2},{7,3},{8,12},{9,13},{10,... | collective-permute-start | bytes 2236424 | tf_op jit(solution)/shard_map/ppermute | solution.py:90
  45.8 13.8 %collective-permute-done.7.refs_0_.refs_6_.refs_1_ = bf16[208,1792]{1,0:T(8,128)(2,1)S(1)} collective-permute-done((bf16[208,1792]{1,0:T(8,128)(2,1)S(1)}, bf16[208,1792]{1,0:T(8,128)(2,1)S(1)}, u32[]{:S(2)}, u32[]{:S(2)}) %collective-permute-start.7) | collective-permute-done | bytes 745504 | tf_op jit(solution)/shard_map/ppermute | solution.py:90
  59.6 0.4 collective-permute-done.6.refs_5_.refs_0_
  60.0 2.9 %collective-permute-done.8.refs_1_.refs_7_ = bf16[240,1792]{1,0:T(8,128)(2,1)S(1)} collective-permute-done((bf16[240,1792]{1,0:T(8,128)(2,1)S(1)}, bf16[240,1792]{1,0:T(8,128)(2,1)S(1)}, u32[]{:S(2)}, u32[]{:S(2)}) %collective-permute-start.8) | collective-permute-done | bytes 860192 | tf_op jit(solution)/shard_map/ppermute | solution.py:90
  62.9 0.1 collect_fourth.1
  63.0 1.1 %collective-permute-start.10 = (bf16[144,1792]{1,0:T(8,128)(2,1)S(1)}, bf16[144,1792]{1,0:T(8,128)(2,1)S(1)}, u32[]{:S(2)}, u32[]{:S(2)}) collective-permute-start(bf16[144,1792]{1,0:T(8,128)(2,1)S(1)} %get-tuple-element.109), channel_id=1, source_target_pairs={{0,4},{1,5},{2,6},{3,7},{4,0},{5,1},{6,2},{7,3},{8,12},{9,13},{10,... | collective-permute-start | bytes 1548296 | tf_op jit(solution)/shard_map/ppermute | solution.py:90
  64.1 0.0 collective-permute-start.11
  64.1 1.5 %collective-permute-start.9 = (bf16[144,1792]{1,0:T(8,128)(2,1)S(1)}, bf16[144,1792]{1,0:T(8,128)(2,1)S(1)}, u32[]{:S(2)}, u32[]{:S(2)}) collective-permute-start(bf16[144,1792]{1,0:T(8,128)(2,1)S(1)} %get-tuple-element.109), channel_id=1, source_target_pairs={{0,2},{1,3},{2,0},{3,1},{4,6},{5,7},{6,4},{7,5},{8,10},{9,11},{10,... | collective-permute-start | bytes 1548296 | tf_op jit(solution)/shard_map/ppermute | solution.py:90
  65.6 3.2 %accumulate_second.1 = (f32[256,1792]{1,0:T(8,128)S(1)}, f32[256,1792]{1,0:T(8,128)S(1)}) custom-call(bf16[168,1792]{1,0:T(8,128)(2,1)S(1)} %copy-done, bf16[168,1792]{1,0:T(8,128)(2,1)S(1)} %collective-permute-done.refs_1_, bf16[168,1792]{1,0:T(8,128)(2,1)S(1)} %collective-permute-done.1.refs_2_, bf16[144,1792]{1,0:T(8,128)(2,1)S(1)} %collective-permute-done.2.refs_3_, ...), custom_call_target="tpu_custom_call" | custom-call | flops 1000 | bytes 1000 | tf_op jit(solution)/shard_map/accumulate_second/pallas_call | solution.py:125
  68.8 3.9 %accumulate_third.1 = (f32[256,1792]{1,0:T(8,128)S(1)}, f32[256,1792]{1,0:T(8,128)S(1)}) custom-call(bf16[168,1792]{1,0:T(8,128)(2,1)S(1)} %copy-done, bf16[168,1792]{1,0:T(8,128)(2,1)S(1)} %collective-permute-done.refs_1_, bf16[168,1792]{1,0:T(8,128)(2,1)S(1)} %collective-permute-done.1.refs_2_, ...), custom_call_target="tpu_custom_call", output_to_operand_aliasing={{0}: (10, {}), {1}: (11, {})} | custom-call | flops 1000 | bytes 1000 | tf_op jit(solution)/shard_map/accumulate_third/pallas_call | solution.py:125
  72.7 0.3 collective-permute-done.10.refs_3_.refs_1_
  73.0 2.3 %collective-permute-done.11.refs_4_.refs_2_ = bf16[144,1792]{1,0:T(8,128)(2,1)S(1)} collective-permute-done((bf16[144,1792]{1,0:T(8,128)(2,1)S(1)}, bf16[144,1792]{1,0:T(8,128)(2,1)S(1)}, u32[]{:S(2)}, u32[]{:S(2)}) %collective-permute-start.11) | collective-permute-done | bytes 516128 | tf_op jit(solution)/shard_map/ppermute | solution.py:90
  75.3 0.1 collect_fifth.1
  75.4 1.3 %collective-permute-start.14 = (bf16[136,1792]{1,0:T(8,128)(2,1)S(1)}, bf16[136,1792]{1,0:T(8,128)(2,1)S(1)}, u32[]{:S(2)}, u32[]{:S(2)}) collective-permute-start(bf16[136,1792]{1,0:T(8,128)(2,1)S(1)} %get-tuple-element.123), channel_id=1, source_target_pairs={{0,4},{1,5},{2,6},{3,7},{4,0},{5,1},{6,2},{7,3},{8,12},{9,13},{10,... | collective-permute-start | bytes 1462280 | tf_op jit(solution)/shard_map/ppermute | solution.py:90
  76.6 0.9 %collective-permute-start.13 = (bf16[128,1792]{1,0:T(8,128)(2,1)S(1)}, bf16[128,1792]{1,0:T(8,128)(2,1)S(1)}, u32[]{:S(2)}, u32[]{:S(2)}) collective-permute-start(bf16[128,1792]{1,0:T(8,128)(2,1)S(1)} %get-tuple-element.122), channel_id=1, source_target_pairs={{0,2},{1,3},{2,0},{3,1},{4,6},{5,7},{6,4},{7,5},{8,10},{9,11},{10,... | collective-permute-start | bytes 1376264 | tf_op jit(solution)/shard_map/ppermute | solution.py:90
  77.5 2.0 %accumulate_fourth.1 = (f32[256,1792]{1,0:T(8,128)S(1)}, f32[256,1792]{1,0:T(8,128)S(1)}) custom-call(bf16[144,1792]{1,0:T(8,128)(2,1)S(1)} %collective-permute-done.9.refs_2_.refs_0_, bf16[144,1792]{1,0:T(8,128)(2,1)S(1)} %collective-permute-done.10.refs_3_.refs_1_, ...), custom_call_target="tpu_custom_call", output_to_operand_aliasing={{0}: (5, {}), {1}: (6, {})} | custom-call | flops 1000 | bytes 1000 | tf_op jit(solution)/shard_map/accumulate_fourth/pallas_call | solution.py:125
  79.5 5.6 %collective-permute-done.13.refs_0_ = bf16[128,1792]{1,0:T(8,128)(2,1)S(1)} collective-permute-done((bf16[128,1792]{1,0:T(8,128)(2,1)S(1)}, bf16[128,1792]{1,0:T(8,128)(2,1)S(1)}, u32[]{:S(2)}, u32[]{:S(2)}) %collective-permute-start.13) | collective-permute-done | bytes 458784 | tf_op jit(solution)/shard_map/ppermute | solution.py:90
  85.1 1.0 %finish_other.1 = bf16[256,1792]{1,0:T(8,128)(2,1)S(1)} custom-call(bf16[128,1792]{1,0:T(8,128)(2,1)S(1)} %collective-permute-done.13.refs_0_, bf16[136,1792]{1,0:T(8,128)(2,1)S(1)} %collective-permute-done.14.refs_1_, bf16[144,1792]{1,0:T(8,128)(2,1)S(1)} %collective-permute-done.11.refs_4_.refs_2_, ...), custom_call_target="tpu_custom_call" | custom-call | flops 1000 | bytes 1000 | tf_op jit(solution)/shard_map/finish_other/pallas_call | solution.py:125
  86.2 0.1 collective-permute-start.15
  86.2 1.4 %finish_own.1.kept_ref = f32[256,1792]{1,0:T(8,128)S(1)} custom-call(bf16[128,1792]{1,0:T(8,128)(2,1)S(1)} %collective-permute-done.13.refs_0_, bf16[136,1792]{1,0:T(8,128)(2,1)S(1)} %collective-permute-done.14.refs_1_, bf16[144,1792]{1,0:T(8,128)(2,1)S(1)} %collective-permute-done.11.refs_4_.refs_2_, ...), custom_call_target="tpu_custom_call", output_to_operand_aliasing={{}: (4, {})} | custom-call | flops 1000 | bytes 1000 | tf_op jit(solution)/shard_map/finish_own/pallas_call | solution.py:125
  87.6 1.1 %collective-permute-done.15.given_ref = bf16[256,1792]{1,0:T(8,128)(2,1)S(1)} collective-permute-done((bf16[256,1792]{1,0:T(8,128)(2,1)S(1)}, bf16[256,1792]{1,0:T(8,128)(2,1)S(1)}, u32[]{:S(2)}, u32[]{:S(2)}) %collective-permute-start.15) | collective-permute-done | bytes 917536 | tf_op jit(solution)/shard_map/ppermute | solution.py:90
  88.7 1.2 %final.1 = bf16[256,1792]{1,0:T(8,128)(2,1)} custom-call(s32[1]{0:T(128)S(6)} %copy.27.count_ref, f32[256,1792]{1,0:T(8,128)S(1)} %finish_own.1.kept_ref, bf16[256,1792]{1,0:T(8,128)(2,1)S(1)} %collective-permute-done.15.given_ref), custom_call_target="tpu_custom_call" | custom-call | flops 1000 | bytes 1000 | tf_op jit(solution)/shard_map/final/pallas_call | solution.py:125
  (21 shorter events, 0.1 us)
Async XLA Ops:
  2.8 19.5 %collective-permute-start = (bf16[168,1792]{1,0:T(8,128)(2,1)}, bf16[168,1792]{1,0:T(8,128)(2,1)S(1)}, u32[]{:S(2)}, u32[]{:S(2)}) collective-permute-start(bf16[168,1792]{1,0:T(8,128)(2,1)} %get-tuple-element.71.refs_0_), channel_id=1, source_target_pairs={{0,2},{1,3},{2,0},{3,1},{4,6},{5,7},{6,4},{7,5},{8,10},{9,11},{10,... | collective-permute-start | bytes 1806344 | tf_op jit(solution)/shard_map/ppermute | solution.py:90
  5.8 16.5 %collective-permute-start.1 = (bf16[168,1792]{1,0:T(8,128)(2,1)}, bf16[168,1792]{1,0:T(8,128)(2,1)S(1)}, u32[]{:S(2)}, u32[]{:S(2)}) collective-permute-start(bf16[168,1792]{1,0:T(8,128)(2,1)} %get-tuple-element.71.refs_0_), channel_id=1, source_target_pairs={{0,4},{1,5},{2,6},{3,7},{4,0},{5,1},{6,2},{7,3},{8,12},{9,13},{10,... | collective-permute-start | bytes 1806344 | tf_op jit(solution)/shard_map/ppermute | solution.py:90
  7.4 15.0 %collective-permute-start.2 = (bf16[144,1792]{1,0:T(8,128)(2,1)}, bf16[144,1792]{1,0:T(8,128)(2,1)S(1)}, u32[]{:S(2)}, u32[]{:S(2)}) collective-permute-start(bf16[144,1792]{1,0:T(8,128)(2,1)} %get-tuple-element.72), channel_id=1, source_target_pairs={{0,8},{1,9},{2,10},{3,11},{4,12},{5,13},{6,14},{7,15},{8,16},{9,17... | collective-permute-start | bytes 1548296 | tf_op jit(solution)/shard_map/ppermute | solution.py:90
  9.7 1.2 %copy-start.1 = (bf16[1,256,1792]{2,1,0:T(8,128)(2,1)S(1)}, bf16[1,256,1792]{2,1,0:T(8,128)(2,1)}, u32[]{:S(2)}) copy-start(bf16[1,256,1792]{2,1,0:T(8,128)(2,1)} %param.13) | copy-start | bytes 2752516
  10.8 1.9 %copy-start.3 = (bf16[1792,896]{1,0:T(8,128)(2,1)S(1)}, bf16[1792,896]{1,0:T(8,128)(2,1)}, u32[]{:S(2)}) copy-start(bf16[1792,896]{1,0:T(8,128)(2,1)} %value_ref.1) | copy-start | bytes 9633796
  12.7 1.0 %copy-start.5 = (bf16[1792,128]{1,0:T(8,128)(2,1)S(1)}, bf16[1792,128]{1,0:T(8,128)(2,1)}, u32[]{:S(2)}) copy-start(bf16[1792,128]{1,0:T(8,128)(2,1)} %query_ref.1) | copy-start | bytes 1376260
  13.8 1.0 %copy-start.6 = (bf16[1792,128]{1,0:T(8,128)(2,1)S(1)}, bf16[1792,128]{1,0:T(8,128)(2,1)}, u32[]{:S(2)}) copy-start(bf16[1792,128]{1,0:T(8,128)(2,1)} %key_ref.1) | copy-start | bytes 1376260
  14.8 0.7 copy-start.7
  15.5 6.8 %copy-start = (bf16[168,1792]{1,0:T(8,128)(2,1)S(1)}, bf16[168,1792]{1,0:T(8,128)(2,1)}, u32[]{:S(2)}) copy-start(bf16[168,1792]{1,0:T(8,128)(2,1)} %get-tuple-element.71.refs_0_) | copy-start | bytes 1806340
  15.5 13.8 %copy-start.4 = (bf16[896,1792]{1,0:T(8,128)(2,1)S(1)}, bf16[896,1792]{1,0:T(8,128)(2,1)}, u32[]{:S(2)}) copy-start(bf16[896,1792]{1,0:T(8,128)(2,1)} %out_ref.1) | copy-start | bytes 9633796
  19.3 6.4 %copy-start.9 = (f32[1792]{0:T(1024)S(1)}, f32[1792]{0:T(1024)}, u32[]{:S(2)}) copy-start(f32[1792]{0:T(1024)} %param.22) | copy-start | bytes 21508
  19.3 6.4 %copy-start.8 = (f32[1,256,8]{1,2,0:T(8,128)S(1)}, f32[1,256,8]{1,2,0:T(8,128)}, u32[]{:S(2)}) copy-start(f32[1,256,8]{1,2,0:T(8,128)} %param.15) | copy-start | bytes 24580
  19.3 10.1 %copy-start.2 = (bf16[1,256,1792]{2,1,0:T(8,128)(2,1)S(1)}, bf16[1,256,1792]{2,1,0:T(8,128)(2,1)}, u32[]{:S(2)}) copy-start(bf16[1,256,1792]{2,1,0:T(8,128)(2,1)} %param.13) | copy-start | bytes 2752516
  22.5 20.2 %collective-permute-start.4 = (bf16[232,1792]{1,0:T(8,128)(2,1)S(1)}, bf16[232,1792]{1,0:T(8,128)(2,1)S(1)}, u32[]{:S(2)}, u32[]{:S(2)}) collective-permute-start(bf16[232,1792]{1,0:T(8,128)(2,1)S(1)} %get-tuple-element.83), channel_id=1, source_target_pairs={{0,4},{1,5},{2,6},{3,7},{4,0},{5,1},{6,2},{7,3},{8,12},{9,13},{10,... | collective-permute-start | bytes 2494472 | tf_op jit(solution)/shard_map/ppermute | solution.py:90
  23.1 19.6 %collective-permute-start.3 = (bf16[224,1792]{1,0:T(8,128)(2,1)S(1)}, bf16[224,1792]{1,0:T(8,128)(2,1)S(1)}, u32[]{:S(2)}, u32[]{:S(2)}) collective-permute-start(bf16[224,1792]{1,0:T(8,128)(2,1)S(1)} %get-tuple-element.82), channel_id=1, source_target_pairs={{0,2},{1,3},{2,0},{3,1},{4,6},{5,7},{6,4},{7,5},{8,10},{9,11},{10,... | collective-permute-start | bytes 2408456 | tf_op jit(solution)/shard_map/ppermute | solution.py:90
  23.6 19.1 %collective-permute-start.5 = (bf16[216,1792]{1,0:T(8,128)(2,1)S(1)}, bf16[216,1792]{1,0:T(8,128)(2,1)S(1)}, u32[]{:S(2)}, u32[]{:S(2)}) collective-permute-start(bf16[216,1792]{1,0:T(8,128)(2,1)S(1)} %get-tuple-element.84), channel_id=1, source_target_pairs={{0,8},{1,9},{2,10},{3,11},{4,12},{5,13},{6,14},{7,15},{8,16},{9,17... | collective-permute-start | bytes 2322440 | tf_op jit(solution)/shard_map/ppermute | solution.py:90
  42.9 20.0 %collective-permute-start.8 = (bf16[240,1792]{1,0:T(8,128)(2,1)S(1)}, bf16[240,1792]{1,0:T(8,128)(2,1)S(1)}, u32[]{:S(2)}, u32[]{:S(2)}) collective-permute-start(bf16[240,1792]{1,0:T(8,128)(2,1)S(1)} %get-tuple-element.102), channel_id=1, source_target_pairs={{0,8},{1,9},{2,10},{3,11},{4,12},{5,13},{6,14},{7,15},{8,16},{9,17... | collective-permute-start | bytes 2580488 | tf_op jit(solution)/shard_map/ppermute | solution.py:90
  43.0 17.0 %collective-permute-start.6 = (bf16[224,1792]{1,0:T(8,128)(2,1)S(1)}, bf16[224,1792]{1,0:T(8,128)(2,1)S(1)}, u32[]{:S(2)}, u32[]{:S(2)}) collective-permute-start(bf16[224,1792]{1,0:T(8,128)(2,1)S(1)} %get-tuple-element.100), channel_id=1, source_target_pairs={{0,2},{1,3},{2,0},{3,1},{4,6},{5,7},{6,4},{7,5},{8,10},{9,11},{10,... | collective-permute-start | bytes 2408456 | tf_op jit(solution)/shard_map/ppermute | solution.py:90
  44.3 15.3 %collective-permute-start.7 = (bf16[208,1792]{1,0:T(8,128)(2,1)S(1)}, bf16[208,1792]{1,0:T(8,128)(2,1)S(1)}, u32[]{:S(2)}, u32[]{:S(2)}) collective-permute-start(bf16[208,1792]{1,0:T(8,128)(2,1)S(1)} %get-tuple-element.101), channel_id=1, source_target_pairs={{0,4},{1,5},{2,6},{3,7},{4,0},{5,1},{6,2},{7,3},{8,12},{9,13},{10,... | collective-permute-start | bytes 2236424 | tf_op jit(solution)/shard_map/ppermute | solution.py:90
  45.8 19.8 %collective-permute-start.12 = (bf16[256,1792]{1,0:T(8,128)(2,1)S(1)}, bf16[256,1792]{1,0:T(8,128)(2,1)S(1)}, u32[]{:S(2)}, u32[]{:S(2)}) collective-permute-start(bf16[256,1792]{1,0:T(8,128)(2,1)S(1)} %get-tuple-element.114.refs_7_.refs_8_.refs_3_), channel_id=1, source_target_pairs={{0,1},{1,0},{2,3},{3,2},{4,5},{5,4},{6,7},{7,6},{8,9},{9,8},{10,11... | collective-permute-start | bytes 2752520 | tf_op jit(solution)/shard_map/ppermute | solution.py:90
  63.0 10.0 %collective-permute-start.10 = (bf16[144,1792]{1,0:T(8,128)(2,1)S(1)}, bf16[144,1792]{1,0:T(8,128)(2,1)S(1)}, u32[]{:S(2)}, u32[]{:S(2)}) collective-permute-start(bf16[144,1792]{1,0:T(8,128)(2,1)S(1)} %get-tuple-element.109), channel_id=1, source_target_pairs={{0,4},{1,5},{2,6},{3,7},{4,0},{5,1},{6,2},{7,3},{8,12},{9,13},{10,... | collective-permute-start | bytes 1548296 | tf_op jit(solution)/shard_map/ppermute | solution.py:90
  64.1 11.2 %collective-permute-start.11 = (bf16[144,1792]{1,0:T(8,128)(2,1)S(1)}, bf16[144,1792]{1,0:T(8,128)(2,1)S(1)}, u32[]{:S(2)}, u32[]{:S(2)}) collective-permute-start(bf16[144,1792]{1,0:T(8,128)(2,1)S(1)} %get-tuple-element.110), channel_id=1, source_target_pairs={{0,8},{1,9},{2,10},{3,11},{4,12},{5,13},{6,14},{7,15},{8,16},{9,17... | collective-permute-start | bytes 1548296 | tf_op jit(solution)/shard_map/ppermute | solution.py:90
  64.1 11.2 %collective-permute-start.9 = (bf16[144,1792]{1,0:T(8,128)(2,1)S(1)}, bf16[144,1792]{1,0:T(8,128)(2,1)S(1)}, u32[]{:S(2)}, u32[]{:S(2)}) collective-permute-start(bf16[144,1792]{1,0:T(8,128)(2,1)S(1)} %get-tuple-element.109), channel_id=1, source_target_pairs={{0,2},{1,3},{2,0},{3,1},{4,6},{5,7},{6,4},{7,5},{8,10},{9,11},{10,... | collective-permute-start | bytes 1548296 | tf_op jit(solution)/shard_map/ppermute | solution.py:90
  75.4 9.7 %collective-permute-start.14 = (bf16[136,1792]{1,0:T(8,128)(2,1)S(1)}, bf16[136,1792]{1,0:T(8,128)(2,1)S(1)}, u32[]{:S(2)}, u32[]{:S(2)}) collective-permute-start(bf16[136,1792]{1,0:T(8,128)(2,1)S(1)} %get-tuple-element.123), channel_id=1, source_target_pairs={{0,4},{1,5},{2,6},{3,7},{4,0},{5,1},{6,2},{7,3},{8,12},{9,13},{10,... | collective-permute-start | bytes 1462280 | tf_op jit(solution)/shard_map/ppermute | solution.py:90
  76.6 8.5 %collective-permute-start.13 = (bf16[128,1792]{1,0:T(8,128)(2,1)S(1)}, bf16[128,1792]{1,0:T(8,128)(2,1)S(1)}, u32[]{:S(2)}, u32[]{:S(2)}) collective-permute-start(bf16[128,1792]{1,0:T(8,128)(2,1)S(1)} %get-tuple-element.122), channel_id=1, source_target_pairs={{0,2},{1,3},{2,0},{3,1},{4,6},{5,7},{6,4},{7,5},{8,10},{9,11},{10,... | collective-permute-start | bytes 1376264 | tf_op jit(solution)/shard_map/ppermute | solution.py:90
  86.2 2.5 %collective-permute-start.15 = (bf16[256,1792]{1,0:T(8,128)(2,1)S(1)}, bf16[256,1792]{1,0:T(8,128)(2,1)S(1)}, u32[]{:S(2)}, u32[]{:S(2)}) collective-permute-start(bf16[256,1792]{1,0:T(8,128)(2,1)S(1)} %finish_other.1), channel_id=1, source_target_pairs={{0,1},{1,0},{2,3},{3,2},{4,5},{5,4},{6,7},{7,6},{8,9},{9,8},{10,11... | collective-permute-start | bytes 2752520 | tf_op jit(solution)/shard_map/ppermute | solution.py:90

commit v8 on v7

--- a/solution.py
+++ b/solution.py
@@ -591,11 +591,12 @@
     )
     near2, far2, deep2 = together(near2, far2, deep2)
 
+    held = 2 * main // 3
     deep3_main, line = collect(
         (far2, deep2),
         (
             ((1, 0, wide),),
-            ((1, wide, wide + 4 * narrow), (0, wide + wide - cut - main, wide + wide - cut)),
+            ((1, wide, wide + 4 * narrow), (0, 2 * wide - cut - main, 2 * wide - cut - main + held)),
         ),
         "collect_fourth",
     )
@@ -615,13 +616,12 @@
     )
     near3, far3, deep3, *acc = together(near3, far3, deep3, *acc)
 
-    held = 2 * main // 3
+    two = 2 * main
     sends = collect(
         (near2, far2, near3, far3, deep3),
         (
-            ((1, 0, main), (3, 0, main), (3, 2 * main, 2 * main + held)),
-            ((0, main, 2 * main), (2, main, 2 * main), (2, 2 * main + held, wide))
-            + ((4, narrow, 2 * narrow),),
+            ((1, 0, main), (1, two + held, wide), (3, 0, main), (3, two, two + held)),
+            ((0, main, two), (2, main, two), (2, two + held, wide), (4, narrow, 2 * narrow)),
         ),
         "collect_fifth",
     )
@@ -635,12 +635,13 @@
         "accumulate_fourth",
     )
     weights = (near4, far4, deep3)
-    two, tail = 2 * main, 2 * main + main - held
+    line, then = 4 * narrow, two - held
     last = [
-        ((0, 0, main), (1, 0, main), (2, 4 * narrow, 4 * narrow + main)),
-        ((0, main, main + held), (1, main, main + held), (0, two, two + held)),
-        ((0, main + held, two), (1, main + held, two), (1, two, tail)),
-        runs(1, tail, edge),
+        ((0, 0, held), (1, 0, held), (2, line, line + held)),
+        ((0, held, main), (1, held, main), (0, main, then)),
+        ((0, then, then + held), (1, main, main + held), (0, then + main, then + main + held)),
+        ((0, then + held, then + main), (1, main + held, two), (1, two, two + main - held)),
+        runs(1, two + main - held, edge),
     ]
     (given,) = accumulate(rows[1:], weights, last, acc[1:], jnp.bfloat16, "finish_other")
     (kept,) = accumulate(

time: 90.3 us -> 90.6 us (level)
  transfers between devices with their start and end apart: 16 -> 16, of which waited for: 9 -> 8; matrix products, arithmetic and copies ran while one was open for 1% -> 1% of each run, Pallas kernels for 23% -> 23%
where the time goes in v8:
time: 90.6 us; the launch traced here: 90.1 us
  waiting for transfers between devices  41 us (45%)
  Pallas kernels  25.4 us (28%)
  starting transfers between devices  15.7 us (17%)
  local copies, waits for them, and re-layouts  6.61 us (7%)
  between operations  1.46 us (2%)
    ppermute x16, waiting for transfers between devices, permute(): return lax.ppermute(array, 'req', [(i, target(i)) for i in range(count)])  41 us
    pallas_call x14, Pallas kernels, kernel_call(): pl.pallas_call(body, out_shape=out_shape, in_specs=specs or vmem(len(oper...  25.4 us
    ppermute x16, starting transfers between devices, permute(): return lax.ppermute(array, 'req', [(i, target(i)) for i in range(count)])  15.7 us
    unnamed x20, local copies, waits for them, and re-layouts  5.89 us
  transfers between devices with their start and end apart: 16, of which 8 were waited for; matrix products, arithmetic and copies ran while one was open for 1% of the time, Pallas kernels for 23%

profile of v8, /device:TPU:0, one launch (start us, length us, event | category | flops | bytes accessed | tf_op | source)
XLA Modules:
  0.0 90.1 jit_solution(17705111864596975430)
XLA Ops:
  0.6 2.2 %shard.1 = (bf16[168,1792]{1,0:T(8,128)(2,1)}, bf16[144,1792]{1,0:T(8,128)(2,1)}) custom-call(bf16[56,1792]{1,0:T(8,128)(2,1)} %bitcast.17, bf16[56,1792]{1,0:T(8,128)(2,1)} %bitcast.18, bf16[56,1792]{1,0:T(8,128)(2,1)} %bitcast.19), custom_call_target="tpu_custom_call" | custom-call | flops 1000 | bytes 1000 | tf_op jit(solution)/shard_map/shard/pallas_call | solution.py:125
  2.8 3.0 %collective-permute-start = (bf16[168,1792]{1,0:T(8,128)(2,1)}, bf16[168,1792]{1,0:T(8,128)(2,1)S(1)}, u32[]{:S(2)}, u32[]{:S(2)}) collective-permute-start(bf16[168,1792]{1,0:T(8,128)(2,1)} %get-tuple-element.71.refs_0_), channel_id=1, source_target_pairs={{0,2},{1,3},{2,0},{3,1},{4,6},{5,7},{6,4},{7,5},{8,10},{9,11},{10,... | collective-permute-start | bytes 1806344 | tf_op jit(solution)/shard_map/ppermute | solution.py:90
  5.8 1.5 %collective-permute-start.1 = (bf16[168,1792]{1,0:T(8,128)(2,1)}, bf16[168,1792]{1,0:T(8,128)(2,1)S(1)}, u32[]{:S(2)}, u32[]{:S(2)}) collective-permute-start(bf16[168,1792]{1,0:T(8,128)(2,1)} %get-tuple-element.71.refs_0_), channel_id=1, source_target_pairs={{0,4},{1,5},{2,6},{3,7},{4,0},{5,1},{6,2},{7,3},{8,12},{9,13},{10,... | collective-permute-start | bytes 1806344 | tf_op jit(solution)/shard_map/ppermute | solution.py:90
  7.4 1.6 %collective-permute-start.2 = (bf16[144,1792]{1,0:T(8,128)(2,1)}, bf16[144,1792]{1,0:T(8,128)(2,1)S(1)}, u32[]{:S(2)}, u32[]{:S(2)}) collective-permute-start(bf16[144,1792]{1,0:T(8,128)(2,1)} %get-tuple-element.72), channel_id=1, source_target_pairs={{0,8},{1,9},{2,10},{3,11},{4,12},{5,13},{6,14},{7,15},{8,16},{9,17... | collective-permute-start | bytes 1548296 | tf_op jit(solution)/shard_map/ppermute | solution.py:90
  8.9 0.7 broadcast_in_dim.16.gain_ref
  9.7 0.0 copy-start.1
  9.7 1.2 %copy-done.1 = bf16[1,256,1792]{2,1,0:T(8,128)(2,1)S(1)} copy-done((bf16[1,256,1792]{2,1,0:T(8,128)(2,1)S(1)}, bf16[1,256,1792]{2,1,0:T(8,128)(2,1)}, u32[]{:S(2)}) %copy-start.1) | copy-done | bytes 917528
  10.8 1.9 %copy-done.3 = bf16[1792,896]{1,0:T(8,128)(2,1)S(1)} copy-done((bf16[1792,896]{1,0:T(8,128)(2,1)S(1)}, bf16[1792,896]{1,0:T(8,128)(2,1)}, u32[]{:S(2)}) %copy-start.3) | copy-done | bytes 3211288
  12.7 1.0 %copy-done.5 = bf16[1792,128]{1,0:T(8,128)(2,1)S(1)} copy-done((bf16[1792,128]{1,0:T(8,128)(2,1)S(1)}, bf16[1792,128]{1,0:T(8,128)(2,1)}, u32[]{:S(2)}) %copy-start.5) | copy-done | bytes 458776
  13.8 1.0 %copy-done.6 = bf16[1792,128]{1,0:T(8,128)(2,1)S(1)} copy-done((bf16[1792,128]{1,0:T(8,128)(2,1)S(1)}, bf16[1792,128]{1,0:T(8,128)(2,1)}, u32[]{:S(2)}) %copy-start.6) | copy-done | bytes 458776
  14.8 0.7 copy-done.7
  15.5 3.7 %project.1 = (bf16[256,128]{1,0:T(8,128)(2,1)S(1)}, bf16[256,128]{1,0:T(8,128)(2,1)S(1)}, bf16[256,896]{1,0:T(8,128)(2,1)S(1)}) custom-call(bf16[256,1792]{1,0:T(8,128)(2,1)S(1)} %bitcast.13, bf16[16,1792]{1,0:T(8,128)(2,1)S(1)} %broadcast_in_dim.15.edge_ref, f32[1,1792]{1,0:T(1,128)S(1)} %broadcast_in_dim.16.gain_ref, f32[3,1792]{1,0:T(4,128)S(1)} %copy-done.7, ...), custom_call_target="tpu_custom_call" | custom-call | flops 1000 | bytes 1000 | tf_op jit(solution)/shard_map/project/pallas_call | solution.py:125
  19.3 0.0 copy-start.9
  19.3 0.0 copy-start.8
  19.3 0.0 copy-start.2
  19.3 3.1 %collective-permute-done.2.refs_3_ = bf16[144,1792]{1,0:T(8,128)(2,1)S(1)} collective-permute-done((bf16[144,1792]{1,0:T(8,128)(2,1)}, bf16[144,1792]{1,0:T(8,128)(2,1)S(1)}, u32[]{:S(2)}, u32[]{:S(2)}) %collective-permute-start.2) | collective-permute-done | bytes 516128 | tf_op jit(solution)/shard_map/ppermute | solution.py:90
  22.4 0.0 collective-permute-done.refs_1_
  22.4 0.2 collect_second.1
  22.5 0.6 collective-permute-start.4
  23.1 0.5 collective-permute-start.3
  23.6 1.3 %collective-permute-start.5 = (bf16[216,1792]{1,0:T(8,128)(2,1)S(1)}, bf16[216,1792]{1,0:T(8,128)(2,1)S(1)}, u32[]{:S(2)}, u32[]{:S(2)}) collective-permute-start(bf16[216,1792]{1,0:T(8,128)(2,1)S(1)} %get-tuple-element.84), channel_id=1, source_target_pairs={{0,8},{1,9},{2,10},{3,11},{4,12},{5,13},{6,14},{7,15},{8,16},{9,17... | collective-permute-start | bytes 2322440 | tf_op jit(solution)/shard_map/ppermute | solution.py:90
  25.7 3.7 %attend.1 = (f32[256,896]{1,0:T(8,128)S(1)}, f32[256,8]{1,0:T(8,128)S(1)}, f32[273,1,896]{2,1,0:T(1,128)}, f32[8,273]{1,0:T(8,128)}) custom-call(s32[1]{0:T(128)S(6)} %copy.27.count_ref, f32[8,256]{1,0:T(8,128)S(1)} %bitcast.15, bf16[256,128]{1,0:T(8,128)(2,1)S(1)} %get-tuple-element.88.queries_ref, bf16[256,128]{1,0:T(8,128)(2,1)S(1)} %get-tuple-element.89.keys_ref, ...), custom_call_target="tpu_custom_call" | custom-call | flops 1000 | bytes 1000 | tf_op jit(solution)/shard_map/attend/pallas_call | solution.py:125
  29.4 2.6 %mix.1 = (bf16[256,1792]{1,0:T(8,128)(2,1)S(1)}, bf16[256,1792]{1,0:T(8,128)(2,1)S(1)}) custom-call(f32[256,896]{1,0:T(8,128)S(1)} %get-tuple-element.91.numer_ref, f32[256,8]{1,0:T(8,128)S(1)} %get-tuple-element.92.denom_ref, bf16[256,1792]{1,0:T(8,128)(2,1)S(1)} %bitcast.14, bf16[896,1792]{1,0:T(8,128)(2,1)S(1)} %copy-done.4, ...), custom_call_target="tpu_custom_call" | custom-call | flops 1000 | bytes 1000 | tf_op jit(solution)/shard_map/mix/pallas_call | solution.py:125
  32.0 10.7 %collective-permute-done.5.refs_2_.refs_6_.refs_4_ = bf16[216,1792]{1,0:T(8,128)(2,1)S(1)} collective-permute-done((bf16[216,1792]{1,0:T(8,128)(2,1)S(1)}, bf16[216,1792]{1,0:T(8,128)(2,1)S(1)}, u32[]{:S(2)}, u32[]{:S(2)}) %collective-permute-start.5) | collective-permute-done | bytes 774176 | tf_op jit(solution)/shard_map/ppermute | solution.py:90
  42.7 0.2 collect_third.1
  42.9 0.1 collective-permute-start.8
  43.0 1.4 %collective-permute-start.6 = (bf16[224,1792]{1,0:T(8,128)(2,1)S(1)}, bf16[224,1792]{1,0:T(8,128)(2,1)S(1)}, u32[]{:S(2)}, u32[]{:S(2)}) collective-permute-start(bf16[224,1792]{1,0:T(8,128)(2,1)S(1)} %get-tuple-element.100), channel_id=1, source_target_pairs={{0,2},{1,3},{2,0},{3,1},{4,6},{5,7},{6,4},{7,5},{8,10},{9,11},{10,... | collective-permute-start | bytes 2408456 | tf_op jit(solution)/shard_map/ppermute | solution.py:90
  44.3 1.5 %collective-permute-start.7 = (bf16[208,1792]{1,0:T(8,128)(2,1)S(1)}, bf16[208,1792]{1,0:T(8,128)(2,1)S(1)}, u32[]{:S(2)}, u32[]{:S(2)}) collective-permute-start(bf16[208,1792]{1,0:T(8,128)(2,1)S(1)} %get-tuple-element.101), channel_id=1, source_target_pairs={{0,4},{1,5},{2,6},{3,7},{4,0},{5,1},{6,2},{7,3},{8,12},{9,13},{10,... | collective-permute-start | bytes 2236424 | tf_op jit(solution)/shard_map/ppermute | solution.py:90
  45.8 13.8 %collective-permute-done.7.refs_0_.refs_6_.refs_1_ = bf16[208,1792]{1,0:T(8,128)(2,1)S(1)} collective-permute-done((bf16[208,1792]{1,0:T(8,128)(2,1)S(1)}, bf16[208,1792]{1,0:T(8,128)(2,1)S(1)}, u32[]{:S(2)}, u32[]{:S(2)}) %collective-permute-start.7) | collective-permute-done | bytes 745504 | tf_op jit(solution)/shard_map/ppermute | solution.py:90
  59.6 0.4 collective-permute-done.6.refs_5_.refs_0_
  60.0 2.9 %collective-permute-done.8.refs_1_.refs_7_ = bf16[240,1792]{1,0:T(8,128)(2,1)S(1)} collective-permute-done((bf16[240,1792]{1,0:T(8,128)(2,1)S(1)}, bf16[240,1792]{1,0:T(8,128)(2,1)S(1)}, u32[]{:S(2)}, u32[]{:S(2)}) %collective-permute-start.8) | collective-permute-done | bytes 860192 | tf_op jit(solution)/shard_map/ppermute | solution.py:90
  62.9 0.1 collect_fourth.1
  63.0 1.1 %collective-permute-start.10 = (bf16[144,1792]{1,0:T(8,128)(2,1)S(1)}, bf16[144,1792]{1,0:T(8,128)(2,1)S(1)}, u32[]{:S(2)}, u32[]{:S(2)}) collective-permute-start(bf16[144,1792]{1,0:T(8,128)(2,1)S(1)} %get-tuple-element.109), channel_id=1, source_target_pairs={{0,4},{1,5},{2,6},{3,7},{4,0},{5,1},{6,2},{7,3},{8,12},{9,13},{10,... | collective-permute-start | bytes 1548296 | tf_op jit(solution)/shard_map/ppermute | solution.py:90
  64.1 1.5 %collective-permute-start.9 = (bf16[144,1792]{1,0:T(8,128)(2,1)S(1)}, bf16[144,1792]{1,0:T(8,128)(2,1)S(1)}, u32[]{:S(2)}, u32[]{:S(2)}) collective-permute-start(bf16[144,1792]{1,0:T(8,128)(2,1)S(1)} %get-tuple-element.109), channel_id=1, source_target_pairs={{0,2},{1,3},{2,0},{3,1},{4,6},{5,7},{6,4},{7,5},{8,10},{9,11},{10,... | collective-permute-start | bytes 1548296 | tf_op jit(solution)/shard_map/ppermute | solution.py:90
  65.6 0.0 collective-permute-start.11
  65.6 3.2 %accumulate_second.1 = (f32[256,1792]{1,0:T(8,128)S(1)}, f32[256,1792]{1,0:T(8,128)S(1)}) custom-call(bf16[168,1792]{1,0:T(8,128)(2,1)S(1)} %copy-done, bf16[168,1792]{1,0:T(8,128)(2,1)S(1)} %collective-permute-done.refs_1_, bf16[168,1792]{1,0:T(8,128)(2,1)S(1)} %collective-permute-done.1.refs_2_, bf16[144,1792]{1,0:T(8,128)(2,1)S(1)} %collective-permute-done.2.refs_3_, ...), custom_call_target="tpu_custom_call" | custom-call | flops 1000 | bytes 1000 | tf_op jit(solution)/shard_map/accumulate_second/pallas_call | solution.py:125
  68.8 3.9 %accumulate_third.1 = (f32[256,1792]{1,0:T(8,128)S(1)}, f32[256,1792]{1,0:T(8,128)S(1)}) custom-call(bf16[168,1792]{1,0:T(8,128)(2,1)S(1)} %copy-done, bf16[168,1792]{1,0:T(8,128)(2,1)S(1)} %collective-permute-done.refs_1_, bf16[168,1792]{1,0:T(8,128)(2,1)S(1)} %collective-permute-done.1.refs_2_, ...), custom_call_target="tpu_custom_call", output_to_operand_aliasing={{0}: (10, {}), {1}: (11, {})} | custom-call | flops 1000 | bytes 1000 | tf_op jit(solution)/shard_map/accumulate_third/pallas_call | solution.py:125
  72.7 3.1 %collective-permute-done.11.refs_4_.refs_2_ = bf16[128,1792]{1,0:T(8,128)(2,1)S(1)} collective-permute-done((bf16[128,1792]{1,0:T(8,128)(2,1)S(1)}, bf16[128,1792]{1,0:T(8,128)(2,1)S(1)}, u32[]{:S(2)}, u32[]{:S(2)}) %collective-permute-start.11) | collective-permute-done | bytes 458784 | tf_op jit(solution)/shard_map/ppermute | solution.py:90
  75.9 0.1 collect_fifth.1
  76.0 0.6 collective-permute-start.13
  76.6 0.9 %collective-permute-start.14 = (bf16[136,1792]{1,0:T(8,128)(2,1)S(1)}, bf16[136,1792]{1,0:T(8,128)(2,1)S(1)}, u32[]{:S(2)}, u32[]{:S(2)}) collective-permute-start(bf16[136,1792]{1,0:T(8,128)(2,1)S(1)} %get-tuple-element.123), channel_id=1, source_target_pairs={{0,4},{1,5},{2,6},{3,7},{4,0},{5,1},{6,2},{7,3},{8,12},{9,13},{10,... | collective-permute-start | bytes 1462280 | tf_op jit(solution)/shard_map/ppermute | solution.py:90
  77.5 2.0 %accumulate_fourth.1 = (f32[256,1792]{1,0:T(8,128)S(1)}, f32[256,1792]{1,0:T(8,128)S(1)}) custom-call(bf16[144,1792]{1,0:T(8,128)(2,1)S(1)} %collective-permute-done.9.refs_2_.refs_0_, bf16[144,1792]{1,0:T(8,128)(2,1)S(1)} %collective-permute-done.10.refs_3_.refs_1_, ...), custom_call_target="tpu_custom_call", output_to_operand_aliasing={{0}: (5, {}), {1}: (6, {})} | custom-call | flops 1000 | bytes 1000 | tf_op jit(solution)/shard_map/accumulate_fourth/pallas_call | solution.py:125
  79.5 5.9 %collective-permute-done.14.refs_1_ = bf16[136,1792]{1,0:T(8,128)(2,1)S(1)} collective-permute-done((bf16[136,1792]{1,0:T(8,128)(2,1)S(1)}, bf16[136,1792]{1,0:T(8,128)(2,1)S(1)}, u32[]{:S(2)}, u32[]{:S(2)}) %collective-permute-start.14) | collective-permute-done | bytes 487456 | tf_op jit(solution)/shard_map/ppermute | solution.py:90
  85.4 1.0 %finish_other.1 = bf16[256,1792]{1,0:T(8,128)(2,1)S(1)} custom-call(bf16[144,1792]{1,0:T(8,128)(2,1)S(1)} %collective-permute-done.13.refs_0_, bf16[136,1792]{1,0:T(8,128)(2,1)S(1)} %collective-permute-done.14.refs_1_, bf16[128,1792]{1,0:T(8,128)(2,1)S(1)} %collective-permute-done.11.refs_4_.refs_2_, ...), custom_call_target="tpu_custom_call" | custom-call | flops 1000 | bytes 1000 | tf_op jit(solution)/shard_map/finish_other/pallas_call | solution.py:125
  86.4 0.1 collective-permute-start.15
  86.5 1.4 %finish_own.1.kept_ref = f32[256,1792]{1,0:T(8,128)S(1)} custom-call(bf16[144,1792]{1,0:T(8,128)(2,1)S(1)} %collective-permute-done.13.refs_0_, bf16[136,1792]{1,0:T(8,128)(2,1)S(1)} %collective-permute-done.14.refs_1_, bf16[128,1792]{1,0:T(8,128)(2,1)S(1)} %collective-permute-done.11.refs_4_.refs_2_, ...), custom_call_target="tpu_custom_call", output_to_operand_aliasing={{}: (4, {})} | custom-call | flops 1000 | bytes 1000 | tf_op jit(solution)/shard_map/finish_own/pallas_call | solution.py:125
  87.9 1.1 %collective-permute-done.15.given_ref = bf16[256,1792]{1,0:T(8,128)(2,1)S(1)} collective-permute-done((bf16[256,1792]{1,0:T(8,128)(2,1)S(1)}, bf16[256,1792]{1,0:T(8,128)(2,1)S(1)}, u32[]{:S(2)}, u32[]{:S(2)}) %collective-permute-start.15) | collective-permute-done | bytes 917536 | tf_op jit(solution)/shard_map/ppermute | solution.py:90
  88.9 1.2 %final.1 = bf16[256,1792]{1,0:T(8,128)(2,1)} custom-call(s32[1]{0:T(128)S(6)} %copy.27.count_ref, f32[256,1792]{1,0:T(8,128)S(1)} %finish_own.1.kept_ref, bf16[256,1792]{1,0:T(8,128)(2,1)S(1)} %collective-permute-done.15.given_ref), custom_call_target="tpu_custom_call" | custom-call | flops 1000 | bytes 1000 | tf_op jit(solution)/shard_map/final/pallas_call | solution.py:125
  (21 shorter events, 0.1 us)
Async XLA Ops:
  2.8 19.5 %collective-permute-start = (bf16[168,1792]{1,0:T(8,128)(2,1)}, bf16[168,1792]{1,0:T(8,128)(2,1)S(1)}, u32[]{:S(2)}, u32[]{:S(2)}) collective-permute-start(bf16[168,1792]{1,0:T(8,128)(2,1)} %get-tuple-element.71.refs_0_), channel_id=1, source_target_pairs={{0,2},{1,3},{2,0},{3,1},{4,6},{5,7},{6,4},{7,5},{8,10},{9,11},{10,... | collective-permute-start | bytes 1806344 | tf_op jit(solution)/shard_map/ppermute | solution.py:90
  5.8 16.5 %collective-permute-start.1 = (bf16[168,1792]{1,0:T(8,128)(2,1)}, bf16[168,1792]{1,0:T(8,128)(2,1)S(1)}, u32[]{:S(2)}, u32[]{:S(2)}) collective-permute-start(bf16[168,1792]{1,0:T(8,128)(2,1)} %get-tuple-element.71.refs_0_), channel_id=1, source_target_pairs={{0,4},{1,5},{2,6},{3,7},{4,0},{5,1},{6,2},{7,3},{8,12},{9,13},{10,... | collective-permute-start | bytes 1806344 | tf_op jit(solution)/shard_map/ppermute | solution.py:90
  7.4 15.0 %collective-permute-start.2 = (bf16[144,1792]{1,0:T(8,128)(2,1)}, bf16[144,1792]{1,0:T(8,128)(2,1)S(1)}, u32[]{:S(2)}, u32[]{:S(2)}) collective-permute-start(bf16[144,1792]{1,0:T(8,128)(2,1)} %get-tuple-element.72), channel_id=1, source_target_pairs={{0,8},{1,9},{2,10},{3,11},{4,12},{5,13},{6,14},{7,15},{8,16},{9,17... | collective-permute-start | bytes 1548296 | tf_op jit(solution)/shard_map/ppermute | solution.py:90
  9.7 1.2 %copy-start.1 = (bf16[1,256,1792]{2,1,0:T(8,128)(2,1)S(1)}, bf16[1,256,1792]{2,1,0:T(8,128)(2,1)}, u32[]{:S(2)}) copy-start(bf16[1,256,1792]{2,1,0:T(8,128)(2,1)} %param.13) | copy-start | bytes 2752516
  10.8 1.9 %copy-start.3 = (bf16[1792,896]{1,0:T(8,128)(2,1)S(1)}, bf16[1792,896]{1,0:T(8,128)(2,1)}, u32[]{:S(2)}) copy-start(bf16[1792,896]{1,0:T(8,128)(2,1)} %value_ref.1) | copy-start | bytes 9633796
  12.7 1.0 %copy-start.5 = (bf16[1792,128]{1,0:T(8,128)(2,1)S(1)}, bf16[1792,128]{1,0:T(8,128)(2,1)}, u32[]{:S(2)}) copy-start(bf16[1792,128]{1,0:T(8,128)(2,1)} %query_ref.1) | copy-start | bytes 1376260
  13.8 1.0 %copy-start.6 = (bf16[1792,128]{1,0:T(8,128)(2,1)S(1)}, bf16[1792,128]{1,0:T(8,128)(2,1)}, u32[]{:S(2)}) copy-start(bf16[1792,128]{1,0:T(8,128)(2,1)} %key_ref.1) | copy-start | bytes 1376260
  14.8 0.7 copy-start.7
  15.5 6.8 %copy-start = (bf16[168,1792]{1,0:T(8,128)(2,1)S(1)}, bf16[168,1792]{1,0:T(8,128)(2,1)}, u32[]{:S(2)}) copy-start(bf16[168,1792]{1,0:T(8,128)(2,1)} %get-tuple-element.71.refs_0_) | copy-start | bytes 1806340
  15.5 13.8 %copy-start.4 = (bf16[896,1792]{1,0:T(8,128)(2,1)S(1)}, bf16[896,1792]{1,0:T(8,128)(2,1)}, u32[]{:S(2)}) copy-start(bf16[896,1792]{1,0:T(8,128)(2,1)} %out_ref.1) | copy-start | bytes 9633796
  19.3 6.4 %copy-start.9 = (f32[1792]{0:T(1024)S(1)}, f32[1792]{0:T(1024)}, u32[]{:S(2)}) copy-start(f32[1792]{0:T(1024)} %param.22) | copy-start | bytes 21508
  19.3 6.4 %copy-start.8 = (f32[1,256,8]{1,2,0:T(8,128)S(1)}, f32[1,256,8]{1,2,0:T(8,128)}, u32[]{:S(2)}) copy-start(f32[1,256,8]{1,2,0:T(8,128)} %param.15) | copy-start | bytes 24580
  19.3 10.1 %copy-start.2 = (bf16[1,256,1792]{2,1,0:T(8,128)(2,1)S(1)}, bf16[1,256,1792]{2,1,0:T(8,128)(2,1)}, u32[]{:S(2)}) copy-start(bf16[1,256,1792]{2,1,0:T(8,128)(2,1)} %param.13) | copy-start | bytes 2752516
  22.5 20.2 %collective-permute-start.4 = (bf16[232,1792]{1,0:T(8,128)(2,1)S(1)}, bf16[232,1792]{1,0:T(8,128)(2,1)S(1)}, u32[]{:S(2)}, u32[]{:S(2)}) collective-permute-start(bf16[232,1792]{1,0:T(8,128)(2,1)S(1)} %get-tuple-element.83), channel_id=1, source_target_pairs={{0,4},{1,5},{2,6},{3,7},{4,0},{5,1},{6,2},{7,3},{8,12},{9,13},{10,... | collective-permute-start | bytes 2494472 | tf_op jit(solution)/shard_map/ppermute | solution.py:90
  23.1 19.6 %collective-permute-start.3 = (bf16[224,1792]{1,0:T(8,128)(2,1)S(1)}, bf16[224,1792]{1,0:T(8,128)(2,1)S(1)}, u32[]{:S(2)}, u32[]{:S(2)}) collective-permute-start(bf16[224,1792]{1,0:T(8,128)(2,1)S(1)} %get-tuple-element.82), channel_id=1, source_target_pairs={{0,2},{1,3},{2,0},{3,1},{4,6},{5,7},{6,4},{7,5},{8,10},{9,11},{10,... | collective-permute-start | bytes 2408456 | tf_op jit(solution)/shard_map/ppermute | solution.py:90
  23.6 19.1 %collective-permute-start.5 = (bf16[216,1792]{1,0:T(8,128)(2,1)S(1)}, bf16[216,1792]{1,0:T(8,128)(2,1)S(1)}, u32[]{:S(2)}, u32[]{:S(2)}) collective-permute-start(bf16[216,1792]{1,0:T(8,128)(2,1)S(1)} %get-tuple-element.84), channel_id=1, source_target_pairs={{0,8},{1,9},{2,10},{3,11},{4,12},{5,13},{6,14},{7,15},{8,16},{9,17... | collective-permute-start | bytes 2322440 | tf_op jit(solution)/shard_map/ppermute | solution.py:90
  42.9 20.0 %collective-permute-start.8 = (bf16[240,1792]{1,0:T(8,128)(2,1)S(1)}, bf16[240,1792]{1,0:T(8,128)(2,1)S(1)}, u32[]{:S(2)}, u32[]{:S(2)}) collective-permute-start(bf16[240,1792]{1,0:T(8,128)(2,1)S(1)} %get-tuple-element.102), channel_id=1, source_target_pairs={{0,8},{1,9},{2,10},{3,11},{4,12},{5,13},{6,14},{7,15},{8,16},{9,17... | collective-permute-start | bytes 2580488 | tf_op jit(solution)/shard_map/ppermute | solution.py:90
  43.0 17.0 %collective-permute-start.6 = (bf16[224,1792]{1,0:T(8,128)(2,1)S(1)}, bf16[224,1792]{1,0:T(8,128)(2,1)S(1)}, u32[]{:S(2)}, u32[]{:S(2)}) collective-permute-start(bf16[224,1792]{1,0:T(8,128)(2,1)S(1)} %get-tuple-element.100), channel_id=1, source_target_pairs={{0,2},{1,3},{2,0},{3,1},{4,6},{5,7},{6,4},{7,5},{8,10},{9,11},{10,... | collective-permute-start | bytes 2408456 | tf_op jit(solution)/shard_map/ppermute | solution.py:90
  44.3 15.3 %collective-permute-start.7 = (bf16[208,1792]{1,0:T(8,128)(2,1)S(1)}, bf16[208,1792]{1,0:T(8,128)(2,1)S(1)}, u32[]{:S(2)}, u32[]{:S(2)}) collective-permute-start(bf16[208,1792]{1,0:T(8,128)(2,1)S(1)} %get-tuple-element.101), channel_id=1, source_target_pairs={{0,4},{1,5},{2,6},{3,7},{4,0},{5,1},{6,2},{7,3},{8,12},{9,13},{10,... | collective-permute-start | bytes 2236424 | tf_op jit(solution)/shard_map/ppermute | solution.py:90
  45.8 19.8 %collective-permute-start.12 = (bf16[256,1792]{1,0:T(8,128)(2,1)S(1)}, bf16[256,1792]{1,0:T(8,128)(2,1)S(1)}, u32[]{:S(2)}, u32[]{:S(2)}) collective-permute-start(bf16[256,1792]{1,0:T(8,128)(2,1)S(1)} %get-tuple-element.114.refs_7_.refs_8_.refs_3_), channel_id=1, source_target_pairs={{0,1},{1,0},{2,3},{3,2},{4,5},{5,4},{6,7},{7,6},{8,9},{9,8},{10,11... | collective-permute-start | bytes 2752520 | tf_op jit(solution)/shard_map/ppermute | solution.py:90
  63.0 12.9 %collective-permute-start.10 = (bf16[144,1792]{1,0:T(8,128)(2,1)S(1)}, bf16[144,1792]{1,0:T(8,128)(2,1)S(1)}, u32[]{:S(2)}, u32[]{:S(2)}) collective-permute-start(bf16[144,1792]{1,0:T(8,128)(2,1)S(1)} %get-tuple-element.109), channel_id=1, source_target_pairs={{0,4},{1,5},{2,6},{3,7},{4,0},{5,1},{6,2},{7,3},{8,12},{9,13},{10,... | collective-permute-start | bytes 1548296 | tf_op jit(solution)/shard_map/ppermute | solution.py:90
  64.1 11.8 %collective-permute-start.9 = (bf16[144,1792]{1,0:T(8,128)(2,1)S(1)}, bf16[144,1792]{1,0:T(8,128)(2,1)S(1)}, u32[]{:S(2)}, u32[]{:S(2)}) collective-permute-start(bf16[144,1792]{1,0:T(8,128)(2,1)S(1)} %get-tuple-element.109), channel_id=1, source_target_pairs={{0,2},{1,3},{2,0},{3,1},{4,6},{5,7},{6,4},{7,5},{8,10},{9,11},{10,... | collective-permute-start | bytes 1548296 | tf_op jit(solution)/shard_map/ppermute | solution.py:90
  65.6 10.3 %collective-permute-start.11 = (bf16[128,1792]{1,0:T(8,128)(2,1)S(1)}, bf16[128,1792]{1,0:T(8,128)(2,1)S(1)}, u32[]{:S(2)}, u32[]{:S(2)}) collective-permute-start(bf16[128,1792]{1,0:T(8,128)(2,1)S(1)} %get-tuple-element.110), channel_id=1, source_target_pairs={{0,8},{1,9},{2,10},{3,11},{4,12},{5,13},{6,14},{7,15},{8,16},{9,17... | collective-permute-start | bytes 1376264 | tf_op jit(solution)/shard_map/ppermute | solution.py:90
  76.0 9.4 %collective-permute-start.13 = (bf16[144,1792]{1,0:T(8,128)(2,1)S(1)}, bf16[144,1792]{1,0:T(8,128)(2,1)S(1)}, u32[]{:S(2)}, u32[]{:S(2)}) collective-permute-start(bf16[144,1792]{1,0:T(8,128)(2,1)S(1)} %get-tuple-element.122), channel_id=1, source_target_pairs={{0,2},{1,3},{2,0},{3,1},{4,6},{5,7},{6,4},{7,5},{8,10},{9,11},{10,... | collective-permute-start | bytes 1548296 | tf_op jit(solution)/shard_map/ppermute | solution.py:90
  76.6 8.8 %collective-permute-start.14 = (bf16[136,1792]{1,0:T(8,128)(2,1)S(1)}, bf16[136,1792]{1,0:T(8,128)(2,1)S(1)}, u32[]{:S(2)}, u32[]{:S(2)}) collective-permute-start(bf16[136,1792]{1,0:T(8,128)(2,1)S(1)} %get-tuple-element.123), channel_id=1, source_target_pairs={{0,4},{1,5},{2,6},{3,7},{4,0},{5,1},{6,2},{7,3},{8,12},{9,13},{10,... | collective-permute-start | bytes 1462280 | tf_op jit(solution)/shard_map/ppermute | solution.py:90
  86.4 2.5 %collective-permute-start.15 = (bf16[256,1792]{1,0:T(8,128)(2,1)S(1)}, bf16[256,1792]{1,0:T(8,128)(2,1)S(1)}, u32[]{:S(2)}, u32[]{:S(2)}) collective-permute-start(bf16[256,1792]{1,0:T(8,128)(2,1)S(1)} %finish_other.1), channel_id=1, source_target_pairs={{0,1},{1,0},{2,3},{3,2},{4,5},{5,4},{6,7},{7,6},{8,9},{9,8},{10,11... | collective-permute-start | bytes 2752520 | tf_op jit(solution)/shard_map/ppermute | solution.py:90

commit v9 on v8

--- a/solution.py
+++ b/solution.py
@@ -104,7 +104,7 @@
 
 def next_plane(array):
     count = lax.axis_size("req")
-    return permute(array, lambda i: (i + 8) % count)
+    return permute(array, lambda i: (i + (8 if i % 2 else count - 8)) % count)
 
 
 def together(*arrays):

time: 90.6 us -> 96.4 us (1.064)
  starting transfers between devices: 15.7 us -> 21.7 us
    ppermute x16, starting transfers between devices: 15.7 us -> 21.7 us  [permute(): return lax.ppermute(array, 'req', [(i, target(i)) for i in range(count)])]
  transfers between devices with their start and end apart: 16 -> 16, of which waited for: 8 -> 8; matrix products, arithmetic and copies ran while one was open for 1% -> 1% of each run, Pallas kernels for 23% -> 21%
where the time goes in v9:
time: 96.4 us; the launch traced here: 96 us
  waiting for transfers between devices  40.9 us (42%)
  Pallas kernels  25.4 us (26%)
  starting transfers between devices  21.7 us (23%)
  local copies, waits for them, and re-layouts  6.61 us (7%)
  between operations  1.45 us (2%)
    ppermute x16, waiting for transfers between devices, permute(): return lax.ppermute(array, 'req', [(i, target(i)) for i in range(count)])  40.9 us
    pallas_call x14, Pallas kernels, kernel_call(): pl.pallas_call(body, out_shape=out_shape, in_specs=specs or vmem(len(oper...  25.4 us
    ppermute x16, starting transfers between devices, permute(): return lax.ppermute(array, 'req', [(i, target(i)) for i in range(count)])  21.7 us
    unnamed x20, local copies, waits for them, and re-layouts  5.89 us
  transfers between devices with their start and end apart: 16, of which 8 were waited for; matrix products, arithmetic and copies ran while one was open for 1% of the time, Pallas kernels for 21%

profile of v9, /device:TPU:0, one launch (start us, length us, event | category | flops | bytes accessed | tf_op | source)
XLA Modules:
  0.0 96.0 jit_solution(8877796154923184086)
XLA Ops:
  0.6 2.2 %shard.1 = (bf16[168,1792]{1,0:T(8,128)(2,1)}, bf16[144,1792]{1,0:T(8,128)(2,1)}) custom-call(bf16[56,1792]{1,0:T(8,128)(2,1)} %bitcast.17, bf16[56,1792]{1,0:T(8,128)(2,1)} %bitcast.18, bf16[56,1792]{1,0:T(8,128)(2,1)} %bitcast.19), custom_call_target="tpu_custom_call" | custom-call | flops 1000 | bytes 1000 | tf_op jit(solution)/shard_map/shard/pallas_call | solution.py:125
  2.8 3.0 %collective-permute-start = (bf16[168,1792]{1,0:T(8,128)(2,1)}, bf16[168,1792]{1,0:T(8,128)(2,1)S(1)}, u32[]{:S(2)}, u32[]{:S(2)}) collective-permute-start(bf16[168,1792]{1,0:T(8,128)(2,1)} %get-tuple-element.71.refs_0_), channel_id=1, source_target_pairs={{0,2},{1,3},{2,0},{3,1},{4,6},{5,7},{6,4},{7,5},{8,10},{9,11},{10,... | collective-permute-start | bytes 1806344 | tf_op jit(solution)/shard_map/ppermute | solution.py:90
  5.8 1.5 %collective-permute-start.1 = (bf16[168,1792]{1,0:T(8,128)(2,1)}, bf16[168,1792]{1,0:T(8,128)(2,1)S(1)}, u32[]{:S(2)}, u32[]{:S(2)}) collective-permute-start(bf16[168,1792]{1,0:T(8,128)(2,1)} %get-tuple-element.71.refs_0_), channel_id=1, source_target_pairs={{0,4},{1,5},{2,6},{3,7},{4,0},{5,1},{6,2},{7,3},{8,12},{9,13},{10,... | collective-permute-start | bytes 1806344 | tf_op jit(solution)/shard_map/ppermute | solution.py:90
  7.4 3.6 %collective-permute-start.2 = (bf16[144,1792]{1,0:T(8,128)(2,1)}, bf16[144,1792]{1,0:T(8,128)(2,1)S(1)}, u32[]{:S(2)}, u32[]{:S(2)}) collective-permute-start(bf16[144,1792]{1,0:T(8,128)(2,1)} %get-tuple-element.72), channel_id=1, source_target_pairs={{0,24},{1,9},{2,26},{3,11},{4,28},{5,13},{6,30},{7,15},{8,0},{9,17... | collective-permute-start | bytes 1548296 | tf_op jit(solution)/shard_map/ppermute | solution.py:90
  11.0 0.7 broadcast_in_dim.16.gain_ref
  11.7 0.0 copy-start.1
  11.7 1.2 %copy-done.1 = bf16[1,256,1792]{2,1,0:T(8,128)(2,1)S(1)} copy-done((bf16[1,256,1792]{2,1,0:T(8,128)(2,1)S(1)}, bf16[1,256,1792]{2,1,0:T(8,128)(2,1)}, u32[]{:S(2)}) %copy-start.1) | copy-done | bytes 917528
  12.9 1.9 %copy-done.3 = bf16[1792,896]{1,0:T(8,128)(2,1)S(1)} copy-done((bf16[1792,896]{1,0:T(8,128)(2,1)S(1)}, bf16[1792,896]{1,0:T(8,128)(2,1)}, u32[]{:S(2)}) %copy-start.3) | copy-done | bytes 3211288
  14.8 1.0 %copy-done.5 = bf16[1792,128]{1,0:T(8,128)(2,1)S(1)} copy-done((bf16[1792,128]{1,0:T(8,128)(2,1)S(1)}, bf16[1792,128]{1,0:T(8,128)(2,1)}, u32[]{:S(2)}) %copy-start.5) | copy-done | bytes 458776
  15.8 1.0 %copy-done.6 = bf16[1792,128]{1,0:T(8,128)(2,1)S(1)} copy-done((bf16[1792,128]{1,0:T(8,128)(2,1)S(1)}, bf16[1792,128]{1,0:T(8,128)(2,1)}, u32[]{:S(2)}) %copy-start.6) | copy-done | bytes 458776
  16.8 0.7 copy-done.7
  17.6 3.7 %project.1 = (bf16[256,128]{1,0:T(8,128)(2,1)S(1)}, bf16[256,128]{1,0:T(8,128)(2,1)S(1)}, bf16[256,896]{1,0:T(8,128)(2,1)S(1)}) custom-call(bf16[256,1792]{1,0:T(8,128)(2,1)S(1)} %bitcast.13, bf16[16,1792]{1,0:T(8,128)(2,1)S(1)} %broadcast_in_dim.15.edge_ref, f32[1,1792]{1,0:T(1,128)S(1)} %broadcast_in_dim.16.gain_ref, f32[3,1792]{1,0:T(4,128)S(1)} %copy-done.7, ...), custom_call_target="tpu_custom_call" | custom-call | flops 1000 | bytes 1000 | tf_op jit(solution)/shard_map/project/pallas_call | solution.py:125
  21.3 0.0 copy-start.9
  21.3 0.0 copy-start.8
  21.3 0.0 copy-start.2
  21.3 0.9 collective-permute-done.2.refs_3_
  22.2 0.2 collect_second.1
  22.4 0.6 collective-permute-start.4
  23.0 0.4 collective-permute-start.3
  23.4 3.6 %collective-permute-start.5 = (bf16[216,1792]{1,0:T(8,128)(2,1)S(1)}, bf16[216,1792]{1,0:T(8,128)(2,1)S(1)}, u32[]{:S(2)}, u32[]{:S(2)}) collective-permute-start(bf16[216,1792]{1,0:T(8,128)(2,1)S(1)} %get-tuple-element.84), channel_id=1, source_target_pairs={{0,24},{1,9},{2,26},{3,11},{4,28},{5,13},{6,30},{7,15},{8,0},{9,17... | collective-permute-start | bytes 2322440 | tf_op jit(solution)/shard_map/ppermute | solution.py:90
  27.7 3.7 %attend.1 = (f32[256,896]{1,0:T(8,128)S(1)}, f32[256,8]{1,0:T(8,128)S(1)}, f32[273,1,896]{2,1,0:T(1,128)}, f32[8,273]{1,0:T(8,128)}) custom-call(s32[1]{0:T(128)S(6)} %copy.27.count_ref, f32[8,256]{1,0:T(8,128)S(1)} %bitcast.15, bf16[256,128]{1,0:T(8,128)(2,1)S(1)} %get-tuple-element.88.queries_ref, bf16[256,128]{1,0:T(8,128)(2,1)S(1)} %get-tuple-element.89.keys_ref, ...), custom_call_target="tpu_custom_call" | custom-call | flops 1000 | bytes 1000 | tf_op jit(solution)/shard_map/attend/pallas_call | solution.py:125
  31.4 2.6 %mix.1 = (bf16[256,1792]{1,0:T(8,128)(2,1)S(1)}, bf16[256,1792]{1,0:T(8,128)(2,1)S(1)}) custom-call(f32[256,896]{1,0:T(8,128)S(1)} %get-tuple-element.91.numer_ref, f32[256,8]{1,0:T(8,128)S(1)} %get-tuple-element.92.denom_ref, bf16[256,1792]{1,0:T(8,128)(2,1)S(1)} %bitcast.14, bf16[896,1792]{1,0:T(8,128)(2,1)S(1)} %copy-done.4, ...), custom_call_target="tpu_custom_call" | custom-call | flops 1000 | bytes 1000 | tf_op jit(solution)/shard_map/mix/pallas_call | solution.py:125
  34.0 8.6 %collective-permute-done.5.refs_2_.refs_6_.refs_4_ = bf16[216,1792]{1,0:T(8,128)(2,1)S(1)} collective-permute-done((bf16[216,1792]{1,0:T(8,128)(2,1)S(1)}, bf16[216,1792]{1,0:T(8,128)(2,1)S(1)}, u32[]{:S(2)}, u32[]{:S(2)}) %collective-permute-start.5) | collective-permute-done | bytes 774176 | tf_op jit(solution)/shard_map/ppermute | solution.py:90
  42.6 0.2 collect_third.1
  42.8 2.3 %collective-permute-start.8 = (bf16[240,1792]{1,0:T(8,128)(2,1)S(1)}, bf16[240,1792]{1,0:T(8,128)(2,1)S(1)}, u32[]{:S(2)}, u32[]{:S(2)}) collective-permute-start(bf16[240,1792]{1,0:T(8,128)(2,1)S(1)} %get-tuple-element.102), channel_id=1, source_target_pairs={{0,24},{1,9},{2,26},{3,11},{4,28},{5,13},{6,30},{7,15},{8,0},{9,17... | collective-permute-start | bytes 2580488 | tf_op jit(solution)/shard_map/ppermute | solution.py:90
  45.1 0.8 collective-permute-start.6
  45.9 0.9 collective-permute-start.7
  46.8 0.0 collective-permute-start.12
  46.8 14.0 %collective-permute-done.7.refs_0_.refs_6_.refs_1_ = bf16[208,1792]{1,0:T(8,128)(2,1)S(1)} collective-permute-done((bf16[208,1792]{1,0:T(8,128)(2,1)S(1)}, bf16[208,1792]{1,0:T(8,128)(2,1)S(1)}, u32[]{:S(2)}, u32[]{:S(2)}) %collective-permute-start.7) | collective-permute-done | bytes 745504 | tf_op jit(solution)/shard_map/ppermute | solution.py:90
  60.8 3.1 %collective-permute-done.8.refs_1_.refs_7_ = bf16[240,1792]{1,0:T(8,128)(2,1)S(1)} collective-permute-done((bf16[240,1792]{1,0:T(8,128)(2,1)S(1)}, bf16[240,1792]{1,0:T(8,128)(2,1)S(1)}, u32[]{:S(2)}, u32[]{:S(2)}) %collective-permute-start.8) | collective-permute-done | bytes 860192 | tf_op jit(solution)/shard_map/ppermute | solution.py:90
  64.0 0.1 collect_fourth.1
  64.0 1.4 %collective-permute-start.10 = (bf16[144,1792]{1,0:T(8,128)(2,1)S(1)}, bf16[144,1792]{1,0:T(8,128)(2,1)S(1)}, u32[]{:S(2)}, u32[]{:S(2)}) collective-permute-start(bf16[144,1792]{1,0:T(8,128)(2,1)S(1)} %get-tuple-element.109), channel_id=1, source_target_pairs={{0,4},{1,5},{2,6},{3,7},{4,0},{5,1},{6,2},{7,3},{8,12},{9,13},{10,... | collective-permute-start | bytes 1548296 | tf_op jit(solution)/shard_map/ppermute | solution.py:90
  65.4 1.2 %collective-permute-start.9 = (bf16[144,1792]{1,0:T(8,128)(2,1)S(1)}, bf16[144,1792]{1,0:T(8,128)(2,1)S(1)}, u32[]{:S(2)}, u32[]{:S(2)}) collective-permute-start(bf16[144,1792]{1,0:T(8,128)(2,1)S(1)} %get-tuple-element.109), channel_id=1, source_target_pairs={{0,2},{1,3},{2,0},{3,1},{4,6},{5,7},{6,4},{7,5},{8,10},{9,11},{10,... | collective-permute-start | bytes 1548296 | tf_op jit(solution)/shard_map/ppermute | solution.py:90
  66.6 1.1 %collective-permute-start.11 = (bf16[128,1792]{1,0:T(8,128)(2,1)S(1)}, bf16[128,1792]{1,0:T(8,128)(2,1)S(1)}, u32[]{:S(2)}, u32[]{:S(2)}) collective-permute-start(bf16[128,1792]{1,0:T(8,128)(2,1)S(1)} %get-tuple-element.110), channel_id=1, source_target_pairs={{0,24},{1,9},{2,26},{3,11},{4,28},{5,13},{6,30},{7,15},{8,0},{9,17... | collective-permute-start | bytes 1376264 | tf_op jit(solution)/shard_map/ppermute | solution.py:90
  67.7 3.2 %accumulate_second.1 = (f32[256,1792]{1,0:T(8,128)S(1)}, f32[256,1792]{1,0:T(8,128)S(1)}) custom-call(bf16[168,1792]{1,0:T(8,128)(2,1)S(1)} %copy-done, bf16[168,1792]{1,0:T(8,128)(2,1)S(1)} %collective-permute-done.refs_1_, bf16[168,1792]{1,0:T(8,128)(2,1)S(1)} %collective-permute-done.1.refs_2_, bf16[144,1792]{1,0:T(8,128)(2,1)S(1)} %collective-permute-done.2.refs_3_, ...), custom_call_target="tpu_custom_call" | custom-call | flops 1000 | bytes 1000 | tf_op jit(solution)/shard_map/accumulate_second/pallas_call | solution.py:125
  70.9 3.9 %accumulate_third.1 = (f32[256,1792]{1,0:T(8,128)S(1)}, f32[256,1792]{1,0:T(8,128)S(1)}) custom-call(bf16[168,1792]{1,0:T(8,128)(2,1)S(1)} %copy-done, bf16[168,1792]{1,0:T(8,128)(2,1)S(1)} %collective-permute-done.refs_1_, bf16[168,1792]{1,0:T(8,128)(2,1)S(1)} %collective-permute-done.1.refs_2_, ...), custom_call_target="tpu_custom_call", output_to_operand_aliasing={{0}: (10, {}), {1}: (11, {})} | custom-call | flops 1000 | bytes 1000 | tf_op jit(solution)/shard_map/accumulate_third/pallas_call | solution.py:125
  74.8 4.1 %collective-permute-done.11.refs_4_.refs_2_ = bf16[128,1792]{1,0:T(8,128)(2,1)S(1)} collective-permute-done((bf16[128,1792]{1,0:T(8,128)(2,1)S(1)}, bf16[128,1792]{1,0:T(8,128)(2,1)S(1)}, u32[]{:S(2)}, u32[]{:S(2)}) %collective-permute-start.11) | collective-permute-done | bytes 458784 | tf_op jit(solution)/shard_map/ppermute | solution.py:90
  78.9 0.1 collect_fifth.1
  79.0 0.6 collective-permute-start.13
  79.6 0.6 collective-permute-start.14
  80.2 2.0 %accumulate_fourth.1 = (f32[256,1792]{1,0:T(8,128)S(1)}, f32[256,1792]{1,0:T(8,128)S(1)}) custom-call(bf16[144,1792]{1,0:T(8,128)(2,1)S(1)} %collective-permute-done.9.refs_2_.refs_0_, bf16[144,1792]{1,0:T(8,128)(2,1)S(1)} %collective-permute-done.10.refs_3_.refs_1_, ...), custom_call_target="tpu_custom_call", output_to_operand_aliasing={{0}: (5, {}), {1}: (6, {})} | custom-call | flops 1000 | bytes 1000 | tf_op jit(solution)/shard_map/accumulate_fourth/pallas_call | solution.py:125
  82.2 8.4 %collective-permute-done.14.refs_1_ = bf16[136,1792]{1,0:T(8,128)(2,1)S(1)} collective-permute-done((bf16[136,1792]{1,0:T(8,128)(2,1)S(1)}, bf16[136,1792]{1,0:T(8,128)(2,1)S(1)}, u32[]{:S(2)}, u32[]{:S(2)}) %collective-permute-start.14) | collective-permute-done | bytes 487456 | tf_op jit(solution)/shard_map/ppermute | solution.py:90
  90.7 0.5 collective-permute-done.13.refs_0_
  91.2 1.0 %finish_other.1 = bf16[256,1792]{1,0:T(8,128)(2,1)S(1)} custom-call(bf16[144,1792]{1,0:T(8,128)(2,1)S(1)} %collective-permute-done.13.refs_0_, bf16[136,1792]{1,0:T(8,128)(2,1)S(1)} %collective-permute-done.14.refs_1_, bf16[128,1792]{1,0:T(8,128)(2,1)S(1)} %collective-permute-done.11.refs_4_.refs_2_, ...), custom_call_target="tpu_custom_call" | custom-call | flops 1000 | bytes 1000 | tf_op jit(solution)/shard_map/finish_other/pallas_call | solution.py:125
  92.2 0.1 collective-permute-start.15
  92.3 1.4 %finish_own.1.kept_ref = f32[256,1792]{1,0:T(8,128)S(1)} custom-call(bf16[144,1792]{1,0:T(8,128)(2,1)S(1)} %collective-permute-done.13.refs_0_, bf16[136,1792]{1,0:T(8,128)(2,1)S(1)} %collective-permute-done.14.refs_1_, bf16[128,1792]{1,0:T(8,128)(2,1)S(1)} %collective-permute-done.11.refs_4_.refs_2_, ...), custom_call_target="tpu_custom_call", output_to_operand_aliasing={{}: (4, {})} | custom-call | flops 1000 | bytes 1000 | tf_op jit(solution)/shard_map/finish_own/pallas_call | solution.py:125
  93.7 1.1 %collective-permute-done.15.given_ref = bf16[256,1792]{1,0:T(8,128)(2,1)S(1)} collective-permute-done((bf16[256,1792]{1,0:T(8,128)(2,1)S(1)}, bf16[256,1792]{1,0:T(8,128)(2,1)S(1)}, u32[]{:S(2)}, u32[]{:S(2)}) %collective-permute-start.15) | collective-permute-done | bytes 917536 | tf_op jit(solution)/shard_map/ppermute | solution.py:90
  94.8 1.2 %final.1 = bf16[256,1792]{1,0:T(8,128)(2,1)} custom-call(s32[1]{0:T(128)S(6)} %copy.27.count_ref, f32[256,1792]{1,0:T(8,128)S(1)} %finish_own.1.kept_ref, bf16[256,1792]{1,0:T(8,128)(2,1)S(1)} %collective-permute-done.15.given_ref), custom_call_target="tpu_custom_call" | custom-call | flops 1000 | bytes 1000 | tf_op jit(solution)/shard_map/final/pallas_call | solution.py:125
  (21 shorter events, 0.1 us)
Async XLA Ops:
  2.8 19.4 %collective-permute-start = (bf16[168,1792]{1,0:T(8,128)(2,1)}, bf16[168,1792]{1,0:T(8,128)(2,1)S(1)}, u32[]{:S(2)}, u32[]{:S(2)}) collective-permute-start(bf16[168,1792]{1,0:T(8,128)(2,1)} %get-tuple-element.71.refs_0_), channel_id=1, source_target_pairs={{0,2},{1,3},{2,0},{3,1},{4,6},{5,7},{6,4},{7,5},{8,10},{9,11},{10,... | collective-permute-start | bytes 1806344 | tf_op jit(solution)/shard_map/ppermute | solution.py:90
  5.8 16.4 %collective-permute-start.1 = (bf16[168,1792]{1,0:T(8,128)(2,1)}, bf16[168,1792]{1,0:T(8,128)(2,1)S(1)}, u32[]{:S(2)}, u32[]{:S(2)}) collective-permute-start(bf16[168,1792]{1,0:T(8,128)(2,1)} %get-tuple-element.71.refs_0_), channel_id=1, source_target_pairs={{0,4},{1,5},{2,6},{3,7},{4,0},{5,1},{6,2},{7,3},{8,12},{9,13},{10,... | collective-permute-start | bytes 1806344 | tf_op jit(solution)/shard_map/ppermute | solution.py:90
  7.4 14.8 %collective-permute-start.2 = (bf16[144,1792]{1,0:T(8,128)(2,1)}, bf16[144,1792]{1,0:T(8,128)(2,1)S(1)}, u32[]{:S(2)}, u32[]{:S(2)}) collective-permute-start(bf16[144,1792]{1,0:T(8,128)(2,1)} %get-tuple-element.72), channel_id=1, source_target_pairs={{0,24},{1,9},{2,26},{3,11},{4,28},{5,13},{6,30},{7,15},{8,0},{9,17... | collective-permute-start | bytes 1548296 | tf_op jit(solution)/shard_map/ppermute | solution.py:90
  11.7 1.2 %copy-start.1 = (bf16[1,256,1792]{2,1,0:T(8,128)(2,1)S(1)}, bf16[1,256,1792]{2,1,0:T(8,128)(2,1)}, u32[]{:S(2)}) copy-start(bf16[1,256,1792]{2,1,0:T(8,128)(2,1)} %param.13) | copy-start | bytes 2752516
  12.9 1.9 %copy-start.3 = (bf16[1792,896]{1,0:T(8,128)(2,1)S(1)}, bf16[1792,896]{1,0:T(8,128)(2,1)}, u32[]{:S(2)}) copy-start(bf16[1792,896]{1,0:T(8,128)(2,1)} %value_ref.1) | copy-start | bytes 9633796
  14.8 1.0 %copy-start.5 = (bf16[1792,128]{1,0:T(8,128)(2,1)S(1)}, bf16[1792,128]{1,0:T(8,128)(2,1)}, u32[]{:S(2)}) copy-start(bf16[1792,128]{1,0:T(8,128)(2,1)} %query_ref.1) | copy-start | bytes 1376260
  15.8 1.0 %copy-start.6 = (bf16[1792,128]{1,0:T(8,128)(2,1)S(1)}, bf16[1792,128]{1,0:T(8,128)(2,1)}, u32[]{:S(2)}) copy-start(bf16[1792,128]{1,0:T(8,128)(2,1)} %key_ref.1) | copy-start | bytes 1376260
  16.8 0.7 copy-start.7
  17.6 4.7 %copy-start = (bf16[168,1792]{1,0:T(8,128)(2,1)S(1)}, bf16[168,1792]{1,0:T(8,128)(2,1)}, u32[]{:S(2)}) copy-start(bf16[168,1792]{1,0:T(8,128)(2,1)} %get-tuple-element.71.refs_0_) | copy-start | bytes 1806340
  17.6 13.8 %copy-start.4 = (bf16[896,1792]{1,0:T(8,128)(2,1)S(1)}, bf16[896,1792]{1,0:T(8,128)(2,1)}, u32[]{:S(2)}) copy-start(bf16[896,1792]{1,0:T(8,128)(2,1)} %out_ref.1) | copy-start | bytes 9633796
  21.3 6.4 %copy-start.9 = (f32[1792]{0:T(1024)S(1)}, f32[1792]{0:T(1024)}, u32[]{:S(2)}) copy-start(f32[1792]{0:T(1024)} %param.22) | copy-start | bytes 21508
  21.3 6.4 %copy-start.8 = (f32[1,256,8]{1,2,0:T(8,128)S(1)}, f32[1,256,8]{1,2,0:T(8,128)}, u32[]{:S(2)}) copy-start(f32[1,256,8]{1,2,0:T(8,128)} %param.15) | copy-start | bytes 24580
  21.3 10.1 %copy-start.2 = (bf16[1,256,1792]{2,1,0:T(8,128)(2,1)S(1)}, bf16[1,256,1792]{2,1,0:T(8,128)(2,1)}, u32[]{:S(2)}) copy-start(bf16[1,256,1792]{2,1,0:T(8,128)(2,1)} %param.13) | copy-start | bytes 2752516
  22.4 20.2 %collective-permute-start.4 = (bf16[232,1792]{1,0:T(8,128)(2,1)S(1)}, bf16[232,1792]{1,0:T(8,128)(2,1)S(1)}, u32[]{:S(2)}, u32[]{:S(2)}) collective-permute-start(bf16[232,1792]{1,0:T(8,128)(2,1)S(1)} %get-tuple-element.83), channel_id=1, source_target_pairs={{0,4},{1,5},{2,6},{3,7},{4,0},{5,1},{6,2},{7,3},{8,12},{9,13},{10,... | collective-permute-start | bytes 2494472 | tf_op jit(solution)/shard_map/ppermute | solution.py:90
  23.0 19.6 %collective-permute-start.3 = (bf16[224,1792]{1,0:T(8,128)(2,1)S(1)}, bf16[224,1792]{1,0:T(8,128)(2,1)S(1)}, u32[]{:S(2)}, u32[]{:S(2)}) collective-permute-start(bf16[224,1792]{1,0:T(8,128)(2,1)S(1)} %get-tuple-element.82), channel_id=1, source_target_pairs={{0,2},{1,3},{2,0},{3,1},{4,6},{5,7},{6,4},{7,5},{8,10},{9,11},{10,... | collective-permute-start | bytes 2408456 | tf_op jit(solution)/shard_map/ppermute | solution.py:90
  23.4 19.2 %collective-permute-start.5 = (bf16[216,1792]{1,0:T(8,128)(2,1)S(1)}, bf16[216,1792]{1,0:T(8,128)(2,1)S(1)}, u32[]{:S(2)}, u32[]{:S(2)}) collective-permute-start(bf16[216,1792]{1,0:T(8,128)(2,1)S(1)} %get-tuple-element.84), channel_id=1, source_target_pairs={{0,24},{1,9},{2,26},{3,11},{4,28},{5,13},{6,30},{7,15},{8,0},{9,17... | collective-permute-start | bytes 2322440 | tf_op jit(solution)/shard_map/ppermute | solution.py:90
  42.8 21.2 %collective-permute-start.8 = (bf16[240,1792]{1,0:T(8,128)(2,1)S(1)}, bf16[240,1792]{1,0:T(8,128)(2,1)S(1)}, u32[]{:S(2)}, u32[]{:S(2)}) collective-permute-start(bf16[240,1792]{1,0:T(8,128)(2,1)S(1)} %get-tuple-element.102), channel_id=1, source_target_pairs={{0,24},{1,9},{2,26},{3,11},{4,28},{5,13},{6,30},{7,15},{8,0},{9,17... | collective-permute-start | bytes 2580488 | tf_op jit(solution)/shard_map/ppermute | solution.py:90
  45.1 15.7 %collective-permute-start.6 = (bf16[224,1792]{1,0:T(8,128)(2,1)S(1)}, bf16[224,1792]{1,0:T(8,128)(2,1)S(1)}, u32[]{:S(2)}, u32[]{:S(2)}) collective-permute-start(bf16[224,1792]{1,0:T(8,128)(2,1)S(1)} %get-tuple-element.100), channel_id=1, source_target_pairs={{0,2},{1,3},{2,0},{3,1},{4,6},{5,7},{6,4},{7,5},{8,10},{9,11},{10,... | collective-permute-start | bytes 2408456 | tf_op jit(solution)/shard_map/ppermute | solution.py:90
  45.9 14.9 %collective-permute-start.7 = (bf16[208,1792]{1,0:T(8,128)(2,1)S(1)}, bf16[208,1792]{1,0:T(8,128)(2,1)S(1)}, u32[]{:S(2)}, u32[]{:S(2)}) collective-permute-start(bf16[208,1792]{1,0:T(8,128)(2,1)S(1)} %get-tuple-element.101), channel_id=1, source_target_pairs={{0,4},{1,5},{2,6},{3,7},{4,0},{5,1},{6,2},{7,3},{8,12},{9,13},{10,... | collective-permute-start | bytes 2236424 | tf_op jit(solution)/shard_map/ppermute | solution.py:90
  46.8 20.9 %collective-permute-start.12 = (bf16[256,1792]{1,0:T(8,128)(2,1)S(1)}, bf16[256,1792]{1,0:T(8,128)(2,1)S(1)}, u32[]{:S(2)}, u32[]{:S(2)}) collective-permute-start(bf16[256,1792]{1,0:T(8,128)(2,1)S(1)} %get-tuple-element.114.refs_7_.refs_8_.refs_3_), channel_id=1, source_target_pairs={{0,1},{1,0},{2,3},{3,2},{4,5},{5,4},{6,7},{7,6},{8,9},{9,8},{10,11... | collective-permute-start | bytes 2752520 | tf_op jit(solution)/shard_map/ppermute | solution.py:90
  64.0 14.9 %collective-permute-start.10 = (bf16[144,1792]{1,0:T(8,128)(2,1)S(1)}, bf16[144,1792]{1,0:T(8,128)(2,1)S(1)}, u32[]{:S(2)}, u32[]{:S(2)}) collective-permute-start(bf16[144,1792]{1,0:T(8,128)(2,1)S(1)} %get-tuple-element.109), channel_id=1, source_target_pairs={{0,4},{1,5},{2,6},{3,7},{4,0},{5,1},{6,2},{7,3},{8,12},{9,13},{10,... | collective-permute-start | bytes 1548296 | tf_op jit(solution)/shard_map/ppermute | solution.py:90
  65.4 13.5 %collective-permute-start.9 = (bf16[144,1792]{1,0:T(8,128)(2,1)S(1)}, bf16[144,1792]{1,0:T(8,128)(2,1)S(1)}, u32[]{:S(2)}, u32[]{:S(2)}) collective-permute-start(bf16[144,1792]{1,0:T(8,128)(2,1)S(1)} %get-tuple-element.109), channel_id=1, source_target_pairs={{0,2},{1,3},{2,0},{3,1},{4,6},{5,7},{6,4},{7,5},{8,10},{9,11},{10,... | collective-permute-start | bytes 1548296 | tf_op jit(solution)/shard_map/ppermute | solution.py:90
  66.6 12.3 %collective-permute-start.11 = (bf16[128,1792]{1,0:T(8,128)(2,1)S(1)}, bf16[128,1792]{1,0:T(8,128)(2,1)S(1)}, u32[]{:S(2)}, u32[]{:S(2)}) collective-permute-start(bf16[128,1792]{1,0:T(8,128)(2,1)S(1)} %get-tuple-element.110), channel_id=1, source_target_pairs={{0,24},{1,9},{2,26},{3,11},{4,28},{5,13},{6,30},{7,15},{8,0},{9,17... | collective-permute-start | bytes 1376264 | tf_op jit(solution)/shard_map/ppermute | solution.py:90
  79.0 12.2 %collective-permute-start.13 = (bf16[144,1792]{1,0:T(8,128)(2,1)S(1)}, bf16[144,1792]{1,0:T(8,128)(2,1)S(1)}, u32[]{:S(2)}, u32[]{:S(2)}) collective-permute-start(bf16[144,1792]{1,0:T(8,128)(2,1)S(1)} %get-tuple-element.122), channel_id=1, source_target_pairs={{0,2},{1,3},{2,0},{3,1},{4,6},{5,7},{6,4},{7,5},{8,10},{9,11},{10,... | collective-permute-start | bytes 1548296 | tf_op jit(solution)/shard_map/ppermute | solution.py:90
  79.6 11.0 %collective-permute-start.14 = (bf16[136,1792]{1,0:T(8,128)(2,1)S(1)}, bf16[136,1792]{1,0:T(8,128)(2,1)S(1)}, u32[]{:S(2)}, u32[]{:S(2)}) collective-permute-start(bf16[136,1792]{1,0:T(8,128)(2,1)S(1)} %get-tuple-element.123), channel_id=1, source_target_pairs={{0,4},{1,5},{2,6},{3,7},{4,0},{5,1},{6,2},{7,3},{8,12},{9,13},{10,... | collective-permute-start | bytes 1462280 | tf_op jit(solution)/shard_map/ppermute | solution.py:90
  92.2 2.5 %collective-permute-start.15 = (bf16[256,1792]{1,0:T(8,128)(2,1)S(1)}, bf16[256,1792]{1,0:T(8,128)(2,1)S(1)}, u32[]{:S(2)}, u32[]{:S(2)}) collective-permute-start(bf16[256,1792]{1,0:T(8,128)(2,1)S(1)} %finish_other.1), channel_id=1, source_target_pairs={{0,1},{1,0},{2,3},{3,2},{4,5},{5,4},{6,7},{7,6},{8,9},{9,8},{10,11... | collective-permute-start | bytes 2752520 | tf_op jit(solution)/shard_map/ppermute | solution.py:90

commit v10 on v8

--- a/solution.py
+++ b/solution.py
@@ -620,12 +620,13 @@
     sends = collect(
         (near2, far2, near3, far3, deep3),
         (
-            ((1, 0, main), (1, two + held, wide), (3, 0, main), (3, two, two + held)),
-            ((0, main, two), (2, main, two), (2, two + held, wide), (4, narrow, 2 * narrow)),
+            ((1, 0, main), (1, two + held, wide), (3, 0, main)),
+            ((0, main, two), (2, main, two), (2, two + held, wide)),
+            ((4, 3 * narrow, 4 * narrow + held),),
         ),
         "collect_fifth",
     )
-    near4, far4 = slot(*zip((flip_near, flip_far), sends))
+    near4, far4, deep4 = slot(*zip((flip_near, flip_far, next_plane), sends))
     acc = accumulate(
         rows,
         (near3, far3, deep3),
@@ -634,14 +635,14 @@
         jnp.float32,
         "accumulate_fourth",
     )
-    weights = (near4, far4, deep3)
+    weights = (near4, far4, deep3, deep4)
     line, then = 4 * narrow, two - held
     last = [
         ((0, 0, held), (1, 0, held), (2, line, line + held)),
         ((0, held, main), (1, held, main), (0, main, then)),
-        ((0, then, then + held), (1, main, main + held), (0, then + main, then + main + held)),
+        ((0, then, then + held), (1, main, main + held), (3, narrow, narrow + held)),
         ((0, then + held, then + main), (1, main + held, two), (1, two, two + main - held)),
-        runs(1, two + main - held, edge),
+        runs(3, 0, edge),
     ]
     (given,) = accumulate(rows[1:], weights, last, acc[1:], jnp.bfloat16, "finish_other")
     (kept,) = accumulate(

time: 90.6 us -> 90.2 us (level)
    ppermute x16 -> x17, waiting for transfers between devices: 41 us -> 40.7 us  [permute(): return lax.ppermute(array, 'req', [(i, target(i)) for i in range(count)])]
    ppermute x16 -> x17, starting transfers between devices: 15.7 us -> 15.7 us  [permute(): return lax.ppermute(array, 'req', [(i, target(i)) for i in range(count)])]
  transfers between devices with their start and end apart: 16 -> 17, of which waited for: 8 -> 8; matrix products, arithmetic and copies ran while one was open for 1% -> 1% of each run, Pallas kernels for 23% -> 23%
where the time goes in v10:
time: 90.2 us; the launch traced here: 89.8 us
  waiting for transfers between devices  40.7 us (45%)
  Pallas kernels  25.3 us (28%)
  starting transfers between devices  15.7 us (17%)
  local copies, waits for them, and re-layouts  6.61 us (7%)
  between operations  1.46 us (2%)
    ppermute x17, waiting for transfers between devices, permute(): return lax.ppermute(array, 'req', [(i, target(i)) for i in range(count)])  40.7 us
    pallas_call x14, Pallas kernels, kernel_call(): pl.pallas_call(body, out_shape=out_shape, in_specs=specs or vmem(len(oper...  25.3 us
    ppermute x17, starting transfers between devices, permute(): return lax.ppermute(array, 'req', [(i, target(i)) for i in range(count)])  15.7 us
    unnamed x20, local copies, waits for them, and re-layouts  5.89 us
  transfers between devices with their start and end apart: 17, of which 8 were waited for; matrix products, arithmetic and copies ran while one was open for 1% of the time, Pallas kernels for 23%

profile of v10, /device:TPU:0, one launch (start us, length us, event | category | flops | bytes accessed | tf_op | source)
XLA Modules:
  0.0 89.8 jit_solution(11064940975631217375)
XLA Ops:
  0.6 2.2 %shard.1 = (bf16[168,1792]{1,0:T(8,128)(2,1)}, bf16[144,1792]{1,0:T(8,128)(2,1)}) custom-call(bf16[56,1792]{1,0:T(8,128)(2,1)} %bitcast.17, bf16[56,1792]{1,0:T(8,128)(2,1)} %bitcast.18, bf16[56,1792]{1,0:T(8,128)(2,1)} %bitcast.19), custom_call_target="tpu_custom_call" | custom-call | flops 1000 | bytes 1000 | tf_op jit(solution)/shard_map/shard/pallas_call | solution.py:125
  2.8 3.0 %collective-permute-start = (bf16[168,1792]{1,0:T(8,128)(2,1)}, bf16[168,1792]{1,0:T(8,128)(2,1)S(1)}, u32[]{:S(2)}, u32[]{:S(2)}) collective-permute-start(bf16[168,1792]{1,0:T(8,128)(2,1)} %get-tuple-element.73.refs_0_), channel_id=1, source_target_pairs={{0,2},{1,3},{2,0},{3,1},{4,6},{5,7},{6,4},{7,5},{8,10},{9,11},{10,... | collective-permute-start | bytes 1806344 | tf_op jit(solution)/shard_map/ppermute | solution.py:90
  5.8 1.5 %collective-permute-start.1 = (bf16[168,1792]{1,0:T(8,128)(2,1)}, bf16[168,1792]{1,0:T(8,128)(2,1)S(1)}, u32[]{:S(2)}, u32[]{:S(2)}) collective-permute-start(bf16[168,1792]{1,0:T(8,128)(2,1)} %get-tuple-element.73.refs_0_), channel_id=1, source_target_pairs={{0,4},{1,5},{2,6},{3,7},{4,0},{5,1},{6,2},{7,3},{8,12},{9,13},{10,... | collective-permute-start | bytes 1806344 | tf_op jit(solution)/shard_map/ppermute | solution.py:90
  7.4 1.6 %collective-permute-start.2 = (bf16[144,1792]{1,0:T(8,128)(2,1)}, bf16[144,1792]{1,0:T(8,128)(2,1)S(1)}, u32[]{:S(2)}, u32[]{:S(2)}) collective-permute-start(bf16[144,1792]{1,0:T(8,128)(2,1)} %get-tuple-element.74), channel_id=1, source_target_pairs={{0,8},{1,9},{2,10},{3,11},{4,12},{5,13},{6,14},{7,15},{8,16},{9,17... | collective-permute-start | bytes 1548296 | tf_op jit(solution)/shard_map/ppermute | solution.py:90
  8.9 0.7 broadcast_in_dim.16.gain_ref
  9.7 0.0 copy-start.1
  9.7 1.2 %copy-done.1 = bf16[1,256,1792]{2,1,0:T(8,128)(2,1)S(1)} copy-done((bf16[1,256,1792]{2,1,0:T(8,128)(2,1)S(1)}, bf16[1,256,1792]{2,1,0:T(8,128)(2,1)}, u32[]{:S(2)}) %copy-start.1) | copy-done | bytes 917528
  10.8 1.9 %copy-done.3 = bf16[1792,896]{1,0:T(8,128)(2,1)S(1)} copy-done((bf16[1792,896]{1,0:T(8,128)(2,1)S(1)}, bf16[1792,896]{1,0:T(8,128)(2,1)}, u32[]{:S(2)}) %copy-start.3) | copy-done | bytes 3211288
  12.7 1.0 %copy-done.5 = bf16[1792,128]{1,0:T(8,128)(2,1)S(1)} copy-done((bf16[1792,128]{1,0:T(8,128)(2,1)S(1)}, bf16[1792,128]{1,0:T(8,128)(2,1)}, u32[]{:S(2)}) %copy-start.5) | copy-done | bytes 458776
  13.8 1.0 %copy-done.6 = bf16[1792,128]{1,0:T(8,128)(2,1)S(1)} copy-done((bf16[1792,128]{1,0:T(8,128)(2,1)S(1)}, bf16[1792,128]{1,0:T(8,128)(2,1)}, u32[]{:S(2)}) %copy-start.6) | copy-done | bytes 458776
  14.8 0.7 copy-done.7
  15.5 3.7 %project.1 = (bf16[256,128]{1,0:T(8,128)(2,1)S(1)}, bf16[256,128]{1,0:T(8,128)(2,1)S(1)}, bf16[256,896]{1,0:T(8,128)(2,1)S(1)}) custom-call(bf16[256,1792]{1,0:T(8,128)(2,1)S(1)} %bitcast.13, bf16[16,1792]{1,0:T(8,128)(2,1)S(1)} %broadcast_in_dim.15.edge_ref, f32[1,1792]{1,0:T(1,128)S(1)} %broadcast_in_dim.16.gain_ref, f32[3,1792]{1,0:T(4,128)S(1)} %copy-done.7, ...), custom_call_target="tpu_custom_call" | custom-call | flops 1000 | bytes 1000 | tf_op jit(solution)/shard_map/project/pallas_call | solution.py:125
  19.3 0.0 copy-start.9
  19.3 0.0 copy-start.8
  19.3 0.0 copy-start.2
  19.3 3.1 %collective-permute-done.2.refs_3_ = bf16[144,1792]{1,0:T(8,128)(2,1)S(1)} collective-permute-done((bf16[144,1792]{1,0:T(8,128)(2,1)}, bf16[144,1792]{1,0:T(8,128)(2,1)S(1)}, u32[]{:S(2)}, u32[]{:S(2)}) %collective-permute-start.2) | collective-permute-done | bytes 516128 | tf_op jit(solution)/shard_map/ppermute | solution.py:90
  22.4 0.0 collective-permute-done.refs_1_
  22.4 0.2 collect_second.1
  22.5 0.6 collective-permute-start.4
  23.1 0.5 collective-permute-start.3
  23.6 1.3 %collective-permute-start.5 = (bf16[216,1792]{1,0:T(8,128)(2,1)S(1)}, bf16[216,1792]{1,0:T(8,128)(2,1)S(1)}, u32[]{:S(2)}, u32[]{:S(2)}) collective-permute-start(bf16[216,1792]{1,0:T(8,128)(2,1)S(1)} %get-tuple-element.86), channel_id=1, source_target_pairs={{0,8},{1,9},{2,10},{3,11},{4,12},{5,13},{6,14},{7,15},{8,16},{9,17... | collective-permute-start | bytes 2322440 | tf_op jit(solution)/shard_map/ppermute | solution.py:90
  25.7 3.7 %attend.1 = (f32[256,896]{1,0:T(8,128)S(1)}, f32[256,8]{1,0:T(8,128)S(1)}, f32[273,1,896]{2,1,0:T(1,128)}, f32[8,273]{1,0:T(8,128)}) custom-call(s32[1]{0:T(128)S(6)} %copy.27.count_ref, f32[8,256]{1,0:T(8,128)S(1)} %bitcast.15, bf16[256,128]{1,0:T(8,128)(2,1)S(1)} %get-tuple-element.90.queries_ref, bf16[256,128]{1,0:T(8,128)(2,1)S(1)} %get-tuple-element.91.keys_ref, ...), custom_call_target="tpu_custom_call" | custom-call | flops 1000 | bytes 1000 | tf_op jit(solution)/shard_map/attend/pallas_call | solution.py:125
  29.4 2.6 %mix.1 = (bf16[256,1792]{1,0:T(8,128)(2,1)S(1)}, bf16[256,1792]{1,0:T(8,128)(2,1)S(1)}) custom-call(f32[256,896]{1,0:T(8,128)S(1)} %get-tuple-element.93.numer_ref, f32[256,8]{1,0:T(8,128)S(1)} %get-tuple-element.94.denom_ref, bf16[256,1792]{1,0:T(8,128)(2,1)S(1)} %bitcast.14, bf16[896,1792]{1,0:T(8,128)(2,1)S(1)} %copy-done.4, ...), custom_call_target="tpu_custom_call" | custom-call | flops 1000 | bytes 1000 | tf_op jit(solution)/shard_map/mix/pallas_call | solution.py:125
  32.0 10.7 %collective-permute-done.5.refs_2_.refs_6_.refs_4_ = bf16[216,1792]{1,0:T(8,128)(2,1)S(1)} collective-permute-done((bf16[216,1792]{1,0:T(8,128)(2,1)S(1)}, bf16[216,1792]{1,0:T(8,128)(2,1)S(1)}, u32[]{:S(2)}, u32[]{:S(2)}) %collective-permute-start.5) | collective-permute-done | bytes 774176 | tf_op jit(solution)/shard_map/ppermute | solution.py:90
  42.7 0.2 collect_third.1
  42.9 0.1 collective-permute-start.8
  43.0 1.4 %collective-permute-start.6 = (bf16[224,1792]{1,0:T(8,128)(2,1)S(1)}, bf16[224,1792]{1,0:T(8,128)(2,1)S(1)}, u32[]{:S(2)}, u32[]{:S(2)}) collective-permute-start(bf16[224,1792]{1,0:T(8,128)(2,1)S(1)} %get-tuple-element.102), channel_id=1, source_target_pairs={{0,2},{1,3},{2,0},{3,1},{4,6},{5,7},{6,4},{7,5},{8,10},{9,11},{10,... | collective-permute-start | bytes 2408456 | tf_op jit(solution)/shard_map/ppermute | solution.py:90
  44.3 1.5 %collective-permute-start.7 = (bf16[208,1792]{1,0:T(8,128)(2,1)S(1)}, bf16[208,1792]{1,0:T(8,128)(2,1)S(1)}, u32[]{:S(2)}, u32[]{:S(2)}) collective-permute-start(bf16[208,1792]{1,0:T(8,128)(2,1)S(1)} %get-tuple-element.103), channel_id=1, source_target_pairs={{0,4},{1,5},{2,6},{3,7},{4,0},{5,1},{6,2},{7,3},{8,12},{9,13},{10,... | collective-permute-start | bytes 2236424 | tf_op jit(solution)/shard_map/ppermute | solution.py:90
  45.8 13.8 %collective-permute-done.7.refs_0_.refs_6_.refs_1_ = bf16[208,1792]{1,0:T(8,128)(2,1)S(1)} collective-permute-done((bf16[208,1792]{1,0:T(8,128)(2,1)S(1)}, bf16[208,1792]{1,0:T(8,128)(2,1)S(1)}, u32[]{:S(2)}, u32[]{:S(2)}) %collective-permute-start.7) | collective-permute-done | bytes 745504 | tf_op jit(solution)/shard_map/ppermute | solution.py:90
  59.6 0.4 collective-permute-done.6.refs_5_.refs_0_
  60.0 2.9 %collective-permute-done.8.refs_1_.refs_7_ = bf16[240,1792]{1,0:T(8,128)(2,1)S(1)} collective-permute-done((bf16[240,1792]{1,0:T(8,128)(2,1)S(1)}, bf16[240,1792]{1,0:T(8,128)(2,1)S(1)}, u32[]{:S(2)}, u32[]{:S(2)}) %collective-permute-start.8) | collective-permute-done | bytes 860192 | tf_op jit(solution)/shard_map/ppermute | solution.py:90
  62.9 0.1 collect_fourth.1
  63.0 1.1 %collective-permute-start.10 = (bf16[144,1792]{1,0:T(8,128)(2,1)S(1)}, bf16[144,1792]{1,0:T(8,128)(2,1)S(1)}, u32[]{:S(2)}, u32[]{:S(2)}) collective-permute-start(bf16[144,1792]{1,0:T(8,128)(2,1)S(1)} %get-tuple-element.111), channel_id=1, source_target_pairs={{0,4},{1,5},{2,6},{3,7},{4,0},{5,1},{6,2},{7,3},{8,12},{9,13},{10,... | collective-permute-start | bytes 1548296 | tf_op jit(solution)/shard_map/ppermute | solution.py:90
  64.1 1.5 %collective-permute-start.9 = (bf16[144,1792]{1,0:T(8,128)(2,1)S(1)}, bf16[144,1792]{1,0:T(8,128)(2,1)S(1)}, u32[]{:S(2)}, u32[]{:S(2)}) collective-permute-start(bf16[144,1792]{1,0:T(8,128)(2,1)S(1)} %get-tuple-element.111), channel_id=1, source_target_pairs={{0,2},{1,3},{2,0},{3,1},{4,6},{5,7},{6,4},{7,5},{8,10},{9,11},{10,... | collective-permute-start | bytes 1548296 | tf_op jit(solution)/shard_map/ppermute | solution.py:90
  65.6 0.0 collective-permute-start.11
  65.6 3.2 %accumulate_second.1 = (f32[256,1792]{1,0:T(8,128)S(1)}, f32[256,1792]{1,0:T(8,128)S(1)}) custom-call(bf16[168,1792]{1,0:T(8,128)(2,1)S(1)} %copy-done, bf16[168,1792]{1,0:T(8,128)(2,1)S(1)} %collective-permute-done.refs_1_, bf16[168,1792]{1,0:T(8,128)(2,1)S(1)} %collective-permute-done.1.refs_2_, bf16[144,1792]{1,0:T(8,128)(2,1)S(1)} %collective-permute-done.2.refs_3_, ...), custom_call_target="tpu_custom_call" | custom-call | flops 1000 | bytes 1000 | tf_op jit(solution)/shard_map/accumulate_second/pallas_call | solution.py:125
  68.8 3.9 %accumulate_third.1 = (f32[256,1792]{1,0:T(8,128)S(1)}, f32[256,1792]{1,0:T(8,128)S(1)}) custom-call(bf16[168,1792]{1,0:T(8,128)(2,1)S(1)} %copy-done, bf16[168,1792]{1,0:T(8,128)(2,1)S(1)} %collective-permute-done.refs_1_, bf16[168,1792]{1,0:T(8,128)(2,1)S(1)} %collective-permute-done.1.refs_2_, ...), custom_call_target="tpu_custom_call", output_to_operand_aliasing={{0}: (10, {}), {1}: (11, {})} | custom-call | flops 1000 | bytes 1000 | tf_op jit(solution)/shard_map/accumulate_third/pallas_call | solution.py:125
  72.7 3.1 %collective-permute-done.11.refs_4_.refs_2_ = bf16[128,1792]{1,0:T(8,128)(2,1)S(1)} collective-permute-done((bf16[128,1792]{1,0:T(8,128)(2,1)S(1)}, bf16[128,1792]{1,0:T(8,128)(2,1)S(1)}, u32[]{:S(2)}, u32[]{:S(2)}) %collective-permute-start.11) | collective-permute-done | bytes 458784 | tf_op jit(solution)/shard_map/ppermute | solution.py:90
  75.9 0.1 collect_fifth.1
  76.0 0.6 collective-permute-start.13
  76.6 0.9 %collective-permute-start.14 = (bf16[112,1792]{1,0:T(8,128)(2,1)S(1)}, bf16[112,1792]{1,0:T(8,128)(2,1)S(1)}, u32[]{:S(2)}, u32[]{:S(2)}) collective-permute-start(bf16[112,1792]{1,0:T(8,128)(2,1)S(1)} %get-tuple-element.125), channel_id=1, source_target_pairs={{0,4},{1,5},{2,6},{3,7},{4,0},{5,1},{6,2},{7,3},{8,12},{9,13},{10,... | collective-permute-start | bytes 1204232 | tf_op jit(solution)/shard_map/ppermute | solution.py:90
  77.5 2.0 %accumulate_fourth.1 = (f32[256,1792]{1,0:T(8,128)S(1)}, f32[256,1792]{1,0:T(8,128)S(1)}) custom-call(bf16[144,1792]{1,0:T(8,128)(2,1)S(1)} %collective-permute-done.9.refs_2_.refs_0_, bf16[144,1792]{1,0:T(8,128)(2,1)S(1)} %collective-permute-done.10.refs_3_.refs_1_, ...), custom_call_target="tpu_custom_call", output_to_operand_aliasing={{0}: (5, {}), {1}: (6, {})} | custom-call | flops 1000 | bytes 1000 | tf_op jit(solution)/shard_map/accumulate_fourth/pallas_call | solution.py:125
  79.5 5.5 %collective-permute-done.15.refs_3_ = bf16[56,1792]{1,0:T(8,128)(2,1)S(1)} collective-permute-done((bf16[56,1792]{1,0:T(8,128)(2,1)S(1)}, bf16[56,1792]{1,0:T(8,128)(2,1)S(1)}, u32[]{:S(2)}, u32[]{:S(2)}) %collective-permute-start.15) | collective-permute-done | bytes 200736 | tf_op jit(solution)/shard_map/ppermute | solution.py:90
  85.1 1.0 %finish_other.1 = bf16[256,1792]{1,0:T(8,128)(2,1)S(1)} custom-call(bf16[112,1792]{1,0:T(8,128)(2,1)S(1)} %collective-permute-done.13.refs_0_, bf16[112,1792]{1,0:T(8,128)(2,1)S(1)} %collective-permute-done.14.refs_1_, bf16[128,1792]{1,0:T(8,128)(2,1)S(1)} %collective-permute-done.11.refs_4_.refs_2_, bf16[56,1792]{1,0:T(8,128)(2,1)S(1)} %collective-permute-done.15.refs_3_, ...), custom_call_target="tpu_custom_call" | custom-call | flops 1000 | bytes 1000 | tf_op jit(solution)/shard_map/finish_other/pallas_call | solution.py:125
  86.1 0.1 collective-permute-start.16
  86.2 1.4 %finish_own.1.kept_ref = f32[256,1792]{1,0:T(8,128)S(1)} custom-call(bf16[112,1792]{1,0:T(8,128)(2,1)S(1)} %collective-permute-done.13.refs_0_, bf16[112,1792]{1,0:T(8,128)(2,1)S(1)} %collective-permute-done.14.refs_1_, bf16[128,1792]{1,0:T(8,128)(2,1)S(1)} %collective-permute-done.11.refs_4_.refs_2_, ...), custom_call_target="tpu_custom_call", output_to_operand_aliasing={{}: (5, {})} | custom-call | flops 1000 | bytes 1000 | tf_op jit(solution)/shard_map/finish_own/pallas_call | solution.py:125
  87.5 1.1 %collective-permute-done.16.given_ref = bf16[256,1792]{1,0:T(8,128)(2,1)S(1)} collective-permute-done((bf16[256,1792]{1,0:T(8,128)(2,1)S(1)}, bf16[256,1792]{1,0:T(8,128)(2,1)S(1)}, u32[]{:S(2)}, u32[]{:S(2)}) %collective-permute-start.16) | collective-permute-done | bytes 917536 | tf_op jit(solution)/shard_map/ppermute | solution.py:90
  88.6 1.2 %final.1 = bf16[256,1792]{1,0:T(8,128)(2,1)} custom-call(s32[1]{0:T(128)S(6)} %copy.27.count_ref, f32[256,1792]{1,0:T(8,128)S(1)} %finish_own.1.kept_ref, bf16[256,1792]{1,0:T(8,128)(2,1)S(1)} %collective-permute-done.16.given_ref), custom_call_target="tpu_custom_call" | custom-call | flops 1000 | bytes 1000 | tf_op jit(solution)/shard_map/final/pallas_call | solution.py:125
  (23 shorter events, 0.1 us)
Async XLA Ops:
  2.8 19.5 %collective-permute-start = (bf16[168,1792]{1,0:T(8,128)(2,1)}, bf16[168,1792]{1,0:T(8,128)(2,1)S(1)}, u32[]{:S(2)}, u32[]{:S(2)}) collective-permute-start(bf16[168,1792]{1,0:T(8,128)(2,1)} %get-tuple-element.73.refs_0_), channel_id=1, source_target_pairs={{0,2},{1,3},{2,0},{3,1},{4,6},{5,7},{6,4},{7,5},{8,10},{9,11},{10,... | collective-permute-start | bytes 1806344 | tf_op jit(solution)/shard_map/ppermute | solution.py:90
  5.8 16.5 %collective-permute-start.1 = (bf16[168,1792]{1,0:T(8,128)(2,1)}, bf16[168,1792]{1,0:T(8,128)(2,1)S(1)}, u32[]{:S(2)}, u32[]{:S(2)}) collective-permute-start(bf16[168,1792]{1,0:T(8,128)(2,1)} %get-tuple-element.73.refs_0_), channel_id=1, source_target_pairs={{0,4},{1,5},{2,6},{3,7},{4,0},{5,1},{6,2},{7,3},{8,12},{9,13},{10,... | collective-permute-start | bytes 1806344 | tf_op jit(solution)/shard_map/ppermute | solution.py:90
  7.4 15.0 %collective-permute-start.2 = (bf16[144,1792]{1,0:T(8,128)(2,1)}, bf16[144,1792]{1,0:T(8,128)(2,1)S(1)}, u32[]{:S(2)}, u32[]{:S(2)}) collective-permute-start(bf16[144,1792]{1,0:T(8,128)(2,1)} %get-tuple-element.74), channel_id=1, source_target_pairs={{0,8},{1,9},{2,10},{3,11},{4,12},{5,13},{6,14},{7,15},{8,16},{9,17... | collective-permute-start | bytes 1548296 | tf_op jit(solution)/shard_map/ppermute | solution.py:90
  9.7 1.2 %copy-start.1 = (bf16[1,256,1792]{2,1,0:T(8,128)(2,1)S(1)}, bf16[1,256,1792]{2,1,0:T(8,128)(2,1)}, u32[]{:S(2)}) copy-start(bf16[1,256,1792]{2,1,0:T(8,128)(2,1)} %param.13) | copy-start | bytes 2752516
  10.8 1.9 %copy-start.3 = (bf16[1792,896]{1,0:T(8,128)(2,1)S(1)}, bf16[1792,896]{1,0:T(8,128)(2,1)}, u32[]{:S(2)}) copy-start(bf16[1792,896]{1,0:T(8,128)(2,1)} %value_ref.1) | copy-start | bytes 9633796
  12.7 1.0 %copy-start.5 = (bf16[1792,128]{1,0:T(8,128)(2,1)S(1)}, bf16[1792,128]{1,0:T(8,128)(2,1)}, u32[]{:S(2)}) copy-start(bf16[1792,128]{1,0:T(8,128)(2,1)} %query_ref.1) | copy-start | bytes 1376260
  13.8 1.0 %copy-start.6 = (bf16[1792,128]{1,0:T(8,128)(2,1)S(1)}, bf16[1792,128]{1,0:T(8,128)(2,1)}, u32[]{:S(2)}) copy-start(bf16[1792,128]{1,0:T(8,128)(2,1)} %key_ref.1) | copy-start | bytes 1376260
  14.8 0.7 copy-start.7
  15.5 6.8 %copy-start = (bf16[168,1792]{1,0:T(8,128)(2,1)S(1)}, bf16[168,1792]{1,0:T(8,128)(2,1)}, u32[]{:S(2)}) copy-start(bf16[168,1792]{1,0:T(8,128)(2,1)} %get-tuple-element.73.refs_0_) | copy-start | bytes 1806340
  15.5 13.8 %copy-start.4 = (bf16[896,1792]{1,0:T(8,128)(2,1)S(1)}, bf16[896,1792]{1,0:T(8,128)(2,1)}, u32[]{:S(2)}) copy-start(bf16[896,1792]{1,0:T(8,128)(2,1)} %out_ref.1) | copy-start | bytes 9633796
  19.3 6.4 %copy-start.9 = (f32[1792]{0:T(1024)S(1)}, f32[1792]{0:T(1024)}, u32[]{:S(2)}) copy-start(f32[1792]{0:T(1024)} %param.22) | copy-start | bytes 21508
  19.3 6.4 %copy-start.8 = (f32[1,256,8]{1,2,0:T(8,128)S(1)}, f32[1,256,8]{1,2,0:T(8,128)}, u32[]{:S(2)}) copy-start(f32[1,256,8]{1,2,0:T(8,128)} %param.15) | copy-start | bytes 24580
  19.3 10.1 %copy-start.2 = (bf16[1,256,1792]{2,1,0:T(8,128)(2,1)S(1)}, bf16[1,256,1792]{2,1,0:T(8,128)(2,1)}, u32[]{:S(2)}) copy-start(bf16[1,256,1792]{2,1,0:T(8,128)(2,1)} %param.13) | copy-start | bytes 2752516
  22.5 20.2 %collective-permute-start.4 = (bf16[232,1792]{1,0:T(8,128)(2,1)S(1)}, bf16[232,1792]{1,0:T(8,128)(2,1)S(1)}, u32[]{:S(2)}, u32[]{:S(2)}) collective-permute-start(bf16[232,1792]{1,0:T(8,128)(2,1)S(1)} %get-tuple-element.85), channel_id=1, source_target_pairs={{0,4},{1,5},{2,6},{3,7},{4,0},{5,1},{6,2},{7,3},{8,12},{9,13},{10,... | collective-permute-start | bytes 2494472 | tf_op jit(solution)/shard_map/ppermute | solution.py:90
  23.1 19.6 %collective-permute-start.3 = (bf16[224,1792]{1,0:T(8,128)(2,1)S(1)}, bf16[224,1792]{1,0:T(8,128)(2,1)S(1)}, u32[]{:S(2)}, u32[]{:S(2)}) collective-permute-start(bf16[224,1792]{1,0:T(8,128)(2,1)S(1)} %get-tuple-element.84), channel_id=1, source_target_pairs={{0,2},{1,3},{2,0},{3,1},{4,6},{5,7},{6,4},{7,5},{8,10},{9,11},{10,... | collective-permute-start | bytes 2408456 | tf_op jit(solution)/shard_map/ppermute | solution.py:90
  23.6 19.1 %collective-permute-start.5 = (bf16[216,1792]{1,0:T(8,128)(2,1)S(1)}, bf16[216,1792]{1,0:T(8,128)(2,1)S(1)}, u32[]{:S(2)}, u32[]{:S(2)}) collective-permute-start(bf16[216,1792]{1,0:T(8,128)(2,1)S(1)} %get-tuple-element.86), channel_id=1, source_target_pairs={{0,8},{1,9},{2,10},{3,11},{4,12},{5,13},{6,14},{7,15},{8,16},{9,17... | collective-permute-start | bytes 2322440 | tf_op jit(solution)/shard_map/ppermute | solution.py:90
  42.9 20.0 %collective-permute-start.8 = (bf16[240,1792]{1,0:T(8,128)(2,1)S(1)}, bf16[240,1792]{1,0:T(8,128)(2,1)S(1)}, u32[]{:S(2)}, u32[]{:S(2)}) collective-permute-start(bf16[240,1792]{1,0:T(8,128)(2,1)S(1)} %get-tuple-element.104), channel_id=1, source_target_pairs={{0,8},{1,9},{2,10},{3,11},{4,12},{5,13},{6,14},{7,15},{8,16},{9,17... | collective-permute-start | bytes 2580488 | tf_op jit(solution)/shard_map/ppermute | solution.py:90
  43.0 17.0 %collective-permute-start.6 = (bf16[224,1792]{1,0:T(8,128)(2,1)S(1)}, bf16[224,1792]{1,0:T(8,128)(2,1)S(1)}, u32[]{:S(2)}, u32[]{:S(2)}) collective-permute-start(bf16[224,1792]{1,0:T(8,128)(2,1)S(1)} %get-tuple-element.102), channel_id=1, source_target_pairs={{0,2},{1,3},{2,0},{3,1},{4,6},{5,7},{6,4},{7,5},{8,10},{9,11},{10,... | collective-permute-start | bytes 2408456 | tf_op jit(solution)/shard_map/ppermute | solution.py:90
  44.3 15.3 %collective-permute-start.7 = (bf16[208,1792]{1,0:T(8,128)(2,1)S(1)}, bf16[208,1792]{1,0:T(8,128)(2,1)S(1)}, u32[]{:S(2)}, u32[]{:S(2)}) collective-permute-start(bf16[208,1792]{1,0:T(8,128)(2,1)S(1)} %get-tuple-element.103), channel_id=1, source_target_pairs={{0,4},{1,5},{2,6},{3,7},{4,0},{5,1},{6,2},{7,3},{8,12},{9,13},{10,... | collective-permute-start | bytes 2236424 | tf_op jit(solution)/shard_map/ppermute | solution.py:90
  45.8 19.8 %collective-permute-start.12 = (bf16[256,1792]{1,0:T(8,128)(2,1)S(1)}, bf16[256,1792]{1,0:T(8,128)(2,1)S(1)}, u32[]{:S(2)}, u32[]{:S(2)}) collective-permute-start(bf16[256,1792]{1,0:T(8,128)(2,1)S(1)} %get-tuple-element.116.refs_7_.refs_8_.refs_3_.refs_4_), channel_id=1, source_target_pairs={{0,1},{1,0},{2,3},{3,2},{4,5},{5,4},{6,7},{7,6},{8,9},{9,8},{10,11... | collective-permute-start | bytes 2752520 | tf_op jit(solution)/shard_map/ppermute | solution.py:90
  63.0 12.9 %collective-permute-start.10 = (bf16[144,1792]{1,0:T(8,128)(2,1)S(1)}, bf16[144,1792]{1,0:T(8,128)(2,1)S(1)}, u32[]{:S(2)}, u32[]{:S(2)}) collective-permute-start(bf16[144,1792]{1,0:T(8,128)(2,1)S(1)} %get-tuple-element.111), channel_id=1, source_target_pairs={{0,4},{1,5},{2,6},{3,7},{4,0},{5,1},{6,2},{7,3},{8,12},{9,13},{10,... | collective-permute-start | bytes 1548296 | tf_op jit(solution)/shard_map/ppermute | solution.py:90
  64.1 11.8 %collective-permute-start.9 = (bf16[144,1792]{1,0:T(8,128)(2,1)S(1)}, bf16[144,1792]{1,0:T(8,128)(2,1)S(1)}, u32[]{:S(2)}, u32[]{:S(2)}) collective-permute-start(bf16[144,1792]{1,0:T(8,128)(2,1)S(1)} %get-tuple-element.111), channel_id=1, source_target_pairs={{0,2},{1,3},{2,0},{3,1},{4,6},{5,7},{6,4},{7,5},{8,10},{9,11},{10,... | collective-permute-start | bytes 1548296 | tf_op jit(solution)/shard_map/ppermute | solution.py:90
  65.6 10.3 %collective-permute-start.11 = (bf16[128,1792]{1,0:T(8,128)(2,1)S(1)}, bf16[128,1792]{1,0:T(8,128)(2,1)S(1)}, u32[]{:S(2)}, u32[]{:S(2)}) collective-permute-start(bf16[128,1792]{1,0:T(8,128)(2,1)S(1)} %get-tuple-element.112), channel_id=1, source_target_pairs={{0,8},{1,9},{2,10},{3,11},{4,12},{5,13},{6,14},{7,15},{8,16},{9,17... | collective-permute-start | bytes 1376264 | tf_op jit(solution)/shard_map/ppermute | solution.py:90
  76.0 9.1 %collective-permute-start.13 = (bf16[112,1792]{1,0:T(8,128)(2,1)S(1)}, bf16[112,1792]{1,0:T(8,128)(2,1)S(1)}, u32[]{:S(2)}, u32[]{:S(2)}) collective-permute-start(bf16[112,1792]{1,0:T(8,128)(2,1)S(1)} %get-tuple-element.124), channel_id=1, source_target_pairs={{0,2},{1,3},{2,0},{3,1},{4,6},{5,7},{6,4},{7,5},{8,10},{9,11},{10,... | collective-permute-start | bytes 1204232 | tf_op jit(solution)/shard_map/ppermute | solution.py:90
  76.6 8.5 %collective-permute-start.14 = (bf16[112,1792]{1,0:T(8,128)(2,1)S(1)}, bf16[112,1792]{1,0:T(8,128)(2,1)S(1)}, u32[]{:S(2)}, u32[]{:S(2)}) collective-permute-start(bf16[112,1792]{1,0:T(8,128)(2,1)S(1)} %get-tuple-element.125), channel_id=1, source_target_pairs={{0,4},{1,5},{2,6},{3,7},{4,0},{5,1},{6,2},{7,3},{8,12},{9,13},{10,... | collective-permute-start | bytes 1204232 | tf_op jit(solution)/shard_map/ppermute | solution.py:90
  77.5 7.5 %collective-permute-start.15 = (bf16[56,1792]{1,0:T(8,128)(2,1)S(1)}, bf16[56,1792]{1,0:T(8,128)(2,1)S(1)}, u32[]{:S(2)}, u32[]{:S(2)}) collective-permute-start(bf16[56,1792]{1,0:T(8,128)(2,1)S(1)} %get-tuple-element.126), channel_id=1, source_target_pairs={{0,8},{1,9},{2,10},{3,11},{4,12},{5,13},{6,14},{7,15},{8,16},{9,17... | collective-permute-start | bytes 602120 | tf_op jit(solution)/shard_map/ppermute | solution.py:90
  86.1 2.5 %collective-permute-start.16 = (bf16[256,1792]{1,0:T(8,128)(2,1)S(1)}, bf16[256,1792]{1,0:T(8,128)(2,1)S(1)}, u32[]{:S(2)}, u32[]{:S(2)}) collective-permute-start(bf16[256,1792]{1,0:T(8,128)(2,1)S(1)} %finish_other.1), channel_id=1, source_target_pairs={{0,1},{1,0},{2,3},{3,2},{4,5},{5,4},{6,7},{7,6},{8,9},{9,8},{10,11... | collective-permute-start | bytes 2752520 | tf_op jit(solution)/shard_map/ppermute | solution.py:90

commit v11 on v10

--- a/solution.py
+++ b/solution.py
@@ -103,8 +103,7 @@
 
 
 def next_plane(array):
-    count = lax.axis_size("req")
-    return permute(array, lambda i: (i + 8) % count)
+    return permute(array, lambda i: i ^ (16 if i // 8 in (1, 2) else 8))
 
 
 def together(*arrays):

time: 90.2 us -> 88.1 us (0.977)
  waiting for transfers between devices: 40.7 us -> 32.8 us
  starting transfers between devices: 15.7 us -> 21.4 us
    ppermute x17, waiting for transfers between devices: 40.7 us -> 32.8 us  [permute(): return lax.ppermute(array, 'req', [(i, target(i)) for i in range(count)])]
    ppermute x17, starting transfers between devices: 15.7 us -> 21.4 us  [permute(): return lax.ppermute(array, 'req', [(i, target(i)) for i in range(count)])]
where the time goes in v11:
time: 88.1 us; the launch traced here: 87.6 us
  waiting for transfers between devices  32.8 us (37%)
  Pallas kernels  25.3 us (29%)
  starting transfers between devices  21.4 us (24%)
  local copies, waits for them, and re-layouts  6.61 us (8%)
  between operations  1.47 us (2%)
    ppermute x17, waiting for transfers between devices, permute(): return lax.ppermute(array, 'req', [(i, target(i)) for i in range(count)])  32.8 us
    pallas_call x14, Pallas kernels, kernel_call(): pl.pallas_call(body, out_shape=out_shape, in_specs=specs or vmem(len(oper...  25.3 us
    ppermute x17, starting transfers between devices, permute(): return lax.ppermute(array, 'req', [(i, target(i)) for i in range(count)])  21.4 us
    unnamed x20, local copies, waits for them, and re-layouts  5.89 us
  transfers between devices with their start and end apart: 17, of which 8 were waited for; matrix products, arithmetic and copies ran while one was open for 1% of the time, Pallas kernels for 23%

profile of v11, /device:TPU:0, one launch (start us, length us, event | category | flops | bytes accessed | tf_op | source)
XLA Modules:
  0.0 87.6 jit_solution(9287569558979809655)
XLA Ops:
  0.6 2.2 %shard.1 = (bf16[168,1792]{1,0:T(8,128)(2,1)}, bf16[144,1792]{1,0:T(8,128)(2,1)}) custom-call(bf16[56,1792]{1,0:T(8,128)(2,1)} %bitcast.17, bf16[56,1792]{1,0:T(8,128)(2,1)} %bitcast.18, bf16[56,1792]{1,0:T(8,128)(2,1)} %bitcast.19), custom_call_target="tpu_custom_call" | custom-call | flops 1000 | bytes 1000 | tf_op jit(solution)/shard_map/shard/pallas_call | solution.py:124
  2.8 3.0 %collective-permute-start = (bf16[168,1792]{1,0:T(8,128)(2,1)}, bf16[168,1792]{1,0:T(8,128)(2,1)S(1)}, u32[]{:S(2)}, u32[]{:S(2)}) collective-permute-start(bf16[168,1792]{1,0:T(8,128)(2,1)} %get-tuple-element.73.refs_0_), channel_id=1, source_target_pairs={{0,2},{1,3},{2,0},{3,1},{4,6},{5,7},{6,4},{7,5},{8,10},{9,11},{10,... | collective-permute-start | bytes 1806344 | tf_op jit(solution)/shard_map/ppermute | solution.py:90
  5.8 1.5 %collective-permute-start.1 = (bf16[168,1792]{1,0:T(8,128)(2,1)}, bf16[168,1792]{1,0:T(8,128)(2,1)S(1)}, u32[]{:S(2)}, u32[]{:S(2)}) collective-permute-start(bf16[168,1792]{1,0:T(8,128)(2,1)} %get-tuple-element.73.refs_0_), channel_id=1, source_target_pairs={{0,4},{1,5},{2,6},{3,7},{4,0},{5,1},{6,2},{7,3},{8,12},{9,13},{10,... | collective-permute-start | bytes 1806344 | tf_op jit(solution)/shard_map/ppermute | solution.py:90
  7.4 1.6 %collective-permute-start.2 = (bf16[144,1792]{1,0:T(8,128)(2,1)}, bf16[144,1792]{1,0:T(8,128)(2,1)S(1)}, u32[]{:S(2)}, u32[]{:S(2)}) collective-permute-start(bf16[144,1792]{1,0:T(8,128)(2,1)} %get-tuple-element.74), channel_id=1, source_target_pairs={{0,8},{1,9},{2,10},{3,11},{4,12},{5,13},{6,14},{7,15},{8,24},{9,25... | collective-permute-start | bytes 1548296 | tf_op jit(solution)/shard_map/ppermute | solution.py:90
  8.9 0.7 broadcast_in_dim.16.gain_ref
  9.7 0.0 copy-start.1
  9.7 1.2 %copy-done.1 = bf16[1,256,1792]{2,1,0:T(8,128)(2,1)S(1)} copy-done((bf16[1,256,1792]{2,1,0:T(8,128)(2,1)S(1)}, bf16[1,256,1792]{2,1,0:T(8,128)(2,1)}, u32[]{:S(2)}) %copy-start.1) | copy-done | bytes 917528
  10.8 1.9 %copy-done.3 = bf16[1792,896]{1,0:T(8,128)(2,1)S(1)} copy-done((bf16[1792,896]{1,0:T(8,128)(2,1)S(1)}, bf16[1792,896]{1,0:T(8,128)(2,1)}, u32[]{:S(2)}) %copy-start.3) | copy-done | bytes 3211288
  12.7 1.0 %copy-done.5 = bf16[1792,128]{1,0:T(8,128)(2,1)S(1)} copy-done((bf16[1792,128]{1,0:T(8,128)(2,1)S(1)}, bf16[1792,128]{1,0:T(8,128)(2,1)}, u32[]{:S(2)}) %copy-start.5) | copy-done | bytes 458776
  13.8 1.0 %copy-done.6 = bf16[1792,128]{1,0:T(8,128)(2,1)S(1)} copy-done((bf16[1792,128]{1,0:T(8,128)(2,1)S(1)}, bf16[1792,128]{1,0:T(8,128)(2,1)}, u32[]{:S(2)}) %copy-start.6) | copy-done | bytes 458776
  14.8 0.7 copy-done.7
  15.5 3.7 %project.1 = (bf16[256,128]{1,0:T(8,128)(2,1)S(1)}, bf16[256,128]{1,0:T(8,128)(2,1)S(1)}, bf16[256,896]{1,0:T(8,128)(2,1)S(1)}) custom-call(bf16[256,1792]{1,0:T(8,128)(2,1)S(1)} %bitcast.13, bf16[16,1792]{1,0:T(8,128)(2,1)S(1)} %broadcast_in_dim.15.edge_ref, f32[1,1792]{1,0:T(1,128)S(1)} %broadcast_in_dim.16.gain_ref, f32[3,1792]{1,0:T(4,128)S(1)} %copy-done.7, ...), custom_call_target="tpu_custom_call" | custom-call | flops 1000 | bytes 1000 | tf_op jit(solution)/shard_map/project/pallas_call | solution.py:124
  19.3 0.0 copy-start.9
  19.3 0.0 copy-start.8
  19.3 0.0 copy-start.2
  19.3 2.1 %collective-permute-done.2.refs_3_ = bf16[144,1792]{1,0:T(8,128)(2,1)S(1)} collective-permute-done((bf16[144,1792]{1,0:T(8,128)(2,1)}, bf16[144,1792]{1,0:T(8,128)(2,1)S(1)}, u32[]{:S(2)}, u32[]{:S(2)}) %collective-permute-start.2) | collective-permute-done | bytes 516128 | tf_op jit(solution)/shard_map/ppermute | solution.py:90
  21.4 0.2 collect_second.1
  21.6 1.3 %collective-permute-start.4 = (bf16[232,1792]{1,0:T(8,128)(2,1)S(1)}, bf16[232,1792]{1,0:T(8,128)(2,1)S(1)}, u32[]{:S(2)}, u32[]{:S(2)}) collective-permute-start(bf16[232,1792]{1,0:T(8,128)(2,1)S(1)} %get-tuple-element.85), channel_id=1, source_target_pairs={{0,4},{1,5},{2,6},{3,7},{4,0},{5,1},{6,2},{7,3},{8,12},{9,13},{10,... | collective-permute-start | bytes 2494472 | tf_op jit(solution)/shard_map/ppermute | solution.py:90
  22.9 0.5 collective-permute-start.3
  23.4 1.6 %collective-permute-start.5 = (bf16[216,1792]{1,0:T(8,128)(2,1)S(1)}, bf16[216,1792]{1,0:T(8,128)(2,1)S(1)}, u32[]{:S(2)}, u32[]{:S(2)}) collective-permute-start(bf16[216,1792]{1,0:T(8,128)(2,1)S(1)} %get-tuple-element.86), channel_id=1, source_target_pairs={{0,8},{1,9},{2,10},{3,11},{4,12},{5,13},{6,14},{7,15},{8,24},{9,25... | collective-permute-start | bytes 2322440 | tf_op jit(solution)/shard_map/ppermute | solution.py:90
  25.7 3.7 %attend.1 = (f32[256,896]{1,0:T(8,128)S(1)}, f32[256,8]{1,0:T(8,128)S(1)}, f32[273,1,896]{2,1,0:T(1,128)}, f32[8,273]{1,0:T(8,128)}) custom-call(s32[1]{0:T(128)S(6)} %copy.27.count_ref, f32[8,256]{1,0:T(8,128)S(1)} %bitcast.15, bf16[256,128]{1,0:T(8,128)(2,1)S(1)} %get-tuple-element.90.queries_ref, bf16[256,128]{1,0:T(8,128)(2,1)S(1)} %get-tuple-element.91.keys_ref, ...), custom_call_target="tpu_custom_call" | custom-call | flops 1000 | bytes 1000 | tf_op jit(solution)/shard_map/attend/pallas_call | solution.py:124
  29.4 2.6 %mix.1 = (bf16[256,1792]{1,0:T(8,128)(2,1)S(1)}, bf16[256,1792]{1,0:T(8,128)(2,1)S(1)}) custom-call(f32[256,896]{1,0:T(8,128)S(1)} %get-tuple-element.93.numer_ref, f32[256,8]{1,0:T(8,128)S(1)} %get-tuple-element.94.denom_ref, bf16[256,1792]{1,0:T(8,128)(2,1)S(1)} %bitcast.14, bf16[896,1792]{1,0:T(8,128)(2,1)S(1)} %copy-done.4, ...), custom_call_target="tpu_custom_call" | custom-call | flops 1000 | bytes 1000 | tf_op jit(solution)/shard_map/mix/pallas_call | solution.py:124
  32.0 9.7 %collective-permute-done.5.refs_2_.refs_6_.refs_4_ = bf16[216,1792]{1,0:T(8,128)(2,1)S(1)} collective-permute-done((bf16[216,1792]{1,0:T(8,128)(2,1)S(1)}, bf16[216,1792]{1,0:T(8,128)(2,1)S(1)}, u32[]{:S(2)}, u32[]{:S(2)}) %collective-permute-start.5) | collective-permute-done | bytes 774176 | tf_op jit(solution)/shard_map/ppermute | solution.py:90
  41.6 0.2 collect_third.1
  41.8 1.0 %collective-permute-start.8 = (bf16[240,1792]{1,0:T(8,128)(2,1)S(1)}, bf16[240,1792]{1,0:T(8,128)(2,1)S(1)}, u32[]{:S(2)}, u32[]{:S(2)}) collective-permute-start(bf16[240,1792]{1,0:T(8,128)(2,1)S(1)} %get-tuple-element.104), channel_id=1, source_target_pairs={{0,8},{1,9},{2,10},{3,11},{4,12},{5,13},{6,14},{7,15},{8,24},{9,25... | collective-permute-start | bytes 2580488 | tf_op jit(solution)/shard_map/ppermute | solution.py:90
  42.8 1.2 %collective-permute-start.6 = (bf16[224,1792]{1,0:T(8,128)(2,1)S(1)}, bf16[224,1792]{1,0:T(8,128)(2,1)S(1)}, u32[]{:S(2)}, u32[]{:S(2)}) collective-permute-start(bf16[224,1792]{1,0:T(8,128)(2,1)S(1)} %get-tuple-element.102), channel_id=1, source_target_pairs={{0,2},{1,3},{2,0},{3,1},{4,6},{5,7},{6,4},{7,5},{8,10},{9,11},{10,... | collective-permute-start | bytes 2408456 | tf_op jit(solution)/shard_map/ppermute | solution.py:90
  44.1 0.5 collective-permute-start.7
  44.6 14.6 %collective-permute-done.7.refs_0_.refs_6_.refs_1_ = bf16[208,1792]{1,0:T(8,128)(2,1)S(1)} collective-permute-done((bf16[208,1792]{1,0:T(8,128)(2,1)S(1)}, bf16[208,1792]{1,0:T(8,128)(2,1)S(1)}, u32[]{:S(2)}, u32[]{:S(2)}) %collective-permute-start.7) | collective-permute-done | bytes 745504 | tf_op jit(solution)/shard_map/ppermute | solution.py:90
  59.2 0.5 collective-permute-done.6.refs_5_.refs_0_
  59.8 1.2 %collective-permute-done.8.refs_1_.refs_7_ = bf16[240,1792]{1,0:T(8,128)(2,1)S(1)} collective-permute-done((bf16[240,1792]{1,0:T(8,128)(2,1)S(1)}, bf16[240,1792]{1,0:T(8,128)(2,1)S(1)}, u32[]{:S(2)}, u32[]{:S(2)}) %collective-permute-start.8) | collective-permute-done | bytes 860192 | tf_op jit(solution)/shard_map/ppermute | solution.py:90
  61.0 0.1 collect_fourth.1
  61.1 0.8 collective-permute-start.10
  61.9 0.8 collective-permute-start.9
  62.7 2.8 %collective-permute-start.11 = (bf16[128,1792]{1,0:T(8,128)(2,1)S(1)}, bf16[128,1792]{1,0:T(8,128)(2,1)S(1)}, u32[]{:S(2)}, u32[]{:S(2)}) collective-permute-start(bf16[128,1792]{1,0:T(8,128)(2,1)S(1)} %get-tuple-element.112), channel_id=1, source_target_pairs={{0,8},{1,9},{2,10},{3,11},{4,12},{5,13},{6,14},{7,15},{8,24},{9,25... | collective-permute-start | bytes 1376264 | tf_op jit(solution)/shard_map/ppermute | solution.py:90
  65.5 3.2 %accumulate_second.1 = (f32[256,1792]{1,0:T(8,128)S(1)}, f32[256,1792]{1,0:T(8,128)S(1)}) custom-call(bf16[168,1792]{1,0:T(8,128)(2,1)S(1)} %copy-done, bf16[168,1792]{1,0:T(8,128)(2,1)S(1)} %collective-permute-done.refs_1_, bf16[168,1792]{1,0:T(8,128)(2,1)S(1)} %collective-permute-done.1.refs_2_, bf16[144,1792]{1,0:T(8,128)(2,1)S(1)} %collective-permute-done.2.refs_3_, ...), custom_call_target="tpu_custom_call" | custom-call | flops 1000 | bytes 1000 | tf_op jit(solution)/shard_map/accumulate_second/pallas_call | solution.py:124
  68.7 3.9 %accumulate_third.1 = (f32[256,1792]{1,0:T(8,128)S(1)}, f32[256,1792]{1,0:T(8,128)S(1)}) custom-call(bf16[168,1792]{1,0:T(8,128)(2,1)S(1)} %copy-done, bf16[168,1792]{1,0:T(8,128)(2,1)S(1)} %collective-permute-done.refs_1_, bf16[168,1792]{1,0:T(8,128)(2,1)S(1)} %collective-permute-done.1.refs_2_, ...), custom_call_target="tpu_custom_call", output_to_operand_aliasing={{0}: (10, {}), {1}: (11, {})} | custom-call | flops 1000 | bytes 1000 | tf_op jit(solution)/shard_map/accumulate_third/pallas_call | solution.py:124
  72.7 1.0 %collective-permute-done.9.refs_2_.refs_0_ = bf16[144,1792]{1,0:T(8,128)(2,1)S(1)} collective-permute-done((bf16[144,1792]{1,0:T(8,128)(2,1)S(1)}, bf16[144,1792]{1,0:T(8,128)(2,1)S(1)}, u32[]{:S(2)}, u32[]{:S(2)}) %collective-permute-start.9) | collective-permute-done | bytes 516128 | tf_op jit(solution)/shard_map/ppermute | solution.py:90
  73.7 0.1 collect_fifth.1
  73.8 0.2 collective-permute-start.13
  74.0 2.3 %collective-permute-start.14 = (bf16[112,1792]{1,0:T(8,128)(2,1)S(1)}, bf16[112,1792]{1,0:T(8,128)(2,1)S(1)}, u32[]{:S(2)}, u32[]{:S(2)}) collective-permute-start(bf16[112,1792]{1,0:T(8,128)(2,1)S(1)} %get-tuple-element.125), channel_id=1, source_target_pairs={{0,4},{1,5},{2,6},{3,7},{4,0},{5,1},{6,2},{7,3},{8,12},{9,13},{10,... | collective-permute-start | bytes 1204232 | tf_op jit(solution)/shard_map/ppermute | solution.py:90
  76.3 2.1 %collective-permute-start.15 = (bf16[56,1792]{1,0:T(8,128)(2,1)S(1)}, bf16[56,1792]{1,0:T(8,128)(2,1)S(1)}, u32[]{:S(2)}, u32[]{:S(2)}) collective-permute-start(bf16[56,1792]{1,0:T(8,128)(2,1)S(1)} %get-tuple-element.126), channel_id=1, source_target_pairs={{0,8},{1,9},{2,10},{3,11},{4,12},{5,13},{6,14},{7,15},{8,24},{9,25... | collective-permute-start | bytes 602120 | tf_op jit(solution)/shard_map/ppermute | solution.py:90
  78.4 2.0 %accumulate_fourth.1 = (f32[256,1792]{1,0:T(8,128)S(1)}, f32[256,1792]{1,0:T(8,128)S(1)}) custom-call(bf16[144,1792]{1,0:T(8,128)(2,1)S(1)} %collective-permute-done.9.refs_2_.refs_0_, bf16[144,1792]{1,0:T(8,128)(2,1)S(1)} %collective-permute-done.10.refs_3_.refs_1_, ...), custom_call_target="tpu_custom_call", output_to_operand_aliasing={{0}: (5, {}), {1}: (6, {})} | custom-call | flops 1000 | bytes 1000 | tf_op jit(solution)/shard_map/accumulate_fourth/pallas_call | solution.py:124
  80.4 2.5 %collective-permute-done.15.refs_3_ = bf16[56,1792]{1,0:T(8,128)(2,1)S(1)} collective-permute-done((bf16[56,1792]{1,0:T(8,128)(2,1)S(1)}, bf16[56,1792]{1,0:T(8,128)(2,1)S(1)}, u32[]{:S(2)}, u32[]{:S(2)}) %collective-permute-start.15) | collective-permute-done | bytes 200736 | tf_op jit(solution)/shard_map/ppermute | solution.py:90
  82.9 1.0 %finish_other.1 = bf16[256,1792]{1,0:T(8,128)(2,1)S(1)} custom-call(bf16[112,1792]{1,0:T(8,128)(2,1)S(1)} %collective-permute-done.13.refs_0_, bf16[112,1792]{1,0:T(8,128)(2,1)S(1)} %collective-permute-done.14.refs_1_, bf16[128,1792]{1,0:T(8,128)(2,1)S(1)} %collective-permute-done.11.refs_4_.refs_2_, bf16[56,1792]{1,0:T(8,128)(2,1)S(1)} %collective-permute-done.15.refs_3_, ...), custom_call_target="tpu_custom_call" | custom-call | flops 1000 | bytes 1000 | tf_op jit(solution)/shard_map/finish_other/pallas_call | solution.py:124
  83.9 0.1 collective-permute-start.16
  84.0 1.4 %finish_own.1.kept_ref = f32[256,1792]{1,0:T(8,128)S(1)} custom-call(bf16[112,1792]{1,0:T(8,128)(2,1)S(1)} %collective-permute-done.13.refs_0_, bf16[112,1792]{1,0:T(8,128)(2,1)S(1)} %collective-permute-done.14.refs_1_, bf16[128,1792]{1,0:T(8,128)(2,1)S(1)} %collective-permute-done.11.refs_4_.refs_2_, ...), custom_call_target="tpu_custom_call", output_to_operand_aliasing={{}: (5, {})} | custom-call | flops 1000 | bytes 1000 | tf_op jit(solution)/shard_map/finish_own/pallas_call | solution.py:124
  85.4 1.1 %collective-permute-done.16.given_ref = bf16[256,1792]{1,0:T(8,128)(2,1)S(1)} collective-permute-done((bf16[256,1792]{1,0:T(8,128)(2,1)S(1)}, bf16[256,1792]{1,0:T(8,128)(2,1)S(1)}, u32[]{:S(2)}, u32[]{:S(2)}) %collective-permute-start.16) | collective-permute-done | bytes 917536 | tf_op jit(solution)/shard_map/ppermute | solution.py:90
  86.5 1.2 %final.1 = bf16[256,1792]{1,0:T(8,128)(2,1)} custom-call(s32[1]{0:T(128)S(6)} %copy.27.count_ref, f32[256,1792]{1,0:T(8,128)S(1)} %finish_own.1.kept_ref, bf16[256,1792]{1,0:T(8,128)(2,1)S(1)} %collective-permute-done.16.given_ref), custom_call_target="tpu_custom_call" | custom-call | flops 1000 | bytes 1000 | tf_op jit(solution)/shard_map/final/pallas_call | solution.py:124
  (23 shorter events, 0.1 us)
Async XLA Ops:
  2.8 18.6 %collective-permute-start = (bf16[168,1792]{1,0:T(8,128)(2,1)}, bf16[168,1792]{1,0:T(8,128)(2,1)S(1)}, u32[]{:S(2)}, u32[]{:S(2)}) collective-permute-start(bf16[168,1792]{1,0:T(8,128)(2,1)} %get-tuple-element.73.refs_0_), channel_id=1, source_target_pairs={{0,2},{1,3},{2,0},{3,1},{4,6},{5,7},{6,4},{7,5},{8,10},{9,11},{10,... | collective-permute-start | bytes 1806344 | tf_op jit(solution)/shard_map/ppermute | solution.py:90
  5.8 15.6 %collective-permute-start.1 = (bf16[168,1792]{1,0:T(8,128)(2,1)}, bf16[168,1792]{1,0:T(8,128)(2,1)S(1)}, u32[]{:S(2)}, u32[]{:S(2)}) collective-permute-start(bf16[168,1792]{1,0:T(8,128)(2,1)} %get-tuple-element.73.refs_0_), channel_id=1, source_target_pairs={{0,4},{1,5},{2,6},{3,7},{4,0},{5,1},{6,2},{7,3},{8,12},{9,13},{10,... | collective-permute-start | bytes 1806344 | tf_op jit(solution)/shard_map/ppermute | solution.py:90
  7.4 14.0 %collective-permute-start.2 = (bf16[144,1792]{1,0:T(8,128)(2,1)}, bf16[144,1792]{1,0:T(8,128)(2,1)S(1)}, u32[]{:S(2)}, u32[]{:S(2)}) collective-permute-start(bf16[144,1792]{1,0:T(8,128)(2,1)} %get-tuple-element.74), channel_id=1, source_target_pairs={{0,8},{1,9},{2,10},{3,11},{4,12},{5,13},{6,14},{7,15},{8,24},{9,25... | collective-permute-start | bytes 1548296 | tf_op jit(solution)/shard_map/ppermute | solution.py:90
  9.7 1.2 %copy-start.1 = (bf16[1,256,1792]{2,1,0:T(8,128)(2,1)S(1)}, bf16[1,256,1792]{2,1,0:T(8,128)(2,1)}, u32[]{:S(2)}) copy-start(bf16[1,256,1792]{2,1,0:T(8,128)(2,1)} %param.13) | copy-start | bytes 2752516
  10.8 1.9 %copy-start.3 = (bf16[1792,896]{1,0:T(8,128)(2,1)S(1)}, bf16[1792,896]{1,0:T(8,128)(2,1)}, u32[]{:S(2)}) copy-start(bf16[1792,896]{1,0:T(8,128)(2,1)} %value_ref.1) | copy-start | bytes 9633796
  12.7 1.0 %copy-start.5 = (bf16[1792,128]{1,0:T(8,128)(2,1)S(1)}, bf16[1792,128]{1,0:T(8,128)(2,1)}, u32[]{:S(2)}) copy-start(bf16[1792,128]{1,0:T(8,128)(2,1)} %query_ref.1) | copy-start | bytes 1376260
  13.8 1.0 %copy-start.6 = (bf16[1792,128]{1,0:T(8,128)(2,1)S(1)}, bf16[1792,128]{1,0:T(8,128)(2,1)}, u32[]{:S(2)}) copy-start(bf16[1792,128]{1,0:T(8,128)(2,1)} %key_ref.1) | copy-start | bytes 1376260
  14.8 0.7 copy-start.7
  15.5 5.9 %copy-start = (bf16[168,1792]{1,0:T(8,128)(2,1)S(1)}, bf16[168,1792]{1,0:T(8,128)(2,1)}, u32[]{:S(2)}) copy-start(bf16[168,1792]{1,0:T(8,128)(2,1)} %get-tuple-element.73.refs_0_) | copy-start | bytes 1806340
  15.5 13.8 %copy-start.4 = (bf16[896,1792]{1,0:T(8,128)(2,1)S(1)}, bf16[896,1792]{1,0:T(8,128)(2,1)}, u32[]{:S(2)}) copy-start(bf16[896,1792]{1,0:T(8,128)(2,1)} %out_ref.1) | copy-start | bytes 9633796
  19.3 6.4 %copy-start.9 = (f32[1792]{0:T(1024)S(1)}, f32[1792]{0:T(1024)}, u32[]{:S(2)}) copy-start(f32[1792]{0:T(1024)} %param.22) | copy-start | bytes 21508
  19.3 6.4 %copy-start.8 = (f32[1,256,8]{1,2,0:T(8,128)S(1)}, f32[1,256,8]{1,2,0:T(8,128)}, u32[]{:S(2)}) copy-start(f32[1,256,8]{1,2,0:T(8,128)} %param.15) | copy-start | bytes 24580
  19.3 10.1 %copy-start.2 = (bf16[1,256,1792]{2,1,0:T(8,128)(2,1)S(1)}, bf16[1,256,1792]{2,1,0:T(8,128)(2,1)}, u32[]{:S(2)}) copy-start(bf16[1,256,1792]{2,1,0:T(8,128)(2,1)} %param.13) | copy-start | bytes 2752516
  21.6 20.1 %collective-permute-start.4 = (bf16[232,1792]{1,0:T(8,128)(2,1)S(1)}, bf16[232,1792]{1,0:T(8,128)(2,1)S(1)}, u32[]{:S(2)}, u32[]{:S(2)}) collective-permute-start(bf16[232,1792]{1,0:T(8,128)(2,1)S(1)} %get-tuple-element.85), channel_id=1, source_target_pairs={{0,4},{1,5},{2,6},{3,7},{4,0},{5,1},{6,2},{7,3},{8,12},{9,13},{10,... | collective-permute-start | bytes 2494472 | tf_op jit(solution)/shard_map/ppermute | solution.py:90
  22.9 18.8 %collective-permute-start.3 = (bf16[224,1792]{1,0:T(8,128)(2,1)S(1)}, bf16[224,1792]{1,0:T(8,128)(2,1)S(1)}, u32[]{:S(2)}, u32[]{:S(2)}) collective-permute-start(bf16[224,1792]{1,0:T(8,128)(2,1)S(1)} %get-tuple-element.84), channel_id=1, source_target_pairs={{0,2},{1,3},{2,0},{3,1},{4,6},{5,7},{6,4},{7,5},{8,10},{9,11},{10,... | collective-permute-start | bytes 2408456 | tf_op jit(solution)/shard_map/ppermute | solution.py:90
  23.4 18.2 %collective-permute-start.5 = (bf16[216,1792]{1,0:T(8,128)(2,1)S(1)}, bf16[216,1792]{1,0:T(8,128)(2,1)S(1)}, u32[]{:S(2)}, u32[]{:S(2)}) collective-permute-start(bf16[216,1792]{1,0:T(8,128)(2,1)S(1)} %get-tuple-element.86), channel_id=1, source_target_pairs={{0,8},{1,9},{2,10},{3,11},{4,12},{5,13},{6,14},{7,15},{8,24},{9,25... | collective-permute-start | bytes 2322440 | tf_op jit(solution)/shard_map/ppermute | solution.py:90
  41.8 19.2 %collective-permute-start.8 = (bf16[240,1792]{1,0:T(8,128)(2,1)S(1)}, bf16[240,1792]{1,0:T(8,128)(2,1)S(1)}, u32[]{:S(2)}, u32[]{:S(2)}) collective-permute-start(bf16[240,1792]{1,0:T(8,128)(2,1)S(1)} %get-tuple-element.104), channel_id=1, source_target_pairs={{0,8},{1,9},{2,10},{3,11},{4,12},{5,13},{6,14},{7,15},{8,24},{9,25... | collective-permute-start | bytes 2580488 | tf_op jit(solution)/shard_map/ppermute | solution.py:90
  42.8 17.0 %collective-permute-start.6 = (bf16[224,1792]{1,0:T(8,128)(2,1)S(1)}, bf16[224,1792]{1,0:T(8,128)(2,1)S(1)}, u32[]{:S(2)}, u32[]{:S(2)}) collective-permute-start(bf16[224,1792]{1,0:T(8,128)(2,1)S(1)} %get-tuple-element.102), channel_id=1, source_target_pairs={{0,2},{1,3},{2,0},{3,1},{4,6},{5,7},{6,4},{7,5},{8,10},{9,11},{10,... | collective-permute-start | bytes 2408456 | tf_op jit(solution)/shard_map/ppermute | solution.py:90
  44.1 15.2 %collective-permute-start.7 = (bf16[208,1792]{1,0:T(8,128)(2,1)S(1)}, bf16[208,1792]{1,0:T(8,128)(2,1)S(1)}, u32[]{:S(2)}, u32[]{:S(2)}) collective-permute-start(bf16[208,1792]{1,0:T(8,128)(2,1)S(1)} %get-tuple-element.103), channel_id=1, source_target_pairs={{0,4},{1,5},{2,6},{3,7},{4,0},{5,1},{6,2},{7,3},{8,12},{9,13},{10,... | collective-permute-start | bytes 2236424 | tf_op jit(solution)/shard_map/ppermute | solution.py:90
  44.6 20.9 %collective-permute-start.12 = (bf16[256,1792]{1,0:T(8,128)(2,1)S(1)}, bf16[256,1792]{1,0:T(8,128)(2,1)S(1)}, u32[]{:S(2)}, u32[]{:S(2)}) collective-permute-start(bf16[256,1792]{1,0:T(8,128)(2,1)S(1)} %get-tuple-element.116.refs_7_.refs_8_.refs_3_.refs_4_), channel_id=1, source_target_pairs={{0,1},{1,0},{2,3},{3,2},{4,5},{5,4},{6,7},{7,6},{8,9},{9,8},{10,11... | collective-permute-start | bytes 2752520 | tf_op jit(solution)/shard_map/ppermute | solution.py:90
  61.1 11.6 %collective-permute-start.10 = (bf16[144,1792]{1,0:T(8,128)(2,1)S(1)}, bf16[144,1792]{1,0:T(8,128)(2,1)S(1)}, u32[]{:S(2)}, u32[]{:S(2)}) collective-permute-start(bf16[144,1792]{1,0:T(8,128)(2,1)S(1)} %get-tuple-element.111), channel_id=1, source_target_pairs={{0,4},{1,5},{2,6},{3,7},{4,0},{5,1},{6,2},{7,3},{8,12},{9,13},{10,... | collective-permute-start | bytes 1548296 | tf_op jit(solution)/shard_map/ppermute | solution.py:90
  61.9 11.8 %collective-permute-start.9 = (bf16[144,1792]{1,0:T(8,128)(2,1)S(1)}, bf16[144,1792]{1,0:T(8,128)(2,1)S(1)}, u32[]{:S(2)}, u32[]{:S(2)}) collective-permute-start(bf16[144,1792]{1,0:T(8,128)(2,1)S(1)} %get-tuple-element.111), channel_id=1, source_target_pairs={{0,2},{1,3},{2,0},{3,1},{4,6},{5,7},{6,4},{7,5},{8,10},{9,11},{10,... | collective-permute-start | bytes 1548296 | tf_op jit(solution)/shard_map/ppermute | solution.py:90
  62.7 9.9 %collective-permute-start.11 = (bf16[128,1792]{1,0:T(8,128)(2,1)S(1)}, bf16[128,1792]{1,0:T(8,128)(2,1)S(1)}, u32[]{:S(2)}, u32[]{:S(2)}) collective-permute-start(bf16[128,1792]{1,0:T(8,128)(2,1)S(1)} %get-tuple-element.112), channel_id=1, source_target_pairs={{0,8},{1,9},{2,10},{3,11},{4,12},{5,13},{6,14},{7,15},{8,24},{9,25... | collective-permute-start | bytes 1376264 | tf_op jit(solution)/shard_map/ppermute | solution.py:90
  73.8 9.2 %collective-permute-start.13 = (bf16[112,1792]{1,0:T(8,128)(2,1)S(1)}, bf16[112,1792]{1,0:T(8,128)(2,1)S(1)}, u32[]{:S(2)}, u32[]{:S(2)}) collective-permute-start(bf16[112,1792]{1,0:T(8,128)(2,1)S(1)} %get-tuple-element.124), channel_id=1, source_target_pairs={{0,2},{1,3},{2,0},{3,1},{4,6},{5,7},{6,4},{7,5},{8,10},{9,11},{10,... | collective-permute-start | bytes 1204232 | tf_op jit(solution)/shard_map/ppermute | solution.py:90
  74.0 9.0 %collective-permute-start.14 = (bf16[112,1792]{1,0:T(8,128)(2,1)S(1)}, bf16[112,1792]{1,0:T(8,128)(2,1)S(1)}, u32[]{:S(2)}, u32[]{:S(2)}) collective-permute-start(bf16[112,1792]{1,0:T(8,128)(2,1)S(1)} %get-tuple-element.125), channel_id=1, source_target_pairs={{0,4},{1,5},{2,6},{3,7},{4,0},{5,1},{6,2},{7,3},{8,12},{9,13},{10,... | collective-permute-start | bytes 1204232 | tf_op jit(solution)/shard_map/ppermute | solution.py:90
  76.3 6.6 %collective-permute-start.15 = (bf16[56,1792]{1,0:T(8,128)(2,1)S(1)}, bf16[56,1792]{1,0:T(8,128)(2,1)S(1)}, u32[]{:S(2)}, u32[]{:S(2)}) collective-permute-start(bf16[56,1792]{1,0:T(8,128)(2,1)S(1)} %get-tuple-element.126), channel_id=1, source_target_pairs={{0,8},{1,9},{2,10},{3,11},{4,12},{5,13},{6,14},{7,15},{8,24},{9,25... | collective-permute-start | bytes 602120 | tf_op jit(solution)/shard_map/ppermute | solution.py:90
  83.9 2.5 %collective-permute-start.16 = (bf16[256,1792]{1,0:T(8,128)(2,1)S(1)}, bf16[256,1792]{1,0:T(8,128)(2,1)S(1)}, u32[]{:S(2)}, u32[]{:S(2)}) collective-permute-start(bf16[256,1792]{1,0:T(8,128)(2,1)S(1)} %finish_other.1), channel_id=1, source_target_pairs={{0,1},{1,0},{2,3},{3,2},{4,5},{5,4},{6,7},{7,6},{8,9},{9,8},{10,11... | collective-permute-start | bytes 2752520 | tf_op jit(solution)/shard_map/ppermute | solution.py:90

commit v12 on v11

--- a/solution.py
+++ b/solution.py
@@ -591,15 +591,21 @@
     near2, far2, deep2 = together(near2, far2, deep2)
 
     held = 2 * main // 3
-    deep3_main, line = collect(
-        (far2, deep2),
+    two = 2 * main
+    sends = collect(
+        (near2, far2, deep2),
         (
-            ((1, 0, wide),),
-            ((1, wide, wide + 4 * narrow), (0, 2 * wide - cut - main, 2 * wide - cut - main + held)),
+            ((2, main, wide),),
+            ((2, 0, main), (2, two, wide)),
+            ((2, wide, wide + 4 * narrow), (1, 2 * wide - cut - main, 2 * wide - cut - main + held)),
+            ((2, 0, main), (1, 0, main), (1, two + held, wide)),
+            ((2, main, two), (0, main, two)),
         ),
         "collect_fourth",
     )
-    near3, far3, deep3 = slot((flip_near, deep3_main), (flip_far, deep3_main), (next_plane, line))
+    sends = together(*sends)
+    near3, far3, deep3 = flip_near(sends[0]), flip_far(sends[1]), next_plane(sends[2])
+    near3_more, far3_more = flip_near(sends[3]), flip_far(sends[4])
     acc = accumulate(
         rows,
         (shard, near, far, far1, deep1, near2, far2, deep2),
@@ -615,33 +621,33 @@
     )
     near3, far3, deep3, *acc = together(near3, far3, deep3, *acc)
 
-    two = 2 * main
     sends = collect(
-        (near2, far2, near3, far3, deep3),
+        (near3, far3, deep3),
         (
-            ((1, 0, main), (1, two + held, wide), (3, 0, main)),
-            ((0, main, two), (2, main, two), (2, two + held, wide)),
-            ((4, 3 * narrow, 4 * narrow + held),),
+            ((1, 0, main),),
+            ((0, 0, main), (0, main + held, two)),
+            ((2, 3 * narrow, 4 * narrow + held),),
         ),
         "collect_fifth",
     )
     near4, far4, deep4 = slot(*zip((flip_near, flip_far, next_plane), sends))
+    line = 4 * narrow
     acc = accumulate(
         rows,
-        (near3, far3, deep3),
-        [runs(0, 0, main), runs(1, 0, main)] + [runs(2, k * narrow, edge) for k in range(4)],
+        (near3, near3_more, far3, far3_more, deep3),
+        [((1, 0, main), (0, 0, main), (0, main, two)), ((2, 0, main), (3, 0, main), (2, main, two))]
+        + [((1, main, main + held), (3, main, main + held), (4, line, line + held))]
+        + [((1, main + held, two), (3, main + held, two), (1, two, two + main - held))]
+        + [runs(4, k * narrow, edge) for k in range(4)],
         tuple(acc),
         jnp.float32,
         "accumulate_fourth",
     )
-    weights = (near4, far4, deep3, deep4)
-    line, then = 4 * narrow, two - held
+    weights = (near4, far4, deep4)
     last = [
-        ((0, 0, held), (1, 0, held), (2, line, line + held)),
-        ((0, held, main), (1, held, main), (0, main, then)),
-        ((0, then, then + held), (1, main, main + held), (3, narrow, narrow + held)),
-        ((0, then + held, then + main), (1, main + held, two), (1, two, two + main - held)),
-        runs(3, 0, edge),
+        ((0, 0, held), (1, 0, held), (2, narrow, narrow + held)),
+        ((0, held, main), (1, held, main), (1, main, two - held)),
+        runs(2, 0, edge),
     ]
     (given,) = accumulate(rows[1:], weights, last, acc[1:], jnp.bfloat16, "finish_other")
     (kept,) = accumulate(

time: 88.1 us -> 89.2 us (1.012)
  starting transfers between devices: 21.4 us -> 24 us
  waiting for transfers between devices: 32.8 us -> 31.4 us
    ppermute x17 -> x19, starting transfers between devices: 21.4 us -> 24 us  [permute(): return lax.ppermute(array, 'req', [(i, target(i)) for i in range(count)])]
    ppermute x17 -> x19, waiting for transfers between devices: 32.8 us -> 31.4 us  [permute(): return lax.ppermute(array, 'req', [(i, target(i)) for i in range(count)])]
  transfers between devices with their start and end apart: 17 -> 19, of which waited for: 8 -> 7; matrix products, arithmetic and copies ran while one was open for 1% -> 1% of each run, Pallas kernels for 23% -> 23%
where the time goes in v12:
time: 89.2 us; the launch traced here: 88.8 us
  waiting for transfers between devices  31.4 us (35%)
  Pallas kernels  25.4 us (28%)
  starting transfers between devices  24 us (27%)
  local copies, waits for them, and re-layouts  6.61 us (7%)
  between operations  1.48 us (2%)
    ppermute x19, waiting for transfers between devices, permute(): return lax.ppermute(array, 'req', [(i, target(i)) for i in range(count)])  31.4 us
    pallas_call x14, Pallas kernels, kernel_call(): pl.pallas_call(body, out_shape=out_shape, in_specs=specs or vmem(len(oper...  25.4 us
    ppermute x19, starting transfers between devices, permute(): return lax.ppermute(array, 'req', [(i, target(i)) for i in range(count)])  24 us
    unnamed x20, local copies, waits for them, and re-layouts  5.89 us
  transfers between devices with their start and end apart: 19, of which 7 were waited for; matrix products, arithmetic and copies ran while one was open for 1% of the time, Pallas kernels for 23%

profile of v12, /device:TPU:0, one launch (start us, length us, event | category | flops | bytes accessed | tf_op | source)
XLA Modules:
  0.0 88.8 jit_solution(61713053465115589)
XLA Ops:
  0.6 2.2 %shard.1 = (bf16[168,1792]{1,0:T(8,128)(2,1)}, bf16[144,1792]{1,0:T(8,128)(2,1)}) custom-call(bf16[56,1792]{1,0:T(8,128)(2,1)} %bitcast.17, bf16[56,1792]{1,0:T(8,128)(2,1)} %bitcast.18, bf16[56,1792]{1,0:T(8,128)(2,1)} %bitcast.19), custom_call_target="tpu_custom_call" | custom-call | flops 1000 | bytes 1000 | tf_op jit(solution)/shard_map/shard/pallas_call | solution.py:124
  2.8 3.0 %collective-permute-start = (bf16[168,1792]{1,0:T(8,128)(2,1)}, bf16[168,1792]{1,0:T(8,128)(2,1)S(1)}, u32[]{:S(2)}, u32[]{:S(2)}) collective-permute-start(bf16[168,1792]{1,0:T(8,128)(2,1)} %get-tuple-element.70.refs_0_), channel_id=1, source_target_pairs={{0,2},{1,3},{2,0},{3,1},{4,6},{5,7},{6,4},{7,5},{8,10},{9,11},{10,... | collective-permute-start | bytes 1806344 | tf_op jit(solution)/shard_map/ppermute | solution.py:90
  5.8 1.5 %collective-permute-start.1 = (bf16[168,1792]{1,0:T(8,128)(2,1)}, bf16[168,1792]{1,0:T(8,128)(2,1)S(1)}, u32[]{:S(2)}, u32[]{:S(2)}) collective-permute-start(bf16[168,1792]{1,0:T(8,128)(2,1)} %get-tuple-element.70.refs_0_), channel_id=1, source_target_pairs={{0,4},{1,5},{2,6},{3,7},{4,0},{5,1},{6,2},{7,3},{8,12},{9,13},{10,... | collective-permute-start | bytes 1806344 | tf_op jit(solution)/shard_map/ppermute | solution.py:90
  7.4 1.6 %collective-permute-start.2 = (bf16[144,1792]{1,0:T(8,128)(2,1)}, bf16[144,1792]{1,0:T(8,128)(2,1)S(1)}, u32[]{:S(2)}, u32[]{:S(2)}) collective-permute-start(bf16[144,1792]{1,0:T(8,128)(2,1)} %get-tuple-element.71), channel_id=1, source_target_pairs={{0,8},{1,9},{2,10},{3,11},{4,12},{5,13},{6,14},{7,15},{8,24},{9,25... | collective-permute-start | bytes 1548296 | tf_op jit(solution)/shard_map/ppermute | solution.py:90
  8.9 0.7 broadcast_in_dim.16.gain_ref
  9.7 0.0 copy-start.1
  9.7 1.2 %copy-done.1 = bf16[1,256,1792]{2,1,0:T(8,128)(2,1)S(1)} copy-done((bf16[1,256,1792]{2,1,0:T(8,128)(2,1)S(1)}, bf16[1,256,1792]{2,1,0:T(8,128)(2,1)}, u32[]{:S(2)}) %copy-start.1) | copy-done | bytes 917528
  10.8 1.9 %copy-done.3 = bf16[1792,896]{1,0:T(8,128)(2,1)S(1)} copy-done((bf16[1792,896]{1,0:T(8,128)(2,1)S(1)}, bf16[1792,896]{1,0:T(8,128)(2,1)}, u32[]{:S(2)}) %copy-start.3) | copy-done | bytes 3211288
  12.7 1.0 %copy-done.5 = bf16[1792,128]{1,0:T(8,128)(2,1)S(1)} copy-done((bf16[1792,128]{1,0:T(8,128)(2,1)S(1)}, bf16[1792,128]{1,0:T(8,128)(2,1)}, u32[]{:S(2)}) %copy-start.5) | copy-done | bytes 458776
  13.8 1.0 %copy-done.6 = bf16[1792,128]{1,0:T(8,128)(2,1)S(1)} copy-done((bf16[1792,128]{1,0:T(8,128)(2,1)S(1)}, bf16[1792,128]{1,0:T(8,128)(2,1)}, u32[]{:S(2)}) %copy-start.6) | copy-done | bytes 458776
  14.8 0.7 copy-done.7
  15.5 3.7 %project.1 = (bf16[256,128]{1,0:T(8,128)(2,1)S(1)}, bf16[256,128]{1,0:T(8,128)(2,1)S(1)}, bf16[256,896]{1,0:T(8,128)(2,1)S(1)}) custom-call(bf16[256,1792]{1,0:T(8,128)(2,1)S(1)} %bitcast.13, bf16[16,1792]{1,0:T(8,128)(2,1)S(1)} %broadcast_in_dim.15.edge_ref, f32[1,1792]{1,0:T(1,128)S(1)} %broadcast_in_dim.16.gain_ref, f32[3,1792]{1,0:T(4,128)S(1)} %copy-done.7, ...), custom_call_target="tpu_custom_call" | custom-call | flops 1000 | bytes 1000 | tf_op jit(solution)/shard_map/project/pallas_call | solution.py:124
  19.3 0.0 copy-start.8
  19.3 0.0 copy-start.2
  19.3 2.1 %collective-permute-done.2.refs_3_ = bf16[144,1792]{1,0:T(8,128)(2,1)S(1)} collective-permute-done((bf16[144,1792]{1,0:T(8,128)(2,1)}, bf16[144,1792]{1,0:T(8,128)(2,1)S(1)}, u32[]{:S(2)}, u32[]{:S(2)}) %collective-permute-start.2) | collective-permute-done | bytes 516128 | tf_op jit(solution)/shard_map/ppermute | solution.py:90
  21.4 0.2 collect_second.1
  21.6 1.3 %collective-permute-start.4 = (bf16[232,1792]{1,0:T(8,128)(2,1)S(1)}, bf16[232,1792]{1,0:T(8,128)(2,1)S(1)}, u32[]{:S(2)}, u32[]{:S(2)}) collective-permute-start(bf16[232,1792]{1,0:T(8,128)(2,1)S(1)} %get-tuple-element.82), channel_id=1, source_target_pairs={{0,4},{1,5},{2,6},{3,7},{4,0},{5,1},{6,2},{7,3},{8,12},{9,13},{10,... | collective-permute-start | bytes 2494472 | tf_op jit(solution)/shard_map/ppermute | solution.py:90
  22.9 0.5 collective-permute-start.3
  23.4 1.6 %collective-permute-start.5 = (bf16[216,1792]{1,0:T(8,128)(2,1)S(1)}, bf16[216,1792]{1,0:T(8,128)(2,1)S(1)}, u32[]{:S(2)}, u32[]{:S(2)}) collective-permute-start(bf16[216,1792]{1,0:T(8,128)(2,1)S(1)} %get-tuple-element.83), channel_id=1, source_target_pairs={{0,8},{1,9},{2,10},{3,11},{4,12},{5,13},{6,14},{7,15},{8,24},{9,25... | collective-permute-start | bytes 2322440 | tf_op jit(solution)/shard_map/ppermute | solution.py:90
  25.7 3.7 %attend.1 = (f32[256,896]{1,0:T(8,128)S(1)}, f32[256,8]{1,0:T(8,128)S(1)}, f32[273,1,896]{2,1,0:T(1,128)}, f32[8,273]{1,0:T(8,128)}) custom-call(s32[1]{0:T(128)S(6)} %copy.27.count_ref, f32[8,256]{1,0:T(8,128)S(1)} %bitcast.15, bf16[256,128]{1,0:T(8,128)(2,1)S(1)} %get-tuple-element.87.queries_ref, bf16[256,128]{1,0:T(8,128)(2,1)S(1)} %get-tuple-element.88.keys_ref, ...), custom_call_target="tpu_custom_call" | custom-call | flops 1000 | bytes 1000 | tf_op jit(solution)/shard_map/attend/pallas_call | solution.py:124
  29.4 2.6 %mix.1 = (bf16[256,1792]{1,0:T(8,128)(2,1)S(1)}, bf16[256,1792]{1,0:T(8,128)(2,1)S(1)}) custom-call(f32[256,896]{1,0:T(8,128)S(1)} %get-tuple-element.90.numer_ref, f32[256,8]{1,0:T(8,128)S(1)} %get-tuple-element.91.denom_ref, bf16[256,1792]{1,0:T(8,128)(2,1)S(1)} %bitcast.14, bf16[896,1792]{1,0:T(8,128)(2,1)S(1)} %copy-done.4, ...), custom_call_target="tpu_custom_call" | custom-call | flops 1000 | bytes 1000 | tf_op jit(solution)/shard_map/mix/pallas_call | solution.py:124
  32.0 9.7 %collective-permute-done.5.refs_2_.refs_6_.refs_4_ = bf16[216,1792]{1,0:T(8,128)(2,1)S(1)} collective-permute-done((bf16[216,1792]{1,0:T(8,128)(2,1)S(1)}, bf16[216,1792]{1,0:T(8,128)(2,1)S(1)}, u32[]{:S(2)}, u32[]{:S(2)}) %collective-permute-start.5) | collective-permute-done | bytes 774176 | tf_op jit(solution)/shard_map/ppermute | solution.py:90
  41.6 0.2 collect_third.1
  41.8 1.0 %collective-permute-start.8 = (bf16[240,1792]{1,0:T(8,128)(2,1)S(1)}, bf16[240,1792]{1,0:T(8,128)(2,1)S(1)}, u32[]{:S(2)}, u32[]{:S(2)}) collective-permute-start(bf16[240,1792]{1,0:T(8,128)(2,1)S(1)} %get-tuple-element.101), channel_id=1, source_target_pairs={{0,8},{1,9},{2,10},{3,11},{4,12},{5,13},{6,14},{7,15},{8,24},{9,25... | collective-permute-start | bytes 2580488 | tf_op jit(solution)/shard_map/ppermute | solution.py:90
  42.8 1.2 %collective-permute-start.6 = (bf16[224,1792]{1,0:T(8,128)(2,1)S(1)}, bf16[224,1792]{1,0:T(8,128)(2,1)S(1)}, u32[]{:S(2)}, u32[]{:S(2)}) collective-permute-start(bf16[224,1792]{1,0:T(8,128)(2,1)S(1)} %get-tuple-element.99), channel_id=1, source_target_pairs={{0,2},{1,3},{2,0},{3,1},{4,6},{5,7},{6,4},{7,5},{8,10},{9,11},{10,... | collective-permute-start | bytes 2408456 | tf_op jit(solution)/shard_map/ppermute | solution.py:90
  44.1 0.5 collective-permute-start.7
  44.6 14.6 %collective-permute-done.7.refs_1_.refs_6_ = bf16[208,1792]{1,0:T(8,128)(2,1)S(1)} collective-permute-done((bf16[208,1792]{1,0:T(8,128)(2,1)S(1)}, bf16[208,1792]{1,0:T(8,128)(2,1)S(1)}, u32[]{:S(2)}, u32[]{:S(2)}) %collective-permute-start.7) | collective-permute-done | bytes 745504 | tf_op jit(solution)/shard_map/ppermute | solution.py:90
  59.2 0.5 collective-permute-done.6.refs_0_.refs_5_
  59.8 1.2 %collective-permute-done.8.refs_2_.refs_7_ = bf16[240,1792]{1,0:T(8,128)(2,1)S(1)} collective-permute-done((bf16[240,1792]{1,0:T(8,128)(2,1)S(1)}, bf16[240,1792]{1,0:T(8,128)(2,1)S(1)}, u32[]{:S(2)}, u32[]{:S(2)}) %collective-permute-start.8) | collective-permute-done | bytes 860192 | tf_op jit(solution)/shard_map/ppermute | solution.py:90
  61.0 0.1 collect_fourth.1
  61.1 2.0 %collective-permute-start.11 = (bf16[128,1792]{1,0:T(8,128)(2,1)S(1)}, bf16[128,1792]{1,0:T(8,128)(2,1)S(1)}, u32[]{:S(2)}, u32[]{:S(2)}) collective-permute-start(bf16[128,1792]{1,0:T(8,128)(2,1)S(1)} %get-tuple-element.107), channel_id=1, source_target_pairs={{0,8},{1,9},{2,10},{3,11},{4,12},{5,13},{6,14},{7,15},{8,24},{9,25... | collective-permute-start | bytes 1376264 | tf_op jit(solution)/shard_map/ppermute | solution.py:90
  63.1 0.8 collective-permute-start.10
  63.9 0.8 collective-permute-start.9
  64.7 1.2 %collective-permute-start.16 = (bf16[112,1792]{1,0:T(8,128)(2,1)S(1)}, bf16[112,1792]{1,0:T(8,128)(2,1)S(1)}, u32[]{:S(2)}, u32[]{:S(2)}) collective-permute-start(bf16[112,1792]{1,0:T(8,128)(2,1)S(1)} %get-tuple-element.122), channel_id=1, source_target_pairs={{0,2},{1,3},{2,0},{3,1},{4,6},{5,7},{6,4},{7,5},{8,10},{9,11},{10,... | collective-permute-start | bytes 1204232 | tf_op jit(solution)/shard_map/ppermute | solution.py:90
  65.9 1.3 %collective-permute-start.17 = (bf16[96,1792]{1,0:T(8,128)(2,1)S(1)}, bf16[96,1792]{1,0:T(8,128)(2,1)S(1)}, u32[]{:S(2)}, u32[]{:S(2)}) collective-permute-start(bf16[96,1792]{1,0:T(8,128)(2,1)S(1)} %get-tuple-element.123), channel_id=1, source_target_pairs={{0,4},{1,5},{2,6},{3,7},{4,0},{5,1},{6,2},{7,3},{8,12},{9,13},{10,... | collective-permute-start | bytes 1032200 | tf_op jit(solution)/shard_map/ppermute | solution.py:90
  67.2 3.2 %accumulate_second.1 = (f32[256,1792]{1,0:T(8,128)S(1)}, f32[256,1792]{1,0:T(8,128)S(1)}) custom-call(bf16[168,1792]{1,0:T(8,128)(2,1)S(1)} %copy-done, bf16[168,1792]{1,0:T(8,128)(2,1)S(1)} %collective-permute-done.refs_1_, bf16[168,1792]{1,0:T(8,128)(2,1)S(1)} %collective-permute-done.1.refs_2_, bf16[144,1792]{1,0:T(8,128)(2,1)S(1)} %collective-permute-done.2.refs_3_, ...), custom_call_target="tpu_custom_call" | custom-call | flops 1000 | bytes 1000 | tf_op jit(solution)/shard_map/accumulate_second/pallas_call | solution.py:124
  70.4 3.9 %accumulate_third.1 = (f32[256,1792]{1,0:T(8,128)S(1)}, f32[256,1792]{1,0:T(8,128)S(1)}) custom-call(bf16[168,1792]{1,0:T(8,128)(2,1)S(1)} %copy-done, bf16[168,1792]{1,0:T(8,128)(2,1)S(1)} %collective-permute-done.refs_1_, bf16[168,1792]{1,0:T(8,128)(2,1)S(1)} %collective-permute-done.1.refs_2_, ...), custom_call_target="tpu_custom_call", output_to_operand_aliasing={{0}: (10, {}), {1}: (11, {})} | custom-call | flops 1000 | bytes 1000 | tf_op jit(solution)/shard_map/accumulate_third/pallas_call | solution.py:124
  74.4 0.8 collective-permute-start.14
  75.2 3.4 %collective-permute-start.15 = (bf16[56,1792]{1,0:T(8,128)(2,1)S(1)}, bf16[56,1792]{1,0:T(8,128)(2,1)S(1)}, u32[]{:S(2)}, u32[]{:S(2)}) collective-permute-start(bf16[56,1792]{1,0:T(8,128)(2,1)S(1)} %get-tuple-element.118), channel_id=1, source_target_pairs={{0,8},{1,9},{2,10},{3,11},{4,12},{5,13},{6,14},{7,15},{8,24},{9,25... | collective-permute-start | bytes 602120 | tf_op jit(solution)/shard_map/ppermute | solution.py:90
  78.7 1.4 %collective-permute-start.13 = (bf16[48,1792]{1,0:T(8,128)(2,1)S(1)}, bf16[48,1792]{1,0:T(8,128)(2,1)S(1)}, u32[]{:S(2)}, u32[]{:S(2)}) collective-permute-start(bf16[48,1792]{1,0:T(8,128)(2,1)S(1)} %get-tuple-element.116), channel_id=1, source_target_pairs={{0,2},{1,3},{2,0},{3,1},{4,6},{5,7},{6,4},{7,5},{8,10},{9,11},{10,... | collective-permute-start | bytes 516104 | tf_op jit(solution)/shard_map/ppermute | solution.py:90
  80.0 0.0 collective-permute-done.16.refs_1_
  80.0 2.0 %accumulate_fourth.1 = (f32[256,1792]{1,0:T(8,128)S(1)}, f32[256,1792]{1,0:T(8,128)S(1)}) custom-call(bf16[96,1792]{1,0:T(8,128)(2,1)S(1)} %collective-permute-done.9.refs_0_, bf16[112,1792]{1,0:T(8,128)(2,1)S(1)} %collective-permute-done.16.refs_1_, ...), custom_call_target="tpu_custom_call", output_to_operand_aliasing={{0}: (7, {}), {1}: (8, {})} | custom-call | flops 1000 | bytes 1000 | tf_op jit(solution)/shard_map/accumulate_fourth/pallas_call | solution.py:124
  82.1 2.0 %collective-permute-done.13.refs_0_ = bf16[48,1792]{1,0:T(8,128)(2,1)S(1)} collective-permute-done((bf16[48,1792]{1,0:T(8,128)(2,1)S(1)}, bf16[48,1792]{1,0:T(8,128)(2,1)S(1)}, u32[]{:S(2)}, u32[]{:S(2)}) %collective-permute-start.13) | collective-permute-done | bytes 172064 | tf_op jit(solution)/shard_map/ppermute | solution.py:90
  84.1 1.0 %finish_other.1 = bf16[256,1792]{1,0:T(8,128)(2,1)S(1)} custom-call(bf16[48,1792]{1,0:T(8,128)(2,1)S(1)} %collective-permute-done.13.refs_0_, bf16[64,1792]{1,0:T(8,128)(2,1)S(1)} %collective-permute-done.14.refs_1_, bf16[56,1792]{1,0:T(8,128)(2,1)S(1)} %collective-permute-done.15.refs_2_, ...), custom_call_target="tpu_custom_call" | custom-call | flops 1000 | bytes 1000 | tf_op jit(solution)/shard_map/finish_other/pallas_call | solution.py:124
  85.1 0.1 collective-permute-start.18
  85.2 1.3 %finish_own.1.kept_ref = f32[256,1792]{1,0:T(8,128)S(1)} custom-call(bf16[48,1792]{1,0:T(8,128)(2,1)S(1)} %collective-permute-done.13.refs_0_, bf16[64,1792]{1,0:T(8,128)(2,1)S(1)} %collective-permute-done.14.refs_1_, bf16[56,1792]{1,0:T(8,128)(2,1)S(1)} %collective-permute-done.15.refs_2_, ...), custom_call_target="tpu_custom_call", output_to_operand_aliasing={{}: (4, {})} | custom-call | flops 1000 | bytes 1000 | tf_op jit(solution)/shard_map/finish_own/pallas_call | solution.py:124
  86.5 1.1 %collective-permute-done.18.given_ref = bf16[256,1792]{1,0:T(8,128)(2,1)S(1)} collective-permute-done((bf16[256,1792]{1,0:T(8,128)(2,1)S(1)}, bf16[256,1792]{1,0:T(8,128)(2,1)S(1)}, u32[]{:S(2)}, u32[]{:S(2)}) %collective-permute-start.18) | collective-permute-done | bytes 917536 | tf_op jit(solution)/shard_map/ppermute | solution.py:90
  87.6 1.2 %final.1 = bf16[256,1792]{1,0:T(8,128)(2,1)} custom-call(s32[1]{0:T(128)S(6)} %copy.27.count_ref, f32[256,1792]{1,0:T(8,128)S(1)} %finish_own.1.kept_ref, bf16[256,1792]{1,0:T(8,128)(2,1)S(1)} %collective-permute-done.18.given_ref), custom_call_target="tpu_custom_call" | custom-call | flops 1000 | bytes 1000 | tf_op jit(solution)/shard_map/final/pallas_call | solution.py:124
  (27 shorter events, 0.1 us)
Async XLA Ops:
  2.8 18.6 %collective-permute-start = (bf16[168,1792]{1,0:T(8,128)(2,1)}, bf16[168,1792]{1,0:T(8,128)(2,1)S(1)}, u32[]{:S(2)}, u32[]{:S(2)}) collective-permute-start(bf16[168,1792]{1,0:T(8,128)(2,1)} %get-tuple-element.70.refs_0_), channel_id=1, source_target_pairs={{0,2},{1,3},{2,0},{3,1},{4,6},{5,7},{6,4},{7,5},{8,10},{9,11},{10,... | collective-permute-start | bytes 1806344 | tf_op jit(solution)/shard_map/ppermute | solution.py:90
  5.8 15.6 %collective-permute-start.1 = (bf16[168,1792]{1,0:T(8,128)(2,1)}, bf16[168,1792]{1,0:T(8,128)(2,1)S(1)}, u32[]{:S(2)}, u32[]{:S(2)}) collective-permute-start(bf16[168,1792]{1,0:T(8,128)(2,1)} %get-tuple-element.70.refs_0_), channel_id=1, source_target_pairs={{0,4},{1,5},{2,6},{3,7},{4,0},{5,1},{6,2},{7,3},{8,12},{9,13},{10,... | collective-permute-start | bytes 1806344 | tf_op jit(solution)/shard_map/ppermute | solution.py:90
  7.4 14.0 %collective-permute-start.2 = (bf16[144,1792]{1,0:T(8,128)(2,1)}, bf16[144,1792]{1,0:T(8,128)(2,1)S(1)}, u32[]{:S(2)}, u32[]{:S(2)}) collective-permute-start(bf16[144,1792]{1,0:T(8,128)(2,1)} %get-tuple-element.71), channel_id=1, source_target_pairs={{0,8},{1,9},{2,10},{3,11},{4,12},{5,13},{6,14},{7,15},{8,24},{9,25... | collective-permute-start | bytes 1548296 | tf_op jit(solution)/shard_map/ppermute | solution.py:90
  9.7 1.2 %copy-start.1 = (bf16[1,256,1792]{2,1,0:T(8,128)(2,1)S(1)}, bf16[1,256,1792]{2,1,0:T(8,128)(2,1)}, u32[]{:S(2)}) copy-start(bf16[1,256,1792]{2,1,0:T(8,128)(2,1)} %param.13) | copy-start | bytes 2752516
  10.8 1.9 %copy-start.3 = (bf16[1792,896]{1,0:T(8,128)(2,1)S(1)}, bf16[1792,896]{1,0:T(8,128)(2,1)}, u32[]{:S(2)}) copy-start(bf16[1792,896]{1,0:T(8,128)(2,1)} %value_ref.1) | copy-start | bytes 9633796
  12.7 1.0 %copy-start.5 = (bf16[1792,128]{1,0:T(8,128)(2,1)S(1)}, bf16[1792,128]{1,0:T(8,128)(2,1)}, u32[]{:S(2)}) copy-start(bf16[1792,128]{1,0:T(8,128)(2,1)} %query_ref.1) | copy-start | bytes 1376260
  13.8 1.0 %copy-start.6 = (bf16[1792,128]{1,0:T(8,128)(2,1)S(1)}, bf16[1792,128]{1,0:T(8,128)(2,1)}, u32[]{:S(2)}) copy-start(bf16[1792,128]{1,0:T(8,128)(2,1)} %key_ref.1) | copy-start | bytes 1376260
  14.8 0.7 copy-start.7
  15.5 5.9 %copy-start = (bf16[168,1792]{1,0:T(8,128)(2,1)S(1)}, bf16[168,1792]{1,0:T(8,128)(2,1)}, u32[]{:S(2)}) copy-start(bf16[168,1792]{1,0:T(8,128)(2,1)} %get-tuple-element.70.refs_0_) | copy-start | bytes 1806340
  15.5 13.8 %copy-start.4 = (bf16[896,1792]{1,0:T(8,128)(2,1)S(1)}, bf16[896,1792]{1,0:T(8,128)(2,1)}, u32[]{:S(2)}) copy-start(bf16[896,1792]{1,0:T(8,128)(2,1)} %out_ref.1) | copy-start | bytes 9633796
  19.3 6.4 %copy-start.9 = (f32[1792]{0:T(1024)S(1)}, f32[1792]{0:T(1024)}, u32[]{:S(2)}) copy-start(f32[1792]{0:T(1024)} %param.22) | copy-start | bytes 21508
  19.3 6.4 %copy-start.8 = (f32[1,256,8]{1,2,0:T(8,128)S(1)}, f32[1,256,8]{1,2,0:T(8,128)}, u32[]{:S(2)}) copy-start(f32[1,256,8]{1,2,0:T(8,128)} %param.15) | copy-start | bytes 24580
  19.3 10.1 %copy-start.2 = (bf16[1,256,1792]{2,1,0:T(8,128)(2,1)S(1)}, bf16[1,256,1792]{2,1,0:T(8,128)(2,1)}, u32[]{:S(2)}) copy-start(bf16[1,256,1792]{2,1,0:T(8,128)(2,1)} %param.13) | copy-start | bytes 2752516
  21.6 20.1 %collective-permute-start.4 = (bf16[232,1792]{1,0:T(8,128)(2,1)S(1)}, bf16[232,1792]{1,0:T(8,128)(2,1)S(1)}, u32[]{:S(2)}, u32[]{:S(2)}) collective-permute-start(bf16[232,1792]{1,0:T(8,128)(2,1)S(1)} %get-tuple-element.82), channel_id=1, source_target_pairs={{0,4},{1,5},{2,6},{3,7},{4,0},{5,1},{6,2},{7,3},{8,12},{9,13},{10,... | collective-permute-start | bytes 2494472 | tf_op jit(solution)/shard_map/ppermute | solution.py:90
  22.9 18.8 %collective-permute-start.3 = (bf16[224,1792]{1,0:T(8,128)(2,1)S(1)}, bf16[224,1792]{1,0:T(8,128)(2,1)S(1)}, u32[]{:S(2)}, u32[]{:S(2)}) collective-permute-start(bf16[224,1792]{1,0:T(8,128)(2,1)S(1)} %get-tuple-element.81), channel_id=1, source_target_pairs={{0,2},{1,3},{2,0},{3,1},{4,6},{5,7},{6,4},{7,5},{8,10},{9,11},{10,... | collective-permute-start | bytes 2408456 | tf_op jit(solution)/shard_map/ppermute | solution.py:90
  23.4 18.2 %collective-permute-start.5 = (bf16[216,1792]{1,0:T(8,128)(2,1)S(1)}, bf16[216,1792]{1,0:T(8,128)(2,1)S(1)}, u32[]{:S(2)}, u32[]{:S(2)}) collective-permute-start(bf16[216,1792]{1,0:T(8,128)(2,1)S(1)} %get-tuple-element.83), channel_id=1, source_target_pairs={{0,8},{1,9},{2,10},{3,11},{4,12},{5,13},{6,14},{7,15},{8,24},{9,25... | collective-permute-start | bytes 2322440 | tf_op jit(solution)/shard_map/ppermute | solution.py:90
  41.8 19.2 %collective-permute-start.8 = (bf16[240,1792]{1,0:T(8,128)(2,1)S(1)}, bf16[240,1792]{1,0:T(8,128)(2,1)S(1)}, u32[]{:S(2)}, u32[]{:S(2)}) collective-permute-start(bf16[240,1792]{1,0:T(8,128)(2,1)S(1)} %get-tuple-element.101), channel_id=1, source_target_pairs={{0,8},{1,9},{2,10},{3,11},{4,12},{5,13},{6,14},{7,15},{8,24},{9,25... | collective-permute-start | bytes 2580488 | tf_op jit(solution)/shard_map/ppermute | solution.py:90
  42.8 17.0 %collective-permute-start.6 = (bf16[224,1792]{1,0:T(8,128)(2,1)S(1)}, bf16[224,1792]{1,0:T(8,128)(2,1)S(1)}, u32[]{:S(2)}, u32[]{:S(2)}) collective-permute-start(bf16[224,1792]{1,0:T(8,128)(2,1)S(1)} %get-tuple-element.99), channel_id=1, source_target_pairs={{0,2},{1,3},{2,0},{3,1},{4,6},{5,7},{6,4},{7,5},{8,10},{9,11},{10,... | collective-permute-start | bytes 2408456 | tf_op jit(solution)/shard_map/ppermute | solution.py:90
  44.1 15.2 %collective-permute-start.7 = (bf16[208,1792]{1,0:T(8,128)(2,1)S(1)}, bf16[208,1792]{1,0:T(8,128)(2,1)S(1)}, u32[]{:S(2)}, u32[]{:S(2)}) collective-permute-start(bf16[208,1792]{1,0:T(8,128)(2,1)S(1)} %get-tuple-element.100), channel_id=1, source_target_pairs={{0,4},{1,5},{2,6},{3,7},{4,0},{5,1},{6,2},{7,3},{8,12},{9,13},{10,... | collective-permute-start | bytes 2236424 | tf_op jit(solution)/shard_map/ppermute | solution.py:90
  44.6 21.3 %collective-permute-start.12 = (bf16[256,1792]{1,0:T(8,128)(2,1)S(1)}, bf16[256,1792]{1,0:T(8,128)(2,1)S(1)}, u32[]{:S(2)}, u32[]{:S(2)}) collective-permute-start(bf16[256,1792]{1,0:T(8,128)(2,1)S(1)} %get-tuple-element.108.refs_7_.refs_8_.refs_5_.refs_3_), channel_id=1, source_target_pairs={{0,1},{1,0},{2,3},{3,2},{4,5},{5,4},{6,7},{7,6},{8,9},{9,8},{10,11... | collective-permute-start | bytes 2752520 | tf_op jit(solution)/shard_map/ppermute | solution.py:90
  61.1 13.2 %collective-permute-start.11 = (bf16[128,1792]{1,0:T(8,128)(2,1)S(1)}, bf16[128,1792]{1,0:T(8,128)(2,1)S(1)}, u32[]{:S(2)}, u32[]{:S(2)}) collective-permute-start(bf16[128,1792]{1,0:T(8,128)(2,1)S(1)} %get-tuple-element.107), channel_id=1, source_target_pairs={{0,8},{1,9},{2,10},{3,11},{4,12},{5,13},{6,14},{7,15},{8,24},{9,25... | collective-permute-start | bytes 1376264 | tf_op jit(solution)/shard_map/ppermute | solution.py:90
  63.1 11.2 %collective-permute-start.10 = (bf16[96,1792]{1,0:T(8,128)(2,1)S(1)}, bf16[96,1792]{1,0:T(8,128)(2,1)S(1)}, u32[]{:S(2)}, u32[]{:S(2)}) collective-permute-start(bf16[96,1792]{1,0:T(8,128)(2,1)S(1)} %get-tuple-element.106), channel_id=1, source_target_pairs={{0,4},{1,5},{2,6},{3,7},{4,0},{5,1},{6,2},{7,3},{8,12},{9,13},{10,... | collective-permute-start | bytes 1032200 | tf_op jit(solution)/shard_map/ppermute | solution.py:90
  63.9 10.4 %collective-permute-start.9 = (bf16[96,1792]{1,0:T(8,128)(2,1)S(1)}, bf16[96,1792]{1,0:T(8,128)(2,1)S(1)}, u32[]{:S(2)}, u32[]{:S(2)}) collective-permute-start(bf16[96,1792]{1,0:T(8,128)(2,1)S(1)} %get-tuple-element.105), channel_id=1, source_target_pairs={{0,2},{1,3},{2,0},{3,1},{4,6},{5,7},{6,4},{7,5},{8,10},{9,11},{10,... | collective-permute-start | bytes 1032200 | tf_op jit(solution)/shard_map/ppermute | solution.py:90
  64.7 15.3 %collective-permute-start.16 = (bf16[112,1792]{1,0:T(8,128)(2,1)S(1)}, bf16[112,1792]{1,0:T(8,128)(2,1)S(1)}, u32[]{:S(2)}, u32[]{:S(2)}) collective-permute-start(bf16[112,1792]{1,0:T(8,128)(2,1)S(1)} %get-tuple-element.122), channel_id=1, source_target_pairs={{0,2},{1,3},{2,0},{3,1},{4,6},{5,7},{6,4},{7,5},{8,10},{9,11},{10,... | collective-permute-start | bytes 1204232 | tf_op jit(solution)/shard_map/ppermute | solution.py:90
  65.9 14.1 %collective-permute-start.17 = (bf16[96,1792]{1,0:T(8,128)(2,1)S(1)}, bf16[96,1792]{1,0:T(8,128)(2,1)S(1)}, u32[]{:S(2)}, u32[]{:S(2)}) collective-permute-start(bf16[96,1792]{1,0:T(8,128)(2,1)S(1)} %get-tuple-element.123), channel_id=1, source_target_pairs={{0,4},{1,5},{2,6},{3,7},{4,0},{5,1},{6,2},{7,3},{8,12},{9,13},{10,... | collective-permute-start | bytes 1032200 | tf_op jit(solution)/shard_map/ppermute | solution.py:90
  74.4 9.7 %collective-permute-start.14 = (bf16[64,1792]{1,0:T(8,128)(2,1)S(1)}, bf16[64,1792]{1,0:T(8,128)(2,1)S(1)}, u32[]{:S(2)}, u32[]{:S(2)}) collective-permute-start(bf16[64,1792]{1,0:T(8,128)(2,1)S(1)} %get-tuple-element.117), channel_id=1, source_target_pairs={{0,4},{1,5},{2,6},{3,7},{4,0},{5,1},{6,2},{7,3},{8,12},{9,13},{10,... | collective-permute-start | bytes 688136 | tf_op jit(solution)/shard_map/ppermute | solution.py:90
  75.2 8.8 %collective-permute-start.15 = (bf16[56,1792]{1,0:T(8,128)(2,1)S(1)}, bf16[56,1792]{1,0:T(8,128)(2,1)S(1)}, u32[]{:S(2)}, u32[]{:S(2)}) collective-permute-start(bf16[56,1792]{1,0:T(8,128)(2,1)S(1)} %get-tuple-element.118), channel_id=1, source_target_pairs={{0,8},{1,9},{2,10},{3,11},{4,12},{5,13},{6,14},{7,15},{8,24},{9,25... | collective-permute-start | bytes 602120 | tf_op jit(solution)/shard_map/ppermute | solution.py:90
  78.7 5.4 %collective-permute-start.13 = (bf16[48,1792]{1,0:T(8,128)(2,1)S(1)}, bf16[48,1792]{1,0:T(8,128)(2,1)S(1)}, u32[]{:S(2)}, u32[]{:S(2)}) collective-permute-start(bf16[48,1792]{1,0:T(8,128)(2,1)S(1)} %get-tuple-element.116), channel_id=1, source_target_pairs={{0,2},{1,3},{2,0},{3,1},{4,6},{5,7},{6,4},{7,5},{8,10},{9,11},{10,... | collective-permute-start | bytes 516104 | tf_op jit(solution)/shard_map/ppermute | solution.py:90
  85.1 2.5 %collective-permute-start.18 = (bf16[256,1792]{1,0:T(8,128)(2,1)S(1)}, bf16[256,1792]{1,0:T(8,128)(2,1)S(1)}, u32[]{:S(2)}, u32[]{:S(2)}) collective-permute-start(bf16[256,1792]{1,0:T(8,128)(2,1)S(1)} %finish_other.1), channel_id=1, source_target_pairs={{0,1},{1,0},{2,3},{3,2},{4,5},{5,4},{6,7},{7,6},{8,9},{9,8},{10,11... | collective-permute-start | bytes 2752520 | tf_op jit(solution)/shard_map/ppermute | solution.py:90

commit v13 on v12

--- a/solution.py
+++ b/solution.py
@@ -565,21 +565,24 @@
     else:
         end_norm = end_norm.T
     mixed_rows, mlp_in = mix(numerator, denominator, rows_in, out_weight, mlp_gain, value_len)
-    near1, far1, deep1, mixed_rows, mlp_in, end_state, end_norm = together(
-        near1, far1, deep1, mixed_rows, mlp_in, end_state, end_norm
-    )
-
-    sends = collect(
-        (near1, far1, deep1),
+    middle = local_len // 2
+    other_top, other_end = flip_core(mlp_in[:middle]), flip_core(mlp_in[middle:])
+    near1, far1, deep1, mixed_rows, mlp_in, other_top, other_end, end_state, end_norm = together(
+        near1, far1, deep1, mixed_rows, mlp_in, other_top, other_end, end_state, end_norm
+    )
+
+    *sends, other_in = collect(
+        (near1, far1, deep1, other_top, other_end),
         (
             ((2, 0, wide), (1, 0, cut)),
             ((2, 0, wide), (0, cut, wide)),
             ((2, 0, wide + 3 * narrow), (1, wide + wide - cut, wide + full - cut)),
+            ((3, 0, middle), (4, 0, local_len - middle)),
         ),
         "collect_third",
     )
     near2, far2, deep2 = slot(*zip((flip_near, flip_far, next_plane), sends))
-    rows = (mlp_in, flip_core(mlp_in))
+    rows = (mlp_in, other_in)
     acc = accumulate(
         rows,
         (shard, near, far, deep, near1, far1, deep1),
@@ -588,7 +591,7 @@
         jnp.float32,
         "accumulate_second",
     )
-    near2, far2, deep2 = together(near2, far2, deep2)
+    near2, far2, deep2, *acc = together(near2, far2, deep2, *acc)
 
     held = 2 * main // 3
     two = 2 * main
@@ -632,23 +635,16 @@
     )
     near4, far4, deep4 = slot(*zip((flip_near, flip_far, next_plane), sends))
     line = 4 * narrow
-    acc = accumulate(
-        rows,
-        (near3, near3_more, far3, far3_more, deep3),
-        [((1, 0, main), (0, 0, main), (0, main, two)), ((2, 0, main), (3, 0, main), (2, main, two))]
-        + [((1, main, main + held), (3, main, main + held), (4, line, line + held))]
-        + [((1, main + held, two), (3, main + held, two), (1, two, two + main - held))]
-        + [runs(4, k * narrow, edge) for k in range(4)],
-        tuple(acc),
-        jnp.float32,
-        "accumulate_fourth",
-    )
-    weights = (near4, far4, deep4)
+    weights = (near3, near3_more, far3, far3_more, deep3, near4, far4, deep4)
     last = [
-        ((0, 0, held), (1, 0, held), (2, narrow, narrow + held)),
-        ((0, held, main), (1, held, main), (1, main, two - held)),
-        runs(2, 0, edge),
+        ((1, 0, main), (0, 0, main), (0, main, two)),
+        ((2, 0, main), (3, 0, main), (2, main, two)),
+        ((1, main, main + held), (3, main, main + held), (4, line, line + held)),
+        ((1, main + held, two), (3, main + held, two), (1, two, two + main - held)),
+        ((5, 0, held), (6, 0, held), (7, narrow, narrow + held)),
+        ((5, held, main), (6, held, main), (6, main, two - held)),
     ]
+    last += [runs(4, k * narrow, edge) for k in range(4)] + [runs(7, 0, edge)]
     (given,) = accumulate(rows[1:], weights, last, acc[1:], jnp.bfloat16, "finish_other")
     (kept,) = accumulate(
         rows[:1], weights, last, acc[:1], jnp.float32, "finish_own", residual=mixed_rows

time: 89.2 us -> 90 us (level)
  waiting for transfers between devices: 31.4 us -> 33.4 us
  Pallas kernels: 25.4 us -> 23.5 us
    ppermute x19 -> x20, waiting for transfers between devices: 31.4 us -> 33.4 us  [permute(): return lax.ppermute(array, 'req', [(i, target(i)) for i in range(count)])]
    pallas_call x14 -> x13, Pallas kernels: 25.4 us -> 23.5 us  [kernel_call(): pl.pallas_call(body, out_shape=out_shape, in_specs=specs or vmem(len(oper...]
    ppermute x19 -> x20, starting transfers between devices: 24 us -> 24.5 us  [permute(): return lax.ppermute(array, 'req', [(i, target(i)) for i in range(count)])]
  transfers between devices with their start and end apart: 19 -> 20, of which waited for: 7 -> 12; matrix products, arithmetic and copies ran while one was open for 1% -> 1% of each run, Pallas kernels for 23% -> 21%
where the time goes in v13:
time: 90 us; the launch traced here: 89.6 us
  waiting for transfers between devices  33.4 us (37%)
  starting transfers between devices  24.5 us (27%)
  Pallas kernels  23.5 us (26%)
  local copies, waits for them, and re-layouts  6.67 us (7%)
  between operations  1.53 us (2%)
    ppermute x20, waiting for transfers between devices, permute(): return lax.ppermute(array, 'req', [(i, target(i)) for i in range(count)])  33.4 us
    ppermute x20, starting transfers between devices, permute(): return lax.ppermute(array, 'req', [(i, target(i)) for i in range(count)])  24.5 us
    pallas_call x13, Pallas kernels, kernel_call(): pl.pallas_call(body, out_shape=out_shape, in_specs=specs or vmem(len(oper...  23.5 us
    unnamed x20, local copies, waits for them, and re-layouts  5.89 us
  transfers between devices with their start and end apart: 20, of which 12 were waited for; matrix products, arithmetic and copies ran while one was open for 1% of the time, Pallas kernels for 21%

profile of v13, /device:TPU:0, one launch (start us, length us, event | category | flops | bytes accessed | tf_op | source)
XLA Modules:
  0.0 89.6 jit_solution(10254545042234086202)
XLA Ops:
  0.6 2.2 %shard.1 = (bf16[168,1792]{1,0:T(8,128)(2,1)}, bf16[144,1792]{1,0:T(8,128)(2,1)}) custom-call(bf16[56,1792]{1,0:T(8,128)(2,1)} %bitcast.17, bf16[56,1792]{1,0:T(8,128)(2,1)} %bitcast.18, bf16[56,1792]{1,0:T(8,128)(2,1)} %bitcast.19), custom_call_target="tpu_custom_call" | custom-call | flops 1000 | bytes 1000 | tf_op jit(solution)/shard_map/shard/pallas_call | solution.py:124
  2.8 3.0 %collective-permute-start = (bf16[168,1792]{1,0:T(8,128)(2,1)}, bf16[168,1792]{1,0:T(8,128)(2,1)S(1)}, u32[]{:S(2)}, u32[]{:S(2)}) collective-permute-start(bf16[168,1792]{1,0:T(8,128)(2,1)} %get-tuple-element.79.refs_0_), channel_id=1, source_target_pairs={{0,2},{1,3},{2,0},{3,1},{4,6},{5,7},{6,4},{7,5},{8,10},{9,11},{10,... | collective-permute-start | bytes 1806344 | tf_op jit(solution)/shard_map/ppermute | solution.py:90
  5.8 1.5 %collective-permute-start.1 = (bf16[168,1792]{1,0:T(8,128)(2,1)}, bf16[168,1792]{1,0:T(8,128)(2,1)S(1)}, u32[]{:S(2)}, u32[]{:S(2)}) collective-permute-start(bf16[168,1792]{1,0:T(8,128)(2,1)} %get-tuple-element.79.refs_0_), channel_id=1, source_target_pairs={{0,4},{1,5},{2,6},{3,7},{4,0},{5,1},{6,2},{7,3},{8,12},{9,13},{10,... | collective-permute-start | bytes 1806344 | tf_op jit(solution)/shard_map/ppermute | solution.py:90
  7.4 1.6 %collective-permute-start.2 = (bf16[144,1792]{1,0:T(8,128)(2,1)}, bf16[144,1792]{1,0:T(8,128)(2,1)S(1)}, u32[]{:S(2)}, u32[]{:S(2)}) collective-permute-start(bf16[144,1792]{1,0:T(8,128)(2,1)} %get-tuple-element.80), channel_id=1, source_target_pairs={{0,8},{1,9},{2,10},{3,11},{4,12},{5,13},{6,14},{7,15},{8,24},{9,25... | collective-permute-start | bytes 1548296 | tf_op jit(solution)/shard_map/ppermute | solution.py:90
  8.9 0.7 broadcast_in_dim.16.gain_ref
  9.7 1.2 %copy-done.1 = bf16[1,256,1792]{2,1,0:T(8,128)(2,1)S(1)} copy-done((bf16[1,256,1792]{2,1,0:T(8,128)(2,1)S(1)}, bf16[1,256,1792]{2,1,0:T(8,128)(2,1)}, u32[]{:S(2)}) %copy-start.1) | copy-done | bytes 917528
  10.8 1.9 %copy-done.3 = bf16[1792,896]{1,0:T(8,128)(2,1)S(1)} copy-done((bf16[1792,896]{1,0:T(8,128)(2,1)S(1)}, bf16[1792,896]{1,0:T(8,128)(2,1)}, u32[]{:S(2)}) %copy-start.3) | copy-done | bytes 3211288
  12.7 1.0 %copy-done.5 = bf16[1792,128]{1,0:T(8,128)(2,1)S(1)} copy-done((bf16[1792,128]{1,0:T(8,128)(2,1)S(1)}, bf16[1792,128]{1,0:T(8,128)(2,1)}, u32[]{:S(2)}) %copy-start.5) | copy-done | bytes 458776
  13.8 1.0 %copy-done.6 = bf16[1792,128]{1,0:T(8,128)(2,1)S(1)} copy-done((bf16[1792,128]{1,0:T(8,128)(2,1)S(1)}, bf16[1792,128]{1,0:T(8,128)(2,1)}, u32[]{:S(2)}) %copy-start.6) | copy-done | bytes 458776
  14.8 0.7 copy-done.7
  15.5 3.7 %project.1 = (bf16[256,128]{1,0:T(8,128)(2,1)S(1)}, bf16[256,128]{1,0:T(8,128)(2,1)S(1)}, bf16[256,896]{1,0:T(8,128)(2,1)S(1)}) custom-call(bf16[256,1792]{1,0:T(8,128)(2,1)S(1)} %bitcast.13, bf16[16,1792]{1,0:T(8,128)(2,1)S(1)} %broadcast_in_dim.15.edge_ref, f32[1,1792]{1,0:T(1,128)S(1)} %broadcast_in_dim.16.gain_ref, f32[3,1792]{1,0:T(4,128)S(1)} %copy-done.7, ...), custom_call_target="tpu_custom_call" | custom-call | flops 1000 | bytes 1000 | tf_op jit(solution)/shard_map/project/pallas_call | solution.py:124
  20.0 1.4 %collective-permute-done.2.refs_3_ = bf16[144,1792]{1,0:T(8,128)(2,1)S(1)} collective-permute-done((bf16[144,1792]{1,0:T(8,128)(2,1)}, bf16[144,1792]{1,0:T(8,128)(2,1)S(1)}, u32[]{:S(2)}, u32[]{:S(2)}) %collective-permute-start.2) | collective-permute-done | bytes 516128 | tf_op jit(solution)/shard_map/ppermute | solution.py:90
  21.4 0.2 collect_second.1
  21.6 1.3 %collective-permute-start.5 = (bf16[216,1792]{1,0:T(8,128)(2,1)S(1)}, bf16[216,1792]{1,0:T(8,128)(2,1)S(1)}, u32[]{:S(2)}, u32[]{:S(2)}) collective-permute-start(bf16[216,1792]{1,0:T(8,128)(2,1)S(1)} %get-tuple-element.92), channel_id=1, source_target_pairs={{0,8},{1,9},{2,10},{3,11},{4,12},{5,13},{6,14},{7,15},{8,24},{9,25... | collective-permute-start | bytes 2322440 | tf_op jit(solution)/shard_map/ppermute | solution.py:90
  22.9 0.5 collective-permute-start.3
  23.4 1.5 %collective-permute-start.4 = (bf16[232,1792]{1,0:T(8,128)(2,1)S(1)}, bf16[232,1792]{1,0:T(8,128)(2,1)S(1)}, u32[]{:S(2)}, u32[]{:S(2)}) collective-permute-start(bf16[232,1792]{1,0:T(8,128)(2,1)S(1)} %get-tuple-element.91), channel_id=1, source_target_pairs={{0,4},{1,5},{2,6},{3,7},{4,0},{5,1},{6,2},{7,3},{8,12},{9,13},{10,... | collective-permute-start | bytes 2494472 | tf_op jit(solution)/shard_map/ppermute | solution.py:90
  25.0 3.7 %attend.1 = (f32[256,896]{1,0:T(8,128)S(1)}, f32[256,8]{1,0:T(8,128)S(1)}, f32[273,1,896]{2,1,0:T(1,128)}, f32[8,273]{1,0:T(8,128)}) custom-call(s32[1]{0:T(128)S(6)} %copy.23.count_ref, f32[8,256]{1,0:T(8,128)S(1)} %bitcast.15, bf16[256,128]{1,0:T(8,128)(2,1)S(1)} %get-tuple-element.96.queries_ref, bf16[256,128]{1,0:T(8,128)(2,1)S(1)} %get-tuple-element.97.keys_ref, ...), custom_call_target="tpu_custom_call" | custom-call | flops 1000 | bytes 1000 | tf_op jit(solution)/shard_map/attend/pallas_call | solution.py:124
  28.7 2.6 %mix.1 = (bf16[256,1792]{1,0:T(8,128)(2,1)S(1)}, bf16[256,1792]{1,0:T(8,128)(2,1)S(1)}) custom-call(f32[256,896]{1,0:T(8,128)S(1)} %get-tuple-element.99.numer_ref, f32[256,8]{1,0:T(8,128)S(1)} %get-tuple-element.100.denom_ref, bf16[256,1792]{1,0:T(8,128)(2,1)S(1)} %bitcast.14, bf16[896,1792]{1,0:T(8,128)(2,1)S(1)} %copy-done.4, ...), custom_call_target="tpu_custom_call" | custom-call | flops 1000 | bytes 1000 | tf_op jit(solution)/shard_map/mix/pallas_call | solution.py:124
  31.3 0.1 collective-permute-start.7
  31.4 0.5 collective-permute-start.6
  31.9 8.2 %collective-permute-done.5.refs_2_.refs_6_.refs_4_ = bf16[216,1792]{1,0:T(8,128)(2,1)S(1)} collective-permute-done((bf16[216,1792]{1,0:T(8,128)(2,1)S(1)}, bf16[216,1792]{1,0:T(8,128)(2,1)S(1)}, u32[]{:S(2)}, u32[]{:S(2)}) %collective-permute-start.5) | collective-permute-done | bytes 774176 | tf_op jit(solution)/shard_map/ppermute | solution.py:90
  40.1 1.3 %collective-permute-done.3.refs_0_.refs_4_ = bf16[224,1792]{1,0:T(8,128)(2,1)S(1)} collective-permute-done((bf16[224,1792]{1,0:T(8,128)(2,1)S(1)}, bf16[224,1792]{1,0:T(8,128)(2,1)S(1)}, u32[]{:S(2)}, u32[]{:S(2)}) %collective-permute-start.3) | collective-permute-done | bytes 802848 | tf_op jit(solution)/shard_map/ppermute | solution.py:90
  41.4 0.9 collective-permute-done.4.refs_1_.refs_5_.refs_3_
  42.3 0.2 collect_third.1
  42.5 2.4 %collective-permute-start.10 = (bf16[240,1792]{1,0:T(8,128)(2,1)S(1)}, bf16[240,1792]{1,0:T(8,128)(2,1)S(1)}, u32[]{:S(2)}, u32[]{:S(2)}) collective-permute-start(bf16[240,1792]{1,0:T(8,128)(2,1)S(1)} %get-tuple-element.115), channel_id=1, source_target_pairs={{0,8},{1,9},{2,10},{3,11},{4,12},{5,13},{6,14},{7,15},{8,24},{9,25... | collective-permute-start | bytes 2580488 | tf_op jit(solution)/shard_map/ppermute | solution.py:90
  44.9 1.4 %collective-permute-start.8 = (bf16[224,1792]{1,0:T(8,128)(2,1)S(1)}, bf16[224,1792]{1,0:T(8,128)(2,1)S(1)}, u32[]{:S(2)}, u32[]{:S(2)}) collective-permute-start(bf16[224,1792]{1,0:T(8,128)(2,1)S(1)} %get-tuple-element.113), channel_id=1, source_target_pairs={{0,2},{1,3},{2,0},{3,1},{4,6},{5,7},{6,4},{7,5},{8,10},{9,11},{10,... | collective-permute-start | bytes 2408456 | tf_op jit(solution)/shard_map/ppermute | solution.py:90
  46.3 1.5 %collective-permute-start.9 = (bf16[208,1792]{1,0:T(8,128)(2,1)S(1)}, bf16[208,1792]{1,0:T(8,128)(2,1)S(1)}, u32[]{:S(2)}, u32[]{:S(2)}) collective-permute-start(bf16[208,1792]{1,0:T(8,128)(2,1)S(1)} %get-tuple-element.114), channel_id=1, source_target_pairs={{0,4},{1,5},{2,6},{3,7},{4,0},{5,1},{6,2},{7,3},{8,12},{9,13},{10,... | collective-permute-start | bytes 2236424 | tf_op jit(solution)/shard_map/ppermute | solution.py:90
  47.8 3.2 %accumulate_second.1 = (f32[256,1792]{1,0:T(8,128)S(1)}, f32[256,1792]{1,0:T(8,128)S(1)}) custom-call(bf16[168,1792]{1,0:T(8,128)(2,1)S(1)} %copy-done, bf16[168,1792]{1,0:T(8,128)(2,1)S(1)} %collective-permute-done.refs_1_, bf16[168,1792]{1,0:T(8,128)(2,1)S(1)} %collective-permute-done.1.refs_2_, bf16[144,1792]{1,0:T(8,128)(2,1)S(1)} %collective-permute-done.2.refs_3_, ...), custom_call_target="tpu_custom_call" | custom-call | flops 1000 | bytes 1000 | tf_op jit(solution)/shard_map/accumulate_second/pallas_call | solution.py:124
  51.0 10.2 %collective-permute-done.9.refs_1_.refs_6_ = bf16[208,1792]{1,0:T(8,128)(2,1)S(1)} collective-permute-done((bf16[208,1792]{1,0:T(8,128)(2,1)S(1)}, bf16[208,1792]{1,0:T(8,128)(2,1)S(1)}, u32[]{:S(2)}, u32[]{:S(2)}) %collective-permute-start.9) | collective-permute-done | bytes 745504 | tf_op jit(solution)/shard_map/ppermute | solution.py:90
  61.3 0.7 collective-permute-done.10.refs_2_.refs_7_
  62.0 0.1 collect_fourth.1
  62.1 2.0 %collective-permute-start.13 = (bf16[128,1792]{1,0:T(8,128)(2,1)S(1)}, bf16[128,1792]{1,0:T(8,128)(2,1)S(1)}, u32[]{:S(2)}, u32[]{:S(2)}) collective-permute-start(bf16[128,1792]{1,0:T(8,128)(2,1)S(1)} %get-tuple-element.128), channel_id=1, source_target_pairs={{0,8},{1,9},{2,10},{3,11},{4,12},{5,13},{6,14},{7,15},{8,24},{9,25... | collective-permute-start | bytes 1376264 | tf_op jit(solution)/shard_map/ppermute | solution.py:90
  64.1 1.3 %collective-permute-start.11 = (bf16[96,1792]{1,0:T(8,128)(2,1)S(1)}, bf16[96,1792]{1,0:T(8,128)(2,1)S(1)}, u32[]{:S(2)}, u32[]{:S(2)}) collective-permute-start(bf16[96,1792]{1,0:T(8,128)(2,1)S(1)} %get-tuple-element.126), channel_id=1, source_target_pairs={{0,2},{1,3},{2,0},{3,1},{4,6},{5,7},{6,4},{7,5},{8,10},{9,11},{10,... | collective-permute-start | bytes 1032200 | tf_op jit(solution)/shard_map/ppermute | solution.py:90
  65.4 1.7 %collective-permute-start.12 = (bf16[96,1792]{1,0:T(8,128)(2,1)S(1)}, bf16[96,1792]{1,0:T(8,128)(2,1)S(1)}, u32[]{:S(2)}, u32[]{:S(2)}) collective-permute-start(bf16[96,1792]{1,0:T(8,128)(2,1)S(1)} %get-tuple-element.127), channel_id=1, source_target_pairs={{0,4},{1,5},{2,6},{3,7},{4,0},{5,1},{6,2},{7,3},{8,12},{9,13},{10,... | collective-permute-start | bytes 1032200 | tf_op jit(solution)/shard_map/ppermute | solution.py:90
  67.1 0.6 collective-permute-start.14
  67.7 0.5 collective-permute-start.15
  68.2 3.9 %accumulate_third.1 = (f32[256,1792]{1,0:T(8,128)S(1)}, f32[256,1792]{1,0:T(8,128)S(1)}) custom-call(bf16[168,1792]{1,0:T(8,128)(2,1)S(1)} %copy-done, bf16[168,1792]{1,0:T(8,128)(2,1)S(1)} %collective-permute-done.refs_1_, bf16[168,1792]{1,0:T(8,128)(2,1)S(1)} %collective-permute-done.1.refs_2_, ...), custom_call_target="tpu_custom_call", output_to_operand_aliasing={{0}: (10, {}), {1}: (11, {})} | custom-call | flops 1000 | bytes 1000 | tf_op jit(solution)/shard_map/accumulate_third/pallas_call | solution.py:124
  72.1 2.3 %collective-permute-done.11.refs_0_ = bf16[96,1792]{1,0:T(8,128)(2,1)S(1)} collective-permute-done((bf16[96,1792]{1,0:T(8,128)(2,1)S(1)}, bf16[96,1792]{1,0:T(8,128)(2,1)S(1)}, u32[]{:S(2)}, u32[]{:S(2)}) %collective-permute-start.11) | collective-permute-done | bytes 344096 | tf_op jit(solution)/shard_map/ppermute | solution.py:90
  74.4 2.0 %collective-permute-done.12.refs_1_.refs_2_ = bf16[96,1792]{1,0:T(8,128)(2,1)S(1)} collective-permute-done((bf16[96,1792]{1,0:T(8,128)(2,1)S(1)}, bf16[96,1792]{1,0:T(8,128)(2,1)S(1)}, u32[]{:S(2)}, u32[]{:S(2)}) %collective-permute-start.12) | collective-permute-done | bytes 344096 | tf_op jit(solution)/shard_map/ppermute | solution.py:90
  76.5 1.7 %collective-permute-start.17 = (bf16[64,1792]{1,0:T(8,128)(2,1)S(1)}, bf16[64,1792]{1,0:T(8,128)(2,1)S(1)}, u32[]{:S(2)}, u32[]{:S(2)}) collective-permute-start(bf16[64,1792]{1,0:T(8,128)(2,1)S(1)} %get-tuple-element.139), channel_id=1, source_target_pairs={{0,4},{1,5},{2,6},{3,7},{4,0},{5,1},{6,2},{7,3},{8,12},{9,13},{10,... | collective-permute-start | bytes 688136 | tf_op jit(solution)/shard_map/ppermute | solution.py:90
  78.2 0.6 collective-permute-start.18
  78.8 0.7 collective-permute-start.16
  79.5 4.7 %collective-permute-done.16.refs_5_ = bf16[48,1792]{1,0:T(8,128)(2,1)S(1)} collective-permute-done((bf16[48,1792]{1,0:T(8,128)(2,1)S(1)}, bf16[48,1792]{1,0:T(8,128)(2,1)S(1)}, u32[]{:S(2)}, u32[]{:S(2)}) %collective-permute-start.16) | collective-permute-done | bytes 172064 | tf_op jit(solution)/shard_map/ppermute | solution.py:90
  84.2 0.6 collective-permute-done.18.refs_7_
  84.8 1.0 %finish_other.1 = bf16[256,1792]{1,0:T(8,128)(2,1)S(1)} custom-call(bf16[96,1792]{1,0:T(8,128)(2,1)S(1)} %collective-permute-done.11.refs_0_, bf16[112,1792]{1,0:T(8,128)(2,1)S(1)} %collective-permute-done.14.refs_1_, bf16[96,1792]{1,0:T(8,128)(2,1)S(1)} %collective-permute-done.12.refs_1_.refs_2_, bf16[96,1792]{1,0:T(8,128)(2,1)S(1)} %collective-permute-done.15.refs_3_, ...), custom_call_target="tpu_custom_call" | custom-call | flops 1000 | bytes 1000 | tf_op jit(solution)/shard_map/finish_other/pallas_call | solution.py:124
  85.9 1.4 %finish_own.1.kept_ref = f32[256,1792]{1,0:T(8,128)S(1)} custom-call(bf16[96,1792]{1,0:T(8,128)(2,1)S(1)} %collective-permute-done.11.refs_0_, bf16[112,1792]{1,0:T(8,128)(2,1)S(1)} %collective-permute-done.14.refs_1_, bf16[96,1792]{1,0:T(8,128)(2,1)S(1)} %collective-permute-done.12.refs_1_.refs_2_, ...), custom_call_target="tpu_custom_call", output_to_operand_aliasing={{}: (9, {})} | custom-call | flops 1000 | bytes 1000 | tf_op jit(solution)/shard_map/finish_own/pallas_call | solution.py:124
  87.4 1.0 %collective-permute-done.19.given_ref = bf16[256,1792]{1,0:T(8,128)(2,1)S(1)} collective-permute-done((bf16[256,1792]{1,0:T(8,128)(2,1)S(1)}, bf16[256,1792]{1,0:T(8,128)(2,1)S(1)}, u32[]{:S(2)}, u32[]{:S(2)}) %collective-permute-start.19) | collective-permute-done | bytes 917536 | tf_op jit(solution)/shard_map/ppermute | solution.py:90
  88.4 1.2 %final.1 = bf16[256,1792]{1,0:T(8,128)(2,1)} custom-call(s32[1]{0:T(128)S(6)} %copy.23.count_ref, f32[256,1792]{1,0:T(8,128)S(1)} %finish_own.1.kept_ref, bf16[256,1792]{1,0:T(8,128)(2,1)S(1)} %collective-permute-done.19.given_ref), custom_call_target="tpu_custom_call" | custom-call | flops 1000 | bytes 1000 | tf_op jit(solution)/shard_map/final/pallas_call | solution.py:124
  (29 shorter events, 0.3 us)
Async XLA Ops:
  2.8 18.6 %collective-permute-start = (bf16[168,1792]{1,0:T(8,128)(2,1)}, bf16[168,1792]{1,0:T(8,128)(2,1)S(1)}, u32[]{:S(2)}, u32[]{:S(2)}) collective-permute-start(bf16[168,1792]{1,0:T(8,128)(2,1)} %get-tuple-element.79.refs_0_), channel_id=1, source_target_pairs={{0,2},{1,3},{2,0},{3,1},{4,6},{5,7},{6,4},{7,5},{8,10},{9,11},{10,... | collective-permute-start | bytes 1806344 | tf_op jit(solution)/shard_map/ppermute | solution.py:90
  5.8 15.6 %collective-permute-start.1 = (bf16[168,1792]{1,0:T(8,128)(2,1)}, bf16[168,1792]{1,0:T(8,128)(2,1)S(1)}, u32[]{:S(2)}, u32[]{:S(2)}) collective-permute-start(bf16[168,1792]{1,0:T(8,128)(2,1)} %get-tuple-element.79.refs_0_), channel_id=1, source_target_pairs={{0,4},{1,5},{2,6},{3,7},{4,0},{5,1},{6,2},{7,3},{8,12},{9,13},{10,... | collective-permute-start | bytes 1806344 | tf_op jit(solution)/shard_map/ppermute | solution.py:90
  7.4 14.0 %collective-permute-start.2 = (bf16[144,1792]{1,0:T(8,128)(2,1)}, bf16[144,1792]{1,0:T(8,128)(2,1)S(1)}, u32[]{:S(2)}, u32[]{:S(2)}) collective-permute-start(bf16[144,1792]{1,0:T(8,128)(2,1)} %get-tuple-element.80), channel_id=1, source_target_pairs={{0,8},{1,9},{2,10},{3,11},{4,12},{5,13},{6,14},{7,15},{8,24},{9,25... | collective-permute-start | bytes 1548296 | tf_op jit(solution)/shard_map/ppermute | solution.py:90
  9.7 1.2 %copy-start.1 = (bf16[1,256,1792]{2,1,0:T(8,128)(2,1)S(1)}, bf16[1,256,1792]{2,1,0:T(8,128)(2,1)}, u32[]{:S(2)}) copy-start(bf16[1,256,1792]{2,1,0:T(8,128)(2,1)} %param.13) | copy-start | bytes 2752516
  10.8 1.9 %copy-start.3 = (bf16[1792,896]{1,0:T(8,128)(2,1)S(1)}, bf16[1792,896]{1,0:T(8,128)(2,1)}, u32[]{:S(2)}) copy-start(bf16[1792,896]{1,0:T(8,128)(2,1)} %value_ref.1) | copy-start | bytes 9633796
  12.7 1.0 %copy-start.5 = (bf16[1792,128]{1,0:T(8,128)(2,1)S(1)}, bf16[1792,128]{1,0:T(8,128)(2,1)}, u32[]{:S(2)}) copy-start(bf16[1792,128]{1,0:T(8,128)(2,1)} %query_ref.1) | copy-start | bytes 1376260
  13.8 1.0 %copy-start.6 = (bf16[1792,128]{1,0:T(8,128)(2,1)S(1)}, bf16[1792,128]{1,0:T(8,128)(2,1)}, u32[]{:S(2)}) copy-start(bf16[1792,128]{1,0:T(8,128)(2,1)} %key_ref.1) | copy-start | bytes 1376260
  14.8 0.7 copy-start.7
  15.5 4.5 %copy-start.9 = (f32[1792]{0:T(1024)S(1)}, f32[1792]{0:T(1024)}, u32[]{:S(2)}) copy-start(f32[1792]{0:T(1024)} %param.22) | copy-start | bytes 21508
  15.5 5.9 %copy-start = (bf16[168,1792]{1,0:T(8,128)(2,1)S(1)}, bf16[168,1792]{1,0:T(8,128)(2,1)}, u32[]{:S(2)}) copy-start(bf16[168,1792]{1,0:T(8,128)(2,1)} %get-tuple-element.79.refs_0_) | copy-start | bytes 1806340
  15.5 13.1 %copy-start.4 = (bf16[896,1792]{1,0:T(8,128)(2,1)S(1)}, bf16[896,1792]{1,0:T(8,128)(2,1)}, u32[]{:S(2)}) copy-start(bf16[896,1792]{1,0:T(8,128)(2,1)} %out_ref.1) | copy-start | bytes 9633796
  19.3 5.7 %copy-start.8 = (f32[1,256,8]{1,2,0:T(8,128)S(1)}, f32[1,256,8]{1,2,0:T(8,128)}, u32[]{:S(2)}) copy-start(f32[1,256,8]{1,2,0:T(8,128)} %param.15) | copy-start | bytes 24580
  19.3 9.4 %copy-start.2 = (bf16[1,256,1792]{2,1,0:T(8,128)(2,1)S(1)}, bf16[1,256,1792]{2,1,0:T(8,128)(2,1)}, u32[]{:S(2)}) copy-start(bf16[1,256,1792]{2,1,0:T(8,128)(2,1)} %param.13) | copy-start | bytes 2752516
  21.6 18.5 %collective-permute-start.5 = (bf16[216,1792]{1,0:T(8,128)(2,1)S(1)}, bf16[216,1792]{1,0:T(8,128)(2,1)S(1)}, u32[]{:S(2)}, u32[]{:S(2)}) collective-permute-start(bf16[216,1792]{1,0:T(8,128)(2,1)S(1)} %get-tuple-element.92), channel_id=1, source_target_pairs={{0,8},{1,9},{2,10},{3,11},{4,12},{5,13},{6,14},{7,15},{8,24},{9,25... | collective-permute-start | bytes 2322440 | tf_op jit(solution)/shard_map/ppermute | solution.py:90
  22.9 18.5 %collective-permute-start.3 = (bf16[224,1792]{1,0:T(8,128)(2,1)S(1)}, bf16[224,1792]{1,0:T(8,128)(2,1)S(1)}, u32[]{:S(2)}, u32[]{:S(2)}) collective-permute-start(bf16[224,1792]{1,0:T(8,128)(2,1)S(1)} %get-tuple-element.90), channel_id=1, source_target_pairs={{0,2},{1,3},{2,0},{3,1},{4,6},{5,7},{6,4},{7,5},{8,10},{9,11},{10,... | collective-permute-start | bytes 2408456 | tf_op jit(solution)/shard_map/ppermute | solution.py:90
  23.4 18.8 %collective-permute-start.4 = (bf16[232,1792]{1,0:T(8,128)(2,1)S(1)}, bf16[232,1792]{1,0:T(8,128)(2,1)S(1)}, u32[]{:S(2)}, u32[]{:S(2)}) collective-permute-start(bf16[232,1792]{1,0:T(8,128)(2,1)S(1)} %get-tuple-element.91), channel_id=1, source_target_pairs={{0,4},{1,5},{2,6},{3,7},{4,0},{5,1},{6,2},{7,3},{8,12},{9,13},{10,... | collective-permute-start | bytes 2494472 | tf_op jit(solution)/shard_map/ppermute | solution.py:90
  31.3 10.9 %collective-permute-start.7 = (bf16[128,1792]{1,0:T(8,128)(2,1)S(1)}, bf16[128,1792]{1,0:T(8,128)(2,1)S(1)}, u32[]{:S(2)}, u32[]{:S(2)}) collective-permute-start(bf16[128,1792]{1,0:T(8,128)(2,1)S(1)} %get-tuple-element.152), channel_id=1, source_target_pairs={{0,1},{1,0},{2,3},{3,2},{4,5},{5,4},{6,7},{7,6},{8,9},{9,8},{10,11... | collective-permute-start | bytes 1376264 | tf_op jit(solution)/shard_map/ppermute | solution.py:90
  31.4 10.9 %collective-permute-start.6 = (bf16[128,1792]{1,0:T(8,128)(2,1)S(1)}, bf16[128,1792]{1,0:T(8,128)(2,1)S(1)}, u32[]{:S(2)}, u32[]{:S(2)}) collective-permute-start(bf16[128,1792]{1,0:T(8,128)(2,1)S(1)} %get-tuple-element.153), channel_id=1, source_target_pairs={{0,1},{1,0},{2,3},{3,2},{4,5},{5,4},{6,7},{7,6},{8,9},{9,8},{10,11... | collective-permute-start | bytes 1376264 | tf_op jit(solution)/shard_map/ppermute | solution.py:90
  42.5 19.5 %collective-permute-start.10 = (bf16[240,1792]{1,0:T(8,128)(2,1)S(1)}, bf16[240,1792]{1,0:T(8,128)(2,1)S(1)}, u32[]{:S(2)}, u32[]{:S(2)}) collective-permute-start(bf16[240,1792]{1,0:T(8,128)(2,1)S(1)} %get-tuple-element.115), channel_id=1, source_target_pairs={{0,8},{1,9},{2,10},{3,11},{4,12},{5,13},{6,14},{7,15},{8,24},{9,25... | collective-permute-start | bytes 2580488 | tf_op jit(solution)/shard_map/ppermute | solution.py:90
  44.9 16.4 %collective-permute-start.8 = (bf16[224,1792]{1,0:T(8,128)(2,1)S(1)}, bf16[224,1792]{1,0:T(8,128)(2,1)S(1)}, u32[]{:S(2)}, u32[]{:S(2)}) collective-permute-start(bf16[224,1792]{1,0:T(8,128)(2,1)S(1)} %get-tuple-element.113), channel_id=1, source_target_pairs={{0,2},{1,3},{2,0},{3,1},{4,6},{5,7},{6,4},{7,5},{8,10},{9,11},{10,... | collective-permute-start | bytes 2408456 | tf_op jit(solution)/shard_map/ppermute | solution.py:90
  46.3 14.9 %collective-permute-start.9 = (bf16[208,1792]{1,0:T(8,128)(2,1)S(1)}, bf16[208,1792]{1,0:T(8,128)(2,1)S(1)}, u32[]{:S(2)}, u32[]{:S(2)}) collective-permute-start(bf16[208,1792]{1,0:T(8,128)(2,1)S(1)} %get-tuple-element.114), channel_id=1, source_target_pairs={{0,4},{1,5},{2,6},{3,7},{4,0},{5,1},{6,2},{7,3},{8,12},{9,13},{10,... | collective-permute-start | bytes 2236424 | tf_op jit(solution)/shard_map/ppermute | solution.py:90
  62.1 14.3 %collective-permute-start.13 = (bf16[128,1792]{1,0:T(8,128)(2,1)S(1)}, bf16[128,1792]{1,0:T(8,128)(2,1)S(1)}, u32[]{:S(2)}, u32[]{:S(2)}) collective-permute-start(bf16[128,1792]{1,0:T(8,128)(2,1)S(1)} %get-tuple-element.128), channel_id=1, source_target_pairs={{0,8},{1,9},{2,10},{3,11},{4,12},{5,13},{6,14},{7,15},{8,24},{9,25... | collective-permute-start | bytes 1376264 | tf_op jit(solution)/shard_map/ppermute | solution.py:90
  64.1 10.3 %collective-permute-start.11 = (bf16[96,1792]{1,0:T(8,128)(2,1)S(1)}, bf16[96,1792]{1,0:T(8,128)(2,1)S(1)}, u32[]{:S(2)}, u32[]{:S(2)}) collective-permute-start(bf16[96,1792]{1,0:T(8,128)(2,1)S(1)} %get-tuple-element.126), channel_id=1, source_target_pairs={{0,2},{1,3},{2,0},{3,1},{4,6},{5,7},{6,4},{7,5},{8,10},{9,11},{10,... | collective-permute-start | bytes 1032200 | tf_op jit(solution)/shard_map/ppermute | solution.py:90
  65.4 11.0 %collective-permute-start.12 = (bf16[96,1792]{1,0:T(8,128)(2,1)S(1)}, bf16[96,1792]{1,0:T(8,128)(2,1)S(1)}, u32[]{:S(2)}, u32[]{:S(2)}) collective-permute-start(bf16[96,1792]{1,0:T(8,128)(2,1)S(1)} %get-tuple-element.127), channel_id=1, source_target_pairs={{0,4},{1,5},{2,6},{3,7},{4,0},{5,1},{6,2},{7,3},{8,12},{9,13},{10,... | collective-permute-start | bytes 1032200 | tf_op jit(solution)/shard_map/ppermute | solution.py:90
  67.1 17.7 %collective-permute-start.14 = (bf16[112,1792]{1,0:T(8,128)(2,1)S(1)}, bf16[112,1792]{1,0:T(8,128)(2,1)S(1)}, u32[]{:S(2)}, u32[]{:S(2)}) collective-permute-start(bf16[112,1792]{1,0:T(8,128)(2,1)S(1)} %get-tuple-element.134), channel_id=1, source_target_pairs={{0,2},{1,3},{2,0},{3,1},{4,6},{5,7},{6,4},{7,5},{8,10},{9,11},{10,... | collective-permute-start | bytes 1204232 | tf_op jit(solution)/shard_map/ppermute | solution.py:90
  67.7 17.1 %collective-permute-start.15 = (bf16[96,1792]{1,0:T(8,128)(2,1)S(1)}, bf16[96,1792]{1,0:T(8,128)(2,1)S(1)}, u32[]{:S(2)}, u32[]{:S(2)}) collective-permute-start(bf16[96,1792]{1,0:T(8,128)(2,1)S(1)} %get-tuple-element.136), channel_id=1, source_target_pairs={{0,4},{1,5},{2,6},{3,7},{4,0},{5,1},{6,2},{7,3},{8,12},{9,13},{10,... | collective-permute-start | bytes 1032200 | tf_op jit(solution)/shard_map/ppermute | solution.py:90
  76.5 8.4 %collective-permute-start.17 = (bf16[64,1792]{1,0:T(8,128)(2,1)S(1)}, bf16[64,1792]{1,0:T(8,128)(2,1)S(1)}, u32[]{:S(2)}, u32[]{:S(2)}) collective-permute-start(bf16[64,1792]{1,0:T(8,128)(2,1)S(1)} %get-tuple-element.139), channel_id=1, source_target_pairs={{0,4},{1,5},{2,6},{3,7},{4,0},{5,1},{6,2},{7,3},{8,12},{9,13},{10,... | collective-permute-start | bytes 688136 | tf_op jit(solution)/shard_map/ppermute | solution.py:90
  78.2 6.6 %collective-permute-start.18 = (bf16[56,1792]{1,0:T(8,128)(2,1)S(1)}, bf16[56,1792]{1,0:T(8,128)(2,1)S(1)}, u32[]{:S(2)}, u32[]{:S(2)}) collective-permute-start(bf16[56,1792]{1,0:T(8,128)(2,1)S(1)} %get-tuple-element.140), channel_id=1, source_target_pairs={{0,8},{1,9},{2,10},{3,11},{4,12},{5,13},{6,14},{7,15},{8,24},{9,25... | collective-permute-start | bytes 602120 | tf_op jit(solution)/shard_map/ppermute | solution.py:90
  78.8 5.4 %collective-permute-start.16 = (bf16[48,1792]{1,0:T(8,128)(2,1)S(1)}, bf16[48,1792]{1,0:T(8,128)(2,1)S(1)}, u32[]{:S(2)}, u32[]{:S(2)}) collective-permute-start(bf16[48,1792]{1,0:T(8,128)(2,1)S(1)} %get-tuple-element.138), channel_id=1, source_target_pairs={{0,2},{1,3},{2,0},{3,1},{4,6},{5,7},{6,4},{7,5},{8,10},{9,11},{10,... | collective-permute-start | bytes 516104 | tf_op jit(solution)/shard_map/ppermute | solution.py:90
  85.9 2.5 %collective-permute-start.19 = (bf16[256,1792]{1,0:T(8,128)(2,1)S(1)}, bf16[256,1792]{1,0:T(8,128)(2,1)S(1)}, u32[]{:S(2)}, u32[]{:S(2)}) collective-permute-start(bf16[256,1792]{1,0:T(8,128)(2,1)S(1)} %finish_other.1), channel_id=1, source_target_pairs={{0,1},{1,0},{2,3},{3,2},{4,5},{5,4},{6,7},{7,6},{8,9},{9,8},{10,11... | collective-permute-start | bytes 2752520 | tf_op jit(solution)/shard_map/ppermute | solution.py:90

commit v14 on v13

--- a/solution.py
+++ b/solution.py
@@ -565,23 +565,28 @@
     else:
         end_norm = end_norm.T
     mixed_rows, mlp_in = mix(numerator, denominator, rows_in, out_weight, mlp_gain, value_len)
+    near1, far1, deep1, mixed_rows, mlp_in, end_state, end_norm = together(
+        near1, far1, deep1, mixed_rows, mlp_in, end_state, end_norm
+    )
+
     middle = local_len // 2
-    other_top, other_end = flip_core(mlp_in[:middle]), flip_core(mlp_in[middle:])
-    near1, far1, deep1, mixed_rows, mlp_in, other_top, other_end, end_state, end_norm = together(
-        near1, far1, deep1, mixed_rows, mlp_in, other_top, other_end, end_state, end_norm
-    )
-
-    *sends, other_in = collect(
-        (near1, far1, deep1, other_top, other_end),
+    *sends, top, end = collect(
+        (near1, far1, deep1, mlp_in),
         (
             ((2, 0, wide), (1, 0, cut)),
             ((2, 0, wide), (0, cut, wide)),
             ((2, 0, wide + 3 * narrow), (1, wide + wide - cut, wide + full - cut)),
-            ((3, 0, middle), (4, 0, local_len - middle)),
+            ((3, 0, middle),),
+            ((3, middle, local_len),),
         ),
         "collect_third",
     )
     near2, far2, deep2 = slot(*zip((flip_near, flip_far, next_plane), sends))
+    (other_in,) = collect(
+        (flip_core(top), flip_core(end)),
+        (((0, 0, middle), (1, 0, local_len - middle)),),
+        "collect_rows",
+    )
     rows = (mlp_in, other_in)
     acc = accumulate(
         rows,

time: 90 us -> 89 us (0.989)
  starting transfers between devices: 24.5 us -> 22.8 us
    ppermute x20, starting transfers between devices: 24.5 us -> 22.8 us  [permute(): return lax.ppermute(array, 'req', [(i, target(i)) for i in range(count)])]
    pallas_call x13 -> x14, Pallas kernels: 23.5 us -> 23.6 us  [kernel_call(): pl.pallas_call(body, out_shape=out_shape, in_specs=specs or vmem(len(oper...]
  transfers between devices with their start and end apart: 20 -> 20, of which waited for: 12 -> 11; matrix products, arithmetic and copies ran while one was open for 1% -> 1% of each run, Pallas kernels for 21% -> 21%
where the time goes in v14:
time: 89 us; the launch traced here: 88.6 us
  waiting for transfers between devices  34.2 us (38%)
  Pallas kernels  23.6 us (27%)
  starting transfers between devices  22.8 us (26%)
  local copies, waits for them, and re-layouts  6.61 us (7%)
  between operations  1.46 us (2%)
    ppermute x20, waiting for transfers between devices, permute(): return lax.ppermute(array, 'req', [(i, target(i)) for i in range(count)])  34.2 us
    pallas_call x14, Pallas kernels, kernel_call(): pl.pallas_call(body, out_shape=out_shape, in_specs=specs or vmem(len(oper...  23.6 us
    ppermute x20, starting transfers between devices, permute(): return lax.ppermute(array, 'req', [(i, target(i)) for i in range(count)])  22.8 us
    unnamed x20, local copies, waits for them, and re-layouts  5.89 us
  transfers between devices with their start and end apart: 20, of which 11 were waited for; matrix products, arithmetic and copies ran while one was open for 1% of the time, Pallas kernels for 21%

profile of v14, /device:TPU:0, one launch (start us, length us, event | category | flops | bytes accessed | tf_op | source)
XLA Modules:
  0.0 88.6 jit_solution(13340681242958836367)
XLA Ops:
  0.6 2.2 %shard.1 = (bf16[168,1792]{1,0:T(8,128)(2,1)}, bf16[144,1792]{1,0:T(8,128)(2,1)}) custom-call(bf16[56,1792]{1,0:T(8,128)(2,1)} %bitcast.17, bf16[56,1792]{1,0:T(8,128)(2,1)} %bitcast.18, bf16[56,1792]{1,0:T(8,128)(2,1)} %bitcast.19), custom_call_target="tpu_custom_call" | custom-call | flops 1000 | bytes 1000 | tf_op jit(solution)/shard_map/shard/pallas_call | solution.py:124
  2.8 3.0 %collective-permute-start = (bf16[168,1792]{1,0:T(8,128)(2,1)}, bf16[168,1792]{1,0:T(8,128)(2,1)S(1)}, u32[]{:S(2)}, u32[]{:S(2)}) collective-permute-start(bf16[168,1792]{1,0:T(8,128)(2,1)} %get-tuple-element.78.refs_0_), channel_id=1, source_target_pairs={{0,2},{1,3},{2,0},{3,1},{4,6},{5,7},{6,4},{7,5},{8,10},{9,11},{10,... | collective-permute-start | bytes 1806344 | tf_op jit(solution)/shard_map/ppermute | solution.py:90
  5.8 1.5 %collective-permute-start.1 = (bf16[168,1792]{1,0:T(8,128)(2,1)}, bf16[168,1792]{1,0:T(8,128)(2,1)S(1)}, u32[]{:S(2)}, u32[]{:S(2)}) collective-permute-start(bf16[168,1792]{1,0:T(8,128)(2,1)} %get-tuple-element.78.refs_0_), channel_id=1, source_target_pairs={{0,4},{1,5},{2,6},{3,7},{4,0},{5,1},{6,2},{7,3},{8,12},{9,13},{10,... | collective-permute-start | bytes 1806344 | tf_op jit(solution)/shard_map/ppermute | solution.py:90
  7.4 1.6 %collective-permute-start.2 = (bf16[144,1792]{1,0:T(8,128)(2,1)}, bf16[144,1792]{1,0:T(8,128)(2,1)S(1)}, u32[]{:S(2)}, u32[]{:S(2)}) collective-permute-start(bf16[144,1792]{1,0:T(8,128)(2,1)} %get-tuple-element.79), channel_id=1, source_target_pairs={{0,8},{1,9},{2,10},{3,11},{4,12},{5,13},{6,14},{7,15},{8,24},{9,25... | collective-permute-start | bytes 1548296 | tf_op jit(solution)/shard_map/ppermute | solution.py:90
  8.9 0.7 broadcast_in_dim.16.gain_ref
  9.7 1.2 %copy-done.1 = bf16[1,256,1792]{2,1,0:T(8,128)(2,1)S(1)} copy-done((bf16[1,256,1792]{2,1,0:T(8,128)(2,1)S(1)}, bf16[1,256,1792]{2,1,0:T(8,128)(2,1)}, u32[]{:S(2)}) %copy-start.1) | copy-done | bytes 917528
  10.8 1.9 %copy-done.3 = bf16[1792,896]{1,0:T(8,128)(2,1)S(1)} copy-done((bf16[1792,896]{1,0:T(8,128)(2,1)S(1)}, bf16[1792,896]{1,0:T(8,128)(2,1)}, u32[]{:S(2)}) %copy-start.3) | copy-done | bytes 3211288
  12.7 1.0 %copy-done.5 = bf16[1792,128]{1,0:T(8,128)(2,1)S(1)} copy-done((bf16[1792,128]{1,0:T(8,128)(2,1)S(1)}, bf16[1792,128]{1,0:T(8,128)(2,1)}, u32[]{:S(2)}) %copy-start.5) | copy-done | bytes 458776
  13.8 1.0 %copy-done.6 = bf16[1792,128]{1,0:T(8,128)(2,1)S(1)} copy-done((bf16[1792,128]{1,0:T(8,128)(2,1)S(1)}, bf16[1792,128]{1,0:T(8,128)(2,1)}, u32[]{:S(2)}) %copy-start.6) | copy-done | bytes 458776
  14.8 0.7 copy-done.7
  15.5 3.7 %project.1 = (bf16[256,128]{1,0:T(8,128)(2,1)S(1)}, bf16[256,128]{1,0:T(8,128)(2,1)S(1)}, bf16[256,896]{1,0:T(8,128)(2,1)S(1)}) custom-call(bf16[256,1792]{1,0:T(8,128)(2,1)S(1)} %bitcast.13, bf16[16,1792]{1,0:T(8,128)(2,1)S(1)} %broadcast_in_dim.15.edge_ref, f32[1,1792]{1,0:T(1,128)S(1)} %broadcast_in_dim.16.gain_ref, f32[3,1792]{1,0:T(4,128)S(1)} %copy-done.7, ...), custom_call_target="tpu_custom_call" | custom-call | flops 1000 | bytes 1000 | tf_op jit(solution)/shard_map/project/pallas_call | solution.py:124
  19.3 2.1 %collective-permute-done.2.refs_3_ = bf16[144,1792]{1,0:T(8,128)(2,1)S(1)} collective-permute-done((bf16[144,1792]{1,0:T(8,128)(2,1)}, bf16[144,1792]{1,0:T(8,128)(2,1)S(1)}, u32[]{:S(2)}, u32[]{:S(2)}) %collective-permute-start.2) | collective-permute-done | bytes 516128 | tf_op jit(solution)/shard_map/ppermute | solution.py:90
  21.4 0.2 collect_second.1
  21.6 1.3 %collective-permute-start.4 = (bf16[232,1792]{1,0:T(8,128)(2,1)S(1)}, bf16[232,1792]{1,0:T(8,128)(2,1)S(1)}, u32[]{:S(2)}, u32[]{:S(2)}) collective-permute-start(bf16[232,1792]{1,0:T(8,128)(2,1)S(1)} %get-tuple-element.90), channel_id=1, source_target_pairs={{0,4},{1,5},{2,6},{3,7},{4,0},{5,1},{6,2},{7,3},{8,12},{9,13},{10,... | collective-permute-start | bytes 2494472 | tf_op jit(solution)/shard_map/ppermute | solution.py:90
  22.9 0.5 collective-permute-start.3
  23.4 1.6 %collective-permute-start.5 = (bf16[216,1792]{1,0:T(8,128)(2,1)S(1)}, bf16[216,1792]{1,0:T(8,128)(2,1)S(1)}, u32[]{:S(2)}, u32[]{:S(2)}) collective-permute-start(bf16[216,1792]{1,0:T(8,128)(2,1)S(1)} %get-tuple-element.91), channel_id=1, source_target_pairs={{0,8},{1,9},{2,10},{3,11},{4,12},{5,13},{6,14},{7,15},{8,24},{9,25... | collective-permute-start | bytes 2322440 | tf_op jit(solution)/shard_map/ppermute | solution.py:90
  25.7 3.7 %attend.1 = (f32[256,896]{1,0:T(8,128)S(1)}, f32[256,8]{1,0:T(8,128)S(1)}, f32[273,1,896]{2,1,0:T(1,128)}, f32[8,273]{1,0:T(8,128)}) custom-call(s32[1]{0:T(128)S(6)} %copy.23.count_ref, f32[8,256]{1,0:T(8,128)S(1)} %bitcast.15, bf16[256,128]{1,0:T(8,128)(2,1)S(1)} %get-tuple-element.95.queries_ref, bf16[256,128]{1,0:T(8,128)(2,1)S(1)} %get-tuple-element.96.keys_ref, ...), custom_call_target="tpu_custom_call" | custom-call | flops 1000 | bytes 1000 | tf_op jit(solution)/shard_map/attend/pallas_call | solution.py:124
  29.4 2.6 %mix.1 = (bf16[256,1792]{1,0:T(8,128)(2,1)S(1)}, bf16[256,1792]{1,0:T(8,128)(2,1)S(1)}) custom-call(f32[256,896]{1,0:T(8,128)S(1)} %get-tuple-element.98.numer_ref, f32[256,8]{1,0:T(8,128)S(1)} %get-tuple-element.99.denom_ref, bf16[256,1792]{1,0:T(8,128)(2,1)S(1)} %bitcast.14, bf16[896,1792]{1,0:T(8,128)(2,1)S(1)} %copy-done.4, ...), custom_call_target="tpu_custom_call" | custom-call | flops 1000 | bytes 1000 | tf_op jit(solution)/shard_map/mix/pallas_call | solution.py:124
  32.0 9.7 %collective-permute-done.5.refs_2_.refs_6_.refs_4_ = bf16[216,1792]{1,0:T(8,128)(2,1)S(1)} collective-permute-done((bf16[216,1792]{1,0:T(8,128)(2,1)S(1)}, bf16[216,1792]{1,0:T(8,128)(2,1)S(1)}, u32[]{:S(2)}, u32[]{:S(2)}) %collective-permute-start.5) | collective-permute-done | bytes 774176 | tf_op jit(solution)/shard_map/ppermute | solution.py:90
  41.6 0.2 collect_third.1
  41.9 1.0 %collective-permute-start.8 = (bf16[240,1792]{1,0:T(8,128)(2,1)S(1)}, bf16[240,1792]{1,0:T(8,128)(2,1)S(1)}, u32[]{:S(2)}, u32[]{:S(2)}) collective-permute-start(bf16[240,1792]{1,0:T(8,128)(2,1)S(1)} %get-tuple-element.113), channel_id=1, source_target_pairs={{0,8},{1,9},{2,10},{3,11},{4,12},{5,13},{6,14},{7,15},{8,24},{9,25... | collective-permute-start | bytes 2580488 | tf_op jit(solution)/shard_map/ppermute | solution.py:90
  42.9 1.2 %collective-permute-start.6 = (bf16[224,1792]{1,0:T(8,128)(2,1)S(1)}, bf16[224,1792]{1,0:T(8,128)(2,1)S(1)}, u32[]{:S(2)}, u32[]{:S(2)}) collective-permute-start(bf16[224,1792]{1,0:T(8,128)(2,1)S(1)} %get-tuple-element.111), channel_id=1, source_target_pairs={{0,2},{1,3},{2,0},{3,1},{4,6},{5,7},{6,4},{7,5},{8,10},{9,11},{10,... | collective-permute-start | bytes 2408456 | tf_op jit(solution)/shard_map/ppermute | solution.py:90
  44.1 0.5 collective-permute-start.7
  44.6 0.5 collective-permute-start.10
  45.1 1.3 %collective-permute-done.9.refs_0_ = bf16[128,1792]{1,0:T(8,128)(2,1)S(1)} collective-permute-done((bf16[128,1792]{1,0:T(8,128)(2,1)S(1)}, bf16[128,1792]{1,0:T(8,128)(2,1)S(1)}, u32[]{:S(2)}, u32[]{:S(2)}) %collective-permute-start.9) | collective-permute-done | bytes 458784 | tf_op jit(solution)/shard_map/ppermute | solution.py:90
  46.5 0.7 collective-permute-done.10.refs_1_
  47.2 3.2 %accumulate_second.1 = (f32[256,1792]{1,0:T(8,128)S(1)}, f32[256,1792]{1,0:T(8,128)S(1)}) custom-call(bf16[168,1792]{1,0:T(8,128)(2,1)S(1)} %copy-done, bf16[168,1792]{1,0:T(8,128)(2,1)S(1)} %collective-permute-done.refs_1_, bf16[168,1792]{1,0:T(8,128)(2,1)S(1)} %collective-permute-done.1.refs_2_, bf16[144,1792]{1,0:T(8,128)(2,1)S(1)} %collective-permute-done.2.refs_3_, ...), custom_call_target="tpu_custom_call" | custom-call | flops 1000 | bytes 1000 | tf_op jit(solution)/shard_map/accumulate_second/pallas_call | solution.py:124
  50.4 8.9 %collective-permute-done.7.refs_1_.refs_6_ = bf16[208,1792]{1,0:T(8,128)(2,1)S(1)} collective-permute-done((bf16[208,1792]{1,0:T(8,128)(2,1)S(1)}, bf16[208,1792]{1,0:T(8,128)(2,1)S(1)}, u32[]{:S(2)}, u32[]{:S(2)}) %collective-permute-start.7) | collective-permute-done | bytes 745504 | tf_op jit(solution)/shard_map/ppermute | solution.py:90
  59.3 0.5 collective-permute-done.6.refs_0_.refs_5_
  59.8 1.2 %collective-permute-done.8.refs_2_.refs_7_ = bf16[240,1792]{1,0:T(8,128)(2,1)S(1)} collective-permute-done((bf16[240,1792]{1,0:T(8,128)(2,1)S(1)}, bf16[240,1792]{1,0:T(8,128)(2,1)S(1)}, u32[]{:S(2)}, u32[]{:S(2)}) %collective-permute-start.8) | collective-permute-done | bytes 860192 | tf_op jit(solution)/shard_map/ppermute | solution.py:90
  61.1 0.1 collect_fourth.1
  61.2 2.0 %collective-permute-start.13 = (bf16[128,1792]{1,0:T(8,128)(2,1)S(1)}, bf16[128,1792]{1,0:T(8,128)(2,1)S(1)}, u32[]{:S(2)}, u32[]{:S(2)}) collective-permute-start(bf16[128,1792]{1,0:T(8,128)(2,1)S(1)} %get-tuple-element.126), channel_id=1, source_target_pairs={{0,8},{1,9},{2,10},{3,11},{4,12},{5,13},{6,14},{7,15},{8,24},{9,25... | collective-permute-start | bytes 1376264 | tf_op jit(solution)/shard_map/ppermute | solution.py:90
  63.2 1.4 %collective-permute-start.11 = (bf16[96,1792]{1,0:T(8,128)(2,1)S(1)}, bf16[96,1792]{1,0:T(8,128)(2,1)S(1)}, u32[]{:S(2)}, u32[]{:S(2)}) collective-permute-start(bf16[96,1792]{1,0:T(8,128)(2,1)S(1)} %get-tuple-element.124), channel_id=1, source_target_pairs={{0,2},{1,3},{2,0},{3,1},{4,6},{5,7},{6,4},{7,5},{8,10},{9,11},{10,... | collective-permute-start | bytes 1032200 | tf_op jit(solution)/shard_map/ppermute | solution.py:90
  64.5 0.2 collective-permute-start.12
  64.8 1.2 %collective-permute-start.14 = (bf16[112,1792]{1,0:T(8,128)(2,1)S(1)}, bf16[112,1792]{1,0:T(8,128)(2,1)S(1)}, u32[]{:S(2)}, u32[]{:S(2)}) collective-permute-start(bf16[112,1792]{1,0:T(8,128)(2,1)S(1)} %get-tuple-element.132), channel_id=1, source_target_pairs={{0,2},{1,3},{2,0},{3,1},{4,6},{5,7},{6,4},{7,5},{8,10},{9,11},{10,... | collective-permute-start | bytes 1204232 | tf_op jit(solution)/shard_map/ppermute | solution.py:90
  66.0 1.3 %collective-permute-start.15 = (bf16[96,1792]{1,0:T(8,128)(2,1)S(1)}, bf16[96,1792]{1,0:T(8,128)(2,1)S(1)}, u32[]{:S(2)}, u32[]{:S(2)}) collective-permute-start(bf16[96,1792]{1,0:T(8,128)(2,1)S(1)} %get-tuple-element.134), channel_id=1, source_target_pairs={{0,4},{1,5},{2,6},{3,7},{4,0},{5,1},{6,2},{7,3},{8,12},{9,13},{10,... | collective-permute-start | bytes 1032200 | tf_op jit(solution)/shard_map/ppermute | solution.py:90
  67.2 3.9 %accumulate_third.1 = (f32[256,1792]{1,0:T(8,128)S(1)}, f32[256,1792]{1,0:T(8,128)S(1)}) custom-call(bf16[168,1792]{1,0:T(8,128)(2,1)S(1)} %copy-done, bf16[168,1792]{1,0:T(8,128)(2,1)S(1)} %collective-permute-done.refs_1_, bf16[168,1792]{1,0:T(8,128)(2,1)S(1)} %collective-permute-done.1.refs_2_, ...), custom_call_target="tpu_custom_call", output_to_operand_aliasing={{0}: (10, {}), {1}: (11, {})} | custom-call | flops 1000 | bytes 1000 | tf_op jit(solution)/shard_map/accumulate_third/pallas_call | solution.py:124
  71.2 3.0 %collective-permute-done.11.refs_0_ = bf16[96,1792]{1,0:T(8,128)(2,1)S(1)} collective-permute-done((bf16[96,1792]{1,0:T(8,128)(2,1)S(1)}, bf16[96,1792]{1,0:T(8,128)(2,1)S(1)}, u32[]{:S(2)}, u32[]{:S(2)}) %collective-permute-start.11) | collective-permute-done | bytes 344096 | tf_op jit(solution)/shard_map/ppermute | solution.py:90
  74.2 1.4 %collective-permute-done.12.refs_1_.refs_2_ = bf16[96,1792]{1,0:T(8,128)(2,1)S(1)} collective-permute-done((bf16[96,1792]{1,0:T(8,128)(2,1)S(1)}, bf16[96,1792]{1,0:T(8,128)(2,1)S(1)}, u32[]{:S(2)}, u32[]{:S(2)}) %collective-permute-start.12) | collective-permute-done | bytes 344096 | tf_op jit(solution)/shard_map/ppermute | solution.py:90
  75.6 0.3 collective-permute-start.17
  75.9 2.5 %collective-permute-start.18 = (bf16[56,1792]{1,0:T(8,128)(2,1)S(1)}, bf16[56,1792]{1,0:T(8,128)(2,1)S(1)}, u32[]{:S(2)}, u32[]{:S(2)}) collective-permute-start(bf16[56,1792]{1,0:T(8,128)(2,1)S(1)} %get-tuple-element.138), channel_id=1, source_target_pairs={{0,8},{1,9},{2,10},{3,11},{4,12},{5,13},{6,14},{7,15},{8,24},{9,25... | collective-permute-start | bytes 602120 | tf_op jit(solution)/shard_map/ppermute | solution.py:90
  78.4 1.1 %collective-permute-start.16 = (bf16[48,1792]{1,0:T(8,128)(2,1)S(1)}, bf16[48,1792]{1,0:T(8,128)(2,1)S(1)}, u32[]{:S(2)}, u32[]{:S(2)}) collective-permute-start(bf16[48,1792]{1,0:T(8,128)(2,1)S(1)} %get-tuple-element.136), channel_id=1, source_target_pairs={{0,2},{1,3},{2,0},{3,1},{4,6},{5,7},{6,4},{7,5},{8,10},{9,11},{10,... | collective-permute-start | bytes 516104 | tf_op jit(solution)/shard_map/ppermute | solution.py:90
  79.5 4.3 %collective-permute-done.16.refs_5_ = bf16[48,1792]{1,0:T(8,128)(2,1)S(1)} collective-permute-done((bf16[48,1792]{1,0:T(8,128)(2,1)S(1)}, bf16[48,1792]{1,0:T(8,128)(2,1)S(1)}, u32[]{:S(2)}, u32[]{:S(2)}) %collective-permute-start.16) | collective-permute-done | bytes 172064 | tf_op jit(solution)/shard_map/ppermute | solution.py:90
  83.8 1.0 %finish_other.1 = bf16[256,1792]{1,0:T(8,128)(2,1)S(1)} custom-call(bf16[96,1792]{1,0:T(8,128)(2,1)S(1)} %collective-permute-done.11.refs_0_, bf16[112,1792]{1,0:T(8,128)(2,1)S(1)} %collective-permute-done.14.refs_1_, bf16[96,1792]{1,0:T(8,128)(2,1)S(1)} %collective-permute-done.12.refs_1_.refs_2_, bf16[96,1792]{1,0:T(8,128)(2,1)S(1)} %collective-permute-done.15.refs_3_, ...), custom_call_target="tpu_custom_call" | custom-call | flops 1000 | bytes 1000 | tf_op jit(solution)/shard_map/finish_other/pallas_call | solution.py:124
  84.9 0.1 collective-permute-start.19
  85.0 1.4 %finish_own.1.kept_ref = f32[256,1792]{1,0:T(8,128)S(1)} custom-call(bf16[96,1792]{1,0:T(8,128)(2,1)S(1)} %collective-permute-done.11.refs_0_, bf16[112,1792]{1,0:T(8,128)(2,1)S(1)} %collective-permute-done.14.refs_1_, bf16[96,1792]{1,0:T(8,128)(2,1)S(1)} %collective-permute-done.12.refs_1_.refs_2_, ...), custom_call_target="tpu_custom_call", output_to_operand_aliasing={{}: (9, {})} | custom-call | flops 1000 | bytes 1000 | tf_op jit(solution)/shard_map/finish_own/pallas_call | solution.py:124
  86.4 1.0 %collective-permute-done.19.given_ref = bf16[256,1792]{1,0:T(8,128)(2,1)S(1)} collective-permute-done((bf16[256,1792]{1,0:T(8,128)(2,1)S(1)}, bf16[256,1792]{1,0:T(8,128)(2,1)S(1)}, u32[]{:S(2)}, u32[]{:S(2)}) %collective-permute-start.19) | collective-permute-done | bytes 917536 | tf_op jit(solution)/shard_map/ppermute | solution.py:90
  87.4 1.2 %final.1 = bf16[256,1792]{1,0:T(8,128)(2,1)} custom-call(s32[1]{0:T(128)S(6)} %copy.23.count_ref, f32[256,1792]{1,0:T(8,128)S(1)} %finish_own.1.kept_ref, bf16[256,1792]{1,0:T(8,128)(2,1)S(1)} %collective-permute-done.19.given_ref), custom_call_target="tpu_custom_call" | custom-call | flops 1000 | bytes 1000 | tf_op jit(solution)/shard_map/final/pallas_call | solution.py:124
  (29 shorter events, 0.2 us)
Async XLA Ops:
  2.8 18.6 %collective-permute-start = (bf16[168,1792]{1,0:T(8,128)(2,1)}, bf16[168,1792]{1,0:T(8,128)(2,1)S(1)}, u32[]{:S(2)}, u32[]{:S(2)}) collective-permute-start(bf16[168,1792]{1,0:T(8,128)(2,1)} %get-tuple-element.78.refs_0_), channel_id=1, source_target_pairs={{0,2},{1,3},{2,0},{3,1},{4,6},{5,7},{6,4},{7,5},{8,10},{9,11},{10,... | collective-permute-start | bytes 1806344 | tf_op jit(solution)/shard_map/ppermute | solution.py:90
  5.8 15.6 %collective-permute-start.1 = (bf16[168,1792]{1,0:T(8,128)(2,1)}, bf16[168,1792]{1,0:T(8,128)(2,1)S(1)}, u32[]{:S(2)}, u32[]{:S(2)}) collective-permute-start(bf16[168,1792]{1,0:T(8,128)(2,1)} %get-tuple-element.78.refs_0_), channel_id=1, source_target_pairs={{0,4},{1,5},{2,6},{3,7},{4,0},{5,1},{6,2},{7,3},{8,12},{9,13},{10,... | collective-permute-start | bytes 1806344 | tf_op jit(solution)/shard_map/ppermute | solution.py:90
  7.4 14.0 %collective-permute-start.2 = (bf16[144,1792]{1,0:T(8,128)(2,1)}, bf16[144,1792]{1,0:T(8,128)(2,1)S(1)}, u32[]{:S(2)}, u32[]{:S(2)}) collective-permute-start(bf16[144,1792]{1,0:T(8,128)(2,1)} %get-tuple-element.79), channel_id=1, source_target_pairs={{0,8},{1,9},{2,10},{3,11},{4,12},{5,13},{6,14},{7,15},{8,24},{9,25... | collective-permute-start | bytes 1548296 | tf_op jit(solution)/shard_map/ppermute | solution.py:90
  9.7 1.2 %copy-start.1 = (bf16[1,256,1792]{2,1,0:T(8,128)(2,1)S(1)}, bf16[1,256,1792]{2,1,0:T(8,128)(2,1)}, u32[]{:S(2)}) copy-start(bf16[1,256,1792]{2,1,0:T(8,128)(2,1)} %param.13) | copy-start | bytes 2752516
  10.8 1.9 %copy-start.3 = (bf16[1792,896]{1,0:T(8,128)(2,1)S(1)}, bf16[1792,896]{1,0:T(8,128)(2,1)}, u32[]{:S(2)}) copy-start(bf16[1792,896]{1,0:T(8,128)(2,1)} %value_ref.1) | copy-start | bytes 9633796
  12.7 1.0 %copy-start.5 = (bf16[1792,128]{1,0:T(8,128)(2,1)S(1)}, bf16[1792,128]{1,0:T(8,128)(2,1)}, u32[]{:S(2)}) copy-start(bf16[1792,128]{1,0:T(8,128)(2,1)} %query_ref.1) | copy-start | bytes 1376260
  13.8 1.0 %copy-start.6 = (bf16[1792,128]{1,0:T(8,128)(2,1)S(1)}, bf16[1792,128]{1,0:T(8,128)(2,1)}, u32[]{:S(2)}) copy-start(bf16[1792,128]{1,0:T(8,128)(2,1)} %key_ref.1) | copy-start | bytes 1376260
  14.8 0.7 copy-start.7
  15.5 5.9 %copy-start = (bf16[168,1792]{1,0:T(8,128)(2,1)S(1)}, bf16[168,1792]{1,0:T(8,128)(2,1)}, u32[]{:S(2)}) copy-start(bf16[168,1792]{1,0:T(8,128)(2,1)} %get-tuple-element.78.refs_0_) | copy-start | bytes 1806340
  15.5 13.8 %copy-start.4 = (bf16[896,1792]{1,0:T(8,128)(2,1)S(1)}, bf16[896,1792]{1,0:T(8,128)(2,1)}, u32[]{:S(2)}) copy-start(bf16[896,1792]{1,0:T(8,128)(2,1)} %out_ref.1) | copy-start | bytes 9633796
  19.3 6.4 %copy-start.9 = (f32[1792]{0:T(1024)S(1)}, f32[1792]{0:T(1024)}, u32[]{:S(2)}) copy-start(f32[1792]{0:T(1024)} %param.22) | copy-start | bytes 21508
  19.3 6.4 %copy-start.8 = (f32[1,256,8]{1,2,0:T(8,128)S(1)}, f32[1,256,8]{1,2,0:T(8,128)}, u32[]{:S(2)}) copy-start(f32[1,256,8]{1,2,0:T(8,128)} %param.15) | copy-start | bytes 24580
  19.3 10.1 %copy-start.2 = (bf16[1,256,1792]{2,1,0:T(8,128)(2,1)S(1)}, bf16[1,256,1792]{2,1,0:T(8,128)(2,1)}, u32[]{:S(2)}) copy-start(bf16[1,256,1792]{2,1,0:T(8,128)(2,1)} %param.13) | copy-start | bytes 2752516
  21.6 20.1 %collective-permute-start.4 = (bf16[232,1792]{1,0:T(8,128)(2,1)S(1)}, bf16[232,1792]{1,0:T(8,128)(2,1)S(1)}, u32[]{:S(2)}, u32[]{:S(2)}) collective-permute-start(bf16[232,1792]{1,0:T(8,128)(2,1)S(1)} %get-tuple-element.90), channel_id=1, source_target_pairs={{0,4},{1,5},{2,6},{3,7},{4,0},{5,1},{6,2},{7,3},{8,12},{9,13},{10,... | collective-permute-start | bytes 2494472 | tf_op jit(solution)/shard_map/ppermute | solution.py:90
  22.9 18.8 %collective-permute-start.3 = (bf16[224,1792]{1,0:T(8,128)(2,1)S(1)}, bf16[224,1792]{1,0:T(8,128)(2,1)S(1)}, u32[]{:S(2)}, u32[]{:S(2)}) collective-permute-start(bf16[224,1792]{1,0:T(8,128)(2,1)S(1)} %get-tuple-element.89), channel_id=1, source_target_pairs={{0,2},{1,3},{2,0},{3,1},{4,6},{5,7},{6,4},{7,5},{8,10},{9,11},{10,... | collective-permute-start | bytes 2408456 | tf_op jit(solution)/shard_map/ppermute | solution.py:90
  23.4 18.2 %collective-permute-start.5 = (bf16[216,1792]{1,0:T(8,128)(2,1)S(1)}, bf16[216,1792]{1,0:T(8,128)(2,1)S(1)}, u32[]{:S(2)}, u32[]{:S(2)}) collective-permute-start(bf16[216,1792]{1,0:T(8,128)(2,1)S(1)} %get-tuple-element.91), channel_id=1, source_target_pairs={{0,8},{1,9},{2,10},{3,11},{4,12},{5,13},{6,14},{7,15},{8,24},{9,25... | collective-permute-start | bytes 2322440 | tf_op jit(solution)/shard_map/ppermute | solution.py:90
  41.9 19.2 %collective-permute-start.8 = (bf16[240,1792]{1,0:T(8,128)(2,1)S(1)}, bf16[240,1792]{1,0:T(8,128)(2,1)S(1)}, u32[]{:S(2)}, u32[]{:S(2)}) collective-permute-start(bf16[240,1792]{1,0:T(8,128)(2,1)S(1)} %get-tuple-element.113), channel_id=1, source_target_pairs={{0,8},{1,9},{2,10},{3,11},{4,12},{5,13},{6,14},{7,15},{8,24},{9,25... | collective-permute-start | bytes 2580488 | tf_op jit(solution)/shard_map/ppermute | solution.py:90
  42.9 17.0 %collective-permute-start.6 = (bf16[224,1792]{1,0:T(8,128)(2,1)S(1)}, bf16[224,1792]{1,0:T(8,128)(2,1)S(1)}, u32[]{:S(2)}, u32[]{:S(2)}) collective-permute-start(bf16[224,1792]{1,0:T(8,128)(2,1)S(1)} %get-tuple-element.111), channel_id=1, source_target_pairs={{0,2},{1,3},{2,0},{3,1},{4,6},{5,7},{6,4},{7,5},{8,10},{9,11},{10,... | collective-permute-start | bytes 2408456 | tf_op jit(solution)/shard_map/ppermute | solution.py:90
  44.1 15.2 %collective-permute-start.7 = (bf16[208,1792]{1,0:T(8,128)(2,1)S(1)}, bf16[208,1792]{1,0:T(8,128)(2,1)S(1)}, u32[]{:S(2)}, u32[]{:S(2)}) collective-permute-start(bf16[208,1792]{1,0:T(8,128)(2,1)S(1)} %get-tuple-element.112), channel_id=1, source_target_pairs={{0,4},{1,5},{2,6},{3,7},{4,0},{5,1},{6,2},{7,3},{8,12},{9,13},{10,... | collective-permute-start | bytes 2236424 | tf_op jit(solution)/shard_map/ppermute | solution.py:90
  44.6 1.8 %collective-permute-start.9 = (bf16[128,1792]{1,0:T(8,128)(2,1)S(1)}, bf16[128,1792]{1,0:T(8,128)(2,1)S(1)}, u32[]{:S(2)}, u32[]{:S(2)}) collective-permute-start(bf16[128,1792]{1,0:T(8,128)(2,1)S(1)} %get-tuple-element.117), channel_id=1, source_target_pairs={{0,1},{1,0},{2,3},{3,2},{4,5},{5,4},{6,7},{7,6},{8,9},{9,8},{10,11... | collective-permute-start | bytes 1376264 | tf_op jit(solution)/shard_map/ppermute | solution.py:90
  44.6 2.5 %collective-permute-start.10 = (bf16[128,1792]{1,0:T(8,128)(2,1)S(1)}, bf16[128,1792]{1,0:T(8,128)(2,1)S(1)}, u32[]{:S(2)}, u32[]{:S(2)}) collective-permute-start(bf16[128,1792]{1,0:T(8,128)(2,1)S(1)} %get-tuple-element.118), channel_id=1, source_target_pairs={{0,1},{1,0},{2,3},{3,2},{4,5},{5,4},{6,7},{7,6},{8,9},{9,8},{10,11... | collective-permute-start | bytes 1376264 | tf_op jit(solution)/shard_map/ppermute | solution.py:90
  61.2 14.4 %collective-permute-start.13 = (bf16[128,1792]{1,0:T(8,128)(2,1)S(1)}, bf16[128,1792]{1,0:T(8,128)(2,1)S(1)}, u32[]{:S(2)}, u32[]{:S(2)}) collective-permute-start(bf16[128,1792]{1,0:T(8,128)(2,1)S(1)} %get-tuple-element.126), channel_id=1, source_target_pairs={{0,8},{1,9},{2,10},{3,11},{4,12},{5,13},{6,14},{7,15},{8,24},{9,25... | collective-permute-start | bytes 1376264 | tf_op jit(solution)/shard_map/ppermute | solution.py:90
  63.2 11.0 %collective-permute-start.11 = (bf16[96,1792]{1,0:T(8,128)(2,1)S(1)}, bf16[96,1792]{1,0:T(8,128)(2,1)S(1)}, u32[]{:S(2)}, u32[]{:S(2)}) collective-permute-start(bf16[96,1792]{1,0:T(8,128)(2,1)S(1)} %get-tuple-element.124), channel_id=1, source_target_pairs={{0,2},{1,3},{2,0},{3,1},{4,6},{5,7},{6,4},{7,5},{8,10},{9,11},{10,... | collective-permute-start | bytes 1032200 | tf_op jit(solution)/shard_map/ppermute | solution.py:90
  64.5 11.0 %collective-permute-start.12 = (bf16[96,1792]{1,0:T(8,128)(2,1)S(1)}, bf16[96,1792]{1,0:T(8,128)(2,1)S(1)}, u32[]{:S(2)}, u32[]{:S(2)}) collective-permute-start(bf16[96,1792]{1,0:T(8,128)(2,1)S(1)} %get-tuple-element.125), channel_id=1, source_target_pairs={{0,4},{1,5},{2,6},{3,7},{4,0},{5,1},{6,2},{7,3},{8,12},{9,13},{10,... | collective-permute-start | bytes 1032200 | tf_op jit(solution)/shard_map/ppermute | solution.py:90
  64.8 19.1 %collective-permute-start.14 = (bf16[112,1792]{1,0:T(8,128)(2,1)S(1)}, bf16[112,1792]{1,0:T(8,128)(2,1)S(1)}, u32[]{:S(2)}, u32[]{:S(2)}) collective-permute-start(bf16[112,1792]{1,0:T(8,128)(2,1)S(1)} %get-tuple-element.132), channel_id=1, source_target_pairs={{0,2},{1,3},{2,0},{3,1},{4,6},{5,7},{6,4},{7,5},{8,10},{9,11},{10,... | collective-permute-start | bytes 1204232 | tf_op jit(solution)/shard_map/ppermute | solution.py:90
  66.0 17.9 %collective-permute-start.15 = (bf16[96,1792]{1,0:T(8,128)(2,1)S(1)}, bf16[96,1792]{1,0:T(8,128)(2,1)S(1)}, u32[]{:S(2)}, u32[]{:S(2)}) collective-permute-start(bf16[96,1792]{1,0:T(8,128)(2,1)S(1)} %get-tuple-element.134), channel_id=1, source_target_pairs={{0,4},{1,5},{2,6},{3,7},{4,0},{5,1},{6,2},{7,3},{8,12},{9,13},{10,... | collective-permute-start | bytes 1032200 | tf_op jit(solution)/shard_map/ppermute | solution.py:90
  75.6 8.2 %collective-permute-start.17 = (bf16[64,1792]{1,0:T(8,128)(2,1)S(1)}, bf16[64,1792]{1,0:T(8,128)(2,1)S(1)}, u32[]{:S(2)}, u32[]{:S(2)}) collective-permute-start(bf16[64,1792]{1,0:T(8,128)(2,1)S(1)} %get-tuple-element.137), channel_id=1, source_target_pairs={{0,4},{1,5},{2,6},{3,7},{4,0},{5,1},{6,2},{7,3},{8,12},{9,13},{10,... | collective-permute-start | bytes 688136 | tf_op jit(solution)/shard_map/ppermute | solution.py:90
  75.9 7.9 %collective-permute-start.18 = (bf16[56,1792]{1,0:T(8,128)(2,1)S(1)}, bf16[56,1792]{1,0:T(8,128)(2,1)S(1)}, u32[]{:S(2)}, u32[]{:S(2)}) collective-permute-start(bf16[56,1792]{1,0:T(8,128)(2,1)S(1)} %get-tuple-element.138), channel_id=1, source_target_pairs={{0,8},{1,9},{2,10},{3,11},{4,12},{5,13},{6,14},{7,15},{8,24},{9,25... | collective-permute-start | bytes 602120 | tf_op jit(solution)/shard_map/ppermute | solution.py:90
  78.4 5.4 %collective-permute-start.16 = (bf16[48,1792]{1,0:T(8,128)(2,1)S(1)}, bf16[48,1792]{1,0:T(8,128)(2,1)S(1)}, u32[]{:S(2)}, u32[]{:S(2)}) collective-permute-start(bf16[48,1792]{1,0:T(8,128)(2,1)S(1)} %get-tuple-element.136), channel_id=1, source_target_pairs={{0,2},{1,3},{2,0},{3,1},{4,6},{5,7},{6,4},{7,5},{8,10},{9,11},{10,... | collective-permute-start | bytes 516104 | tf_op jit(solution)/shard_map/ppermute | solution.py:90
  84.9 2.5 %collective-permute-start.19 = (bf16[256,1792]{1,0:T(8,128)(2,1)S(1)}, bf16[256,1792]{1,0:T(8,128)(2,1)S(1)}, u32[]{:S(2)}, u32[]{:S(2)}) collective-permute-start(bf16[256,1792]{1,0:T(8,128)(2,1)S(1)} %finish_other.1), channel_id=1, source_target_pairs={{0,1},{1,0},{2,3},{3,2},{4,5},{5,4},{6,7},{7,6},{8,9},{9,8},{10,11... | collective-permute-start | bytes 2752520 | tf_op jit(solution)/shard_map/ppermute | solution.py:90

commit v15 on v14

--- a/solution.py
+++ b/solution.py
@@ -598,15 +598,14 @@
     )
     near2, far2, deep2, *acc = together(near2, far2, deep2, *acc)
 
-    held = 2 * main // 3
     two = 2 * main
     sends = collect(
         (near2, far2, deep2),
         (
             ((2, main, wide),),
             ((2, 0, main), (2, two, wide)),
-            ((2, wide, wide + 4 * narrow), (1, 2 * wide - cut - main, 2 * wide - cut - main + held)),
-            ((2, 0, main), (1, 0, main), (1, two + held, wide)),
+            ((2, wide, wide + 4 * narrow), (1, 2 * wide - cut - main, 2 * wide - cut)),
+            ((2, 0, main), (1, 0, main)),
             ((2, main, two), (0, main, two)),
         ),
         "collect_fourth",
@@ -633,8 +632,8 @@
         (near3, far3, deep3),
         (
             ((1, 0, main),),
-            ((0, 0, main), (0, main + held, two)),
-            ((2, 3 * narrow, 4 * narrow + held),),
+            ((0, 0, main),),
+            ((2, 3 * narrow, 4 * narrow + main),),
         ),
         "collect_fifth",
     )
@@ -644,10 +643,8 @@
     last = [
         ((1, 0, main), (0, 0, main), (0, main, two)),
         ((2, 0, main), (3, 0, main), (2, main, two)),
-        ((1, main, main + held), (3, main, main + held), (4, line, line + held)),
-        ((1, main + held, two), (3, main + held, two), (1, two, two + main - held)),
-        ((5, 0, held), (6, 0, held), (7, narrow, narrow + held)),
-        ((5, held, main), (6, held, main), (6, main, two - held)),
+        ((1, main, two), (3, main, two), (4, line, line + main)),
+        ((5, 0, main), (6, 0, main), (7, narrow, narrow + main)),
     ]
     last += [runs(4, k * narrow, edge) for k in range(4)] + [runs(7, 0, edge)]
     (given,) = accumulate(rows[1:], weights, last, acc[1:], jnp.bfloat16, "finish_other")

time: 89 us -> 88.7 us (level)
  transfers between devices with their start and end apart: 20 -> 20, of which waited for: 11 -> 12; matrix products, arithmetic and copies ran while one was open for 1% -> 1% of each run, Pallas kernels for 21% -> 21%
where the time goes in v15:
time: 88.7 us; the launch traced here: 88.2 us
  waiting for transfers between devices  34.1 us (38%)
  Pallas kernels  23.5 us (26%)
  starting transfers between devices  22.5 us (25%)
  local copies, waits for them, and re-layouts  6.61 us (7%)
  between operations  1.46 us (2%)
    ppermute x20, waiting for transfers between devices, permute(): return lax.ppermute(array, 'req', [(i, target(i)) for i in range(count)])  34.1 us
    pallas_call x14, Pallas kernels, kernel_call(): pl.pallas_call(body, out_shape=out_shape, in_specs=specs or vmem(len(oper...  23.5 us
    ppermute x20, starting transfers between devices, permute(): return lax.ppermute(array, 'req', [(i, target(i)) for i in range(count)])  22.5 us
    unnamed x20, local copies, waits for them, and re-layouts  5.89 us
  transfers between devices with their start and end apart: 20, of which 12 were waited for; matrix products, arithmetic and copies ran while one was open for 1% of the time, Pallas kernels for 21%

profile of v15, /device:TPU:0, one launch (start us, length us, event | category | flops | bytes accessed | tf_op | source)
XLA Modules:
  0.0 88.2 jit_solution(9683080531477400809)
XLA Ops:
  0.6 2.2 %shard.1 = (bf16[168,1792]{1,0:T(8,128)(2,1)}, bf16[144,1792]{1,0:T(8,128)(2,1)}) custom-call(bf16[56,1792]{1,0:T(8,128)(2,1)} %bitcast.17, bf16[56,1792]{1,0:T(8,128)(2,1)} %bitcast.18, bf16[56,1792]{1,0:T(8,128)(2,1)} %bitcast.19), custom_call_target="tpu_custom_call" | custom-call | flops 1000 | bytes 1000 | tf_op jit(solution)/shard_map/shard/pallas_call | solution.py:124
  2.8 3.0 %collective-permute-start = (bf16[168,1792]{1,0:T(8,128)(2,1)}, bf16[168,1792]{1,0:T(8,128)(2,1)S(1)}, u32[]{:S(2)}, u32[]{:S(2)}) collective-permute-start(bf16[168,1792]{1,0:T(8,128)(2,1)} %get-tuple-element.78.refs_0_), channel_id=1, source_target_pairs={{0,2},{1,3},{2,0},{3,1},{4,6},{5,7},{6,4},{7,5},{8,10},{9,11},{10,... | collective-permute-start | bytes 1806344 | tf_op jit(solution)/shard_map/ppermute | solution.py:90
  5.8 1.5 %collective-permute-start.1 = (bf16[168,1792]{1,0:T(8,128)(2,1)}, bf16[168,1792]{1,0:T(8,128)(2,1)S(1)}, u32[]{:S(2)}, u32[]{:S(2)}) collective-permute-start(bf16[168,1792]{1,0:T(8,128)(2,1)} %get-tuple-element.78.refs_0_), channel_id=1, source_target_pairs={{0,4},{1,5},{2,6},{3,7},{4,0},{5,1},{6,2},{7,3},{8,12},{9,13},{10,... | collective-permute-start | bytes 1806344 | tf_op jit(solution)/shard_map/ppermute | solution.py:90
  7.4 1.6 %collective-permute-start.2 = (bf16[144,1792]{1,0:T(8,128)(2,1)}, bf16[144,1792]{1,0:T(8,128)(2,1)S(1)}, u32[]{:S(2)}, u32[]{:S(2)}) collective-permute-start(bf16[144,1792]{1,0:T(8,128)(2,1)} %get-tuple-element.79), channel_id=1, source_target_pairs={{0,8},{1,9},{2,10},{3,11},{4,12},{5,13},{6,14},{7,15},{8,24},{9,25... | collective-permute-start | bytes 1548296 | tf_op jit(solution)/shard_map/ppermute | solution.py:90
  8.9 0.7 broadcast_in_dim.16.gain_ref
  9.7 1.2 %copy-done.1 = bf16[1,256,1792]{2,1,0:T(8,128)(2,1)S(1)} copy-done((bf16[1,256,1792]{2,1,0:T(8,128)(2,1)S(1)}, bf16[1,256,1792]{2,1,0:T(8,128)(2,1)}, u32[]{:S(2)}) %copy-start.1) | copy-done | bytes 917528
  10.8 1.9 %copy-done.3 = bf16[1792,896]{1,0:T(8,128)(2,1)S(1)} copy-done((bf16[1792,896]{1,0:T(8,128)(2,1)S(1)}, bf16[1792,896]{1,0:T(8,128)(2,1)}, u32[]{:S(2)}) %copy-start.3) | copy-done | bytes 3211288
  12.7 1.0 %copy-done.5 = bf16[1792,128]{1,0:T(8,128)(2,1)S(1)} copy-done((bf16[1792,128]{1,0:T(8,128)(2,1)S(1)}, bf16[1792,128]{1,0:T(8,128)(2,1)}, u32[]{:S(2)}) %copy-start.5) | copy-done | bytes 458776
  13.8 1.0 %copy-done.6 = bf16[1792,128]{1,0:T(8,128)(2,1)S(1)} copy-done((bf16[1792,128]{1,0:T(8,128)(2,1)S(1)}, bf16[1792,128]{1,0:T(8,128)(2,1)}, u32[]{:S(2)}) %copy-start.6) | copy-done | bytes 458776
  14.8 0.7 copy-done.7
  15.5 3.7 %project.1 = (bf16[256,128]{1,0:T(8,128)(2,1)S(1)}, bf16[256,128]{1,0:T(8,128)(2,1)S(1)}, bf16[256,896]{1,0:T(8,128)(2,1)S(1)}) custom-call(bf16[256,1792]{1,0:T(8,128)(2,1)S(1)} %bitcast.13, bf16[16,1792]{1,0:T(8,128)(2,1)S(1)} %broadcast_in_dim.15.edge_ref, f32[1,1792]{1,0:T(1,128)S(1)} %broadcast_in_dim.16.gain_ref, f32[3,1792]{1,0:T(4,128)S(1)} %copy-done.7, ...), custom_call_target="tpu_custom_call" | custom-call | flops 1000 | bytes 1000 | tf_op jit(solution)/shard_map/project/pallas_call | solution.py:124
  19.3 2.1 %collective-permute-done.2.refs_3_ = bf16[144,1792]{1,0:T(8,128)(2,1)S(1)} collective-permute-done((bf16[144,1792]{1,0:T(8,128)(2,1)}, bf16[144,1792]{1,0:T(8,128)(2,1)S(1)}, u32[]{:S(2)}, u32[]{:S(2)}) %collective-permute-start.2) | collective-permute-done | bytes 516128 | tf_op jit(solution)/shard_map/ppermute | solution.py:90
  21.4 0.2 collect_second.1
  21.6 1.3 %collective-permute-start.4 = (bf16[232,1792]{1,0:T(8,128)(2,1)S(1)}, bf16[232,1792]{1,0:T(8,128)(2,1)S(1)}, u32[]{:S(2)}, u32[]{:S(2)}) collective-permute-start(bf16[232,1792]{1,0:T(8,128)(2,1)S(1)} %get-tuple-element.90), channel_id=1, source_target_pairs={{0,4},{1,5},{2,6},{3,7},{4,0},{5,1},{6,2},{7,3},{8,12},{9,13},{10,... | collective-permute-start | bytes 2494472 | tf_op jit(solution)/shard_map/ppermute | solution.py:90
  22.9 0.5 collective-permute-start.3
  23.4 1.6 %collective-permute-start.5 = (bf16[216,1792]{1,0:T(8,128)(2,1)S(1)}, bf16[216,1792]{1,0:T(8,128)(2,1)S(1)}, u32[]{:S(2)}, u32[]{:S(2)}) collective-permute-start(bf16[216,1792]{1,0:T(8,128)(2,1)S(1)} %get-tuple-element.91), channel_id=1, source_target_pairs={{0,8},{1,9},{2,10},{3,11},{4,12},{5,13},{6,14},{7,15},{8,24},{9,25... | collective-permute-start | bytes 2322440 | tf_op jit(solution)/shard_map/ppermute | solution.py:90
  25.7 3.7 %attend.1 = (f32[256,896]{1,0:T(8,128)S(1)}, f32[256,8]{1,0:T(8,128)S(1)}, f32[273,1,896]{2,1,0:T(1,128)}, f32[8,273]{1,0:T(8,128)}) custom-call(s32[1]{0:T(128)S(6)} %copy.23.count_ref, f32[8,256]{1,0:T(8,128)S(1)} %bitcast.15, bf16[256,128]{1,0:T(8,128)(2,1)S(1)} %get-tuple-element.95.queries_ref, bf16[256,128]{1,0:T(8,128)(2,1)S(1)} %get-tuple-element.96.keys_ref, ...), custom_call_target="tpu_custom_call" | custom-call | flops 1000 | bytes 1000 | tf_op jit(solution)/shard_map/attend/pallas_call | solution.py:124
  29.4 2.6 %mix.1 = (bf16[256,1792]{1,0:T(8,128)(2,1)S(1)}, bf16[256,1792]{1,0:T(8,128)(2,1)S(1)}) custom-call(f32[256,896]{1,0:T(8,128)S(1)} %get-tuple-element.98.numer_ref, f32[256,8]{1,0:T(8,128)S(1)} %get-tuple-element.99.denom_ref, bf16[256,1792]{1,0:T(8,128)(2,1)S(1)} %bitcast.14, bf16[896,1792]{1,0:T(8,128)(2,1)S(1)} %copy-done.4, ...), custom_call_target="tpu_custom_call" | custom-call | flops 1000 | bytes 1000 | tf_op jit(solution)/shard_map/mix/pallas_call | solution.py:124
  32.0 9.7 %collective-permute-done.5.refs_2_.refs_6_.refs_4_ = bf16[216,1792]{1,0:T(8,128)(2,1)S(1)} collective-permute-done((bf16[216,1792]{1,0:T(8,128)(2,1)S(1)}, bf16[216,1792]{1,0:T(8,128)(2,1)S(1)}, u32[]{:S(2)}, u32[]{:S(2)}) %collective-permute-start.5) | collective-permute-done | bytes 774176 | tf_op jit(solution)/shard_map/ppermute | solution.py:90
  41.6 0.2 collect_third.1
  41.9 1.0 %collective-permute-start.8 = (bf16[240,1792]{1,0:T(8,128)(2,1)S(1)}, bf16[240,1792]{1,0:T(8,128)(2,1)S(1)}, u32[]{:S(2)}, u32[]{:S(2)}) collective-permute-start(bf16[240,1792]{1,0:T(8,128)(2,1)S(1)} %get-tuple-element.113), channel_id=1, source_target_pairs={{0,8},{1,9},{2,10},{3,11},{4,12},{5,13},{6,14},{7,15},{8,24},{9,25... | collective-permute-start | bytes 2580488 | tf_op jit(solution)/shard_map/ppermute | solution.py:90
  42.9 1.2 %collective-permute-start.6 = (bf16[224,1792]{1,0:T(8,128)(2,1)S(1)}, bf16[224,1792]{1,0:T(8,128)(2,1)S(1)}, u32[]{:S(2)}, u32[]{:S(2)}) collective-permute-start(bf16[224,1792]{1,0:T(8,128)(2,1)S(1)} %get-tuple-element.111), channel_id=1, source_target_pairs={{0,2},{1,3},{2,0},{3,1},{4,6},{5,7},{6,4},{7,5},{8,10},{9,11},{10,... | collective-permute-start | bytes 2408456 | tf_op jit(solution)/shard_map/ppermute | solution.py:90
  44.1 0.5 collective-permute-start.7
  44.6 0.5 collective-permute-start.10
  45.1 1.3 %collective-permute-done.9.refs_0_ = bf16[128,1792]{1,0:T(8,128)(2,1)S(1)} collective-permute-done((bf16[128,1792]{1,0:T(8,128)(2,1)S(1)}, bf16[128,1792]{1,0:T(8,128)(2,1)S(1)}, u32[]{:S(2)}, u32[]{:S(2)}) %collective-permute-start.9) | collective-permute-done | bytes 458784 | tf_op jit(solution)/shard_map/ppermute | solution.py:90
  46.5 0.7 collective-permute-done.10.refs_1_
  47.2 3.2 %accumulate_second.1 = (f32[256,1792]{1,0:T(8,128)S(1)}, f32[256,1792]{1,0:T(8,128)S(1)}) custom-call(bf16[168,1792]{1,0:T(8,128)(2,1)S(1)} %copy-done, bf16[168,1792]{1,0:T(8,128)(2,1)S(1)} %collective-permute-done.refs_1_, bf16[168,1792]{1,0:T(8,128)(2,1)S(1)} %collective-permute-done.1.refs_2_, bf16[144,1792]{1,0:T(8,128)(2,1)S(1)} %collective-permute-done.2.refs_3_, ...), custom_call_target="tpu_custom_call" | custom-call | flops 1000 | bytes 1000 | tf_op jit(solution)/shard_map/accumulate_second/pallas_call | solution.py:124
  50.4 8.9 %collective-permute-done.7.refs_1_.refs_6_ = bf16[208,1792]{1,0:T(8,128)(2,1)S(1)} collective-permute-done((bf16[208,1792]{1,0:T(8,128)(2,1)S(1)}, bf16[208,1792]{1,0:T(8,128)(2,1)S(1)}, u32[]{:S(2)}, u32[]{:S(2)}) %collective-permute-start.7) | collective-permute-done | bytes 745504 | tf_op jit(solution)/shard_map/ppermute | solution.py:90
  59.3 0.5 collective-permute-done.6.refs_0_.refs_5_
  59.8 1.2 %collective-permute-done.8.refs_2_.refs_7_ = bf16[240,1792]{1,0:T(8,128)(2,1)S(1)} collective-permute-done((bf16[240,1792]{1,0:T(8,128)(2,1)S(1)}, bf16[240,1792]{1,0:T(8,128)(2,1)S(1)}, u32[]{:S(2)}, u32[]{:S(2)}) %collective-permute-start.8) | collective-permute-done | bytes 860192 | tf_op jit(solution)/shard_map/ppermute | solution.py:90
  61.1 0.1 collect_fourth.1
  61.2 2.0 %collective-permute-start.13 = (bf16[144,1792]{1,0:T(8,128)(2,1)S(1)}, bf16[144,1792]{1,0:T(8,128)(2,1)S(1)}, u32[]{:S(2)}, u32[]{:S(2)}) collective-permute-start(bf16[144,1792]{1,0:T(8,128)(2,1)S(1)} %get-tuple-element.126), channel_id=1, source_target_pairs={{0,8},{1,9},{2,10},{3,11},{4,12},{5,13},{6,14},{7,15},{8,24},{9,25... | collective-permute-start | bytes 1548296 | tf_op jit(solution)/shard_map/ppermute | solution.py:90
  63.2 1.4 %collective-permute-start.11 = (bf16[96,1792]{1,0:T(8,128)(2,1)S(1)}, bf16[96,1792]{1,0:T(8,128)(2,1)S(1)}, u32[]{:S(2)}, u32[]{:S(2)}) collective-permute-start(bf16[96,1792]{1,0:T(8,128)(2,1)S(1)} %get-tuple-element.124), channel_id=1, source_target_pairs={{0,2},{1,3},{2,0},{3,1},{4,6},{5,7},{6,4},{7,5},{8,10},{9,11},{10,... | collective-permute-start | bytes 1032200 | tf_op jit(solution)/shard_map/ppermute | solution.py:90
  64.5 0.2 collective-permute-start.12
  64.8 1.2 %collective-permute-start.14 = (bf16[96,1792]{1,0:T(8,128)(2,1)S(1)}, bf16[96,1792]{1,0:T(8,128)(2,1)S(1)}, u32[]{:S(2)}, u32[]{:S(2)}) collective-permute-start(bf16[96,1792]{1,0:T(8,128)(2,1)S(1)} %get-tuple-element.132), channel_id=1, source_target_pairs={{0,2},{1,3},{2,0},{3,1},{4,6},{5,7},{6,4},{7,5},{8,10},{9,11},{10,... | collective-permute-start | bytes 1032200 | tf_op jit(solution)/shard_map/ppermute | solution.py:90
  66.0 1.3 %collective-permute-start.15 = (bf16[96,1792]{1,0:T(8,128)(2,1)S(1)}, bf16[96,1792]{1,0:T(8,128)(2,1)S(1)}, u32[]{:S(2)}, u32[]{:S(2)}) collective-permute-start(bf16[96,1792]{1,0:T(8,128)(2,1)S(1)} %get-tuple-element.134), channel_id=1, source_target_pairs={{0,4},{1,5},{2,6},{3,7},{4,0},{5,1},{6,2},{7,3},{8,12},{9,13},{10,... | collective-permute-start | bytes 1032200 | tf_op jit(solution)/shard_map/ppermute | solution.py:90
  67.2 3.9 %accumulate_third.1 = (f32[256,1792]{1,0:T(8,128)S(1)}, f32[256,1792]{1,0:T(8,128)S(1)}) custom-call(bf16[168,1792]{1,0:T(8,128)(2,1)S(1)} %copy-done, bf16[168,1792]{1,0:T(8,128)(2,1)S(1)} %collective-permute-done.refs_1_, bf16[168,1792]{1,0:T(8,128)(2,1)S(1)} %collective-permute-done.1.refs_2_, ...), custom_call_target="tpu_custom_call", output_to_operand_aliasing={{0}: (10, {}), {1}: (11, {})} | custom-call | flops 1000 | bytes 1000 | tf_op jit(solution)/shard_map/accumulate_third/pallas_call | solution.py:124
  71.2 2.5 %collective-permute-done.11.refs_0_ = bf16[96,1792]{1,0:T(8,128)(2,1)S(1)} collective-permute-done((bf16[96,1792]{1,0:T(8,128)(2,1)S(1)}, bf16[96,1792]{1,0:T(8,128)(2,1)S(1)}, u32[]{:S(2)}, u32[]{:S(2)}) %collective-permute-start.11) | collective-permute-done | bytes 344096 | tf_op jit(solution)/shard_map/ppermute | solution.py:90
  73.7 1.5 %collective-permute-done.12.refs_1_.refs_2_ = bf16[96,1792]{1,0:T(8,128)(2,1)S(1)} collective-permute-done((bf16[96,1792]{1,0:T(8,128)(2,1)S(1)}, bf16[96,1792]{1,0:T(8,128)(2,1)S(1)}, u32[]{:S(2)}, u32[]{:S(2)}) %collective-permute-start.12) | collective-permute-done | bytes 344096 | tf_op jit(solution)/shard_map/ppermute | solution.py:90
  75.2 2.2 %collective-permute-start.18 = (bf16[72,1792]{1,0:T(8,128)(2,1)S(1)}, bf16[72,1792]{1,0:T(8,128)(2,1)S(1)}, u32[]{:S(2)}, u32[]{:S(2)}) collective-permute-start(bf16[72,1792]{1,0:T(8,128)(2,1)S(1)} %get-tuple-element.138), channel_id=1, source_target_pairs={{0,8},{1,9},{2,10},{3,11},{4,12},{5,13},{6,14},{7,15},{8,24},{9,25... | collective-permute-start | bytes 774152 | tf_op jit(solution)/shard_map/ppermute | solution.py:90
  77.4 0.7 collective-permute-start.16
  78.1 0.8 collective-permute-start.17
  78.8 4.0 %collective-permute-done.16.refs_5_ = bf16[48,1792]{1,0:T(8,128)(2,1)S(1)} collective-permute-done((bf16[48,1792]{1,0:T(8,128)(2,1)S(1)}, bf16[48,1792]{1,0:T(8,128)(2,1)S(1)}, u32[]{:S(2)}, u32[]{:S(2)}) %collective-permute-start.16) | collective-permute-done | bytes 172064 | tf_op jit(solution)/shard_map/ppermute | solution.py:90
  82.8 0.7 collective-permute-done.17.refs_6_
  83.5 1.0 %finish_other.1 = bf16[256,1792]{1,0:T(8,128)(2,1)S(1)} custom-call(bf16[96,1792]{1,0:T(8,128)(2,1)S(1)} %collective-permute-done.11.refs_0_, bf16[96,1792]{1,0:T(8,128)(2,1)S(1)} %collective-permute-done.14.refs_1_, bf16[96,1792]{1,0:T(8,128)(2,1)S(1)} %collective-permute-done.12.refs_1_.refs_2_, bf16[96,1792]{1,0:T(8,128)(2,1)S(1)} %collective-permute-done.15.refs_3_, ...), custom_call_target="tpu_custom_call" | custom-call | flops 1000 | bytes 1000 | tf_op jit(solution)/shard_map/finish_other/pallas_call | solution.py:124
  84.6 1.4 %finish_own.1.kept_ref = f32[256,1792]{1,0:T(8,128)S(1)} custom-call(bf16[96,1792]{1,0:T(8,128)(2,1)S(1)} %collective-permute-done.11.refs_0_, bf16[96,1792]{1,0:T(8,128)(2,1)S(1)} %collective-permute-done.14.refs_1_, bf16[96,1792]{1,0:T(8,128)(2,1)S(1)} %collective-permute-done.12.refs_1_.refs_2_, ...), custom_call_target="tpu_custom_call", output_to_operand_aliasing={{}: (9, {})} | custom-call | flops 1000 | bytes 1000 | tf_op jit(solution)/shard_map/finish_own/pallas_call | solution.py:124
  86.0 1.1 %collective-permute-done.19.given_ref = bf16[256,1792]{1,0:T(8,128)(2,1)S(1)} collective-permute-done((bf16[256,1792]{1,0:T(8,128)(2,1)S(1)}, bf16[256,1792]{1,0:T(8,128)(2,1)S(1)}, u32[]{:S(2)}, u32[]{:S(2)}) %collective-permute-start.19) | collective-permute-done | bytes 917536 | tf_op jit(solution)/shard_map/ppermute | solution.py:90
  87.0 1.2 %final.1 = bf16[256,1792]{1,0:T(8,128)(2,1)} custom-call(s32[1]{0:T(128)S(6)} %copy.23.count_ref, f32[256,1792]{1,0:T(8,128)S(1)} %finish_own.1.kept_ref, bf16[256,1792]{1,0:T(8,128)(2,1)S(1)} %collective-permute-done.19.given_ref), custom_call_target="tpu_custom_call" | custom-call | flops 1000 | bytes 1000 | tf_op jit(solution)/shard_map/final/pallas_call | solution.py:124
  (29 shorter events, 0.2 us)
Async XLA Ops:
  2.8 18.6 %collective-permute-start = (bf16[168,1792]{1,0:T(8,128)(2,1)}, bf16[168,1792]{1,0:T(8,128)(2,1)S(1)}, u32[]{:S(2)}, u32[]{:S(2)}) collective-permute-start(bf16[168,1792]{1,0:T(8,128)(2,1)} %get-tuple-element.78.refs_0_), channel_id=1, source_target_pairs={{0,2},{1,3},{2,0},{3,1},{4,6},{5,7},{6,4},{7,5},{8,10},{9,11},{10,... | collective-permute-start | bytes 1806344 | tf_op jit(solution)/shard_map/ppermute | solution.py:90
  5.8 15.6 %collective-permute-start.1 = (bf16[168,1792]{1,0:T(8,128)(2,1)}, bf16[168,1792]{1,0:T(8,128)(2,1)S(1)}, u32[]{:S(2)}, u32[]{:S(2)}) collective-permute-start(bf16[168,1792]{1,0:T(8,128)(2,1)} %get-tuple-element.78.refs_0_), channel_id=1, source_target_pairs={{0,4},{1,5},{2,6},{3,7},{4,0},{5,1},{6,2},{7,3},{8,12},{9,13},{10,... | collective-permute-start | bytes 1806344 | tf_op jit(solution)/shard_map/ppermute | solution.py:90
  7.4 14.0 %collective-permute-start.2 = (bf16[144,1792]{1,0:T(8,128)(2,1)}, bf16[144,1792]{1,0:T(8,128)(2,1)S(1)}, u32[]{:S(2)}, u32[]{:S(2)}) collective-permute-start(bf16[144,1792]{1,0:T(8,128)(2,1)} %get-tuple-element.79), channel_id=1, source_target_pairs={{0,8},{1,9},{2,10},{3,11},{4,12},{5,13},{6,14},{7,15},{8,24},{9,25... | collective-permute-start | bytes 1548296 | tf_op jit(solution)/shard_map/ppermute | solution.py:90
  9.7 1.2 %copy-start.1 = (bf16[1,256,1792]{2,1,0:T(8,128)(2,1)S(1)}, bf16[1,256,1792]{2,1,0:T(8,128)(2,1)}, u32[]{:S(2)}) copy-start(bf16[1,256,1792]{2,1,0:T(8,128)(2,1)} %param.13) | copy-start | bytes 2752516
  10.8 1.9 %copy-start.3 = (bf16[1792,896]{1,0:T(8,128)(2,1)S(1)}, bf16[1792,896]{1,0:T(8,128)(2,1)}, u32[]{:S(2)}) copy-start(bf16[1792,896]{1,0:T(8,128)(2,1)} %value_ref.1) | copy-start | bytes 9633796
  12.7 1.0 %copy-start.5 = (bf16[1792,128]{1,0:T(8,128)(2,1)S(1)}, bf16[1792,128]{1,0:T(8,128)(2,1)}, u32[]{:S(2)}) copy-start(bf16[1792,128]{1,0:T(8,128)(2,1)} %query_ref.1) | copy-start | bytes 1376260
  13.8 1.0 %copy-start.6 = (bf16[1792,128]{1,0:T(8,128)(2,1)S(1)}, bf16[1792,128]{1,0:T(8,128)(2,1)}, u32[]{:S(2)}) copy-start(bf16[1792,128]{1,0:T(8,128)(2,1)} %key_ref.1) | copy-start | bytes 1376260
  14.8 0.7 copy-start.7
  15.5 5.9 %copy-start = (bf16[168,1792]{1,0:T(8,128)(2,1)S(1)}, bf16[168,1792]{1,0:T(8,128)(2,1)}, u32[]{:S(2)}) copy-start(bf16[168,1792]{1,0:T(8,128)(2,1)} %get-tuple-element.78.refs_0_) | copy-start | bytes 1806340
  15.5 13.8 %copy-start.4 = (bf16[896,1792]{1,0:T(8,128)(2,1)S(1)}, bf16[896,1792]{1,0:T(8,128)(2,1)}, u32[]{:S(2)}) copy-start(bf16[896,1792]{1,0:T(8,128)(2,1)} %out_ref.1) | copy-start | bytes 9633796
  19.3 6.4 %copy-start.9 = (f32[1792]{0:T(1024)S(1)}, f32[1792]{0:T(1024)}, u32[]{:S(2)}) copy-start(f32[1792]{0:T(1024)} %param.22) | copy-start | bytes 21508
  19.3 6.4 %copy-start.8 = (f32[1,256,8]{1,2,0:T(8,128)S(1)}, f32[1,256,8]{1,2,0:T(8,128)}, u32[]{:S(2)}) copy-start(f32[1,256,8]{1,2,0:T(8,128)} %param.15) | copy-start | bytes 24580
  19.3 10.1 %copy-start.2 = (bf16[1,256,1792]{2,1,0:T(8,128)(2,1)S(1)}, bf16[1,256,1792]{2,1,0:T(8,128)(2,1)}, u32[]{:S(2)}) copy-start(bf16[1,256,1792]{2,1,0:T(8,128)(2,1)} %param.13) | copy-start | bytes 2752516
  21.6 20.1 %collective-permute-start.4 = (bf16[232,1792]{1,0:T(8,128)(2,1)S(1)}, bf16[232,1792]{1,0:T(8,128)(2,1)S(1)}, u32[]{:S(2)}, u32[]{:S(2)}) collective-permute-start(bf16[232,1792]{1,0:T(8,128)(2,1)S(1)} %get-tuple-element.90), channel_id=1, source_target_pairs={{0,4},{1,5},{2,6},{3,7},{4,0},{5,1},{6,2},{7,3},{8,12},{9,13},{10,... | collective-permute-start | bytes 2494472 | tf_op jit(solution)/shard_map/ppermute | solution.py:90
  22.9 18.8 %collective-permute-start.3 = (bf16[224,1792]{1,0:T(8,128)(2,1)S(1)}, bf16[224,1792]{1,0:T(8,128)(2,1)S(1)}, u32[]{:S(2)}, u32[]{:S(2)}) collective-permute-start(bf16[224,1792]{1,0:T(8,128)(2,1)S(1)} %get-tuple-element.89), channel_id=1, source_target_pairs={{0,2},{1,3},{2,0},{3,1},{4,6},{5,7},{6,4},{7,5},{8,10},{9,11},{10,... | collective-permute-start | bytes 2408456 | tf_op jit(solution)/shard_map/ppermute | solution.py:90
  23.4 18.2 %collective-permute-start.5 = (bf16[216,1792]{1,0:T(8,128)(2,1)S(1)}, bf16[216,1792]{1,0:T(8,128)(2,1)S(1)}, u32[]{:S(2)}, u32[]{:S(2)}) collective-permute-start(bf16[216,1792]{1,0:T(8,128)(2,1)S(1)} %get-tuple-element.91), channel_id=1, source_target_pairs={{0,8},{1,9},{2,10},{3,11},{4,12},{5,13},{6,14},{7,15},{8,24},{9,25... | collective-permute-start | bytes 2322440 | tf_op jit(solution)/shard_map/ppermute | solution.py:90
  41.9 19.2 %collective-permute-start.8 = (bf16[240,1792]{1,0:T(8,128)(2,1)S(1)}, bf16[240,1792]{1,0:T(8,128)(2,1)S(1)}, u32[]{:S(2)}, u32[]{:S(2)}) collective-permute-start(bf16[240,1792]{1,0:T(8,128)(2,1)S(1)} %get-tuple-element.113), channel_id=1, source_target_pairs={{0,8},{1,9},{2,10},{3,11},{4,12},{5,13},{6,14},{7,15},{8,24},{9,25... | collective-permute-start | bytes 2580488 | tf_op jit(solution)/shard_map/ppermute | solution.py:90
  42.9 17.0 %collective-permute-start.6 = (bf16[224,1792]{1,0:T(8,128)(2,1)S(1)}, bf16[224,1792]{1,0:T(8,128)(2,1)S(1)}, u32[]{:S(2)}, u32[]{:S(2)}) collective-permute-start(bf16[224,1792]{1,0:T(8,128)(2,1)S(1)} %get-tuple-element.111), channel_id=1, source_target_pairs={{0,2},{1,3},{2,0},{3,1},{4,6},{5,7},{6,4},{7,5},{8,10},{9,11},{10,... | collective-permute-start | bytes 2408456 | tf_op jit(solution)/shard_map/ppermute | solution.py:90
  44.1 15.2 %collective-permute-start.7 = (bf16[208,1792]{1,0:T(8,128)(2,1)S(1)}, bf16[208,1792]{1,0:T(8,128)(2,1)S(1)}, u32[]{:S(2)}, u32[]{:S(2)}) collective-permute-start(bf16[208,1792]{1,0:T(8,128)(2,1)S(1)} %get-tuple-element.112), channel_id=1, source_target_pairs={{0,4},{1,5},{2,6},{3,7},{4,0},{5,1},{6,2},{7,3},{8,12},{9,13},{10,... | collective-permute-start | bytes 2236424 | tf_op jit(solution)/shard_map/ppermute | solution.py:90
  44.6 1.8 %collective-permute-start.9 = (bf16[128,1792]{1,0:T(8,128)(2,1)S(1)}, bf16[128,1792]{1,0:T(8,128)(2,1)S(1)}, u32[]{:S(2)}, u32[]{:S(2)}) collective-permute-start(bf16[128,1792]{1,0:T(8,128)(2,1)S(1)} %get-tuple-element.117), channel_id=1, source_target_pairs={{0,1},{1,0},{2,3},{3,2},{4,5},{5,4},{6,7},{7,6},{8,9},{9,8},{10,11... | collective-permute-start | bytes 1376264 | tf_op jit(solution)/shard_map/ppermute | solution.py:90
  44.6 2.5 %collective-permute-start.10 = (bf16[128,1792]{1,0:T(8,128)(2,1)S(1)}, bf16[128,1792]{1,0:T(8,128)(2,1)S(1)}, u32[]{:S(2)}, u32[]{:S(2)}) collective-permute-start(bf16[128,1792]{1,0:T(8,128)(2,1)S(1)} %get-tuple-element.118), channel_id=1, source_target_pairs={{0,1},{1,0},{2,3},{3,2},{4,5},{5,4},{6,7},{7,6},{8,9},{9,8},{10,11... | collective-permute-start | bytes 1376264 | tf_op jit(solution)/shard_map/ppermute | solution.py:90
  61.2 14.0 %collective-permute-start.13 = (bf16[144,1792]{1,0:T(8,128)(2,1)S(1)}, bf16[144,1792]{1,0:T(8,128)(2,1)S(1)}, u32[]{:S(2)}, u32[]{:S(2)}) collective-permute-start(bf16[144,1792]{1,0:T(8,128)(2,1)S(1)} %get-tuple-element.126), channel_id=1, source_target_pairs={{0,8},{1,9},{2,10},{3,11},{4,12},{5,13},{6,14},{7,15},{8,24},{9,25... | collective-permute-start | bytes 1548296 | tf_op jit(solution)/shard_map/ppermute | solution.py:90
  63.2 10.5 %collective-permute-start.11 = (bf16[96,1792]{1,0:T(8,128)(2,1)S(1)}, bf16[96,1792]{1,0:T(8,128)(2,1)S(1)}, u32[]{:S(2)}, u32[]{:S(2)}) collective-permute-start(bf16[96,1792]{1,0:T(8,128)(2,1)S(1)} %get-tuple-element.124), channel_id=1, source_target_pairs={{0,2},{1,3},{2,0},{3,1},{4,6},{5,7},{6,4},{7,5},{8,10},{9,11},{10,... | collective-permute-start | bytes 1032200 | tf_op jit(solution)/shard_map/ppermute | solution.py:90
  64.5 10.7 %collective-permute-start.12 = (bf16[96,1792]{1,0:T(8,128)(2,1)S(1)}, bf16[96,1792]{1,0:T(8,128)(2,1)S(1)}, u32[]{:S(2)}, u32[]{:S(2)}) collective-permute-start(bf16[96,1792]{1,0:T(8,128)(2,1)S(1)} %get-tuple-element.125), channel_id=1, source_target_pairs={{0,4},{1,5},{2,6},{3,7},{4,0},{5,1},{6,2},{7,3},{8,12},{9,13},{10,... | collective-permute-start | bytes 1032200 | tf_op jit(solution)/shard_map/ppermute | solution.py:90
  64.8 18.7 %collective-permute-start.14 = (bf16[96,1792]{1,0:T(8,128)(2,1)S(1)}, bf16[96,1792]{1,0:T(8,128)(2,1)S(1)}, u32[]{:S(2)}, u32[]{:S(2)}) collective-permute-start(bf16[96,1792]{1,0:T(8,128)(2,1)S(1)} %get-tuple-element.132), channel_id=1, source_target_pairs={{0,2},{1,3},{2,0},{3,1},{4,6},{5,7},{6,4},{7,5},{8,10},{9,11},{10,... | collective-permute-start | bytes 1032200 | tf_op jit(solution)/shard_map/ppermute | solution.py:90
  66.0 17.5 %collective-permute-start.15 = (bf16[96,1792]{1,0:T(8,128)(2,1)S(1)}, bf16[96,1792]{1,0:T(8,128)(2,1)S(1)}, u32[]{:S(2)}, u32[]{:S(2)}) collective-permute-start(bf16[96,1792]{1,0:T(8,128)(2,1)S(1)} %get-tuple-element.134), channel_id=1, source_target_pairs={{0,4},{1,5},{2,6},{3,7},{4,0},{5,1},{6,2},{7,3},{8,12},{9,13},{10,... | collective-permute-start | bytes 1032200 | tf_op jit(solution)/shard_map/ppermute | solution.py:90
  75.2 8.2 %collective-permute-start.18 = (bf16[72,1792]{1,0:T(8,128)(2,1)S(1)}, bf16[72,1792]{1,0:T(8,128)(2,1)S(1)}, u32[]{:S(2)}, u32[]{:S(2)}) collective-permute-start(bf16[72,1792]{1,0:T(8,128)(2,1)S(1)} %get-tuple-element.138), channel_id=1, source_target_pairs={{0,8},{1,9},{2,10},{3,11},{4,12},{5,13},{6,14},{7,15},{8,24},{9,25... | collective-permute-start | bytes 774152 | tf_op jit(solution)/shard_map/ppermute | solution.py:90
  77.4 5.4 %collective-permute-start.16 = (bf16[48,1792]{1,0:T(8,128)(2,1)S(1)}, bf16[48,1792]{1,0:T(8,128)(2,1)S(1)}, u32[]{:S(2)}, u32[]{:S(2)}) collective-permute-start(bf16[48,1792]{1,0:T(8,128)(2,1)S(1)} %get-tuple-element.136), channel_id=1, source_target_pairs={{0,2},{1,3},{2,0},{3,1},{4,6},{5,7},{6,4},{7,5},{8,10},{9,11},{10,... | collective-permute-start | bytes 516104 | tf_op jit(solution)/shard_map/ppermute | solution.py:90
  78.1 5.4 %collective-permute-start.17 = (bf16[48,1792]{1,0:T(8,128)(2,1)S(1)}, bf16[48,1792]{1,0:T(8,128)(2,1)S(1)}, u32[]{:S(2)}, u32[]{:S(2)}) collective-permute-start(bf16[48,1792]{1,0:T(8,128)(2,1)S(1)} %get-tuple-element.137), channel_id=1, source_target_pairs={{0,4},{1,5},{2,6},{3,7},{4,0},{5,1},{6,2},{7,3},{8,12},{9,13},{10,... | collective-permute-start | bytes 516104 | tf_op jit(solution)/shard_map/ppermute | solution.py:90
  84.5 2.5 %collective-permute-start.19 = (bf16[256,1792]{1,0:T(8,128)(2,1)S(1)}, bf16[256,1792]{1,0:T(8,128)(2,1)S(1)}, u32[]{:S(2)}, u32[]{:S(2)}) collective-permute-start(bf16[256,1792]{1,0:T(8,128)(2,1)S(1)} %finish_other.1), channel_id=1, source_target_pairs={{0,1},{1,0},{2,3},{3,2},{4,5},{5,4},{6,7},{7,6},{8,9},{9,8},{10,11... | collective-permute-start | bytes 2752520 | tf_op jit(solution)/shard_map/ppermute | solution.py:90

commit v16 on v15

--- a/solution.py
+++ b/solution.py
@@ -103,7 +103,7 @@
 
 
 def next_plane(array):
-    return permute(array, lambda i: i ^ (16 if i // 8 in (1, 2) else 8))
+    return permute(array, lambda i: i ^ (8 if i // 8 in (1, 2) else 16))
 
 
 def together(*arrays):

time: 88.7 us -> 87.9 us (level)
  waiting for transfers between devices: 34.1 us -> 28.8 us
  starting transfers between devices: 22.5 us -> 27.1 us
    ppermute x20, waiting for transfers between devices: 34.1 us -> 28.8 us  [permute(): return lax.ppermute(array, 'req', [(i, target(i)) for i in range(count)])]
    ppermute x20, starting transfers between devices: 22.5 us -> 27.1 us  [permute(): return lax.ppermute(array, 'req', [(i, target(i)) for i in range(count)])]
  transfers between devices with their start and end apart: 20 -> 20, of which waited for: 12 -> 13; matrix products, arithmetic and copies ran while one was open for 1% -> 1% of each run, Pallas kernels for 21% -> 21%
where the time goes in v16:
time: 87.9 us; the launch traced here: 87.5 us
  waiting for transfers between devices  28.8 us (33%)
  starting transfers between devices  27.1 us (31%)
  Pallas kernels  23.6 us (27%)
  local copies, waits for them, and re-layouts  6.61 us (8%)
  between operations  1.45 us (2%)
    ppermute x20, waiting for transfers between devices, permute(): return lax.ppermute(array, 'req', [(i, target(i)) for i in range(count)])  28.8 us
    ppermute x20, starting transfers between devices, permute(): return lax.ppermute(array, 'req', [(i, target(i)) for i in range(count)])  27.1 us
    pallas_call x14, Pallas kernels, kernel_call(): pl.pallas_call(body, out_shape=out_shape, in_specs=specs or vmem(len(oper...  23.6 us
    unnamed x20, local copies, waits for them, and re-layouts  5.89 us
  transfers between devices with their start and end apart: 20, of which 13 were waited for; matrix products, arithmetic and copies ran while one was open for 1% of the time, Pallas kernels for 21%

profile of v16, /device:TPU:0, one launch (start us, length us, event | category | flops | bytes accessed | tf_op | source)
XLA Modules:
  0.0 87.5 jit_solution(6151992652785418312)
XLA Ops:
  0.6 2.2 %shard.1 = (bf16[168,1792]{1,0:T(8,128)(2,1)}, bf16[144,1792]{1,0:T(8,128)(2,1)}) custom-call(bf16[56,1792]{1,0:T(8,128)(2,1)} %bitcast.17, bf16[56,1792]{1,0:T(8,128)(2,1)} %bitcast.18, bf16[56,1792]{1,0:T(8,128)(2,1)} %bitcast.19), custom_call_target="tpu_custom_call" | custom-call | flops 1000 | bytes 1000 | tf_op jit(solution)/shard_map/shard/pallas_call | solution.py:124
  2.8 3.0 %collective-permute-start = (bf16[168,1792]{1,0:T(8,128)(2,1)}, bf16[168,1792]{1,0:T(8,128)(2,1)S(1)}, u32[]{:S(2)}, u32[]{:S(2)}) collective-permute-start(bf16[168,1792]{1,0:T(8,128)(2,1)} %get-tuple-element.78.refs_0_), channel_id=1, source_target_pairs={{0,2},{1,3},{2,0},{3,1},{4,6},{5,7},{6,4},{7,5},{8,10},{9,11},{10,... | collective-permute-start | bytes 1806344 | tf_op jit(solution)/shard_map/ppermute | solution.py:90
  5.8 1.5 %collective-permute-start.1 = (bf16[168,1792]{1,0:T(8,128)(2,1)}, bf16[168,1792]{1,0:T(8,128)(2,1)S(1)}, u32[]{:S(2)}, u32[]{:S(2)}) collective-permute-start(bf16[168,1792]{1,0:T(8,128)(2,1)} %get-tuple-element.78.refs_0_), channel_id=1, source_target_pairs={{0,4},{1,5},{2,6},{3,7},{4,0},{5,1},{6,2},{7,3},{8,12},{9,13},{10,... | collective-permute-start | bytes 1806344 | tf_op jit(solution)/shard_map/ppermute | solution.py:90
  7.4 2.6 %collective-permute-start.2 = (bf16[144,1792]{1,0:T(8,128)(2,1)}, bf16[144,1792]{1,0:T(8,128)(2,1)S(1)}, u32[]{:S(2)}, u32[]{:S(2)}) collective-permute-start(bf16[144,1792]{1,0:T(8,128)(2,1)} %get-tuple-element.79), channel_id=1, source_target_pairs={{0,16},{1,17},{2,18},{3,19},{4,20},{5,21},{6,22},{7,23},{8,0},{9,1... | collective-permute-start | bytes 1548296 | tf_op jit(solution)/shard_map/ppermute | solution.py:90
  10.0 0.7 broadcast_in_dim.16.gain_ref
  10.7 1.2 %copy-done.1 = bf16[1,256,1792]{2,1,0:T(8,128)(2,1)S(1)} copy-done((bf16[1,256,1792]{2,1,0:T(8,128)(2,1)S(1)}, bf16[1,256,1792]{2,1,0:T(8,128)(2,1)}, u32[]{:S(2)}) %copy-start.1) | copy-done | bytes 917528
  11.9 1.9 %copy-done.3 = bf16[1792,896]{1,0:T(8,128)(2,1)S(1)} copy-done((bf16[1792,896]{1,0:T(8,128)(2,1)S(1)}, bf16[1792,896]{1,0:T(8,128)(2,1)}, u32[]{:S(2)}) %copy-start.3) | copy-done | bytes 3211288
  13.8 1.0 %copy-done.5 = bf16[1792,128]{1,0:T(8,128)(2,1)S(1)} copy-done((bf16[1792,128]{1,0:T(8,128)(2,1)S(1)}, bf16[1792,128]{1,0:T(8,128)(2,1)}, u32[]{:S(2)}) %copy-start.5) | copy-done | bytes 458776
  14.8 1.0 %copy-done.6 = bf16[1792,128]{1,0:T(8,128)(2,1)S(1)} copy-done((bf16[1792,128]{1,0:T(8,128)(2,1)S(1)}, bf16[1792,128]{1,0:T(8,128)(2,1)}, u32[]{:S(2)}) %copy-start.6) | copy-done | bytes 458776
  15.8 0.7 copy-done.7
  16.5 3.7 %project.1 = (bf16[256,128]{1,0:T(8,128)(2,1)S(1)}, bf16[256,128]{1,0:T(8,128)(2,1)S(1)}, bf16[256,896]{1,0:T(8,128)(2,1)S(1)}) custom-call(bf16[256,1792]{1,0:T(8,128)(2,1)S(1)} %bitcast.13, bf16[16,1792]{1,0:T(8,128)(2,1)S(1)} %broadcast_in_dim.15.edge_ref, f32[1,1792]{1,0:T(1,128)S(1)} %broadcast_in_dim.16.gain_ref, f32[3,1792]{1,0:T(4,128)S(1)} %copy-done.7, ...), custom_call_target="tpu_custom_call" | custom-call | flops 1000 | bytes 1000 | tf_op jit(solution)/shard_map/project/pallas_call | solution.py:124
  20.3 0.4 collective-permute-done.2.refs_3_
  20.7 0.4 collective-permute-done.1.refs_2_
  21.1 0.2 collect_second.1
  21.3 1.6 %collective-permute-start.4 = (bf16[232,1792]{1,0:T(8,128)(2,1)S(1)}, bf16[232,1792]{1,0:T(8,128)(2,1)S(1)}, u32[]{:S(2)}, u32[]{:S(2)}) collective-permute-start(bf16[232,1792]{1,0:T(8,128)(2,1)S(1)} %get-tuple-element.90), channel_id=1, source_target_pairs={{0,4},{1,5},{2,6},{3,7},{4,0},{5,1},{6,2},{7,3},{8,12},{9,13},{10,... | collective-permute-start | bytes 2494472 | tf_op jit(solution)/shard_map/ppermute | solution.py:90
  22.9 0.5 collective-permute-start.3
  23.4 2.6 %collective-permute-start.5 = (bf16[216,1792]{1,0:T(8,128)(2,1)S(1)}, bf16[216,1792]{1,0:T(8,128)(2,1)S(1)}, u32[]{:S(2)}, u32[]{:S(2)}) collective-permute-start(bf16[216,1792]{1,0:T(8,128)(2,1)S(1)} %get-tuple-element.91), channel_id=1, source_target_pairs={{0,16},{1,17},{2,18},{3,19},{4,20},{5,21},{6,22},{7,23},{8,0},{9,1... | collective-permute-start | bytes 2322440 | tf_op jit(solution)/shard_map/ppermute | solution.py:90
  26.7 3.7 %attend.1 = (f32[256,896]{1,0:T(8,128)S(1)}, f32[256,8]{1,0:T(8,128)S(1)}, f32[273,1,896]{2,1,0:T(1,128)}, f32[8,273]{1,0:T(8,128)}) custom-call(s32[1]{0:T(128)S(6)} %copy.23.count_ref, f32[8,256]{1,0:T(8,128)S(1)} %bitcast.15, bf16[256,128]{1,0:T(8,128)(2,1)S(1)} %get-tuple-element.95.queries_ref, bf16[256,128]{1,0:T(8,128)(2,1)S(1)} %get-tuple-element.96.keys_ref, ...), custom_call_target="tpu_custom_call" | custom-call | flops 1000 | bytes 1000 | tf_op jit(solution)/shard_map/attend/pallas_call | solution.py:124
  30.4 2.6 %mix.1 = (bf16[256,1792]{1,0:T(8,128)(2,1)S(1)}, bf16[256,1792]{1,0:T(8,128)(2,1)S(1)}) custom-call(f32[256,896]{1,0:T(8,128)S(1)} %get-tuple-element.98.numer_ref, f32[256,8]{1,0:T(8,128)S(1)} %get-tuple-element.99.denom_ref, bf16[256,1792]{1,0:T(8,128)(2,1)S(1)} %bitcast.14, bf16[896,1792]{1,0:T(8,128)(2,1)S(1)} %copy-done.4, ...), custom_call_target="tpu_custom_call" | custom-call | flops 1000 | bytes 1000 | tf_op jit(solution)/shard_map/mix/pallas_call | solution.py:124
  33.0 7.9 %collective-permute-done.5.refs_2_.refs_6_.refs_4_ = bf16[216,1792]{1,0:T(8,128)(2,1)S(1)} collective-permute-done((bf16[216,1792]{1,0:T(8,128)(2,1)S(1)}, bf16[216,1792]{1,0:T(8,128)(2,1)S(1)}, u32[]{:S(2)}, u32[]{:S(2)}) %collective-permute-start.5) | collective-permute-done | bytes 774176 | tf_op jit(solution)/shard_map/ppermute | solution.py:90
  40.8 0.2 collective-permute-done.3.refs_0_.refs_4_
  41.0 0.2 collect_third.1
  41.2 3.3 %collective-permute-start.8 = (bf16[240,1792]{1,0:T(8,128)(2,1)S(1)}, bf16[240,1792]{1,0:T(8,128)(2,1)S(1)}, u32[]{:S(2)}, u32[]{:S(2)}) collective-permute-start(bf16[240,1792]{1,0:T(8,128)(2,1)S(1)} %get-tuple-element.113), channel_id=1, source_target_pairs={{0,16},{1,17},{2,18},{3,19},{4,20},{5,21},{6,22},{7,23},{8,0},{9,1... | collective-permute-start | bytes 2580488 | tf_op jit(solution)/shard_map/ppermute | solution.py:90
  44.5 1.4 %collective-permute-start.6 = (bf16[224,1792]{1,0:T(8,128)(2,1)S(1)}, bf16[224,1792]{1,0:T(8,128)(2,1)S(1)}, u32[]{:S(2)}, u32[]{:S(2)}) collective-permute-start(bf16[224,1792]{1,0:T(8,128)(2,1)S(1)} %get-tuple-element.111), channel_id=1, source_target_pairs={{0,2},{1,3},{2,0},{3,1},{4,6},{5,7},{6,4},{7,5},{8,10},{9,11},{10,... | collective-permute-start | bytes 2408456 | tf_op jit(solution)/shard_map/ppermute | solution.py:90
  45.9 0.5 collective-permute-start.7
  46.4 0.5 collective-permute-start.10
  47.0 1.3 %collective-permute-done.9.refs_0_ = bf16[128,1792]{1,0:T(8,128)(2,1)S(1)} collective-permute-done((bf16[128,1792]{1,0:T(8,128)(2,1)S(1)}, bf16[128,1792]{1,0:T(8,128)(2,1)S(1)}, u32[]{:S(2)}, u32[]{:S(2)}) %collective-permute-start.9) | collective-permute-done | bytes 458784 | tf_op jit(solution)/shard_map/ppermute | solution.py:90
  48.3 0.7 collective-permute-done.10.refs_1_
  49.0 3.2 %accumulate_second.1 = (f32[256,1792]{1,0:T(8,128)S(1)}, f32[256,1792]{1,0:T(8,128)S(1)}) custom-call(bf16[168,1792]{1,0:T(8,128)(2,1)S(1)} %copy-done, bf16[168,1792]{1,0:T(8,128)(2,1)S(1)} %collective-permute-done.refs_1_, bf16[168,1792]{1,0:T(8,128)(2,1)S(1)} %collective-permute-done.1.refs_2_, bf16[144,1792]{1,0:T(8,128)(2,1)S(1)} %collective-permute-done.2.refs_3_, ...), custom_call_target="tpu_custom_call" | custom-call | flops 1000 | bytes 1000 | tf_op jit(solution)/shard_map/accumulate_second/pallas_call | solution.py:124
  52.2 8.9 %collective-permute-done.7.refs_1_.refs_6_ = bf16[208,1792]{1,0:T(8,128)(2,1)S(1)} collective-permute-done((bf16[208,1792]{1,0:T(8,128)(2,1)S(1)}, bf16[208,1792]{1,0:T(8,128)(2,1)S(1)}, u32[]{:S(2)}, u32[]{:S(2)}) %collective-permute-start.7) | collective-permute-done | bytes 745504 | tf_op jit(solution)/shard_map/ppermute | solution.py:90
  61.1 0.1 collective-permute-done.6.refs_0_.refs_5_
  61.4 2.6 %collective-permute-start.13 = (bf16[144,1792]{1,0:T(8,128)(2,1)S(1)}, bf16[144,1792]{1,0:T(8,128)(2,1)S(1)}, u32[]{:S(2)}, u32[]{:S(2)}) collective-permute-start(bf16[144,1792]{1,0:T(8,128)(2,1)S(1)} %get-tuple-element.126), channel_id=1, source_target_pairs={{0,16},{1,17},{2,18},{3,19},{4,20},{5,21},{6,22},{7,23},{8,0},{9,1... | collective-permute-start | bytes 1548296 | tf_op jit(solution)/shard_map/ppermute | solution.py:90
  64.0 1.4 %collective-permute-start.11 = (bf16[96,1792]{1,0:T(8,128)(2,1)S(1)}, bf16[96,1792]{1,0:T(8,128)(2,1)S(1)}, u32[]{:S(2)}, u32[]{:S(2)}) collective-permute-start(bf16[96,1792]{1,0:T(8,128)(2,1)S(1)} %get-tuple-element.124), channel_id=1, source_target_pairs={{0,2},{1,3},{2,0},{3,1},{4,6},{5,7},{6,4},{7,5},{8,10},{9,11},{10,... | collective-permute-start | bytes 1032200 | tf_op jit(solution)/shard_map/ppermute | solution.py:90
  65.4 0.4 collective-permute-start.12
  65.7 1.1 %collective-permute-start.14 = (bf16[96,1792]{1,0:T(8,128)(2,1)S(1)}, bf16[96,1792]{1,0:T(8,128)(2,1)S(1)}, u32[]{:S(2)}, u32[]{:S(2)}) collective-permute-start(bf16[96,1792]{1,0:T(8,128)(2,1)S(1)} %get-tuple-element.132), channel_id=1, source_target_pairs={{0,2},{1,3},{2,0},{3,1},{4,6},{5,7},{6,4},{7,5},{8,10},{9,11},{10,... | collective-permute-start | bytes 1032200 | tf_op jit(solution)/shard_map/ppermute | solution.py:90
  66.8 1.3 %collective-permute-start.15 = (bf16[96,1792]{1,0:T(8,128)(2,1)S(1)}, bf16[96,1792]{1,0:T(8,128)(2,1)S(1)}, u32[]{:S(2)}, u32[]{:S(2)}) collective-permute-start(bf16[96,1792]{1,0:T(8,128)(2,1)S(1)} %get-tuple-element.134), channel_id=1, source_target_pairs={{0,4},{1,5},{2,6},{3,7},{4,0},{5,1},{6,2},{7,3},{8,12},{9,13},{10,... | collective-permute-start | bytes 1032200 | tf_op jit(solution)/shard_map/ppermute | solution.py:90
  68.1 3.9 %accumulate_third.1 = (f32[256,1792]{1,0:T(8,128)S(1)}, f32[256,1792]{1,0:T(8,128)S(1)}) custom-call(bf16[168,1792]{1,0:T(8,128)(2,1)S(1)} %copy-done, bf16[168,1792]{1,0:T(8,128)(2,1)S(1)} %collective-permute-done.refs_1_, bf16[168,1792]{1,0:T(8,128)(2,1)S(1)} %collective-permute-done.1.refs_2_, ...), custom_call_target="tpu_custom_call", output_to_operand_aliasing={{0}: (10, {}), {1}: (11, {})} | custom-call | flops 1000 | bytes 1000 | tf_op jit(solution)/shard_map/accumulate_third/pallas_call | solution.py:124
  72.0 2.7 %collective-permute-done.11.refs_0_ = bf16[96,1792]{1,0:T(8,128)(2,1)S(1)} collective-permute-done((bf16[96,1792]{1,0:T(8,128)(2,1)S(1)}, bf16[96,1792]{1,0:T(8,128)(2,1)S(1)}, u32[]{:S(2)}, u32[]{:S(2)}) %collective-permute-start.11) | collective-permute-done | bytes 344096 | tf_op jit(solution)/shard_map/ppermute | solution.py:90
  74.6 1.1 %collective-permute-done.12.refs_1_.refs_2_ = bf16[96,1792]{1,0:T(8,128)(2,1)S(1)} collective-permute-done((bf16[96,1792]{1,0:T(8,128)(2,1)S(1)}, bf16[96,1792]{1,0:T(8,128)(2,1)S(1)}, u32[]{:S(2)}, u32[]{:S(2)}) %collective-permute-start.12) | collective-permute-done | bytes 344096 | tf_op jit(solution)/shard_map/ppermute | solution.py:90
  75.8 0.4 collective-permute-start.18
  76.2 1.1 %collective-permute-start.16 = (bf16[48,1792]{1,0:T(8,128)(2,1)S(1)}, bf16[48,1792]{1,0:T(8,128)(2,1)S(1)}, u32[]{:S(2)}, u32[]{:S(2)}) collective-permute-start(bf16[48,1792]{1,0:T(8,128)(2,1)S(1)} %get-tuple-element.136), channel_id=1, source_target_pairs={{0,2},{1,3},{2,0},{3,1},{4,6},{5,7},{6,4},{7,5},{8,10},{9,11},{10,... | collective-permute-start | bytes 516104 | tf_op jit(solution)/shard_map/ppermute | solution.py:90
  77.3 1.3 %collective-permute-start.17 = (bf16[48,1792]{1,0:T(8,128)(2,1)S(1)}, bf16[48,1792]{1,0:T(8,128)(2,1)S(1)}, u32[]{:S(2)}, u32[]{:S(2)}) collective-permute-start(bf16[48,1792]{1,0:T(8,128)(2,1)S(1)} %get-tuple-element.137), channel_id=1, source_target_pairs={{0,4},{1,5},{2,6},{3,7},{4,0},{5,1},{6,2},{7,3},{8,12},{9,13},{10,... | collective-permute-start | bytes 516104 | tf_op jit(solution)/shard_map/ppermute | solution.py:90
  78.5 3.1 %collective-permute-done.16.refs_5_ = bf16[48,1792]{1,0:T(8,128)(2,1)S(1)} collective-permute-done((bf16[48,1792]{1,0:T(8,128)(2,1)S(1)}, bf16[48,1792]{1,0:T(8,128)(2,1)S(1)}, u32[]{:S(2)}, u32[]{:S(2)}) %collective-permute-start.16) | collective-permute-done | bytes 172064 | tf_op jit(solution)/shard_map/ppermute | solution.py:90
  81.6 1.1 %collective-permute-done.17.refs_6_ = bf16[48,1792]{1,0:T(8,128)(2,1)S(1)} collective-permute-done((bf16[48,1792]{1,0:T(8,128)(2,1)S(1)}, bf16[48,1792]{1,0:T(8,128)(2,1)S(1)}, u32[]{:S(2)}, u32[]{:S(2)}) %collective-permute-start.17) | collective-permute-done | bytes 172064 | tf_op jit(solution)/shard_map/ppermute | solution.py:90
  82.7 1.0 %finish_other.1 = bf16[256,1792]{1,0:T(8,128)(2,1)S(1)} custom-call(bf16[96,1792]{1,0:T(8,128)(2,1)S(1)} %collective-permute-done.11.refs_0_, bf16[96,1792]{1,0:T(8,128)(2,1)S(1)} %collective-permute-done.14.refs_1_, bf16[96,1792]{1,0:T(8,128)(2,1)S(1)} %collective-permute-done.12.refs_1_.refs_2_, bf16[96,1792]{1,0:T(8,128)(2,1)S(1)} %collective-permute-done.15.refs_3_, ...), custom_call_target="tpu_custom_call" | custom-call | flops 1000 | bytes 1000 | tf_op jit(solution)/shard_map/finish_other/pallas_call | solution.py:124
  83.8 1.4 %finish_own.1.kept_ref = f32[256,1792]{1,0:T(8,128)S(1)} custom-call(bf16[96,1792]{1,0:T(8,128)(2,1)S(1)} %collective-permute-done.11.refs_0_, bf16[96,1792]{1,0:T(8,128)(2,1)S(1)} %collective-permute-done.14.refs_1_, bf16[96,1792]{1,0:T(8,128)(2,1)S(1)} %collective-permute-done.12.refs_1_.refs_2_, ...), custom_call_target="tpu_custom_call", output_to_operand_aliasing={{}: (9, {})} | custom-call | flops 1000 | bytes 1000 | tf_op jit(solution)/shard_map/finish_own/pallas_call | solution.py:124
  85.2 1.1 %collective-permute-done.19.given_ref = bf16[256,1792]{1,0:T(8,128)(2,1)S(1)} collective-permute-done((bf16[256,1792]{1,0:T(8,128)(2,1)S(1)}, bf16[256,1792]{1,0:T(8,128)(2,1)S(1)}, u32[]{:S(2)}, u32[]{:S(2)}) %collective-permute-start.19) | collective-permute-done | bytes 917536 | tf_op jit(solution)/shard_map/ppermute | solution.py:90
  86.3 1.2 %final.1 = bf16[256,1792]{1,0:T(8,128)(2,1)} custom-call(s32[1]{0:T(128)S(6)} %copy.23.count_ref, f32[256,1792]{1,0:T(8,128)S(1)} %finish_own.1.kept_ref, bf16[256,1792]{1,0:T(8,128)(2,1)S(1)} %collective-permute-done.19.given_ref), custom_call_target="tpu_custom_call" | custom-call | flops 1000 | bytes 1000 | tf_op jit(solution)/shard_map/final/pallas_call | solution.py:124
  (29 shorter events, 0.4 us)
Async XLA Ops:
  2.8 17.9 %collective-permute-start = (bf16[168,1792]{1,0:T(8,128)(2,1)}, bf16[168,1792]{1,0:T(8,128)(2,1)S(1)}, u32[]{:S(2)}, u32[]{:S(2)}) collective-permute-start(bf16[168,1792]{1,0:T(8,128)(2,1)} %get-tuple-element.78.refs_0_), channel_id=1, source_target_pairs={{0,2},{1,3},{2,0},{3,1},{4,6},{5,7},{6,4},{7,5},{8,10},{9,11},{10,... | collective-permute-start | bytes 1806344 | tf_op jit(solution)/shard_map/ppermute | solution.py:90
  5.8 15.3 %collective-permute-start.1 = (bf16[168,1792]{1,0:T(8,128)(2,1)}, bf16[168,1792]{1,0:T(8,128)(2,1)S(1)}, u32[]{:S(2)}, u32[]{:S(2)}) collective-permute-start(bf16[168,1792]{1,0:T(8,128)(2,1)} %get-tuple-element.78.refs_0_), channel_id=1, source_target_pairs={{0,4},{1,5},{2,6},{3,7},{4,0},{5,1},{6,2},{7,3},{8,12},{9,13},{10,... | collective-permute-start | bytes 1806344 | tf_op jit(solution)/shard_map/ppermute | solution.py:90
  7.4 13.4 %collective-permute-start.2 = (bf16[144,1792]{1,0:T(8,128)(2,1)}, bf16[144,1792]{1,0:T(8,128)(2,1)S(1)}, u32[]{:S(2)}, u32[]{:S(2)}) collective-permute-start(bf16[144,1792]{1,0:T(8,128)(2,1)} %get-tuple-element.79), channel_id=1, source_target_pairs={{0,16},{1,17},{2,18},{3,19},{4,20},{5,21},{6,22},{7,23},{8,0},{9,1... | collective-permute-start | bytes 1548296 | tf_op jit(solution)/shard_map/ppermute | solution.py:90
  10.7 1.2 %copy-start.1 = (bf16[1,256,1792]{2,1,0:T(8,128)(2,1)S(1)}, bf16[1,256,1792]{2,1,0:T(8,128)(2,1)}, u32[]{:S(2)}) copy-start(bf16[1,256,1792]{2,1,0:T(8,128)(2,1)} %param.13) | copy-start | bytes 2752516
  11.8 1.9 %copy-start.3 = (bf16[1792,896]{1,0:T(8,128)(2,1)S(1)}, bf16[1792,896]{1,0:T(8,128)(2,1)}, u32[]{:S(2)}) copy-start(bf16[1792,896]{1,0:T(8,128)(2,1)} %value_ref.1) | copy-start | bytes 9633796
  13.8 1.0 %copy-start.5 = (bf16[1792,128]{1,0:T(8,128)(2,1)S(1)}, bf16[1792,128]{1,0:T(8,128)(2,1)}, u32[]{:S(2)}) copy-start(bf16[1792,128]{1,0:T(8,128)(2,1)} %query_ref.1) | copy-start | bytes 1376260
  14.8 1.0 %copy-start.6 = (bf16[1792,128]{1,0:T(8,128)(2,1)S(1)}, bf16[1792,128]{1,0:T(8,128)(2,1)}, u32[]{:S(2)}) copy-start(bf16[1792,128]{1,0:T(8,128)(2,1)} %key_ref.1) | copy-start | bytes 1376260
  15.8 0.7 copy-start.7
  16.5 4.6 %copy-start = (bf16[168,1792]{1,0:T(8,128)(2,1)S(1)}, bf16[168,1792]{1,0:T(8,128)(2,1)}, u32[]{:S(2)}) copy-start(bf16[168,1792]{1,0:T(8,128)(2,1)} %get-tuple-element.78.refs_0_) | copy-start | bytes 1806340
  16.5 13.8 %copy-start.4 = (bf16[896,1792]{1,0:T(8,128)(2,1)S(1)}, bf16[896,1792]{1,0:T(8,128)(2,1)}, u32[]{:S(2)}) copy-start(bf16[896,1792]{1,0:T(8,128)(2,1)} %out_ref.1) | copy-start | bytes 9633796
  20.3 6.4 %copy-start.9 = (f32[1792]{0:T(1024)S(1)}, f32[1792]{0:T(1024)}, u32[]{:S(2)}) copy-start(f32[1792]{0:T(1024)} %param.22) | copy-start | bytes 21508
  20.3 6.4 %copy-start.8 = (f32[1,256,8]{1,2,0:T(8,128)S(1)}, f32[1,256,8]{1,2,0:T(8,128)}, u32[]{:S(2)}) copy-start(f32[1,256,8]{1,2,0:T(8,128)} %param.15) | copy-start | bytes 24580
  20.3 10.1 %copy-start.2 = (bf16[1,256,1792]{2,1,0:T(8,128)(2,1)S(1)}, bf16[1,256,1792]{2,1,0:T(8,128)(2,1)}, u32[]{:S(2)}) copy-start(bf16[1,256,1792]{2,1,0:T(8,128)(2,1)} %param.13) | copy-start | bytes 2752516
  21.3 19.8 %collective-permute-start.4 = (bf16[232,1792]{1,0:T(8,128)(2,1)S(1)}, bf16[232,1792]{1,0:T(8,128)(2,1)S(1)}, u32[]{:S(2)}, u32[]{:S(2)}) collective-permute-start(bf16[232,1792]{1,0:T(8,128)(2,1)S(1)} %get-tuple-element.90), channel_id=1, source_target_pairs={{0,4},{1,5},{2,6},{3,7},{4,0},{5,1},{6,2},{7,3},{8,12},{9,13},{10,... | collective-permute-start | bytes 2494472 | tf_op jit(solution)/shard_map/ppermute | solution.py:90
  22.9 18.2 %collective-permute-start.3 = (bf16[224,1792]{1,0:T(8,128)(2,1)S(1)}, bf16[224,1792]{1,0:T(8,128)(2,1)S(1)}, u32[]{:S(2)}, u32[]{:S(2)}) collective-permute-start(bf16[224,1792]{1,0:T(8,128)(2,1)S(1)} %get-tuple-element.89), channel_id=1, source_target_pairs={{0,2},{1,3},{2,0},{3,1},{4,6},{5,7},{6,4},{7,5},{8,10},{9,11},{10,... | collective-permute-start | bytes 2408456 | tf_op jit(solution)/shard_map/ppermute | solution.py:90
  23.4 17.4 %collective-permute-start.5 = (bf16[216,1792]{1,0:T(8,128)(2,1)S(1)}, bf16[216,1792]{1,0:T(8,128)(2,1)S(1)}, u32[]{:S(2)}, u32[]{:S(2)}) collective-permute-start(bf16[216,1792]{1,0:T(8,128)(2,1)S(1)} %get-tuple-element.91), channel_id=1, source_target_pairs={{0,16},{1,17},{2,18},{3,19},{4,20},{5,21},{6,22},{7,23},{8,0},{9,1... | collective-permute-start | bytes 2322440 | tf_op jit(solution)/shard_map/ppermute | solution.py:90
  41.2 20.0 %collective-permute-start.8 = (bf16[240,1792]{1,0:T(8,128)(2,1)S(1)}, bf16[240,1792]{1,0:T(8,128)(2,1)S(1)}, u32[]{:S(2)}, u32[]{:S(2)}) collective-permute-start(bf16[240,1792]{1,0:T(8,128)(2,1)S(1)} %get-tuple-element.113), channel_id=1, source_target_pairs={{0,16},{1,17},{2,18},{3,19},{4,20},{5,21},{6,22},{7,23},{8,0},{9,1... | collective-permute-start | bytes 2580488 | tf_op jit(solution)/shard_map/ppermute | solution.py:90
  44.5 16.7 %collective-permute-start.6 = (bf16[224,1792]{1,0:T(8,128)(2,1)S(1)}, bf16[224,1792]{1,0:T(8,128)(2,1)S(1)}, u32[]{:S(2)}, u32[]{:S(2)}) collective-permute-start(bf16[224,1792]{1,0:T(8,128)(2,1)S(1)} %get-tuple-element.111), channel_id=1, source_target_pairs={{0,2},{1,3},{2,0},{3,1},{4,6},{5,7},{6,4},{7,5},{8,10},{9,11},{10,... | collective-permute-start | bytes 2408456 | tf_op jit(solution)/shard_map/ppermute | solution.py:90
  45.9 15.2 %collective-permute-start.7 = (bf16[208,1792]{1,0:T(8,128)(2,1)S(1)}, bf16[208,1792]{1,0:T(8,128)(2,1)S(1)}, u32[]{:S(2)}, u32[]{:S(2)}) collective-permute-start(bf16[208,1792]{1,0:T(8,128)(2,1)S(1)} %get-tuple-element.112), channel_id=1, source_target_pairs={{0,4},{1,5},{2,6},{3,7},{4,0},{5,1},{6,2},{7,3},{8,12},{9,13},{10,... | collective-permute-start | bytes 2236424 | tf_op jit(solution)/shard_map/ppermute | solution.py:90
  46.4 1.8 %collective-permute-start.9 = (bf16[128,1792]{1,0:T(8,128)(2,1)S(1)}, bf16[128,1792]{1,0:T(8,128)(2,1)S(1)}, u32[]{:S(2)}, u32[]{:S(2)}) collective-permute-start(bf16[128,1792]{1,0:T(8,128)(2,1)S(1)} %get-tuple-element.117), channel_id=1, source_target_pairs={{0,1},{1,0},{2,3},{3,2},{4,5},{5,4},{6,7},{7,6},{8,9},{9,8},{10,11... | collective-permute-start | bytes 1376264 | tf_op jit(solution)/shard_map/ppermute | solution.py:90
  46.4 2.5 %collective-permute-start.10 = (bf16[128,1792]{1,0:T(8,128)(2,1)S(1)}, bf16[128,1792]{1,0:T(8,128)(2,1)S(1)}, u32[]{:S(2)}, u32[]{:S(2)}) collective-permute-start(bf16[128,1792]{1,0:T(8,128)(2,1)S(1)} %get-tuple-element.118), channel_id=1, source_target_pairs={{0,1},{1,0},{2,3},{3,2},{4,5},{5,4},{6,7},{7,6},{8,9},{9,8},{10,11... | collective-permute-start | bytes 1376264 | tf_op jit(solution)/shard_map/ppermute | solution.py:90
  61.4 14.4 %collective-permute-start.13 = (bf16[144,1792]{1,0:T(8,128)(2,1)S(1)}, bf16[144,1792]{1,0:T(8,128)(2,1)S(1)}, u32[]{:S(2)}, u32[]{:S(2)}) collective-permute-start(bf16[144,1792]{1,0:T(8,128)(2,1)S(1)} %get-tuple-element.126), channel_id=1, source_target_pairs={{0,16},{1,17},{2,18},{3,19},{4,20},{5,21},{6,22},{7,23},{8,0},{9,1... | collective-permute-start | bytes 1548296 | tf_op jit(solution)/shard_map/ppermute | solution.py:90
  64.0 10.6 %collective-permute-start.11 = (bf16[96,1792]{1,0:T(8,128)(2,1)S(1)}, bf16[96,1792]{1,0:T(8,128)(2,1)S(1)}, u32[]{:S(2)}, u32[]{:S(2)}) collective-permute-start(bf16[96,1792]{1,0:T(8,128)(2,1)S(1)} %get-tuple-element.124), channel_id=1, source_target_pairs={{0,2},{1,3},{2,0},{3,1},{4,6},{5,7},{6,4},{7,5},{8,10},{9,11},{10,... | collective-permute-start | bytes 1032200 | tf_op jit(solution)/shard_map/ppermute | solution.py:90
  65.4 10.4 %collective-permute-start.12 = (bf16[96,1792]{1,0:T(8,128)(2,1)S(1)}, bf16[96,1792]{1,0:T(8,128)(2,1)S(1)}, u32[]{:S(2)}, u32[]{:S(2)}) collective-permute-start(bf16[96,1792]{1,0:T(8,128)(2,1)S(1)} %get-tuple-element.125), channel_id=1, source_target_pairs={{0,4},{1,5},{2,6},{3,7},{4,0},{5,1},{6,2},{7,3},{8,12},{9,13},{10,... | collective-permute-start | bytes 1032200 | tf_op jit(solution)/shard_map/ppermute | solution.py:90
  65.7 17.0 %collective-permute-start.14 = (bf16[96,1792]{1,0:T(8,128)(2,1)S(1)}, bf16[96,1792]{1,0:T(8,128)(2,1)S(1)}, u32[]{:S(2)}, u32[]{:S(2)}) collective-permute-start(bf16[96,1792]{1,0:T(8,128)(2,1)S(1)} %get-tuple-element.132), channel_id=1, source_target_pairs={{0,2},{1,3},{2,0},{3,1},{4,6},{5,7},{6,4},{7,5},{8,10},{9,11},{10,... | collective-permute-start | bytes 1032200 | tf_op jit(solution)/shard_map/ppermute | solution.py:90
  66.8 15.9 %collective-permute-start.15 = (bf16[96,1792]{1,0:T(8,128)(2,1)S(1)}, bf16[96,1792]{1,0:T(8,128)(2,1)S(1)}, u32[]{:S(2)}, u32[]{:S(2)}) collective-permute-start(bf16[96,1792]{1,0:T(8,128)(2,1)S(1)} %get-tuple-element.134), channel_id=1, source_target_pairs={{0,4},{1,5},{2,6},{3,7},{4,0},{5,1},{6,2},{7,3},{8,12},{9,13},{10,... | collective-permute-start | bytes 1032200 | tf_op jit(solution)/shard_map/ppermute | solution.py:90
  75.8 6.9 %collective-permute-start.18 = (bf16[72,1792]{1,0:T(8,128)(2,1)S(1)}, bf16[72,1792]{1,0:T(8,128)(2,1)S(1)}, u32[]{:S(2)}, u32[]{:S(2)}) collective-permute-start(bf16[72,1792]{1,0:T(8,128)(2,1)S(1)} %get-tuple-element.138), channel_id=1, source_target_pairs={{0,16},{1,17},{2,18},{3,19},{4,20},{5,21},{6,22},{7,23},{8,0},{9,1... | collective-permute-start | bytes 774152 | tf_op jit(solution)/shard_map/ppermute | solution.py:90
  76.2 5.4 %collective-permute-start.16 = (bf16[48,1792]{1,0:T(8,128)(2,1)S(1)}, bf16[48,1792]{1,0:T(8,128)(2,1)S(1)}, u32[]{:S(2)}, u32[]{:S(2)}) collective-permute-start(bf16[48,1792]{1,0:T(8,128)(2,1)S(1)} %get-tuple-element.136), channel_id=1, source_target_pairs={{0,2},{1,3},{2,0},{3,1},{4,6},{5,7},{6,4},{7,5},{8,10},{9,11},{10,... | collective-permute-start | bytes 516104 | tf_op jit(solution)/shard_map/ppermute | solution.py:90
  77.3 5.4 %collective-permute-start.17 = (bf16[48,1792]{1,0:T(8,128)(2,1)S(1)}, bf16[48,1792]{1,0:T(8,128)(2,1)S(1)}, u32[]{:S(2)}, u32[]{:S(2)}) collective-permute-start(bf16[48,1792]{1,0:T(8,128)(2,1)S(1)} %get-tuple-element.137), channel_id=1, source_target_pairs={{0,4},{1,5},{2,6},{3,7},{4,0},{5,1},{6,2},{7,3},{8,12},{9,13},{10,... | collective-permute-start | bytes 516104 | tf_op jit(solution)/shard_map/ppermute | solution.py:90
  83.7 2.5 %collective-permute-start.19 = (bf16[256,1792]{1,0:T(8,128)(2,1)S(1)}, bf16[256,1792]{1,0:T(8,128)(2,1)S(1)}, u32[]{:S(2)}, u32[]{:S(2)}) collective-permute-start(bf16[256,1792]{1,0:T(8,128)(2,1)S(1)} %finish_other.1), channel_id=1, source_target_pairs={{0,1},{1,0},{2,3},{3,2},{4,5},{5,4},{6,7},{7,6},{8,9},{9,8},{10,11... | collective-permute-start | bytes 2752520 | tf_op jit(solution)/shard_map/ppermute | solution.py:90

commit v17 on v16

--- a/solution.py
+++ b/solution.py
@@ -610,9 +610,7 @@
         ),
         "collect_fourth",
     )
-    sends = together(*sends)
-    near3, far3, deep3 = flip_near(sends[0]), flip_far(sends[1]), next_plane(sends[2])
-    near3_more, far3_more = flip_near(sends[3]), flip_far(sends[4])
+    near3, far3, deep3 = slot(*zip((flip_near, flip_far, next_plane), sends))
     acc = accumulate(
         rows,
         (shard, near, far, far1, deep1, near2, far2, deep2),
@@ -626,7 +624,8 @@
         jnp.float32,
         "accumulate_third",
     )
-    near3, far3, deep3, *acc = together(near3, far3, deep3, *acc)
+    near3_more, far3_more, *acc = together(*sends[3:], *acc)
+    near3_more, far3_more = flip_near(near3_more), flip_far(far3_more)
 
     sends = collect(
         (near3, far3, deep3),

time: 87.9 us -> 88.8 us (1.010)
  waiting for transfers between devices: 28.8 us -> 30.3 us
    ppermute x20, waiting for transfers between devices: 28.8 us -> 30.3 us  [permute(): return lax.ppermute(array, 'req', [(i, target(i)) for i in range(count)])]
where the time goes in v17:
time: 88.8 us; the launch traced here: 88.4 us
  waiting for transfers between devices  30.3 us (34%)
  starting transfers between devices  26.4 us (30%)
  Pallas kernels  23.6 us (27%)
  local copies, waits for them, and re-layouts  6.61 us (7%)
  between operations  1.46 us (2%)
    ppermute x20, waiting for transfers between devices, permute(): return lax.ppermute(array, 'req', [(i, target(i)) for i in range(count)])  30.3 us
    ppermute x20, starting transfers between devices, permute(): return lax.ppermute(array, 'req', [(i, target(i)) for i in range(count)])  26.4 us
    pallas_call x14, Pallas kernels, kernel_call(): pl.pallas_call(body, out_shape=out_shape, in_specs=specs or vmem(len(oper...  23.6 us
    unnamed x20, local copies, waits for them, and re-layouts  5.89 us
  transfers between devices with their start and end apart: 20, of which 13 were waited for; matrix products, arithmetic and copies ran while one was open for 1% of the time, Pallas kernels for 21%

profile of v17, /device:TPU:0, one launch (start us, length us, event | category | flops | bytes accessed | tf_op | source)
XLA Modules:
  0.0 88.4 jit_solution(243218776893238715)
XLA Ops:
  0.6 2.2 %shard.1 = (bf16[168,1792]{1,0:T(8,128)(2,1)}, bf16[144,1792]{1,0:T(8,128)(2,1)}) custom-call(bf16[56,1792]{1,0:T(8,128)(2,1)} %bitcast.17, bf16[56,1792]{1,0:T(8,128)(2,1)} %bitcast.18, bf16[56,1792]{1,0:T(8,128)(2,1)} %bitcast.19), custom_call_target="tpu_custom_call" | custom-call | flops 1000 | bytes 1000 | tf_op jit(solution)/shard_map/shard/pallas_call | solution.py:124
  2.8 3.0 %collective-permute-start = (bf16[168,1792]{1,0:T(8,128)(2,1)}, bf16[168,1792]{1,0:T(8,128)(2,1)S(1)}, u32[]{:S(2)}, u32[]{:S(2)}) collective-permute-start(bf16[168,1792]{1,0:T(8,128)(2,1)} %get-tuple-element.83.refs_0_), channel_id=1, source_target_pairs={{0,2},{1,3},{2,0},{3,1},{4,6},{5,7},{6,4},{7,5},{8,10},{9,11},{10,... | collective-permute-start | bytes 1806344 | tf_op jit(solution)/shard_map/ppermute | solution.py:90
  5.8 1.5 %collective-permute-start.1 = (bf16[168,1792]{1,0:T(8,128)(2,1)}, bf16[168,1792]{1,0:T(8,128)(2,1)S(1)}, u32[]{:S(2)}, u32[]{:S(2)}) collective-permute-start(bf16[168,1792]{1,0:T(8,128)(2,1)} %get-tuple-element.83.refs_0_), channel_id=1, source_target_pairs={{0,4},{1,5},{2,6},{3,7},{4,0},{5,1},{6,2},{7,3},{8,12},{9,13},{10,... | collective-permute-start | bytes 1806344 | tf_op jit(solution)/shard_map/ppermute | solution.py:90
  7.4 2.6 %collective-permute-start.2 = (bf16[144,1792]{1,0:T(8,128)(2,1)}, bf16[144,1792]{1,0:T(8,128)(2,1)S(1)}, u32[]{:S(2)}, u32[]{:S(2)}) collective-permute-start(bf16[144,1792]{1,0:T(8,128)(2,1)} %get-tuple-element.84), channel_id=1, source_target_pairs={{0,16},{1,17},{2,18},{3,19},{4,20},{5,21},{6,22},{7,23},{8,0},{9,1... | collective-permute-start | bytes 1548296 | tf_op jit(solution)/shard_map/ppermute | solution.py:90
  10.0 0.7 broadcast_in_dim.16.gain_ref
  10.7 1.2 %copy-done.1 = bf16[1,256,1792]{2,1,0:T(8,128)(2,1)S(1)} copy-done((bf16[1,256,1792]{2,1,0:T(8,128)(2,1)S(1)}, bf16[1,256,1792]{2,1,0:T(8,128)(2,1)}, u32[]{:S(2)}) %copy-start.1) | copy-done | bytes 917528
  11.9 1.9 %copy-done.3 = bf16[1792,896]{1,0:T(8,128)(2,1)S(1)} copy-done((bf16[1792,896]{1,0:T(8,128)(2,1)S(1)}, bf16[1792,896]{1,0:T(8,128)(2,1)}, u32[]{:S(2)}) %copy-start.3) | copy-done | bytes 3211288
  13.8 1.0 %copy-done.5 = bf16[1792,128]{1,0:T(8,128)(2,1)S(1)} copy-done((bf16[1792,128]{1,0:T(8,128)(2,1)S(1)}, bf16[1792,128]{1,0:T(8,128)(2,1)}, u32[]{:S(2)}) %copy-start.5) | copy-done | bytes 458776
  14.8 1.0 %copy-done.6 = bf16[1792,128]{1,0:T(8,128)(2,1)S(1)} copy-done((bf16[1792,128]{1,0:T(8,128)(2,1)S(1)}, bf16[1792,128]{1,0:T(8,128)(2,1)}, u32[]{:S(2)}) %copy-start.6) | copy-done | bytes 458776
  15.8 0.7 copy-done.7
  16.5 3.7 %project.1 = (bf16[256,128]{1,0:T(8,128)(2,1)S(1)}, bf16[256,128]{1,0:T(8,128)(2,1)S(1)}, bf16[256,896]{1,0:T(8,128)(2,1)S(1)}) custom-call(bf16[256,1792]{1,0:T(8,128)(2,1)S(1)} %bitcast.13, bf16[16,1792]{1,0:T(8,128)(2,1)S(1)} %broadcast_in_dim.15.edge_ref, f32[1,1792]{1,0:T(1,128)S(1)} %broadcast_in_dim.16.gain_ref, f32[3,1792]{1,0:T(4,128)S(1)} %copy-done.7, ...), custom_call_target="tpu_custom_call" | custom-call | flops 1000 | bytes 1000 | tf_op jit(solution)/shard_map/project/pallas_call | solution.py:124
  20.3 0.4 collective-permute-done.2.refs_3_
  20.7 0.4 collective-permute-done.1.refs_2_
  21.1 0.2 collect_second.1
  21.3 1.6 %collective-permute-start.4 = (bf16[232,1792]{1,0:T(8,128)(2,1)S(1)}, bf16[232,1792]{1,0:T(8,128)(2,1)S(1)}, u32[]{:S(2)}, u32[]{:S(2)}) collective-permute-start(bf16[232,1792]{1,0:T(8,128)(2,1)S(1)} %get-tuple-element.95), channel_id=1, source_target_pairs={{0,4},{1,5},{2,6},{3,7},{4,0},{5,1},{6,2},{7,3},{8,12},{9,13},{10,... | collective-permute-start | bytes 2494472 | tf_op jit(solution)/shard_map/ppermute | solution.py:90
  22.9 0.5 collective-permute-start.3
  23.4 2.6 %collective-permute-start.5 = (bf16[216,1792]{1,0:T(8,128)(2,1)S(1)}, bf16[216,1792]{1,0:T(8,128)(2,1)S(1)}, u32[]{:S(2)}, u32[]{:S(2)}) collective-permute-start(bf16[216,1792]{1,0:T(8,128)(2,1)S(1)} %get-tuple-element.96), channel_id=1, source_target_pairs={{0,16},{1,17},{2,18},{3,19},{4,20},{5,21},{6,22},{7,23},{8,0},{9,1... | collective-permute-start | bytes 2322440 | tf_op jit(solution)/shard_map/ppermute | solution.py:90
  26.7 3.7 %attend.1 = (f32[256,896]{1,0:T(8,128)S(1)}, f32[256,8]{1,0:T(8,128)S(1)}, f32[273,1,896]{2,1,0:T(1,128)}, f32[8,273]{1,0:T(8,128)}) custom-call(s32[1]{0:T(128)S(6)} %copy.23.count_ref, f32[8,256]{1,0:T(8,128)S(1)} %bitcast.15, bf16[256,128]{1,0:T(8,128)(2,1)S(1)} %get-tuple-element.100.queries_ref, bf16[256,128]{1,0:T(8,128)(2,1)S(1)} %get-tuple-element.101.keys_ref, ...), custom_call_target="tpu_custom_call" | custom-call | flops 1000 | bytes 1000 | tf_op jit(solution)/shard_map/attend/pallas_call | solution.py:124
  30.4 2.6 %mix.1 = (bf16[256,1792]{1,0:T(8,128)(2,1)S(1)}, bf16[256,1792]{1,0:T(8,128)(2,1)S(1)}) custom-call(f32[256,896]{1,0:T(8,128)S(1)} %get-tuple-element.103.numer_ref, f32[256,8]{1,0:T(8,128)S(1)} %get-tuple-element.104.denom_ref, bf16[256,1792]{1,0:T(8,128)(2,1)S(1)} %bitcast.14, bf16[896,1792]{1,0:T(8,128)(2,1)S(1)} %copy-done.4, ...), custom_call_target="tpu_custom_call" | custom-call | flops 1000 | bytes 1000 | tf_op jit(solution)/shard_map/mix/pallas_call | solution.py:124
  33.0 7.9 %collective-permute-done.5.refs_2_.refs_6_.refs_4_ = bf16[216,1792]{1,0:T(8,128)(2,1)S(1)} collective-permute-done((bf16[216,1792]{1,0:T(8,128)(2,1)S(1)}, bf16[216,1792]{1,0:T(8,128)(2,1)S(1)}, u32[]{:S(2)}, u32[]{:S(2)}) %collective-permute-start.5) | collective-permute-done | bytes 774176 | tf_op jit(solution)/shard_map/ppermute | solution.py:90
  40.8 0.2 collective-permute-done.3.refs_0_.refs_4_
  41.0 0.2 collect_third.1
  41.2 3.3 %collective-permute-start.8 = (bf16[240,1792]{1,0:T(8,128)(2,1)S(1)}, bf16[240,1792]{1,0:T(8,128)(2,1)S(1)}, u32[]{:S(2)}, u32[]{:S(2)}) collective-permute-start(bf16[240,1792]{1,0:T(8,128)(2,1)S(1)} %get-tuple-element.118), channel_id=1, source_target_pairs={{0,16},{1,17},{2,18},{3,19},{4,20},{5,21},{6,22},{7,23},{8,0},{9,1... | collective-permute-start | bytes 2580488 | tf_op jit(solution)/shard_map/ppermute | solution.py:90
  44.5 1.4 %collective-permute-start.6 = (bf16[224,1792]{1,0:T(8,128)(2,1)S(1)}, bf16[224,1792]{1,0:T(8,128)(2,1)S(1)}, u32[]{:S(2)}, u32[]{:S(2)}) collective-permute-start(bf16[224,1792]{1,0:T(8,128)(2,1)S(1)} %get-tuple-element.116), channel_id=1, source_target_pairs={{0,2},{1,3},{2,0},{3,1},{4,6},{5,7},{6,4},{7,5},{8,10},{9,11},{10,... | collective-permute-start | bytes 2408456 | tf_op jit(solution)/shard_map/ppermute | solution.py:90
  45.9 0.5 collective-permute-start.7
  46.4 0.5 collective-permute-start.10
  47.0 1.3 %collective-permute-done.9.refs_0_ = bf16[128,1792]{1,0:T(8,128)(2,1)S(1)} collective-permute-done((bf16[128,1792]{1,0:T(8,128)(2,1)S(1)}, bf16[128,1792]{1,0:T(8,128)(2,1)S(1)}, u32[]{:S(2)}, u32[]{:S(2)}) %collective-permute-start.9) | collective-permute-done | bytes 458784 | tf_op jit(solution)/shard_map/ppermute | solution.py:90
  48.3 0.7 collective-permute-done.10.refs_1_
  49.0 3.2 %accumulate_second.1 = (f32[256,1792]{1,0:T(8,128)S(1)}, f32[256,1792]{1,0:T(8,128)S(1)}) custom-call(bf16[168,1792]{1,0:T(8,128)(2,1)S(1)} %copy-done, bf16[168,1792]{1,0:T(8,128)(2,1)S(1)} %collective-permute-done.refs_1_, bf16[168,1792]{1,0:T(8,128)(2,1)S(1)} %collective-permute-done.1.refs_2_, bf16[144,1792]{1,0:T(8,128)(2,1)S(1)} %collective-permute-done.2.refs_3_, ...), custom_call_target="tpu_custom_call" | custom-call | flops 1000 | bytes 1000 | tf_op jit(solution)/shard_map/accumulate_second/pallas_call | solution.py:124
  52.2 8.9 %collective-permute-done.7.refs_1_.refs_6_ = bf16[208,1792]{1,0:T(8,128)(2,1)S(1)} collective-permute-done((bf16[208,1792]{1,0:T(8,128)(2,1)S(1)}, bf16[208,1792]{1,0:T(8,128)(2,1)S(1)}, u32[]{:S(2)}, u32[]{:S(2)}) %collective-permute-start.7) | collective-permute-done | bytes 745504 | tf_op jit(solution)/shard_map/ppermute | solution.py:90
  61.1 0.1 collective-permute-done.6.refs_0_.refs_5_
  61.2 0.1 collect_fourth.1
  61.4 2.6 %collective-permute-start.13 = (bf16[144,1792]{1,0:T(8,128)(2,1)S(1)}, bf16[144,1792]{1,0:T(8,128)(2,1)S(1)}, u32[]{:S(2)}, u32[]{:S(2)}) collective-permute-start(bf16[144,1792]{1,0:T(8,128)(2,1)S(1)} %get-tuple-element.134), channel_id=1, source_target_pairs={{0,16},{1,17},{2,18},{3,19},{4,20},{5,21},{6,22},{7,23},{8,0},{9,1... | collective-permute-start | bytes 1548296 | tf_op jit(solution)/shard_map/ppermute | solution.py:90
  64.0 1.4 %collective-permute-start.11 = (bf16[96,1792]{1,0:T(8,128)(2,1)S(1)}, bf16[96,1792]{1,0:T(8,128)(2,1)S(1)}, u32[]{:S(2)}, u32[]{:S(2)}) collective-permute-start(bf16[96,1792]{1,0:T(8,128)(2,1)S(1)} %get-tuple-element.132), channel_id=1, source_target_pairs={{0,2},{1,3},{2,0},{3,1},{4,6},{5,7},{6,4},{7,5},{8,10},{9,11},{10,... | collective-permute-start | bytes 1032200 | tf_op jit(solution)/shard_map/ppermute | solution.py:90
  65.4 0.4 collective-permute-start.12
  65.7 3.9 %accumulate_third.1 = (f32[256,1792]{1,0:T(8,128)S(1)}, f32[256,1792]{1,0:T(8,128)S(1)}) custom-call(bf16[168,1792]{1,0:T(8,128)(2,1)S(1)} %copy-done, bf16[168,1792]{1,0:T(8,128)(2,1)S(1)} %collective-permute-done.refs_1_, bf16[168,1792]{1,0:T(8,128)(2,1)S(1)} %collective-permute-done.1.refs_2_, ...), custom_call_target="tpu_custom_call", output_to_operand_aliasing={{0}: (10, {}), {1}: (11, {})} | custom-call | flops 1000 | bytes 1000 | tf_op jit(solution)/shard_map/accumulate_third/pallas_call | solution.py:124
  69.6 1.1 %collective-permute-start.14 = (bf16[96,1792]{1,0:T(8,128)(2,1)S(1)}, bf16[96,1792]{1,0:T(8,128)(2,1)S(1)}, u32[]{:S(2)}, u32[]{:S(2)}) collective-permute-start(bf16[96,1792]{1,0:T(8,128)(2,1)S(1)} %get-tuple-element.142), channel_id=1, source_target_pairs={{0,2},{1,3},{2,0},{3,1},{4,6},{5,7},{6,4},{7,5},{8,10},{9,11},{10,... | collective-permute-start | bytes 1032200 | tf_op jit(solution)/shard_map/ppermute | solution.py:90
  70.8 1.3 %collective-permute-start.15 = (bf16[96,1792]{1,0:T(8,128)(2,1)S(1)}, bf16[96,1792]{1,0:T(8,128)(2,1)S(1)}, u32[]{:S(2)}, u32[]{:S(2)}) collective-permute-start(bf16[96,1792]{1,0:T(8,128)(2,1)S(1)} %get-tuple-element.144), channel_id=1, source_target_pairs={{0,4},{1,5},{2,6},{3,7},{4,0},{5,1},{6,2},{7,3},{8,12},{9,13},{10,... | collective-permute-start | bytes 1032200 | tf_op jit(solution)/shard_map/ppermute | solution.py:90
  72.1 2.8 %collective-permute-done.11.refs_0_ = bf16[96,1792]{1,0:T(8,128)(2,1)S(1)} collective-permute-done((bf16[96,1792]{1,0:T(8,128)(2,1)S(1)}, bf16[96,1792]{1,0:T(8,128)(2,1)S(1)}, u32[]{:S(2)}, u32[]{:S(2)}) %collective-permute-start.11) | collective-permute-done | bytes 344096 | tf_op jit(solution)/shard_map/ppermute | solution.py:90
  74.9 1.4 %collective-permute-done.12.refs_1_.refs_2_ = bf16[96,1792]{1,0:T(8,128)(2,1)S(1)} collective-permute-done((bf16[96,1792]{1,0:T(8,128)(2,1)S(1)}, bf16[96,1792]{1,0:T(8,128)(2,1)S(1)}, u32[]{:S(2)}, u32[]{:S(2)}) %collective-permute-start.12) | collective-permute-done | bytes 344096 | tf_op jit(solution)/shard_map/ppermute | solution.py:90
  76.4 1.4 %collective-permute-start.16 = (bf16[48,1792]{1,0:T(8,128)(2,1)S(1)}, bf16[48,1792]{1,0:T(8,128)(2,1)S(1)}, u32[]{:S(2)}, u32[]{:S(2)}) collective-permute-start(bf16[48,1792]{1,0:T(8,128)(2,1)S(1)} %get-tuple-element.146), channel_id=1, source_target_pairs={{0,2},{1,3},{2,0},{3,1},{4,6},{5,7},{6,4},{7,5},{8,10},{9,11},{10,... | collective-permute-start | bytes 516104 | tf_op jit(solution)/shard_map/ppermute | solution.py:90
  77.8 0.6 collective-permute-start.17
  78.4 3.9 %collective-permute-done.16.refs_5_ = bf16[48,1792]{1,0:T(8,128)(2,1)S(1)} collective-permute-done((bf16[48,1792]{1,0:T(8,128)(2,1)S(1)}, bf16[48,1792]{1,0:T(8,128)(2,1)S(1)}, u32[]{:S(2)}, u32[]{:S(2)}) %collective-permute-start.16) | collective-permute-done | bytes 172064 | tf_op jit(solution)/shard_map/ppermute | solution.py:90
  82.3 1.3 %collective-permute-done.17.refs_6_ = bf16[48,1792]{1,0:T(8,128)(2,1)S(1)} collective-permute-done((bf16[48,1792]{1,0:T(8,128)(2,1)S(1)}, bf16[48,1792]{1,0:T(8,128)(2,1)S(1)}, u32[]{:S(2)}, u32[]{:S(2)}) %collective-permute-start.17) | collective-permute-done | bytes 172064 | tf_op jit(solution)/shard_map/ppermute | solution.py:90
  83.6 1.0 %finish_other.1 = bf16[256,1792]{1,0:T(8,128)(2,1)S(1)} custom-call(bf16[96,1792]{1,0:T(8,128)(2,1)S(1)} %collective-permute-done.11.refs_0_, bf16[96,1792]{1,0:T(8,128)(2,1)S(1)} %collective-permute-done.14.refs_1_, bf16[96,1792]{1,0:T(8,128)(2,1)S(1)} %collective-permute-done.12.refs_1_.refs_2_, bf16[96,1792]{1,0:T(8,128)(2,1)S(1)} %collective-permute-done.15.refs_3_, ...), custom_call_target="tpu_custom_call" | custom-call | flops 1000 | bytes 1000 | tf_op jit(solution)/shard_map/finish_other/pallas_call | solution.py:124
  84.7 1.4 %finish_own.1.kept_ref = f32[256,1792]{1,0:T(8,128)S(1)} custom-call(bf16[96,1792]{1,0:T(8,128)(2,1)S(1)} %collective-permute-done.11.refs_0_, bf16[96,1792]{1,0:T(8,128)(2,1)S(1)} %collective-permute-done.14.refs_1_, bf16[96,1792]{1,0:T(8,128)(2,1)S(1)} %collective-permute-done.12.refs_1_.refs_2_, ...), custom_call_target="tpu_custom_call", output_to_operand_aliasing={{}: (9, {})} | custom-call | flops 1000 | bytes 1000 | tf_op jit(solution)/shard_map/finish_own/pallas_call | solution.py:124
  86.1 1.1 %collective-permute-done.19.given_ref = bf16[256,1792]{1,0:T(8,128)(2,1)S(1)} collective-permute-done((bf16[256,1792]{1,0:T(8,128)(2,1)S(1)}, bf16[256,1792]{1,0:T(8,128)(2,1)S(1)}, u32[]{:S(2)}, u32[]{:S(2)}) %collective-permute-start.19) | collective-permute-done | bytes 917536 | tf_op jit(solution)/shard_map/ppermute | solution.py:90
  87.2 1.2 %final.1 = bf16[256,1792]{1,0:T(8,128)(2,1)} custom-call(s32[1]{0:T(128)S(6)} %copy.23.count_ref, f32[256,1792]{1,0:T(8,128)S(1)} %finish_own.1.kept_ref, bf16[256,1792]{1,0:T(8,128)(2,1)S(1)} %collective-permute-done.19.given_ref), custom_call_target="tpu_custom_call" | custom-call | flops 1000 | bytes 1000 | tf_op jit(solution)/shard_map/final/pallas_call | solution.py:124
  (29 shorter events, 0.3 us)
Async XLA Ops:
  2.8 17.9 %collective-permute-start = (bf16[168,1792]{1,0:T(8,128)(2,1)}, bf16[168,1792]{1,0:T(8,128)(2,1)S(1)}, u32[]{:S(2)}, u32[]{:S(2)}) collective-permute-start(bf16[168,1792]{1,0:T(8,128)(2,1)} %get-tuple-element.83.refs_0_), channel_id=1, source_target_pairs={{0,2},{1,3},{2,0},{3,1},{4,6},{5,7},{6,4},{7,5},{8,10},{9,11},{10,... | collective-permute-start | bytes 1806344 | tf_op jit(solution)/shard_map/ppermute | solution.py:90
  5.8 15.3 %collective-permute-start.1 = (bf16[168,1792]{1,0:T(8,128)(2,1)}, bf16[168,1792]{1,0:T(8,128)(2,1)S(1)}, u32[]{:S(2)}, u32[]{:S(2)}) collective-permute-start(bf16[168,1792]{1,0:T(8,128)(2,1)} %get-tuple-element.83.refs_0_), channel_id=1, source_target_pairs={{0,4},{1,5},{2,6},{3,7},{4,0},{5,1},{6,2},{7,3},{8,12},{9,13},{10,... | collective-permute-start | bytes 1806344 | tf_op jit(solution)/shard_map/ppermute | solution.py:90
  7.4 13.4 %collective-permute-start.2 = (bf16[144,1792]{1,0:T(8,128)(2,1)}, bf16[144,1792]{1,0:T(8,128)(2,1)S(1)}, u32[]{:S(2)}, u32[]{:S(2)}) collective-permute-start(bf16[144,1792]{1,0:T(8,128)(2,1)} %get-tuple-element.84), channel_id=1, source_target_pairs={{0,16},{1,17},{2,18},{3,19},{4,20},{5,21},{6,22},{7,23},{8,0},{9,1... | collective-permute-start | bytes 1548296 | tf_op jit(solution)/shard_map/ppermute | solution.py:90
  10.7 1.2 %copy-start.1 = (bf16[1,256,1792]{2,1,0:T(8,128)(2,1)S(1)}, bf16[1,256,1792]{2,1,0:T(8,128)(2,1)}, u32[]{:S(2)}) copy-start(bf16[1,256,1792]{2,1,0:T(8,128)(2,1)} %param.13) | copy-start | bytes 2752516
  11.8 1.9 %copy-start.3 = (bf16[1792,896]{1,0:T(8,128)(2,1)S(1)}, bf16[1792,896]{1,0:T(8,128)(2,1)}, u32[]{:S(2)}) copy-start(bf16[1792,896]{1,0:T(8,128)(2,1)} %value_ref.1) | copy-start | bytes 9633796
  13.8 1.0 %copy-start.5 = (bf16[1792,128]{1,0:T(8,128)(2,1)S(1)}, bf16[1792,128]{1,0:T(8,128)(2,1)}, u32[]{:S(2)}) copy-start(bf16[1792,128]{1,0:T(8,128)(2,1)} %query_ref.1) | copy-start | bytes 1376260
  14.8 1.0 %copy-start.6 = (bf16[1792,128]{1,0:T(8,128)(2,1)S(1)}, bf16[1792,128]{1,0:T(8,128)(2,1)}, u32[]{:S(2)}) copy-start(bf16[1792,128]{1,0:T(8,128)(2,1)} %key_ref.1) | copy-start | bytes 1376260
  15.8 0.7 copy-start.7
  16.5 4.6 %copy-start = (bf16[168,1792]{1,0:T(8,128)(2,1)S(1)}, bf16[168,1792]{1,0:T(8,128)(2,1)}, u32[]{:S(2)}) copy-start(bf16[168,1792]{1,0:T(8,128)(2,1)} %get-tuple-element.83.refs_0_) | copy-start | bytes 1806340
  16.5 13.8 %copy-start.4 = (bf16[896,1792]{1,0:T(8,128)(2,1)S(1)}, bf16[896,1792]{1,0:T(8,128)(2,1)}, u32[]{:S(2)}) copy-start(bf16[896,1792]{1,0:T(8,128)(2,1)} %out_ref.1) | copy-start | bytes 9633796
  20.3 6.4 %copy-start.9 = (f32[1792]{0:T(1024)S(1)}, f32[1792]{0:T(1024)}, u32[]{:S(2)}) copy-start(f32[1792]{0:T(1024)} %param.22) | copy-start | bytes 21508
  20.3 6.4 %copy-start.8 = (f32[1,256,8]{1,2,0:T(8,128)S(1)}, f32[1,256,8]{1,2,0:T(8,128)}, u32[]{:S(2)}) copy-start(f32[1,256,8]{1,2,0:T(8,128)} %param.15) | copy-start | bytes 24580
  20.3 10.1 %copy-start.2 = (bf16[1,256,1792]{2,1,0:T(8,128)(2,1)S(1)}, bf16[1,256,1792]{2,1,0:T(8,128)(2,1)}, u32[]{:S(2)}) copy-start(bf16[1,256,1792]{2,1,0:T(8,128)(2,1)} %param.13) | copy-start | bytes 2752516
  21.3 19.8 %collective-permute-start.4 = (bf16[232,1792]{1,0:T(8,128)(2,1)S(1)}, bf16[232,1792]{1,0:T(8,128)(2,1)S(1)}, u32[]{:S(2)}, u32[]{:S(2)}) collective-permute-start(bf16[232,1792]{1,0:T(8,128)(2,1)S(1)} %get-tuple-element.95), channel_id=1, source_target_pairs={{0,4},{1,5},{2,6},{3,7},{4,0},{5,1},{6,2},{7,3},{8,12},{9,13},{10,... | collective-permute-start | bytes 2494472 | tf_op jit(solution)/shard_map/ppermute | solution.py:90
  22.9 18.2 %collective-permute-start.3 = (bf16[224,1792]{1,0:T(8,128)(2,1)S(1)}, bf16[224,1792]{1,0:T(8,128)(2,1)S(1)}, u32[]{:S(2)}, u32[]{:S(2)}) collective-permute-start(bf16[224,1792]{1,0:T(8,128)(2,1)S(1)} %get-tuple-element.94), channel_id=1, source_target_pairs={{0,2},{1,3},{2,0},{3,1},{4,6},{5,7},{6,4},{7,5},{8,10},{9,11},{10,... | collective-permute-start | bytes 2408456 | tf_op jit(solution)/shard_map/ppermute | solution.py:90
  23.4 17.4 %collective-permute-start.5 = (bf16[216,1792]{1,0:T(8,128)(2,1)S(1)}, bf16[216,1792]{1,0:T(8,128)(2,1)S(1)}, u32[]{:S(2)}, u32[]{:S(2)}) collective-permute-start(bf16[216,1792]{1,0:T(8,128)(2,1)S(1)} %get-tuple-element.96), channel_id=1, source_target_pairs={{0,16},{1,17},{2,18},{3,19},{4,20},{5,21},{6,22},{7,23},{8,0},{9,1... | collective-permute-start | bytes 2322440 | tf_op jit(solution)/shard_map/ppermute | solution.py:90
  41.2 20.0 %collective-permute-start.8 = (bf16[240,1792]{1,0:T(8,128)(2,1)S(1)}, bf16[240,1792]{1,0:T(8,128)(2,1)S(1)}, u32[]{:S(2)}, u32[]{:S(2)}) collective-permute-start(bf16[240,1792]{1,0:T(8,128)(2,1)S(1)} %get-tuple-element.118), channel_id=1, source_target_pairs={{0,16},{1,17},{2,18},{3,19},{4,20},{5,21},{6,22},{7,23},{8,0},{9,1... | collective-permute-start | bytes 2580488 | tf_op jit(solution)/shard_map/ppermute | solution.py:90
  44.5 16.7 %collective-permute-start.6 = (bf16[224,1792]{1,0:T(8,128)(2,1)S(1)}, bf16[224,1792]{1,0:T(8,128)(2,1)S(1)}, u32[]{:S(2)}, u32[]{:S(2)}) collective-permute-start(bf16[224,1792]{1,0:T(8,128)(2,1)S(1)} %get-tuple-element.116), channel_id=1, source_target_pairs={{0,2},{1,3},{2,0},{3,1},{4,6},{5,7},{6,4},{7,5},{8,10},{9,11},{10,... | collective-permute-start | bytes 2408456 | tf_op jit(solution)/shard_map/ppermute | solution.py:90
  45.9 15.2 %collective-permute-start.7 = (bf16[208,1792]{1,0:T(8,128)(2,1)S(1)}, bf16[208,1792]{1,0:T(8,128)(2,1)S(1)}, u32[]{:S(2)}, u32[]{:S(2)}) collective-permute-start(bf16[208,1792]{1,0:T(8,128)(2,1)S(1)} %get-tuple-element.117), channel_id=1, source_target_pairs={{0,4},{1,5},{2,6},{3,7},{4,0},{5,1},{6,2},{7,3},{8,12},{9,13},{10,... | collective-permute-start | bytes 2236424 | tf_op jit(solution)/shard_map/ppermute | solution.py:90
  46.4 1.8 %collective-permute-start.9 = (bf16[128,1792]{1,0:T(8,128)(2,1)S(1)}, bf16[128,1792]{1,0:T(8,128)(2,1)S(1)}, u32[]{:S(2)}, u32[]{:S(2)}) collective-permute-start(bf16[128,1792]{1,0:T(8,128)(2,1)S(1)} %get-tuple-element.122), channel_id=1, source_target_pairs={{0,1},{1,0},{2,3},{3,2},{4,5},{5,4},{6,7},{7,6},{8,9},{9,8},{10,11... | collective-permute-start | bytes 1376264 | tf_op jit(solution)/shard_map/ppermute | solution.py:90
  46.4 2.5 %collective-permute-start.10 = (bf16[128,1792]{1,0:T(8,128)(2,1)S(1)}, bf16[128,1792]{1,0:T(8,128)(2,1)S(1)}, u32[]{:S(2)}, u32[]{:S(2)}) collective-permute-start(bf16[128,1792]{1,0:T(8,128)(2,1)S(1)} %get-tuple-element.123), channel_id=1, source_target_pairs={{0,1},{1,0},{2,3},{3,2},{4,5},{5,4},{6,7},{7,6},{8,9},{9,8},{10,11... | collective-permute-start | bytes 1376264 | tf_op jit(solution)/shard_map/ppermute | solution.py:90
  61.4 14.9 %collective-permute-start.13 = (bf16[144,1792]{1,0:T(8,128)(2,1)S(1)}, bf16[144,1792]{1,0:T(8,128)(2,1)S(1)}, u32[]{:S(2)}, u32[]{:S(2)}) collective-permute-start(bf16[144,1792]{1,0:T(8,128)(2,1)S(1)} %get-tuple-element.134), channel_id=1, source_target_pairs={{0,16},{1,17},{2,18},{3,19},{4,20},{5,21},{6,22},{7,23},{8,0},{9,1... | collective-permute-start | bytes 1548296 | tf_op jit(solution)/shard_map/ppermute | solution.py:90
  64.0 10.9 %collective-permute-start.11 = (bf16[96,1792]{1,0:T(8,128)(2,1)S(1)}, bf16[96,1792]{1,0:T(8,128)(2,1)S(1)}, u32[]{:S(2)}, u32[]{:S(2)}) collective-permute-start(bf16[96,1792]{1,0:T(8,128)(2,1)S(1)} %get-tuple-element.132), channel_id=1, source_target_pairs={{0,2},{1,3},{2,0},{3,1},{4,6},{5,7},{6,4},{7,5},{8,10},{9,11},{10,... | collective-permute-start | bytes 1032200 | tf_op jit(solution)/shard_map/ppermute | solution.py:90
  65.4 10.9 %collective-permute-start.12 = (bf16[96,1792]{1,0:T(8,128)(2,1)S(1)}, bf16[96,1792]{1,0:T(8,128)(2,1)S(1)}, u32[]{:S(2)}, u32[]{:S(2)}) collective-permute-start(bf16[96,1792]{1,0:T(8,128)(2,1)S(1)} %get-tuple-element.133), channel_id=1, source_target_pairs={{0,4},{1,5},{2,6},{3,7},{4,0},{5,1},{6,2},{7,3},{8,12},{9,13},{10,... | collective-permute-start | bytes 1032200 | tf_op jit(solution)/shard_map/ppermute | solution.py:90
  69.6 14.0 %collective-permute-start.14 = (bf16[96,1792]{1,0:T(8,128)(2,1)S(1)}, bf16[96,1792]{1,0:T(8,128)(2,1)S(1)}, u32[]{:S(2)}, u32[]{:S(2)}) collective-permute-start(bf16[96,1792]{1,0:T(8,128)(2,1)S(1)} %get-tuple-element.142), channel_id=1, source_target_pairs={{0,2},{1,3},{2,0},{3,1},{4,6},{5,7},{6,4},{7,5},{8,10},{9,11},{10,... | collective-permute-start | bytes 1032200 | tf_op jit(solution)/shard_map/ppermute | solution.py:90
  70.8 12.8 %collective-permute-start.15 = (bf16[96,1792]{1,0:T(8,128)(2,1)S(1)}, bf16[96,1792]{1,0:T(8,128)(2,1)S(1)}, u32[]{:S(2)}, u32[]{:S(2)}) collective-permute-start(bf16[96,1792]{1,0:T(8,128)(2,1)S(1)} %get-tuple-element.144), channel_id=1, source_target_pairs={{0,4},{1,5},{2,6},{3,7},{4,0},{5,1},{6,2},{7,3},{8,12},{9,13},{10,... | collective-permute-start | bytes 1032200 | tf_op jit(solution)/shard_map/ppermute | solution.py:90
  76.3 7.2 %collective-permute-start.18 = (bf16[72,1792]{1,0:T(8,128)(2,1)S(1)}, bf16[72,1792]{1,0:T(8,128)(2,1)S(1)}, u32[]{:S(2)}, u32[]{:S(2)}) collective-permute-start(bf16[72,1792]{1,0:T(8,128)(2,1)S(1)} %get-tuple-element.148), channel_id=1, source_target_pairs={{0,16},{1,17},{2,18},{3,19},{4,20},{5,21},{6,22},{7,23},{8,0},{9,1... | collective-permute-start | bytes 774152 | tf_op jit(solution)/shard_map/ppermute | solution.py:90
  76.4 5.9 %collective-permute-start.16 = (bf16[48,1792]{1,0:T(8,128)(2,1)S(1)}, bf16[48,1792]{1,0:T(8,128)(2,1)S(1)}, u32[]{:S(2)}, u32[]{:S(2)}) collective-permute-start(bf16[48,1792]{1,0:T(8,128)(2,1)S(1)} %get-tuple-element.146), channel_id=1, source_target_pairs={{0,2},{1,3},{2,0},{3,1},{4,6},{5,7},{6,4},{7,5},{8,10},{9,11},{10,... | collective-permute-start | bytes 516104 | tf_op jit(solution)/shard_map/ppermute | solution.py:90
  77.8 5.8 %collective-permute-start.17 = (bf16[48,1792]{1,0:T(8,128)(2,1)S(1)}, bf16[48,1792]{1,0:T(8,128)(2,1)S(1)}, u32[]{:S(2)}, u32[]{:S(2)}) collective-permute-start(bf16[48,1792]{1,0:T(8,128)(2,1)S(1)} %get-tuple-element.147), channel_id=1, source_target_pairs={{0,4},{1,5},{2,6},{3,7},{4,0},{5,1},{6,2},{7,3},{8,12},{9,13},{10,... | collective-permute-start | bytes 516104 | tf_op jit(solution)/shard_map/ppermute | solution.py:90
  84.6 2.5 %collective-permute-start.19 = (bf16[256,1792]{1,0:T(8,128)(2,1)S(1)}, bf16[256,1792]{1,0:T(8,128)(2,1)S(1)}, u32[]{:S(2)}, u32[]{:S(2)}) collective-permute-start(bf16[256,1792]{1,0:T(8,128)(2,1)S(1)} %finish_other.1), channel_id=1, source_target_pairs={{0,1},{1,0},{2,3},{3,2},{4,5},{5,4},{6,7},{7,6},{8,9},{9,8},{10,11... | collective-permute-start | bytes 2752520 | tf_op jit(solution)/shard_map/ppermute | solution.py:90

commit v18 on v17

--- a/solution.py
+++ b/solution.py
@@ -574,14 +574,17 @@
         (near1, far1, deep1, mlp_in),
         (
             ((2, 0, wide), (1, 0, cut)),
-            ((2, 0, wide), (0, cut, wide)),
+            ((2, 0, wide),),
             ((2, 0, wide + 3 * narrow), (1, wide + wide - cut, wide + full - cut)),
+            ((0, cut, wide),),
             ((3, 0, middle),),
             ((3, middle, local_len),),
         ),
         "collect_third",
     )
-    near2, far2, deep2 = slot(*zip((flip_near, flip_far, next_plane), sends))
+    sends = together(*sends)
+    near2, far2, deep2 = flip_near(sends[0]), flip_far(sends[1]), next_plane(sends[2])
+    second2 = flip_far(sends[3])
     (other_in,) = collect(
         (flip_core(top), flip_core(end)),
         (((0, 0, middle), (1, 0, local_len - middle)),),
@@ -596,36 +599,39 @@
         jnp.float32,
         "accumulate_second",
     )
-    near2, far2, deep2, *acc = together(near2, far2, deep2, *acc)
+    second2, deep2, *acc = together(second2, deep2, *acc)
 
     two = 2 * main
     sends = collect(
-        (near2, far2, deep2),
+        (second2, deep2),
         (
-            ((2, main, wide),),
-            ((2, 0, main), (2, two, wide)),
-            ((2, wide, wide + 4 * narrow), (1, 2 * wide - cut - main, 2 * wide - cut)),
-            ((2, 0, main), (1, 0, main)),
-            ((2, main, two), (0, main, two)),
+            ((1, main, wide),),
+            ((1, 0, main), (1, two, wide)),
+            ((1, wide, wide + 4 * narrow), (0, wide - cut - main, wide - cut)),
         ),
         "collect_fourth",
     )
     near3, far3, deep3 = slot(*zip((flip_near, flip_far, next_plane), sends))
     acc = accumulate(
         rows,
-        (shard, near, far, far1, deep1, near2, far2, deep2),
-        [runs(i, 0, main) for i in (5, 6, 7)]
-        + list(split_runs((5, wide), (6, wide), main))
+        (shard, near, far, far1, deep1, near2, far2, second2, deep2),
+        [runs(i, 0, main) for i in (5, 6, 8)]
+        + list(split_runs((5, wide), (7, 0), main))
         + [runs(i, wide, edge) for i in (0, 1, 2)]
         + [runs(3, wide + wide - cut, edge)]
         + [runs(4, wide + k * narrow, edge) for k in range(3)]
-        + [runs(7, wide + k * narrow, edge) for k in range(4)],
+        + [runs(8, wide + k * narrow, edge) for k in range(4)],
         tuple(acc),
         jnp.float32,
         "accumulate_third",
     )
-    near3_more, far3_more, *acc = together(*sends[3:], *acc)
-    near3_more, far3_more = flip_near(near3_more), flip_far(far3_more)
+    near2, far2, *acc = together(near2, far2, *acc)
+    sends = collect(
+        (near2, far2, deep2),
+        (((2, 0, main), (1, 0, main)), ((2, main, two), (0, main, two))),
+        "collect_more",
+    )
+    near3_more, far3_more = flip_near(sends[0]), flip_far(sends[1])
 
     sends = collect(
         (near3, far3, deep3),

time: 88.8 us -> 88.8 us (level)
  starting transfers between devices: 26.4 us -> 29.6 us
  waiting for transfers between devices: 30.3 us -> 27.2 us
    ppermute x20 -> x21, starting transfers between devices: 26.4 us -> 29.6 us  [permute(): return lax.ppermute(array, 'req', [(i, target(i)) for i in range(count)])]
    ppermute x20 -> x21, waiting for transfers between devices: 30.3 us -> 27.2 us  [permute(): return lax.ppermute(array, 'req', [(i, target(i)) for i in range(count)])]
    pallas_call x14 -> x15, Pallas kernels: 23.6 us -> 23.6 us  [kernel_call(): pl.pallas_call(body, out_shape=out_shape, in_specs=specs or vmem(len(oper...]
  transfers between devices with their start and end apart: 20 -> 21, of which waited for: 13 -> 10; matrix products, arithmetic and copies ran while one was open for 1% -> 1% of each run, Pallas kernels for 21% -> 21%
where the time goes in v18:
time: 88.8 us; the launch traced here: 88.4 us
  starting transfers between devices  29.6 us (33%)
  waiting for transfers between devices  27.2 us (31%)
  Pallas kernels  23.6 us (27%)
  local copies, waits for them, and re-layouts  6.61 us (7%)
  between operations  1.46 us (2%)
    ppermute x21, starting transfers between devices, permute(): return lax.ppermute(array, 'req', [(i, target(i)) for i in range(count)])  29.6 us
    ppermute x21, waiting for transfers between devices, permute(): return lax.ppermute(array, 'req', [(i, target(i)) for i in range(count)])  27.2 us
    pallas_call x15, Pallas kernels, kernel_call(): pl.pallas_call(body, out_shape=out_shape, in_specs=specs or vmem(len(oper...  23.6 us
    unnamed x20, local copies, waits for them, and re-layouts  5.89 us
  transfers between devices with their start and end apart: 21, of which 10 were waited for; matrix products, arithmetic and copies ran while one was open for 1% of the time, Pallas kernels for 21%

profile of v18, /device:TPU:0, one launch (start us, length us, event | category | flops | bytes accessed | tf_op | source)
XLA Modules:
  0.0 88.4 jit_solution(16642153212165694438)
XLA Ops:
  0.6 2.2 %shard.1 = (bf16[168,1792]{1,0:T(8,128)(2,1)}, bf16[144,1792]{1,0:T(8,128)(2,1)}) custom-call(bf16[56,1792]{1,0:T(8,128)(2,1)} %bitcast.17, bf16[56,1792]{1,0:T(8,128)(2,1)} %bitcast.18, bf16[56,1792]{1,0:T(8,128)(2,1)} %bitcast.19), custom_call_target="tpu_custom_call" | custom-call | flops 1000 | bytes 1000 | tf_op jit(solution)/shard_map/shard/pallas_call | solution.py:124
  2.8 3.0 %collective-permute-start = (bf16[168,1792]{1,0:T(8,128)(2,1)}, bf16[168,1792]{1,0:T(8,128)(2,1)S(1)}, u32[]{:S(2)}, u32[]{:S(2)}) collective-permute-start(bf16[168,1792]{1,0:T(8,128)(2,1)} %get-tuple-element.78.refs_0_), channel_id=1, source_target_pairs={{0,2},{1,3},{2,0},{3,1},{4,6},{5,7},{6,4},{7,5},{8,10},{9,11},{10,... | collective-permute-start | bytes 1806344 | tf_op jit(solution)/shard_map/ppermute | solution.py:90
  5.8 1.5 %collective-permute-start.1 = (bf16[168,1792]{1,0:T(8,128)(2,1)}, bf16[168,1792]{1,0:T(8,128)(2,1)S(1)}, u32[]{:S(2)}, u32[]{:S(2)}) collective-permute-start(bf16[168,1792]{1,0:T(8,128)(2,1)} %get-tuple-element.78.refs_0_), channel_id=1, source_target_pairs={{0,4},{1,5},{2,6},{3,7},{4,0},{5,1},{6,2},{7,3},{8,12},{9,13},{10,... | collective-permute-start | bytes 1806344 | tf_op jit(solution)/shard_map/ppermute | solution.py:90
  7.4 2.6 %collective-permute-start.2 = (bf16[144,1792]{1,0:T(8,128)(2,1)}, bf16[144,1792]{1,0:T(8,128)(2,1)S(1)}, u32[]{:S(2)}, u32[]{:S(2)}) collective-permute-start(bf16[144,1792]{1,0:T(8,128)(2,1)} %get-tuple-element.79), channel_id=1, source_target_pairs={{0,16},{1,17},{2,18},{3,19},{4,20},{5,21},{6,22},{7,23},{8,0},{9,1... | collective-permute-start | bytes 1548296 | tf_op jit(solution)/shard_map/ppermute | solution.py:90
  10.0 0.7 broadcast_in_dim.16.gain_ref
  10.7 1.2 %copy-done.1 = bf16[1,256,1792]{2,1,0:T(8,128)(2,1)S(1)} copy-done((bf16[1,256,1792]{2,1,0:T(8,128)(2,1)S(1)}, bf16[1,256,1792]{2,1,0:T(8,128)(2,1)}, u32[]{:S(2)}) %copy-start.1) | copy-done | bytes 917528
  11.9 1.9 %copy-done.3 = bf16[1792,896]{1,0:T(8,128)(2,1)S(1)} copy-done((bf16[1792,896]{1,0:T(8,128)(2,1)S(1)}, bf16[1792,896]{1,0:T(8,128)(2,1)}, u32[]{:S(2)}) %copy-start.3) | copy-done | bytes 3211288
  13.8 1.0 %copy-done.5 = bf16[1792,128]{1,0:T(8,128)(2,1)S(1)} copy-done((bf16[1792,128]{1,0:T(8,128)(2,1)S(1)}, bf16[1792,128]{1,0:T(8,128)(2,1)}, u32[]{:S(2)}) %copy-start.5) | copy-done | bytes 458776
  14.8 1.0 %copy-done.6 = bf16[1792,128]{1,0:T(8,128)(2,1)S(1)} copy-done((bf16[1792,128]{1,0:T(8,128)(2,1)S(1)}, bf16[1792,128]{1,0:T(8,128)(2,1)}, u32[]{:S(2)}) %copy-start.6) | copy-done | bytes 458776
  15.8 0.7 copy-done.7
  16.5 3.7 %project.1 = (bf16[256,128]{1,0:T(8,128)(2,1)S(1)}, bf16[256,128]{1,0:T(8,128)(2,1)S(1)}, bf16[256,896]{1,0:T(8,128)(2,1)S(1)}) custom-call(bf16[256,1792]{1,0:T(8,128)(2,1)S(1)} %bitcast.13, bf16[16,1792]{1,0:T(8,128)(2,1)S(1)} %broadcast_in_dim.15.edge_ref, f32[1,1792]{1,0:T(1,128)S(1)} %broadcast_in_dim.16.gain_ref, f32[3,1792]{1,0:T(4,128)S(1)} %copy-done.7, ...), custom_call_target="tpu_custom_call" | custom-call | flops 1000 | bytes 1000 | tf_op jit(solution)/shard_map/project/pallas_call | solution.py:124
  20.3 0.4 collective-permute-done.2.refs_3_
  20.7 0.4 collective-permute-done.1.refs_2_
  21.1 0.2 collect_second.1
  21.3 1.6 %collective-permute-start.4 = (bf16[232,1792]{1,0:T(8,128)(2,1)S(1)}, bf16[232,1792]{1,0:T(8,128)(2,1)S(1)}, u32[]{:S(2)}, u32[]{:S(2)}) collective-permute-start(bf16[232,1792]{1,0:T(8,128)(2,1)S(1)} %get-tuple-element.90), channel_id=1, source_target_pairs={{0,4},{1,5},{2,6},{3,7},{4,0},{5,1},{6,2},{7,3},{8,12},{9,13},{10,... | collective-permute-start | bytes 2494472 | tf_op jit(solution)/shard_map/ppermute | solution.py:90
  22.9 0.5 collective-permute-start.3
  23.4 2.6 %collective-permute-start.5 = (bf16[216,1792]{1,0:T(8,128)(2,1)S(1)}, bf16[216,1792]{1,0:T(8,128)(2,1)S(1)}, u32[]{:S(2)}, u32[]{:S(2)}) collective-permute-start(bf16[216,1792]{1,0:T(8,128)(2,1)S(1)} %get-tuple-element.91), channel_id=1, source_target_pairs={{0,16},{1,17},{2,18},{3,19},{4,20},{5,21},{6,22},{7,23},{8,0},{9,1... | collective-permute-start | bytes 2322440 | tf_op jit(solution)/shard_map/ppermute | solution.py:90
  26.7 3.7 %attend.1 = (f32[256,896]{1,0:T(8,128)S(1)}, f32[256,8]{1,0:T(8,128)S(1)}, f32[273,1,896]{2,1,0:T(1,128)}, f32[8,273]{1,0:T(8,128)}) custom-call(s32[1]{0:T(128)S(6)} %copy.23.count_ref, f32[8,256]{1,0:T(8,128)S(1)} %bitcast.15, bf16[256,128]{1,0:T(8,128)(2,1)S(1)} %get-tuple-element.95.queries_ref, bf16[256,128]{1,0:T(8,128)(2,1)S(1)} %get-tuple-element.96.keys_ref, ...), custom_call_target="tpu_custom_call" | custom-call | flops 1000 | bytes 1000 | tf_op jit(solution)/shard_map/attend/pallas_call | solution.py:124
  30.4 2.6 %mix.1 = (bf16[256,1792]{1,0:T(8,128)(2,1)S(1)}, bf16[256,1792]{1,0:T(8,128)(2,1)S(1)}) custom-call(f32[256,896]{1,0:T(8,128)S(1)} %get-tuple-element.98.numer_ref, f32[256,8]{1,0:T(8,128)S(1)} %get-tuple-element.99.denom_ref, bf16[256,1792]{1,0:T(8,128)(2,1)S(1)} %bitcast.14, bf16[896,1792]{1,0:T(8,128)(2,1)S(1)} %copy-done.4, ...), custom_call_target="tpu_custom_call" | custom-call | flops 1000 | bytes 1000 | tf_op jit(solution)/shard_map/mix/pallas_call | solution.py:124
  33.0 7.8 %collective-permute-done.5.refs_2_.refs_6_.refs_4_ = bf16[216,1792]{1,0:T(8,128)(2,1)S(1)} collective-permute-done((bf16[216,1792]{1,0:T(8,128)(2,1)S(1)}, bf16[216,1792]{1,0:T(8,128)(2,1)S(1)}, u32[]{:S(2)}, u32[]{:S(2)}) %collective-permute-start.5) | collective-permute-done | bytes 774176 | tf_op jit(solution)/shard_map/ppermute | solution.py:90
  40.8 0.2 collective-permute-done.3.refs_0_.refs_4_
  41.0 0.2 collect_third.1
  41.2 3.3 %collective-permute-start.7 = (bf16[240,1792]{1,0:T(8,128)(2,1)S(1)}, bf16[240,1792]{1,0:T(8,128)(2,1)S(1)}, u32[]{:S(2)}, u32[]{:S(2)}) collective-permute-start(bf16[240,1792]{1,0:T(8,128)(2,1)S(1)} %get-tuple-element.113), channel_id=1, source_target_pairs={{0,16},{1,17},{2,18},{3,19},{4,20},{5,21},{6,22},{7,23},{8,0},{9,1... | collective-permute-start | bytes 2580488 | tf_op jit(solution)/shard_map/ppermute | solution.py:90
  44.5 0.5 collective-permute-start.9
  45.0 1.4 %collective-permute-start.13 = (bf16[224,1792]{1,0:T(8,128)(2,1)S(1)}, bf16[224,1792]{1,0:T(8,128)(2,1)S(1)}, u32[]{:S(2)}, u32[]{:S(2)}) collective-permute-start(bf16[224,1792]{1,0:T(8,128)(2,1)S(1)} %get-tuple-element.124), channel_id=1, source_target_pairs={{0,2},{1,3},{2,0},{3,1},{4,6},{5,7},{6,4},{7,5},{8,10},{9,11},{10,... | collective-permute-start | bytes 2408456 | tf_op jit(solution)/shard_map/ppermute | solution.py:90
  46.4 0.5 collective-permute-start.6
  47.0 1.5 %collective-permute-start.14 = (bf16[144,1792]{1,0:T(8,128)(2,1)S(1)}, bf16[144,1792]{1,0:T(8,128)(2,1)S(1)}, u32[]{:S(2)}, u32[]{:S(2)}) collective-permute-start(bf16[144,1792]{1,0:T(8,128)(2,1)S(1)} %get-tuple-element.125), channel_id=1, source_target_pairs={{0,4},{1,5},{2,6},{3,7},{4,0},{5,1},{6,2},{7,3},{8,12},{9,13},{10,... | collective-permute-start | bytes 1548296 | tf_op jit(solution)/shard_map/ppermute | solution.py:90
  48.5 3.2 %accumulate_second.1 = (f32[256,1792]{1,0:T(8,128)S(1)}, f32[256,1792]{1,0:T(8,128)S(1)}) custom-call(bf16[168,1792]{1,0:T(8,128)(2,1)S(1)} %copy-done, bf16[168,1792]{1,0:T(8,128)(2,1)S(1)} %collective-permute-done.refs_1_, bf16[168,1792]{1,0:T(8,128)(2,1)S(1)} %collective-permute-done.1.refs_2_, bf16[144,1792]{1,0:T(8,128)(2,1)S(1)} %collective-permute-done.2.refs_3_, ...), custom_call_target="tpu_custom_call" | custom-call | flops 1000 | bytes 1000 | tf_op jit(solution)/shard_map/accumulate_second/pallas_call | solution.py:124
  51.7 3.2 %collective-permute-done.6.refs_0_.refs_7_ = bf16[64,1792]{1,0:T(8,128)(2,1)S(1)} collective-permute-done((bf16[64,1792]{1,0:T(8,128)(2,1)S(1)}, bf16[64,1792]{1,0:T(8,128)(2,1)S(1)}, u32[]{:S(2)}, u32[]{:S(2)}) %collective-permute-start.6) | collective-permute-done | bytes 229408 | tf_op jit(solution)/shard_map/ppermute | solution.py:90
  54.9 5.3 %collective-permute-done.7.refs_1_.refs_8_.refs_2_ = bf16[240,1792]{1,0:T(8,128)(2,1)S(1)} collective-permute-done((bf16[240,1792]{1,0:T(8,128)(2,1)S(1)}, bf16[240,1792]{1,0:T(8,128)(2,1)S(1)}, u32[]{:S(2)}, u32[]{:S(2)}) %collective-permute-start.7) | collective-permute-done | bytes 860192 | tf_op jit(solution)/shard_map/ppermute | solution.py:90
  60.3 0.1 collect_fourth.1
  60.4 3.6 %collective-permute-start.12 = (bf16[144,1792]{1,0:T(8,128)(2,1)S(1)}, bf16[144,1792]{1,0:T(8,128)(2,1)S(1)}, u32[]{:S(2)}, u32[]{:S(2)}) collective-permute-start(bf16[144,1792]{1,0:T(8,128)(2,1)S(1)} %get-tuple-element.122), channel_id=1, source_target_pairs={{0,16},{1,17},{2,18},{3,19},{4,20},{5,21},{6,22},{7,23},{8,0},{9,1... | collective-permute-start | bytes 1548296 | tf_op jit(solution)/shard_map/ppermute | solution.py:90
  64.0 1.4 %collective-permute-start.10 = (bf16[96,1792]{1,0:T(8,128)(2,1)S(1)}, bf16[96,1792]{1,0:T(8,128)(2,1)S(1)}, u32[]{:S(2)}, u32[]{:S(2)}) collective-permute-start(bf16[96,1792]{1,0:T(8,128)(2,1)S(1)} %get-tuple-element.120), channel_id=1, source_target_pairs={{0,2},{1,3},{2,0},{3,1},{4,6},{5,7},{6,4},{7,5},{8,10},{9,11},{10,... | collective-permute-start | bytes 1032200 | tf_op jit(solution)/shard_map/ppermute | solution.py:90
  65.3 0.4 collective-permute-start.11
  65.8 3.9 %accumulate_third.1 = (f32[256,1792]{1,0:T(8,128)S(1)}, f32[256,1792]{1,0:T(8,128)S(1)}) custom-call(bf16[168,1792]{1,0:T(8,128)(2,1)S(1)} %copy-done, bf16[168,1792]{1,0:T(8,128)(2,1)S(1)} %collective-permute-done.refs_1_, bf16[168,1792]{1,0:T(8,128)(2,1)S(1)} %collective-permute-done.1.refs_2_, ...), custom_call_target="tpu_custom_call", output_to_operand_aliasing={{0}: (11, {}), {1}: (12, {})} | custom-call | flops 1000 | bytes 1000 | tf_op jit(solution)/shard_map/accumulate_third/pallas_call | solution.py:124
  69.8 1.5 %collective-permute-start.15 = (bf16[96,1792]{1,0:T(8,128)(2,1)S(1)}, bf16[96,1792]{1,0:T(8,128)(2,1)S(1)}, u32[]{:S(2)}, u32[]{:S(2)}) collective-permute-start(bf16[96,1792]{1,0:T(8,128)(2,1)S(1)} %get-tuple-element.132), channel_id=1, source_target_pairs={{0,2},{1,3},{2,0},{3,1},{4,6},{5,7},{6,4},{7,5},{8,10},{9,11},{10,... | collective-permute-start | bytes 1032200 | tf_op jit(solution)/shard_map/ppermute | solution.py:90
  71.2 0.8 collective-permute-start.16
  72.1 1.6 %collective-permute-done.10.refs_0_ = bf16[96,1792]{1,0:T(8,128)(2,1)S(1)} collective-permute-done((bf16[96,1792]{1,0:T(8,128)(2,1)S(1)}, bf16[96,1792]{1,0:T(8,128)(2,1)S(1)}, u32[]{:S(2)}, u32[]{:S(2)}) %collective-permute-start.10) | collective-permute-done | bytes 344096 | tf_op jit(solution)/shard_map/ppermute | solution.py:90
  73.8 1.7 %collective-permute-start.19 = (bf16[72,1792]{1,0:T(8,128)(2,1)S(1)}, bf16[72,1792]{1,0:T(8,128)(2,1)S(1)}, u32[]{:S(2)}, u32[]{:S(2)}) collective-permute-start(bf16[72,1792]{1,0:T(8,128)(2,1)S(1)} %get-tuple-element.138), channel_id=1, source_target_pairs={{0,16},{1,17},{2,18},{3,19},{4,20},{5,21},{6,22},{7,23},{8,0},{9,1... | collective-permute-start | bytes 774152 | tf_op jit(solution)/shard_map/ppermute | solution.py:90
  75.4 1.0 %collective-permute-start.17 = (bf16[48,1792]{1,0:T(8,128)(2,1)S(1)}, bf16[48,1792]{1,0:T(8,128)(2,1)S(1)}, u32[]{:S(2)}, u32[]{:S(2)}) collective-permute-start(bf16[48,1792]{1,0:T(8,128)(2,1)S(1)} %get-tuple-element.136), channel_id=1, source_target_pairs={{0,2},{1,3},{2,0},{3,1},{4,6},{5,7},{6,4},{7,5},{8,10},{9,11},{10,... | collective-permute-start | bytes 516104 | tf_op jit(solution)/shard_map/ppermute | solution.py:90
  76.4 0.2 collective-permute-start.18
  76.6 6.7 %collective-permute-done.17.refs_5_ = bf16[48,1792]{1,0:T(8,128)(2,1)S(1)} collective-permute-done((bf16[48,1792]{1,0:T(8,128)(2,1)S(1)}, bf16[48,1792]{1,0:T(8,128)(2,1)S(1)}, u32[]{:S(2)}, u32[]{:S(2)}) %collective-permute-start.17) | collective-permute-done | bytes 172064 | tf_op jit(solution)/shard_map/ppermute | solution.py:90
  83.2 0.4 collective-permute-done.18.refs_6_
  83.6 1.0 %finish_other.1 = bf16[256,1792]{1,0:T(8,128)(2,1)S(1)} custom-call(bf16[96,1792]{1,0:T(8,128)(2,1)S(1)} %collective-permute-done.10.refs_0_, bf16[96,1792]{1,0:T(8,128)(2,1)S(1)} %collective-permute-done.15.refs_1_, bf16[96,1792]{1,0:T(8,128)(2,1)S(1)} %collective-permute-done.11.refs_1_.refs_2_, bf16[96,1792]{1,0:T(8,128)(2,1)S(1)} %collective-permute-done.16.refs_3_, ...), custom_call_target="tpu_custom_call" | custom-call | flops 1000 | bytes 1000 | tf_op jit(solution)/shard_map/finish_other/pallas_call | solution.py:124
  84.7 0.1 collective-permute-start.20
  84.8 1.4 %finish_own.1.kept_ref = f32[256,1792]{1,0:T(8,128)S(1)} custom-call(bf16[96,1792]{1,0:T(8,128)(2,1)S(1)} %collective-permute-done.10.refs_0_, bf16[96,1792]{1,0:T(8,128)(2,1)S(1)} %collective-permute-done.15.refs_1_, bf16[96,1792]{1,0:T(8,128)(2,1)S(1)} %collective-permute-done.11.refs_1_.refs_2_, ...), custom_call_target="tpu_custom_call", output_to_operand_aliasing={{}: (9, {})} | custom-call | flops 1000 | bytes 1000 | tf_op jit(solution)/shard_map/finish_own/pallas_call | solution.py:124
  86.2 1.0 %collective-permute-done.20.given_ref = bf16[256,1792]{1,0:T(8,128)(2,1)S(1)} collective-permute-done((bf16[256,1792]{1,0:T(8,128)(2,1)S(1)}, bf16[256,1792]{1,0:T(8,128)(2,1)S(1)}, u32[]{:S(2)}, u32[]{:S(2)}) %collective-permute-start.20) | collective-permute-done | bytes 917536 | tf_op jit(solution)/shard_map/ppermute | solution.py:90
  87.2 1.2 %final.1 = bf16[256,1792]{1,0:T(8,128)(2,1)} custom-call(s32[1]{0:T(128)S(6)} %copy.23.count_ref, f32[256,1792]{1,0:T(8,128)S(1)} %finish_own.1.kept_ref, bf16[256,1792]{1,0:T(8,128)(2,1)S(1)} %collective-permute-done.20.given_ref), custom_call_target="tpu_custom_call" | custom-call | flops 1000 | bytes 1000 | tf_op jit(solution)/shard_map/final/pallas_call | solution.py:124
  (32 shorter events, 0.3 us)
Async XLA Ops:
  2.8 17.9 %collective-permute-start = (bf16[168,1792]{1,0:T(8,128)(2,1)}, bf16[168,1792]{1,0:T(8,128)(2,1)S(1)}, u32[]{:S(2)}, u32[]{:S(2)}) collective-permute-start(bf16[168,1792]{1,0:T(8,128)(2,1)} %get-tuple-element.78.refs_0_), channel_id=1, source_target_pairs={{0,2},{1,3},{2,0},{3,1},{4,6},{5,7},{6,4},{7,5},{8,10},{9,11},{10,... | collective-permute-start | bytes 1806344 | tf_op jit(solution)/shard_map/ppermute | solution.py:90
  5.8 15.3 %collective-permute-start.1 = (bf16[168,1792]{1,0:T(8,128)(2,1)}, bf16[168,1792]{1,0:T(8,128)(2,1)S(1)}, u32[]{:S(2)}, u32[]{:S(2)}) collective-permute-start(bf16[168,1792]{1,0:T(8,128)(2,1)} %get-tuple-element.78.refs_0_), channel_id=1, source_target_pairs={{0,4},{1,5},{2,6},{3,7},{4,0},{5,1},{6,2},{7,3},{8,12},{9,13},{10,... | collective-permute-start | bytes 1806344 | tf_op jit(solution)/shard_map/ppermute | solution.py:90
  7.4 13.4 %collective-permute-start.2 = (bf16[144,1792]{1,0:T(8,128)(2,1)}, bf16[144,1792]{1,0:T(8,128)(2,1)S(1)}, u32[]{:S(2)}, u32[]{:S(2)}) collective-permute-start(bf16[144,1792]{1,0:T(8,128)(2,1)} %get-tuple-element.79), channel_id=1, source_target_pairs={{0,16},{1,17},{2,18},{3,19},{4,20},{5,21},{6,22},{7,23},{8,0},{9,1... | collective-permute-start | bytes 1548296 | tf_op jit(solution)/shard_map/ppermute | solution.py:90
  10.7 1.2 %copy-start.1 = (bf16[1,256,1792]{2,1,0:T(8,128)(2,1)S(1)}, bf16[1,256,1792]{2,1,0:T(8,128)(2,1)}, u32[]{:S(2)}) copy-start(bf16[1,256,1792]{2,1,0:T(8,128)(2,1)} %param.13) | copy-start | bytes 2752516
  11.8 1.9 %copy-start.3 = (bf16[1792,896]{1,0:T(8,128)(2,1)S(1)}, bf16[1792,896]{1,0:T(8,128)(2,1)}, u32[]{:S(2)}) copy-start(bf16[1792,896]{1,0:T(8,128)(2,1)} %value_ref.1) | copy-start | bytes 9633796
  13.8 1.0 %copy-start.5 = (bf16[1792,128]{1,0:T(8,128)(2,1)S(1)}, bf16[1792,128]{1,0:T(8,128)(2,1)}, u32[]{:S(2)}) copy-start(bf16[1792,128]{1,0:T(8,128)(2,1)} %query_ref.1) | copy-start | bytes 1376260
  14.8 1.0 %copy-start.6 = (bf16[1792,128]{1,0:T(8,128)(2,1)S(1)}, bf16[1792,128]{1,0:T(8,128)(2,1)}, u32[]{:S(2)}) copy-start(bf16[1792,128]{1,0:T(8,128)(2,1)} %key_ref.1) | copy-start | bytes 1376260
  15.8 0.7 copy-start.7
  16.5 4.6 %copy-start = (bf16[168,1792]{1,0:T(8,128)(2,1)S(1)}, bf16[168,1792]{1,0:T(8,128)(2,1)}, u32[]{:S(2)}) copy-start(bf16[168,1792]{1,0:T(8,128)(2,1)} %get-tuple-element.78.refs_0_) | copy-start | bytes 1806340
  16.5 13.8 %copy-start.4 = (bf16[896,1792]{1,0:T(8,128)(2,1)S(1)}, bf16[896,1792]{1,0:T(8,128)(2,1)}, u32[]{:S(2)}) copy-start(bf16[896,1792]{1,0:T(8,128)(2,1)} %out_ref.1) | copy-start | bytes 9633796
  20.3 6.4 %copy-start.9 = (f32[1792]{0:T(1024)S(1)}, f32[1792]{0:T(1024)}, u32[]{:S(2)}) copy-start(f32[1792]{0:T(1024)} %param.22) | copy-start | bytes 21508
  20.3 6.4 %copy-start.8 = (f32[1,256,8]{1,2,0:T(8,128)S(1)}, f32[1,256,8]{1,2,0:T(8,128)}, u32[]{:S(2)}) copy-start(f32[1,256,8]{1,2,0:T(8,128)} %param.15) | copy-start | bytes 24580
  20.3 10.1 %copy-start.2 = (bf16[1,256,1792]{2,1,0:T(8,128)(2,1)S(1)}, bf16[1,256,1792]{2,1,0:T(8,128)(2,1)}, u32[]{:S(2)}) copy-start(bf16[1,256,1792]{2,1,0:T(8,128)(2,1)} %param.13) | copy-start | bytes 2752516
  21.3 19.8 %collective-permute-start.4 = (bf16[232,1792]{1,0:T(8,128)(2,1)S(1)}, bf16[232,1792]{1,0:T(8,128)(2,1)S(1)}, u32[]{:S(2)}, u32[]{:S(2)}) collective-permute-start(bf16[232,1792]{1,0:T(8,128)(2,1)S(1)} %get-tuple-element.90), channel_id=1, source_target_pairs={{0,4},{1,5},{2,6},{3,7},{4,0},{5,1},{6,2},{7,3},{8,12},{9,13},{10,... | collective-permute-start | bytes 2494472 | tf_op jit(solution)/shard_map/ppermute | solution.py:90
  22.9 18.2 %collective-permute-start.3 = (bf16[224,1792]{1,0:T(8,128)(2,1)S(1)}, bf16[224,1792]{1,0:T(8,128)(2,1)S(1)}, u32[]{:S(2)}, u32[]{:S(2)}) collective-permute-start(bf16[224,1792]{1,0:T(8,128)(2,1)S(1)} %get-tuple-element.89), channel_id=1, source_target_pairs={{0,2},{1,3},{2,0},{3,1},{4,6},{5,7},{6,4},{7,5},{8,10},{9,11},{10,... | collective-permute-start | bytes 2408456 | tf_op jit(solution)/shard_map/ppermute | solution.py:90
  23.4 17.4 %collective-permute-start.5 = (bf16[216,1792]{1,0:T(8,128)(2,1)S(1)}, bf16[216,1792]{1,0:T(8,128)(2,1)S(1)}, u32[]{:S(2)}, u32[]{:S(2)}) collective-permute-start(bf16[216,1792]{1,0:T(8,128)(2,1)S(1)} %get-tuple-element.91), channel_id=1, source_target_pairs={{0,16},{1,17},{2,18},{3,19},{4,20},{5,21},{6,22},{7,23},{8,0},{9,1... | collective-permute-start | bytes 2322440 | tf_op jit(solution)/shard_map/ppermute | solution.py:90
  41.2 19.0 %collective-permute-start.7 = (bf16[240,1792]{1,0:T(8,128)(2,1)S(1)}, bf16[240,1792]{1,0:T(8,128)(2,1)S(1)}, u32[]{:S(2)}, u32[]{:S(2)}) collective-permute-start(bf16[240,1792]{1,0:T(8,128)(2,1)S(1)} %get-tuple-element.113), channel_id=1, source_target_pairs={{0,16},{1,17},{2,18},{3,19},{4,20},{5,21},{6,22},{7,23},{8,0},{9,1... | collective-permute-start | bytes 2580488 | tf_op jit(solution)/shard_map/ppermute | solution.py:90
  44.5 2.5 %collective-permute-start.8 = (bf16[128,1792]{1,0:T(8,128)(2,1)S(1)}, bf16[128,1792]{1,0:T(8,128)(2,1)S(1)}, u32[]{:S(2)}, u32[]{:S(2)}) collective-permute-start(bf16[128,1792]{1,0:T(8,128)(2,1)S(1)} %get-tuple-element.114), channel_id=1, source_target_pairs={{0,1},{1,0},{2,3},{3,2},{4,5},{5,4},{6,7},{7,6},{8,9},{9,8},{10,11... | collective-permute-start | bytes 1376264 | tf_op jit(solution)/shard_map/ppermute | solution.py:90
  44.5 4.0 %collective-permute-start.9 = (bf16[128,1792]{1,0:T(8,128)(2,1)S(1)}, bf16[128,1792]{1,0:T(8,128)(2,1)S(1)}, u32[]{:S(2)}, u32[]{:S(2)}) collective-permute-start(bf16[128,1792]{1,0:T(8,128)(2,1)S(1)} %get-tuple-element.115), channel_id=1, source_target_pairs={{0,1},{1,0},{2,3},{3,2},{4,5},{5,4},{6,7},{7,6},{8,9},{9,8},{10,11... | collective-permute-start | bytes 1376264 | tf_op jit(solution)/shard_map/ppermute | solution.py:90
  45.0 20.8 %collective-permute-start.13 = (bf16[224,1792]{1,0:T(8,128)(2,1)S(1)}, bf16[224,1792]{1,0:T(8,128)(2,1)S(1)}, u32[]{:S(2)}, u32[]{:S(2)}) collective-permute-start(bf16[224,1792]{1,0:T(8,128)(2,1)S(1)} %get-tuple-element.124), channel_id=1, source_target_pairs={{0,2},{1,3},{2,0},{3,1},{4,6},{5,7},{6,4},{7,5},{8,10},{9,11},{10,... | collective-permute-start | bytes 2408456 | tf_op jit(solution)/shard_map/ppermute | solution.py:90
  46.4 8.5 %collective-permute-start.6 = (bf16[64,1792]{1,0:T(8,128)(2,1)S(1)}, bf16[64,1792]{1,0:T(8,128)(2,1)S(1)}, u32[]{:S(2)}, u32[]{:S(2)}) collective-permute-start(bf16[64,1792]{1,0:T(8,128)(2,1)S(1)} %get-tuple-element.112), channel_id=1, source_target_pairs={{0,4},{1,5},{2,6},{3,7},{4,0},{5,1},{6,2},{7,3},{8,12},{9,13},{10,... | collective-permute-start | bytes 688136 | tf_op jit(solution)/shard_map/ppermute | solution.py:90
  47.0 18.8 %collective-permute-start.14 = (bf16[144,1792]{1,0:T(8,128)(2,1)S(1)}, bf16[144,1792]{1,0:T(8,128)(2,1)S(1)}, u32[]{:S(2)}, u32[]{:S(2)}) collective-permute-start(bf16[144,1792]{1,0:T(8,128)(2,1)S(1)} %get-tuple-element.125), channel_id=1, source_target_pairs={{0,4},{1,5},{2,6},{3,7},{4,0},{5,1},{6,2},{7,3},{8,12},{9,13},{10,... | collective-permute-start | bytes 1548296 | tf_op jit(solution)/shard_map/ppermute | solution.py:90
  60.4 13.4 %collective-permute-start.12 = (bf16[144,1792]{1,0:T(8,128)(2,1)S(1)}, bf16[144,1792]{1,0:T(8,128)(2,1)S(1)}, u32[]{:S(2)}, u32[]{:S(2)}) collective-permute-start(bf16[144,1792]{1,0:T(8,128)(2,1)S(1)} %get-tuple-element.122), channel_id=1, source_target_pairs={{0,16},{1,17},{2,18},{3,19},{4,20},{5,21},{6,22},{7,23},{8,0},{9,1... | collective-permute-start | bytes 1548296 | tf_op jit(solution)/shard_map/ppermute | solution.py:90
  64.0 9.7 %collective-permute-start.10 = (bf16[96,1792]{1,0:T(8,128)(2,1)S(1)}, bf16[96,1792]{1,0:T(8,128)(2,1)S(1)}, u32[]{:S(2)}, u32[]{:S(2)}) collective-permute-start(bf16[96,1792]{1,0:T(8,128)(2,1)S(1)} %get-tuple-element.120), channel_id=1, source_target_pairs={{0,2},{1,3},{2,0},{3,1},{4,6},{5,7},{6,4},{7,5},{8,10},{9,11},{10,... | collective-permute-start | bytes 1032200 | tf_op jit(solution)/shard_map/ppermute | solution.py:90
  65.3 8.4 %collective-permute-start.11 = (bf16[96,1792]{1,0:T(8,128)(2,1)S(1)}, bf16[96,1792]{1,0:T(8,128)(2,1)S(1)}, u32[]{:S(2)}, u32[]{:S(2)}) collective-permute-start(bf16[96,1792]{1,0:T(8,128)(2,1)S(1)} %get-tuple-element.121), channel_id=1, source_target_pairs={{0,4},{1,5},{2,6},{3,7},{4,0},{5,1},{6,2},{7,3},{8,12},{9,13},{10,... | collective-permute-start | bytes 1032200 | tf_op jit(solution)/shard_map/ppermute | solution.py:90
  69.8 13.9 %collective-permute-start.15 = (bf16[96,1792]{1,0:T(8,128)(2,1)S(1)}, bf16[96,1792]{1,0:T(8,128)(2,1)S(1)}, u32[]{:S(2)}, u32[]{:S(2)}) collective-permute-start(bf16[96,1792]{1,0:T(8,128)(2,1)S(1)} %get-tuple-element.132), channel_id=1, source_target_pairs={{0,2},{1,3},{2,0},{3,1},{4,6},{5,7},{6,4},{7,5},{8,10},{9,11},{10,... | collective-permute-start | bytes 1032200 | tf_op jit(solution)/shard_map/ppermute | solution.py:90
  71.2 12.4 %collective-permute-start.16 = (bf16[96,1792]{1,0:T(8,128)(2,1)S(1)}, bf16[96,1792]{1,0:T(8,128)(2,1)S(1)}, u32[]{:S(2)}, u32[]{:S(2)}) collective-permute-start(bf16[96,1792]{1,0:T(8,128)(2,1)S(1)} %get-tuple-element.134), channel_id=1, source_target_pairs={{0,4},{1,5},{2,6},{3,7},{4,0},{5,1},{6,2},{7,3},{8,12},{9,13},{10,... | collective-permute-start | bytes 1032200 | tf_op jit(solution)/shard_map/ppermute | solution.py:90
  73.8 9.9 %collective-permute-start.19 = (bf16[72,1792]{1,0:T(8,128)(2,1)S(1)}, bf16[72,1792]{1,0:T(8,128)(2,1)S(1)}, u32[]{:S(2)}, u32[]{:S(2)}) collective-permute-start(bf16[72,1792]{1,0:T(8,128)(2,1)S(1)} %get-tuple-element.138), channel_id=1, source_target_pairs={{0,16},{1,17},{2,18},{3,19},{4,20},{5,21},{6,22},{7,23},{8,0},{9,1... | collective-permute-start | bytes 774152 | tf_op jit(solution)/shard_map/ppermute | solution.py:90
  75.4 7.8 %collective-permute-start.17 = (bf16[48,1792]{1,0:T(8,128)(2,1)S(1)}, bf16[48,1792]{1,0:T(8,128)(2,1)S(1)}, u32[]{:S(2)}, u32[]{:S(2)}) collective-permute-start(bf16[48,1792]{1,0:T(8,128)(2,1)S(1)} %get-tuple-element.136), channel_id=1, source_target_pairs={{0,2},{1,3},{2,0},{3,1},{4,6},{5,7},{6,4},{7,5},{8,10},{9,11},{10,... | collective-permute-start | bytes 516104 | tf_op jit(solution)/shard_map/ppermute | solution.py:90
  76.4 7.2 %collective-permute-start.18 = (bf16[48,1792]{1,0:T(8,128)(2,1)S(1)}, bf16[48,1792]{1,0:T(8,128)(2,1)S(1)}, u32[]{:S(2)}, u32[]{:S(2)}) collective-permute-start(bf16[48,1792]{1,0:T(8,128)(2,1)S(1)} %get-tuple-element.137), channel_id=1, source_target_pairs={{0,4},{1,5},{2,6},{3,7},{4,0},{5,1},{6,2},{7,3},{8,12},{9,13},{10,... | collective-permute-start | bytes 516104 | tf_op jit(solution)/shard_map/ppermute | solution.py:90
  84.7 2.5 %collective-permute-start.20 = (bf16[256,1792]{1,0:T(8,128)(2,1)S(1)}, bf16[256,1792]{1,0:T(8,128)(2,1)S(1)}, u32[]{:S(2)}, u32[]{:S(2)}) collective-permute-start(bf16[256,1792]{1,0:T(8,128)(2,1)S(1)} %finish_other.1), channel_id=1, source_target_pairs={{0,1},{1,0},{2,3},{3,2},{4,5},{5,4},{6,7},{7,6},{8,9},{9,8},{10,11... | collective-permute-start | bytes 2752520 | tf_op jit(solution)/shard_map/ppermute | solution.py:90

commit v19 on v11

--- a/solution.py
+++ b/solution.py
@@ -103,7 +103,7 @@
 
 
 def next_plane(array):
-    return permute(array, lambda i: i ^ (16 if i // 8 in (1, 2) else 8))
+    return permute(array, lambda i: i ^ (8 if i // 8 in (1, 2) else 16))
 
 
 def together(*arrays):

time: 88.1 us -> 88.1 us (level)
  starting transfers between devices: 21.4 us -> 25.5 us
  waiting for transfers between devices: 32.8 us -> 28.8 us
    ppermute x17, starting transfers between devices: 21.4 us -> 25.5 us  [permute(): return lax.ppermute(array, 'req', [(i, target(i)) for i in range(count)])]
    ppermute x17, waiting for transfers between devices: 32.8 us -> 28.8 us  [permute(): return lax.ppermute(array, 'req', [(i, target(i)) for i in range(count)])]
  transfers between devices with their start and end apart: 17 -> 17, of which waited for: 8 -> 9; matrix products, arithmetic and copies ran while one was open for 1% -> 1% of each run, Pallas kernels for 23% -> 23%
where the time goes in v19:
time: 88.1 us; the launch traced here: 87.7 us
  waiting for transfers between devices  28.8 us (33%)
  starting transfers between devices  25.5 us (29%)
  Pallas kernels  25.3 us (29%)
  local copies, waits for them, and re-layouts  6.61 us (8%)
  between operations  1.46 us (2%)
    ppermute x17, waiting for transfers between devices, permute(): return lax.ppermute(array, 'req', [(i, target(i)) for i in range(count)])  28.8 us
    ppermute x17, starting transfers between devices, permute(): return lax.ppermute(array, 'req', [(i, target(i)) for i in range(count)])  25.5 us
    pallas_call x14, Pallas kernels, kernel_call(): pl.pallas_call(body, out_shape=out_shape, in_specs=specs or vmem(len(oper...  25.3 us
    unnamed x20, local copies, waits for them, and re-layouts  5.89 us
  transfers between devices with their start and end apart: 17, of which 9 were waited for; matrix products, arithmetic and copies ran while one was open for 1% of the time, Pallas kernels for 23%

profile of v19, /device:TPU:0, one launch (start us, length us, event | category | flops | bytes accessed | tf_op | source)
XLA Modules:
  0.0 87.7 jit_solution(4110263439365189490)
XLA Ops:
  0.6 2.2 %shard.1 = (bf16[168,1792]{1,0:T(8,128)(2,1)}, bf16[144,1792]{1,0:T(8,128)(2,1)}) custom-call(bf16[56,1792]{1,0:T(8,128)(2,1)} %bitcast.17, bf16[56,1792]{1,0:T(8,128)(2,1)} %bitcast.18, bf16[56,1792]{1,0:T(8,128)(2,1)} %bitcast.19), custom_call_target="tpu_custom_call" | custom-call | flops 1000 | bytes 1000 | tf_op jit(solution)/shard_map/shard/pallas_call | solution.py:124
  2.8 3.0 %collective-permute-start = (bf16[168,1792]{1,0:T(8,128)(2,1)}, bf16[168,1792]{1,0:T(8,128)(2,1)S(1)}, u32[]{:S(2)}, u32[]{:S(2)}) collective-permute-start(bf16[168,1792]{1,0:T(8,128)(2,1)} %get-tuple-element.73.refs_0_), channel_id=1, source_target_pairs={{0,2},{1,3},{2,0},{3,1},{4,6},{5,7},{6,4},{7,5},{8,10},{9,11},{10,... | collective-permute-start | bytes 1806344 | tf_op jit(solution)/shard_map/ppermute | solution.py:90
  5.8 1.5 %collective-permute-start.1 = (bf16[168,1792]{1,0:T(8,128)(2,1)}, bf16[168,1792]{1,0:T(8,128)(2,1)S(1)}, u32[]{:S(2)}, u32[]{:S(2)}) collective-permute-start(bf16[168,1792]{1,0:T(8,128)(2,1)} %get-tuple-element.73.refs_0_), channel_id=1, source_target_pairs={{0,4},{1,5},{2,6},{3,7},{4,0},{5,1},{6,2},{7,3},{8,12},{9,13},{10,... | collective-permute-start | bytes 1806344 | tf_op jit(solution)/shard_map/ppermute | solution.py:90
  7.4 2.6 %collective-permute-start.2 = (bf16[144,1792]{1,0:T(8,128)(2,1)}, bf16[144,1792]{1,0:T(8,128)(2,1)S(1)}, u32[]{:S(2)}, u32[]{:S(2)}) collective-permute-start(bf16[144,1792]{1,0:T(8,128)(2,1)} %get-tuple-element.74), channel_id=1, source_target_pairs={{0,16},{1,17},{2,18},{3,19},{4,20},{5,21},{6,22},{7,23},{8,0},{9,1... | collective-permute-start | bytes 1548296 | tf_op jit(solution)/shard_map/ppermute | solution.py:90
  10.0 0.7 broadcast_in_dim.16.gain_ref
  10.7 0.0 copy-start.1
  10.7 1.2 %copy-done.1 = bf16[1,256,1792]{2,1,0:T(8,128)(2,1)S(1)} copy-done((bf16[1,256,1792]{2,1,0:T(8,128)(2,1)S(1)}, bf16[1,256,1792]{2,1,0:T(8,128)(2,1)}, u32[]{:S(2)}) %copy-start.1) | copy-done | bytes 917528
  11.9 1.9 %copy-done.3 = bf16[1792,896]{1,0:T(8,128)(2,1)S(1)} copy-done((bf16[1792,896]{1,0:T(8,128)(2,1)S(1)}, bf16[1792,896]{1,0:T(8,128)(2,1)}, u32[]{:S(2)}) %copy-start.3) | copy-done | bytes 3211288
  13.8 1.0 %copy-done.5 = bf16[1792,128]{1,0:T(8,128)(2,1)S(1)} copy-done((bf16[1792,128]{1,0:T(8,128)(2,1)S(1)}, bf16[1792,128]{1,0:T(8,128)(2,1)}, u32[]{:S(2)}) %copy-start.5) | copy-done | bytes 458776
  14.8 1.0 %copy-done.6 = bf16[1792,128]{1,0:T(8,128)(2,1)S(1)} copy-done((bf16[1792,128]{1,0:T(8,128)(2,1)S(1)}, bf16[1792,128]{1,0:T(8,128)(2,1)}, u32[]{:S(2)}) %copy-start.6) | copy-done | bytes 458776
  15.8 0.7 copy-done.7
  16.5 3.7 %project.1 = (bf16[256,128]{1,0:T(8,128)(2,1)S(1)}, bf16[256,128]{1,0:T(8,128)(2,1)S(1)}, bf16[256,896]{1,0:T(8,128)(2,1)S(1)}) custom-call(bf16[256,1792]{1,0:T(8,128)(2,1)S(1)} %bitcast.13, bf16[16,1792]{1,0:T(8,128)(2,1)S(1)} %broadcast_in_dim.15.edge_ref, f32[1,1792]{1,0:T(1,128)S(1)} %broadcast_in_dim.16.gain_ref, f32[3,1792]{1,0:T(4,128)S(1)} %copy-done.7, ...), custom_call_target="tpu_custom_call" | custom-call | flops 1000 | bytes 1000 | tf_op jit(solution)/shard_map/project/pallas_call | solution.py:124
  20.3 0.0 copy-start.9
  20.3 0.0 copy-start.2
  20.3 0.4 collective-permute-done.2.refs_3_
  20.7 0.4 collective-permute-done.1.refs_2_
  21.1 0.2 collect_second.1
  21.3 1.6 %collective-permute-start.4 = (bf16[232,1792]{1,0:T(8,128)(2,1)S(1)}, bf16[232,1792]{1,0:T(8,128)(2,1)S(1)}, u32[]{:S(2)}, u32[]{:S(2)}) collective-permute-start(bf16[232,1792]{1,0:T(8,128)(2,1)S(1)} %get-tuple-element.85), channel_id=1, source_target_pairs={{0,4},{1,5},{2,6},{3,7},{4,0},{5,1},{6,2},{7,3},{8,12},{9,13},{10,... | collective-permute-start | bytes 2494472 | tf_op jit(solution)/shard_map/ppermute | solution.py:90
  22.9 0.5 collective-permute-start.3
  23.4 2.6 %collective-permute-start.5 = (bf16[216,1792]{1,0:T(8,128)(2,1)S(1)}, bf16[216,1792]{1,0:T(8,128)(2,1)S(1)}, u32[]{:S(2)}, u32[]{:S(2)}) collective-permute-start(bf16[216,1792]{1,0:T(8,128)(2,1)S(1)} %get-tuple-element.86), channel_id=1, source_target_pairs={{0,16},{1,17},{2,18},{3,19},{4,20},{5,21},{6,22},{7,23},{8,0},{9,1... | collective-permute-start | bytes 2322440 | tf_op jit(solution)/shard_map/ppermute | solution.py:90
  26.7 3.7 %attend.1 = (f32[256,896]{1,0:T(8,128)S(1)}, f32[256,8]{1,0:T(8,128)S(1)}, f32[273,1,896]{2,1,0:T(1,128)}, f32[8,273]{1,0:T(8,128)}) custom-call(s32[1]{0:T(128)S(6)} %copy.27.count_ref, f32[8,256]{1,0:T(8,128)S(1)} %bitcast.15, bf16[256,128]{1,0:T(8,128)(2,1)S(1)} %get-tuple-element.90.queries_ref, bf16[256,128]{1,0:T(8,128)(2,1)S(1)} %get-tuple-element.91.keys_ref, ...), custom_call_target="tpu_custom_call" | custom-call | flops 1000 | bytes 1000 | tf_op jit(solution)/shard_map/attend/pallas_call | solution.py:124
  30.4 2.6 %mix.1 = (bf16[256,1792]{1,0:T(8,128)(2,1)S(1)}, bf16[256,1792]{1,0:T(8,128)(2,1)S(1)}) custom-call(f32[256,896]{1,0:T(8,128)S(1)} %get-tuple-element.93.numer_ref, f32[256,8]{1,0:T(8,128)S(1)} %get-tuple-element.94.denom_ref, bf16[256,1792]{1,0:T(8,128)(2,1)S(1)} %bitcast.14, bf16[896,1792]{1,0:T(8,128)(2,1)S(1)} %copy-done.4, ...), custom_call_target="tpu_custom_call" | custom-call | flops 1000 | bytes 1000 | tf_op jit(solution)/shard_map/mix/pallas_call | solution.py:124
  33.0 7.8 %collective-permute-done.5.refs_2_.refs_6_.refs_4_ = bf16[216,1792]{1,0:T(8,128)(2,1)S(1)} collective-permute-done((bf16[216,1792]{1,0:T(8,128)(2,1)S(1)}, bf16[216,1792]{1,0:T(8,128)(2,1)S(1)}, u32[]{:S(2)}, u32[]{:S(2)}) %collective-permute-start.5) | collective-permute-done | bytes 774176 | tf_op jit(solution)/shard_map/ppermute | solution.py:90
  40.8 0.2 collective-permute-done.3.refs_0_.refs_4_
  41.0 0.2 collect_third.1
  41.2 3.3 %collective-permute-start.8 = (bf16[240,1792]{1,0:T(8,128)(2,1)S(1)}, bf16[240,1792]{1,0:T(8,128)(2,1)S(1)}, u32[]{:S(2)}, u32[]{:S(2)}) collective-permute-start(bf16[240,1792]{1,0:T(8,128)(2,1)S(1)} %get-tuple-element.104), channel_id=1, source_target_pairs={{0,16},{1,17},{2,18},{3,19},{4,20},{5,21},{6,22},{7,23},{8,0},{9,1... | collective-permute-start | bytes 2580488 | tf_op jit(solution)/shard_map/ppermute | solution.py:90
  44.4 1.4 %collective-permute-start.6 = (bf16[224,1792]{1,0:T(8,128)(2,1)S(1)}, bf16[224,1792]{1,0:T(8,128)(2,1)S(1)}, u32[]{:S(2)}, u32[]{:S(2)}) collective-permute-start(bf16[224,1792]{1,0:T(8,128)(2,1)S(1)} %get-tuple-element.102), channel_id=1, source_target_pairs={{0,2},{1,3},{2,0},{3,1},{4,6},{5,7},{6,4},{7,5},{8,10},{9,11},{10,... | collective-permute-start | bytes 2408456 | tf_op jit(solution)/shard_map/ppermute | solution.py:90
  45.9 0.5 collective-permute-start.7
  46.4 15.7 %collective-permute-done.7.refs_0_.refs_6_.refs_1_ = bf16[208,1792]{1,0:T(8,128)(2,1)S(1)} collective-permute-done((bf16[208,1792]{1,0:T(8,128)(2,1)S(1)}, bf16[208,1792]{1,0:T(8,128)(2,1)S(1)}, u32[]{:S(2)}, u32[]{:S(2)}) %collective-permute-start.7) | collective-permute-done | bytes 745504 | tf_op jit(solution)/shard_map/ppermute | solution.py:90
  62.1 0.1 collect_fourth.1
  62.1 0.2 collective-permute-start.10
  62.3 1.6 %collective-permute-start.9 = (bf16[144,1792]{1,0:T(8,128)(2,1)S(1)}, bf16[144,1792]{1,0:T(8,128)(2,1)S(1)}, u32[]{:S(2)}, u32[]{:S(2)}) collective-permute-start(bf16[144,1792]{1,0:T(8,128)(2,1)S(1)} %get-tuple-element.111), channel_id=1, source_target_pairs={{0,2},{1,3},{2,0},{3,1},{4,6},{5,7},{6,4},{7,5},{8,10},{9,11},{10,... | collective-permute-start | bytes 1548296 | tf_op jit(solution)/shard_map/ppermute | solution.py:90
  63.9 1.4 %collective-permute-start.11 = (bf16[128,1792]{1,0:T(8,128)(2,1)S(1)}, bf16[128,1792]{1,0:T(8,128)(2,1)S(1)}, u32[]{:S(2)}, u32[]{:S(2)}) collective-permute-start(bf16[128,1792]{1,0:T(8,128)(2,1)S(1)} %get-tuple-element.112), channel_id=1, source_target_pairs={{0,16},{1,17},{2,18},{3,19},{4,20},{5,21},{6,22},{7,23},{8,0},{9,1... | collective-permute-start | bytes 1376264 | tf_op jit(solution)/shard_map/ppermute | solution.py:90
  65.3 3.2 %accumulate_second.1 = (f32[256,1792]{1,0:T(8,128)S(1)}, f32[256,1792]{1,0:T(8,128)S(1)}) custom-call(bf16[168,1792]{1,0:T(8,128)(2,1)S(1)} %copy-done, bf16[168,1792]{1,0:T(8,128)(2,1)S(1)} %collective-permute-done.refs_1_, bf16[168,1792]{1,0:T(8,128)(2,1)S(1)} %collective-permute-done.1.refs_2_, bf16[144,1792]{1,0:T(8,128)(2,1)S(1)} %collective-permute-done.2.refs_3_, ...), custom_call_target="tpu_custom_call" | custom-call | flops 1000 | bytes 1000 | tf_op jit(solution)/shard_map/accumulate_second/pallas_call | solution.py:124
  68.5 3.9 %accumulate_third.1 = (f32[256,1792]{1,0:T(8,128)S(1)}, f32[256,1792]{1,0:T(8,128)S(1)}) custom-call(bf16[168,1792]{1,0:T(8,128)(2,1)S(1)} %copy-done, bf16[168,1792]{1,0:T(8,128)(2,1)S(1)} %collective-permute-done.refs_1_, bf16[168,1792]{1,0:T(8,128)(2,1)S(1)} %collective-permute-done.1.refs_2_, ...), custom_call_target="tpu_custom_call", output_to_operand_aliasing={{0}: (10, {}), {1}: (11, {})} | custom-call | flops 1000 | bytes 1000 | tf_op jit(solution)/shard_map/accumulate_third/pallas_call | solution.py:124
  72.5 1.2 %collective-permute-done.9.refs_2_.refs_0_ = bf16[144,1792]{1,0:T(8,128)(2,1)S(1)} collective-permute-done((bf16[144,1792]{1,0:T(8,128)(2,1)S(1)}, bf16[144,1792]{1,0:T(8,128)(2,1)S(1)}, u32[]{:S(2)}, u32[]{:S(2)}) %collective-permute-start.9) | collective-permute-done | bytes 516128 | tf_op jit(solution)/shard_map/ppermute | solution.py:90
  73.7 0.1 collect_fifth.1
  73.7 1.4 %collective-permute-start.13 = (bf16[112,1792]{1,0:T(8,128)(2,1)S(1)}, bf16[112,1792]{1,0:T(8,128)(2,1)S(1)}, u32[]{:S(2)}, u32[]{:S(2)}) collective-permute-start(bf16[112,1792]{1,0:T(8,128)(2,1)S(1)} %get-tuple-element.124), channel_id=1, source_target_pairs={{0,2},{1,3},{2,0},{3,1},{4,6},{5,7},{6,4},{7,5},{8,10},{9,11},{10,... | collective-permute-start | bytes 1204232 | tf_op jit(solution)/shard_map/ppermute | solution.py:90
  75.1 1.7 %collective-permute-start.14 = (bf16[112,1792]{1,0:T(8,128)(2,1)S(1)}, bf16[112,1792]{1,0:T(8,128)(2,1)S(1)}, u32[]{:S(2)}, u32[]{:S(2)}) collective-permute-start(bf16[112,1792]{1,0:T(8,128)(2,1)S(1)} %get-tuple-element.125), channel_id=1, source_target_pairs={{0,4},{1,5},{2,6},{3,7},{4,0},{5,1},{6,2},{7,3},{8,12},{9,13},{10,... | collective-permute-start | bytes 1204232 | tf_op jit(solution)/shard_map/ppermute | solution.py:90
  76.8 2.2 %collective-permute-start.15 = (bf16[56,1792]{1,0:T(8,128)(2,1)S(1)}, bf16[56,1792]{1,0:T(8,128)(2,1)S(1)}, u32[]{:S(2)}, u32[]{:S(2)}) collective-permute-start(bf16[56,1792]{1,0:T(8,128)(2,1)S(1)} %get-tuple-element.126), channel_id=1, source_target_pairs={{0,16},{1,17},{2,18},{3,19},{4,20},{5,21},{6,22},{7,23},{8,0},{9,1... | collective-permute-start | bytes 602120 | tf_op jit(solution)/shard_map/ppermute | solution.py:90
  79.0 2.0 %accumulate_fourth.1 = (f32[256,1792]{1,0:T(8,128)S(1)}, f32[256,1792]{1,0:T(8,128)S(1)}) custom-call(bf16[144,1792]{1,0:T(8,128)(2,1)S(1)} %collective-permute-done.9.refs_2_.refs_0_, bf16[144,1792]{1,0:T(8,128)(2,1)S(1)} %collective-permute-done.10.refs_3_.refs_1_, ...), custom_call_target="tpu_custom_call", output_to_operand_aliasing={{0}: (5, {}), {1}: (6, {})} | custom-call | flops 1000 | bytes 1000 | tf_op jit(solution)/shard_map/accumulate_fourth/pallas_call | solution.py:124
  81.0 1.5 %collective-permute-done.15.refs_3_ = bf16[56,1792]{1,0:T(8,128)(2,1)S(1)} collective-permute-done((bf16[56,1792]{1,0:T(8,128)(2,1)S(1)}, bf16[56,1792]{1,0:T(8,128)(2,1)S(1)}, u32[]{:S(2)}, u32[]{:S(2)}) %collective-permute-start.15) | collective-permute-done | bytes 200736 | tf_op jit(solution)/shard_map/ppermute | solution.py:90
  82.6 0.4 collective-permute-done.14.refs_1_
  83.0 1.0 %finish_other.1 = bf16[256,1792]{1,0:T(8,128)(2,1)S(1)} custom-call(bf16[112,1792]{1,0:T(8,128)(2,1)S(1)} %collective-permute-done.13.refs_0_, bf16[112,1792]{1,0:T(8,128)(2,1)S(1)} %collective-permute-done.14.refs_1_, bf16[128,1792]{1,0:T(8,128)(2,1)S(1)} %collective-permute-done.11.refs_4_.refs_2_, bf16[56,1792]{1,0:T(8,128)(2,1)S(1)} %collective-permute-done.15.refs_3_, ...), custom_call_target="tpu_custom_call" | custom-call | flops 1000 | bytes 1000 | tf_op jit(solution)/shard_map/finish_other/pallas_call | solution.py:124
  84.0 0.1 collective-permute-start.16
  84.1 1.4 %finish_own.1.kept_ref = f32[256,1792]{1,0:T(8,128)S(1)} custom-call(bf16[112,1792]{1,0:T(8,128)(2,1)S(1)} %collective-permute-done.13.refs_0_, bf16[112,1792]{1,0:T(8,128)(2,1)S(1)} %collective-permute-done.14.refs_1_, bf16[128,1792]{1,0:T(8,128)(2,1)S(1)} %collective-permute-done.11.refs_4_.refs_2_, ...), custom_call_target="tpu_custom_call", output_to_operand_aliasing={{}: (5, {})} | custom-call | flops 1000 | bytes 1000 | tf_op jit(solution)/shard_map/finish_own/pallas_call | solution.py:124
  85.5 1.1 %collective-permute-done.16.given_ref = bf16[256,1792]{1,0:T(8,128)(2,1)S(1)} collective-permute-done((bf16[256,1792]{1,0:T(8,128)(2,1)S(1)}, bf16[256,1792]{1,0:T(8,128)(2,1)S(1)}, u32[]{:S(2)}, u32[]{:S(2)}) %collective-permute-start.16) | collective-permute-done | bytes 917536 | tf_op jit(solution)/shard_map/ppermute | solution.py:90
  86.5 1.2 %final.1 = bf16[256,1792]{1,0:T(8,128)(2,1)} custom-call(s32[1]{0:T(128)S(6)} %copy.27.count_ref, f32[256,1792]{1,0:T(8,128)S(1)} %finish_own.1.kept_ref, bf16[256,1792]{1,0:T(8,128)(2,1)S(1)} %collective-permute-done.16.given_ref), custom_call_target="tpu_custom_call" | custom-call | flops 1000 | bytes 1000 | tf_op jit(solution)/shard_map/final/pallas_call | solution.py:124
  (23 shorter events, 0.1 us)
Async XLA Ops:
  2.8 17.9 %collective-permute-start = (bf16[168,1792]{1,0:T(8,128)(2,1)}, bf16[168,1792]{1,0:T(8,128)(2,1)S(1)}, u32[]{:S(2)}, u32[]{:S(2)}) collective-permute-start(bf16[168,1792]{1,0:T(8,128)(2,1)} %get-tuple-element.73.refs_0_), channel_id=1, source_target_pairs={{0,2},{1,3},{2,0},{3,1},{4,6},{5,7},{6,4},{7,5},{8,10},{9,11},{10,... | collective-permute-start | bytes 1806344 | tf_op jit(solution)/shard_map/ppermute | solution.py:90
  5.8 15.3 %collective-permute-start.1 = (bf16[168,1792]{1,0:T(8,128)(2,1)}, bf16[168,1792]{1,0:T(8,128)(2,1)S(1)}, u32[]{:S(2)}, u32[]{:S(2)}) collective-permute-start(bf16[168,1792]{1,0:T(8,128)(2,1)} %get-tuple-element.73.refs_0_), channel_id=1, source_target_pairs={{0,4},{1,5},{2,6},{3,7},{4,0},{5,1},{6,2},{7,3},{8,12},{9,13},{10,... | collective-permute-start | bytes 1806344 | tf_op jit(solution)/shard_map/ppermute | solution.py:90
  7.4 13.4 %collective-permute-start.2 = (bf16[144,1792]{1,0:T(8,128)(2,1)}, bf16[144,1792]{1,0:T(8,128)(2,1)S(1)}, u32[]{:S(2)}, u32[]{:S(2)}) collective-permute-start(bf16[144,1792]{1,0:T(8,128)(2,1)} %get-tuple-element.74), channel_id=1, source_target_pairs={{0,16},{1,17},{2,18},{3,19},{4,20},{5,21},{6,22},{7,23},{8,0},{9,1... | collective-permute-start | bytes 1548296 | tf_op jit(solution)/shard_map/ppermute | solution.py:90
  10.7 1.2 %copy-start.1 = (bf16[1,256,1792]{2,1,0:T(8,128)(2,1)S(1)}, bf16[1,256,1792]{2,1,0:T(8,128)(2,1)}, u32[]{:S(2)}) copy-start(bf16[1,256,1792]{2,1,0:T(8,128)(2,1)} %param.13) | copy-start | bytes 2752516
  11.8 1.9 %copy-start.3 = (bf16[1792,896]{1,0:T(8,128)(2,1)S(1)}, bf16[1792,896]{1,0:T(8,128)(2,1)}, u32[]{:S(2)}) copy-start(bf16[1792,896]{1,0:T(8,128)(2,1)} %value_ref.1) | copy-start | bytes 9633796
  13.8 1.0 %copy-start.5 = (bf16[1792,128]{1,0:T(8,128)(2,1)S(1)}, bf16[1792,128]{1,0:T(8,128)(2,1)}, u32[]{:S(2)}) copy-start(bf16[1792,128]{1,0:T(8,128)(2,1)} %query_ref.1) | copy-start | bytes 1376260
  14.8 1.0 %copy-start.6 = (bf16[1792,128]{1,0:T(8,128)(2,1)S(1)}, bf16[1792,128]{1,0:T(8,128)(2,1)}, u32[]{:S(2)}) copy-start(bf16[1792,128]{1,0:T(8,128)(2,1)} %key_ref.1) | copy-start | bytes 1376260
  15.8 0.7 copy-start.7
  16.5 4.6 %copy-start = (bf16[168,1792]{1,0:T(8,128)(2,1)S(1)}, bf16[168,1792]{1,0:T(8,128)(2,1)}, u32[]{:S(2)}) copy-start(bf16[168,1792]{1,0:T(8,128)(2,1)} %get-tuple-element.73.refs_0_) | copy-start | bytes 1806340
  16.5 13.8 %copy-start.4 = (bf16[896,1792]{1,0:T(8,128)(2,1)S(1)}, bf16[896,1792]{1,0:T(8,128)(2,1)}, u32[]{:S(2)}) copy-start(bf16[896,1792]{1,0:T(8,128)(2,1)} %out_ref.1) | copy-start | bytes 9633796
  20.3 6.4 %copy-start.9 = (f32[1792]{0:T(1024)S(1)}, f32[1792]{0:T(1024)}, u32[]{:S(2)}) copy-start(f32[1792]{0:T(1024)} %param.22) | copy-start | bytes 21508
  20.3 6.4 %copy-start.8 = (f32[1,256,8]{1,2,0:T(8,128)S(1)}, f32[1,256,8]{1,2,0:T(8,128)}, u32[]{:S(2)}) copy-start(f32[1,256,8]{1,2,0:T(8,128)} %param.15) | copy-start | bytes 24580
  20.3 10.1 %copy-start.2 = (bf16[1,256,1792]{2,1,0:T(8,128)(2,1)S(1)}, bf16[1,256,1792]{2,1,0:T(8,128)(2,1)}, u32[]{:S(2)}) copy-start(bf16[1,256,1792]{2,1,0:T(8,128)(2,1)} %param.13) | copy-start | bytes 2752516
  21.3 19.8 %collective-permute-start.4 = (bf16[232,1792]{1,0:T(8,128)(2,1)S(1)}, bf16[232,1792]{1,0:T(8,128)(2,1)S(1)}, u32[]{:S(2)}, u32[]{:S(2)}) collective-permute-start(bf16[232,1792]{1,0:T(8,128)(2,1)S(1)} %get-tuple-element.85), channel_id=1, source_target_pairs={{0,4},{1,5},{2,6},{3,7},{4,0},{5,1},{6,2},{7,3},{8,12},{9,13},{10,... | collective-permute-start | bytes 2494472 | tf_op jit(solution)/shard_map/ppermute | solution.py:90
  22.9 18.2 %collective-permute-start.3 = (bf16[224,1792]{1,0:T(8,128)(2,1)S(1)}, bf16[224,1792]{1,0:T(8,128)(2,1)S(1)}, u32[]{:S(2)}, u32[]{:S(2)}) collective-permute-start(bf16[224,1792]{1,0:T(8,128)(2,1)S(1)} %get-tuple-element.84), channel_id=1, source_target_pairs={{0,2},{1,3},{2,0},{3,1},{4,6},{5,7},{6,4},{7,5},{8,10},{9,11},{10,... | collective-permute-start | bytes 2408456 | tf_op jit(solution)/shard_map/ppermute | solution.py:90
  23.4 17.4 %collective-permute-start.5 = (bf16[216,1792]{1,0:T(8,128)(2,1)S(1)}, bf16[216,1792]{1,0:T(8,128)(2,1)S(1)}, u32[]{:S(2)}, u32[]{:S(2)}) collective-permute-start(bf16[216,1792]{1,0:T(8,128)(2,1)S(1)} %get-tuple-element.86), channel_id=1, source_target_pairs={{0,16},{1,17},{2,18},{3,19},{4,20},{5,21},{6,22},{7,23},{8,0},{9,1... | collective-permute-start | bytes 2322440 | tf_op jit(solution)/shard_map/ppermute | solution.py:90
  41.2 20.9 %collective-permute-start.8 = (bf16[240,1792]{1,0:T(8,128)(2,1)S(1)}, bf16[240,1792]{1,0:T(8,128)(2,1)S(1)}, u32[]{:S(2)}, u32[]{:S(2)}) collective-permute-start(bf16[240,1792]{1,0:T(8,128)(2,1)S(1)} %get-tuple-element.104), channel_id=1, source_target_pairs={{0,16},{1,17},{2,18},{3,19},{4,20},{5,21},{6,22},{7,23},{8,0},{9,1... | collective-permute-start | bytes 2580488 | tf_op jit(solution)/shard_map/ppermute | solution.py:90
  44.4 17.6 %collective-permute-start.6 = (bf16[224,1792]{1,0:T(8,128)(2,1)S(1)}, bf16[224,1792]{1,0:T(8,128)(2,1)S(1)}, u32[]{:S(2)}, u32[]{:S(2)}) collective-permute-start(bf16[224,1792]{1,0:T(8,128)(2,1)S(1)} %get-tuple-element.102), channel_id=1, source_target_pairs={{0,2},{1,3},{2,0},{3,1},{4,6},{5,7},{6,4},{7,5},{8,10},{9,11},{10,... | collective-permute-start | bytes 2408456 | tf_op jit(solution)/shard_map/ppermute | solution.py:90
  45.9 16.2 %collective-permute-start.7 = (bf16[208,1792]{1,0:T(8,128)(2,1)S(1)}, bf16[208,1792]{1,0:T(8,128)(2,1)S(1)}, u32[]{:S(2)}, u32[]{:S(2)}) collective-permute-start(bf16[208,1792]{1,0:T(8,128)(2,1)S(1)} %get-tuple-element.103), channel_id=1, source_target_pairs={{0,4},{1,5},{2,6},{3,7},{4,0},{5,1},{6,2},{7,3},{8,12},{9,13},{10,... | collective-permute-start | bytes 2236424 | tf_op jit(solution)/shard_map/ppermute | solution.py:90
  46.4 18.9 %collective-permute-start.12 = (bf16[256,1792]{1,0:T(8,128)(2,1)S(1)}, bf16[256,1792]{1,0:T(8,128)(2,1)S(1)}, u32[]{:S(2)}, u32[]{:S(2)}) collective-permute-start(bf16[256,1792]{1,0:T(8,128)(2,1)S(1)} %get-tuple-element.116.refs_7_.refs_8_.refs_3_.refs_4_), channel_id=1, source_target_pairs={{0,1},{1,0},{2,3},{3,2},{4,5},{5,4},{6,7},{7,6},{8,9},{9,8},{10,11... | collective-permute-start | bytes 2752520 | tf_op jit(solution)/shard_map/ppermute | solution.py:90
  62.1 10.3 %collective-permute-start.10 = (bf16[144,1792]{1,0:T(8,128)(2,1)S(1)}, bf16[144,1792]{1,0:T(8,128)(2,1)S(1)}, u32[]{:S(2)}, u32[]{:S(2)}) collective-permute-start(bf16[144,1792]{1,0:T(8,128)(2,1)S(1)} %get-tuple-element.111), channel_id=1, source_target_pairs={{0,4},{1,5},{2,6},{3,7},{4,0},{5,1},{6,2},{7,3},{8,12},{9,13},{10,... | collective-permute-start | bytes 1548296 | tf_op jit(solution)/shard_map/ppermute | solution.py:90
  62.3 11.4 %collective-permute-start.9 = (bf16[144,1792]{1,0:T(8,128)(2,1)S(1)}, bf16[144,1792]{1,0:T(8,128)(2,1)S(1)}, u32[]{:S(2)}, u32[]{:S(2)}) collective-permute-start(bf16[144,1792]{1,0:T(8,128)(2,1)S(1)} %get-tuple-element.111), channel_id=1, source_target_pairs={{0,2},{1,3},{2,0},{3,1},{4,6},{5,7},{6,4},{7,5},{8,10},{9,11},{10,... | collective-permute-start | bytes 1548296 | tf_op jit(solution)/shard_map/ppermute | solution.py:90
  63.9 8.5 %collective-permute-start.11 = (bf16[128,1792]{1,0:T(8,128)(2,1)S(1)}, bf16[128,1792]{1,0:T(8,128)(2,1)S(1)}, u32[]{:S(2)}, u32[]{:S(2)}) collective-permute-start(bf16[128,1792]{1,0:T(8,128)(2,1)S(1)} %get-tuple-element.112), channel_id=1, source_target_pairs={{0,16},{1,17},{2,18},{3,19},{4,20},{5,21},{6,22},{7,23},{8,0},{9,1... | collective-permute-start | bytes 1376264 | tf_op jit(solution)/shard_map/ppermute | solution.py:90
  73.7 8.8 %collective-permute-start.13 = (bf16[112,1792]{1,0:T(8,128)(2,1)S(1)}, bf16[112,1792]{1,0:T(8,128)(2,1)S(1)}, u32[]{:S(2)}, u32[]{:S(2)}) collective-permute-start(bf16[112,1792]{1,0:T(8,128)(2,1)S(1)} %get-tuple-element.124), channel_id=1, source_target_pairs={{0,2},{1,3},{2,0},{3,1},{4,6},{5,7},{6,4},{7,5},{8,10},{9,11},{10,... | collective-permute-start | bytes 1204232 | tf_op jit(solution)/shard_map/ppermute | solution.py:90
  75.1 7.9 %collective-permute-start.14 = (bf16[112,1792]{1,0:T(8,128)(2,1)S(1)}, bf16[112,1792]{1,0:T(8,128)(2,1)S(1)}, u32[]{:S(2)}, u32[]{:S(2)}) collective-permute-start(bf16[112,1792]{1,0:T(8,128)(2,1)S(1)} %get-tuple-element.125), channel_id=1, source_target_pairs={{0,4},{1,5},{2,6},{3,7},{4,0},{5,1},{6,2},{7,3},{8,12},{9,13},{10,... | collective-permute-start | bytes 1204232 | tf_op jit(solution)/shard_map/ppermute | solution.py:90
  76.8 5.7 %collective-permute-start.15 = (bf16[56,1792]{1,0:T(8,128)(2,1)S(1)}, bf16[56,1792]{1,0:T(8,128)(2,1)S(1)}, u32[]{:S(2)}, u32[]{:S(2)}) collective-permute-start(bf16[56,1792]{1,0:T(8,128)(2,1)S(1)} %get-tuple-element.126), channel_id=1, source_target_pairs={{0,16},{1,17},{2,18},{3,19},{4,20},{5,21},{6,22},{7,23},{8,0},{9,1... | collective-permute-start | bytes 602120 | tf_op jit(solution)/shard_map/ppermute | solution.py:90
  84.0 2.5 %collective-permute-start.16 = (bf16[256,1792]{1,0:T(8,128)(2,1)S(1)}, bf16[256,1792]{1,0:T(8,128)(2,1)S(1)}, u32[]{:S(2)}, u32[]{:S(2)}) collective-permute-start(bf16[256,1792]{1,0:T(8,128)(2,1)S(1)} %finish_other.1), channel_id=1, source_target_pairs={{0,1},{1,0},{2,3},{3,2},{4,5},{5,4},{6,7},{7,6},{8,9},{9,8},{10,11... | collective-permute-start | bytes 2752520 | tf_op jit(solution)/shard_map/ppermute | solution.py:90

commit v20 on v16

--- a/solution.py
+++ b/solution.py
@@ -468,16 +468,18 @@
     main_ref[...] = jnp.concatenate(tops, axis=0).astype(jnp.bfloat16)
 
 
-def final_body(step, count_ref, kept_ref, given_ref, out_ref):
-    count = kept_ref.shape[0]
-
-    @pl.loop(0, count // step)
-    def _(block):
-        first = pl.multiple_of(block * step, step)
+def final_body(step, count_ref, kept_ref, given_ref, out_ref, done, sems):
+    copies = []
+    for block in range(kept_ref.shape[0] // step):
+        first = block * step
         at = pl.ds(first, step)
         total = kept_ref[at, :] + given_ref[at, :].astype(jnp.float32)
         row = lax.broadcasted_iota(jnp.int32, total.shape, 0) + first
-        out_ref[at, :] = jnp.where(row < count_ref[0], total, 0.0).astype(out_ref.dtype)
+        done[at, :] = jnp.where(row < count_ref[0], total, 0.0).astype(done.dtype)
+        copies.append(pltpu.make_async_copy(done.at[at, :], out_ref.at[at, :], sems.at[block]))
+        copies[-1].start()
+    for copy in copies:
+        copy.wait()
 
 
 def local(
@@ -651,15 +653,18 @@
     (kept,) = accumulate(
         rows[:1], weights, last, acc[:1], jnp.float32, "finish_own", residual=mixed_rows
     )
-    result = kernel_call(
+    result = pl.pallas_call(
         functools.partial(final_body, 64),
-        "final",
-        like(local_len, model, jnp.bfloat16),
-        valid_count,
-        kept,
-        flip_core(given),
-        specs=[pl.BlockSpec(memory_space=pltpu.SMEM)] + vmem(2),
-    )
+        out_shape=like(local_len, model, jnp.bfloat16),
+        in_specs=[pl.BlockSpec(memory_space=pltpu.SMEM)] + vmem(2),
+        out_specs=pl.BlockSpec(memory_space=pl.ANY),
+        scratch_shapes=[
+            pltpu.VMEM((local_len, model), jnp.bfloat16),
+            pltpu.SemaphoreType.DMA((local_len // 64,)),
+        ],
+        compiler_params=pltpu.CompilerParams(vmem_limit_bytes=24 * 1024 * 1024),
+        name="final",
+    )(valid_count, kept, flip_core(given))
     return (
         result[None],
         end_state.reshape((1, 1) + end_state.shape[:1] + end_state.shape[-1:]),

time: 87.9 us -> 87.9 us (level)
    pallas_call x14 -> x13, Pallas kernels: 23.6 us -> 22.4 us  [kernel_call(): pl.pallas_call(body, out_shape=out_shape, in_specs=specs or vmem(len(oper...]
    pallas_call x0 -> x1, Pallas kernels: none -> 1.02 us  [local(): pl.pallas_call(functools.partial(final_body, 64), out_shape=like(local_le...]
where the time goes in v20:
time: 87.9 us; the launch traced here: 87.4 us
  waiting for transfers between devices  28.8 us (33%)
  starting transfers between devices  27.1 us (31%)
  Pallas kernels  23.4 us (27%)
  local copies, waits for them, and re-layouts  6.61 us (8%)
  between operations  1.61 us (2%)
    ppermute x20, waiting for transfers between devices, permute(): return lax.ppermute(array, 'req', [(i, target(i)) for i in range(count)])  28.8 us
    ppermute x20, starting transfers between devices, permute(): return lax.ppermute(array, 'req', [(i, target(i)) for i in range(count)])  27.1 us
    pallas_call x13, Pallas kernels, kernel_call(): pl.pallas_call(body, out_shape=out_shape, in_specs=specs or vmem(len(oper...  22.4 us
    unnamed x20, local copies, waits for them, and re-layouts  5.89 us
  transfers between devices with their start and end apart: 20, of which 13 were waited for; matrix products, arithmetic and copies ran while one was open for 1% of the time, Pallas kernels for 21%

profile of v20, /device:TPU:0, one launch (start us, length us, event | category | flops | bytes accessed | tf_op | source)
XLA Modules:
  0.0 87.4 jit_solution(13196490455528469462)
XLA Ops:
  0.6 2.2 %shard.1 = (bf16[168,1792]{1,0:T(8,128)(2,1)}, bf16[144,1792]{1,0:T(8,128)(2,1)}) custom-call(bf16[56,1792]{1,0:T(8,128)(2,1)} %bitcast.17, bf16[56,1792]{1,0:T(8,128)(2,1)} %bitcast.18, bf16[56,1792]{1,0:T(8,128)(2,1)} %bitcast.19), custom_call_target="tpu_custom_call" | custom-call | flops 1000 | bytes 1000 | tf_op jit(solution)/shard_map/shard/pallas_call | solution.py:124
  2.8 3.0 %collective-permute-start = (bf16[168,1792]{1,0:T(8,128)(2,1)}, bf16[168,1792]{1,0:T(8,128)(2,1)S(1)}, u32[]{:S(2)}, u32[]{:S(2)}) collective-permute-start(bf16[168,1792]{1,0:T(8,128)(2,1)} %get-tuple-element.78.refs_0_), channel_id=1, source_target_pairs={{0,2},{1,3},{2,0},{3,1},{4,6},{5,7},{6,4},{7,5},{8,10},{9,11},{10,... | collective-permute-start | bytes 1806344 | tf_op jit(solution)/shard_map/ppermute | solution.py:90
  5.8 1.5 %collective-permute-start.1 = (bf16[168,1792]{1,0:T(8,128)(2,1)}, bf16[168,1792]{1,0:T(8,128)(2,1)S(1)}, u32[]{:S(2)}, u32[]{:S(2)}) collective-permute-start(bf16[168,1792]{1,0:T(8,128)(2,1)} %get-tuple-element.78.refs_0_), channel_id=1, source_target_pairs={{0,4},{1,5},{2,6},{3,7},{4,0},{5,1},{6,2},{7,3},{8,12},{9,13},{10,... | collective-permute-start | bytes 1806344 | tf_op jit(solution)/shard_map/ppermute | solution.py:90
  7.4 2.6 %collective-permute-start.2 = (bf16[144,1792]{1,0:T(8,128)(2,1)}, bf16[144,1792]{1,0:T(8,128)(2,1)S(1)}, u32[]{:S(2)}, u32[]{:S(2)}) collective-permute-start(bf16[144,1792]{1,0:T(8,128)(2,1)} %get-tuple-element.79), channel_id=1, source_target_pairs={{0,16},{1,17},{2,18},{3,19},{4,20},{5,21},{6,22},{7,23},{8,0},{9,1... | collective-permute-start | bytes 1548296 | tf_op jit(solution)/shard_map/ppermute | solution.py:90
  10.0 0.7 broadcast_in_dim.16.gain_ref
  10.7 1.2 %copy-done.1 = bf16[1,256,1792]{2,1,0:T(8,128)(2,1)S(1)} copy-done((bf16[1,256,1792]{2,1,0:T(8,128)(2,1)S(1)}, bf16[1,256,1792]{2,1,0:T(8,128)(2,1)}, u32[]{:S(2)}) %copy-start.1) | copy-done | bytes 917528
  11.9 1.9 %copy-done.3 = bf16[1792,896]{1,0:T(8,128)(2,1)S(1)} copy-done((bf16[1792,896]{1,0:T(8,128)(2,1)S(1)}, bf16[1792,896]{1,0:T(8,128)(2,1)}, u32[]{:S(2)}) %copy-start.3) | copy-done | bytes 3211288
  13.8 1.0 %copy-done.5 = bf16[1792,128]{1,0:T(8,128)(2,1)S(1)} copy-done((bf16[1792,128]{1,0:T(8,128)(2,1)S(1)}, bf16[1792,128]{1,0:T(8,128)(2,1)}, u32[]{:S(2)}) %copy-start.5) | copy-done | bytes 458776
  14.8 1.0 %copy-done.6 = bf16[1792,128]{1,0:T(8,128)(2,1)S(1)} copy-done((bf16[1792,128]{1,0:T(8,128)(2,1)S(1)}, bf16[1792,128]{1,0:T(8,128)(2,1)}, u32[]{:S(2)}) %copy-start.6) | copy-done | bytes 458776
  15.8 0.7 copy-done.7
  16.5 3.7 %project.1 = (bf16[256,128]{1,0:T(8,128)(2,1)S(1)}, bf16[256,128]{1,0:T(8,128)(2,1)S(1)}, bf16[256,896]{1,0:T(8,128)(2,1)S(1)}) custom-call(bf16[256,1792]{1,0:T(8,128)(2,1)S(1)} %bitcast.13, bf16[16,1792]{1,0:T(8,128)(2,1)S(1)} %broadcast_in_dim.15.edge_ref, f32[1,1792]{1,0:T(1,128)S(1)} %broadcast_in_dim.16.gain_ref, f32[3,1792]{1,0:T(4,128)S(1)} %copy-done.7, ...), custom_call_target="tpu_custom_call" | custom-call | flops 1000 | bytes 1000 | tf_op jit(solution)/shard_map/project/pallas_call | solution.py:124
  20.3 0.4 collective-permute-done.2.refs_3_
  20.7 0.4 collective-permute-done.1.refs_2_
  21.1 0.2 collect_second.1
  21.3 1.6 %collective-permute-start.4 = (bf16[232,1792]{1,0:T(8,128)(2,1)S(1)}, bf16[232,1792]{1,0:T(8,128)(2,1)S(1)}, u32[]{:S(2)}, u32[]{:S(2)}) collective-permute-start(bf16[232,1792]{1,0:T(8,128)(2,1)S(1)} %get-tuple-element.90), channel_id=1, source_target_pairs={{0,4},{1,5},{2,6},{3,7},{4,0},{5,1},{6,2},{7,3},{8,12},{9,13},{10,... | collective-permute-start | bytes 2494472 | tf_op jit(solution)/shard_map/ppermute | solution.py:90
  22.9 0.5 collective-permute-start.3
  23.4 2.6 %collective-permute-start.5 = (bf16[216,1792]{1,0:T(8,128)(2,1)S(1)}, bf16[216,1792]{1,0:T(8,128)(2,1)S(1)}, u32[]{:S(2)}, u32[]{:S(2)}) collective-permute-start(bf16[216,1792]{1,0:T(8,128)(2,1)S(1)} %get-tuple-element.91), channel_id=1, source_target_pairs={{0,16},{1,17},{2,18},{3,19},{4,20},{5,21},{6,22},{7,23},{8,0},{9,1... | collective-permute-start | bytes 2322440 | tf_op jit(solution)/shard_map/ppermute | solution.py:90
  26.7 3.7 %attend.1 = (f32[256,896]{1,0:T(8,128)S(1)}, f32[256,8]{1,0:T(8,128)S(1)}, f32[273,1,896]{2,1,0:T(1,128)}, f32[8,273]{1,0:T(8,128)}) custom-call(s32[1]{0:T(128)S(6)} %copy.23.count_ref, f32[8,256]{1,0:T(8,128)S(1)} %bitcast.15, bf16[256,128]{1,0:T(8,128)(2,1)S(1)} %get-tuple-element.95.queries_ref, bf16[256,128]{1,0:T(8,128)(2,1)S(1)} %get-tuple-element.96.keys_ref, ...), custom_call_target="tpu_custom_call" | custom-call | flops 1000 | bytes 1000 | tf_op jit(solution)/shard_map/attend/pallas_call | solution.py:124
  30.4 2.6 %mix.1 = (bf16[256,1792]{1,0:T(8,128)(2,1)S(1)}, bf16[256,1792]{1,0:T(8,128)(2,1)S(1)}) custom-call(f32[256,896]{1,0:T(8,128)S(1)} %get-tuple-element.98.numer_ref, f32[256,8]{1,0:T(8,128)S(1)} %get-tuple-element.99.denom_ref, bf16[256,1792]{1,0:T(8,128)(2,1)S(1)} %bitcast.14, bf16[896,1792]{1,0:T(8,128)(2,1)S(1)} %copy-done.4, ...), custom_call_target="tpu_custom_call" | custom-call | flops 1000 | bytes 1000 | tf_op jit(solution)/shard_map/mix/pallas_call | solution.py:124
  33.0 7.9 %collective-permute-done.5.refs_2_.refs_6_.refs_4_ = bf16[216,1792]{1,0:T(8,128)(2,1)S(1)} collective-permute-done((bf16[216,1792]{1,0:T(8,128)(2,1)S(1)}, bf16[216,1792]{1,0:T(8,128)(2,1)S(1)}, u32[]{:S(2)}, u32[]{:S(2)}) %collective-permute-start.5) | collective-permute-done | bytes 774176 | tf_op jit(solution)/shard_map/ppermute | solution.py:90
  40.8 0.2 collective-permute-done.3.refs_0_.refs_4_
  41.0 0.2 collect_third.1
  41.2 3.3 %collective-permute-start.8 = (bf16[240,1792]{1,0:T(8,128)(2,1)S(1)}, bf16[240,1792]{1,0:T(8,128)(2,1)S(1)}, u32[]{:S(2)}, u32[]{:S(2)}) collective-permute-start(bf16[240,1792]{1,0:T(8,128)(2,1)S(1)} %get-tuple-element.113), channel_id=1, source_target_pairs={{0,16},{1,17},{2,18},{3,19},{4,20},{5,21},{6,22},{7,23},{8,0},{9,1... | collective-permute-start | bytes 2580488 | tf_op jit(solution)/shard_map/ppermute | solution.py:90
  44.5 1.4 %collective-permute-start.6 = (bf16[224,1792]{1,0:T(8,128)(2,1)S(1)}, bf16[224,1792]{1,0:T(8,128)(2,1)S(1)}, u32[]{:S(2)}, u32[]{:S(2)}) collective-permute-start(bf16[224,1792]{1,0:T(8,128)(2,1)S(1)} %get-tuple-element.111), channel_id=1, source_target_pairs={{0,2},{1,3},{2,0},{3,1},{4,6},{5,7},{6,4},{7,5},{8,10},{9,11},{10,... | collective-permute-start | bytes 2408456 | tf_op jit(solution)/shard_map/ppermute | solution.py:90
  45.9 0.5 collective-permute-start.7
  46.4 0.5 collective-permute-start.10
  47.0 1.3 %collective-permute-done.9.refs_0_ = bf16[128,1792]{1,0:T(8,128)(2,1)S(1)} collective-permute-done((bf16[128,1792]{1,0:T(8,128)(2,1)S(1)}, bf16[128,1792]{1,0:T(8,128)(2,1)S(1)}, u32[]{:S(2)}, u32[]{:S(2)}) %collective-permute-start.9) | collective-permute-done | bytes 458784 | tf_op jit(solution)/shard_map/ppermute | solution.py:90
  48.3 0.7 collective-permute-done.10.refs_1_
  49.0 3.2 %accumulate_second.1 = (f32[256,1792]{1,0:T(8,128)S(1)}, f32[256,1792]{1,0:T(8,128)S(1)}) custom-call(bf16[168,1792]{1,0:T(8,128)(2,1)S(1)} %copy-done, bf16[168,1792]{1,0:T(8,128)(2,1)S(1)} %collective-permute-done.refs_1_, bf16[168,1792]{1,0:T(8,128)(2,1)S(1)} %collective-permute-done.1.refs_2_, bf16[144,1792]{1,0:T(8,128)(2,1)S(1)} %collective-permute-done.2.refs_3_, ...), custom_call_target="tpu_custom_call" | custom-call | flops 1000 | bytes 1000 | tf_op jit(solution)/shard_map/accumulate_second/pallas_call | solution.py:124
  52.2 8.9 %collective-permute-done.7.refs_1_.refs_6_ = bf16[208,1792]{1,0:T(8,128)(2,1)S(1)} collective-permute-done((bf16[208,1792]{1,0:T(8,128)(2,1)S(1)}, bf16[208,1792]{1,0:T(8,128)(2,1)S(1)}, u32[]{:S(2)}, u32[]{:S(2)}) %collective-permute-start.7) | collective-permute-done | bytes 745504 | tf_op jit(solution)/shard_map/ppermute | solution.py:90
  61.1 0.1 collective-permute-done.6.refs_0_.refs_5_
  61.4 2.6 %collective-permute-start.13 = (bf16[144,1792]{1,0:T(8,128)(2,1)S(1)}, bf16[144,1792]{1,0:T(8,128)(2,1)S(1)}, u32[]{:S(2)}, u32[]{:S(2)}) collective-permute-start(bf16[144,1792]{1,0:T(8,128)(2,1)S(1)} %get-tuple-element.126), channel_id=1, source_target_pairs={{0,16},{1,17},{2,18},{3,19},{4,20},{5,21},{6,22},{7,23},{8,0},{9,1... | collective-permute-start | bytes 1548296 | tf_op jit(solution)/shard_map/ppermute | solution.py:90
  64.0 1.4 %collective-permute-start.11 = (bf16[96,1792]{1,0:T(8,128)(2,1)S(1)}, bf16[96,1792]{1,0:T(8,128)(2,1)S(1)}, u32[]{:S(2)}, u32[]{:S(2)}) collective-permute-start(bf16[96,1792]{1,0:T(8,128)(2,1)S(1)} %get-tuple-element.124), channel_id=1, source_target_pairs={{0,2},{1,3},{2,0},{3,1},{4,6},{5,7},{6,4},{7,5},{8,10},{9,11},{10,... | collective-permute-start | bytes 1032200 | tf_op jit(solution)/shard_map/ppermute | solution.py:90
  65.4 0.4 collective-permute-start.12
  65.7 1.1 %collective-permute-start.14 = (bf16[96,1792]{1,0:T(8,128)(2,1)S(1)}, bf16[96,1792]{1,0:T(8,128)(2,1)S(1)}, u32[]{:S(2)}, u32[]{:S(2)}) collective-permute-start(bf16[96,1792]{1,0:T(8,128)(2,1)S(1)} %get-tuple-element.132), channel_id=1, source_target_pairs={{0,2},{1,3},{2,0},{3,1},{4,6},{5,7},{6,4},{7,5},{8,10},{9,11},{10,... | collective-permute-start | bytes 1032200 | tf_op jit(solution)/shard_map/ppermute | solution.py:90
  66.8 1.3 %collective-permute-start.15 = (bf16[96,1792]{1,0:T(8,128)(2,1)S(1)}, bf16[96,1792]{1,0:T(8,128)(2,1)S(1)}, u32[]{:S(2)}, u32[]{:S(2)}) collective-permute-start(bf16[96,1792]{1,0:T(8,128)(2,1)S(1)} %get-tuple-element.134), channel_id=1, source_target_pairs={{0,4},{1,5},{2,6},{3,7},{4,0},{5,1},{6,2},{7,3},{8,12},{9,13},{10,... | collective-permute-start | bytes 1032200 | tf_op jit(solution)/shard_map/ppermute | solution.py:90
  68.1 3.9 %accumulate_third.1 = (f32[256,1792]{1,0:T(8,128)S(1)}, f32[256,1792]{1,0:T(8,128)S(1)}) custom-call(bf16[168,1792]{1,0:T(8,128)(2,1)S(1)} %copy-done, bf16[168,1792]{1,0:T(8,128)(2,1)S(1)} %collective-permute-done.refs_1_, bf16[168,1792]{1,0:T(8,128)(2,1)S(1)} %collective-permute-done.1.refs_2_, ...), custom_call_target="tpu_custom_call", output_to_operand_aliasing={{0}: (10, {}), {1}: (11, {})} | custom-call | flops 1000 | bytes 1000 | tf_op jit(solution)/shard_map/accumulate_third/pallas_call | solution.py:124
  72.0 2.7 %collective-permute-done.11.refs_0_ = bf16[96,1792]{1,0:T(8,128)(2,1)S(1)} collective-permute-done((bf16[96,1792]{1,0:T(8,128)(2,1)S(1)}, bf16[96,1792]{1,0:T(8,128)(2,1)S(1)}, u32[]{:S(2)}, u32[]{:S(2)}) %collective-permute-start.11) | collective-permute-done | bytes 344096 | tf_op jit(solution)/shard_map/ppermute | solution.py:90
  74.6 1.1 %collective-permute-done.12.refs_1_.refs_2_ = bf16[96,1792]{1,0:T(8,128)(2,1)S(1)} collective-permute-done((bf16[96,1792]{1,0:T(8,128)(2,1)S(1)}, bf16[96,1792]{1,0:T(8,128)(2,1)S(1)}, u32[]{:S(2)}, u32[]{:S(2)}) %collective-permute-start.12) | collective-permute-done | bytes 344096 | tf_op jit(solution)/shard_map/ppermute | solution.py:90
  75.8 0.4 collective-permute-start.18
  76.2 1.1 %collective-permute-start.16 = (bf16[48,1792]{1,0:T(8,128)(2,1)S(1)}, bf16[48,1792]{1,0:T(8,128)(2,1)S(1)}, u32[]{:S(2)}, u32[]{:S(2)}) collective-permute-start(bf16[48,1792]{1,0:T(8,128)(2,1)S(1)} %get-tuple-element.136), channel_id=1, source_target_pairs={{0,2},{1,3},{2,0},{3,1},{4,6},{5,7},{6,4},{7,5},{8,10},{9,11},{10,... | collective-permute-start | bytes 516104 | tf_op jit(solution)/shard_map/ppermute | solution.py:90
  77.3 1.3 %collective-permute-start.17 = (bf16[48,1792]{1,0:T(8,128)(2,1)S(1)}, bf16[48,1792]{1,0:T(8,128)(2,1)S(1)}, u32[]{:S(2)}, u32[]{:S(2)}) collective-permute-start(bf16[48,1792]{1,0:T(8,128)(2,1)S(1)} %get-tuple-element.137), channel_id=1, source_target_pairs={{0,4},{1,5},{2,6},{3,7},{4,0},{5,1},{6,2},{7,3},{8,12},{9,13},{10,... | collective-permute-start | bytes 516104 | tf_op jit(solution)/shard_map/ppermute | solution.py:90
  78.5 3.1 %collective-permute-done.16.refs_5_ = bf16[48,1792]{1,0:T(8,128)(2,1)S(1)} collective-permute-done((bf16[48,1792]{1,0:T(8,128)(2,1)S(1)}, bf16[48,1792]{1,0:T(8,128)(2,1)S(1)}, u32[]{:S(2)}, u32[]{:S(2)}) %collective-permute-start.16) | collective-permute-done | bytes 172064 | tf_op jit(solution)/shard_map/ppermute | solution.py:90
  81.6 1.1 %collective-permute-done.17.refs_6_ = bf16[48,1792]{1,0:T(8,128)(2,1)S(1)} collective-permute-done((bf16[48,1792]{1,0:T(8,128)(2,1)S(1)}, bf16[48,1792]{1,0:T(8,128)(2,1)S(1)}, u32[]{:S(2)}, u32[]{:S(2)}) %collective-permute-start.17) | collective-permute-done | bytes 172064 | tf_op jit(solution)/shard_map/ppermute | solution.py:90
  82.7 1.0 %finish_other.1 = bf16[256,1792]{1,0:T(8,128)(2,1)S(1)} custom-call(bf16[96,1792]{1,0:T(8,128)(2,1)S(1)} %collective-permute-done.11.refs_0_, bf16[96,1792]{1,0:T(8,128)(2,1)S(1)} %collective-permute-done.14.refs_1_, bf16[96,1792]{1,0:T(8,128)(2,1)S(1)} %collective-permute-done.12.refs_1_.refs_2_, bf16[96,1792]{1,0:T(8,128)(2,1)S(1)} %collective-permute-done.15.refs_3_, ...), custom_call_target="tpu_custom_call" | custom-call | flops 1000 | bytes 1000 | tf_op jit(solution)/shard_map/finish_other/pallas_call | solution.py:124
  83.8 1.4 %finish_own.1.kept_ref = f32[256,1792]{1,0:T(8,128)S(1)} custom-call(bf16[96,1792]{1,0:T(8,128)(2,1)S(1)} %collective-permute-done.11.refs_0_, bf16[96,1792]{1,0:T(8,128)(2,1)S(1)} %collective-permute-done.14.refs_1_, bf16[96,1792]{1,0:T(8,128)(2,1)S(1)} %collective-permute-done.12.refs_1_.refs_2_, ...), custom_call_target="tpu_custom_call", output_to_operand_aliasing={{}: (9, {})} | custom-call | flops 1000 | bytes 1000 | tf_op jit(solution)/shard_map/finish_own/pallas_call | solution.py:124
  85.2 1.1 %collective-permute-done.19.given_ref = bf16[256,1792]{1,0:T(8,128)(2,1)S(1)} collective-permute-done((bf16[256,1792]{1,0:T(8,128)(2,1)S(1)}, bf16[256,1792]{1,0:T(8,128)(2,1)S(1)}, u32[]{:S(2)}, u32[]{:S(2)}) %collective-permute-start.19) | collective-permute-done | bytes 917536 | tf_op jit(solution)/shard_map/ppermute | solution.py:90
  86.3 1.0 %final.1 = bf16[256,1792]{1,0:T(8,128)(2,1)} custom-call(s32[1]{0:T(128)S(6)} %copy.23.count_ref, f32[256,1792]{1,0:T(8,128)S(1)} %finish_own.1.kept_ref, bf16[256,1792]{1,0:T(8,128)(2,1)S(1)} %collective-permute-done.19.given_ref), custom_call_target="tpu_custom_call" | custom-call | tf_op jit(solution)/shard_map/final/pallas_call | solution.py:656
  (29 shorter events, 0.4 us)
Async XLA Ops:
  2.8 17.9 %collective-permute-start = (bf16[168,1792]{1,0:T(8,128)(2,1)}, bf16[168,1792]{1,0:T(8,128)(2,1)S(1)}, u32[]{:S(2)}, u32[]{:S(2)}) collective-permute-start(bf16[168,1792]{1,0:T(8,128)(2,1)} %get-tuple-element.78.refs_0_), channel_id=1, source_target_pairs={{0,2},{1,3},{2,0},{3,1},{4,6},{5,7},{6,4},{7,5},{8,10},{9,11},{10,... | collective-permute-start | bytes 1806344 | tf_op jit(solution)/shard_map/ppermute | solution.py:90
  5.8 15.3 %collective-permute-start.1 = (bf16[168,1792]{1,0:T(8,128)(2,1)}, bf16[168,1792]{1,0:T(8,128)(2,1)S(1)}, u32[]{:S(2)}, u32[]{:S(2)}) collective-permute-start(bf16[168,1792]{1,0:T(8,128)(2,1)} %get-tuple-element.78.refs_0_), channel_id=1, source_target_pairs={{0,4},{1,5},{2,6},{3,7},{4,0},{5,1},{6,2},{7,3},{8,12},{9,13},{10,... | collective-permute-start | bytes 1806344 | tf_op jit(solution)/shard_map/ppermute | solution.py:90
  7.4 13.4 %collective-permute-start.2 = (bf16[144,1792]{1,0:T(8,128)(2,1)}, bf16[144,1792]{1,0:T(8,128)(2,1)S(1)}, u32[]{:S(2)}, u32[]{:S(2)}) collective-permute-start(bf16[144,1792]{1,0:T(8,128)(2,1)} %get-tuple-element.79), channel_id=1, source_target_pairs={{0,16},{1,17},{2,18},{3,19},{4,20},{5,21},{6,22},{7,23},{8,0},{9,1... | collective-permute-start | bytes 1548296 | tf_op jit(solution)/shard_map/ppermute | solution.py:90
  10.7 1.2 %copy-start.1 = (bf16[1,256,1792]{2,1,0:T(8,128)(2,1)S(1)}, bf16[1,256,1792]{2,1,0:T(8,128)(2,1)}, u32[]{:S(2)}) copy-start(bf16[1,256,1792]{2,1,0:T(8,128)(2,1)} %param.13) | copy-start | bytes 2752516
  11.8 1.9 %copy-start.3 = (bf16[1792,896]{1,0:T(8,128)(2,1)S(1)}, bf16[1792,896]{1,0:T(8,128)(2,1)}, u32[]{:S(2)}) copy-start(bf16[1792,896]{1,0:T(8,128)(2,1)} %value_ref.1) | copy-start | bytes 9633796
  13.8 1.0 %copy-start.5 = (bf16[1792,128]{1,0:T(8,128)(2,1)S(1)}, bf16[1792,128]{1,0:T(8,128)(2,1)}, u32[]{:S(2)}) copy-start(bf16[1792,128]{1,0:T(8,128)(2,1)} %query_ref.1) | copy-start | bytes 1376260
  14.8 1.0 %copy-start.6 = (bf16[1792,128]{1,0:T(8,128)(2,1)S(1)}, bf16[1792,128]{1,0:T(8,128)(2,1)}, u32[]{:S(2)}) copy-start(bf16[1792,128]{1,0:T(8,128)(2,1)} %key_ref.1) | copy-start | bytes 1376260
  15.8 0.7 copy-start.7
  16.5 4.6 %copy-start = (bf16[168,1792]{1,0:T(8,128)(2,1)S(1)}, bf16[168,1792]{1,0:T(8,128)(2,1)}, u32[]{:S(2)}) copy-start(bf16[168,1792]{1,0:T(8,128)(2,1)} %get-tuple-element.78.refs_0_) | copy-start | bytes 1806340
  16.5 13.8 %copy-start.4 = (bf16[896,1792]{1,0:T(8,128)(2,1)S(1)}, bf16[896,1792]{1,0:T(8,128)(2,1)}, u32[]{:S(2)}) copy-start(bf16[896,1792]{1,0:T(8,128)(2,1)} %out_ref.1) | copy-start | bytes 9633796
  20.3 6.4 %copy-start.9 = (f32[1792]{0:T(1024)S(1)}, f32[1792]{0:T(1024)}, u32[]{:S(2)}) copy-start(f32[1792]{0:T(1024)} %param.22) | copy-start | bytes 21508
  20.3 6.4 %copy-start.8 = (f32[1,256,8]{1,2,0:T(8,128)S(1)}, f32[1,256,8]{1,2,0:T(8,128)}, u32[]{:S(2)}) copy-start(f32[1,256,8]{1,2,0:T(8,128)} %param.15) | copy-start | bytes 24580
  20.3 10.1 %copy-start.2 = (bf16[1,256,1792]{2,1,0:T(8,128)(2,1)S(1)}, bf16[1,256,1792]{2,1,0:T(8,128)(2,1)}, u32[]{:S(2)}) copy-start(bf16[1,256,1792]{2,1,0:T(8,128)(2,1)} %param.13) | copy-start | bytes 2752516
  21.3 19.8 %collective-permute-start.4 = (bf16[232,1792]{1,0:T(8,128)(2,1)S(1)}, bf16[232,1792]{1,0:T(8,128)(2,1)S(1)}, u32[]{:S(2)}, u32[]{:S(2)}) collective-permute-start(bf16[232,1792]{1,0:T(8,128)(2,1)S(1)} %get-tuple-element.90), channel_id=1, source_target_pairs={{0,4},{1,5},{2,6},{3,7},{4,0},{5,1},{6,2},{7,3},{8,12},{9,13},{10,... | collective-permute-start | bytes 2494472 | tf_op jit(solution)/shard_map/ppermute | solution.py:90
  22.9 18.2 %collective-permute-start.3 = (bf16[224,1792]{1,0:T(8,128)(2,1)S(1)}, bf16[224,1792]{1,0:T(8,128)(2,1)S(1)}, u32[]{:S(2)}, u32[]{:S(2)}) collective-permute-start(bf16[224,1792]{1,0:T(8,128)(2,1)S(1)} %get-tuple-element.89), channel_id=1, source_target_pairs={{0,2},{1,3},{2,0},{3,1},{4,6},{5,7},{6,4},{7,5},{8,10},{9,11},{10,... | collective-permute-start | bytes 2408456 | tf_op jit(solution)/shard_map/ppermute | solution.py:90
  23.4 17.4 %collective-permute-start.5 = (bf16[216,1792]{1,0:T(8,128)(2,1)S(1)}, bf16[216,1792]{1,0:T(8,128)(2,1)S(1)}, u32[]{:S(2)}, u32[]{:S(2)}) collective-permute-start(bf16[216,1792]{1,0:T(8,128)(2,1)S(1)} %get-tuple-element.91), channel_id=1, source_target_pairs={{0,16},{1,17},{2,18},{3,19},{4,20},{5,21},{6,22},{7,23},{8,0},{9,1... | collective-permute-start | bytes 2322440 | tf_op jit(solution)/shard_map/ppermute | solution.py:90
  41.2 20.0 %collective-permute-start.8 = (bf16[240,1792]{1,0:T(8,128)(2,1)S(1)}, bf16[240,1792]{1,0:T(8,128)(2,1)S(1)}, u32[]{:S(2)}, u32[]{:S(2)}) collective-permute-start(bf16[240,1792]{1,0:T(8,128)(2,1)S(1)} %get-tuple-element.113), channel_id=1, source_target_pairs={{0,16},{1,17},{2,18},{3,19},{4,20},{5,21},{6,22},{7,23},{8,0},{9,1... | collective-permute-start | bytes 2580488 | tf_op jit(solution)/shard_map/ppermute | solution.py:90
  44.5 16.7 %collective-permute-start.6 = (bf16[224,1792]{1,0:T(8,128)(2,1)S(1)}, bf16[224,1792]{1,0:T(8,128)(2,1)S(1)}, u32[]{:S(2)}, u32[]{:S(2)}) collective-permute-start(bf16[224,1792]{1,0:T(8,128)(2,1)S(1)} %get-tuple-element.111), channel_id=1, source_target_pairs={{0,2},{1,3},{2,0},{3,1},{4,6},{5,7},{6,4},{7,5},{8,10},{9,11},{10,... | collective-permute-start | bytes 2408456 | tf_op jit(solution)/shard_map/ppermute | solution.py:90
  45.9 15.2 %collective-permute-start.7 = (bf16[208,1792]{1,0:T(8,128)(2,1)S(1)}, bf16[208,1792]{1,0:T(8,128)(2,1)S(1)}, u32[]{:S(2)}, u32[]{:S(2)}) collective-permute-start(bf16[208,1792]{1,0:T(8,128)(2,1)S(1)} %get-tuple-element.112), channel_id=1, source_target_pairs={{0,4},{1,5},{2,6},{3,7},{4,0},{5,1},{6,2},{7,3},{8,12},{9,13},{10,... | collective-permute-start | bytes 2236424 | tf_op jit(solution)/shard_map/ppermute | solution.py:90
  46.4 1.8 %collective-permute-start.9 = (bf16[128,1792]{1,0:T(8,128)(2,1)S(1)}, bf16[128,1792]{1,0:T(8,128)(2,1)S(1)}, u32[]{:S(2)}, u32[]{:S(2)}) collective-permute-start(bf16[128,1792]{1,0:T(8,128)(2,1)S(1)} %get-tuple-element.117), channel_id=1, source_target_pairs={{0,1},{1,0},{2,3},{3,2},{4,5},{5,4},{6,7},{7,6},{8,9},{9,8},{10,11... | collective-permute-start | bytes 1376264 | tf_op jit(solution)/shard_map/ppermute | solution.py:90
  46.4 2.5 %collective-permute-start.10 = (bf16[128,1792]{1,0:T(8,128)(2,1)S(1)}, bf16[128,1792]{1,0:T(8,128)(2,1)S(1)}, u32[]{:S(2)}, u32[]{:S(2)}) collective-permute-start(bf16[128,1792]{1,0:T(8,128)(2,1)S(1)} %get-tuple-element.118), channel_id=1, source_target_pairs={{0,1},{1,0},{2,3},{3,2},{4,5},{5,4},{6,7},{7,6},{8,9},{9,8},{10,11... | collective-permute-start | bytes 1376264 | tf_op jit(solution)/shard_map/ppermute | solution.py:90
  61.4 14.4 %collective-permute-start.13 = (bf16[144,1792]{1,0:T(8,128)(2,1)S(1)}, bf16[144,1792]{1,0:T(8,128)(2,1)S(1)}, u32[]{:S(2)}, u32[]{:S(2)}) collective-permute-start(bf16[144,1792]{1,0:T(8,128)(2,1)S(1)} %get-tuple-element.126), channel_id=1, source_target_pairs={{0,16},{1,17},{2,18},{3,19},{4,20},{5,21},{6,22},{7,23},{8,0},{9,1... | collective-permute-start | bytes 1548296 | tf_op jit(solution)/shard_map/ppermute | solution.py:90
  64.0 10.6 %collective-permute-start.11 = (bf16[96,1792]{1,0:T(8,128)(2,1)S(1)}, bf16[96,1792]{1,0:T(8,128)(2,1)S(1)}, u32[]{:S(2)}, u32[]{:S(2)}) collective-permute-start(bf16[96,1792]{1,0:T(8,128)(2,1)S(1)} %get-tuple-element.124), channel_id=1, source_target_pairs={{0,2},{1,3},{2,0},{3,1},{4,6},{5,7},{6,4},{7,5},{8,10},{9,11},{10,... | collective-permute-start | bytes 1032200 | tf_op jit(solution)/shard_map/ppermute | solution.py:90
  65.4 10.4 %collective-permute-start.12 = (bf16[96,1792]{1,0:T(8,128)(2,1)S(1)}, bf16[96,1792]{1,0:T(8,128)(2,1)S(1)}, u32[]{:S(2)}, u32[]{:S(2)}) collective-permute-start(bf16[96,1792]{1,0:T(8,128)(2,1)S(1)} %get-tuple-element.125), channel_id=1, source_target_pairs={{0,4},{1,5},{2,6},{3,7},{4,0},{5,1},{6,2},{7,3},{8,12},{9,13},{10,... | collective-permute-start | bytes 1032200 | tf_op jit(solution)/shard_map/ppermute | solution.py:90
  65.7 17.0 %collective-permute-start.14 = (bf16[96,1792]{1,0:T(8,128)(2,1)S(1)}, bf16[96,1792]{1,0:T(8,128)(2,1)S(1)}, u32[]{:S(2)}, u32[]{:S(2)}) collective-permute-start(bf16[96,1792]{1,0:T(8,128)(2,1)S(1)} %get-tuple-element.132), channel_id=1, source_target_pairs={{0,2},{1,3},{2,0},{3,1},{4,6},{5,7},{6,4},{7,5},{8,10},{9,11},{10,... | collective-permute-start | bytes 1032200 | tf_op jit(solution)/shard_map/ppermute | solution.py:90
  66.8 15.9 %collective-permute-start.15 = (bf16[96,1792]{1,0:T(8,128)(2,1)S(1)}, bf16[96,1792]{1,0:T(8,128)(2,1)S(1)}, u32[]{:S(2)}, u32[]{:S(2)}) collective-permute-start(bf16[96,1792]{1,0:T(8,128)(2,1)S(1)} %get-tuple-element.134), channel_id=1, source_target_pairs={{0,4},{1,5},{2,6},{3,7},{4,0},{5,1},{6,2},{7,3},{8,12},{9,13},{10,... | collective-permute-start | bytes 1032200 | tf_op jit(solution)/shard_map/ppermute | solution.py:90
  75.8 6.9 %collective-permute-start.18 = (bf16[72,1792]{1,0:T(8,128)(2,1)S(1)}, bf16[72,1792]{1,0:T(8,128)(2,1)S(1)}, u32[]{:S(2)}, u32[]{:S(2)}) collective-permute-start(bf16[72,1792]{1,0:T(8,128)(2,1)S(1)} %get-tuple-element.138), channel_id=1, source_target_pairs={{0,16},{1,17},{2,18},{3,19},{4,20},{5,21},{6,22},{7,23},{8,0},{9,1... | collective-permute-start | bytes 774152 | tf_op jit(solution)/shard_map/ppermute | solution.py:90
  76.2 5.4 %collective-permute-start.16 = (bf16[48,1792]{1,0:T(8,128)(2,1)S(1)}, bf16[48,1792]{1,0:T(8,128)(2,1)S(1)}, u32[]{:S(2)}, u32[]{:S(2)}) collective-permute-start(bf16[48,1792]{1,0:T(8,128)(2,1)S(1)} %get-tuple-element.136), channel_id=1, source_target_pairs={{0,2},{1,3},{2,0},{3,1},{4,6},{5,7},{6,4},{7,5},{8,10},{9,11},{10,... | collective-permute-start | bytes 516104 | tf_op jit(solution)/shard_map/ppermute | solution.py:90
  77.3 5.4 %collective-permute-start.17 = (bf16[48,1792]{1,0:T(8,128)(2,1)S(1)}, bf16[48,1792]{1,0:T(8,128)(2,1)S(1)}, u32[]{:S(2)}, u32[]{:S(2)}) collective-permute-start(bf16[48,1792]{1,0:T(8,128)(2,1)S(1)} %get-tuple-element.137), channel_id=1, source_target_pairs={{0,4},{1,5},{2,6},{3,7},{4,0},{5,1},{6,2},{7,3},{8,12},{9,13},{10,... | collective-permute-start | bytes 516104 | tf_op jit(solution)/shard_map/ppermute | solution.py:90
  83.7 2.5 %collective-permute-start.19 = (bf16[256,1792]{1,0:T(8,128)(2,1)S(1)}, bf16[256,1792]{1,0:T(8,128)(2,1)S(1)}, u32[]{:S(2)}, u32[]{:S(2)}) collective-permute-start(bf16[256,1792]{1,0:T(8,128)(2,1)S(1)} %finish_other.1), channel_id=1, source_target_pairs={{0,1},{1,0},{2,3},{3,2},{4,5},{5,4},{6,7},{7,6},{8,9},{9,8},{10,11... | collective-permute-start | bytes 2752520 | tf_op jit(solution)/shard_map/ppermute | solution.py:90

commit v21 on v20

--- a/solution.py
+++ b/solution.py
@@ -628,18 +628,10 @@
         jnp.float32,
         "accumulate_third",
     )
-    near3, far3, deep3, *acc = together(near3, far3, deep3, *acc)
-
-    sends = collect(
-        (near3, far3, deep3),
-        (
-            ((1, 0, main),),
-            ((0, 0, main),),
-            ((2, 3 * narrow, 4 * narrow + main),),
-        ),
-        "collect_fifth",
-    )
-    near4, far4, deep4 = slot(*zip((flip_near, flip_far, next_plane), sends))
+    near3, far3, *acc = together(near3, far3, *acc)
+
+    near4, far4 = flip_near(far3[:main]), flip_far(near3[:main])
+    deep4 = next_plane(deep3[3 * narrow :])
     line = 4 * narrow
     weights = (near3, near3_more, far3, far3_more, deep3, near4, far4, deep4)
     last = [

time: 87.9 us -> 91.7 us (1.043)
  starting transfers between devices: 27.1 us -> 29.7 us
  waiting for transfers between devices: 28.8 us -> 30 us
    ppermute x20, starting transfers between devices: 27.1 us -> 29.7 us  [permute(): return lax.ppermute(array, 'req', [(i, target(i)) for i in range(count)])]
    ppermute x20, waiting for transfers between devices: 28.8 us -> 30 us  [permute(): return lax.ppermute(array, 'req', [(i, target(i)) for i in range(count)])]
    pallas_call x13 -> x12, Pallas kernels: 22.4 us -> 22.3 us  [kernel_call(): pl.pallas_call(body, out_shape=out_shape, in_specs=specs or vmem(len(oper...]
  transfers between devices with their start and end apart: 20 -> 20, of which waited for: 13 -> 12; matrix products, arithmetic and copies ran while one was open for 1% -> 1% of each run, Pallas kernels for 21% -> 20%
where the time goes in v21:
time: 91.7 us; the launch traced here: 91.3 us
  waiting for transfers between devices  30 us (33%)
  starting transfers between devices  29.7 us (32%)
  Pallas kernels  23.3 us (25%)
  local copies, waits for them, and re-layouts  6.65 us (7%)
  between operations  1.63 us (2%)
    ppermute x20, waiting for transfers between devices, permute(): return lax.ppermute(array, 'req', [(i, target(i)) for i in range(count)])  30 us
    ppermute x20, starting transfers between devices, permute(): return lax.ppermute(array, 'req', [(i, target(i)) for i in range(count)])  29.7 us
    pallas_call x12, Pallas kernels, kernel_call(): pl.pallas_call(body, out_shape=out_shape, in_specs=specs or vmem(len(oper...  22.3 us
    unnamed x20, local copies, waits for them, and re-layouts  5.89 us
  transfers between devices with their start and end apart: 20, of which 12 were waited for; matrix products, arithmetic and copies ran while one was open for 1% of the time, Pallas kernels for 20%

profile of v21, /device:TPU:0, one launch (start us, length us, event | category | flops | bytes accessed | tf_op | source)
XLA Modules:
  0.0 91.3 jit_solution(3775432755302371678)
XLA Ops:
  0.6 2.2 %shard.1 = (bf16[168,1792]{1,0:T(8,128)(2,1)}, bf16[144,1792]{1,0:T(8,128)(2,1)}) custom-call(bf16[56,1792]{1,0:T(8,128)(2,1)} %bitcast.17, bf16[56,1792]{1,0:T(8,128)(2,1)} %bitcast.18, bf16[56,1792]{1,0:T(8,128)(2,1)} %bitcast.19), custom_call_target="tpu_custom_call" | custom-call | flops 1000 | bytes 1000 | tf_op jit(solution)/shard_map/shard/pallas_call | solution.py:124
  2.8 3.0 %collective-permute-start = (bf16[168,1792]{1,0:T(8,128)(2,1)}, bf16[168,1792]{1,0:T(8,128)(2,1)S(1)}, u32[]{:S(2)}, u32[]{:S(2)}) collective-permute-start(bf16[168,1792]{1,0:T(8,128)(2,1)} %get-tuple-element.71.refs_0_), channel_id=1, source_target_pairs={{0,2},{1,3},{2,0},{3,1},{4,6},{5,7},{6,4},{7,5},{8,10},{9,11},{10,... | collective-permute-start | bytes 1806344 | tf_op jit(solution)/shard_map/ppermute | solution.py:90
  5.8 1.5 %collective-permute-start.1 = (bf16[168,1792]{1,0:T(8,128)(2,1)}, bf16[168,1792]{1,0:T(8,128)(2,1)S(1)}, u32[]{:S(2)}, u32[]{:S(2)}) collective-permute-start(bf16[168,1792]{1,0:T(8,128)(2,1)} %get-tuple-element.71.refs_0_), channel_id=1, source_target_pairs={{0,4},{1,5},{2,6},{3,7},{4,0},{5,1},{6,2},{7,3},{8,12},{9,13},{10,... | collective-permute-start | bytes 1806344 | tf_op jit(solution)/shard_map/ppermute | solution.py:90
  7.4 2.6 %collective-permute-start.2 = (bf16[144,1792]{1,0:T(8,128)(2,1)}, bf16[144,1792]{1,0:T(8,128)(2,1)S(1)}, u32[]{:S(2)}, u32[]{:S(2)}) collective-permute-start(bf16[144,1792]{1,0:T(8,128)(2,1)} %get-tuple-element.72), channel_id=1, source_target_pairs={{0,16},{1,17},{2,18},{3,19},{4,20},{5,21},{6,22},{7,23},{8,0},{9,1... | collective-permute-start | bytes 1548296 | tf_op jit(solution)/shard_map/ppermute | solution.py:90
  10.0 0.7 broadcast_in_dim.16.gain_ref
  10.7 1.2 %copy-done.1 = bf16[1,256,1792]{2,1,0:T(8,128)(2,1)S(1)} copy-done((bf16[1,256,1792]{2,1,0:T(8,128)(2,1)S(1)}, bf16[1,256,1792]{2,1,0:T(8,128)(2,1)}, u32[]{:S(2)}) %copy-start.1) | copy-done | bytes 917528
  11.9 1.9 %copy-done.3 = bf16[1792,896]{1,0:T(8,128)(2,1)S(1)} copy-done((bf16[1792,896]{1,0:T(8,128)(2,1)S(1)}, bf16[1792,896]{1,0:T(8,128)(2,1)}, u32[]{:S(2)}) %copy-start.3) | copy-done | bytes 3211288
  13.8 1.0 %copy-done.5 = bf16[1792,128]{1,0:T(8,128)(2,1)S(1)} copy-done((bf16[1792,128]{1,0:T(8,128)(2,1)S(1)}, bf16[1792,128]{1,0:T(8,128)(2,1)}, u32[]{:S(2)}) %copy-start.5) | copy-done | bytes 458776
  14.8 1.0 %copy-done.6 = bf16[1792,128]{1,0:T(8,128)(2,1)S(1)} copy-done((bf16[1792,128]{1,0:T(8,128)(2,1)S(1)}, bf16[1792,128]{1,0:T(8,128)(2,1)}, u32[]{:S(2)}) %copy-start.6) | copy-done | bytes 458776
  15.8 0.7 copy-done.7
  16.5 3.7 %project.1 = (bf16[256,128]{1,0:T(8,128)(2,1)S(1)}, bf16[256,128]{1,0:T(8,128)(2,1)S(1)}, bf16[256,896]{1,0:T(8,128)(2,1)S(1)}) custom-call(bf16[256,1792]{1,0:T(8,128)(2,1)S(1)} %bitcast.13, bf16[16,1792]{1,0:T(8,128)(2,1)S(1)} %broadcast_in_dim.15.edge_ref, f32[1,1792]{1,0:T(1,128)S(1)} %broadcast_in_dim.16.gain_ref, f32[3,1792]{1,0:T(4,128)S(1)} %copy-done.7, ...), custom_call_target="tpu_custom_call" | custom-call | flops 1000 | bytes 1000 | tf_op jit(solution)/shard_map/project/pallas_call | solution.py:124
  20.3 0.4 collective-permute-done.2.refs_3_
  20.7 0.4 collective-permute-done.1.refs_2_
  21.1 0.2 collect_second.1
  21.3 1.6 %collective-permute-start.4 = (bf16[232,1792]{1,0:T(8,128)(2,1)S(1)}, bf16[232,1792]{1,0:T(8,128)(2,1)S(1)}, u32[]{:S(2)}, u32[]{:S(2)}) collective-permute-start(bf16[232,1792]{1,0:T(8,128)(2,1)S(1)} %get-tuple-element.83), channel_id=1, source_target_pairs={{0,4},{1,5},{2,6},{3,7},{4,0},{5,1},{6,2},{7,3},{8,12},{9,13},{10,... | collective-permute-start | bytes 2494472 | tf_op jit(solution)/shard_map/ppermute | solution.py:90
  22.9 0.5 collective-permute-start.3
  23.4 2.6 %collective-permute-start.5 = (bf16[216,1792]{1,0:T(8,128)(2,1)S(1)}, bf16[216,1792]{1,0:T(8,128)(2,1)S(1)}, u32[]{:S(2)}, u32[]{:S(2)}) collective-permute-start(bf16[216,1792]{1,0:T(8,128)(2,1)S(1)} %get-tuple-element.84), channel_id=1, source_target_pairs={{0,16},{1,17},{2,18},{3,19},{4,20},{5,21},{6,22},{7,23},{8,0},{9,1... | collective-permute-start | bytes 2322440 | tf_op jit(solution)/shard_map/ppermute | solution.py:90
  26.7 3.7 %attend.1 = (f32[256,896]{1,0:T(8,128)S(1)}, f32[256,8]{1,0:T(8,128)S(1)}, f32[273,1,896]{2,1,0:T(1,128)}, f32[8,273]{1,0:T(8,128)}) custom-call(s32[1]{0:T(128)S(6)} %copy.23.count_ref, f32[8,256]{1,0:T(8,128)S(1)} %bitcast.15, bf16[256,128]{1,0:T(8,128)(2,1)S(1)} %get-tuple-element.88.queries_ref, bf16[256,128]{1,0:T(8,128)(2,1)S(1)} %get-tuple-element.89.keys_ref, ...), custom_call_target="tpu_custom_call" | custom-call | flops 1000 | bytes 1000 | tf_op jit(solution)/shard_map/attend/pallas_call | solution.py:124
  30.4 2.6 %mix.1 = (bf16[256,1792]{1,0:T(8,128)(2,1)S(1)}, bf16[256,1792]{1,0:T(8,128)(2,1)S(1)}) custom-call(f32[256,896]{1,0:T(8,128)S(1)} %get-tuple-element.91.numer_ref, f32[256,8]{1,0:T(8,128)S(1)} %get-tuple-element.92.denom_ref, bf16[256,1792]{1,0:T(8,128)(2,1)S(1)} %bitcast.14, bf16[896,1792]{1,0:T(8,128)(2,1)S(1)} %copy-done.4, ...), custom_call_target="tpu_custom_call" | custom-call | flops 1000 | bytes 1000 | tf_op jit(solution)/shard_map/mix/pallas_call | solution.py:124
  33.0 7.9 %collective-permute-done.5.refs_2_.refs_6_.refs_4_ = bf16[216,1792]{1,0:T(8,128)(2,1)S(1)} collective-permute-done((bf16[216,1792]{1,0:T(8,128)(2,1)S(1)}, bf16[216,1792]{1,0:T(8,128)(2,1)S(1)}, u32[]{:S(2)}, u32[]{:S(2)}) %collective-permute-start.5) | collective-permute-done | bytes 774176 | tf_op jit(solution)/shard_map/ppermute | solution.py:90
  40.8 0.2 collective-permute-done.3.refs_0_.refs_4_
  41.0 0.2 collect_third.1
  41.2 3.3 %collective-permute-start.8 = (bf16[240,1792]{1,0:T(8,128)(2,1)S(1)}, bf16[240,1792]{1,0:T(8,128)(2,1)S(1)}, u32[]{:S(2)}, u32[]{:S(2)}) collective-permute-start(bf16[240,1792]{1,0:T(8,128)(2,1)S(1)} %get-tuple-element.106), channel_id=1, source_target_pairs={{0,16},{1,17},{2,18},{3,19},{4,20},{5,21},{6,22},{7,23},{8,0},{9,1... | collective-permute-start | bytes 2580488 | tf_op jit(solution)/shard_map/ppermute | solution.py:90
  44.5 1.4 %collective-permute-start.6 = (bf16[224,1792]{1,0:T(8,128)(2,1)S(1)}, bf16[224,1792]{1,0:T(8,128)(2,1)S(1)}, u32[]{:S(2)}, u32[]{:S(2)}) collective-permute-start(bf16[224,1792]{1,0:T(8,128)(2,1)S(1)} %get-tuple-element.104), channel_id=1, source_target_pairs={{0,2},{1,3},{2,0},{3,1},{4,6},{5,7},{6,4},{7,5},{8,10},{9,11},{10,... | collective-permute-start | bytes 2408456 | tf_op jit(solution)/shard_map/ppermute | solution.py:90
  45.9 0.5 collective-permute-start.7
  46.4 0.5 collective-permute-start.10
  47.0 1.3 %collective-permute-done.9.refs_0_ = bf16[128,1792]{1,0:T(8,128)(2,1)S(1)} collective-permute-done((bf16[128,1792]{1,0:T(8,128)(2,1)S(1)}, bf16[128,1792]{1,0:T(8,128)(2,1)S(1)}, u32[]{:S(2)}, u32[]{:S(2)}) %collective-permute-start.9) | collective-permute-done | bytes 458784 | tf_op jit(solution)/shard_map/ppermute | solution.py:90
  48.3 0.7 collective-permute-done.10.refs_1_
  49.0 3.2 %accumulate_second.1 = (f32[256,1792]{1,0:T(8,128)S(1)}, f32[256,1792]{1,0:T(8,128)S(1)}) custom-call(bf16[168,1792]{1,0:T(8,128)(2,1)S(1)} %copy-done, bf16[168,1792]{1,0:T(8,128)(2,1)S(1)} %collective-permute-done.refs_1_, bf16[168,1792]{1,0:T(8,128)(2,1)S(1)} %collective-permute-done.1.refs_2_, bf16[144,1792]{1,0:T(8,128)(2,1)S(1)} %collective-permute-done.2.refs_3_, ...), custom_call_target="tpu_custom_call" | custom-call | flops 1000 | bytes 1000 | tf_op jit(solution)/shard_map/accumulate_second/pallas_call | solution.py:124
  52.2 8.9 %collective-permute-done.7.refs_1_.refs_6_ = bf16[208,1792]{1,0:T(8,128)(2,1)S(1)} collective-permute-done((bf16[208,1792]{1,0:T(8,128)(2,1)S(1)}, bf16[208,1792]{1,0:T(8,128)(2,1)S(1)}, u32[]{:S(2)}, u32[]{:S(2)}) %collective-permute-start.7) | collective-permute-done | bytes 745504 | tf_op jit(solution)/shard_map/ppermute | solution.py:90
  61.1 0.1 collective-permute-done.6.refs_0_.refs_5_
  61.2 0.1 collect_fourth.1
  61.4 2.5 %collective-permute-start.15 = (bf16[144,1792]{1,0:T(8,128)(2,1)S(1)}, bf16[144,1792]{1,0:T(8,128)(2,1)S(1)}, u32[]{:S(2)}, u32[]{:S(2)}) collective-permute-start(bf16[144,1792]{1,0:T(8,128)(2,1)S(1)} %get-tuple-element.127), channel_id=1, source_target_pairs={{0,16},{1,17},{2,18},{3,19},{4,20},{5,21},{6,22},{7,23},{8,0},{9,1... | collective-permute-start | bytes 1548296 | tf_op jit(solution)/shard_map/ppermute | solution.py:90
  63.8 1.4 %collective-permute-start.11 = (bf16[96,1792]{1,0:T(8,128)(2,1)S(1)}, bf16[96,1792]{1,0:T(8,128)(2,1)S(1)}, u32[]{:S(2)}, u32[]{:S(2)}) collective-permute-start(bf16[96,1792]{1,0:T(8,128)(2,1)S(1)} %get-tuple-element.117), channel_id=1, source_target_pairs={{0,2},{1,3},{2,0},{3,1},{4,6},{5,7},{6,4},{7,5},{8,10},{9,11},{10,... | collective-permute-start | bytes 1032200 | tf_op jit(solution)/shard_map/ppermute | solution.py:90
  65.2 0.5 collective-permute-start.12
  65.7 0.9 collective-permute-start.13
  66.6 1.3 %collective-permute-start.14 = (bf16[96,1792]{1,0:T(8,128)(2,1)S(1)}, bf16[96,1792]{1,0:T(8,128)(2,1)S(1)}, u32[]{:S(2)}, u32[]{:S(2)}) collective-permute-start(bf16[96,1792]{1,0:T(8,128)(2,1)S(1)} %get-tuple-element.126), channel_id=1, source_target_pairs={{0,4},{1,5},{2,6},{3,7},{4,0},{5,1},{6,2},{7,3},{8,12},{9,13},{10,... | collective-permute-start | bytes 1032200 | tf_op jit(solution)/shard_map/ppermute | solution.py:90
  67.9 4.2 %collective-permute-done.15.refs_4_ = bf16[144,1792]{1,0:T(8,128)(2,1)S(1)} collective-permute-done((bf16[144,1792]{1,0:T(8,128)(2,1)S(1)}, bf16[144,1792]{1,0:T(8,128)(2,1)S(1)}, u32[]{:S(2)}, u32[]{:S(2)}) %collective-permute-start.15) | collective-permute-done | bytes 516128 | tf_op jit(solution)/shard_map/ppermute | solution.py:90
  72.1 3.6 %collective-permute-start.18 = (bf16[72,1792]{1,0:T(8,128)(2,1)S(1)}, bf16[72,1792]{1,0:T(8,128)(2,1)S(1)}, u32[]{:S(2)}, u32[]{:S(2)}) collective-permute-start(bf16[72,1792]{1,0:T(8,128)(2,1)S(1)} %slice.12), channel_id=1, source_target_pairs={{0,16},{1,17},{2,18},{3,19},{4,20},{5,21},{6,22},{7,23},{8,0},{9,1... | collective-permute-start | bytes 774152 | tf_op jit(solution)/shard_map/ppermute | solution.py:90
  75.7 3.9 %accumulate_third.1 = (f32[256,1792]{1,0:T(8,128)S(1)}, f32[256,1792]{1,0:T(8,128)S(1)}) custom-call(bf16[168,1792]{1,0:T(8,128)(2,1)S(1)} %copy-done, bf16[168,1792]{1,0:T(8,128)(2,1)S(1)} %collective-permute-done.refs_1_, bf16[168,1792]{1,0:T(8,128)(2,1)S(1)} %collective-permute-done.1.refs_2_, ...), custom_call_target="tpu_custom_call", output_to_operand_aliasing={{0}: (10, {}), {1}: (11, {})} | custom-call | flops 1000 | bytes 1000 | tf_op jit(solution)/shard_map/accumulate_third/pallas_call | solution.py:124
  79.7 1.4 %collective-permute-start.16 = (bf16[48,1792]{1,0:T(8,128)(2,1)S(1)}, bf16[48,1792]{1,0:T(8,128)(2,1)S(1)}, u32[]{:S(2)}, u32[]{:S(2)}) collective-permute-start(bf16[48,1792]{1,0:T(8,128)(2,1)S(1)} %slice.9), channel_id=1, source_target_pairs={{0,2},{1,3},{2,0},{3,1},{4,6},{5,7},{6,4},{7,5},{8,10},{9,11},{10,... | collective-permute-start | bytes 516104 | tf_op jit(solution)/shard_map/ppermute | solution.py:90
  81.2 0.5 collective-permute-start.17
  81.7 3.5 %collective-permute-done.16.refs_5_ = bf16[48,1792]{1,0:T(8,128)(2,1)S(1)} collective-permute-done((bf16[48,1792]{1,0:T(8,128)(2,1)S(1)}, bf16[48,1792]{1,0:T(8,128)(2,1)S(1)}, u32[]{:S(2)}, u32[]{:S(2)}) %collective-permute-start.16) | collective-permute-done | bytes 172064 | tf_op jit(solution)/shard_map/ppermute | solution.py:90
  85.2 1.4 %collective-permute-done.17.refs_6_ = bf16[48,1792]{1,0:T(8,128)(2,1)S(1)} collective-permute-done((bf16[48,1792]{1,0:T(8,128)(2,1)S(1)}, bf16[48,1792]{1,0:T(8,128)(2,1)S(1)}, u32[]{:S(2)}, u32[]{:S(2)}) %collective-permute-start.17) | collective-permute-done | bytes 172064 | tf_op jit(solution)/shard_map/ppermute | solution.py:90
  86.6 1.0 %finish_other.1 = bf16[256,1792]{1,0:T(8,128)(2,1)S(1)} custom-call(bf16[96,1792]{1,0:T(8,128)(2,1)S(1)} %collective-permute-done.11.refs_0_, bf16[96,1792]{1,0:T(8,128)(2,1)S(1)} %collective-permute-done.13.refs_1_, bf16[96,1792]{1,0:T(8,128)(2,1)S(1)} %collective-permute-done.12.refs_2_, bf16[96,1792]{1,0:T(8,128)(2,1)S(1)} %collective-permute-done.14.refs_3_, ...), custom_call_target="tpu_custom_call" | custom-call | flops 1000 | bytes 1000 | tf_op jit(solution)/shard_map/finish_other/pallas_call | solution.py:124
  87.7 1.4 %finish_own.1.kept_ref = f32[256,1792]{1,0:T(8,128)S(1)} custom-call(bf16[96,1792]{1,0:T(8,128)(2,1)S(1)} %collective-permute-done.11.refs_0_, bf16[96,1792]{1,0:T(8,128)(2,1)S(1)} %collective-permute-done.13.refs_1_, bf16[96,1792]{1,0:T(8,128)(2,1)S(1)} %collective-permute-done.12.refs_2_, ...), custom_call_target="tpu_custom_call", output_to_operand_aliasing={{}: (9, {})} | custom-call | flops 1000 | bytes 1000 | tf_op jit(solution)/shard_map/finish_own/pallas_call | solution.py:124
  89.1 1.1 %collective-permute-done.19.given_ref = bf16[256,1792]{1,0:T(8,128)(2,1)S(1)} collective-permute-done((bf16[256,1792]{1,0:T(8,128)(2,1)S(1)}, bf16[256,1792]{1,0:T(8,128)(2,1)S(1)}, u32[]{:S(2)}, u32[]{:S(2)}) %collective-permute-start.19) | collective-permute-done | bytes 917536 | tf_op jit(solution)/shard_map/ppermute | solution.py:90
  90.1 1.0 %final.1 = bf16[256,1792]{1,0:T(8,128)(2,1)} custom-call(s32[1]{0:T(128)S(6)} %copy.23.count_ref, f32[256,1792]{1,0:T(8,128)S(1)} %finish_own.1.kept_ref, bf16[256,1792]{1,0:T(8,128)(2,1)S(1)} %collective-permute-done.19.given_ref), custom_call_target="tpu_custom_call" | custom-call | tf_op jit(solution)/shard_map/final/pallas_call | solution.py:648
  (31 shorter events, 0.2 us)
Async XLA Ops:
  2.8 17.9 %collective-permute-start = (bf16[168,1792]{1,0:T(8,128)(2,1)}, bf16[168,1792]{1,0:T(8,128)(2,1)S(1)}, u32[]{:S(2)}, u32[]{:S(2)}) collective-permute-start(bf16[168,1792]{1,0:T(8,128)(2,1)} %get-tuple-element.71.refs_0_), channel_id=1, source_target_pairs={{0,2},{1,3},{2,0},{3,1},{4,6},{5,7},{6,4},{7,5},{8,10},{9,11},{10,... | collective-permute-start | bytes 1806344 | tf_op jit(solution)/shard_map/ppermute | solution.py:90
  5.8 15.3 %collective-permute-start.1 = (bf16[168,1792]{1,0:T(8,128)(2,1)}, bf16[168,1792]{1,0:T(8,128)(2,1)S(1)}, u32[]{:S(2)}, u32[]{:S(2)}) collective-permute-start(bf16[168,1792]{1,0:T(8,128)(2,1)} %get-tuple-element.71.refs_0_), channel_id=1, source_target_pairs={{0,4},{1,5},{2,6},{3,7},{4,0},{5,1},{6,2},{7,3},{8,12},{9,13},{10,... | collective-permute-start | bytes 1806344 | tf_op jit(solution)/shard_map/ppermute | solution.py:90
  7.4 13.4 %collective-permute-start.2 = (bf16[144,1792]{1,0:T(8,128)(2,1)}, bf16[144,1792]{1,0:T(8,128)(2,1)S(1)}, u32[]{:S(2)}, u32[]{:S(2)}) collective-permute-start(bf16[144,1792]{1,0:T(8,128)(2,1)} %get-tuple-element.72), channel_id=1, source_target_pairs={{0,16},{1,17},{2,18},{3,19},{4,20},{5,21},{6,22},{7,23},{8,0},{9,1... | collective-permute-start | bytes 1548296 | tf_op jit(solution)/shard_map/ppermute | solution.py:90
  10.7 1.2 %copy-start.1 = (bf16[1,256,1792]{2,1,0:T(8,128)(2,1)S(1)}, bf16[1,256,1792]{2,1,0:T(8,128)(2,1)}, u32[]{:S(2)}) copy-start(bf16[1,256,1792]{2,1,0:T(8,128)(2,1)} %param.13) | copy-start | bytes 2752516
  11.8 1.9 %copy-start.3 = (bf16[1792,896]{1,0:T(8,128)(2,1)S(1)}, bf16[1792,896]{1,0:T(8,128)(2,1)}, u32[]{:S(2)}) copy-start(bf16[1792,896]{1,0:T(8,128)(2,1)} %value_ref.1) | copy-start | bytes 9633796
  13.8 1.0 %copy-start.5 = (bf16[1792,128]{1,0:T(8,128)(2,1)S(1)}, bf16[1792,128]{1,0:T(8,128)(2,1)}, u32[]{:S(2)}) copy-start(bf16[1792,128]{1,0:T(8,128)(2,1)} %query_ref.1) | copy-start | bytes 1376260
  14.8 1.0 %copy-start.6 = (bf16[1792,128]{1,0:T(8,128)(2,1)S(1)}, bf16[1792,128]{1,0:T(8,128)(2,1)}, u32[]{:S(2)}) copy-start(bf16[1792,128]{1,0:T(8,128)(2,1)} %key_ref.1) | copy-start | bytes 1376260
  15.8 0.7 copy-start.7
  16.5 4.6 %copy-start = (bf16[168,1792]{1,0:T(8,128)(2,1)S(1)}, bf16[168,1792]{1,0:T(8,128)(2,1)}, u32[]{:S(2)}) copy-start(bf16[168,1792]{1,0:T(8,128)(2,1)} %get-tuple-element.71.refs_0_) | copy-start | bytes 1806340
  16.5 13.8 %copy-start.4 = (bf16[896,1792]{1,0:T(8,128)(2,1)S(1)}, bf16[896,1792]{1,0:T(8,128)(2,1)}, u32[]{:S(2)}) copy-start(bf16[896,1792]{1,0:T(8,128)(2,1)} %out_ref.1) | copy-start | bytes 9633796
  20.3 6.4 %copy-start.9 = (f32[1792]{0:T(1024)S(1)}, f32[1792]{0:T(1024)}, u32[]{:S(2)}) copy-start(f32[1792]{0:T(1024)} %param.22) | copy-start | bytes 21508
  20.3 6.4 %copy-start.8 = (f32[1,256,8]{1,2,0:T(8,128)S(1)}, f32[1,256,8]{1,2,0:T(8,128)}, u32[]{:S(2)}) copy-start(f32[1,256,8]{1,2,0:T(8,128)} %param.15) | copy-start | bytes 24580
  20.3 10.1 %copy-start.2 = (bf16[1,256,1792]{2,1,0:T(8,128)(2,1)S(1)}, bf16[1,256,1792]{2,1,0:T(8,128)(2,1)}, u32[]{:S(2)}) copy-start(bf16[1,256,1792]{2,1,0:T(8,128)(2,1)} %param.13) | copy-start | bytes 2752516
  21.3 19.8 %collective-permute-start.4 = (bf16[232,1792]{1,0:T(8,128)(2,1)S(1)}, bf16[232,1792]{1,0:T(8,128)(2,1)S(1)}, u32[]{:S(2)}, u32[]{:S(2)}) collective-permute-start(bf16[232,1792]{1,0:T(8,128)(2,1)S(1)} %get-tuple-element.83), channel_id=1, source_target_pairs={{0,4},{1,5},{2,6},{3,7},{4,0},{5,1},{6,2},{7,3},{8,12},{9,13},{10,... | collective-permute-start | bytes 2494472 | tf_op jit(solution)/shard_map/ppermute | solution.py:90
  22.9 18.2 %collective-permute-start.3 = (bf16[224,1792]{1,0:T(8,128)(2,1)S(1)}, bf16[224,1792]{1,0:T(8,128)(2,1)S(1)}, u32[]{:S(2)}, u32[]{:S(2)}) collective-permute-start(bf16[224,1792]{1,0:T(8,128)(2,1)S(1)} %get-tuple-element.82), channel_id=1, source_target_pairs={{0,2},{1,3},{2,0},{3,1},{4,6},{5,7},{6,4},{7,5},{8,10},{9,11},{10,... | collective-permute-start | bytes 2408456 | tf_op jit(solution)/shard_map/ppermute | solution.py:90
  23.4 17.4 %collective-permute-start.5 = (bf16[216,1792]{1,0:T(8,128)(2,1)S(1)}, bf16[216,1792]{1,0:T(8,128)(2,1)S(1)}, u32[]{:S(2)}, u32[]{:S(2)}) collective-permute-start(bf16[216,1792]{1,0:T(8,128)(2,1)S(1)} %get-tuple-element.84), channel_id=1, source_target_pairs={{0,16},{1,17},{2,18},{3,19},{4,20},{5,21},{6,22},{7,23},{8,0},{9,1... | collective-permute-start | bytes 2322440 | tf_op jit(solution)/shard_map/ppermute | solution.py:90
  41.2 20.0 %collective-permute-start.8 = (bf16[240,1792]{1,0:T(8,128)(2,1)S(1)}, bf16[240,1792]{1,0:T(8,128)(2,1)S(1)}, u32[]{:S(2)}, u32[]{:S(2)}) collective-permute-start(bf16[240,1792]{1,0:T(8,128)(2,1)S(1)} %get-tuple-element.106), channel_id=1, source_target_pairs={{0,16},{1,17},{2,18},{3,19},{4,20},{5,21},{6,22},{7,23},{8,0},{9,1... | collective-permute-start | bytes 2580488 | tf_op jit(solution)/shard_map/ppermute | solution.py:90
  44.5 16.7 %collective-permute-start.6 = (bf16[224,1792]{1,0:T(8,128)(2,1)S(1)}, bf16[224,1792]{1,0:T(8,128)(2,1)S(1)}, u32[]{:S(2)}, u32[]{:S(2)}) collective-permute-start(bf16[224,1792]{1,0:T(8,128)(2,1)S(1)} %get-tuple-element.104), channel_id=1, source_target_pairs={{0,2},{1,3},{2,0},{3,1},{4,6},{5,7},{6,4},{7,5},{8,10},{9,11},{10,... | collective-permute-start | bytes 2408456 | tf_op jit(solution)/shard_map/ppermute | solution.py:90
  45.9 15.2 %collective-permute-start.7 = (bf16[208,1792]{1,0:T(8,128)(2,1)S(1)}, bf16[208,1792]{1,0:T(8,128)(2,1)S(1)}, u32[]{:S(2)}, u32[]{:S(2)}) collective-permute-start(bf16[208,1792]{1,0:T(8,128)(2,1)S(1)} %get-tuple-element.105), channel_id=1, source_target_pairs={{0,4},{1,5},{2,6},{3,7},{4,0},{5,1},{6,2},{7,3},{8,12},{9,13},{10,... | collective-permute-start | bytes 2236424 | tf_op jit(solution)/shard_map/ppermute | solution.py:90
  46.4 1.8 %collective-permute-start.9 = (bf16[128,1792]{1,0:T(8,128)(2,1)S(1)}, bf16[128,1792]{1,0:T(8,128)(2,1)S(1)}, u32[]{:S(2)}, u32[]{:S(2)}) collective-permute-start(bf16[128,1792]{1,0:T(8,128)(2,1)S(1)} %get-tuple-element.110), channel_id=1, source_target_pairs={{0,1},{1,0},{2,3},{3,2},{4,5},{5,4},{6,7},{7,6},{8,9},{9,8},{10,11... | collective-permute-start | bytes 1376264 | tf_op jit(solution)/shard_map/ppermute | solution.py:90
  46.4 2.5 %collective-permute-start.10 = (bf16[128,1792]{1,0:T(8,128)(2,1)S(1)}, bf16[128,1792]{1,0:T(8,128)(2,1)S(1)}, u32[]{:S(2)}, u32[]{:S(2)}) collective-permute-start(bf16[128,1792]{1,0:T(8,128)(2,1)S(1)} %get-tuple-element.111), channel_id=1, source_target_pairs={{0,1},{1,0},{2,3},{3,2},{4,5},{5,4},{6,7},{7,6},{8,9},{9,8},{10,11... | collective-permute-start | bytes 1376264 | tf_op jit(solution)/shard_map/ppermute | solution.py:90
  61.4 10.7 %collective-permute-start.15 = (bf16[144,1792]{1,0:T(8,128)(2,1)S(1)}, bf16[144,1792]{1,0:T(8,128)(2,1)S(1)}, u32[]{:S(2)}, u32[]{:S(2)}) collective-permute-start(bf16[144,1792]{1,0:T(8,128)(2,1)S(1)} %get-tuple-element.127), channel_id=1, source_target_pairs={{0,16},{1,17},{2,18},{3,19},{4,20},{5,21},{6,22},{7,23},{8,0},{9,1... | collective-permute-start | bytes 1548296 | tf_op jit(solution)/shard_map/ppermute | solution.py:90
  63.8 15.8 %collective-permute-start.11 = (bf16[96,1792]{1,0:T(8,128)(2,1)S(1)}, bf16[96,1792]{1,0:T(8,128)(2,1)S(1)}, u32[]{:S(2)}, u32[]{:S(2)}) collective-permute-start(bf16[96,1792]{1,0:T(8,128)(2,1)S(1)} %get-tuple-element.117), channel_id=1, source_target_pairs={{0,2},{1,3},{2,0},{3,1},{4,6},{5,7},{6,4},{7,5},{8,10},{9,11},{10,... | collective-permute-start | bytes 1032200 | tf_op jit(solution)/shard_map/ppermute | solution.py:90
  65.2 14.5 %collective-permute-start.12 = (bf16[96,1792]{1,0:T(8,128)(2,1)S(1)}, bf16[96,1792]{1,0:T(8,128)(2,1)S(1)}, u32[]{:S(2)}, u32[]{:S(2)}) collective-permute-start(bf16[96,1792]{1,0:T(8,128)(2,1)S(1)} %get-tuple-element.118), channel_id=1, source_target_pairs={{0,4},{1,5},{2,6},{3,7},{4,0},{5,1},{6,2},{7,3},{8,12},{9,13},{10,... | collective-permute-start | bytes 1032200 | tf_op jit(solution)/shard_map/ppermute | solution.py:90
  65.7 16.0 %collective-permute-start.13 = (bf16[96,1792]{1,0:T(8,128)(2,1)S(1)}, bf16[96,1792]{1,0:T(8,128)(2,1)S(1)}, u32[]{:S(2)}, u32[]{:S(2)}) collective-permute-start(bf16[96,1792]{1,0:T(8,128)(2,1)S(1)} %get-tuple-element.124), channel_id=1, source_target_pairs={{0,2},{1,3},{2,0},{3,1},{4,6},{5,7},{6,4},{7,5},{8,10},{9,11},{10,... | collective-permute-start | bytes 1032200 | tf_op jit(solution)/shard_map/ppermute | solution.py:90
  66.6 15.1 %collective-permute-start.14 = (bf16[96,1792]{1,0:T(8,128)(2,1)S(1)}, bf16[96,1792]{1,0:T(8,128)(2,1)S(1)}, u32[]{:S(2)}, u32[]{:S(2)}) collective-permute-start(bf16[96,1792]{1,0:T(8,128)(2,1)S(1)} %get-tuple-element.126), channel_id=1, source_target_pairs={{0,4},{1,5},{2,6},{3,7},{4,0},{5,1},{6,2},{7,3},{8,12},{9,13},{10,... | collective-permute-start | bytes 1032200 | tf_op jit(solution)/shard_map/ppermute | solution.py:90
  72.1 14.4 %collective-permute-start.18 = (bf16[72,1792]{1,0:T(8,128)(2,1)S(1)}, bf16[72,1792]{1,0:T(8,128)(2,1)S(1)}, u32[]{:S(2)}, u32[]{:S(2)}) collective-permute-start(bf16[72,1792]{1,0:T(8,128)(2,1)S(1)} %slice.12), channel_id=1, source_target_pairs={{0,16},{1,17},{2,18},{3,19},{4,20},{5,21},{6,22},{7,23},{8,0},{9,1... | collective-permute-start | bytes 774152 | tf_op jit(solution)/shard_map/ppermute | solution.py:90
  79.7 5.5 %collective-permute-start.16 = (bf16[48,1792]{1,0:T(8,128)(2,1)S(1)}, bf16[48,1792]{1,0:T(8,128)(2,1)S(1)}, u32[]{:S(2)}, u32[]{:S(2)}) collective-permute-start(bf16[48,1792]{1,0:T(8,128)(2,1)S(1)} %slice.9), channel_id=1, source_target_pairs={{0,2},{1,3},{2,0},{3,1},{4,6},{5,7},{6,4},{7,5},{8,10},{9,11},{10,... | collective-permute-start | bytes 516104 | tf_op jit(solution)/shard_map/ppermute | solution.py:90
  81.2 5.4 %collective-permute-start.17 = (bf16[48,1792]{1,0:T(8,128)(2,1)S(1)}, bf16[48,1792]{1,0:T(8,128)(2,1)S(1)}, u32[]{:S(2)}, u32[]{:S(2)}) collective-permute-start(bf16[48,1792]{1,0:T(8,128)(2,1)S(1)} %slice.10), channel_id=1, source_target_pairs={{0,4},{1,5},{2,6},{3,7},{4,0},{5,1},{6,2},{7,3},{8,12},{9,13},{10,... | collective-permute-start | bytes 516104 | tf_op jit(solution)/shard_map/ppermute | solution.py:90
  87.6 2.5 %collective-permute-start.19 = (bf16[256,1792]{1,0:T(8,128)(2,1)S(1)}, bf16[256,1792]{1,0:T(8,128)(2,1)S(1)}, u32[]{:S(2)}, u32[]{:S(2)}) collective-permute-start(bf16[256,1792]{1,0:T(8,128)(2,1)S(1)} %finish_other.1), channel_id=1, source_target_pairs={{0,1},{1,0},{2,3},{3,2},{4,5},{5,4},{6,7},{7,6},{8,9},{9,8},{10,11... | collective-permute-start | bytes 2752520 | tf_op jit(solution)/shard_map/ppermute | solution.py:90
